TPU v7x, 32 devices: a whole 2x2x4 slice. The times are simulated.
32 devices in a mesh: groups: 2 (over y), rows: 4 (over z), tiles: 2 (over x), cols: 2 (over core).
Axes of the slice: x: 2, y: 2, z: 4, core: 2. Of those that a mesh axis runs over, the one named last changes fastest.
Arguments:
- embeddings: bfloat16 [16384, 768], P(('groups', 'rows'), 'cols'), parts along dimension 0
- start: float32 [16384, 64], P(('groups', 'rows'), 'cols'), parts along dimension 0, may hold values from -6 to 6
- pair_list: int32 [16, 2, 8], P(('groups', 'rows', 'tiles')), parts along dimension 0, may hold values from 0 to 63, as said below
- pair_count: int32 [16], P(('groups', 'rows', 'tiles')), parts along dimension 0, may hold values from 2 to 8, as said below
Outputs:
- vectors: float32 [16384, 64], P(('groups', 'rows'), 'cols'), parts along dimension 0
- degree: float32 [16384], P(('groups', 'rows')), parts along dimension 0
There are 2 independent parts, one for each index of `groups`. A program takes and returns all parts, laid end to end along the dimension named above; each array names one. Nothing has to cross between parts.
Inputs may be any that keep to these rules, and one draw needn't show every extreme that they name: For list q let r = q // 2: every pair_list[q, 0, s] lies in r * 16 to (r + 1) * 16 - 1, and pair_list[q, 1, s] differs from pair_list[q, 0, s]. Among the live slots of list q, at most 2 have the same value of pair_list[q, 1, s] // 16; the list with 8 live slots has exactly 2 for every value. `pair_count`: some list has all 8 slots live.
All inputs are finite; a program needn't handle non-finite values.
Results may differ from a plain program's by a relative error of at most 0.0003.
Values may be sent and summed in bfloat16 or wider, within the bound.
No kernel may reach another device: no remote copies, remote signals or barrier semaphores. Data moves between devices by JAX's collectives and lax.ppermute only.
A program may use at most 128 MiB of HBM per device.

v0:
```python
import jax
import jax.numpy as jnp
from jax import lax
from jax.sharding import PartitionSpec as P

BLOCK = 128
ITERS = 2


kernel_gamma = 14.0


def upper_inverse(gram_matrix):
    lower = jnp.linalg.cholesky(gram_matrix)
    identity = jnp.eye(gram_matrix.shape[0], dtype=gram_matrix.dtype)
    inverse = lax.linalg.triangular_solve(lower, identity, left_side=True, lower=True)
    return inverse.T


def pick_blocks(source, chosen_ids):
    block_ids = jnp.arange(source.shape[0], dtype=jnp.int32)
    selector = chosen_ids[:, None] == block_ids[None, :]
    if source.dtype == jnp.bfloat16:
        picked = jnp.einsum(
            "sb,bak->sak", selector.astype(jnp.bfloat16), source, preferred_element_type=jnp.float32
        )
        return picked.astype(jnp.bfloat16)
    return jnp.einsum(
        "sb,bak->sak", selector.astype(jnp.float32), source, precision=lax.Precision.HIGHEST
    )


def distances(left, right):
    inner_prod = jnp.einsum("sak,sck->sac", left, right, preferred_element_type=jnp.float32)
    left_sq = jnp.sum(jnp.square(left.astype(jnp.float32)), axis=-1)
    right_sq = jnp.sum(jnp.square(right.astype(jnp.float32)), axis=-1)
    return left_sq[:, :, None] + right_sq[:, None, :] - 2.0 * inner_prod


def orthonormal(mapped, col_index):
    full_rows = lax.all_gather(mapped, "cols", axis=1, tiled=True)
    gram_part = jnp.dot(full_rows.T, full_rows, precision=lax.Precision.HIGHEST)
    gram_matrix = lax.psum(gram_part, "rows")
    inverse = upper_inverse(gram_matrix)
    own_cols = mapped.shape[1]
    own_part = lax.dynamic_slice_in_dim(inverse, col_index * own_cols, own_cols, 1)
    return jnp.dot(full_rows, own_part, precision=lax.Precision.HIGHEST)


def local(embeddings, start, pair_list, pair_count):
    row_count = lax.axis_size("rows")
    tile_count = lax.axis_size("tiles")
    tile_index = lax.axis_index("tiles")
    row_index = lax.axis_index("rows")
    col_index = lax.axis_index("cols")
    rows_here = embeddings.shape[0]
    blocks_here = rows_here // BLOCK
    slot_count = pair_list.shape[2]
    capacity = slot_count // row_count
    near_ids = pair_list[0, 0]
    far_ids = pair_list[0, 1]
    live_count = pair_count[0]
    positions = jnp.arange(slot_count, dtype=jnp.int32)
    active = positions < live_count
    owners = far_ids // blocks_here
    earlier = (
        (owners[:, None] == owners[None, :])
        & active[None, :]
        & (positions[None, :] < positions[:, None])
    )
    earlier_count = jnp.sum(earlier.astype(jnp.int32), axis=1)
    target = owners * capacity + earlier_count
    placed = ((target[None, :] == positions[:, None]) & active[None, :]).astype(jnp.int32)
    filled = jnp.sum(placed, axis=1)
    near_block = jnp.sum(placed * (near_ids - row_index * blocks_here)[None, :], axis=1)
    far_block = jnp.sum(placed * (far_ids % blocks_here)[None, :], axis=1)
    incoming = lax.all_to_all(
        far_block.reshape(row_count, capacity), "rows", split_axis=0, concat_axis=0, tiled=True
    ).reshape(slot_count)
    source_rows = lax.all_gather(embeddings, "cols", axis=1, tiled=True)
    features = source_rows.shape[1]
    source_blocks = source_rows.reshape(blocks_here, BLOCK, features)
    sent_rows = pick_blocks(source_blocks, incoming).reshape(row_count, capacity * BLOCK, features)
    far_rows = lax.all_to_all(sent_rows, "rows", split_axis=0, concat_axis=0, tiled=True).reshape(
        slot_count, BLOCK, features
    )
    near_rows = pick_blocks(source_blocks, near_block)
    own_blocks = blocks_here // tile_count
    own_rows = lax.dynamic_index_in_dim(
        source_blocks.reshape(own_blocks, tile_count, BLOCK, features),
        tile_index,
        1,
        keepdims=False,
    )
    pair_dist = distances(near_rows, far_rows)
    self_dist = distances(own_rows, own_rows)
    pair_tiles = jnp.where(
        filled[:, None, None] > 0, jnp.exp(-kernel_gamma * (pair_dist - 2.0)), 0.0
    )
    hollow = 1.0 - jnp.eye(BLOCK, dtype=jnp.float32)
    self_tiles = jnp.exp(-kernel_gamma * (self_dist - 2.0)) * hollow[None]
    block_ids = jnp.arange(blocks_here, dtype=jnp.int32)
    near_onehot = ((near_block[None, :] == block_ids[:, None]) & (filled[None, :] > 0)).astype(
        jnp.float32
    )
    in_onehot = (incoming[None, :] == block_ids[:, None]).astype(jnp.float32)
    tile_mask = (jnp.arange(tile_count, dtype=jnp.int32) == tile_index).astype(jnp.float32)

    def spread(near_part, back_part, self_part):
        summed = jnp.einsum("bs,sac->bac", near_onehot, near_part, precision=lax.Precision.HIGHEST)
        summed = summed + jnp.einsum(
            "bs,sac->bac", in_onehot, back_part, precision=lax.Precision.HIGHEST
        )
        diagonal_part = self_part[:, None] * tile_mask[None, :, None, None]
        summed = summed + diagonal_part.reshape(blocks_here, BLOCK, -1)
        return summed.reshape(rows_here, -1)

    col_sums = jnp.sum(pair_tiles, axis=1)
    back_sums = lax.all_to_all(
        col_sums.reshape(row_count, capacity * BLOCK),
        "rows",
        split_axis=0,
        concat_axis=0,
        tiled=True,
    )
    degree_part = spread(
        jnp.sum(pair_tiles, axis=2)[:, :, None],
        back_sums.reshape(slot_count, BLOCK, 1),
        jnp.sum(self_tiles, axis=2)[:, :, None],
    )
    degree = lax.psum(degree_part[:, 0], "tiles")
    inv_root = 1.0 / jnp.sqrt(degree)
    vectors = start
    own_cols = start.shape[1]
    for iteration in range(ITERS):
        blocks_in = (vectors * inv_root[:, None]).reshape(blocks_here, BLOCK, own_cols)
        far_send = pick_blocks(blocks_in, incoming).reshape(row_count, capacity * BLOCK, own_cols)
        far_in = lax.all_to_all(far_send, "rows", split_axis=0, concat_axis=0, tiled=True).reshape(
            slot_count, BLOCK, own_cols
        )
        near_in = pick_blocks(blocks_in, near_block)
        own_in = lax.dynamic_index_in_dim(
            blocks_in.reshape(own_blocks, tile_count, BLOCK, own_cols),
            tile_index,
            1,
            keepdims=False,
        )
        near_out = jnp.einsum("sac,sck->sak", pair_tiles, far_in, precision=lax.Precision.HIGHEST)
        far_out = jnp.einsum("sac,sak->sck", pair_tiles, near_in, precision=lax.Precision.HIGHEST)
        back_out = lax.all_to_all(
            far_out.reshape(row_count, capacity * BLOCK, own_cols),
            "rows",
            split_axis=0,
            concat_axis=0,
            tiled=True,
        )
        self_out = jnp.einsum("mac,mck->mak", self_tiles, own_in, precision=lax.Precision.HIGHEST)
        partial_sum = spread(near_out, back_out.reshape(slot_count, BLOCK, own_cols), self_out)
        mapped = lax.psum(partial_sum, "tiles") * inv_root[:, None]
        vectors = orthonormal(mapped, col_index)
    return (vectors, degree)


def solution(mesh):
    in_specs = (
        P(("groups", "rows"), "cols"),
        P(("groups", "rows"), "cols"),
        P(("groups", "rows", "tiles"), None, None),
        P(("groups", "rows", "tiles")),
    )
    out_specs = (P(("groups", "rows"), "cols"), P(("groups", "rows")))
    return jax.shard_map(local, mesh=mesh, in_specs=in_specs, out_specs=out_specs, check_vma=False)
```

profile of v0, /device:TPU:0, one launch (start us, length us, event | category | flops | bytes accessed | tf_op | source)
XLA Modules:
  0.0 259.5 jit_solution(9090022833745916473)
XLA Ops:
  11.1 11.7 %all_to_all.43 = s32[4,1,2]{2,1,0:T(1,128)S(1)} all-to-all(s32[4,1,2]{2,1,0:T(1,128)S(1)} %bitcast.171), channel_id=1, replica_groups=mesh['groups'=2,'rows'=4,'tiles'=2,'cols'=2] {'rows'}, dimensions={0} | all-to-all | bytes 64 | tf_op jit(solution)/shard_map/all_to_all | solution.py:77
  24.3 3.7 %fusion.7 = bf16[8,128,768]{2,0,1:T(8,128)(2,1)S(1)} fusion(bf16[16,128,768]{2,1,0:T(8,128)(2,1)} %bitcast.154, s32[8]{0:T(128)S(1)} %eq.66), kind=kOutput, calls=%fused_computation.9 | convolution fusion | flops 25952384 | bytes 4718624 | tf_op jit(solution)/shard_map/sb,bak->sak/dot_general | solution.py:24
  28.0 1.5 copy.97
  29.5 5.0 %all-to-all-start.1 = ((bf16[4,256,768]{2,1,0:T(8,128)(2,1)}), bf16[4,256,768]{2,1,0:T(8,128)(2,1)}, u32[]{:S(2)}, u32[]{:S(2)}) async-start(bf16[4,256,768]{2,1,0:T(8,128)(2,1)} %bitcast.158), calls=%async_computation.1 | async-start | bytes 3145728 | tf_op jit(solution)/shard_map/all_to_all | solution.py:84
  34.6 3.0 %multiply_reduce_fusion.2 = (f32[8,128]{0,1:T(8,128)S(1)}, bf16[8,128,768]{2,0,1:T(8,128)(2,1)}) fusion(bf16[16,128,768]{2,1,0:T(8,128)(2,1)S(1)} %bitcast.155, s32[8]{0:T(128)S(1)} %get-tuple-element.8), kind=kOutput, calls=%fused_computation.2 | convolution fusion | flops 28310656 | bytes 4722720 | tf_op jit(solution)/shard_map/sb,bak->sak/dot_general | solution.py:24
  38.1 1.4 fusion.126
  39.5 32.5 %all-to-all-done.1 = bf16[4,256,768]{2,1,0:T(8,128)(2,1)} async-done(((bf16[4,256,768]{2,1,0:T(8,128)(2,1)}), bf16[4,256,768]{2,1,0:T(8,128)(2,1)}, u32[]{:S(2)}, u32[]{:S(2)}) %all-to-all-start.1) | async-done | bytes 1572896 | tf_op jit(solution)/shard_map/all_to_all | solution.py:84
  72.0 1.8 multiply_reduce_fusion.1
  73.8 3.2 %fusion.125 = (f32[8,128]{1,0:T(8,128)}, f32[8,128]{1,0:T(8,128)S(1)}, f32[8,128,128]{2,1,0:T(8,128)S(1)}) fusion(bf16[8,128,768]{2,1,0:T(8,128)(2,1)} %bitcast.9, bf16[8,128,768]{2,0,1:T(8,128)(2,1)} %get-tuple-element.12, f32[8,128]{1,0:T(8,128)S(1)} %add.111, f32[8,128]{1,0:T(8,128)S(1)} %copy.94, pred[8]{0:T(512)(128)(4,1)S(1)} %broadcast_compare_fusion), kind=kOutput, calls=%fused_computation.134 | convolution fusion | flops 202373120 | bytes 3686408 | tf_op jit(solution)/shard_map/sak,sck->sac/dot_general | solution.py:34
  77.0 3.4 %all-to-all-start.2 = ((f32[4,1,256]{2,1,0:T(1,128)}), f32[4,1,256]{2,1,0:T(1,128)S(1)}, u32[]{:S(2)}, u32[]{:S(2)}) async-start(f32[4,1,256]{2,1,0:T(1,128)} %bitcast.10), calls=%async_computation.2 | async-start | bytes 8192 | tf_op jit(solution)/shard_map/all_to_all | solution.py:119
  80.7 5.3 %all-to-all-done.2 = f32[4,1,256]{2,1,0:T(1,128)S(1)} async-done(((f32[4,1,256]{2,1,0:T(1,128)}), f32[4,1,256]{2,1,0:T(1,128)S(1)}, u32[]{:S(2)}, u32[]{:S(2)}) %all-to-all-start.2) | async-done | bytes 4128 | tf_op jit(solution)/shard_map/all_to_all | solution.py:119
  86.2 5.0 %psum.35 = f32[2048]{0:T(1024)S(1)} all-reduce(f32[2048]{0:T(1024)S(1)} %fusion.36), channel_id=1, replica_groups=mesh['groups'=2,'rows'=4,'tiles'=2,'cols'=2] {'tiles'}, use_global_device_ids=true, to_apply=%region_10.11 | all-reduce | flops 2048 | bytes 16384 | tf_op jit(solution)/shard_map/psum | solution.py:131
  93.0 3.3 %all-to-all-start.4 = ((f32[4,256,32]{1,2,0:T(8,128)}), f32[4,256,32]{1,2,0:T(8,128)S(1)}, u32[]{:S(2)}, u32[]{:S(2)}) async-start(f32[4,256,32]{1,2,0:T(8,128)} %copy.107), calls=%async_computation.4 | async-start | bytes 262144 | tf_op jit(solution)/shard_map/all_to_all | solution.py:150
  97.7 4.5 %all-to-all-done.4 = f32[4,256,32]{1,2,0:T(8,128)S(1)} async-done(((f32[4,256,32]{1,2,0:T(8,128)}), f32[4,256,32]{1,2,0:T(8,128)S(1)}, u32[]{:S(2)}, u32[]{:S(2)}) %all-to-all-start.4) | async-done | bytes 131104 | tf_op jit(solution)/shard_map/all_to_all | solution.py:150
  102.2 3.3 %all-to-all-start.3 = ((f32[4,256,32]{1,2,0:T(8,128)}), f32[4,256,32]{1,2,0:T(8,128)S(1)}, u32[]{:S(2)}, u32[]{:S(2)}) async-start(f32[4,256,32]{1,2,0:T(8,128)} %copy.101), calls=%async_computation.3 | async-start | bytes 262144 | tf_op jit(solution)/shard_map/all_to_all | solution.py:138
  106.8 4.6 %all-to-all-done.3 = f32[4,256,32]{1,2,0:T(8,128)S(1)} async-done(((f32[4,256,32]{1,2,0:T(8,128)}), f32[4,256,32]{1,2,0:T(8,128)S(1)}, u32[]{:S(2)}, u32[]{:S(2)}) %all-to-all-start.3) | async-done | bytes 131104 | tf_op jit(solution)/shard_map/all_to_all | solution.py:138
  114.2 22.3 %all-reduce.3.cloned.1.call-done = f32[2048,32]{0,1:T(8,128)} async-done(((f32[2048,32]{0,1:T(8,128)}), f32[2048,32]{0,1:T(8,128)}) %all-reduce.3.cloned.1.call-update) | async-done | bytes 262160 | tf_op jit(solution)/shard_map/psum | solution.py:159
  136.6 1.0 broadcast_multiply_fusion.1
  137.6 2.4 all_gather.10
  140.5 19.0 %psum.37 = f32[64,64]{0,1:T(8,128)S(1)} all-reduce(f32[64,64]{0,1:T(8,128)S(1)} %fusion.127), channel_id=1, replica_groups=mesh['groups'=2,'rows'=4,'tiles'=2,'cols'=2] {'rows'}, use_global_device_ids=true, to_apply=%region_12.13 | all-reduce | flops 4096 | bytes 32768 | tf_op jit(solution)/shard_map/psum | solution.py:43
  159.6 5.8 %cholesky.44 = f32[64,64]{1,0:T(8,128)S(1)} custom-call(f32[64,64]{1,0:T(8,128)S(1)} %fusion.80), custom_call_target="Cholesky" | custom-call | tf_op jit(solution)/shard_map/jit(cholesky)/cholesky | solution.py:14
  166.8 4.9 %custom-call.6 = f32[1,64,64]{1,2,0:T(8,128)S(1)} custom-call(f32[1,64,64]{2,1,0:T(8,128)S(1)} %fusion.75), custom_call_target="InvertDiagBlocksLowerTriangular" | custom-call | tf_op jit(solution)/shard_map/triangular_solve/custom-call.0 | solution.py:16
  174.0 3.3 %all-to-all-start.6 = ((f32[4,256,32]{1,2,0:T(8,128)}), f32[4,256,32]{1,2,0:T(8,128)S(1)}, u32[]{:S(2)}, u32[]{:S(2)}) async-start(f32[4,256,32]{1,2,0:T(8,128)} %copy.119), calls=%async_computation.6 | async-start | bytes 262144 | tf_op jit(solution)/shard_map/all_to_all | solution.py:150
  178.7 4.5 %all-to-all-done.6 = f32[4,256,32]{1,2,0:T(8,128)S(1)} async-done(((f32[4,256,32]{1,2,0:T(8,128)}), f32[4,256,32]{1,2,0:T(8,128)S(1)}, u32[]{:S(2)}, u32[]{:S(2)}) %all-to-all-start.6) | async-done | bytes 131104 | tf_op jit(solution)/shard_map/all_to_all | solution.py:150
  183.3 3.3 %all-to-all-start.5 = ((f32[4,256,32]{1,2,0:T(8,128)}), f32[4,256,32]{1,2,0:T(8,128)S(1)}, u32[]{:S(2)}, u32[]{:S(2)}) async-start(f32[4,256,32]{1,2,0:T(8,128)} %copy.113), calls=%async_computation.5 | async-start | bytes 262144 | tf_op jit(solution)/shard_map/all_to_all | solution.py:138
  187.8 4.7 %all-to-all-done.5 = f32[4,256,32]{1,2,0:T(8,128)S(1)} async-done(((f32[4,256,32]{1,2,0:T(8,128)}), f32[4,256,32]{1,2,0:T(8,128)S(1)}, u32[]{:S(2)}, u32[]{:S(2)}) %all-to-all-start.5) | async-done | bytes 131104 | tf_op jit(solution)/shard_map/all_to_all | solution.py:138
  195.3 21.4 %all-reduce.5.cloned.1.call-done = f32[2048,32]{0,1:T(8,128)} async-done(((f32[2048,32]{0,1:T(8,128)}), f32[2048,32]{0,1:T(8,128)}) %all-reduce.5.cloned.1.call-update) | async-done | bytes 262160 | tf_op jit(solution)/shard_map/psum | solution.py:159
  217.7 2.2 all_gather.11
  220.4 19.0 %psum.39 = f32[64,64]{0,1:T(8,128)S(1)} all-reduce(f32[64,64]{0,1:T(8,128)S(1)} %fusion.128), channel_id=1, replica_groups=mesh['groups'=2,'rows'=4,'tiles'=2,'cols'=2] {'rows'}, use_global_device_ids=true, to_apply=%region_16.19 | all-reduce | flops 4096 | bytes 32768 | tf_op jit(solution)/shard_map/psum | solution.py:43
  239.5 5.8 %cholesky.55 = f32[64,64]{1,0:T(8,128)S(1)} custom-call(f32[64,64]{1,0:T(8,128)S(1)} %fusion.78), custom_call_target="Cholesky" | custom-call | tf_op jit(solution)/shard_map/jit(cholesky)/cholesky | solution.py:14
  246.7 4.9 %custom-call.7 = f32[1,64,64]{1,2,0:T(8,128)S(1)} custom-call(f32[1,64,64]{2,1,0:T(8,128)S(1)} %fusion.76), custom_call_target="InvertDiagBlocksLowerTriangular" | custom-call | tf_op jit(solution)/shard_map/triangular_solve/custom-call.0 | solution.py:16
  251.9 1.1 fusion.81
  (100 shorter events, 25.7 us)
Async XLA Ops:
  7.2 17.1 %all-gather.2.cloned.1.call-start = ((), (), s32[]{:S(2)}) async-start(), calls=%async_computation.7 | async-start | bytes 4718592 | tf_op jit(solution)/shard_map/all_gather | solution.py:80
  28.0 6.6 %copy-start = (bf16[2048,768]{1,0:T(8,128)(2,1)S(1)}, bf16[2048,768]{1,0:T(8,128)(2,1)}, u32[]{:S(2)}) copy-start(bf16[2048,768]{1,0:T(8,128)(2,1)} %all-gather.2.cloned.1.call-done) | copy-start | bytes 9437188
  29.5 42.5 %all-to-all-start.1 = ((bf16[4,256,768]{2,1,0:T(8,128)(2,1)}), bf16[4,256,768]{2,1,0:T(8,128)(2,1)}, u32[]{:S(2)}, u32[]{:S(2)}) async-start(bf16[4,256,768]{2,1,0:T(8,128)(2,1)} %bitcast.158), calls=%async_computation.1 | async-start | bytes 3145728 | tf_op jit(solution)/shard_map/all_to_all | solution.py:84
  39.5 51.7 %copy-start.2 = (f32[2048,32]{0,1:T(8,128)S(1)}, f32[2048,32]{0,1:T(8,128)}, u32[]{:S(2)}) copy-start(f32[2048,32]{0,1:T(8,128)} %param.8) | copy-start | bytes 786436
  77.0 28.6 %copy-start.1 = (f32[8,128,128]{2,1,0:T(8,128)S(1)}, f32[8,128,128]{2,1,0:T(8,128)}, u32[]{:S(2)}) copy-start(f32[8,128,128]{2,1,0:T(8,128)} %get-tuple-element.15) | copy-start | bytes 1572868
  77.0 8.9 %all-to-all-start.2 = ((f32[4,1,256]{2,1,0:T(1,128)}), f32[4,1,256]{2,1,0:T(1,128)S(1)}, u32[]{:S(2)}, u32[]{:S(2)}) async-start(f32[4,1,256]{2,1,0:T(1,128)} %bitcast.10), calls=%async_computation.2 | async-start | bytes 8192 | tf_op jit(solution)/shard_map/all_to_all | solution.py:119
  91.2 15.3 %copy-start.3 = (f32[2048]{0:T(1024)}, f32[2048]{0:T(1024)S(1)}, u32[]{:S(2)}) copy-start(f32[2048]{0:T(1024)S(1)} %psum.35) | copy-start | bytes 24580
  93.0 9.2 %all-to-all-start.4 = ((f32[4,256,32]{1,2,0:T(8,128)}), f32[4,256,32]{1,2,0:T(8,128)S(1)}, u32[]{:S(2)}, u32[]{:S(2)}) async-start(f32[4,256,32]{1,2,0:T(8,128)} %copy.107), calls=%async_computation.4 | async-start | bytes 262144 | tf_op jit(solution)/shard_map/all_to_all | solution.py:150
  102.2 9.2 %all-to-all-start.3 = ((f32[4,256,32]{1,2,0:T(8,128)}), f32[4,256,32]{1,2,0:T(8,128)S(1)}, u32[]{:S(2)}, u32[]{:S(2)}) async-start(f32[4,256,32]{1,2,0:T(8,128)} %copy.101), calls=%async_computation.3 | async-start | bytes 262144 | tf_op jit(solution)/shard_map/all_to_all | solution.py:138
  105.6 31.0 %all-reduce.3.cloned.1.call-start = ((), (), s32[]{:S(2)}) async-start(), calls=%async_computation.8 | async-start | bytes 524288 | tf_op jit(solution)/shard_map/psum | solution.py:159
  174.0 9.2 %all-to-all-start.6 = ((f32[4,256,32]{1,2,0:T(8,128)}), f32[4,256,32]{1,2,0:T(8,128)S(1)}, u32[]{:S(2)}, u32[]{:S(2)}) async-start(f32[4,256,32]{1,2,0:T(8,128)} %copy.119), calls=%async_computation.6 | async-start | bytes 262144 | tf_op jit(solution)/shard_map/all_to_all | solution.py:150
  183.3 9.2 %all-to-all-start.5 = ((f32[4,256,32]{1,2,0:T(8,128)}), f32[4,256,32]{1,2,0:T(8,128)S(1)}, u32[]{:S(2)}, u32[]{:S(2)}) async-start(f32[4,256,32]{1,2,0:T(8,128)} %copy.113), calls=%async_computation.5 | async-start | bytes 262144 | tf_op jit(solution)/shard_map/all_to_all | solution.py:138
  186.6 30.1 %all-reduce.5.cloned.1.call-start = ((), (), s32[]{:S(2)}) async-start(), calls=%async_computation.9 | async-start | bytes 524288 | tf_op jit(solution)/shard_map/psum | solution.py:159
Sparse Core Ops, SparseCore 0:
  9.5 14.7 all-gather.1
  114.3 22.1 all-reduce.2
  195.4 21.2 all-reduce.4
where the time goes:
time: 261 us; the launch traced here: 260 us
  waiting for transfers between devices  101 us (39%)
  blocking collectives  59.2 us (23%)
  other arithmetic  31.4 us (12%)
  matrix products  22.4 us (9%)
  starting transfers between devices  21.8 us (8%)
  between operations  14.9 us (6%)
  local copies, waits for them, and re-layouts  8.85 us (3%)
    psum x2, waiting for transfers between devices, local(): mapped = lax.psum(partial_sum, 'tiles') * inv_root[:, None]  43.8 us
    psum x2, blocking collectives, orthonormal(): gram_matrix = lax.psum(gram_part, 'rows')  38 us
    all_to_all x1, waiting for transfers between devices, local(): lax.all_to_all(sent_rows, 'rows', split_axis=0, concat_axis=0, tiled=True)  32.5 us
    another operation x6, other arithmetic, upper_inverse(): lower = jnp.linalg.cholesky(gram_matrix)  13 us
    all_to_all x1, blocking collectives, local(): lax.all_to_all(far_block.reshape(row_count, capacity), 'rows', split_axis...  11.7 us
    another operation x4, other arithmetic, upper_inverse(): lax.linalg.triangular_solve(lower, identity, left_side=True, lower=True)  11.1 us
    all_to_all x2, waiting for transfers between devices, local(): lax.all_to_all(far_send, 'rows', split_axis=0, concat_axis=0, tiled=True)  9.31 us
    all_to_all x2, waiting for transfers between devices, local(): lax.all_to_all(far_out.reshape(row_count, capacity * BLOCK, own_cols), 'r...  9.05 us
  transfers between devices with their start and end apart: 9, of which 9 were waited for; matrix products, arithmetic and copies ran while one was open for 5% of the time, Pallas kernels for 0%

commit v1 on v0

v1 whole, which is shorter than its diff:
```python
import functools

import jax
import jax.numpy as jnp
from jax import lax
from jax.experimental import pallas as pl
from jax.experimental.pallas import tpu as pltpu
from jax.sharding import PartitionSpec as P

BLOCK = 128
kernel_gamma = 14.0

VMEM = pl.BlockSpec(memory_space=pltpu.VMEM)
SMEM = pl.BlockSpec(memory_space=pltpu.SMEM)
F32 = jnp.float32
BF16 = jnp.bfloat16
HIGHEST = lax.Precision.HIGHEST
NT = (((1,), (1,)), ((), ()))


def call(body, outs, args, smem_in=(), smem_out=(), cycles=1000):
    single = not isinstance(outs, (list, tuple))
    shapes = [outs] if single else list(outs)
    result = pl.pallas_call(
        body,
        out_shape=shapes,
        in_specs=[SMEM if i in smem_in else VMEM for i in range(len(args))],
        out_specs=[SMEM if i in smem_out else VMEM for i in range(len(shapes))],
        compiler_params=pltpu.CompilerParams(vmem_limit_bytes=48 * 2**20),
    )(*args)
    return result[0] if single else result


def sds(shape, dtype):
    return jax.ShapeDtypeStruct(shape, dtype)


def at_block(index):
    return pl.ds(pl.multiple_of(index * BLOCK, BLOCK), BLOCK)


def eye_mask(size):
    return lax.broadcasted_iota(jnp.int32, (size, size), 0) == lax.broadcasted_iota(
        jnp.int32, (size, size), 1
    )


def halves(value):
    high = value.astype(BF16)
    low = (value - high.astype(F32)).astype(BF16)
    return high, low


def pack(tile):
    return jnp.concatenate(halves(tile), axis=0)


def product(packed, values):
    left = jnp.concatenate(halves(values), axis=0)
    both = jnp.dot(jnp.concatenate([left, left], axis=1), packed, preferred_element_type=F32)
    count = values.shape[0]
    return both[:count] + both[count:]


def gram(full):
    high = full.astype(BF16)
    rest = full - high.astype(F32)
    middle = rest.astype(BF16)
    low = (rest - middle.astype(F32)).astype(BF16)
    parts = jnp.concatenate([high, middle, low], axis=0)
    cross = lax.dot_general(parts, parts, NT, preferred_element_type=F32)
    n = full.shape[0]
    total = None
    for i, j in ((2, 2), (1, 2), (2, 1), (0, 2), (2, 0), (1, 1), (0, 1), (1, 0), (0, 0)):
        piece = cross[i * n : (i + 1) * n, j * n : (j + 1) * n]
        total = piece if total is None else total + piece
    return total


def lower_inverse(matrix):
    n = matrix.shape[0]
    rows = lax.broadcasted_iota(jnp.int32, (n, 1), 0)
    state = jnp.concatenate([matrix, eye_mask(n).astype(F32)], axis=1)
    for j in range(n - 1):
        pivot_row = state[j : j + 1, :]
        scaled = pivot_row / state[j : j + 1, j : j + 1]
        column = jnp.where(rows > j, state[:, j : j + 1], 0.0)
        state = state - column * scaled
    pivots = jnp.sum(jnp.where(eye_mask(n), state[:, :n], 0.0), axis=1, keepdims=True)
    return state[:, n:] / jnp.sqrt(pivots)


def both_columns(core, own, other):
    first = core == 0
    return jnp.concatenate(
        [jnp.where(first, own, other), jnp.where(first, other, own)], axis=0
    )


def plan_body(dims, me, *refs):
    row_count, capacity, slots, blocks_here, list_rows = dims
    lists = refs[: len(list_rows)]
    emb = refs[len(list_rows)]
    idx = refs[len(list_rows) + 1]
    sends = refs[len(list_rows) + 2 :]
    row = me[0]

    def clear(i, carry):
        for line in range(6):
            idx[line, i] = 0
        return carry

    lax.fori_loop(0, slots, clear, 0)

    def ranked(ref, line, want, write):
        count = ref[line, 2 * slots]

        def step(s, counts):
            near = ref[line, s]
            far = ref[line, slots + s]
            owner = far // blocks_here
            live = s < count
            return write(s, near, far, owner, live, counts)

        lax.fori_loop(0, slots, step, (0,) * want)

    def write_own(s, near, far, owner, live, counts):
        shift = lax.rem(owner - row + row_count, row_count)
        rank = functools.reduce(
            lambda total, k: total + jnp.where(shift == k, counts[k], 0), range(row_count), 0
        )

        @pl.when(live)
        def _():
            slot = shift * capacity + rank
            idx[0, slot] = near - row * blocks_here
            idx[1, slot] = far
            idx[2, slot] = 1
            idx[3, slot] = s

        return tuple(
            counts[k] + (live & (shift == k)).astype(jnp.int32) for k in range(row_count)
        )

    for k in range(row_count):
        if len(lists) == 1:
            line = lax.rem(row - k + row_count, row_count) * list_rows[0][1] + me[1]
            ref = lists[0]
        else:
            line = 0
            ref = lists[k]
        if k == 0:
            ranked(ref, line, row_count, write_own)

        def write_in(s, near, far, owner, live, counts, k=k):
            hit = live & (owner == row)

            @pl.when(hit)
            def _():
                slot = k * capacity + counts[0]
                idx[4, slot] = far - row * blocks_here
                idx[5, slot] = near

            return (counts[0] + hit.astype(jnp.int32),)

        ranked(ref, line, 1, write_in)
    for k in range(1, row_count):
        for j in range(capacity):
            sends[k - 1][j * BLOCK : (j + 1) * BLOCK, :] = emb[at_block(idx[4, k * capacity + j]), :]


def partial_distance(left, right):
    inner = lax.dot_general(left, right, NT, preferred_element_type=F32)
    left_sq = jnp.sum(jnp.square(left.astype(F32)), axis=1, keepdims=True)
    right_sq = jnp.sum(jnp.square(right.astype(F32)), axis=1, keepdims=True)
    right_row = jnp.sum(jnp.where(eye_mask(BLOCK), right_sq, 0.0), axis=0, keepdims=True)
    return left_sq + right_row - 2.0 * inner


def self_distance_body(own_blocks, tile_count, me, emb, out):
    for i in range(own_blocks):
        block = emb[at_block(i * tile_count + me[1]), :]
        out[i * BLOCK : (i + 1) * BLOCK, :] = partial_distance(block, block)


def pair_distance_body(row_count, capacity, idx, emb, *refs):
    out = refs[-1]
    for k in range(row_count):
        for j in range(capacity):
            slot = k * capacity + j
            left = emb[at_block(idx[0, slot]), :]
            if k == 0:
                right = emb[at_block(idx[4, j]), :]
            else:
                right = refs[k - 1][j * BLOCK : (j + 1) * BLOCK, :]
            out[slot * BLOCK : (slot + 1) * BLOCK, :] = partial_distance(left, right)


def self_tile_body(own_blocks, mine, other, packed, sums):
    for i in range(own_blocks):
        part = slice(i * BLOCK, (i + 1) * BLOCK)
        tile = jnp.exp(-kernel_gamma * (mine[part, :] + other[part, :] - 2.0))
        tile = jnp.where(eye_mask(BLOCK), 0.0, tile)
        packed[i] = pack(tile)
        sums[i : i + 1, :] = jnp.sum(tile, axis=0, keepdims=True)


def pair_tile_body(row_count, capacity, per_core, slots, me, idx, mine, other, self_sums, near_tiles, home_tiles, *refs):
    sends = refs[:-1]
    sums = refs[-1]
    core = me[2]
    sums[0 : 2 * slots, :] = jnp.zeros((2 * slots, BLOCK), F32)
    sums[2 * slots :, :] = self_sums[...]
    for k in range(row_count):
        for j in range(capacity):
            slot = k * capacity + j
            part = slice(slot * BLOCK, (slot + 1) * BLOCK)
            live = idx[2, slot] > 0
            tile = jnp.exp(-kernel_gamma * (mine[part, :] + other[part, :] - 2.0))
            tile = jnp.where(live, tile, 0.0)
            turned = tile.T
            near_tiles[slot] = pack(turned)

            @pl.when(live)
            def _():
                raw = idx[3, slot]
                sums[pl.ds(raw, 1), :] = jnp.sum(turned, axis=0, keepdims=True)
                sums[pl.ds(slots + raw, 1), :] = jnp.sum(tile, axis=0, keepdims=True)

            if k == 0:
                home_tiles[j] = pack(tile)
            else:

                @pl.when(core == j // per_core)
                def _():
                    sends[k - 1][j % per_core] = pack(tile)


def pick_columns(idx, row_count, capacity, source, sends):
    for k in range(1, row_count):
        back = row_count - k
        for j in range(capacity):
            sends[k - 1][:, j * BLOCK : (j + 1) * BLOCK] = source[:, at_block(idx[0, k * capacity + j])]
            place = capacity + j
            sends[k - 1][:, place * BLOCK : (place + 1) * BLOCK] = source[
                :, at_block(idx[4, back * capacity + j])
            ]


def pick_body(row_count, capacity, idx, source, *sends):
    pick_columns(idx, row_count, capacity, source, sends)


def apply_tiles(dims, me, idx, inverse, own, received, near_tiles, home_tiles, sent, shared, self_tiles, out):
    row_count, capacity, per_core, blocks_here, tile_count = dims
    row, tile_index, core = me[0], me[1], me[2]
    out[...] = jnp.zeros(out.shape, F32)

    def scaled(values, block):
        return values * inverse[pl.ds(block, 1), :]

    def add(block, packed, values):
        place = at_block(block)
        out[:, place] = out[:, place] + product(packed, values)

    for i in range(blocks_here // tile_count):
        block = i * tile_count + tile_index
        add(block, self_tiles[i], scaled(own[:, at_block(block)], row * blocks_here + block))
    for k in range(row_count):
        for j in range(capacity):
            slot = k * capacity + j
            if k == 0:
                values = own[:, at_block(idx[4, j])]
            else:
                values = received[row_count - k - 1][:, (capacity + j) * BLOCK : (capacity + j + 1) * BLOCK]
            add(idx[0, slot], near_tiles[slot], scaled(values, idx[1, slot]))
    for k in range(row_count):
        for j in range(capacity):
            if k == 0:
                slot = j
                values = own[:, at_block(idx[0, j])]
                packed = home_tiles[j]
            else:
                inner = j % per_core
                if j < per_core:
                    place = core * per_core + inner
                    packed = sent[k - 1][inner]
                else:
                    place = (1 - core) * per_core + inner
                    packed = shared[k - 1][inner]
                slot = k * capacity + place
                values = received[k - 1][:, at_block(place)]
            add(idx[4, slot], packed, scaled(values, idx[5, slot]))


def first_apply_body(dims, sum_count, me, idx, onehot, *refs):
    row_count = dims[0]
    sums = refs[:sum_count]
    refs = refs[sum_count:]
    others = row_count - 1
    own = refs[0]
    received = refs[1 : 1 + others]
    near_tiles, home_tiles = refs[1 + others : 3 + others]
    sent = refs[3 + others : 3 + 2 * others]
    shared = refs[3 + 2 * others : 3 + 3 * others]
    self_tiles, out, degree, inverse = refs[3 + 3 * others :]
    if sum_count == 1:

        def step(i, total):
            return total + jnp.dot(onehot[i], sums[0][i], precision=HIGHEST, preferred_element_type=F32)

        total = lax.fori_loop(0, sums[0].shape[0], step, jnp.zeros(degree.shape, F32))
    else:
        total = None
        for i in range(sum_count):
            piece = jnp.dot(onehot[i], sums[i][...], precision=HIGHEST, preferred_element_type=F32)
            total = piece if total is None else total + piece
    degree[...] = total
    inverse[...] = 1.0 / jnp.sqrt(total)
    apply_tiles(dims, me, idx, inverse, own, received, near_tiles, home_tiles, sent, shared, self_tiles, out)


def second_apply_body(dims, me, idx, inverse, *refs):
    others = dims[0] - 1
    own = refs[0]
    received = refs[1 : 1 + others]
    near_tiles, home_tiles = refs[1 + others : 3 + others]
    sent = refs[3 + others : 3 + 2 * others]
    shared = refs[3 + 2 * others : 3 + 3 * others]
    self_tiles, out = refs[3 + 3 * others :]
    apply_tiles(dims, me, idx, inverse, own, received, near_tiles, home_tiles, sent, shared, self_tiles, out)


def scale_rows(me, blocks_here, inverse, mine, other, out):
    for b in range(blocks_here):
        part = slice(b * BLOCK, (b + 1) * BLOCK)
        row = inverse[pl.ds(me[0] * blocks_here + b, 1), :]
        out[:, part] = (mine[:, part] + other[:, part]) * row


def mapped_body(row_count, capacity, blocks_here, me, idx, inverse, mine, other, out, *sends):
    scale_rows(me, blocks_here, inverse, mine, other, out)
    pick_columns(idx, row_count, capacity, out, sends)


def last_mapped_body(blocks_here, me, inverse, mine, other, out):
    scale_rows(me, blocks_here, inverse, mine, other, out)


def gram_body(me, own, other, out):
    out[...] = gram(both_columns(me[2], own[...], other[...]))


def factor_body(*refs):
    total = refs[0][...]
    for ref in refs[1:-1]:
        total = total + ref[...]
    refs[-1][...] = lower_inverse(total)


def second_gram_body(me, factor, own, other, mapped, out):
    full = both_columns(me[2], own[...], other[...])
    value = jnp.dot(factor[...], full, precision=HIGHEST, preferred_element_type=F32)
    mapped[...] = value
    out[...] = gram(value)


def final_body(me, mapped, *refs):
    out = refs[-1]
    total = refs[0][...]
    for ref in refs[1:-1]:
        total = total + ref[...]
    factor = lower_inverse(total)
    own_cols = out.shape[0]
    part = jnp.where(me[2] == 0, factor[:own_cols], factor[own_cols:])
    out[...] = jnp.dot(part, mapped[...], precision=HIGHEST, preferred_element_type=F32)


def shift_by(value, axes, size, shift):
    return lax.ppermute(value, axes, [(i, (i + shift) % size) for i in range(size)])


def gather_all(value, axes, size):
    if size > 8:
        return [lax.all_gather(value, axes)]
    return [value] + [shift_by(value, axes, size, k) for k in range(1, size)]


def local(embeddings, start, pair_list, pair_count):
    row_count = lax.axis_size("rows")
    tile_count = lax.axis_size("tiles")
    core_count = lax.axis_size("cols")
    row_index = lax.axis_index("rows")
    tile_index = lax.axis_index("tiles")
    col_index = lax.axis_index("cols")
    me = jnp.stack([row_index, tile_index, col_index]).astype(jnp.int32)
    rows_here, half_features = embeddings.shape
    blocks_here = rows_here // BLOCK
    slots = pair_list.shape[2]
    capacity = slots // row_count
    per_core = capacity // core_count
    own_blocks = blocks_here // tile_count
    own_cols = start.shape[1]
    team = row_count * tile_count
    block_count = row_count * blocks_here
    others = range(1, row_count)

    lists = jnp.concatenate([pair_list.reshape(1, 2 * slots), pair_count.reshape(1, 1)], axis=1)
    lists = gather_all(lists, ("rows", "tiles"), team)
    if len(lists) == 1:
        all_lists = lists[0].reshape(team, 2 * slots + 1)
        plan_lists = [all_lists]
        list_rows = ((team, tile_count),)
        origin = jnp.arange(team, dtype=jnp.int32)
    else:
        all_lists = jnp.concatenate(lists, axis=0)
        plan_lists = [lists[k * tile_count] for k in range(row_count)]
        list_rows = ((1, 0),) * row_count
        origin = (row_index * tile_count + tile_index - jnp.arange(team, dtype=jnp.int32)) % team

    planned = call(
        functools.partial(plan_body, (row_count, capacity, slots, blocks_here, list_rows)),
        [sds((6, slots), jnp.int32)] + [sds((capacity * BLOCK, half_features), BF16) for _ in others],
        [me, *plan_lists, embeddings],
        smem_in=range(1 + len(plan_lists)),
        smem_out=(0,),
    )
    idx, sends = planned[0], planned[1:]
    far = [shift_by(sends[k - 1], "rows", row_count, -k) for k in others]

    self_part = call(
        functools.partial(self_distance_body, own_blocks, tile_count),
        sds((own_blocks * BLOCK, BLOCK), F32),
        [me, embeddings],
        smem_in=(0,),
    )
    self_other = shift_by(self_part, "cols", core_count, 1)
    self_tiles, self_sums = call(
        functools.partial(self_tile_body, own_blocks),
        [sds((own_blocks, 2 * BLOCK, BLOCK), BF16), sds((own_blocks, BLOCK), F32)],
        [self_part, self_other],
    )

    pair_part = call(
        functools.partial(pair_distance_body, row_count, capacity),
        sds((slots * BLOCK, BLOCK), F32),
        [idx, embeddings, *far],
        smem_in=(0,),
    )
    pair_other = shift_by(pair_part, "cols", core_count, 1)

    values = start.T
    start_sends = call(
        functools.partial(pick_body, row_count, capacity),
        [sds((own_cols, 2 * capacity * BLOCK), F32) for _ in others],
        [idx, values],
        smem_in=(0,),
    )
    start_in = [shift_by(start_sends[k - 1], "rows", row_count, k) for k in others]

    tiles = call(
        functools.partial(pair_tile_body, row_count, capacity, per_core, slots),
        [sds((slots, 2 * BLOCK, BLOCK), BF16), sds((capacity, 2 * BLOCK, BLOCK), BF16)]
        + [sds((per_core, 2 * BLOCK, BLOCK), BF16) for _ in others]
        + [sds((2 * slots + own_blocks, BLOCK), F32)],
        [me, idx, pair_part, pair_other, self_sums],
        smem_in=(0, 1),
    )
    near_tiles, home_tiles, tile_sends, sums = tiles[0], tiles[1], tiles[2:-1], tiles[-1]
    all_sums = gather_all(sums, ("rows", "tiles"), team)
    sent = [shift_by(tile_sends[k - 1], "rows", row_count, k) for k in others]
    shared = [shift_by(tile, "cols", core_count, 1) for tile in sent]

    diagonal_ids = origin[:, None] // tile_count * blocks_here + (
        jnp.arange(own_blocks, dtype=jnp.int32)[None, :] * tile_count + origin[:, None] % tile_count
    )
    sum_ids = jnp.concatenate([all_lists[:, : 2 * slots], diagonal_ids], axis=1)
    onehot = (
        sum_ids[:, None, :] == jnp.arange(block_count, dtype=jnp.int32)[None, :, None]
    ).astype(F32)

    dims = (row_count, capacity, per_core, blocks_here, tile_count)
    tile_args = [near_tiles, home_tiles, *sent, *shared, self_tiles]
    block_shape = sds((own_cols, rows_here), F32)
    table = sds((block_count, BLOCK), F32)

    def team_sum(part):
        if tile_count == 2:
            return part, shift_by(part, "tiles", 2, 1)
        return lax.psum(part, "tiles"), jnp.zeros_like(part)

    part, degree, inverse = call(
        functools.partial(first_apply_body, dims, len(all_sums)),
        [block_shape, table, table],
        [me, idx, onehot, *all_sums, values, *start_in, *tile_args],
        smem_in=(0, 1),
    )
    mine, other = team_sum(part)
    first = call(
        functools.partial(mapped_body, row_count, capacity, blocks_here),
        [block_shape] + [sds((own_cols, 2 * capacity * BLOCK), F32) for _ in others],
        [me, idx, inverse, mine, other],
        smem_in=(0, 1),
    )
    mapped, sends = first[0], first[1:]
    received = [shift_by(sends[k - 1], "rows", row_count, k) for k in others]

    mapped_other = shift_by(mapped, "cols", core_count, 1)
    square = sds((2 * own_cols, 2 * own_cols), F32)
    first_gram = call(gram_body, square, [me, mapped, mapped_other], smem_in=(0,))
    grams = [first_gram] + [shift_by(first_gram, "rows", row_count, k) for k in others]
    factor = call(factor_body, square, grams)

    part = call(
        functools.partial(second_apply_body, dims),
        block_shape,
        [me, idx, inverse, mapped, *received, *tile_args],
        smem_in=(0, 1),
    )
    mine, other = team_sum(part)
    second = call(
        functools.partial(last_mapped_body, blocks_here),
        block_shape,
        [me, inverse, mine, other],
        smem_in=(0,),
    )
    second_other = shift_by(second, "cols", core_count, 1)
    full, second_gram = call(
        second_gram_body,
        [sds((2 * own_cols, rows_here), F32), square],
        [me, factor, second, second_other],
        smem_in=(0,),
    )
    grams = [second_gram] + [shift_by(second_gram, "rows", row_count, k) for k in others]
    vectors = call(final_body, block_shape, [me, full, *grams], smem_in=(0,))
    own_degree = lax.dynamic_slice_in_dim(degree, row_index * blocks_here, blocks_here, 0)
    return (vectors.T, own_degree.reshape(rows_here))


def solution(mesh):
    in_specs = (
        P(("groups", "rows"), "cols"),
        P(("groups", "rows"), "cols"),
        P(("groups", "rows", "tiles"), None, None),
        P(("groups", "rows", "tiles")),
    )
    out_specs = (P(("groups", "rows"), "cols"), P(("groups", "rows")))
    return jax.shard_map(local, mesh=mesh, in_specs=in_specs, out_specs=out_specs, check_vma=False)
```

time: 261 us -> 126 us (0.48)
  waiting for transfers between devices: 101 us -> 39.5 us
  blocking collectives: 59.2 us -> 0 us
  starting transfers between devices: 21.8 us -> 56.2 us
  other arithmetic: 31.4 us -> 0.34 us
  Pallas kernels: 0 us -> 25.4 us
  matrix products: 22.4 us -> 0 us
  between operations: 14.9 us -> 1.49 us
  local copies, waits for them, and re-layouts: 8.85 us -> 2.8 us
    ppermute x0 -> x41, starting transfers between devices: none -> 56.2 us  [shift_by(): lax.ppermute(value, axes, [(i, (i + shift) % size) for i in range(size)])]
    all_to_all x6 -> x0, waiting for transfers between devices: 56.2 us -> none  [the longest x1 32.5 us: local(): lax.all_to_all(sent_rows, 'rows', split_axis=0, concat_axis=0, tiled=True)]
    psum x2 -> x0, waiting for transfers between devices: 43.8 us -> none  [local(): mapped = lax.psum(partial_sum, 'tiles') * inv_root[:, None]]
    psum x3 -> x0, blocking collectives: 43 us -> none  [the longest x2 38 us: orthonormal(): gram_matrix = lax.psum(gram_part, 'rows')]
    ppermute x0 -> x41, waiting for transfers between devices: none -> 39.5 us  [shift_by(): lax.ppermute(value, axes, [(i, (i + shift) % size) for i in range(size)])]
    pallas_call x0 -> x14, Pallas kernels: none -> 25.4 us  [call(): pl.pallas_call(body, out_shape=shapes, in_specs=[SMEM if i in smem_in els...]
    another operation x10 -> x1, other arithmetic: 24.1 us -> 0.08 us  [local(): me = jnp.stack([row_index, tile_index, col_index]).astype(jnp.int32)]
    dot_general x24 -> x0, matrix products: 21.9 us -> none  [the longest x2 6.74 us: pick_blocks(): jnp.einsum('sb,bak->sak', selector.astype(jnp.bfloat16), source, preferre...]
  transfers between devices with their start and end apart: 9 -> 41, of which waited for: 9 -> 16; matrix products, arithmetic and copies ran while one was open for 5% -> 1% of each run, Pallas kernels for 0% -> 9%
where the time goes in v1:
time: 126 us
  starting transfers between devices  56.2 us (45%)
  waiting for transfers between devices  39.5 us (31%)
  Pallas kernels  25.4 us (20%)
  local copies, waits for them, and re-layouts  2.8 us (2%)
  between operations  1.49 us (1%)
    ppermute x41, starting transfers between devices, shift_by(): lax.ppermute(value, axes, [(i, (i + shift) % size) for i in range(size)])  56.2 us
    ppermute x41, waiting for transfers between devices, shift_by(): lax.ppermute(value, axes, [(i, (i + shift) % size) for i in range(size)])  39.5 us
    pallas_call x14, Pallas kernels, call(): pl.pallas_call(body, out_shape=shapes, in_specs=[SMEM if i in smem_in els...  25.4 us
  transfers between devices with their start and end apart: 41, of which 16 were waited for; matrix products, arithmetic and copies ran while one was open for 1% of the time, Pallas kernels for 9%

profile of v1, /device:TPU:0, one launch (start us, length us, event | category | flops | bytes accessed | tf_op | source)
XLA Modules:
  0.0 125.8 jit_solution(3142644546838177467)
XLA Ops:
  2.1 3.0 %collective-permute-start = (s32[1,17]{1,0:T(1,128)S(1)}, s32[1,17]{1,0:T(1,128)S(1)}, u32[]{:S(2)}, u32[]{:S(2)}) collective-permute-start(s32[1,17]{1,0:T(1,128)S(1)} %pad_add_fusion.2.refs_0_), channel_id=1, source_target_pairs={{0,4},{2,6},{4,8},{6,10},{8,12},{10,14},{12,0},{14,2},{1,5},{3,7},... | collective-permute-start | bytes 212 | tf_op jit(solution)/shard_map/ppermute | solution.py:380
  5.1 2.6 %collective-permute-start.1 = (s32[1,17]{1,0:T(1,128)S(1)}, s32[1,17]{1,0:T(1,128)S(1)}, u32[]{:S(2)}, u32[]{:S(2)}) collective-permute-start(s32[1,17]{1,0:T(1,128)S(1)} %pad_add_fusion.2.refs_0_), channel_id=1, source_target_pairs={{0,8},{2,10},{4,12},{6,14},{8,0},{10,2},{12,4},{14,6},{1,9},{3,11}... | collective-permute-start | bytes 212 | tf_op jit(solution)/shard_map/ppermute | solution.py:380
  9.6 1.7 %collective-permute-done.2.refs_3_ = s32[1,17]{1,0:T(1,128)S(1)} collective-permute-done((s32[1,17]{1,0:T(1,128)S(1)}, s32[1,17]{1,0:T(1,128)S(1)}, u32[]{:S(2)}, u32[]{:S(2)}) %collective-permute-start.2) | collective-permute-done | bytes 100 | tf_op jit(solution)/shard_map/ppermute | solution.py:380
  12.7 2.0 %shard_map.59 = (s32[6,8]{1,0:T(8,128)S(1)}, bf16[256,384]{1,0:T(8,128)(2,1)S(1)}, bf16[256,384]{1,0:T(8,128)(2,1)S(1)}, bf16[256,384]{1,0:T(8,128)(2,1)S(1)}) custom-call(s32[3]{0:T(128)S(1)} %pad_add_fusion.1.me, s32[1,17]{1,0:T(1,128)S(1)} %pad_add_fusion.2.refs_0_, s32[1,17]{1,0:T(1,128)S(1)} %collective-permute-done.refs_1_, ...), custom_call_target="tpu_custom_call" | custom-call | tf_op jit(solution)/shard_map/pallas_call | solution.py:24
  14.7 3.2 %collective-permute-start.7 = (bf16[256,384]{1,0:T(8,128)(2,1)S(1)}, bf16[256,384]{1,0:T(8,128)(2,1)S(1)}, u32[]{:S(2)}, u32[]{:S(2)}) collective-permute-start(bf16[256,384]{1,0:T(8,128)(2,1)S(1)} %get-tuple-element.27), channel_id=1, source_target_pairs={{0,12},{4,0},{8,4},{12,8},{1,13},{5,1},{9,5},{13,9},{2,14},{6,2},{... | collective-permute-start | bytes 589832 | tf_op jit(solution)/shard_map/ppermute | solution.py:380
  19.6 3.6 %collective-permute-done.7.refs_0_ = bf16[256,384]{1,0:T(8,128)(2,1)S(1)} collective-permute-done((bf16[256,384]{1,0:T(8,128)(2,1)S(1)}, bf16[256,384]{1,0:T(8,128)(2,1)S(1)}, u32[]{:S(2)}, u32[]{:S(2)}) %collective-permute-start.7) | collective-permute-done | bytes 196640 | tf_op jit(solution)/shard_map/ppermute | solution.py:380
  23.3 9.3 %collective-permute-done.8.refs_1_ = bf16[256,384]{1,0:T(8,128)(2,1)S(1)} collective-permute-done((bf16[256,384]{1,0:T(8,128)(2,1)S(1)}, bf16[256,384]{1,0:T(8,128)(2,1)S(1)}, u32[]{:S(2)}, u32[]{:S(2)}) %collective-permute-start.8) | collective-permute-done | bytes 196640 | tf_op jit(solution)/shard_map/ppermute | solution.py:380
  33.8 1.7 %collective-permute-start.3 = (s32[1,17]{1,0:T(1,128)S(1)}, s32[1,17]{1,0:T(1,128)S(1)}, u32[]{:S(2)}, u32[]{:S(2)}) collective-permute-start(s32[1,17]{1,0:T(1,128)S(1)} %pad_add_fusion.2.refs_0_), channel_id=1, source_target_pairs={{0,2},{2,4},{4,6},{6,8},{8,10},{10,12},{12,14},{14,0},{1,3},{3,5},... | collective-permute-start | bytes 212 | tf_op jit(solution)/shard_map/ppermute | solution.py:380
  35.5 2.9 %collective-permute-start.4 = (s32[1,17]{1,0:T(1,128)S(1)}, s32[1,17]{1,0:T(1,128)S(1)}, u32[]{:S(2)}, u32[]{:S(2)}) collective-permute-start(s32[1,17]{1,0:T(1,128)S(1)} %pad_add_fusion.2.refs_0_), channel_id=1, source_target_pairs={{0,6},{2,8},{4,10},{6,12},{8,14},{10,0},{12,2},{14,4},{1,7},{3,9},... | collective-permute-start | bytes 212 | tf_op jit(solution)/shard_map/ppermute | solution.py:380
  39.2 1.8 %collective-permute-start.5 = (s32[1,17]{1,0:T(1,128)S(1)}, s32[1,17]{1,0:T(1,128)S(1)}, u32[]{:S(2)}, u32[]{:S(2)}) collective-permute-start(s32[1,17]{1,0:T(1,128)S(1)} %pad_add_fusion.2.refs_0_), channel_id=1, source_target_pairs={{0,10},{2,12},{4,14},{6,0},{8,2},{10,4},{12,6},{14,8},{1,11},{3,13... | collective-permute-start | bytes 212 | tf_op jit(solution)/shard_map/ppermute | solution.py:380
  41.2 2.9 %collective-permute-start.6 = (s32[1,17]{1,0:T(1,128)S(1)}, s32[1,17]{1,0:T(1,128)S(1)}, u32[]{:S(2)}, u32[]{:S(2)}) collective-permute-start(s32[1,17]{1,0:T(1,128)S(1)} %pad_add_fusion.2.refs_0_), channel_id=1, source_target_pairs={{0,14},{2,0},{4,2},{6,4},{8,6},{10,8},{12,10},{14,12},{1,15},{3,1}... | collective-permute-start | bytes 212 | tf_op jit(solution)/shard_map/ppermute | solution.py:380
  44.1 1.6 %shard_map.63 = (bf16[8,256,128]{2,1,0:T(8,128)(2,1)S(1)}, bf16[2,256,128]{2,1,0:T(8,128)(2,1)S(1)}, bf16[1,256,128]{2,1,0:T(8,128)(2,1)S(1)}, bf16[1,256,128]{2...) custom-call(s32[3]{0:T(128)S(1)} %pad_add_fusion.1.me, ...), custom_call_target="tpu_custom_call" | custom-call | tf_op jit(solution)/shard_map/pallas_call | solution.py:24
  45.8 4.3 %collective-permute-start.21 = (f32[32,512]{1,0:T(8,128)S(1)}, f32[32,512]{1,0:T(8,128)S(1)}, u32[]{:S(2)}, u32[]{:S(2)}) collective-permute-start(f32[32,512]{1,0:T(8,128)S(1)} %get-tuple-element.34), channel_id=1, source_target_pairs={{0,12},{4,0},{8,4},{12,8},{1,13},{5,1},{9,5},{13,9},{2,14},{6,2},{... | collective-permute-start | bytes 196616 | tf_op jit(solution)/shard_map/ppermute | solution.py:380
  50.7 1.5 %collective-permute-start.14 = (f32[24,128]{1,0:T(8,128)S(1)}, f32[24,128]{1,0:T(8,128)S(1)}, u32[]{:S(2)}, u32[]{:S(2)}) collective-permute-start(f32[24,128]{1,0:T(8,128)S(1)} %get-tuple-element.31.refs_0_), channel_id=1, source_target_pairs={{0,6},{2,8},{4,10},{6,12},{8,14},{10,0},{12,2},{14,4},{1,7},{3,9},... | collective-permute-start | bytes 36872 | tf_op jit(solution)/shard_map/ppermute | solution.py:380
  52.3 3.3 %collective-permute-start.15 = (f32[24,128]{1,0:T(8,128)S(1)}, f32[24,128]{1,0:T(8,128)S(1)}, u32[]{:S(2)}, u32[]{:S(2)}) collective-permute-start(f32[24,128]{1,0:T(8,128)S(1)} %get-tuple-element.31.refs_0_), channel_id=1, source_target_pairs={{0,8},{2,10},{4,12},{6,14},{8,0},{10,2},{12,4},{14,6},{1,9},{3,11}... | collective-permute-start | bytes 36872 | tf_op jit(solution)/shard_map/ppermute | solution.py:380
  56.5 2.6 %collective-permute-start.22 = (bf16[1,256,128]{2,1,0:T(8,128)(2,1)S(1)}, bf16[1,256,128]{2,1,0:T(8,128)(2,1)S(1)}, u32[]{:S(2)}, u32[]{:S(2)}) collective-permute-start(bf16[1,256,128]{2,1,0:T(8,128)(2,1)S(1)} %get-tuple-element.37), channel_id=1, source_target_pairs={{0,4},{4,8},{8,12},{12,0},{1,5},{5,9},{9,13},{13,1},{2,6},{6,10},{... | collective-permute-start | bytes 196616 | tf_op jit(solution)/shard_map/ppermute | solution.py:380
  59.2 2.4 %collective-permute-start.24 = (bf16[1,256,128]{2,1,0:T(8,128)(2,1)S(1)}, bf16[1,256,128]{2,1,0:T(8,128)(2,1)S(1)}, u32[]{:S(2)}, u32[]{:S(2)}) collective-permute-start(bf16[1,256,128]{2,1,0:T(8,128)(2,1)S(1)} %get-tuple-element.39), channel_id=1, source_target_pairs={{0,12},{4,0},{8,4},{12,8},{1,13},{5,1},{9,5},{13,9},{2,14},{6,2},{... | collective-permute-start | bytes 196616 | tf_op jit(solution)/shard_map/ppermute | solution.py:380
  61.6 2.0 %collective-permute-start.17 = (f32[24,128]{1,0:T(8,128)S(1)}, f32[24,128]{1,0:T(8,128)S(1)}, u32[]{:S(2)}, u32[]{:S(2)}) collective-permute-start(f32[24,128]{1,0:T(8,128)S(1)} %get-tuple-element.31.refs_0_), channel_id=1, source_target_pairs={{0,12},{2,14},{4,0},{6,2},{8,4},{10,6},{12,8},{14,10},{1,13},{3,15... | collective-permute-start | bytes 36872 | tf_op jit(solution)/shard_map/ppermute | solution.py:380
  63.6 3.2 %collective-permute-start.18 = (f32[24,128]{1,0:T(8,128)S(1)}, f32[24,128]{1,0:T(8,128)S(1)}, u32[]{:S(2)}, u32[]{:S(2)}) collective-permute-start(f32[24,128]{1,0:T(8,128)S(1)} %get-tuple-element.31.refs_0_), channel_id=1, source_target_pairs={{0,14},{2,0},{4,2},{6,4},{8,6},{10,8},{12,10},{14,12},{1,15},{3,1}... | collective-permute-start | bytes 36872 | tf_op jit(solution)/shard_map/ppermute | solution.py:380
  68.6 1.7 %shard_map.65 = (f32[32,2048]{1,0:T(8,128)S(1)}, f32[64,128]{1,0:T(8,128)S(1)}, f32[64,128]{1,0:T(8,128)S(1)}) custom-call(s32[3]{0:T(128)S(1)} %pad_add_fusion.1.me, s32[6,8]{1,0:T(8,128)S(1)} %get-tuple-element.26.idx, f32[8,64,24]{2,1,0:T(8,128)S(1)} %fusion.onehot, f32[24,128]{1,0:T(8,128)S(1)} %get-tuple-element.31.refs_0_, ...), custom_call_target="tpu_custom_call" | custom-call | tf_op jit(solution)/shard_map/pallas_call | solution.py:24
  70.9 7.8 %collective-permute-done.28.other = f32[32,2048]{1,0:T(8,128)S(1)} collective-permute-done((f32[32,2048]{1,0:T(8,128)S(1)}, f32[32,2048]{1,0:T(8,128)S(1)}, u32[]{:S(2)}, u32[]{:S(2)}) %collective-permute-start.28) | collective-permute-done | bytes 262176 | tf_op jit(solution)/shard_map/ppermute | solution.py:380
  79.4 1.8 %collective-permute-start.34 = (f32[32,512]{1,0:T(8,128)S(1)}, f32[32,512]{1,0:T(8,128)S(1)}, u32[]{:S(2)}, u32[]{:S(2)}) collective-permute-start(f32[32,512]{1,0:T(8,128)S(1)} %get-tuple-element.45), channel_id=1, source_target_pairs={{0,8},{4,12},{8,0},{12,4},{1,9},{5,13},{9,1},{13,5},{2,10},{6,14},... | collective-permute-start | bytes 196616 | tf_op jit(solution)/shard_map/ppermute | solution.py:380
  81.2 2.1 %collective-permute-start.35 = (f32[32,512]{1,0:T(8,128)S(1)}, f32[32,512]{1,0:T(8,128)S(1)}, u32[]{:S(2)}, u32[]{:S(2)}) collective-permute-start(f32[32,512]{1,0:T(8,128)S(1)} %get-tuple-element.46), channel_id=1, source_target_pairs={{0,12},{4,0},{8,4},{12,8},{1,13},{5,1},{9,5},{13,9},{2,14},{6,2},{... | collective-permute-start | bytes 196616 | tf_op jit(solution)/shard_map/ppermute | solution.py:380
  83.3 2.7 %collective-permute-done.33.refs_1_ = f32[32,512]{1,0:T(8,128)S(1)} collective-permute-done((f32[32,512]{1,0:T(8,128)S(1)}, f32[32,512]{1,0:T(8,128)S(1)}, u32[]{:S(2)}, u32[]{:S(2)}) %collective-permute-start.33) | collective-permute-done | bytes 65568 | tf_op jit(solution)/shard_map/ppermute | solution.py:380
  89.1 5.6 %collective-permute-done.36.other = f32[32,2048]{1,0:T(8,128)S(1)} collective-permute-done((f32[32,2048]{1,0:T(8,128)S(1)}, f32[32,2048]{1,0:T(8,128)S(1)}, u32[]{:S(2)}, u32[]{:S(2)}) %collective-permute-start.36) | collective-permute-done | bytes 262176 | tf_op jit(solution)/shard_map/ppermute | solution.py:380
  96.4 2.7 %collective-permute-start.30 = (f32[64,64]{1,0:T(8,128)S(1)}, f32[64,64]{1,0:T(8,128)S(1)}, u32[]{:S(2)}, u32[]{:S(2)}) collective-permute-start(f32[64,64]{1,0:T(8,128)S(1)} %shard_map.67.refs_0_), channel_id=1, source_target_pairs={{0,4},{4,8},{8,12},{12,0},{1,5},{5,9},{9,13},{13,1},{2,6},{6,10},{... | collective-permute-start | bytes 49160 | tf_op jit(solution)/shard_map/ppermute | solution.py:380
  99.4 2.2 %collective-permute-start.32 = (f32[64,64]{1,0:T(8,128)S(1)}, f32[64,64]{1,0:T(8,128)S(1)}, u32[]{:S(2)}, u32[]{:S(2)}) collective-permute-start(f32[64,64]{1,0:T(8,128)S(1)} %shard_map.67.refs_0_), channel_id=1, source_target_pairs={{0,12},{4,0},{8,4},{12,8},{1,13},{5,1},{9,5},{13,9},{2,14},{6,2},{... | collective-permute-start | bytes 49160 | tf_op jit(solution)/shard_map/ppermute | solution.py:380
  102.2 2.1 %collective-permute-done.31.refs_2_ = f32[64,64]{1,0:T(8,128)S(1)} collective-permute-done((f32[64,64]{1,0:T(8,128)S(1)}, f32[64,64]{1,0:T(8,128)S(1)}, u32[]{:S(2)}, u32[]{:S(2)}) %collective-permute-start.31) | collective-permute-done | bytes 16416 | tf_op jit(solution)/shard_map/ppermute | solution.py:380
  104.3 5.4 %shard_map.68.factor = f32[64,64]{1,0:T(8,128)S(1)} custom-call(f32[64,64]{1,0:T(8,128)S(1)} %shard_map.67.refs_0_, f32[64,64]{1,0:T(8,128)S(1)} %collective-permute-done.30.refs_1_, f32[64,64]{1,0:T(8,128)S(1)} %collective-permute-done.31.refs_2_, f32[64,64]{1,0:T(8,128)S(1)} %collective-permute-done.32.refs_3_), custom_call_target="tpu_custom_call" | custom-call | tf_op jit(solution)/shard_map/pallas_call | solution.py:24
  109.7 1.5 %shard_map.71 = (f32[64,2048]{1,0:T(8,128)S(1)}, f32[64,64]{1,0:T(8,128)S(1)}) custom-call(s32[3]{0:T(128)S(1)} %pad_add_fusion.1.me, f32[64,64]{1,0:T(8,128)S(1)} %shard_map.68.factor, f32[32,2048]{1,0:T(8,128)S(1)} %shard_map.70.own, f32[32,2048]{1,0:T(8,128)S(1)} %collective-permute-done.37.other), custom_call_target="tpu_custom_call" | custom-call | tf_op jit(solution)/shard_map/pallas_call | solution.py:24
  112.3 2.5 %collective-permute-start.39 = (f32[64,64]{1,0:T(8,128)S(1)}, f32[64,64]{1,0:T(8,128)S(1)}, u32[]{:S(2)}, u32[]{:S(2)}) collective-permute-start(f32[64,64]{1,0:T(8,128)S(1)} %get-tuple-element.48.refs_0_), channel_id=1, source_target_pairs={{0,8},{4,12},{8,0},{12,4},{1,9},{5,13},{9,1},{13,5},{2,10},{6,14},... | collective-permute-start | bytes 49160 | tf_op jit(solution)/shard_map/ppermute | solution.py:380
  118.7 7.0 %shard_map.72 = f32[32,2048]{1,0:T(8,128)} custom-call(s32[3]{0:T(128)S(1)} %pad_add_fusion.1.me, f32[64,2048]{1,0:T(8,128)S(1)} %get-tuple-element.47.mapped, f32[64,64]{1,0:T(8,128)S(1)} %get-tuple-element.48.refs_0_, f32[64,64]{1,0:T(8,128)S(1)} %collective-permute-done.38.refs_1_, f32[64,64]{1,0:T(8,128)S(1)} %collective-permute-done.39.refs_2_, ...), custom_call_target="tpu_custom_call" | custom-call | tf_op jit(solution)/shard_map/pallas_call | solution.py:24
  (80 shorter events, 23.7 us)
Async XLA Ops:
  2.1 7.0 %collective-permute-start = (s32[1,17]{1,0:T(1,128)S(1)}, s32[1,17]{1,0:T(1,128)S(1)}, u32[]{:S(2)}, u32[]{:S(2)}) collective-permute-start(s32[1,17]{1,0:T(1,128)S(1)} %pad_add_fusion.2.refs_0_), channel_id=1, source_target_pairs={{0,4},{2,6},{4,8},{6,10},{8,12},{10,14},{12,0},{14,2},{1,5},{3,7},... | collective-permute-start | bytes 212 | tf_op jit(solution)/shard_map/ppermute | solution.py:380
  14.7 8.6 %collective-permute-start.7 = (bf16[256,384]{1,0:T(8,128)(2,1)S(1)}, bf16[256,384]{1,0:T(8,128)(2,1)S(1)}, u32[]{:S(2)}, u32[]{:S(2)}) collective-permute-start(bf16[256,384]{1,0:T(8,128)(2,1)S(1)} %get-tuple-element.27), channel_id=1, source_target_pairs={{0,12},{4,0},{8,4},{12,8},{1,13},{5,1},{9,5},{13,9},{2,14},{6,2},{... | collective-permute-start | bytes 589832 | tf_op jit(solution)/shard_map/ppermute | solution.py:380
  17.9 14.7 %collective-permute-start.8 = (bf16[256,384]{1,0:T(8,128)(2,1)S(1)}, bf16[256,384]{1,0:T(8,128)(2,1)S(1)}, u32[]{:S(2)}, u32[]{:S(2)}) collective-permute-start(bf16[256,384]{1,0:T(8,128)(2,1)S(1)} %get-tuple-element.28), channel_id=1, source_target_pairs={{0,8},{4,12},{8,0},{12,4},{1,9},{5,13},{9,1},{13,5},{2,10},{6,14},... | collective-permute-start | bytes 589832 | tf_op jit(solution)/shard_map/ppermute | solution.py:380
  17.9 14.7 %collective-permute-start.9 = (bf16[256,384]{1,0:T(8,128)(2,1)S(1)}, bf16[256,384]{1,0:T(8,128)(2,1)S(1)}, u32[]{:S(2)}, u32[]{:S(2)}) collective-permute-start(bf16[256,384]{1,0:T(8,128)(2,1)S(1)} %get-tuple-element.29), channel_id=1, source_target_pairs={{0,4},{4,8},{8,12},{12,0},{1,5},{5,9},{9,13},{13,1},{2,6},{6,10},{... | collective-permute-start | bytes 589832 | tf_op jit(solution)/shard_map/ppermute | solution.py:380
  19.6 19.7 %collective-permute-start.11 = (f32[1024,128]{1,0:T(8,128)S(1)}, f32[1024,128]{1,0:T(8,128)S(1)}, u32[]{:S(2)}, u32[]{:S(2)}) collective-permute-start(f32[1024,128]{1,0:T(8,128)S(1)} %shard_map.61.mine), channel_id=1, source_target_pairs={{0,1},{1,0},{2,3},{3,2},{4,5},{5,4},{6,7},{7,6},{8,9},{9,8},{10,11... | collective-permute-start | bytes 1572872 | tf_op jit(solution)/shard_map/ppermute | solution.py:380
  33.7 7.5 %collective-permute-start.10 = (f32[1024,128]{1,0:T(8,128)S(1)}, f32[1024,128]{1,0:T(8,128)S(1)}, u32[]{:S(2)}, u32[]{:S(2)}) collective-permute-start(f32[1024,128]{1,0:T(8,128)S(1)} %shard_map.60.mine), channel_id=1, source_target_pairs={{0,1},{1,0},{2,3},{3,2},{4,5},{5,4},{6,7},{7,6},{8,9},{9,8},{10,11... | collective-permute-start | bytes 1572872 | tf_op jit(solution)/shard_map/ppermute | solution.py:380
  33.8 11.9 %collective-permute-start.3 = (s32[1,17]{1,0:T(1,128)S(1)}, s32[1,17]{1,0:T(1,128)S(1)}, u32[]{:S(2)}, u32[]{:S(2)}) collective-permute-start(s32[1,17]{1,0:T(1,128)S(1)} %pad_add_fusion.2.refs_0_), channel_id=1, source_target_pairs={{0,2},{2,4},{4,6},{6,8},{8,10},{10,12},{12,14},{14,0},{1,3},{3,5},... | collective-permute-start | bytes 212 | tf_op jit(solution)/shard_map/ppermute | solution.py:380
  35.5 10.3 %collective-permute-start.4 = (s32[1,17]{1,0:T(1,128)S(1)}, s32[1,17]{1,0:T(1,128)S(1)}, u32[]{:S(2)}, u32[]{:S(2)}) collective-permute-start(s32[1,17]{1,0:T(1,128)S(1)} %pad_add_fusion.2.refs_0_), channel_id=1, source_target_pairs={{0,6},{2,8},{4,10},{6,12},{8,14},{10,0},{12,2},{14,4},{1,7},{3,9},... | collective-permute-start | bytes 212 | tf_op jit(solution)/shard_map/ppermute | solution.py:380
  39.0 11.7 %collective-permute-start.19 = (f32[32,512]{1,0:T(8,128)S(1)}, f32[32,512]{1,0:T(8,128)S(1)}, u32[]{:S(2)}, u32[]{:S(2)}) collective-permute-start(f32[32,512]{1,0:T(8,128)S(1)} %get-tuple-element.32), channel_id=1, source_target_pairs={{0,4},{4,8},{8,12},{12,0},{1,5},{5,9},{9,13},{13,1},{2,6},{6,10},{... | collective-permute-start | bytes 196616 | tf_op jit(solution)/shard_map/ppermute | solution.py:380
  39.2 10.9 %collective-permute-start.5 = (s32[1,17]{1,0:T(1,128)S(1)}, s32[1,17]{1,0:T(1,128)S(1)}, u32[]{:S(2)}, u32[]{:S(2)}) collective-permute-start(s32[1,17]{1,0:T(1,128)S(1)} %pad_add_fusion.2.refs_0_), channel_id=1, source_target_pairs={{0,10},{2,12},{4,14},{6,0},{8,2},{10,4},{12,6},{14,8},{1,11},{3,13... | collective-permute-start | bytes 212 | tf_op jit(solution)/shard_map/ppermute | solution.py:380
  41.2 9.5 %collective-permute-start.6 = (s32[1,17]{1,0:T(1,128)S(1)}, s32[1,17]{1,0:T(1,128)S(1)}, u32[]{:S(2)}, u32[]{:S(2)}) collective-permute-start(s32[1,17]{1,0:T(1,128)S(1)} %pad_add_fusion.2.refs_0_), channel_id=1, source_target_pairs={{0,14},{2,0},{4,2},{6,4},{8,6},{10,8},{12,10},{14,12},{1,15},{3,1}... | collective-permute-start | bytes 212 | tf_op jit(solution)/shard_map/ppermute | solution.py:380
  45.7 6.6 %collective-permute-start.20 = (f32[32,512]{1,0:T(8,128)S(1)}, f32[32,512]{1,0:T(8,128)S(1)}, u32[]{:S(2)}, u32[]{:S(2)}) collective-permute-start(f32[32,512]{1,0:T(8,128)S(1)} %get-tuple-element.33), channel_id=1, source_target_pairs={{0,8},{4,12},{8,0},{12,4},{1,9},{5,13},{9,1},{13,5},{2,10},{6,14},... | collective-permute-start | bytes 196616 | tf_op jit(solution)/shard_map/ppermute | solution.py:380
  45.8 9.9 %collective-permute-start.21 = (f32[32,512]{1,0:T(8,128)S(1)}, f32[32,512]{1,0:T(8,128)S(1)}, u32[]{:S(2)}, u32[]{:S(2)}) collective-permute-start(f32[32,512]{1,0:T(8,128)S(1)} %get-tuple-element.34), channel_id=1, source_target_pairs={{0,12},{4,0},{8,4},{12,8},{1,13},{5,1},{9,5},{13,9},{2,14},{6,2},{... | collective-permute-start | bytes 196616 | tf_op jit(solution)/shard_map/ppermute | solution.py:380
  50.1 6.4 %collective-permute-start.12 = (f32[24,128]{1,0:T(8,128)S(1)}, f32[24,128]{1,0:T(8,128)S(1)}, u32[]{:S(2)}, u32[]{:S(2)}) collective-permute-start(f32[24,128]{1,0:T(8,128)S(1)} %get-tuple-element.31.refs_0_), channel_id=1, source_target_pairs={{0,2},{2,4},{4,6},{6,8},{8,10},{10,12},{12,14},{14,0},{1,3},{3,5},... | collective-permute-start | bytes 36872 | tf_op jit(solution)/shard_map/ppermute | solution.py:380
  50.7 8.4 %collective-permute-start.13 = (f32[24,128]{1,0:T(8,128)S(1)}, f32[24,128]{1,0:T(8,128)S(1)}, u32[]{:S(2)}, u32[]{:S(2)}) collective-permute-start(f32[24,128]{1,0:T(8,128)S(1)} %get-tuple-element.31.refs_0_), channel_id=1, source_target_pairs={{0,4},{2,6},{4,8},{6,10},{8,12},{10,14},{12,0},{14,2},{1,5},{3,7},... | collective-permute-start | bytes 36872 | tf_op jit(solution)/shard_map/ppermute | solution.py:380
  50.7 8.5 %collective-permute-start.14 = (f32[24,128]{1,0:T(8,128)S(1)}, f32[24,128]{1,0:T(8,128)S(1)}, u32[]{:S(2)}, u32[]{:S(2)}) collective-permute-start(f32[24,128]{1,0:T(8,128)S(1)} %get-tuple-element.31.refs_0_), channel_id=1, source_target_pairs={{0,6},{2,8},{4,10},{6,12},{8,14},{10,0},{12,2},{14,4},{1,7},{3,9},... | collective-permute-start | bytes 36872 | tf_op jit(solution)/shard_map/ppermute | solution.py:380
  52.3 9.3 %collective-permute-start.15 = (f32[24,128]{1,0:T(8,128)S(1)}, f32[24,128]{1,0:T(8,128)S(1)}, u32[]{:S(2)}, u32[]{:S(2)}) collective-permute-start(f32[24,128]{1,0:T(8,128)S(1)} %get-tuple-element.31.refs_0_), channel_id=1, source_target_pairs={{0,8},{2,10},{4,12},{6,14},{8,0},{10,2},{12,4},{14,6},{1,9},{3,11}... | collective-permute-start | bytes 36872 | tf_op jit(solution)/shard_map/ppermute | solution.py:380
  55.6 7.9 %collective-permute-start.16 = (f32[24,128]{1,0:T(8,128)S(1)}, f32[24,128]{1,0:T(8,128)S(1)}, u32[]{:S(2)}, u32[]{:S(2)}) collective-permute-start(f32[24,128]{1,0:T(8,128)S(1)} %get-tuple-element.31.refs_0_), channel_id=1, source_target_pairs={{0,10},{2,12},{4,14},{6,0},{8,2},{10,4},{12,6},{14,8},{1,11},{3,13... | collective-permute-start | bytes 36872 | tf_op jit(solution)/shard_map/ppermute | solution.py:380
  56.5 10.3 %collective-permute-start.22 = (bf16[1,256,128]{2,1,0:T(8,128)(2,1)S(1)}, bf16[1,256,128]{2,1,0:T(8,128)(2,1)S(1)}, u32[]{:S(2)}, u32[]{:S(2)}) collective-permute-start(bf16[1,256,128]{2,1,0:T(8,128)(2,1)S(1)} %get-tuple-element.37), channel_id=1, source_target_pairs={{0,4},{4,8},{8,12},{12,0},{1,5},{5,9},{9,13},{13,1},{2,6},{6,10},{... | collective-permute-start | bytes 196616 | tf_op jit(solution)/shard_map/ppermute | solution.py:380
  59.1 7.7 %collective-permute-start.23 = (bf16[1,256,128]{2,1,0:T(8,128)(2,1)S(1)}, bf16[1,256,128]{2,1,0:T(8,128)(2,1)S(1)}, u32[]{:S(2)}, u32[]{:S(2)}) collective-permute-start(bf16[1,256,128]{2,1,0:T(8,128)(2,1)S(1)} %get-tuple-element.38), channel_id=1, source_target_pairs={{0,8},{4,12},{8,0},{12,4},{1,9},{5,13},{9,1},{13,5},{2,10},{6,14},... | collective-permute-start | bytes 196616 | tf_op jit(solution)/shard_map/ppermute | solution.py:380
  59.2 8.2 %collective-permute-start.24 = (bf16[1,256,128]{2,1,0:T(8,128)(2,1)S(1)}, bf16[1,256,128]{2,1,0:T(8,128)(2,1)S(1)}, u32[]{:S(2)}, u32[]{:S(2)}) collective-permute-start(bf16[1,256,128]{2,1,0:T(8,128)(2,1)S(1)} %get-tuple-element.39), channel_id=1, source_target_pairs={{0,12},{4,0},{8,4},{12,8},{1,13},{5,1},{9,5},{13,9},{2,14},{6,2},{... | collective-permute-start | bytes 196616 | tf_op jit(solution)/shard_map/ppermute | solution.py:380
  61.6 5.8 %collective-permute-start.17 = (f32[24,128]{1,0:T(8,128)S(1)}, f32[24,128]{1,0:T(8,128)S(1)}, u32[]{:S(2)}, u32[]{:S(2)}) collective-permute-start(f32[24,128]{1,0:T(8,128)S(1)} %get-tuple-element.31.refs_0_), channel_id=1, source_target_pairs={{0,12},{2,14},{4,0},{6,2},{8,4},{10,6},{12,8},{14,10},{1,13},{3,15... | collective-permute-start | bytes 36872 | tf_op jit(solution)/shard_map/ppermute | solution.py:380
  70.3 8.4 %collective-permute-start.28 = (f32[32,2048]{1,0:T(8,128)S(1)}, f32[32,2048]{1,0:T(8,128)S(1)}, u32[]{:S(2)}, u32[]{:S(2)}) collective-permute-start(f32[32,2048]{1,0:T(8,128)S(1)} %get-tuple-element.42.mine), channel_id=1, source_target_pairs={{0,2},{2,0},{1,3},{3,1},{4,6},{6,4},{5,7},{7,5},{8,10},{10,8},{9,1... | collective-permute-start | bytes 786440 | tf_op jit(solution)/shard_map/ppermute | solution.py:380
  79.4 6.6 %collective-permute-start.33 = (f32[32,512]{1,0:T(8,128)S(1)}, f32[32,512]{1,0:T(8,128)S(1)}, u32[]{:S(2)}, u32[]{:S(2)}) collective-permute-start(f32[32,512]{1,0:T(8,128)S(1)} %get-tuple-element.44), channel_id=1, source_target_pairs={{0,4},{4,8},{8,12},{12,0},{1,5},{5,9},{9,13},{13,1},{2,6},{6,10},{... | collective-permute-start | bytes 196616 | tf_op jit(solution)/shard_map/ppermute | solution.py:380
  79.4 7.9 %collective-permute-start.34 = (f32[32,512]{1,0:T(8,128)S(1)}, f32[32,512]{1,0:T(8,128)S(1)}, u32[]{:S(2)}, u32[]{:S(2)}) collective-permute-start(f32[32,512]{1,0:T(8,128)S(1)} %get-tuple-element.45), channel_id=1, source_target_pairs={{0,8},{4,12},{8,0},{12,4},{1,9},{5,13},{9,1},{13,5},{2,10},{6,14},... | collective-permute-start | bytes 196616 | tf_op jit(solution)/shard_map/ppermute | solution.py:380
  81.2 6.1 %collective-permute-start.35 = (f32[32,512]{1,0:T(8,128)S(1)}, f32[32,512]{1,0:T(8,128)S(1)}, u32[]{:S(2)}, u32[]{:S(2)}) collective-permute-start(f32[32,512]{1,0:T(8,128)S(1)} %get-tuple-element.46), channel_id=1, source_target_pairs={{0,12},{4,0},{8,4},{12,8},{1,13},{5,1},{9,5},{13,9},{2,14},{6,2},{... | collective-permute-start | bytes 196616 | tf_op jit(solution)/shard_map/ppermute | solution.py:380
  88.3 6.4 %collective-permute-start.36 = (f32[32,2048]{1,0:T(8,128)S(1)}, f32[32,2048]{1,0:T(8,128)S(1)}, u32[]{:S(2)}, u32[]{:S(2)}) collective-permute-start(f32[32,2048]{1,0:T(8,128)S(1)} %shard_map.69.mine), channel_id=1, source_target_pairs={{0,2},{2,0},{1,3},{3,1},{4,6},{6,4},{5,7},{7,5},{8,10},{10,8},{9,1... | collective-permute-start | bytes 786440 | tf_op jit(solution)/shard_map/ppermute | solution.py:380
  89.1 6.3 %collective-permute-start.29 = (f32[32,2048]{1,0:T(8,128)S(1)}, f32[32,2048]{1,0:T(8,128)S(1)}, u32[]{:S(2)}, u32[]{:S(2)}) collective-permute-start(f32[32,2048]{1,0:T(8,128)S(1)} %get-tuple-element.43.own.refs_0_), channel_id=1, source_target_pairs={{0,1},{1,0},{2,3},{3,2},{4,5},{5,4},{6,7},{7,6},{8,9},{9,8},{10,11... | collective-permute-start | bytes 786440 | tf_op jit(solution)/shard_map/ppermute | solution.py:380
  95.3 14.4 %collective-permute-start.37 = (f32[32,2048]{1,0:T(8,128)S(1)}, f32[32,2048]{1,0:T(8,128)S(1)}, u32[]{:S(2)}, u32[]{:S(2)}) collective-permute-start(f32[32,2048]{1,0:T(8,128)S(1)} %shard_map.70.own), channel_id=1, source_target_pairs={{0,1},{1,0},{2,3},{3,2},{4,5},{5,4},{6,7},{7,6},{8,9},{9,8},{10,11... | collective-permute-start | bytes 786440 | tf_op jit(solution)/shard_map/ppermute | solution.py:380
  96.4 5.8 %collective-permute-start.30 = (f32[64,64]{1,0:T(8,128)S(1)}, f32[64,64]{1,0:T(8,128)S(1)}, u32[]{:S(2)}, u32[]{:S(2)}) collective-permute-start(f32[64,64]{1,0:T(8,128)S(1)} %shard_map.67.refs_0_), channel_id=1, source_target_pairs={{0,4},{4,8},{8,12},{12,0},{1,5},{5,9},{9,13},{13,1},{2,6},{6,10},{... | collective-permute-start | bytes 49160 | tf_op jit(solution)/shard_map/ppermute | solution.py:380
  111.2 6.1 %collective-permute-start.38 = (f32[64,64]{1,0:T(8,128)S(1)}, f32[64,64]{1,0:T(8,128)S(1)}, u32[]{:S(2)}, u32[]{:S(2)}) collective-permute-start(f32[64,64]{1,0:T(8,128)S(1)} %get-tuple-element.48.refs_0_), channel_id=1, source_target_pairs={{0,4},{4,8},{8,12},{12,0},{1,5},{5,9},{9,13},{13,1},{2,6},{6,10},{... | collective-permute-start | bytes 49160 | tf_op jit(solution)/shard_map/ppermute | solution.py:380
  112.3 5.8 %collective-permute-start.39 = (f32[64,64]{1,0:T(8,128)S(1)}, f32[64,64]{1,0:T(8,128)S(1)}, u32[]{:S(2)}, u32[]{:S(2)}) collective-permute-start(f32[64,64]{1,0:T(8,128)S(1)} %get-tuple-element.48.refs_0_), channel_id=1, source_target_pairs={{0,8},{4,12},{8,0},{12,4},{1,9},{5,13},{9,1},{13,5},{2,10},{6,14},... | collective-permute-start | bytes 49160 | tf_op jit(solution)/shard_map/ppermute | solution.py:380
  (12 other events, 56.8 us)

commit v2 on v1

v2 whole, which is shorter than its diff:
```python
import functools

import jax
import jax.numpy as jnp
from jax import lax
from jax.experimental import pallas as pl
from jax.experimental.pallas import tpu as pltpu
from jax.sharding import PartitionSpec as P

BLOCK = 128
kernel_gamma = 14.0

VMEM = pl.BlockSpec(memory_space=pltpu.VMEM)
SMEM = pl.BlockSpec(memory_space=pltpu.SMEM)
ANY = pl.BlockSpec(memory_space=pl.ANY)
F32 = jnp.float32
BF16 = jnp.bfloat16
HIGHEST = lax.Precision.HIGHEST
NT = (((1,), (1,)), ((), ()))


def call(body, outs, args, smem_in=(), smem_out=(), any_in=()):
    single = not isinstance(outs, (list, tuple))
    shapes = [outs] if single else list(outs)
    result = pl.pallas_call(
        body,
        out_shape=shapes,
        in_specs=[
            SMEM if i in smem_in else ANY if i in any_in else VMEM for i in range(len(args))
        ],
        out_specs=[SMEM if i in smem_out else VMEM for i in range(len(shapes))],
        compiler_params=pltpu.CompilerParams(vmem_limit_bytes=48 * 2**20),
    )(*args)
    return result[0] if single else result


def sds(shape, dtype):
    return jax.ShapeDtypeStruct(shape, dtype)


def at_block(index):
    return pl.ds(pl.multiple_of(index * BLOCK, BLOCK), BLOCK)


def eye_mask(size):
    return lax.broadcasted_iota(jnp.int32, (size, size), 0) == lax.broadcasted_iota(
        jnp.int32, (size, size), 1
    )


def halves(value):
    high = value.astype(BF16)
    low = (value - high.astype(F32)).astype(BF16)
    return high, low


def pack(tile):
    return jnp.concatenate(halves(tile), axis=0)


def product(packed, values):
    left = jnp.concatenate(halves(values), axis=0)
    both = jnp.dot(jnp.concatenate([left, left], axis=1), packed, preferred_element_type=F32)
    count = values.shape[0]
    return both[:count] + both[count:]


def gram(full):
    high = full.astype(BF16)
    rest = full - high.astype(F32)
    middle = rest.astype(BF16)
    low = (rest - middle.astype(F32)).astype(BF16)
    parts = jnp.concatenate([high, middle, low], axis=0)
    cross = lax.dot_general(parts, parts, NT, preferred_element_type=F32)
    n = full.shape[0]
    total = None
    for i, j in ((2, 2), (1, 2), (2, 1), (0, 2), (2, 0), (1, 1), (0, 1), (1, 0), (0, 0)):
        piece = cross[i * n : (i + 1) * n, j * n : (j + 1) * n]
        total = piece if total is None else total + piece
    return total


def lower_inverse(matrix, step=4):
    n = matrix.shape[0]
    state = jnp.concatenate([matrix, eye_mask(n).astype(F32)], axis=1)
    done = []
    for j in range(0, n, step):
        top = j // 8 * 8
        if top > n - state.shape[0]:
            done.append(state[:8])
            state = state[8:]
        base = j - top
        rows = lax.broadcasted_iota(jnp.int32, state.shape, 0)
        columns = [jnp.broadcast_to(state[:, j + i : j + i + 1], state.shape) for i in range(step)]
        lines = [state[base + i : base + i + 1, :] for i in range(step)]
        pivot = [[columns[k][base + i : base + i + 1, :] for k in range(step)] for i in range(step)]
        for i in range(step):
            reciprocal = 1.0 / pivot[i][i]
            scaled = lines[i] * reciprocal
            ratio = [pivot[i][k] * reciprocal for k in range(step)]
            for k in range(i + 1, step):
                lines[k] = lines[k] - pivot[k][i] * scaled
                columns[k] = columns[k] - columns[i] * ratio[k]
                for m in range(i + 1, step):
                    pivot[k][m] = pivot[k][m] - pivot[k][i] * ratio[m]
            state = state - jnp.where(rows > base + i, columns[i], 0.0) * scaled
    state = jnp.concatenate([*done, state], axis=0)
    pivots = jnp.sum(jnp.where(eye_mask(n), state[:, :n], 0.0), axis=1, keepdims=True)
    return state[:, n:] / jnp.sqrt(pivots)


def both_columns(core, own, other):
    first = core == 0
    return jnp.concatenate(
        [jnp.where(first, own, other), jnp.where(first, other, own)], axis=0
    )


def plan_body(dims, me, lists, emb, idx, *sends):
    row_count, tile_count, capacity, slots, blocks_here = dims
    row = me[0]

    def clear(i, carry):
        for line in range(6):
            idx[line, i] = 0
        return carry

    lax.fori_loop(0, slots, clear, 0)

    def ranked(line, want, write):
        count = lists[line, 2 * slots]

        def step(s, counts):
            near = lists[line, s]
            far = lists[line, slots + s]
            return write(s, near, far, far // blocks_here, s < count, counts)

        lax.fori_loop(0, slots, step, (0,) * want)

    def write_own(s, near, far, owner, live, counts):
        shift = lax.rem(owner - row + row_count, row_count)
        rank = functools.reduce(
            lambda total, k: total + jnp.where(shift == k, counts[k], 0), range(row_count), 0
        )

        @pl.when(live)
        def _():
            slot = shift * capacity + rank
            idx[0, slot] = near - row * blocks_here
            idx[1, slot] = far
            idx[2, slot] = 1
            idx[3, slot] = s

        return tuple(
            counts[k] + (live & (shift == k)).astype(jnp.int32) for k in range(row_count)
        )

    for k in range(row_count):
        line = lax.rem(row - k + row_count, row_count) * tile_count + me[1]
        if k == 0:
            ranked(line, row_count, write_own)

        def write_in(s, near, far, owner, live, counts, k=k):
            hit = live & (owner == row)

            @pl.when(hit)
            def _():
                slot = k * capacity + counts[0]
                idx[4, slot] = far - row * blocks_here
                idx[5, slot] = near

            return (counts[0] + hit.astype(jnp.int32),)

        ranked(line, 1, write_in)
    for k in range(1, row_count):
        for j in range(capacity):
            sends[k - 1][j * BLOCK : (j + 1) * BLOCK, :] = emb[at_block(idx[4, k * capacity + j]), :]


def partial_distance(left, right):
    inner = lax.dot_general(left, right, NT, preferred_element_type=F32)
    left_sq = jnp.sum(jnp.square(left.astype(F32)), axis=1, keepdims=True)
    right_sq = jnp.sum(jnp.square(right.astype(F32)), axis=1, keepdims=True)
    right_row = jnp.sum(jnp.where(eye_mask(BLOCK), right_sq, 0.0), axis=0, keepdims=True)
    return left_sq + right_row - 2.0 * inner


def self_distance_body(own_blocks, tile_count, me, emb, out):
    for i in range(own_blocks):
        block = emb[at_block(i * tile_count + me[1]), :]
        out[i * BLOCK : (i + 1) * BLOCK, :] = partial_distance(block, block)


def pair_distance_body(row_count, capacity, idx, emb, *refs):
    out = refs[-1]
    for k in range(row_count):
        for j in range(capacity):
            slot = k * capacity + j
            left = emb[at_block(idx[0, slot]), :]
            if k == 0:
                right = emb[at_block(idx[4, j]), :]
            else:
                right = refs[k - 1][j * BLOCK : (j + 1) * BLOCK, :]
            out[slot * BLOCK : (slot + 1) * BLOCK, :] = partial_distance(left, right)


def self_tile_body(own_blocks, mine, other, packed, sums):
    for i in range(own_blocks):
        part = slice(i * BLOCK, (i + 1) * BLOCK)
        tile = jnp.exp(-kernel_gamma * (mine[part, :] + other[part, :] - 2.0))
        tile = jnp.where(eye_mask(BLOCK), 0.0, tile)
        packed[i] = pack(tile)
        sums[i : i + 1, :] = jnp.sum(tile, axis=0, keepdims=True)


def pair_tile_body(row_count, capacity, per_core, slots, me, idx, mine, other, self_sums, near_tiles, home_tiles, sends, sums):
    core = me[2]
    sums[0 : 2 * slots, :] = jnp.zeros((2 * slots, BLOCK), F32)
    sums[2 * slots :, :] = self_sums[...]
    for k in range(row_count):
        for j in range(capacity):
            slot = k * capacity + j
            part = slice(slot * BLOCK, (slot + 1) * BLOCK)
            live = idx[2, slot] > 0
            tile = jnp.exp(-kernel_gamma * (mine[part, :] + other[part, :] - 2.0))
            tile = jnp.where(live, tile, 0.0)
            turned = tile.T
            near_tiles[slot] = pack(turned)

            @pl.when(live)
            def _():
                raw = idx[3, slot]
                sums[pl.ds(raw, 1), :] = jnp.sum(turned, axis=0, keepdims=True)
                sums[pl.ds(slots + raw, 1), :] = jnp.sum(tile, axis=0, keepdims=True)

            if k == 0:
                home_tiles[j] = pack(tile)
            else:

                @pl.when(core == j // per_core)
                def _():
                    sends[lax.rem(me[0] + k, row_count), j % per_core] = pack(tile)


def pick_columns(me, idx, row_count, capacity, source, sends):
    for k in range(1, row_count):
        back = row_count - k
        there = lax.rem(me[0] + k, row_count)
        for j in range(capacity):
            sends[there, :, j * BLOCK : (j + 1) * BLOCK] = source[:, at_block(idx[0, k * capacity + j])]
            place = capacity + j
            sends[there, :, place * BLOCK : (place + 1) * BLOCK] = source[
                :, at_block(idx[4, back * capacity + j])
            ]


def pick_body(row_count, capacity, me, idx, source, *refs):
    pick_columns(me, idx, row_count, capacity, source, refs[-1])


def apply_tiles(dims, me, idx, inverse, own, received, near_tiles, home_tiles, sent, shared, self_tiles, out):
    row_count, capacity, per_core, blocks_here, tile_count = dims
    row, tile_index, core = me[0], me[1], me[2]
    out[...] = jnp.zeros(out.shape, F32)

    def scaled(values, block):
        return values * inverse[pl.ds(block, 1), :]

    def add(block, packed, values):
        place = at_block(block)
        out[:, place] = out[:, place] + product(packed, values)

    for i in range(blocks_here // tile_count):
        block = i * tile_count + tile_index
        add(block, self_tiles[i], scaled(own[:, at_block(block)], row * blocks_here + block))
    for k in range(row_count):
        owner = lax.rem(row + k, row_count)
        for j in range(capacity):
            slot = k * capacity + j
            if k == 0:
                values = own[:, at_block(idx[4, j])]
            else:
                values = received[owner, :, (capacity + j) * BLOCK : (capacity + j + 1) * BLOCK]
            add(idx[0, slot], near_tiles[slot], scaled(values, idx[1, slot]))
    for k in range(row_count):
        source = lax.rem(row - k + row_count, row_count)
        for j in range(capacity):
            if k == 0:
                slot = j
                values = own[:, at_block(idx[0, j])]
                packed = home_tiles[j]
            else:
                inner = j % per_core
                if j < per_core:
                    place = core * per_core + inner
                    packed = sent[source, inner]
                else:
                    place = (1 - core) * per_core + inner
                    packed = shared[source, inner]
                slot = k * capacity + place
                values = received[source, :, at_block(place)]
            add(idx[4, slot], packed, scaled(values, idx[5, slot]))


def first_apply_body(dims, me, idx, onehot, sums, *refs):
    inputs, (out, degree, inverse) = refs[:-3], refs[-3:]
    total = jnp.dot(onehot[...], sums[...], precision=HIGHEST, preferred_element_type=F32)
    degree[...] = total
    inverse[...] = 1.0 / jnp.sqrt(total)
    apply_tiles(dims, me, idx, inverse, *inputs, out)


def second_apply_body(dims, me, idx, inverse, gram_in, *refs):
    inputs, (out, gram_out) = refs[:-2], refs[-2:]
    apply_tiles(dims, me, idx, inverse, *inputs, out)
    gram_out[...] = gram_in[...]


def scale_rows(me, blocks_here, inverse, mine, other, out):
    for b in range(blocks_here):
        part = slice(b * BLOCK, (b + 1) * BLOCK)
        row = inverse[pl.ds(me[0] * blocks_here + b, 1), :]
        out[:, part] = (mine[:, part] + other[:, part]) * row


def mapped_body(row_count, capacity, blocks_here, me, idx, inverse, mine, other, out, sends):
    scale_rows(me, blocks_here, inverse, mine, other, out)
    pick_columns(me, idx, row_count, capacity, out, sends)


def last_mapped_body(blocks_here, me, inverse, mine, other, out):
    scale_rows(me, blocks_here, inverse, mine, other, out)


def gram_body(me, own, other, out):
    out[...] = gram(both_columns(me[2], own[...], other[...]))


def stacked_sum(stack):
    n = stack.shape[1]
    total = stack[:n, :]
    for i in range(1, stack.shape[0] // n):
        total = total + stack[i * n : (i + 1) * n, :]
    return total


def factor_body(after, grams, out):
    out[...] = lower_inverse(stacked_sum(grams))


def second_gram_body(me, factor, own, other, mapped, out):
    full = both_columns(me[2], own[...], other[...])
    value = jnp.dot(factor[...], full, precision=HIGHEST, preferred_element_type=F32)
    mapped[...] = value
    out[...] = gram(value)


def final_body(me, mapped, grams, out):
    factor = lower_inverse(stacked_sum(grams))
    own_cols = out.shape[0]
    part = jnp.where(me[2] == 0, factor[:own_cols], factor[own_cols:])
    out[...] = jnp.dot(part, mapped[...], precision=HIGHEST, preferred_element_type=F32)


def shift_by(value, axes, size, shift):
    return lax.ppermute(value, axes, [(i, (i + shift) % size) for i in range(size)])


def exchange(value):
    return lax.all_to_all(value, "rows", split_axis=0, concat_axis=0, tiled=True)


def gather(value, axes):
    return lax.all_gather(value, axes, axis=0, tiled=True)


def local(embeddings, start, pair_list, pair_count):
    row_count = lax.axis_size("rows")
    tile_count = lax.axis_size("tiles")
    core_count = lax.axis_size("cols")
    row_index = lax.axis_index("rows")
    tile_index = lax.axis_index("tiles")
    col_index = lax.axis_index("cols")
    me = jnp.stack([row_index, tile_index, col_index]).astype(jnp.int32)
    rows_here, half_features = embeddings.shape
    blocks_here = rows_here // BLOCK
    slots = pair_list.shape[2]
    capacity = slots // row_count
    per_core = capacity // core_count
    own_blocks = blocks_here // tile_count
    own_cols = start.shape[1]
    team = row_count * tile_count
    block_count = row_count * blocks_here
    others = range(1, row_count)

    lists = jnp.concatenate([pair_list.reshape(1, 2 * slots), pair_count.reshape(1, 1)], axis=1)
    lists = gather(lists, ("rows", "tiles"))
    planned = call(
        functools.partial(plan_body, (row_count, tile_count, capacity, slots, blocks_here)),
        [sds((6, slots), jnp.int32)] + [sds((capacity * BLOCK, half_features), BF16) for _ in others],
        [me, lists, embeddings],
        smem_in=(0, 1),
        smem_out=(0,),
    )
    idx, sends = planned[0], planned[1:]
    far = [shift_by(sends[k - 1], "rows", row_count, -k) for k in others]

    self_part = call(
        functools.partial(self_distance_body, own_blocks, tile_count),
        sds((own_blocks * BLOCK, BLOCK), F32),
        [me, embeddings],
        smem_in=(0,),
    )
    self_other = shift_by(self_part, "cols", core_count, 1)
    self_tiles, self_sums = call(
        functools.partial(self_tile_body, own_blocks),
        [sds((own_blocks, 2 * BLOCK, BLOCK), BF16), sds((own_blocks, BLOCK), F32)],
        [self_part, self_other],
    )
    values = start.T
    start_sends = call(
        functools.partial(pick_body, row_count, capacity),
        sds((row_count, own_cols, 2 * capacity * BLOCK), F32),
        [me, idx, values, *far[:-1]],
        smem_in=(0, 1),
        any_in=range(3, 2 + row_count),
    )
    start_in = exchange(start_sends)

    pair_part = call(
        functools.partial(pair_distance_body, row_count, capacity),
        sds((slots * BLOCK, BLOCK), F32),
        [idx, embeddings, *far],
        smem_in=(0,),
    )
    pair_other = shift_by(pair_part, "cols", core_count, 1)
    near_tiles, home_tiles, tile_sends, sums = call(
        functools.partial(pair_tile_body, row_count, capacity, per_core, slots),
        [
            sds((slots, 2 * BLOCK, BLOCK), BF16),
            sds((capacity, 2 * BLOCK, BLOCK), BF16),
            sds((row_count, per_core, 2 * BLOCK, BLOCK), BF16),
            sds((2 * slots + own_blocks, BLOCK), F32),
        ],
        [me, idx, pair_part, pair_other, self_sums],
        smem_in=(0, 1),
    )
    all_sums = gather(sums, ("rows", "tiles"))
    sent = exchange(tile_sends)
    shared = shift_by(sent, "cols", core_count, 1)

    team_ids = jnp.arange(team, dtype=jnp.int32)[:, None]
    diagonal_ids = team_ids // tile_count * blocks_here + (
        jnp.arange(own_blocks, dtype=jnp.int32)[None, :] * tile_count + team_ids % tile_count
    )
    sum_ids = jnp.concatenate([lists[:, : 2 * slots], diagonal_ids], axis=1).reshape(1, -1)
    onehot = (sum_ids == jnp.arange(block_count, dtype=jnp.int32)[:, None]).astype(F32)

    dims = (row_count, capacity, per_core, blocks_here, tile_count)
    tile_args = [near_tiles, home_tiles, sent, shared, self_tiles]
    block_shape = sds((own_cols, rows_here), F32)
    table = sds((block_count, BLOCK), F32)
    square = sds((2 * own_cols, 2 * own_cols), F32)

    def team_sum(part):
        if tile_count == 2:
            return part, shift_by(part, "tiles", 2, 1)
        return lax.psum(part, "tiles"), jnp.zeros_like(part)

    part, degree, inverse = call(
        functools.partial(first_apply_body, dims),
        [block_shape, table, table],
        [me, idx, onehot, all_sums, values, start_in, *tile_args],
        smem_in=(0, 1),
    )
    mine, other = team_sum(part)
    mapped, sends = call(
        functools.partial(mapped_body, row_count, capacity, blocks_here),
        [block_shape, sds((row_count, own_cols, 2 * capacity * BLOCK), F32)],
        [me, idx, inverse, mine, other],
        smem_in=(0, 1),
    )
    received = exchange(sends)

    mapped_other = shift_by(mapped, "cols", core_count, 1)
    first_gram = call(gram_body, square, [me, mapped, mapped_other], smem_in=(0,))
    part, first_gram = call(
        functools.partial(second_apply_body, dims),
        [block_shape, square],
        [me, idx, inverse, first_gram, mapped, received, *tile_args],
        smem_in=(0, 1),
    )
    mine, other = team_sum(part)
    first_grams = gather(first_gram, "rows")
    second = call(
        functools.partial(last_mapped_body, blocks_here),
        block_shape,
        [me, inverse, mine, other],
        smem_in=(0,),
    )
    second_other = shift_by(second, "cols", core_count, 1)
    factor = call(factor_body, square, [second, first_grams], any_in=(0,))
    full, second_gram = call(
        second_gram_body,
        [sds((2 * own_cols, rows_here), F32), square],
        [me, factor, second, second_other],
        smem_in=(0,),
    )
    second_grams = gather(second_gram, "rows")
    vectors = call(final_body, block_shape, [me, full, second_grams], smem_in=(0,))
    own_degree = lax.dynamic_slice_in_dim(degree, row_index * blocks_here, blocks_here, 0)
    return (vectors.T, own_degree.reshape(rows_here))


def solution(mesh):
    in_specs = (
        P(("groups", "rows"), "cols"),
        P(("groups", "rows"), "cols"),
        P(("groups", "rows", "tiles"), None, None),
        P(("groups", "rows", "tiles")),
    )
    out_specs = (P(("groups", "rows"), "cols"), P(("groups", "rows")))
    return jax.shard_map(local, mesh=mesh, in_specs=in_specs, out_specs=out_specs, check_vma=False)
```

time: 126 us -> 158 us (1.25)
  blocking collectives: 0 us -> 80 us
  starting transfers between devices: 56.2 us -> 13.9 us
  Pallas kernels: 25.4 us -> 21.1 us
    all_gather x0 -> x4, blocking collectives: none -> 80 us  [gather(): return lax.all_gather(value, axes, axis=0, tiled=True)]
    ppermute x41 -> x10, starting transfers between devices: 56.2 us -> 3.56 us  [shift_by(): lax.ppermute(value, axes, [(i, (i + shift) % size) for i in range(size)])]
    ppermute x41 -> x10, waiting for transfers between devices: 39.5 us -> 26.2 us  [shift_by(): lax.ppermute(value, axes, [(i, (i + shift) % size) for i in range(size)])]
    all_to_all x0 -> x3, waiting for transfers between devices: none -> 12.1 us  [exchange(): lax.all_to_all(value, 'rows', split_axis=0, concat_axis=0, tiled=True)]
    all_to_all x0 -> x3, starting transfers between devices: none -> 10.3 us  [exchange(): lax.all_to_all(value, 'rows', split_axis=0, concat_axis=0, tiled=True)]
    pallas_call x14, Pallas kernels: 25.4 us -> 21.1 us  [call(): pl.pallas_call(body, out_shape=shapes, in_specs=[SMEM if i in smem_in els...]
  transfers between devices with their start and end apart: 41 -> 13, of which waited for: 16 -> 8; matrix products, arithmetic and copies ran while one was open for 1% -> 1% of each run, Pallas kernels for 9% -> 4%
where the time goes in v2:
time: 158 us
  blocking collectives  80 us (51%)
  waiting for transfers between devices  38.3 us (24%)
  Pallas kernels  21.1 us (13%)
  starting transfers between devices  13.9 us (9%)
  local copies, waits for them, and re-layouts  2.87 us (2%)
    all_gather x4, blocking collectives, gather(): return lax.all_gather(value, axes, axis=0, tiled=True)  80 us
    ppermute x10, waiting for transfers between devices, shift_by(): lax.ppermute(value, axes, [(i, (i + shift) % size) for i in range(size)])  26.2 us
    pallas_call x14, Pallas kernels, call(): pl.pallas_call(body, out_shape=shapes, in_specs=[SMEM if i in smem_in els...  21.1 us
    all_to_all x3, waiting for transfers between devices, exchange(): lax.all_to_all(value, 'rows', split_axis=0, concat_axis=0, tiled=True)  12.1 us
    all_to_all x3, starting transfers between devices, exchange(): lax.all_to_all(value, 'rows', split_axis=0, concat_axis=0, tiled=True)  10.3 us
    ppermute x10, starting transfers between devices, shift_by(): lax.ppermute(value, axes, [(i, (i + shift) % size) for i in range(size)])  3.56 us
  transfers between devices with their start and end apart: 13, of which 8 were waited for; matrix products, arithmetic and copies ran while one was open for 1% of the time, Pallas kernels for 4%

profile of v2, /device:TPU:0, one launch (start us, length us, event | category | flops | bytes accessed | tf_op | source)
XLA Modules:
  0.0 157.9 jit_solution(9477695290819549986)
XLA Ops:
  1.3 0.8 reshape.74
  2.1 22.1 %all-gather = s32[8,1,17]{2,1,0:T(1,128)S(1)} all-gather(s32[1,1,17]{2,1,0:T(1,128)S(1)} %add_bitcast_fusion), channel_id=1, replica_groups=mesh['groups'=2,'rows'=4,'tiles'=2,'cols'=2] {'rows','tiles'}, dimensions={0}, use_global_device_ids=true | all-gather | bytes 612 | tf_op jit(solution)/shard_map/all_gather | solution.py:374
  24.3 1.4 copy-done
  25.7 2.1 %shard_map.59 = (s32[6,8]{1,0:T(8,128)S(1)}, bf16[256,384]{1,0:T(8,128)(2,1)S(1)}, bf16[256,384]{1,0:T(8,128)(2,1)S(1)}, bf16[256,384]{1,0:T(8,128)(2,1)S(1)}) custom-call(s32[3]{0:T(128)S(1)} %pad_add_fusion.1.me, s32[8,17]{1,0:T(8,128)S(1)} %bitcast.15, bf16[2048,384]{1,0:T(8,128)(2,1)S(1)} %copy-done), custom_call_target="tpu_custom_call" | custom-call | tf_op jit(solution)/shard_map/pallas_call | solution.py:25
  28.2 1.8 %collective-permute-start.2 = (bf16[256,384]{1,0:T(8,128)(2,1)S(1)}, bf16[256,384]{1,0:T(8,128)(2,1)S(1)}, u32[]{:S(2)}, u32[]{:S(2)}) collective-permute-start(bf16[256,384]{1,0:T(8,128)(2,1)S(1)} %get-tuple-element.24), channel_id=1, source_target_pairs={{0,4},{4,8},{8,12},{12,0},{1,5},{5,9},{9,13},{13,1},{2,6},{6,10},{... | collective-permute-start | bytes 589832 | tf_op jit(solution)/shard_map/ppermute | solution.py:366
  30.0 1.0 shard_map.61.mine
  31.1 4.8 %collective-permute-done.refs_0_ = bf16[256,384]{1,0:T(8,128)(2,1)S(1)} collective-permute-done((bf16[256,384]{1,0:T(8,128)(2,1)S(1)}, bf16[256,384]{1,0:T(8,128)(2,1)S(1)}, u32[]{:S(2)}, u32[]{:S(2)}) %collective-permute-start) | collective-permute-done | bytes 196640 | tf_op jit(solution)/shard_map/ppermute | solution.py:366
  35.8 6.6 %collective-permute-done.1.refs_1_ = bf16[256,384]{1,0:T(8,128)(2,1)S(1)} collective-permute-done((bf16[256,384]{1,0:T(8,128)(2,1)S(1)}, bf16[256,384]{1,0:T(8,128)(2,1)S(1)}, u32[]{:S(2)}, u32[]{:S(2)}) %collective-permute-start.1) | collective-permute-done | bytes 196640 | tf_op jit(solution)/shard_map/ppermute | solution.py:366
  42.4 1.1 shard_map.60.mine
  43.8 1.7 %collective-permute-done.3.other = f32[1024,128]{1,0:T(8,128)S(1)} collective-permute-done((f32[1024,128]{1,0:T(8,128)S(1)}, f32[1024,128]{1,0:T(8,128)S(1)}, u32[]{:S(2)}, u32[]{:S(2)}) %collective-permute-start.3) | collective-permute-done | bytes 524320 | tf_op jit(solution)/shard_map/ppermute | solution.py:366
  45.5 2.3 %shard_map.63 = (bf16[8,256,128]{2,1,0:T(8,128)(2,1)S(1)}, bf16[2,256,128]{2,1,0:T(8,128)(2,1)S(1)}, bf16[4,1,256,128]{3,2,1,0:T(8,128)(2,1)}, f32[24,128]{1,0:T(8,128)S(1)}) custom-call(s32[3]{0:T(128)S(1)} %pad_add_fusion.1.me, s32[6,8]{1,0:T(8,128)S(1)} %get-tuple-element.21.idx, f32[1024,128]{1,0:T(8,128)S(1)} %shard_map.60.mine, ...), custom_call_target="tpu_custom_call" | custom-call | tf_op jit(solution)/shard_map/pallas_call | solution.py:25
  47.8 3.5 %all-to-all-start.1 = ((bf16[4,1,256,128]{3,2,1,0:T(8,128)(2,1)}), bf16[4,1,256,128]{3,2,1,0:T(8,128)(2,1)S(1)}, u32[]{:S(2)}, u32[]{:S(2)}) async-start(bf16[4,1,256,128]{3,2,1,0:T(8,128)(2,1)} %get-tuple-element.29), calls=%async_computation.1 | async-start | bytes 524288 | tf_op jit(solution)/shard_map/all_to_all | solution.py:370
  51.3 1.3 shard_map.64
  52.7 8.0 %all-to-all-done.1.refs_4_ = bf16[4,1,256,128]{3,2,1,0:T(8,128)(2,1)S(1)} async-done(((bf16[4,1,256,128]{3,2,1,0:T(8,128)(2,1)}), bf16[4,1,256,128]{3,2,1,0:T(8,128)(2,1)S(1)}, u32[]{:S(2)}, u32[]{:S(2)}) %all-to-all-start.1) | async-done | bytes 262176 | tf_op jit(solution)/shard_map/all_to_all | solution.py:370
  60.6 3.4 %all-to-all-start = ((f32[4,32,512]{2,1,0:T(8,128)}), f32[4,32,512]{2,1,0:T(8,128)S(1)}, u32[]{:S(2)}, u32[]{:S(2)}) async-start(f32[4,32,512]{2,1,0:T(8,128)} %shard_map.64), calls=%async_computation | async-start | bytes 524288 | tf_op jit(solution)/shard_map/all_to_all | solution.py:370
  64.3 31.1 %all_gather.13.sums = f32[192,128]{1,0:T(8,128)S(1)} all-gather(f32[24,128]{1,0:T(8,128)S(1)} %get-tuple-element.26), channel_id=1, replica_groups=mesh['groups'=2,'rows'=4,'tiles'=2,'cols'=2] {'rows','tiles'}, dimensions={0}, use_global_device_ids=true | all-gather | bytes 110592 | tf_op jit(solution)/shard_map/all_gather | solution.py:374
  95.5 1.3 shard_map.65
  96.9 6.4 %collective-permute-done.6.other = f32[32,2048]{1,0:T(8,128)S(1)} collective-permute-done((f32[32,2048]{1,0:T(8,128)S(1)}, f32[32,2048]{1,0:T(8,128)S(1)}, u32[]{:S(2)}, u32[]{:S(2)}) %collective-permute-start.6) | collective-permute-done | bytes 262176 | tf_op jit(solution)/shard_map/ppermute | solution.py:366
  103.2 1.4 shard_map.66
  104.6 3.4 %all-to-all-start.2 = ((f32[4,32,512]{2,1,0:T(8,128)}), f32[4,32,512]{2,1,0:T(8,128)S(1)}, u32[]{:S(2)}, u32[]{:S(2)}) async-start(f32[4,32,512]{2,1,0:T(8,128)} %get-tuple-element.34), calls=%async_computation.2 | async-start | bytes 524288 | tf_op jit(solution)/shard_map/all_to_all | solution.py:370
  108.1 1.5 collective-permute-done.7.other
  109.6 1.0 shard_map.67.gram_in
  110.6 4.1 %all-to-all-done.2.refs_1_ = f32[4,32,512]{2,1,0:T(8,128)S(1)} async-done(((f32[4,32,512]{2,1,0:T(8,128)}), f32[4,32,512]{2,1,0:T(8,128)S(1)}, u32[]{:S(2)}, u32[]{:S(2)}) %all-to-all-start.2) | async-done | bytes 262176 | tf_op jit(solution)/shard_map/all_to_all | solution.py:370
  114.7 1.0 shard_map.68
  115.7 1.1 collective-permute-start.8
  116.9 5.3 %collective-permute-done.8.other = f32[32,2048]{1,0:T(8,128)S(1)} collective-permute-done((f32[32,2048]{1,0:T(8,128)S(1)}, f32[32,2048]{1,0:T(8,128)S(1)}, u32[]{:S(2)}, u32[]{:S(2)}) %collective-permute-start.8) | collective-permute-done | bytes 262176 | tf_op jit(solution)/shard_map/ppermute | solution.py:366
  122.8 0.6 dynamic-slice_bitcast_fusion
  123.4 13.3 %all_gather.14.grams = f32[256,64]{1,0:T(8,128)S(1)} all-gather(f32[64,64]{1,0:T(8,128)S(1)} %get-tuple-element.36), channel_id=1, replica_groups=mesh['groups'=2,'rows'=4,'tiles'=2,'cols'=2] {'rows'}, dimensions={0}, use_global_device_ids=true | all-gather | bytes 81920 | tf_op jit(solution)/shard_map/all_gather | solution.py:374
  136.8 2.3 %shard_map.70.factor = f32[64,64]{1,0:T(8,128)S(1)} custom-call(f32[32,2048]{1,0:T(8,128)S(1)} %shard_map.69.after.own, f32[256,64]{1,0:T(8,128)S(1)} %all_gather.14.grams), custom_call_target="tpu_custom_call" | custom-call | tf_op jit(solution)/shard_map/pallas_call | solution.py:25
  139.1 1.5 shard_map.71
  140.6 13.4 %all_gather.15.grams = f32[256,64]{1,0:T(8,128)S(1)} all-gather(f32[64,64]{1,0:T(8,128)S(1)} %get-tuple-element.38), channel_id=1, replica_groups=mesh['groups'=2,'rows'=4,'tiles'=2,'cols'=2] {'rows'}, dimensions={0}, use_global_device_ids=true | all-gather | bytes 81920 | tf_op jit(solution)/shard_map/all_gather | solution.py:374
  154.0 3.9 %shard_map.72 = f32[32,2048]{1,0:T(8,128)} custom-call(s32[3]{0:T(128)S(1)} %pad_add_fusion.1.me, f32[64,2048]{1,0:T(8,128)S(1)} %get-tuple-element.37.mapped, f32[256,64]{1,0:T(8,128)S(1)} %all_gather.15.grams), custom_call_target="tpu_custom_call" | custom-call | tf_op jit(solution)/shard_map/pallas_call | solution.py:25
  (28 shorter events, 1.8 us)
Async XLA Ops:
  24.3 1.4 copy-start
  25.7 4.2 %copy-start.1 = (bf16[2048,384]{1,0:T(8,128)(2,1)S(1)}, bf16[2048,384]{1,0:T(8,128)(2,1)}, u32[]{:S(2)}) copy-start(bf16[2048,384]{1,0:T(8,128)(2,1)} %emb.5) | copy-start | bytes 4718596
  27.9 7.9 %collective-permute-start = (bf16[256,384]{1,0:T(8,128)(2,1)S(1)}, bf16[256,384]{1,0:T(8,128)(2,1)S(1)}, u32[]{:S(2)}, u32[]{:S(2)}) collective-permute-start(bf16[256,384]{1,0:T(8,128)(2,1)S(1)} %get-tuple-element.22), channel_id=1, source_target_pairs={{0,12},{4,0},{8,4},{12,8},{1,13},{5,1},{9,5},{13,9},{2,14},{6,2},{... | collective-permute-start | bytes 589832 | tf_op jit(solution)/shard_map/ppermute | solution.py:366
  27.9 14.4 %collective-permute-start.1 = (bf16[256,384]{1,0:T(8,128)(2,1)S(1)}, bf16[256,384]{1,0:T(8,128)(2,1)S(1)}, u32[]{:S(2)}, u32[]{:S(2)}) collective-permute-start(bf16[256,384]{1,0:T(8,128)(2,1)S(1)} %get-tuple-element.23), channel_id=1, source_target_pairs={{0,8},{4,12},{8,0},{12,4},{1,9},{5,13},{9,1},{13,5},{2,10},{6,14},... | collective-permute-start | bytes 589832 | tf_op jit(solution)/shard_map/ppermute | solution.py:366
  28.2 14.2 %collective-permute-start.2 = (bf16[256,384]{1,0:T(8,128)(2,1)S(1)}, bf16[256,384]{1,0:T(8,128)(2,1)S(1)}, u32[]{:S(2)}, u32[]{:S(2)}) collective-permute-start(bf16[256,384]{1,0:T(8,128)(2,1)S(1)} %get-tuple-element.24), channel_id=1, source_target_pairs={{0,4},{4,8},{8,12},{12,0},{1,5},{5,9},{9,13},{13,1},{2,6},{6,10},{... | collective-permute-start | bytes 589832 | tf_op jit(solution)/shard_map/ppermute | solution.py:366
  31.0 12.6 %collective-permute-start.4 = (f32[1024,128]{1,0:T(8,128)S(1)}, f32[1024,128]{1,0:T(8,128)S(1)}, u32[]{:S(2)}, u32[]{:S(2)}) collective-permute-start(f32[1024,128]{1,0:T(8,128)S(1)} %shard_map.61.mine), channel_id=1, source_target_pairs={{0,1},{1,0},{2,3},{3,2},{4,5},{5,4},{6,7},{7,6},{8,9},{9,8},{10,11... | collective-permute-start | bytes 1572872 | tf_op jit(solution)/shard_map/ppermute | solution.py:366
  43.5 7.8 %copy-start.2 = (f32[2048,32]{0,1:T(8,128)S(1)}, f32[2048,32]{0,1:T(8,128)}, u32[]{:S(2)}) copy-start(f32[2048,32]{0,1:T(8,128)} %param.5) | copy-start | bytes 786436
  43.5 2.0 %collective-permute-start.3 = (f32[1024,128]{1,0:T(8,128)S(1)}, f32[1024,128]{1,0:T(8,128)S(1)}, u32[]{:S(2)}, u32[]{:S(2)}) collective-permute-start(f32[1024,128]{1,0:T(8,128)S(1)} %shard_map.60.mine), channel_id=1, source_target_pairs={{0,1},{1,0},{2,3},{3,2},{4,5},{5,4},{6,7},{7,6},{8,9},{9,8},{10,11... | collective-permute-start | bytes 1572872 | tf_op jit(solution)/shard_map/ppermute | solution.py:366
  47.8 12.9 %all-to-all-start.1 = ((bf16[4,1,256,128]{3,2,1,0:T(8,128)(2,1)}), bf16[4,1,256,128]{3,2,1,0:T(8,128)(2,1)S(1)}, u32[]{:S(2)}, u32[]{:S(2)}) async-start(bf16[4,1,256,128]{3,2,1,0:T(8,128)(2,1)} %get-tuple-element.29), calls=%async_computation.1 | async-start | bytes 524288 | tf_op jit(solution)/shard_map/all_to_all | solution.py:370
  60.6 34.8 %all-to-all-start = ((f32[4,32,512]{2,1,0:T(8,128)}), f32[4,32,512]{2,1,0:T(8,128)S(1)}, u32[]{:S(2)}, u32[]{:S(2)}) async-start(f32[4,32,512]{2,1,0:T(8,128)} %shard_map.64), calls=%async_computation | async-start | bytes 524288 | tf_op jit(solution)/shard_map/all_to_all | solution.py:370
  64.3 31.2 %collective-permute-start.5 = (bf16[4,1,256,128]{3,2,1,0:T(8,128)(2,1)S(1)}, bf16[4,1,256,128]{3,2,1,0:T(8,128)(2,1)S(1)}, u32[]{:S(2)}, u32[]{:S(2)}) collective-permute-start(bf16[4,1,256,128]{3,2,1,0:T(8,128)(2,1)S(1)} %all-to-all-done.1.refs_4_), channel_id=1, source_target_pairs={{0,1},{1,0},{2,3},{3,2},{4,5},{5,4},{6,7},{7,6},{8,9},{9,8},{10,11... | collective-permute-start | bytes 786440 | tf_op jit(solution)/shard_map/ppermute | solution.py:366
  96.8 6.4 %collective-permute-start.6 = (f32[32,2048]{1,0:T(8,128)S(1)}, f32[32,2048]{1,0:T(8,128)S(1)}, u32[]{:S(2)}, u32[]{:S(2)}) collective-permute-start(f32[32,2048]{1,0:T(8,128)S(1)} %get-tuple-element.32.mine), channel_id=1, source_target_pairs={{0,2},{2,0},{1,3},{3,1},{4,6},{6,4},{5,7},{7,5},{8,10},{10,8},{9,1... | collective-permute-start | bytes 786440 | tf_op jit(solution)/shard_map/ppermute | solution.py:366
  104.6 10.2 %all-to-all-start.2 = ((f32[4,32,512]{2,1,0:T(8,128)}), f32[4,32,512]{2,1,0:T(8,128)S(1)}, u32[]{:S(2)}, u32[]{:S(2)}) async-start(f32[4,32,512]{2,1,0:T(8,128)} %get-tuple-element.34), calls=%async_computation.2 | async-start | bytes 524288 | tf_op jit(solution)/shard_map/all_to_all | solution.py:370
  108.0 1.6 %collective-permute-start.7 = (f32[32,2048]{1,0:T(8,128)S(1)}, f32[32,2048]{1,0:T(8,128)S(1)}, u32[]{:S(2)}, u32[]{:S(2)}) collective-permute-start(f32[32,2048]{1,0:T(8,128)S(1)} %get-tuple-element.33.own.refs_0_), channel_id=1, source_target_pairs={{0,1},{1,0},{2,3},{3,2},{4,5},{5,4},{6,7},{7,6},{8,9},{9,8},{10,11... | collective-permute-start | bytes 786440 | tf_op jit(solution)/shard_map/ppermute | solution.py:366
  115.7 6.4 %collective-permute-start.8 = (f32[32,2048]{1,0:T(8,128)S(1)}, f32[32,2048]{1,0:T(8,128)S(1)}, u32[]{:S(2)}, u32[]{:S(2)}) collective-permute-start(f32[32,2048]{1,0:T(8,128)S(1)} %get-tuple-element.35.mine), channel_id=1, source_target_pairs={{0,2},{2,0},{1,3},{3,1},{4,6},{6,4},{5,7},{7,5},{8,10},{10,8},{9,1... | collective-permute-start | bytes 786440 | tf_op jit(solution)/shard_map/ppermute | solution.py:366
  122.8 16.4 %collective-permute-start.9 = (f32[32,2048]{1,0:T(8,128)S(1)}, f32[32,2048]{1,0:T(8,128)S(1)}, u32[]{:S(2)}, u32[]{:S(2)}) collective-permute-start(f32[32,2048]{1,0:T(8,128)S(1)} %shard_map.69.after.own), channel_id=1, source_target_pairs={{0,1},{1,0},{2,3},{3,2},{4,5},{5,4},{6,7},{7,6},{8,9},{9,8},{10,11... | collective-permute-start | bytes 786440 | tf_op jit(solution)/shard_map/ppermute | solution.py:366

commit v3 on v2

--- a/solution.py
+++ b/solution.py
@@ -116,8 +116,9 @@
     )
 
 
-def plan_body(dims, me, lists, emb, idx, *sends):
-    row_count, tile_count, capacity, slots, blocks_here = dims
+def plan_body(dims, me, *refs):
+    row_count, capacity, slots, blocks_here = dims
+    lists, (emb, after, idx), sends = refs[:row_count], refs[row_count : row_count + 3], refs[row_count + 3 :]
     row = me[0]
 
     def clear(i, carry):
@@ -127,12 +128,12 @@
 
     lax.fori_loop(0, slots, clear, 0)
 
-    def ranked(line, want, write):
-        count = lists[line, 2 * slots]
+    def ranked(listed, want, write):
+        count = listed[0, 2 * slots]
 
         def step(s, counts):
-            near = lists[line, s]
-            far = lists[line, slots + s]
+            near = listed[0, s]
+            far = listed[0, slots + s]
             return write(s, near, far, far // blocks_here, s < count, counts)
 
         lax.fori_loop(0, slots, step, (0,) * want)
@@ -156,9 +157,8 @@
         )
 
     for k in range(row_count):
-        line = lax.rem(row - k + row_count, row_count) * tile_count + me[1]
         if k == 0:
-            ranked(line, row_count, write_own)
+            ranked(lists[k], row_count, write_own)
 
         def write_in(s, near, far, owner, live, counts, k=k):
             hit = live & (owner == row)
@@ -171,7 +171,7 @@
 
             return (counts[0] + hit.astype(jnp.int32),)
 
-        ranked(line, 1, write_in)
+        ranked(lists[k], 1, write_in)
     for k in range(1, row_count):
         for j in range(capacity):
             sends[k - 1][j * BLOCK : (j + 1) * BLOCK, :] = emb[at_block(idx[4, k * capacity + j]), :]
@@ -213,10 +213,12 @@
         sums[i : i + 1, :] = jnp.sum(tile, axis=0, keepdims=True)
 
 
-def pair_tile_body(row_count, capacity, per_core, slots, me, idx, mine, other, self_sums, near_tiles, home_tiles, sends, sums):
+def pair_tile_body(row_count, capacity, per_core, slots, me, idx, mine, other, self_sums, ids, after, near_tiles, home_tiles, sends, copies, sums):
     core = me[2]
-    sums[0 : 2 * slots, :] = jnp.zeros((2 * slots, BLOCK), F32)
-    sums[2 * slots :, :] = self_sums[...]
+    own_blocks = self_sums.shape[0]
+    sums[...] = jnp.zeros(sums.shape, F32)
+    sums[2 * slots : 2 * slots + own_blocks, :] = self_sums[...]
+    sums[2 * slots + own_blocks : 2 * slots + own_blocks + 1, :] = ids[...]
     for k in range(row_count):
         for j in range(capacity):
             slot = k * capacity + j
@@ -240,6 +242,9 @@
                 @pl.when(core == j // per_core)
                 def _():
                     sends[lax.rem(me[0] + k, row_count), j % per_core] = pack(tile)
+
+    for i in range(copies.shape[0]):
+        copies[i] = sums[...]
 
 
 def pick_columns(me, idx, row_count, capacity, source, sends):
@@ -302,18 +307,36 @@
             add(idx[4, slot], packed, scaled(values, idx[5, slot]))
 
 
-def first_apply_body(dims, me, idx, onehot, sums, *refs):
+def first_apply_body(dims, id_row, me, idx, sums, *refs):
     inputs, (out, degree, inverse) = refs[:-3], refs[-3:]
-    total = jnp.dot(onehot[...], sums[...], precision=HIGHEST, preferred_element_type=F32)
+    team, rows = sums.shape[0], sums.shape[1]
+    blocks = lax.broadcasted_iota(jnp.int32, (degree.shape[0], rows), 0).astype(F32)
+
+    def part(i):
+        chosen = sums[i]
+        onehot = (blocks == chosen[id_row : id_row + 1, :rows]).astype(F32)
+        return jnp.dot(onehot, chosen, precision=HIGHEST, preferred_element_type=F32)
+
+    if team <= 8:
+        total = functools.reduce(lambda total, i: total + part(i), range(1, team), part(0))
+    else:
+        total = lax.fori_loop(1, team, lambda i, total: total + part(i), part(0))
     degree[...] = total
     inverse[...] = 1.0 / jnp.sqrt(total)
     apply_tiles(dims, me, idx, inverse, *inputs, out)
 
 
+def copy_square(square, out):
+    half = square.shape[0] // 2
+    folded = jnp.concatenate([square[:half], square[half:]], axis=1)
+    for i in range(out.shape[0]):
+        out[i] = folded
+
+
 def second_apply_body(dims, me, idx, inverse, gram_in, *refs):
-    inputs, (out, gram_out) = refs[:-2], refs[-2:]
+    inputs, (out, grams) = refs[:-2], refs[-2:]
     apply_tiles(dims, me, idx, inverse, *inputs, out)
-    gram_out[...] = gram_in[...]
+    copy_square(gram_in[...], grams)
 
 
 def scale_rows(me, blocks_here, inverse, mine, other, out):
@@ -328,7 +351,7 @@
     pick_columns(me, idx, row_count, capacity, out, sends)
 
 
-def last_mapped_body(blocks_here, me, inverse, mine, other, out):
+def last_mapped_body(blocks_here, me, inverse, mine, other, after, out):
     scale_rows(me, blocks_here, inverse, mine, other, out)
 
 
@@ -337,11 +360,9 @@
 
 
 def stacked_sum(stack):
-    n = stack.shape[1]
-    total = stack[:n, :]
-    for i in range(1, stack.shape[0] // n):
-        total = total + stack[i * n : (i + 1) * n, :]
-    return total
+    total = functools.reduce(lambda total, i: total + stack[i], range(1, stack.shape[0]), stack[0])
+    width = total.shape[1] // 2
+    return jnp.concatenate([total[:, :width], total[:, width:]], axis=0)
 
 
 def factor_body(after, grams, out):
@@ -352,7 +373,8 @@
     full = both_columns(me[2], own[...], other[...])
     value = jnp.dot(factor[...], full, precision=HIGHEST, preferred_element_type=F32)
     mapped[...] = value
-    out[...] = gram(value)
+    square = gram(value)
+    copy_square(square, out)
 
 
 def final_body(me, mapped, grams, out):
@@ -366,12 +388,8 @@
     return lax.ppermute(value, axes, [(i, (i + shift) % size) for i in range(size)])
 
 
-def exchange(value):
-    return lax.all_to_all(value, "rows", split_axis=0, concat_axis=0, tiled=True)
-
-
-def gather(value, axes):
-    return lax.all_gather(value, axes, axis=0, tiled=True)
+def exchange(value, axes="rows"):
+    return lax.all_to_all(value, axes, split_axis=0, concat_axis=0, tiled=True)
 
 
 def local(embeddings, start, pair_list, pair_count):
@@ -393,40 +411,31 @@
     block_count = row_count * blocks_here
     others = range(1, row_count)
 
-    lists = jnp.concatenate([pair_list.reshape(1, 2 * slots), pair_count.reshape(1, 1)], axis=1)
-    lists = gather(lists, ("rows", "tiles"))
-    planned = call(
-        functools.partial(plan_body, (row_count, tile_count, capacity, slots, blocks_here)),
-        [sds((6, slots), jnp.int32)] + [sds((capacity * BLOCK, half_features), BF16) for _ in others],
-        [me, lists, embeddings],
-        smem_in=(0, 1),
-        smem_out=(0,),
-    )
-    idx, sends = planned[0], planned[1:]
-    far = [shift_by(sends[k - 1], "rows", row_count, -k) for k in others]
-
+    own_list = jnp.concatenate([pair_list.reshape(1, 2 * slots), pair_count.reshape(1, 1)], axis=1)
+    lists = [own_list] + [shift_by(own_list, "rows", row_count, k) for k in others]
     self_part = call(
         functools.partial(self_distance_body, own_blocks, tile_count),
         sds((own_blocks * BLOCK, BLOCK), F32),
         [me, embeddings],
         smem_in=(0,),
     )
+    planned = call(
+        functools.partial(plan_body, (row_count, capacity, slots, blocks_here)),
+        [sds((6, slots), jnp.int32)] + [sds((capacity * BLOCK, half_features), BF16) for _ in others],
+        [me, *lists, embeddings, self_part],
+        smem_in=range(1 + row_count),
+        any_in=(row_count + 2,),
+        smem_out=(0,),
+    )
+    idx, sends = planned[0], planned[1:]
+    far = [shift_by(sends[k - 1], "rows", row_count, -k) for k in others]
+
     self_other = shift_by(self_part, "cols", core_count, 1)
     self_tiles, self_sums = call(
         functools.partial(self_tile_body, own_blocks),
         [sds((own_blocks, 2 * BLOCK, BLOCK), BF16), sds((own_blocks, BLOCK), F32)],
         [self_part, self_other],
     )
-    values = start.T
-    start_sends = call(
-        functools.partial(pick_body, row_count, capacity),
-        sds((row_count, own_cols, 2 * capacity * BLOCK), F32),
-        [me, idx, values, *far[:-1]],
-        smem_in=(0, 1),
-        any_in=range(3, 2 + row_count),
-    )
-    start_in = exchange(start_sends)
-
     pair_part = call(
         functools.partial(pair_distance_body, row_count, capacity),
         sds((slots * BLOCK, BLOCK), F32),
@@ -434,33 +443,46 @@
         smem_in=(0,),
     )
     pair_other = shift_by(pair_part, "cols", core_count, 1)
-    near_tiles, home_tiles, tile_sends, sums = call(
+    values = start.T
+    start_sends = call(
+        functools.partial(pick_body, row_count, capacity),
+        sds((row_count, own_cols, 2 * capacity * BLOCK), F32),
+        [me, idx, values, pair_part],
+        smem_in=(0, 1),
+        any_in=(3,),
+    )
+    start_in = exchange(start_sends)
+
+    id_row = 2 * slots + own_blocks
+    sum_rows = -(-(id_row + 1) // 8) * 8
+    diagonal_ids = row_index * blocks_here + (
+        jnp.arange(own_blocks, dtype=jnp.int32)[None, :] * tile_count + tile_index
+    )
+    ids = jnp.concatenate([own_list[:, : 2 * slots], diagonal_ids], axis=1).astype(F32)
+    ids = jnp.pad(ids, ((0, 0), (0, BLOCK - id_row)), constant_values=-1.0)
+    near_tiles, home_tiles, tile_sends, sums, _ = call(
         functools.partial(pair_tile_body, row_count, capacity, per_core, slots),
         [
             sds((slots, 2 * BLOCK, BLOCK), BF16),
             sds((capacity, 2 * BLOCK, BLOCK), BF16),
             sds((row_count, per_core, 2 * BLOCK, BLOCK), BF16),
-            sds((2 * slots + own_blocks, BLOCK), F32),
+            sds((team, sum_rows, BLOCK), F32),
+            sds((sum_rows, BLOCK), F32),
         ],
-        [me, idx, pair_part, pair_other, self_sums],
+        [me, idx, pair_part, pair_other, self_sums, ids, start_sends],
         smem_in=(0, 1),
-    )
-    all_sums = gather(sums, ("rows", "tiles"))
+        any_in=(6,),
+    )
+    all_sums = exchange(sums, ("rows", "tiles"))
     sent = exchange(tile_sends)
     shared = shift_by(sent, "cols", core_count, 1)
-
-    team_ids = jnp.arange(team, dtype=jnp.int32)[:, None]
-    diagonal_ids = team_ids // tile_count * blocks_here + (
-        jnp.arange(own_blocks, dtype=jnp.int32)[None, :] * tile_count + team_ids % tile_count
-    )
-    sum_ids = jnp.concatenate([lists[:, : 2 * slots], diagonal_ids], axis=1).reshape(1, -1)
-    onehot = (sum_ids == jnp.arange(block_count, dtype=jnp.int32)[:, None]).astype(F32)
 
     dims = (row_count, capacity, per_core, blocks_here, tile_count)
     tile_args = [near_tiles, home_tiles, sent, shared, self_tiles]
     block_shape = sds((own_cols, rows_here), F32)
     table = sds((block_count, BLOCK), F32)
     square = sds((2 * own_cols, 2 * own_cols), F32)
+    squares = sds((row_count, own_cols, 4 * own_cols), F32)
 
     def team_sum(part):
         if tile_count == 2:
@@ -468,9 +490,9 @@
         return lax.psum(part, "tiles"), jnp.zeros_like(part)
 
     part, degree, inverse = call(
-        functools.partial(first_apply_body, dims),
+        functools.partial(first_apply_body, dims, id_row),
         [block_shape, table, table],
-        [me, idx, onehot, all_sums, values, start_in, *tile_args],
+        [me, idx, all_sums, values, start_in, *tile_args],
         smem_in=(0, 1),
     )
     mine, other = team_sum(part)
@@ -484,29 +506,30 @@
 
     mapped_other = shift_by(mapped, "cols", core_count, 1)
     first_gram = call(gram_body, square, [me, mapped, mapped_other], smem_in=(0,))
-    part, first_gram = call(
+    part, first_grams = call(
         functools.partial(second_apply_body, dims),
-        [block_shape, square],
+        [block_shape, squares],
         [me, idx, inverse, first_gram, mapped, received, *tile_args],
         smem_in=(0, 1),
     )
     mine, other = team_sum(part)
-    first_grams = gather(first_gram, "rows")
+    first_grams = exchange(first_grams)
     second = call(
         functools.partial(last_mapped_body, blocks_here),
         block_shape,
-        [me, inverse, mine, other],
+        [me, inverse, mine, other, first_grams],
         smem_in=(0,),
+        any_in=(4,),
     )
     second_other = shift_by(second, "cols", core_count, 1)
     factor = call(factor_body, square, [second, first_grams], any_in=(0,))
-    full, second_gram = call(
+    full, second_grams = call(
         second_gram_body,
-        [sds((2 * own_cols, rows_here), F32), square],
+        [sds((2 * own_cols, rows_here), F32), squares],
         [me, factor, second, second_other],
         smem_in=(0,),
     )
-    second_grams = gather(second_gram, "rows")
+    second_grams = exchange(second_grams)
     vectors = call(final_body, block_shape, [me, full, second_grams], smem_in=(0,))
     own_degree = lax.dynamic_slice_in_dim(degree, row_index * blocks_here, blocks_here, 0)
     return (vectors.T, own_degree.reshape(rows_here))

time: 158 us -> 120 us (0.76)
  blocking collectives: 80 us -> 31.9 us
  starting transfers between devices: 13.9 us -> 21.4 us
  waiting for transfers between devices: 38.3 us -> 40.3 us
    all_gather x4 -> x0, blocking collectives: 80 us -> none  [gather(): return lax.all_gather(value, axes, axis=0, tiled=True)]
    all_to_all x0 -> x3, blocking collectives: none -> 31.9 us  [exchange(): return lax.all_to_all(value, axes, split_axis=0, concat_axis=0, tiled=True)]
    ppermute x10 -> x13, starting transfers between devices: 3.56 us -> 11.3 us  [shift_by(): lax.ppermute(value, axes, [(i, (i + shift) % size) for i in range(size)])]
    all_to_all x3, waiting for transfers between devices: 12.1 us -> 17.2 us  [exchange(): return lax.all_to_all(value, axes, split_axis=0, concat_axis=0, tiled=True)]
    ppermute x10 -> x13, waiting for transfers between devices: 26.2 us -> 23.1 us  [shift_by(): lax.ppermute(value, axes, [(i, (i + shift) % size) for i in range(size)])]
  transfers between devices with their start and end apart: 13 -> 16, of which waited for: 8 -> 8; matrix products, arithmetic and copies ran while one was open for 1% -> 1% of each run, Pallas kernels for 4% -> 6%
where the time goes in v3:
time: 120 us
  waiting for transfers between devices  40.3 us (34%)
  blocking collectives  31.9 us (27%)
  Pallas kernels  21.9 us (18%)
  starting transfers between devices  21.4 us (18%)
  local copies, waits for them, and re-layouts  2.8 us (2%)
  between operations  1.45 us (1%)
    all_to_all x3, blocking collectives, exchange(): return lax.all_to_all(value, axes, split_axis=0, concat_axis=0, tiled=True)  31.9 us
    ppermute x13, waiting for transfers between devices, shift_by(): lax.ppermute(value, axes, [(i, (i + shift) % size) for i in range(size)])  23.1 us
    pallas_call x14, Pallas kernels, call(): pl.pallas_call(body, out_shape=shapes, in_specs=[SMEM if i in smem_in els...  21.9 us
    all_to_all x3, waiting for transfers between devices, exchange(): return lax.all_to_all(value, axes, split_axis=0, concat_axis=0, tiled=True)  17.2 us
    ppermute x13, starting transfers between devices, shift_by(): lax.ppermute(value, axes, [(i, (i + shift) % size) for i in range(size)])  11.3 us
    all_to_all x3, starting transfers between devices, exchange(): return lax.all_to_all(value, axes, split_axis=0, concat_axis=0, tiled=True)  10.1 us
  transfers between devices with their start and end apart: 16, of which 8 were waited for; matrix products, arithmetic and copies ran while one was open for 1% of the time, Pallas kernels for 6%

profile of v3, /device:TPU:0, one launch (start us, length us, event | category | flops | bytes accessed | tf_op | source)
XLA Modules:
  0.0 119.9 jit_solution(9166096075261455926)
XLA Ops:
  0.6 0.8 reshape.49
  2.1 3.0 %collective-permute-start = (s32[1,17]{1,0:T(1,128)S(1)}, s32[1,17]{1,0:T(1,128)S(1)}, u32[]{:S(2)}, u32[]{:S(2)}) collective-permute-start(s32[1,17]{1,0:T(1,128)S(1)} %pad_add_fusion.1.refs_0_), channel_id=1, source_target_pairs={{0,4},{4,8},{8,12},{12,0},{1,5},{5,9},{9,13},{13,1},{2,6},{6,10},{... | collective-permute-start | bytes 212 | tf_op jit(solution)/shard_map/ppermute | solution.py:388
  5.1 2.6 %collective-permute-start.1 = (s32[1,17]{1,0:T(1,128)S(1)}, s32[1,17]{1,0:T(1,128)S(1)}, u32[]{:S(2)}, u32[]{:S(2)}) collective-permute-start(s32[1,17]{1,0:T(1,128)S(1)} %pad_add_fusion.1.refs_0_), channel_id=1, source_target_pairs={{0,8},{4,12},{8,0},{12,4},{1,9},{5,13},{9,1},{13,5},{2,10},{6,14},... | collective-permute-start | bytes 212 | tf_op jit(solution)/shard_map/ppermute | solution.py:388
  7.7 1.3 %collective-permute-start.2 = (s32[1,17]{1,0:T(1,128)S(1)}, s32[1,17]{1,0:T(1,128)S(1)}, u32[]{:S(2)}, u32[]{:S(2)}) collective-permute-start(s32[1,17]{1,0:T(1,128)S(1)} %pad_add_fusion.1.refs_0_), channel_id=1, source_target_pairs={{0,12},{4,0},{8,4},{12,8},{1,13},{5,1},{9,5},{13,9},{2,14},{6,2},{... | collective-permute-start | bytes 212 | tf_op jit(solution)/shard_map/ppermute | solution.py:388
  9.2 1.4 %copy-done = bf16[2048,384]{1,0:T(8,128)(2,1)S(1)} copy-done((bf16[2048,384]{1,0:T(8,128)(2,1)S(1)}, bf16[2048,384]{1,0:T(8,128)(2,1)}, u32[]{:S(2)}) %copy-start) | copy-done | bytes 1572888
  10.6 1.0 shard_map.59.refs_5_.mine
  11.6 2.0 %shard_map.60 = (s32[6,8]{1,0:T(8,128)S(1)}, bf16[256,384]{1,0:T(8,128)(2,1)S(1)}, bf16[256,384]{1,0:T(8,128)(2,1)S(1)}, bf16[256,384]{1,0:T(8,128)(2,1)S(1)}) custom-call(s32[3]{0:T(128)S(1)} %pad_add_fusion.me, s32[1,17]{1,0:T(1,128)S(1)} %pad_add_fusion.1.refs_0_, s32[1,17]{1,0:T(1,128)S(1)} %collective-permute-done.refs_1_, ...), custom_call_target="tpu_custom_call" | custom-call | tf_op jit(solution)/shard_map/pallas_call | solution.py:25
  13.6 2.8 %collective-permute-start.3 = (bf16[256,384]{1,0:T(8,128)(2,1)S(1)}, bf16[256,384]{1,0:T(8,128)(2,1)S(1)}, u32[]{:S(2)}, u32[]{:S(2)}) collective-permute-start(bf16[256,384]{1,0:T(8,128)(2,1)S(1)} %get-tuple-element.22), channel_id=1, source_target_pairs={{0,12},{4,0},{8,4},{12,8},{1,13},{5,1},{9,5},{13,9},{2,14},{6,2},{... | collective-permute-start | bytes 589832 | tf_op jit(solution)/shard_map/ppermute | solution.py:388
  16.5 0.6 collective-permute-start.5
  17.1 4.7 %collective-permute-done.3.refs_0_ = bf16[256,384]{1,0:T(8,128)(2,1)S(1)} collective-permute-done((bf16[256,384]{1,0:T(8,128)(2,1)S(1)}, bf16[256,384]{1,0:T(8,128)(2,1)S(1)}, u32[]{:S(2)}, u32[]{:S(2)}) %collective-permute-start.3) | collective-permute-done | bytes 196640 | tf_op jit(solution)/shard_map/ppermute | solution.py:388
  21.9 10.4 %collective-permute-done.4.refs_1_ = bf16[256,384]{1,0:T(8,128)(2,1)S(1)} collective-permute-done((bf16[256,384]{1,0:T(8,128)(2,1)S(1)}, bf16[256,384]{1,0:T(8,128)(2,1)S(1)}, u32[]{:S(2)}, u32[]{:S(2)}) %collective-permute-start.4) | collective-permute-done | bytes 196640 | tf_op jit(solution)/shard_map/ppermute | solution.py:388
  32.3 1.2 shard_map.61.refs_0_.mine
  33.6 1.3 %shard_map.63.after = f32[4,32,512]{2,1,0:T(8,128)} custom-call(s32[3]{0:T(128)S(1)} %pad_add_fusion.me, s32[6,8]{1,0:T(8,128)S(1)} %get-tuple-element.21.idx, f32[32,2048]{1,0:T(8,128)S(1)} %bitcast.11, f32[1024,128]{1,0:T(8,128)S(1)} %shard_map.61.refs_0_.mine), custom_call_target="tpu_custom_call" | custom-call | tf_op jit(solution)/shard_map/pallas_call | solution.py:25
  35.4 2.2 %shard_map.64 = (bf16[8,256,128]{2,1,0:T(8,128)(2,1)S(1)}, bf16[2,256,128]{2,1,0:T(8,128)(2,1)S(1)}, bf16[4,1,256,128]{3,2,1,0:T(8,128)(2,1)S(1)}, f32[8,32,128]{2,1,0:T(8,128)S(1)}, f32[32,128]{1,0:T(8,128)}) custom-call(s32[3]{0:T(128)S(1)} %pad_add_fusion.me, s32[6,8]{1,0:T(8,128)S(1)} %get-tuple-element.21.idx, f32[1024,128]{1,0:T(8,128)S(1)} %shard_map.61.refs_0_.mine, ...), custom_call_target="tpu_custom_call" | custom-call | tf_op jit(solution)/shard_map/pallas_call | solution.py:25
  37.6 12.3 %all_to_all.30.refs_4_ = bf16[4,1,256,128]{3,2,1,0:T(8,128)(2,1)S(1)} all-to-all(bf16[4,1,256,128]{3,2,1,0:T(8,128)(2,1)S(1)} %get-tuple-element.29), channel_id=1, replica_groups=mesh['groups'=2,'rows'=4,'tiles'=2,'cols'=2] {'rows'}, dimensions={0} | all-to-all | bytes 524288 | tf_op jit(solution)/shard_map/all_to_all | solution.py:392
  49.9 3.4 %all-to-all-start.1 = ((f32[4,32,512]{2,1,0:T(8,128)}), f32[4,32,512]{2,1,0:T(8,128)S(1)}, u32[]{:S(2)}, u32[]{:S(2)}) async-start(f32[4,32,512]{2,1,0:T(8,128)} %shard_map.63.after), calls=%async_computation.1 | async-start | bytes 524288 | tf_op jit(solution)/shard_map/all_to_all | solution.py:392
  53.4 7.9 %all-to-all-done.1.refs_1_ = f32[4,32,512]{2,1,0:T(8,128)S(1)} async-done(((f32[4,32,512]{2,1,0:T(8,128)}), f32[4,32,512]{2,1,0:T(8,128)S(1)}, u32[]{:S(2)}, u32[]{:S(2)}) %all-to-all-start.1) | async-done | bytes 262176 | tf_op jit(solution)/shard_map/all_to_all | solution.py:392
  61.3 10.6 %all_to_all.31.sums = f32[8,32,128]{2,1,0:T(8,128)S(1)} all-to-all(f32[8,32,128]{2,1,0:T(8,128)S(1)} %get-tuple-element.26), channel_id=1, replica_groups=mesh['groups'=2,'rows'=4,'tiles'=2,'cols'=2] {'rows','tiles'}, dimensions={0} | all-to-all | bytes 262144 | tf_op jit(solution)/shard_map/all_to_all | solution.py:392
  71.9 1.7 %shard_map.65 = (f32[32,2048]{1,0:T(8,128)S(1)}, f32[64,128]{1,0:T(8,128)S(1)}, f32[64,128]{1,0:T(8,128)S(1)}) custom-call(s32[3]{0:T(128)S(1)} %pad_add_fusion.me, s32[6,8]{1,0:T(8,128)S(1)} %get-tuple-element.21.idx, f32[8,32,128]{2,1,0:T(8,128)S(1)} %all_to_all.31.sums, f32[32,2048]{1,0:T(8,128)S(1)} %bitcast.12, ...), custom_call_target="tpu_custom_call" | custom-call | tf_op jit(solution)/shard_map/pallas_call | solution.py:25
  73.9 6.2 %collective-permute-done.9.other = f32[32,2048]{1,0:T(8,128)S(1)} collective-permute-done((f32[32,2048]{1,0:T(8,128)S(1)}, f32[32,2048]{1,0:T(8,128)S(1)}, u32[]{:S(2)}, u32[]{:S(2)}) %collective-permute-start.9) | collective-permute-done | bytes 262176 | tf_op jit(solution)/shard_map/ppermute | solution.py:388
  80.0 1.4 %shard_map.66 = (f32[32,2048]{1,0:T(8,128)S(1)}, f32[4,32,512]{2,1,0:T(8,128)}) custom-call(s32[3]{0:T(128)S(1)} %pad_add_fusion.me, s32[6,8]{1,0:T(8,128)S(1)} %get-tuple-element.21.idx, f32[64,128]{1,0:T(8,128)S(1)} %get-tuple-element.31.inverse, f32[32,2048]{1,0:T(8,128)S(1)} %get-tuple-element.32.mine, f32[32,2048]{1,0:T(8,128)S(1)} %collective-permute-done.9.other), custom_call_target="tpu_custom_call" | custom-call | tf_op jit(solution)/shard_map/pallas_call | solution.py:25
  81.4 3.4 %all-to-all-start.3 = ((f32[4,32,512]{2,1,0:T(8,128)}), f32[4,32,512]{2,1,0:T(8,128)S(1)}, u32[]{:S(2)}, u32[]{:S(2)}) async-start(f32[4,32,512]{2,1,0:T(8,128)} %get-tuple-element.34), calls=%async_computation.3 | async-start | bytes 524288 | tf_op jit(solution)/shard_map/all_to_all | solution.py:392
  84.9 1.5 %collective-permute-done.10.other = f32[32,2048]{1,0:T(8,128)S(1)} collective-permute-done((f32[32,2048]{1,0:T(8,128)S(1)}, f32[32,2048]{1,0:T(8,128)S(1)}, u32[]{:S(2)}, u32[]{:S(2)}) %collective-permute-start.10) | collective-permute-done | bytes 262176 | tf_op jit(solution)/shard_map/ppermute | solution.py:388
  86.4 1.0 shard_map.67.gram_in
  87.4 4.1 %all-to-all-done.3.refs_1_ = f32[4,32,512]{2,1,0:T(8,128)S(1)} async-done(((f32[4,32,512]{2,1,0:T(8,128)}), f32[4,32,512]{2,1,0:T(8,128)S(1)}, u32[]{:S(2)}, u32[]{:S(2)}) %all-to-all-start.3) | async-done | bytes 262176 | tf_op jit(solution)/shard_map/all_to_all | solution.py:392
  91.6 1.0 shard_map.68
  92.8 9.0 %all_to_all.32.after.grams = f32[4,32,128]{2,1,0:T(8,128)S(1)} all-to-all(f32[4,32,128]{2,1,0:T(8,128)S(1)} %get-tuple-element.36), channel_id=1, replica_groups=mesh['groups'=2,'rows'=4,'tiles'=2,'cols'=2] {'rows'}, dimensions={0} | all-to-all | bytes 131072 | tf_op jit(solution)/shard_map/all_to_all | solution.py:392
  102.5 2.3 %shard_map.70.factor = f32[64,64]{1,0:T(8,128)S(1)} custom-call(f32[32,2048]{1,0:T(8,128)S(1)} %shard_map.69.after.own, f32[4,32,128]{2,1,0:T(8,128)S(1)} %all_to_all.32.after.grams), custom_call_target="tpu_custom_call" | custom-call | tf_op jit(solution)/shard_map/pallas_call | solution.py:25
  104.8 2.2 %shard_map.71 = (f32[64,2048]{1,0:T(8,128)S(1)}, f32[4,32,128]{2,1,0:T(8,128)}) custom-call(s32[3]{0:T(128)S(1)} %pad_add_fusion.me, f32[64,64]{1,0:T(8,128)S(1)} %shard_map.70.factor, f32[32,2048]{1,0:T(8,128)S(1)} %shard_map.69.after.own, f32[32,2048]{1,0:T(8,128)S(1)} %collective-permute-done.12.other), custom_call_target="tpu_custom_call" | custom-call | tf_op jit(solution)/shard_map/pallas_call | solution.py:25
  107.0 3.3 %all-to-all-start.5 = ((f32[4,32,128]{2,1,0:T(8,128)}), f32[4,32,128]{2,1,0:T(8,128)S(1)}, u32[]{:S(2)}, u32[]{:S(2)}) async-start(f32[4,32,128]{2,1,0:T(8,128)} %get-tuple-element.38), calls=%async_computation.5 | async-start | bytes 131072 | tf_op jit(solution)/shard_map/all_to_all | solution.py:392
  110.9 5.2 %all-to-all-done.5.grams = f32[4,32,128]{2,1,0:T(8,128)S(1)} async-done(((f32[4,32,128]{2,1,0:T(8,128)}), f32[4,32,128]{2,1,0:T(8,128)S(1)}, u32[]{:S(2)}, u32[]{:S(2)}) %all-to-all-start.5) | async-done | bytes 65568 | tf_op jit(solution)/shard_map/all_to_all | solution.py:392
  116.0 3.9 %shard_map.72 = f32[32,2048]{1,0:T(8,128)} custom-call(s32[3]{0:T(128)S(1)} %pad_add_fusion.me, f32[64,2048]{1,0:T(8,128)S(1)} %get-tuple-element.37.mapped, f32[4,32,128]{2,1,0:T(8,128)S(1)} %all-to-all-done.5.grams), custom_call_target="tpu_custom_call" | custom-call | tf_op jit(solution)/shard_map/pallas_call | solution.py:25
  (30 shorter events, 2.8 us)
Async XLA Ops:
  2.1 9.5 %collective-permute-start = (s32[1,17]{1,0:T(1,128)S(1)}, s32[1,17]{1,0:T(1,128)S(1)}, u32[]{:S(2)}, u32[]{:S(2)}) collective-permute-start(s32[1,17]{1,0:T(1,128)S(1)} %pad_add_fusion.1.refs_0_), channel_id=1, source_target_pairs={{0,4},{4,8},{8,12},{12,0},{1,5},{5,9},{9,13},{13,1},{2,6},{6,10},{... | collective-permute-start | bytes 212 | tf_op jit(solution)/shard_map/ppermute | solution.py:388
  5.1 6.5 %collective-permute-start.1 = (s32[1,17]{1,0:T(1,128)S(1)}, s32[1,17]{1,0:T(1,128)S(1)}, u32[]{:S(2)}, u32[]{:S(2)}) collective-permute-start(s32[1,17]{1,0:T(1,128)S(1)} %pad_add_fusion.1.refs_0_), channel_id=1, source_target_pairs={{0,8},{4,12},{8,0},{12,4},{1,9},{5,13},{9,1},{13,5},{2,10},{6,14},... | collective-permute-start | bytes 212 | tf_op jit(solution)/shard_map/ppermute | solution.py:388
  7.7 3.9 %collective-permute-start.2 = (s32[1,17]{1,0:T(1,128)S(1)}, s32[1,17]{1,0:T(1,128)S(1)}, u32[]{:S(2)}, u32[]{:S(2)}) collective-permute-start(s32[1,17]{1,0:T(1,128)S(1)} %pad_add_fusion.1.refs_0_), channel_id=1, source_target_pairs={{0,12},{4,0},{8,4},{12,8},{1,13},{5,1},{9,5},{13,9},{2,14},{6,2},{... | collective-permute-start | bytes 212 | tf_op jit(solution)/shard_map/ppermute | solution.py:388
  9.2 1.4 %copy-start = (bf16[2048,384]{1,0:T(8,128)(2,1)S(1)}, bf16[2048,384]{1,0:T(8,128)(2,1)}, u32[]{:S(2)}) copy-start(bf16[2048,384]{1,0:T(8,128)(2,1)} %emb.3) | copy-start | bytes 4718596
  11.6 20.7 %copy-start.1 = (bf16[2048,384]{1,0:T(8,128)(2,1)S(1)}, bf16[2048,384]{1,0:T(8,128)(2,1)}, u32[]{:S(2)}) copy-start(bf16[2048,384]{1,0:T(8,128)(2,1)} %emb.3) | copy-start | bytes 4718596
  13.6 20.0 %copy-start.2 = (f32[2048,32]{0,1:T(8,128)S(1)}, f32[2048,32]{0,1:T(8,128)}, u32[]{:S(2)}) copy-start(f32[2048,32]{0,1:T(8,128)} %param.5) | copy-start | bytes 786436
  13.6 8.2 %collective-permute-start.3 = (bf16[256,384]{1,0:T(8,128)(2,1)S(1)}, bf16[256,384]{1,0:T(8,128)(2,1)S(1)}, u32[]{:S(2)}, u32[]{:S(2)}) collective-permute-start(bf16[256,384]{1,0:T(8,128)(2,1)S(1)} %get-tuple-element.22), channel_id=1, source_target_pairs={{0,12},{4,0},{8,4},{12,8},{1,13},{5,1},{9,5},{13,9},{2,14},{6,2},{... | collective-permute-start | bytes 589832 | tf_op jit(solution)/shard_map/ppermute | solution.py:388
  16.5 15.8 %collective-permute-start.4 = (bf16[256,384]{1,0:T(8,128)(2,1)S(1)}, bf16[256,384]{1,0:T(8,128)(2,1)S(1)}, u32[]{:S(2)}, u32[]{:S(2)}) collective-permute-start(bf16[256,384]{1,0:T(8,128)(2,1)S(1)} %get-tuple-element.23), channel_id=1, source_target_pairs={{0,8},{4,12},{8,0},{12,4},{1,9},{5,13},{9,1},{13,5},{2,10},{6,14},... | collective-permute-start | bytes 589832 | tf_op jit(solution)/shard_map/ppermute | solution.py:388
  16.5 15.8 %collective-permute-start.5 = (bf16[256,384]{1,0:T(8,128)(2,1)S(1)}, bf16[256,384]{1,0:T(8,128)(2,1)S(1)}, u32[]{:S(2)}, u32[]{:S(2)}) collective-permute-start(bf16[256,384]{1,0:T(8,128)(2,1)S(1)} %get-tuple-element.24), channel_id=1, source_target_pairs={{0,4},{4,8},{8,12},{12,0},{1,5},{5,9},{9,13},{13,1},{2,6},{6,10},{... | collective-permute-start | bytes 589832 | tf_op jit(solution)/shard_map/ppermute | solution.py:388
  17.1 17.8 %collective-permute-start.7 = (f32[1024,128]{1,0:T(8,128)S(1)}, f32[1024,128]{1,0:T(8,128)S(1)}, u32[]{:S(2)}, u32[]{:S(2)}) collective-permute-start(f32[1024,128]{1,0:T(8,128)S(1)} %shard_map.59.refs_5_.mine), channel_id=1, source_target_pairs={{0,1},{1,0},{2,3},{3,2},{4,5},{5,4},{6,7},{7,6},{8,9},{9,8},{10,11... | collective-permute-start | bytes 1572872 | tf_op jit(solution)/shard_map/ppermute | solution.py:388
  33.4 2.0 %collective-permute-start.6 = (f32[1024,128]{1,0:T(8,128)S(1)}, f32[1024,128]{1,0:T(8,128)S(1)}, u32[]{:S(2)}, u32[]{:S(2)}) collective-permute-start(f32[1024,128]{1,0:T(8,128)S(1)} %shard_map.61.refs_0_.mine), channel_id=1, source_target_pairs={{0,1},{1,0},{2,3},{3,2},{4,5},{5,4},{6,7},{7,6},{8,9},{9,8},{10,11... | collective-permute-start | bytes 1572872 | tf_op jit(solution)/shard_map/ppermute | solution.py:388
  49.9 11.4 %all-to-all-start.1 = ((f32[4,32,512]{2,1,0:T(8,128)}), f32[4,32,512]{2,1,0:T(8,128)S(1)}, u32[]{:S(2)}, u32[]{:S(2)}) async-start(f32[4,32,512]{2,1,0:T(8,128)} %shard_map.63.after), calls=%async_computation.1 | async-start | bytes 524288 | tf_op jit(solution)/shard_map/all_to_all | solution.py:392
  53.3 18.6 %collective-permute-start.8 = (bf16[4,1,256,128]{3,2,1,0:T(8,128)(2,1)S(1)}, bf16[4,1,256,128]{3,2,1,0:T(8,128)(2,1)S(1)}, u32[]{:S(2)}, u32[]{:S(2)}) collective-permute-start(bf16[4,1,256,128]{3,2,1,0:T(8,128)(2,1)S(1)} %all_to_all.30.refs_4_), channel_id=1, source_target_pairs={{0,1},{1,0},{2,3},{3,2},{4,5},{5,4},{6,7},{7,6},{8,9},{9,8},{10,11... | collective-permute-start | bytes 786440 | tf_op jit(solution)/shard_map/ppermute | solution.py:388
  73.6 6.4 %collective-permute-start.9 = (f32[32,2048]{1,0:T(8,128)S(1)}, f32[32,2048]{1,0:T(8,128)S(1)}, u32[]{:S(2)}, u32[]{:S(2)}) collective-permute-start(f32[32,2048]{1,0:T(8,128)S(1)} %get-tuple-element.32.mine), channel_id=1, source_target_pairs={{0,2},{2,0},{1,3},{3,1},{4,6},{6,4},{5,7},{7,5},{8,10},{10,8},{9,1... | collective-permute-start | bytes 786440 | tf_op jit(solution)/shard_map/ppermute | solution.py:388
  81.4 10.2 %all-to-all-start.3 = ((f32[4,32,512]{2,1,0:T(8,128)}), f32[4,32,512]{2,1,0:T(8,128)S(1)}, u32[]{:S(2)}, u32[]{:S(2)}) async-start(f32[4,32,512]{2,1,0:T(8,128)} %get-tuple-element.34), calls=%async_computation.3 | async-start | bytes 524288 | tf_op jit(solution)/shard_map/all_to_all | solution.py:392
  84.8 1.6 %collective-permute-start.10 = (f32[32,2048]{1,0:T(8,128)S(1)}, f32[32,2048]{1,0:T(8,128)S(1)}, u32[]{:S(2)}, u32[]{:S(2)}) collective-permute-start(f32[32,2048]{1,0:T(8,128)S(1)} %get-tuple-element.33.own.refs_0_), channel_id=1, source_target_pairs={{0,1},{1,0},{2,3},{3,2},{4,5},{5,4},{6,7},{7,6},{8,9},{9,8},{10,11... | collective-permute-start | bytes 786440 | tf_op jit(solution)/shard_map/ppermute | solution.py:388
  92.5 9.3 %collective-permute-start.11 = (f32[32,2048]{1,0:T(8,128)S(1)}, f32[32,2048]{1,0:T(8,128)S(1)}, u32[]{:S(2)}, u32[]{:S(2)}) collective-permute-start(f32[32,2048]{1,0:T(8,128)S(1)} %get-tuple-element.35.mine), channel_id=1, source_target_pairs={{0,2},{2,0},{1,3},{3,1},{4,6},{6,4},{5,7},{7,5},{8,10},{10,8},{9,1... | collective-permute-start | bytes 786440 | tf_op jit(solution)/shard_map/ppermute | solution.py:388
  102.4 2.4 %collective-permute-start.12 = (f32[32,2048]{1,0:T(8,128)S(1)}, f32[32,2048]{1,0:T(8,128)S(1)}, u32[]{:S(2)}, u32[]{:S(2)}) collective-permute-start(f32[32,2048]{1,0:T(8,128)S(1)} %shard_map.69.after.own), channel_id=1, source_target_pairs={{0,1},{1,0},{2,3},{3,2},{4,5},{5,4},{6,7},{7,6},{8,9},{9,8},{10,11... | collective-permute-start | bytes 786440 | tf_op jit(solution)/shard_map/ppermute | solution.py:388
  107.0 9.1 %all-to-all-start.5 = ((f32[4,32,128]{2,1,0:T(8,128)}), f32[4,32,128]{2,1,0:T(8,128)S(1)}, u32[]{:S(2)}, u32[]{:S(2)}) async-start(f32[4,32,128]{2,1,0:T(8,128)} %get-tuple-element.38), calls=%async_computation.5 | async-start | bytes 131072 | tf_op jit(solution)/shard_map/all_to_all | solution.py:392

commit v4 on v3

--- a/solution.py
+++ b/solution.py
@@ -65,19 +65,31 @@
     return both[:count] + both[count:]
 
 
-def gram(full):
-    high = full.astype(BF16)
-    rest = full - high.astype(F32)
+def thirds(value):
+    high = value.astype(BF16)
+    rest = value - high.astype(F32)
     middle = rest.astype(BF16)
     low = (rest - middle.astype(F32)).astype(BF16)
-    parts = jnp.concatenate([high, middle, low], axis=0)
+    return jnp.concatenate([high, middle, low], axis=0)
+
+
+def gram(parts):
     cross = lax.dot_general(parts, parts, NT, preferred_element_type=F32)
-    n = full.shape[0]
+    n = parts.shape[0] // 3
     total = None
     for i, j in ((2, 2), (1, 2), (2, 1), (0, 2), (2, 0), (1, 1), (0, 1), (1, 0), (0, 0)):
         piece = cross[i * n : (i + 1) * n, j * n : (j + 1) * n]
         total = piece if total is None else total + piece
     return total
+
+
+def times(left, parts):
+    left = thirds(left)
+    m = left.shape[0] // 3
+    product3 = jnp.dot(
+        jnp.concatenate([left, left, left], axis=1), parts, preferred_element_type=F32
+    )
+    return (product3[2 * m :] + product3[m : 2 * m]) + product3[:m]
 
 
 def lower_inverse(matrix, step=4):
@@ -191,16 +203,18 @@
         out[i * BLOCK : (i + 1) * BLOCK, :] = partial_distance(block, block)
 
 
-def pair_distance_body(row_count, capacity, idx, emb, *refs):
-    out = refs[-1]
-    for k in range(row_count):
+def pair_distance_body(shifts, capacity, idx, emb, *refs):
+    far, out = refs[:-1], refs[-1]
+    if shifts[0] == 0:
+        far = (None, *far)
+    for place, k in enumerate(shifts):
         for j in range(capacity):
-            slot = k * capacity + j
-            left = emb[at_block(idx[0, slot]), :]
+            left = emb[at_block(idx[0, k * capacity + j]), :]
             if k == 0:
                 right = emb[at_block(idx[4, j]), :]
             else:
-                right = refs[k - 1][j * BLOCK : (j + 1) * BLOCK, :]
+                right = far[place][j * BLOCK : (j + 1) * BLOCK, :]
+            slot = place * capacity + j
             out[slot * BLOCK : (slot + 1) * BLOCK, :] = partial_distance(left, right)
 
 
@@ -213,54 +227,57 @@
         sums[i : i + 1, :] = jnp.sum(tile, axis=0, keepdims=True)
 
 
-def pair_tile_body(row_count, capacity, per_core, slots, me, idx, mine, other, self_sums, ids, after, near_tiles, home_tiles, sends, copies, sums):
-    core = me[2]
-    own_blocks = self_sums.shape[0]
-    sums[...] = jnp.zeros(sums.shape, F32)
-    sums[2 * slots : 2 * slots + own_blocks, :] = self_sums[...]
-    sums[2 * slots + own_blocks : 2 * slots + own_blocks + 1, :] = ids[...]
+def pair_tile_body(row_count, capacity, per_core, tile_count, blocks_here, me, idx, mine, other, last_mine, last_other, self_sums, *refs):
+    near_tiles, home_tiles = refs[-2 - row_count : -row_count]
+    sends = refs[-row_count : -1]
+    table = refs[-1]
+    row, tile_index, core = me[0], me[1], me[2]
+    first_slots = mine.shape[0] // BLOCK
+    table[...] = jnp.zeros(table.shape, F32)
+    for i in range(self_sums.shape[0]):
+        table[pl.ds(row * blocks_here + i * tile_count + tile_index, 1), :] = self_sums[i : i + 1, :]
+
+    def add(block, line):
+        place = pl.ds(block, 1)
+        table[place, :] = table[place, :] + line
+
     for k in range(row_count):
         for j in range(capacity):
             slot = k * capacity + j
-            part = slice(slot * BLOCK, (slot + 1) * BLOCK)
-            live = idx[2, slot] > 0
-            tile = jnp.exp(-kernel_gamma * (mine[part, :] + other[part, :] - 2.0))
-            tile = jnp.where(live, tile, 0.0)
+            if slot < first_slots:
+                part = slice(slot * BLOCK, (slot + 1) * BLOCK)
+                distance = mine[part, :] + other[part, :]
+            else:
+                part = slice((slot - first_slots) * BLOCK, (slot - first_slots + 1) * BLOCK)
+                distance = last_mine[part, :] + last_other[part, :]
+            tile = jnp.exp(-kernel_gamma * (distance - 2.0))
+            tile = jnp.where(idx[2, slot] > 0, tile, 0.0)
             turned = tile.T
             near_tiles[slot] = pack(turned)
-
-            @pl.when(live)
-            def _():
-                raw = idx[3, slot]
-                sums[pl.ds(raw, 1), :] = jnp.sum(turned, axis=0, keepdims=True)
-                sums[pl.ds(slots + raw, 1), :] = jnp.sum(tile, axis=0, keepdims=True)
-
+            add(row * blocks_here + idx[0, slot], jnp.sum(turned, axis=0, keepdims=True))
+            add(idx[1, slot], jnp.sum(tile, axis=0, keepdims=True))
             if k == 0:
                 home_tiles[j] = pack(tile)
             else:
 
                 @pl.when(core == j // per_core)
                 def _():
-                    sends[lax.rem(me[0] + k, row_count), j % per_core] = pack(tile)
-
-    for i in range(copies.shape[0]):
-        copies[i] = sums[...]
-
-
-def pick_columns(me, idx, row_count, capacity, source, sends):
+                    sends[k - 1][j % per_core] = pack(tile)
+
+
+def pick_columns(idx, row_count, capacity, source, sends):
     for k in range(1, row_count):
         back = row_count - k
-        there = lax.rem(me[0] + k, row_count)
         for j in range(capacity):
-            sends[there, :, j * BLOCK : (j + 1) * BLOCK] = source[:, at_block(idx[0, k * capacity + j])]
+            sends[k - 1][:, j * BLOCK : (j + 1) * BLOCK] = source[:, at_block(idx[0, k * capacity + j])]
             place = capacity + j
-            sends[there, :, place * BLOCK : (place + 1) * BLOCK] = source[
+            sends[k - 1][:, place * BLOCK : (place + 1) * BLOCK] = source[
                 :, at_block(idx[4, back * capacity + j])
             ]
 
 
-def pick_body(row_count, capacity, me, idx, source, *refs):
-    pick_columns(me, idx, row_count, capacity, source, refs[-1])
+def pick_body(row_count, capacity, idx, source, after, *sends):
+    pick_columns(idx, row_count, capacity, source, sends)
 
 
 def apply_tiles(dims, me, idx, inverse, own, received, near_tiles, home_tiles, sent, shared, self_tiles, out):
@@ -279,16 +296,14 @@
         block = i * tile_count + tile_index
         add(block, self_tiles[i], scaled(own[:, at_block(block)], row * blocks_here + block))
     for k in range(row_count):
-        owner = lax.rem(row + k, row_count)
         for j in range(capacity):
             slot = k * capacity + j
             if k == 0:
                 values = own[:, at_block(idx[4, j])]
             else:
-                values = received[owner, :, (capacity + j) * BLOCK : (capacity + j + 1) * BLOCK]
+                values = received[row_count - k - 1][:, (capacity + j) * BLOCK : (capacity + j + 1) * BLOCK]
             add(idx[0, slot], near_tiles[slot], scaled(values, idx[1, slot]))
     for k in range(row_count):
-        source = lax.rem(row - k + row_count, row_count)
         for j in range(capacity):
             if k == 0:
                 slot = j
@@ -298,45 +313,34 @@
                 inner = j % per_core
                 if j < per_core:
                     place = core * per_core + inner
-                    packed = sent[source, inner]
+                    packed = sent[k - 1][inner]
                 else:
                     place = (1 - core) * per_core + inner
-                    packed = shared[source, inner]
+                    packed = shared[k - 1][inner]
                 slot = k * capacity + place
-                values = received[source, :, at_block(place)]
+                values = received[k - 1][:, at_block(place)]
             add(idx[4, slot], packed, scaled(values, idx[5, slot]))
 
 
-def first_apply_body(dims, id_row, me, idx, sums, *refs):
+def split_inputs(row_count, refs):
+    others = row_count - 1
+    received = refs[1 : 1 + others]
+    near_tiles, home_tiles = refs[1 + others : 3 + others]
+    sent = refs[3 + others : 3 + 2 * others]
+    shared = refs[3 + 2 * others : 3 + 3 * others]
+    return (refs[0], received, near_tiles, home_tiles, sent, shared, refs[-1])
+
+
+def first_apply_body(dims, me, idx, mine, other, *refs):
     inputs, (out, degree, inverse) = refs[:-3], refs[-3:]
-    team, rows = sums.shape[0], sums.shape[1]
-    blocks = lax.broadcasted_iota(jnp.int32, (degree.shape[0], rows), 0).astype(F32)
-
-    def part(i):
-        chosen = sums[i]
-        onehot = (blocks == chosen[id_row : id_row + 1, :rows]).astype(F32)
-        return jnp.dot(onehot, chosen, precision=HIGHEST, preferred_element_type=F32)
-
-    if team <= 8:
-        total = functools.reduce(lambda total, i: total + part(i), range(1, team), part(0))
-    else:
-        total = lax.fori_loop(1, team, lambda i, total: total + part(i), part(0))
+    total = mine[...] + other[...]
     degree[...] = total
     inverse[...] = 1.0 / jnp.sqrt(total)
-    apply_tiles(dims, me, idx, inverse, *inputs, out)
-
-
-def copy_square(square, out):
-    half = square.shape[0] // 2
-    folded = jnp.concatenate([square[:half], square[half:]], axis=1)
-    for i in range(out.shape[0]):
-        out[i] = folded
-
-
-def second_apply_body(dims, me, idx, inverse, gram_in, *refs):
-    inputs, (out, grams) = refs[:-2], refs[-2:]
-    apply_tiles(dims, me, idx, inverse, *inputs, out)
-    copy_square(gram_in[...], grams)
+    apply_tiles(dims, me, idx, inverse, *split_inputs(dims[0], inputs), out)
+
+
+def second_apply_body(dims, me, idx, inverse, *refs):
+    apply_tiles(dims, me, idx, inverse, *split_inputs(dims[0], refs[:-1]), refs[-1])
 
 
 def scale_rows(me, blocks_here, inverse, mine, other, out):
@@ -346,50 +350,61 @@
         out[:, part] = (mine[:, part] + other[:, part]) * row
 
 
-def mapped_body(row_count, capacity, blocks_here, me, idx, inverse, mine, other, out, sends):
+def mapped_body(row_count, capacity, blocks_here, me, idx, inverse, mine, other, out, *sends):
     scale_rows(me, blocks_here, inverse, mine, other, out)
-    pick_columns(me, idx, row_count, capacity, out, sends)
+    pick_columns(idx, row_count, capacity, out, sends)
 
 
 def last_mapped_body(blocks_here, me, inverse, mine, other, after, out):
     scale_rows(me, blocks_here, inverse, mine, other, out)
 
 
-def gram_body(me, own, other, out):
-    out[...] = gram(both_columns(me[2], own[...], other[...]))
-
-
-def stacked_sum(stack):
-    total = functools.reduce(lambda total, i: total + stack[i], range(1, stack.shape[0]), stack[0])
+def folded(square):
+    half = square.shape[0] // 2
+    return jnp.concatenate([square[:half], square[half:]], axis=1)
+
+
+def unfolded(mine, other):
+    total = mine[...] + other[...]
     width = total.shape[1] // 2
     return jnp.concatenate([total[:, :width], total[:, width:]], axis=0)
 
 
-def factor_body(after, grams, out):
-    out[...] = lower_inverse(stacked_sum(grams))
+def gram_body(me, own, other, out):
+    out[...] = folded(gram(thirds(both_columns(me[2], own[...], other[...]))))
+
+
+def factor_body(after, mine, other, out):
+    out[...] = lower_inverse(unfolded(mine, other))
 
 
 def second_gram_body(me, factor, own, other, mapped, out):
     full = both_columns(me[2], own[...], other[...])
-    value = jnp.dot(factor[...], full, precision=HIGHEST, preferred_element_type=F32)
-    mapped[...] = value
-    square = gram(value)
-    copy_square(square, out)
-
-
-def final_body(me, mapped, grams, out):
-    factor = lower_inverse(stacked_sum(grams))
+    parts = thirds(times(factor[...], thirds(full)))
+    mapped[...] = parts
+    out[...] = folded(gram(parts))
+
+
+def final_body(me, mapped, mine, other, out):
+    factor = lower_inverse(unfolded(mine, other))
     own_cols = out.shape[0]
     part = jnp.where(me[2] == 0, factor[:own_cols], factor[own_cols:])
-    out[...] = jnp.dot(part, mapped[...], precision=HIGHEST, preferred_element_type=F32)
+    out[...] = times(part, mapped[...])
 
 
 def shift_by(value, axes, size, shift):
     return lax.ppermute(value, axes, [(i, (i + shift) % size) for i in range(size)])
 
 
-def exchange(value, axes="rows"):
-    return lax.all_to_all(value, axes, split_axis=0, concat_axis=0, tiled=True)
+def pair_sum(value, axes):
+    terms = None
+    steps = [(name, 1 << bit) for name in axes for bit in range((lax.axis_size(name) - 1).bit_length())]
+    for name, flip in steps:
+        if terms is not None:
+            value = terms[0] + terms[1]
+        size = lax.axis_size(name)
+        terms = (value, lax.ppermute(value, name, [(i, i ^ flip) for i in range(size)]))
+    return terms
 
 
 def local(embeddings, start, pair_list, pair_count):
@@ -407,7 +422,6 @@
     per_core = capacity // core_count
     own_blocks = blocks_here // tile_count
     own_cols = start.shape[1]
-    team = row_count * tile_count
     block_count = row_count * blocks_here
     others = range(1, row_count)
 
@@ -436,101 +450,95 @@
         [sds((own_blocks, 2 * BLOCK, BLOCK), BF16), sds((own_blocks, BLOCK), F32)],
         [self_part, self_other],
     )
-    pair_part = call(
-        functools.partial(pair_distance_body, row_count, capacity),
-        sds((slots * BLOCK, BLOCK), F32),
-        [idx, embeddings, *far],
-        smem_in=(0,),
-    )
-    pair_other = shift_by(pair_part, "cols", core_count, 1)
     values = start.T
     start_sends = call(
         functools.partial(pick_body, row_count, capacity),
-        sds((row_count, own_cols, 2 * capacity * BLOCK), F32),
-        [me, idx, values, pair_part],
+        [sds((own_cols, 2 * capacity * BLOCK), F32) for _ in others],
+        [idx, values, far[0]],
+        smem_in=(0,),
+        any_in=(2,),
+    )
+    start_in = [shift_by(start_sends[k - 1], "rows", row_count, k) for k in others]
+
+    first_part = call(
+        functools.partial(pair_distance_body, range(row_count - 1), capacity),
+        sds(((slots - capacity) * BLOCK, BLOCK), F32),
+        [idx, embeddings, *far[:-1]],
+        smem_in=(0,),
+    )
+    first_other = shift_by(first_part, "cols", core_count, 1)
+    last_part = call(
+        functools.partial(pair_distance_body, (row_count - 1,), capacity),
+        sds((capacity * BLOCK, BLOCK), F32),
+        [idx, embeddings, far[-1]],
+        smem_in=(0,),
+    )
+    last_other = shift_by(last_part, "cols", core_count, 1)
+    table = sds((block_count, BLOCK), F32)
+    tiles = call(
+        functools.partial(pair_tile_body, row_count, capacity, per_core, tile_count, blocks_here),
+        [sds((slots, 2 * BLOCK, BLOCK), BF16), sds((capacity, 2 * BLOCK, BLOCK), BF16)]
+        + [sds((per_core, 2 * BLOCK, BLOCK), BF16) for _ in others]
+        + [table],
+        [me, idx, first_part, first_other, last_part, last_other, self_sums, *start_in],
         smem_in=(0, 1),
-        any_in=(3,),
-    )
-    start_in = exchange(start_sends)
-
-    id_row = 2 * slots + own_blocks
-    sum_rows = -(-(id_row + 1) // 8) * 8
-    diagonal_ids = row_index * blocks_here + (
-        jnp.arange(own_blocks, dtype=jnp.int32)[None, :] * tile_count + tile_index
-    )
-    ids = jnp.concatenate([own_list[:, : 2 * slots], diagonal_ids], axis=1).astype(F32)
-    ids = jnp.pad(ids, ((0, 0), (0, BLOCK - id_row)), constant_values=-1.0)
-    near_tiles, home_tiles, tile_sends, sums, _ = call(
-        functools.partial(pair_tile_body, row_count, capacity, per_core, slots),
-        [
-            sds((slots, 2 * BLOCK, BLOCK), BF16),
-            sds((capacity, 2 * BLOCK, BLOCK), BF16),
-            sds((row_count, per_core, 2 * BLOCK, BLOCK), BF16),
-            sds((team, sum_rows, BLOCK), F32),
-            sds((sum_rows, BLOCK), F32),
-        ],
-        [me, idx, pair_part, pair_other, self_sums, ids, start_sends],
+        any_in=range(7, 6 + row_count),
+    )
+    near_tiles, home_tiles, tile_sends = tiles[0], tiles[1], tiles[2:-1]
+    degree_terms = pair_sum(tiles[-1], ("tiles", "rows"))
+    sent = [shift_by(tile_sends[k - 1], "rows", row_count, k) for k in others]
+    shared = [shift_by(tile, "cols", core_count, 1) for tile in sent]
+
+    dims = (row_count, capacity, per_core, blocks_here, tile_count)
+    tile_args = [near_tiles, home_tiles, *sent, *shared, self_tiles]
+    block_shape = sds((own_cols, rows_here), F32)
+    square = sds((2 * own_cols, 2 * own_cols), F32)
+    folded_square = sds((own_cols, 4 * own_cols), F32)
+
+    part, degree, inverse = call(
+        functools.partial(first_apply_body, dims),
+        [block_shape, table, table],
+        [me, idx, *degree_terms, values, *start_in, *tile_args],
         smem_in=(0, 1),
-        any_in=(6,),
-    )
-    all_sums = exchange(sums, ("rows", "tiles"))
-    sent = exchange(tile_sends)
-    shared = shift_by(sent, "cols", core_count, 1)
-
-    dims = (row_count, capacity, per_core, blocks_here, tile_count)
-    tile_args = [near_tiles, home_tiles, sent, shared, self_tiles]
-    block_shape = sds((own_cols, rows_here), F32)
-    table = sds((block_count, BLOCK), F32)
-    square = sds((2 * own_cols, 2 * own_cols), F32)
-    squares = sds((row_count, own_cols, 4 * own_cols), F32)
-
-    def team_sum(part):
-        if tile_count == 2:
-            return part, shift_by(part, "tiles", 2, 1)
-        return lax.psum(part, "tiles"), jnp.zeros_like(part)
-
-    part, degree, inverse = call(
-        functools.partial(first_apply_body, dims, id_row),
-        [block_shape, table, table],
-        [me, idx, all_sums, values, start_in, *tile_args],
-        smem_in=(0, 1),
-    )
-    mine, other = team_sum(part)
-    mapped, sends = call(
+    )
+    mine, other = pair_sum(part, ("tiles",))
+    first = call(
         functools.partial(mapped_body, row_count, capacity, blocks_here),
-        [block_shape, sds((row_count, own_cols, 2 * capacity * BLOCK), F32)],
+        [block_shape] + [sds((own_cols, 2 * capacity * BLOCK), F32) for _ in others],
         [me, idx, inverse, mine, other],
         smem_in=(0, 1),
     )
-    received = exchange(sends)
+    mapped, sends = first[0], first[1:]
+    received = [shift_by(sends[k - 1], "rows", row_count, k) for k in others]
 
     mapped_other = shift_by(mapped, "cols", core_count, 1)
-    first_gram = call(gram_body, square, [me, mapped, mapped_other], smem_in=(0,))
-    part, first_grams = call(
+    first_gram = call(gram_body, folded_square, [me, mapped, mapped_other], smem_in=(0,))
+    gram_terms = pair_sum(first_gram, ("rows",))
+    part = call(
         functools.partial(second_apply_body, dims),
-        [block_shape, squares],
-        [me, idx, inverse, first_gram, mapped, received, *tile_args],
+        block_shape,
+        [me, idx, inverse, mapped, *received, *tile_args],
         smem_in=(0, 1),
     )
-    mine, other = team_sum(part)
-    first_grams = exchange(first_grams)
+    mine, other = pair_sum(part, ("tiles",))
     second = call(
         functools.partial(last_mapped_body, blocks_here),
         block_shape,
-        [me, inverse, mine, other, first_grams],
+        [me, inverse, mine, other, gram_terms[0]],
         smem_in=(0,),
         any_in=(4,),
     )
     second_other = shift_by(second, "cols", core_count, 1)
-    factor = call(factor_body, square, [second, first_grams], any_in=(0,))
-    full, second_grams = call(
+    factor = call(factor_body, square, [second, *gram_terms], any_in=(0,))
+    full, second_gram = call(
         second_gram_body,
-        [sds((2 * own_cols, rows_here), F32), squares],
+        [sds((6 * own_cols, rows_here), BF16), folded_square],
         [me, factor, second, second_other],
         smem_in=(0,),
     )
-    second_grams = exchange(second_grams)
-    vectors = call(final_body, block_shape, [me, full, second_grams], smem_in=(0,))
+    vectors = call(
+        final_body, block_shape, [me, full, *pair_sum(second_gram, ("rows",))], smem_in=(0,)
+    )
     own_degree = lax.dynamic_slice_in_dim(degree, row_index * blocks_here, blocks_here, 0)
     return (vectors.T, own_degree.reshape(rows_here))
 

time: 120 us -> 114 us (0.950)
  blocking collectives: 31.9 us -> 0 us
  starting transfers between devices: 21.4 us -> 36.2 us
  waiting for transfers between devices: 40.3 us -> 53.9 us
  Pallas kernels: 21.9 us -> 19 us
    all_to_all x3 -> x0, blocking collectives: 31.9 us -> none  [exchange(): return lax.all_to_all(value, axes, split_axis=0, concat_axis=0, tiled=True)]
    ppermute x0 -> x9, waiting for transfers between devices: none -> 22.1 us  [pair_sum(): lax.ppermute(value, name, [(i, i ^ flip) for i in range(size)])]
    all_to_all x3 -> x0, waiting for transfers between devices: 17.2 us -> none  [exchange(): return lax.all_to_all(value, axes, split_axis=0, concat_axis=0, tiled=True)]
    ppermute x0 -> x9, starting transfers between devices: none -> 14.5 us  [pair_sum(): lax.ppermute(value, name, [(i, i ^ flip) for i in range(size)])]
    ppermute x13 -> x23, starting transfers between devices: 11.3 us -> 21.7 us  [shift_by(): lax.ppermute(value, axes, [(i, (i + shift) % size) for i in range(size)])]
    all_to_all x3 -> x0, starting transfers between devices: 10.1 us -> none  [exchange(): return lax.all_to_all(value, axes, split_axis=0, concat_axis=0, tiled=True)]
    ppermute x13 -> x23, waiting for transfers between devices: 23.1 us -> 31.7 us  [shift_by(): lax.ppermute(value, axes, [(i, (i + shift) % size) for i in range(size)])]
    pallas_call x14 -> x15, Pallas kernels: 21.9 us -> 19 us  [call(): pl.pallas_call(body, out_shape=shapes, in_specs=[SMEM if i in smem_in els...]
  transfers between devices with their start and end apart: 16 -> 32, of which waited for: 8 -> 17; matrix products, arithmetic and copies ran while one was open for 1% -> 1% of each run, Pallas kernels for 6% -> 9%
where the time goes in v4:
time: 114 us
  waiting for transfers between devices  53.9 us (47%)
  starting transfers between devices  36.2 us (32%)
  Pallas kernels  19 us (17%)
  local copies, waits for them, and re-layouts  2.78 us (2%)
  between operations  1.45 us (1%)
    ppermute x23, waiting for transfers between devices, shift_by(): lax.ppermute(value, axes, [(i, (i + shift) % size) for i in range(size)])  31.7 us
    ppermute x9, waiting for transfers between devices, pair_sum(): lax.ppermute(value, name, [(i, i ^ flip) for i in range(size)])  22.1 us
    ppermute x23, starting transfers between devices, shift_by(): lax.ppermute(value, axes, [(i, (i + shift) % size) for i in range(size)])  21.7 us
    pallas_call x15, Pallas kernels, call(): pl.pallas_call(body, out_shape=shapes, in_specs=[SMEM if i in smem_in els...  19 us
    ppermute x9, starting transfers between devices, pair_sum(): lax.ppermute(value, name, [(i, i ^ flip) for i in range(size)])  14.5 us
  transfers between devices with their start and end apart: 32, of which 17 were waited for; matrix products, arithmetic and copies ran while one was open for 1% of the time, Pallas kernels for 9%

profile of v4, /device:TPU:0, one launch (start us, length us, event | category | flops | bytes accessed | tf_op | source)
XLA Modules:
  0.0 113.5 jit_solution(12497342899926596117)
XLA Ops:
  2.1 5.0 %collective-permute-start.2 = (s32[1,17]{1,0:T(1,128)S(1)}, s32[1,17]{1,0:T(1,128)S(1)}, u32[]{:S(2)}, u32[]{:S(2)}) collective-permute-start(s32[1,17]{1,0:T(1,128)S(1)} %pad_add_fusion.1.refs_0_), channel_id=1, source_target_pairs={{0,12},{4,0},{8,4},{12,8},{1,13},{5,1},{9,5},{13,9},{2,14},{6,2},{... | collective-permute-start | bytes 212 | tf_op jit(solution)/shard_map/ppermute | solution.py:396
  8.3 1.4 %copy-done = bf16[2048,384]{1,0:T(8,128)(2,1)S(1)} copy-done((bf16[2048,384]{1,0:T(8,128)(2,1)S(1)}, bf16[2048,384]{1,0:T(8,128)(2,1)}, u32[]{:S(2)}) %copy-start) | copy-done | bytes 1572888
  12.5 2.0 %shard_map.60 = (s32[6,8]{1,0:T(8,128)S(1)}, bf16[256,384]{1,0:T(8,128)(2,1)S(1)}, bf16[256,384]{1,0:T(8,128)(2,1)S(1)}, bf16[256,384]{1,0:T(8,128)(2,1)S(1)}) custom-call(s32[3]{0:T(128)S(1)} %pad_add_fusion.me, s32[1,17]{1,0:T(1,128)S(1)} %pad_add_fusion.1.refs_0_, s32[1,17]{1,0:T(1,128)S(1)} %collective-permute-done.refs_1_, ...), custom_call_target="tpu_custom_call" | custom-call | tf_op jit(solution)/shard_map/pallas_call | solution.py:25
  16.8 4.1 %collective-permute-done.3.refs_0_.after = bf16[256,384]{1,0:T(8,128)(2,1)S(1)} collective-permute-done((bf16[256,384]{1,0:T(8,128)(2,1)S(1)}, bf16[256,384]{1,0:T(8,128)(2,1)S(1)}, u32[]{:S(2)}, u32[]{:S(2)}) %collective-permute-start.3) | collective-permute-done | bytes 196640 | tf_op jit(solution)/shard_map/ppermute | solution.py:396
  20.9 9.5 %collective-permute-done.4.refs_1_ = bf16[256,384]{1,0:T(8,128)(2,1)S(1)} collective-permute-done((bf16[256,384]{1,0:T(8,128)(2,1)S(1)}, bf16[256,384]{1,0:T(8,128)(2,1)S(1)}, u32[]{:S(2)}, u32[]{:S(2)}) %collective-permute-start.4) | collective-permute-done | bytes 196640 | tf_op jit(solution)/shard_map/ppermute | solution.py:396
  31.7 9.0 %collective-permute-done.6.refs_0_ = bf16[256,384]{1,0:T(8,128)(2,1)S(1)} collective-permute-done((bf16[256,384]{1,0:T(8,128)(2,1)S(1)}, bf16[256,384]{1,0:T(8,128)(2,1)S(1)}, u32[]{:S(2)}, u32[]{:S(2)}) %collective-permute-start.6) | collective-permute-done | bytes 196640 | tf_op jit(solution)/shard_map/ppermute | solution.py:396
  43.2 3.0 %collective-permute-start.11 = (f32[32,512]{1,0:T(8,128)S(1)}, f32[32,512]{1,0:T(8,128)S(1)}, u32[]{:S(2)}, u32[]{:S(2)}) collective-permute-start(f32[32,512]{1,0:T(8,128)S(1)} %get-tuple-element.33), channel_id=1, source_target_pairs={{0,12},{4,0},{8,4},{12,8},{1,13},{5,1},{9,5},{13,9},{2,14},{6,2},{... | collective-permute-start | bytes 196616 | tf_op jit(solution)/shard_map/ppermute | solution.py:396
  46.3 2.8 %collective-permute-done.9.refs_0_.refs_1_ = f32[32,512]{1,0:T(8,128)S(1)} collective-permute-done((f32[32,512]{1,0:T(8,128)S(1)}, f32[32,512]{1,0:T(8,128)S(1)}, u32[]{:S(2)}, u32[]{:S(2)}) %collective-permute-start.9) | collective-permute-done | bytes 65568 | tf_op jit(solution)/shard_map/ppermute | solution.py:396
  49.1 1.9 %collective-permute-done.10.refs_1_.refs_2_ = f32[32,512]{1,0:T(8,128)S(1)} collective-permute-done((f32[32,512]{1,0:T(8,128)S(1)}, f32[32,512]{1,0:T(8,128)S(1)}, u32[]{:S(2)}, u32[]{:S(2)}) %collective-permute-start.10) | collective-permute-done | bytes 65568 | tf_op jit(solution)/shard_map/ppermute | solution.py:396
  52.4 1.6 %collective-permute-start.15 = (bf16[1,256,128]{2,1,0:T(8,128)(2,1)S(1)}, bf16[1,256,128]{2,1,0:T(8,128)(2,1)S(1)}, u32[]{:S(2)}, u32[]{:S(2)}) collective-permute-start(bf16[1,256,128]{2,1,0:T(8,128)(2,1)S(1)} %get-tuple-element.37), channel_id=1, source_target_pairs={{0,4},{4,8},{8,12},{12,0},{1,5},{5,9},{9,13},{13,1},{2,6},{6,10},{... | collective-permute-start | bytes 196616 | tf_op jit(solution)/shard_map/ppermute | solution.py:396
  56.4 1.5 %collective-permute-start.12 = (f32[64,128]{1,0:T(8,128)S(1)}, f32[64,128]{1,0:T(8,128)S(1)}, u32[]{:S(2)}, u32[]{:S(2)}) collective-permute-start(f32[64,128]{1,0:T(8,128)S(1)} %get-tuple-element.34), channel_id=1, source_target_pairs={{0,2},{2,0},{1,3},{3,1},{4,6},{6,4},{5,7},{7,5},{8,10},{10,8},{9,1... | collective-permute-start | bytes 98312 | tf_op jit(solution)/shard_map/ppermute | solution.py:406
  57.9 2.4 %collective-permute-done.12 = f32[64,128]{1,0:T(8,128)S(1)} collective-permute-done((f32[64,128]{1,0:T(8,128)S(1)}, f32[64,128]{1,0:T(8,128)S(1)}, u32[]{:S(2)}, u32[]{:S(2)}) %collective-permute-start.12) | collective-permute-done | bytes 32800 | tf_op jit(solution)/shard_map/ppermute | solution.py:406
  61.7 2.6 %collective-permute-done.13 = f32[64,128]{1,0:T(8,128)S(1)} collective-permute-done((f32[64,128]{1,0:T(8,128)S(1)}, f32[64,128]{1,0:T(8,128)S(1)}, u32[]{:S(2)}, u32[]{:S(2)}) %collective-permute-start.13) | collective-permute-done | bytes 32800 | tf_op jit(solution)/shard_map/ppermute | solution.py:406
  64.3 1.9 %collective-permute-start.14 = (f32[64,128]{1,0:T(8,128)S(1)}, f32[64,128]{1,0:T(8,128)S(1)}, u32[]{:S(2)}, u32[]{:S(2)}) collective-permute-start(f32[64,128]{1,0:T(8,128)S(1)} %add.16.mine), channel_id=1, source_target_pairs={{0,8},{4,12},{8,0},{12,4},{1,9},{5,13},{9,1},{13,5},{2,10},{6,14},... | collective-permute-start | bytes 98312 | tf_op jit(solution)/shard_map/ppermute | solution.py:406
  66.1 3.3 %collective-permute-done.14.other = f32[64,128]{1,0:T(8,128)S(1)} collective-permute-done((f32[64,128]{1,0:T(8,128)S(1)}, f32[64,128]{1,0:T(8,128)S(1)}, u32[]{:S(2)}, u32[]{:S(2)}) %collective-permute-start.14) | collective-permute-done | bytes 32800 | tf_op jit(solution)/shard_map/ppermute | solution.py:406
  70.5 1.6 %collective-permute-start.21 = (f32[32,2048]{1,0:T(8,128)S(1)}, f32[32,2048]{1,0:T(8,128)S(1)}, u32[]{:S(2)}, u32[]{:S(2)}) collective-permute-start(f32[32,2048]{1,0:T(8,128)S(1)} %get-tuple-element.42.mine), channel_id=1, source_target_pairs={{0,2},{2,0},{1,3},{3,1},{4,6},{6,4},{5,7},{7,5},{8,10},{10,8},{9,1... | collective-permute-start | bytes 786440 | tf_op jit(solution)/shard_map/ppermute | solution.py:406
  72.0 4.9 %collective-permute-done.21.other = f32[32,2048]{1,0:T(8,128)S(1)} collective-permute-done((f32[32,2048]{1,0:T(8,128)S(1)}, f32[32,2048]{1,0:T(8,128)S(1)}, u32[]{:S(2)}, u32[]{:S(2)}) %collective-permute-start.21) | collective-permute-done | bytes 262176 | tf_op jit(solution)/shard_map/ppermute | solution.py:406
  78.1 1.7 %collective-permute-start.23 = (f32[32,512]{1,0:T(8,128)S(1)}, f32[32,512]{1,0:T(8,128)S(1)}, u32[]{:S(2)}, u32[]{:S(2)}) collective-permute-start(f32[32,512]{1,0:T(8,128)S(1)} %get-tuple-element.45), channel_id=1, source_target_pairs={{0,8},{4,12},{8,0},{12,4},{1,9},{5,13},{9,1},{13,5},{2,10},{6,14},... | collective-permute-start | bytes 196616 | tf_op jit(solution)/shard_map/ppermute | solution.py:396
  79.8 2.3 %collective-permute-start.24 = (f32[32,512]{1,0:T(8,128)S(1)}, f32[32,512]{1,0:T(8,128)S(1)}, u32[]{:S(2)}, u32[]{:S(2)}) collective-permute-start(f32[32,512]{1,0:T(8,128)S(1)} %get-tuple-element.46), channel_id=1, source_target_pairs={{0,12},{4,0},{8,4},{12,8},{1,13},{5,1},{9,5},{13,9},{2,14},{6,2},{... | collective-permute-start | bytes 196616 | tf_op jit(solution)/shard_map/ppermute | solution.py:396
  82.1 1.8 %collective-permute-done.22.refs_1_ = f32[32,512]{1,0:T(8,128)S(1)} collective-permute-done((f32[32,512]{1,0:T(8,128)S(1)}, f32[32,512]{1,0:T(8,128)S(1)}, u32[]{:S(2)}, u32[]{:S(2)}) %collective-permute-start.22) | collective-permute-done | bytes 65568 | tf_op jit(solution)/shard_map/ppermute | solution.py:396
  85.7 1.6 %collective-permute-start.25 = (f32[32,2048]{1,0:T(8,128)S(1)}, f32[32,2048]{1,0:T(8,128)S(1)}, u32[]{:S(2)}, u32[]{:S(2)}) collective-permute-start(f32[32,2048]{1,0:T(8,128)S(1)} %shard_map.68.mine), channel_id=1, source_target_pairs={{0,2},{2,0},{1,3},{3,1},{4,6},{6,4},{5,7},{7,5},{8,10},{10,8},{9,1... | collective-permute-start | bytes 786440 | tf_op jit(solution)/shard_map/ppermute | solution.py:406
  88.3 1.6 %collective-permute-start.27 = (f32[32,128]{1,0:T(8,128)S(1)}, f32[32,128]{1,0:T(8,128)S(1)}, u32[]{:S(2)}, u32[]{:S(2)}) collective-permute-start(f32[32,128]{1,0:T(8,128)S(1)} %shard_map.69), channel_id=1, source_target_pairs={{0,4},{4,0},{8,12},{12,8},{1,5},{5,1},{9,13},{13,9},{2,6},{6,2},{1... | collective-permute-start | bytes 49160 | tf_op jit(solution)/shard_map/ppermute | solution.py:406
  90.0 2.1 %collective-permute-done.27 = f32[32,128]{1,0:T(8,128)S(1)} collective-permute-done((f32[32,128]{1,0:T(8,128)S(1)}, f32[32,128]{1,0:T(8,128)S(1)}, u32[]{:S(2)}, u32[]{:S(2)}) %collective-permute-start.27) | collective-permute-done | bytes 16416 | tf_op jit(solution)/shard_map/ppermute | solution.py:406
  92.8 2.1 %collective-permute-start.28 = (f32[32,128]{1,0:T(8,128)S(1)}, f32[32,128]{1,0:T(8,128)S(1)}, u32[]{:S(2)}, u32[]{:S(2)}) collective-permute-start(f32[32,128]{1,0:T(8,128)S(1)} %add.17.after.mine), channel_id=1, source_target_pairs={{0,8},{4,12},{8,0},{12,4},{1,9},{5,13},{9,1},{13,5},{2,10},{6,14},... | collective-permute-start | bytes 49160 | tf_op jit(solution)/shard_map/ppermute | solution.py:406
  94.8 2.6 %collective-permute-done.28.other = f32[32,128]{1,0:T(8,128)S(1)} collective-permute-done((f32[32,128]{1,0:T(8,128)S(1)}, f32[32,128]{1,0:T(8,128)S(1)}, u32[]{:S(2)}, u32[]{:S(2)}) %collective-permute-start.28) | collective-permute-done | bytes 16416 | tf_op jit(solution)/shard_map/ppermute | solution.py:406
  97.5 2.3 %shard_map.71.factor = f32[64,64]{1,0:T(8,128)S(1)} custom-call(f32[32,2048]{1,0:T(8,128)S(1)} %shard_map.70.after.own, f32[32,128]{1,0:T(8,128)S(1)} %add.17.after.mine, f32[32,128]{1,0:T(8,128)S(1)} %collective-permute-done.28.other), custom_call_target="tpu_custom_call" | custom-call | tf_op jit(solution)/shard_map/pallas_call | solution.py:25
  99.8 1.5 %shard_map.72 = (bf16[192,2048]{1,0:T(8,128)(2,1)S(1)}, f32[32,128]{1,0:T(8,128)S(1)}) custom-call(s32[3]{0:T(128)S(1)} %pad_add_fusion.me, f32[64,64]{1,0:T(8,128)S(1)} %shard_map.71.factor, f32[32,2048]{1,0:T(8,128)S(1)} %shard_map.70.after.own, f32[32,2048]{1,0:T(8,128)S(1)} %collective-permute-done.29.other), custom_call_target="tpu_custom_call" | custom-call | tf_op jit(solution)/shard_map/pallas_call | solution.py:25
  101.3 1.7 %collective-permute-start.30 = (f32[32,128]{1,0:T(8,128)S(1)}, f32[32,128]{1,0:T(8,128)S(1)}, u32[]{:S(2)}, u32[]{:S(2)}) collective-permute-start(f32[32,128]{1,0:T(8,128)S(1)} %get-tuple-element.48), channel_id=1, source_target_pairs={{0,4},{4,0},{8,12},{12,8},{1,5},{5,1},{9,13},{13,9},{2,6},{6,2},{1... | collective-permute-start | bytes 49160 | tf_op jit(solution)/shard_map/ppermute | solution.py:406
  103.0 2.1 %collective-permute-done.30 = f32[32,128]{1,0:T(8,128)S(1)} collective-permute-done((f32[32,128]{1,0:T(8,128)S(1)}, f32[32,128]{1,0:T(8,128)S(1)}, u32[]{:S(2)}, u32[]{:S(2)}) %collective-permute-start.30) | collective-permute-done | bytes 16416 | tf_op jit(solution)/shard_map/ppermute | solution.py:406
  105.1 2.0 %collective-permute-start.31 = (f32[32,128]{1,0:T(8,128)S(1)}, f32[32,128]{1,0:T(8,128)S(1)}, u32[]{:S(2)}, u32[]{:S(2)}) collective-permute-start(f32[32,128]{1,0:T(8,128)S(1)} %add.18.mine), channel_id=1, source_target_pairs={{0,8},{4,12},{8,0},{12,4},{1,9},{5,13},{9,1},{13,5},{2,10},{6,14},... | collective-permute-start | bytes 49160 | tf_op jit(solution)/shard_map/ppermute | solution.py:406
  107.7 2.0 %collective-permute-done.31.other = f32[32,128]{1,0:T(8,128)S(1)} collective-permute-done((f32[32,128]{1,0:T(8,128)S(1)}, f32[32,128]{1,0:T(8,128)S(1)}, u32[]{:S(2)}, u32[]{:S(2)}) %collective-permute-start.31) | collective-permute-done | bytes 16416 | tf_op jit(solution)/shard_map/ppermute | solution.py:406
  109.7 3.8 %shard_map.73 = f32[32,2048]{1,0:T(8,128)} custom-call(s32[3]{0:T(128)S(1)} %pad_add_fusion.me, bf16[192,2048]{1,0:T(8,128)(2,1)S(1)} %get-tuple-element.47.mapped, f32[32,128]{1,0:T(8,128)S(1)} %add.18.mine, f32[32,128]{1,0:T(8,128)S(1)} %collective-permute-done.31.other), custom_call_target="tpu_custom_call" | custom-call | tf_op jit(solution)/shard_map/pallas_call | solution.py:25
  (61 shorter events, 22.3 us)
Async XLA Ops:
  2.1 8.7 %collective-permute-start.2 = (s32[1,17]{1,0:T(1,128)S(1)}, s32[1,17]{1,0:T(1,128)S(1)}, u32[]{:S(2)}, u32[]{:S(2)}) collective-permute-start(s32[1,17]{1,0:T(1,128)S(1)} %pad_add_fusion.1.refs_0_), channel_id=1, source_target_pairs={{0,12},{4,0},{8,4},{12,8},{1,13},{5,1},{9,5},{13,9},{2,14},{6,2},{... | collective-permute-start | bytes 212 | tf_op jit(solution)/shard_map/ppermute | solution.py:396
  7.2 4.4 %collective-permute-start.1 = (s32[1,17]{1,0:T(1,128)S(1)}, s32[1,17]{1,0:T(1,128)S(1)}, u32[]{:S(2)}, u32[]{:S(2)}) collective-permute-start(s32[1,17]{1,0:T(1,128)S(1)} %pad_add_fusion.1.refs_0_), channel_id=1, source_target_pairs={{0,8},{4,12},{8,0},{12,4},{1,9},{5,13},{9,1},{13,5},{2,10},{6,14},... | collective-permute-start | bytes 212 | tf_op jit(solution)/shard_map/ppermute | solution.py:396
  7.2 5.3 %collective-permute-start = (s32[1,17]{1,0:T(1,128)S(1)}, s32[1,17]{1,0:T(1,128)S(1)}, u32[]{:S(2)}, u32[]{:S(2)}) collective-permute-start(s32[1,17]{1,0:T(1,128)S(1)} %pad_add_fusion.1.refs_0_), channel_id=1, source_target_pairs={{0,4},{4,8},{8,12},{12,0},{1,5},{5,9},{9,13},{13,1},{2,6},{6,10},{... | collective-permute-start | bytes 212 | tf_op jit(solution)/shard_map/ppermute | solution.py:396
  10.7 32.5 %collective-permute-start.8 = (f32[1024,128]{1,0:T(8,128)S(1)}, f32[1024,128]{1,0:T(8,128)S(1)}, u32[]{:S(2)}, u32[]{:S(2)}) collective-permute-start(f32[1024,128]{1,0:T(8,128)S(1)} %shard_map.59.refs_5_.mine), channel_id=1, source_target_pairs={{0,1},{1,0},{2,3},{3,2},{4,5},{5,4},{6,7},{7,6},{8,9},{9,8},{10,11... | collective-permute-start | bytes 1572872 | tf_op jit(solution)/shard_map/ppermute | solution.py:396
  14.5 6.4 %collective-permute-start.3 = (bf16[256,384]{1,0:T(8,128)(2,1)S(1)}, bf16[256,384]{1,0:T(8,128)(2,1)S(1)}, u32[]{:S(2)}, u32[]{:S(2)}) collective-permute-start(bf16[256,384]{1,0:T(8,128)(2,1)S(1)} %get-tuple-element.27), channel_id=1, source_target_pairs={{0,12},{4,0},{8,4},{12,8},{1,13},{5,1},{9,5},{13,9},{2,14},{6,2},{... | collective-permute-start | bytes 589832 | tf_op jit(solution)/shard_map/ppermute | solution.py:396
  15.7 14.8 %collective-permute-start.4 = (bf16[256,384]{1,0:T(8,128)(2,1)S(1)}, bf16[256,384]{1,0:T(8,128)(2,1)S(1)}, u32[]{:S(2)}, u32[]{:S(2)}) collective-permute-start(bf16[256,384]{1,0:T(8,128)(2,1)S(1)} %get-tuple-element.28), channel_id=1, source_target_pairs={{0,8},{4,12},{8,0},{12,4},{1,9},{5,13},{9,1},{13,5},{2,10},{6,14},... | collective-permute-start | bytes 589832 | tf_op jit(solution)/shard_map/ppermute | solution.py:396
  31.5 19.5 %collective-permute-start.5 = (f32[768,128]{1,0:T(8,128)S(1)}, f32[768,128]{1,0:T(8,128)S(1)}, u32[]{:S(2)}, u32[]{:S(2)}) collective-permute-start(f32[768,128]{1,0:T(8,128)S(1)} %shard_map.61.mine), channel_id=1, source_target_pairs={{0,1},{1,0},{2,3},{3,2},{4,5},{5,4},{6,7},{7,6},{8,9},{9,8},{10,11... | collective-permute-start | bytes 1179656 | tf_op jit(solution)/shard_map/ppermute | solution.py:396
  31.6 9.1 %collective-permute-start.6 = (bf16[256,384]{1,0:T(8,128)(2,1)S(1)}, bf16[256,384]{1,0:T(8,128)(2,1)S(1)}, u32[]{:S(2)}, u32[]{:S(2)}) collective-permute-start(bf16[256,384]{1,0:T(8,128)(2,1)S(1)} %get-tuple-element.29), channel_id=1, source_target_pairs={{0,4},{4,8},{8,12},{12,0},{1,5},{5,9},{9,13},{13,1},{2,6},{6,10},{... | collective-permute-start | bytes 589832 | tf_op jit(solution)/shard_map/ppermute | solution.py:396
  41.5 9.5 %collective-permute-start.7 = (f32[256,128]{1,0:T(8,128)S(1)}, f32[256,128]{1,0:T(8,128)S(1)}, u32[]{:S(2)}, u32[]{:S(2)}) collective-permute-start(f32[256,128]{1,0:T(8,128)S(1)} %shard_map.62.last_mine), channel_id=1, source_target_pairs={{0,1},{1,0},{2,3},{3,2},{4,5},{5,4},{6,7},{7,6},{8,9},{9,8},{10,11... | collective-permute-start | bytes 393224 | tf_op jit(solution)/shard_map/ppermute | solution.py:396
  42.3 6.8 %collective-permute-start.9 = (f32[32,512]{1,0:T(8,128)S(1)}, f32[32,512]{1,0:T(8,128)S(1)}, u32[]{:S(2)}, u32[]{:S(2)}) collective-permute-start(f32[32,512]{1,0:T(8,128)S(1)} %get-tuple-element.31), channel_id=1, source_target_pairs={{0,4},{4,8},{8,12},{12,0},{1,5},{5,9},{9,13},{13,1},{2,6},{6,10},{... | collective-permute-start | bytes 196616 | tf_op jit(solution)/shard_map/ppermute | solution.py:396
  42.3 8.7 %collective-permute-start.10 = (f32[32,512]{1,0:T(8,128)S(1)}, f32[32,512]{1,0:T(8,128)S(1)}, u32[]{:S(2)}, u32[]{:S(2)}) collective-permute-start(f32[32,512]{1,0:T(8,128)S(1)} %get-tuple-element.32), channel_id=1, source_target_pairs={{0,8},{4,12},{8,0},{12,4},{1,9},{5,13},{9,1},{13,5},{2,10},{6,14},... | collective-permute-start | bytes 196616 | tf_op jit(solution)/shard_map/ppermute | solution.py:396
  43.2 7.8 %collective-permute-start.11 = (f32[32,512]{1,0:T(8,128)S(1)}, f32[32,512]{1,0:T(8,128)S(1)}, u32[]{:S(2)}, u32[]{:S(2)}) collective-permute-start(f32[32,512]{1,0:T(8,128)S(1)} %get-tuple-element.33), channel_id=1, source_target_pairs={{0,12},{4,0},{8,4},{12,8},{1,13},{5,1},{9,5},{13,9},{2,14},{6,2},{... | collective-permute-start | bytes 196616 | tf_op jit(solution)/shard_map/ppermute | solution.py:396
  52.4 8.7 %collective-permute-start.15 = (bf16[1,256,128]{2,1,0:T(8,128)(2,1)S(1)}, bf16[1,256,128]{2,1,0:T(8,128)(2,1)S(1)}, u32[]{:S(2)}, u32[]{:S(2)}) collective-permute-start(bf16[1,256,128]{2,1,0:T(8,128)(2,1)S(1)} %get-tuple-element.37), channel_id=1, source_target_pairs={{0,4},{4,8},{8,12},{12,0},{1,5},{5,9},{9,13},{13,1},{2,6},{6,10},{... | collective-permute-start | bytes 196616 | tf_op jit(solution)/shard_map/ppermute | solution.py:396
  54.0 7.1 %collective-permute-start.16 = (bf16[1,256,128]{2,1,0:T(8,128)(2,1)S(1)}, bf16[1,256,128]{2,1,0:T(8,128)(2,1)S(1)}, u32[]{:S(2)}, u32[]{:S(2)}) collective-permute-start(bf16[1,256,128]{2,1,0:T(8,128)(2,1)S(1)} %get-tuple-element.38), channel_id=1, source_target_pairs={{0,8},{4,12},{8,0},{12,4},{1,9},{5,13},{9,1},{13,5},{2,10},{6,14},... | collective-permute-start | bytes 196616 | tf_op jit(solution)/shard_map/ppermute | solution.py:396
  55.1 6.5 %collective-permute-start.17 = (bf16[1,256,128]{2,1,0:T(8,128)(2,1)S(1)}, bf16[1,256,128]{2,1,0:T(8,128)(2,1)S(1)}, u32[]{:S(2)}, u32[]{:S(2)}) collective-permute-start(bf16[1,256,128]{2,1,0:T(8,128)(2,1)S(1)} %get-tuple-element.39), channel_id=1, source_target_pairs={{0,12},{4,0},{8,4},{12,8},{1,13},{5,1},{9,5},{13,9},{2,14},{6,2},{... | collective-permute-start | bytes 196616 | tf_op jit(solution)/shard_map/ppermute | solution.py:396
  56.4 3.9 %collective-permute-start.12 = (f32[64,128]{1,0:T(8,128)S(1)}, f32[64,128]{1,0:T(8,128)S(1)}, u32[]{:S(2)}, u32[]{:S(2)}) collective-permute-start(f32[64,128]{1,0:T(8,128)S(1)} %get-tuple-element.34), channel_id=1, source_target_pairs={{0,2},{2,0},{1,3},{3,1},{4,6},{6,4},{5,7},{7,5},{8,10},{10,8},{9,1... | collective-permute-start | bytes 98312 | tf_op jit(solution)/shard_map/ppermute | solution.py:406
  60.4 3.9 %collective-permute-start.13 = (f32[64,128]{1,0:T(8,128)S(1)}, f32[64,128]{1,0:T(8,128)S(1)}, u32[]{:S(2)}, u32[]{:S(2)}) collective-permute-start(f32[64,128]{1,0:T(8,128)S(1)} %add.15), channel_id=1, source_target_pairs={{0,4},{4,0},{8,12},{12,8},{1,5},{5,1},{9,13},{13,9},{2,6},{6,2},{1... | collective-permute-start | bytes 98312 | tf_op jit(solution)/shard_map/ppermute | solution.py:406
  61.1 8.4 %collective-permute-start.18 = (bf16[1,256,128]{2,1,0:T(8,128)(2,1)S(1)}, bf16[1,256,128]{2,1,0:T(8,128)(2,1)S(1)}, u32[]{:S(2)}, u32[]{:S(2)}) collective-permute-start(bf16[1,256,128]{2,1,0:T(8,128)(2,1)S(1)} %collective-permute-done.15.refs_6_), channel_id=1, source_target_pairs={{0,1},{1,0},{2,3},{3,2},{4,5},{5,4},{6,7},{7,6},{8,9},{9,8},{10,11... | collective-permute-start | bytes 196616 | tf_op jit(solution)/shard_map/ppermute | solution.py:396
  61.1 8.4 %collective-permute-start.19 = (bf16[1,256,128]{2,1,0:T(8,128)(2,1)S(1)}, bf16[1,256,128]{2,1,0:T(8,128)(2,1)S(1)}, u32[]{:S(2)}, u32[]{:S(2)}) collective-permute-start(bf16[1,256,128]{2,1,0:T(8,128)(2,1)S(1)} %collective-permute-done.16.refs_7_), channel_id=1, source_target_pairs={{0,1},{1,0},{2,3},{3,2},{4,5},{5,4},{6,7},{7,6},{8,9},{9,8},{10,11... | collective-permute-start | bytes 196616 | tf_op jit(solution)/shard_map/ppermute | solution.py:396
  61.6 7.9 %collective-permute-start.20 = (bf16[1,256,128]{2,1,0:T(8,128)(2,1)S(1)}, bf16[1,256,128]{2,1,0:T(8,128)(2,1)S(1)}, u32[]{:S(2)}, u32[]{:S(2)}) collective-permute-start(bf16[1,256,128]{2,1,0:T(8,128)(2,1)S(1)} %collective-permute-done.17.refs_8_), channel_id=1, source_target_pairs={{0,1},{1,0},{2,3},{3,2},{4,5},{5,4},{6,7},{7,6},{8,9},{9,8},{10,11... | collective-permute-start | bytes 196616 | tf_op jit(solution)/shard_map/ppermute | solution.py:396
  64.3 5.2 %collective-permute-start.14 = (f32[64,128]{1,0:T(8,128)S(1)}, f32[64,128]{1,0:T(8,128)S(1)}, u32[]{:S(2)}, u32[]{:S(2)}) collective-permute-start(f32[64,128]{1,0:T(8,128)S(1)} %add.16.mine), channel_id=1, source_target_pairs={{0,8},{4,12},{8,0},{12,4},{1,9},{5,13},{9,1},{13,5},{2,10},{6,14},... | collective-permute-start | bytes 98312 | tf_op jit(solution)/shard_map/ppermute | solution.py:406
  70.5 6.4 %collective-permute-start.21 = (f32[32,2048]{1,0:T(8,128)S(1)}, f32[32,2048]{1,0:T(8,128)S(1)}, u32[]{:S(2)}, u32[]{:S(2)}) collective-permute-start(f32[32,2048]{1,0:T(8,128)S(1)} %get-tuple-element.42.mine), channel_id=1, source_target_pairs={{0,2},{2,0},{1,3},{3,1},{4,6},{6,4},{5,7},{7,5},{8,10},{10,8},{9,1... | collective-permute-start | bytes 786440 | tf_op jit(solution)/shard_map/ppermute | solution.py:406
  77.6 6.2 %collective-permute-start.22 = (f32[32,512]{1,0:T(8,128)S(1)}, f32[32,512]{1,0:T(8,128)S(1)}, u32[]{:S(2)}, u32[]{:S(2)}) collective-permute-start(f32[32,512]{1,0:T(8,128)S(1)} %get-tuple-element.44), channel_id=1, source_target_pairs={{0,4},{4,8},{8,12},{12,0},{1,5},{5,9},{9,13},{13,1},{2,6},{6,10},{... | collective-permute-start | bytes 196616 | tf_op jit(solution)/shard_map/ppermute | solution.py:396
  78.1 6.6 %collective-permute-start.23 = (f32[32,512]{1,0:T(8,128)S(1)}, f32[32,512]{1,0:T(8,128)S(1)}, u32[]{:S(2)}, u32[]{:S(2)}) collective-permute-start(f32[32,512]{1,0:T(8,128)S(1)} %get-tuple-element.45), channel_id=1, source_target_pairs={{0,8},{4,12},{8,0},{12,4},{1,9},{5,13},{9,1},{13,5},{2,10},{6,14},... | collective-permute-start | bytes 196616 | tf_op jit(solution)/shard_map/ppermute | solution.py:396
  79.8 4.9 %collective-permute-start.24 = (f32[32,512]{1,0:T(8,128)S(1)}, f32[32,512]{1,0:T(8,128)S(1)}, u32[]{:S(2)}, u32[]{:S(2)}) collective-permute-start(f32[32,512]{1,0:T(8,128)S(1)} %get-tuple-element.46), channel_id=1, source_target_pairs={{0,12},{4,0},{8,4},{12,8},{1,13},{5,1},{9,5},{13,9},{2,14},{6,2},{... | collective-permute-start | bytes 196616 | tf_op jit(solution)/shard_map/ppermute | solution.py:396
  82.1 5.2 %collective-permute-start.26 = (f32[32,2048]{1,0:T(8,128)S(1)}, f32[32,2048]{1,0:T(8,128)S(1)}, u32[]{:S(2)}, u32[]{:S(2)}) collective-permute-start(f32[32,2048]{1,0:T(8,128)S(1)} %get-tuple-element.43.refs_0_.own), channel_id=1, source_target_pairs={{0,1},{1,0},{2,3},{3,2},{4,5},{5,4},{6,7},{7,6},{8,9},{9,8},{10,11... | collective-permute-start | bytes 786440 | tf_op jit(solution)/shard_map/ppermute | solution.py:396
  85.7 6.4 %collective-permute-start.25 = (f32[32,2048]{1,0:T(8,128)S(1)}, f32[32,2048]{1,0:T(8,128)S(1)}, u32[]{:S(2)}, u32[]{:S(2)}) collective-permute-start(f32[32,2048]{1,0:T(8,128)S(1)} %shard_map.68.mine), channel_id=1, source_target_pairs={{0,2},{2,0},{1,3},{3,1},{4,6},{6,4},{5,7},{7,5},{8,10},{10,8},{9,1... | collective-permute-start | bytes 786440 | tf_op jit(solution)/shard_map/ppermute | solution.py:406
  88.3 3.8 %collective-permute-start.27 = (f32[32,128]{1,0:T(8,128)S(1)}, f32[32,128]{1,0:T(8,128)S(1)}, u32[]{:S(2)}, u32[]{:S(2)}) collective-permute-start(f32[32,128]{1,0:T(8,128)S(1)} %shard_map.69), channel_id=1, source_target_pairs={{0,4},{4,0},{8,12},{12,8},{1,5},{5,1},{9,13},{13,9},{2,6},{6,2},{1... | collective-permute-start | bytes 49160 | tf_op jit(solution)/shard_map/ppermute | solution.py:406
  92.7 7.1 %collective-permute-start.29 = (f32[32,2048]{1,0:T(8,128)S(1)}, f32[32,2048]{1,0:T(8,128)S(1)}, u32[]{:S(2)}, u32[]{:S(2)}) collective-permute-start(f32[32,2048]{1,0:T(8,128)S(1)} %shard_map.70.after.own), channel_id=1, source_target_pairs={{0,1},{1,0},{2,3},{3,2},{4,5},{5,4},{6,7},{7,6},{8,9},{9,8},{10,11... | collective-permute-start | bytes 786440 | tf_op jit(solution)/shard_map/ppermute | solution.py:396
  92.8 4.7 %collective-permute-start.28 = (f32[32,128]{1,0:T(8,128)S(1)}, f32[32,128]{1,0:T(8,128)S(1)}, u32[]{:S(2)}, u32[]{:S(2)}) collective-permute-start(f32[32,128]{1,0:T(8,128)S(1)} %add.17.after.mine), channel_id=1, source_target_pairs={{0,8},{4,12},{8,0},{12,4},{1,9},{5,13},{9,1},{13,5},{2,10},{6,14},... | collective-permute-start | bytes 49160 | tf_op jit(solution)/shard_map/ppermute | solution.py:406
  101.3 3.8 %collective-permute-start.30 = (f32[32,128]{1,0:T(8,128)S(1)}, f32[32,128]{1,0:T(8,128)S(1)}, u32[]{:S(2)}, u32[]{:S(2)}) collective-permute-start(f32[32,128]{1,0:T(8,128)S(1)} %get-tuple-element.48), channel_id=1, source_target_pairs={{0,4},{4,0},{8,12},{12,8},{1,5},{5,1},{9,13},{13,9},{2,6},{6,2},{1... | collective-permute-start | bytes 49160 | tf_op jit(solution)/shard_map/ppermute | solution.py:406
  105.1 4.6 %collective-permute-start.31 = (f32[32,128]{1,0:T(8,128)S(1)}, f32[32,128]{1,0:T(8,128)S(1)}, u32[]{:S(2)}, u32[]{:S(2)}) collective-permute-start(f32[32,128]{1,0:T(8,128)S(1)} %add.18.mine), channel_id=1, source_target_pairs={{0,8},{4,12},{8,0},{12,4},{1,9},{5,13},{9,1},{13,5},{2,10},{6,14},... | collective-permute-start | bytes 49160 | tf_op jit(solution)/shard_map/ppermute | solution.py:406
  (3 other events, 32.4 us)

commit v5 on v4

--- a/solution.py
+++ b/solution.py
@@ -13,22 +13,25 @@
 VMEM = pl.BlockSpec(memory_space=pltpu.VMEM)
 SMEM = pl.BlockSpec(memory_space=pltpu.SMEM)
 ANY = pl.BlockSpec(memory_space=pl.ANY)
+HBM = pl.BlockSpec(memory_space=pltpu.HBM)
 F32 = jnp.float32
 BF16 = jnp.bfloat16
 HIGHEST = lax.Precision.HIGHEST
 NT = (((1,), (1,)), ((), ()))
 
 
-def call(body, outs, args, smem_in=(), smem_out=(), any_in=()):
+def call(body, outs, args, smem_in=(), smem_out=(), any_in=(), hbm_in=(), scratch=()):
     single = not isinstance(outs, (list, tuple))
     shapes = [outs] if single else list(outs)
     result = pl.pallas_call(
         body,
         out_shape=shapes,
         in_specs=[
-            SMEM if i in smem_in else ANY if i in any_in else VMEM for i in range(len(args))
+            SMEM if i in smem_in else ANY if i in any_in else HBM if i in hbm_in else VMEM
+            for i in range(len(args))
         ],
         out_specs=[SMEM if i in smem_out else VMEM for i in range(len(shapes))],
+        scratch_shapes=list(scratch),
         compiler_params=pltpu.CompilerParams(vmem_limit_bytes=48 * 2**20),
     )(*args)
     return result[0] if single else result
@@ -130,8 +133,11 @@
 
 def plan_body(dims, me, *refs):
     row_count, capacity, slots, blocks_here = dims
-    lists, (emb, after, idx), sends = refs[:row_count], refs[row_count : row_count + 3], refs[row_count + 3 :]
+    lists, (emb_hbm, idx) = refs[:row_count], refs[row_count : row_count + 2]
+    sends, (emb, done) = refs[row_count + 2 : -2], refs[-2:]
     row = me[0]
+    copy = pltpu.make_async_copy(emb_hbm, emb, done)
+    copy.start()
 
     def clear(i, carry):
         for line in range(6):
@@ -141,11 +147,11 @@
     lax.fori_loop(0, slots, clear, 0)
 
     def ranked(listed, want, write):
-        count = listed[0, 2 * slots]
+        count = listed[2, 0]
 
         def step(s, counts):
             near = listed[0, s]
-            far = listed[0, slots + s]
+            far = listed[1, s]
             return write(s, near, far, far // blocks_here, s < count, counts)
 
         lax.fori_loop(0, slots, step, (0,) * want)
@@ -184,6 +190,7 @@
             return (counts[0] + hit.astype(jnp.int32),)
 
         ranked(lists[k], 1, write_in)
+    copy.wait()
     for k in range(1, row_count):
         for j in range(capacity):
             sends[k - 1][j * BLOCK : (j + 1) * BLOCK, :] = emb[at_block(idx[4, k * capacity + j]), :]
@@ -203,18 +210,16 @@
         out[i * BLOCK : (i + 1) * BLOCK, :] = partial_distance(block, block)
 
 
-def pair_distance_body(shifts, capacity, idx, emb, *refs):
-    far, out = refs[:-1], refs[-1]
-    if shifts[0] == 0:
-        far = (None, *far)
-    for place, k in enumerate(shifts):
+def pair_distance_body(row_count, capacity, idx, emb, *refs):
+    out = refs[-1]
+    for k in range(row_count):
         for j in range(capacity):
-            left = emb[at_block(idx[0, k * capacity + j]), :]
+            slot = k * capacity + j
+            left = emb[at_block(idx[0, slot]), :]
             if k == 0:
                 right = emb[at_block(idx[4, j]), :]
             else:
-                right = far[place][j * BLOCK : (j + 1) * BLOCK, :]
-            slot = place * capacity + j
+                right = refs[k - 1][j * BLOCK : (j + 1) * BLOCK, :]
             out[slot * BLOCK : (slot + 1) * BLOCK, :] = partial_distance(left, right)
 
 
@@ -227,12 +232,9 @@
         sums[i : i + 1, :] = jnp.sum(tile, axis=0, keepdims=True)
 
 
-def pair_tile_body(row_count, capacity, per_core, tile_count, blocks_here, me, idx, mine, other, last_mine, last_other, self_sums, *refs):
-    near_tiles, home_tiles = refs[-2 - row_count : -row_count]
-    sends = refs[-row_count : -1]
-    table = refs[-1]
+def pair_tile_body(dims, me, idx, mine, other, self_sums, values, near_tiles, home_tiles, table, *sends):
+    row_count, capacity, per_core, blocks_here, tile_count = dims
     row, tile_index, core = me[0], me[1], me[2]
-    first_slots = mine.shape[0] // BLOCK
     table[...] = jnp.zeros(table.shape, F32)
     for i in range(self_sums.shape[0]):
         table[pl.ds(row * blocks_here + i * tile_count + tile_index, 1), :] = self_sums[i : i + 1, :]
@@ -244,13 +246,8 @@
     for k in range(row_count):
         for j in range(capacity):
             slot = k * capacity + j
-            if slot < first_slots:
-                part = slice(slot * BLOCK, (slot + 1) * BLOCK)
-                distance = mine[part, :] + other[part, :]
-            else:
-                part = slice((slot - first_slots) * BLOCK, (slot - first_slots + 1) * BLOCK)
-                distance = last_mine[part, :] + last_other[part, :]
-            tile = jnp.exp(-kernel_gamma * (distance - 2.0))
+            part = slice(slot * BLOCK, (slot + 1) * BLOCK)
+            tile = jnp.exp(-kernel_gamma * (mine[part, :] + other[part, :] - 2.0))
             tile = jnp.where(idx[2, slot] > 0, tile, 0.0)
             turned = tile.T
             near_tiles[slot] = pack(turned)
@@ -262,27 +259,27 @@
 
                 @pl.when(core == j // per_core)
                 def _():
-                    sends[k - 1][j % per_core] = pack(tile)
-
-
-def pick_columns(idx, row_count, capacity, source, sends):
+                    inner = j % per_core
+                    sends[k - 1][inner * BLOCK : (inner + 1) * BLOCK, :] = tile
+
+    pick_columns(idx, row_count, capacity, values, sends, per_core * BLOCK)
+
+
+def pick_columns(idx, row_count, capacity, source, sends, base):
+    count = source.shape[0]
     for k in range(1, row_count):
         back = row_count - k
-        for j in range(capacity):
-            sends[k - 1][:, j * BLOCK : (j + 1) * BLOCK] = source[:, at_block(idx[0, k * capacity + j])]
-            place = capacity + j
-            sends[k - 1][:, place * BLOCK : (place + 1) * BLOCK] = source[
-                :, at_block(idx[4, back * capacity + j])
-            ]
-
-
-def pick_body(row_count, capacity, idx, source, after, *sends):
-    pick_columns(idx, row_count, capacity, source, sends)
-
-
-def apply_tiles(dims, me, idx, inverse, own, received, near_tiles, home_tiles, sent, shared, self_tiles, out):
+        blocks = [idx[0, k * capacity + j] for j in range(capacity)]
+        blocks += [idx[4, back * capacity + j] for j in range(capacity)]
+        for place, block in enumerate(blocks):
+            rows = slice(base + place * count, base + (place + 1) * count)
+            sends[k - 1][rows, :] = source[:, at_block(block)]
+
+
+def apply_tiles(dims, me, idx, inverse, own, received, base, near_tiles, home_tiles, sent, shared, self_tiles, out):
     row_count, capacity, per_core, blocks_here, tile_count = dims
     row, tile_index, core = me[0], me[1], me[2]
+    count = out.shape[0]
     out[...] = jnp.zeros(out.shape, F32)
 
     def scaled(values, block):
@@ -291,6 +288,9 @@
     def add(block, packed, values):
         place = at_block(block)
         out[:, place] = out[:, place] + product(packed, values)
+
+    def arrived(k, place):
+        return received[k - 1][pl.ds(pl.multiple_of(base + place * count, 8), count), :]
 
     for i in range(blocks_here // tile_count):
         block = i * tile_count + tile_index
@@ -301,7 +301,7 @@
             if k == 0:
                 values = own[:, at_block(idx[4, j])]
             else:
-                values = received[row_count - k - 1][:, (capacity + j) * BLOCK : (capacity + j + 1) * BLOCK]
+                values = arrived(row_count - k, capacity + j)
             add(idx[0, slot], near_tiles[slot], scaled(values, idx[1, slot]))
     for k in range(row_count):
         for j in range(capacity):
@@ -311,36 +311,38 @@
                 packed = home_tiles[j]
             else:
                 inner = j % per_core
+                part = slice(inner * BLOCK, (inner + 1) * BLOCK)
                 if j < per_core:
                     place = core * per_core + inner
-                    packed = sent[k - 1][inner]
+                    packed = pack(sent[k - 1][part, :])
                 else:
                     place = (1 - core) * per_core + inner
-                    packed = shared[k - 1][inner]
+                    packed = pack(shared[k - 1][part, :])
                 slot = k * capacity + place
-                values = received[k - 1][:, at_block(place)]
+                values = arrived(k, place)
             add(idx[4, slot], packed, scaled(values, idx[5, slot]))
 
 
-def split_inputs(row_count, refs):
-    others = row_count - 1
-    received = refs[1 : 1 + others]
-    near_tiles, home_tiles = refs[1 + others : 3 + others]
-    sent = refs[3 + others : 3 + 2 * others]
-    shared = refs[3 + 2 * others : 3 + 3 * others]
-    return (refs[0], received, near_tiles, home_tiles, sent, shared, refs[-1])
-
-
-def first_apply_body(dims, me, idx, mine, other, *refs):
-    inputs, (out, degree, inverse) = refs[:-3], refs[-3:]
-    total = mine[...] + other[...]
+def first_apply_body(dims, me, idx, *refs):
+    row_count, per_core = dims[0], dims[2]
+    terms, refs = refs[:row_count], refs[row_count:]
+    own, near_tiles, home_tiles, self_tiles = refs[:4]
+    sent, shared = refs[4 : 3 + row_count], refs[3 + row_count : 2 + 2 * row_count]
+    out, degree, inverse = refs[-3:]
+    total = functools.reduce(lambda total, term: total + term[...], terms[1:], terms[0][...])
     degree[...] = total
     inverse[...] = 1.0 / jnp.sqrt(total)
-    apply_tiles(dims, me, idx, inverse, *split_inputs(dims[0], inputs), out)
-
-
-def second_apply_body(dims, me, idx, inverse, *refs):
-    apply_tiles(dims, me, idx, inverse, *split_inputs(dims[0], refs[:-1]), refs[-1])
+    apply_tiles(
+        dims, me, idx, inverse, own, sent, per_core * BLOCK, near_tiles, home_tiles, sent, shared, self_tiles, out
+    )
+
+
+def second_apply_body(dims, me, idx, inverse, after, *refs):
+    row_count = dims[0]
+    own, near_tiles, home_tiles, self_tiles = refs[:4]
+    sent, shared = refs[4 : 3 + row_count], refs[3 + row_count : 2 + 2 * row_count]
+    received, out = refs[2 + 2 * row_count : -1], refs[-1]
+    apply_tiles(dims, me, idx, inverse, own, received, 0, near_tiles, home_tiles, sent, shared, self_tiles, out)
 
 
 def scale_rows(me, blocks_here, inverse, mine, other, out):
@@ -352,11 +354,11 @@
 
 def mapped_body(row_count, capacity, blocks_here, me, idx, inverse, mine, other, out, *sends):
     scale_rows(me, blocks_here, inverse, mine, other, out)
-    pick_columns(idx, row_count, capacity, out, sends)
-
-
-def last_mapped_body(blocks_here, me, inverse, mine, other, after, out):
-    scale_rows(me, blocks_here, inverse, mine, other, out)
+    pick_columns(idx, row_count, capacity, out, sends, 0)
+
+
+def last_mapped_body(blocks_here, me, inverse, mine, other, *refs):
+    scale_rows(me, blocks_here, inverse, mine, other, refs[-1])
 
 
 def folded(square):
@@ -364,8 +366,8 @@
     return jnp.concatenate([square[:half], square[half:]], axis=1)
 
 
-def unfolded(mine, other):
-    total = mine[...] + other[...]
+def unfolded(terms):
+    total = functools.reduce(lambda total, term: total + term[...], terms[1:], terms[0][...])
     width = total.shape[1] // 2
     return jnp.concatenate([total[:, :width], total[:, width:]], axis=0)
 
@@ -374,8 +376,8 @@
     out[...] = folded(gram(thirds(both_columns(me[2], own[...], other[...]))))
 
 
-def factor_body(after, mine, other, out):
-    out[...] = lower_inverse(unfolded(mine, other))
+def factor_body(after, *refs):
+    refs[-1][...] = lower_inverse(unfolded(refs[:-1]))
 
 
 def second_gram_body(me, factor, own, other, mapped, out):
@@ -385,8 +387,9 @@
     out[...] = folded(gram(parts))
 
 
-def final_body(me, mapped, mine, other, out):
-    factor = lower_inverse(unfolded(mine, other))
+def final_body(me, mapped, *refs):
+    out = refs[-1]
+    factor = lower_inverse(unfolded(refs[:-1]))
     own_cols = out.shape[0]
     part = jnp.where(me[2] == 0, factor[:own_cols], factor[own_cols:])
     out[...] = times(part, mapped[...])
@@ -394,6 +397,10 @@
 
 def shift_by(value, axes, size, shift):
     return lax.ppermute(value, axes, [(i, (i + shift) % size) for i in range(size)])
+
+
+def row_terms(value, row_count):
+    return [value] + [shift_by(value, "rows", row_count, k) for k in range(1, row_count)]
 
 
 def pair_sum(value, axes):
@@ -425,72 +432,60 @@
     block_count = row_count * blocks_here
     others = range(1, row_count)
 
-    own_list = jnp.concatenate([pair_list.reshape(1, 2 * slots), pair_count.reshape(1, 1)], axis=1)
-    lists = [own_list] + [shift_by(own_list, "rows", row_count, k) for k in others]
+    own_list = jnp.concatenate(
+        [pair_list[0], jnp.broadcast_to(pair_count[:, None], (1, slots))], axis=0
+    )
+    lists = row_terms(own_list, row_count)
+    planned = call(
+        functools.partial(plan_body, (row_count, capacity, slots, blocks_here)),
+        [sds((6, slots), jnp.int32)] + [sds((capacity * BLOCK, half_features), BF16) for _ in others],
+        [me, *lists, embeddings],
+        smem_in=range(1 + row_count),
+        hbm_in=(row_count + 1,),
+        smem_out=(0,),
+        scratch=[pltpu.VMEM(embeddings.shape, BF16), pltpu.SemaphoreType.DMA],
+    )
+    idx, sends = planned[0], planned[1:]
+    far = [shift_by(sends[k - 1], "rows", row_count, -k) for k in others]
+
     self_part = call(
         functools.partial(self_distance_body, own_blocks, tile_count),
         sds((own_blocks * BLOCK, BLOCK), F32),
         [me, embeddings],
         smem_in=(0,),
     )
-    planned = call(
-        functools.partial(plan_body, (row_count, capacity, slots, blocks_here)),
-        [sds((6, slots), jnp.int32)] + [sds((capacity * BLOCK, half_features), BF16) for _ in others],
-        [me, *lists, embeddings, self_part],
-        smem_in=range(1 + row_count),
-        any_in=(row_count + 2,),
-        smem_out=(0,),
-    )
-    idx, sends = planned[0], planned[1:]
-    far = [shift_by(sends[k - 1], "rows", row_count, -k) for k in others]
-
     self_other = shift_by(self_part, "cols", core_count, 1)
     self_tiles, self_sums = call(
         functools.partial(self_tile_body, own_blocks),
         [sds((own_blocks, 2 * BLOCK, BLOCK), BF16), sds((own_blocks, BLOCK), F32)],
         [self_part, self_other],
     )
+    pair_part = call(
+        functools.partial(pair_distance_body, row_count, capacity),
+        sds((slots * BLOCK, BLOCK), F32),
+        [idx, embeddings, *far],
+        smem_in=(0,),
+    )
+    pair_other = shift_by(pair_part, "cols", core_count, 1)
+
     values = start.T
-    start_sends = call(
-        functools.partial(pick_body, row_count, capacity),
-        [sds((own_cols, 2 * capacity * BLOCK), F32) for _ in others],
-        [idx, values, far[0]],
-        smem_in=(0,),
-        any_in=(2,),
-    )
-    start_in = [shift_by(start_sends[k - 1], "rows", row_count, k) for k in others]
-
-    first_part = call(
-        functools.partial(pair_distance_body, range(row_count - 1), capacity),
-        sds(((slots - capacity) * BLOCK, BLOCK), F32),
-        [idx, embeddings, *far[:-1]],
-        smem_in=(0,),
-    )
-    first_other = shift_by(first_part, "cols", core_count, 1)
-    last_part = call(
-        functools.partial(pair_distance_body, (row_count - 1,), capacity),
-        sds((capacity * BLOCK, BLOCK), F32),
-        [idx, embeddings, far[-1]],
-        smem_in=(0,),
-    )
-    last_other = shift_by(last_part, "cols", core_count, 1)
+    dims = (row_count, capacity, per_core, blocks_here, tile_count)
     table = sds((block_count, BLOCK), F32)
+    picked = 2 * capacity * own_cols
     tiles = call(
-        functools.partial(pair_tile_body, row_count, capacity, per_core, tile_count, blocks_here),
-        [sds((slots, 2 * BLOCK, BLOCK), BF16), sds((capacity, 2 * BLOCK, BLOCK), BF16)]
-        + [sds((per_core, 2 * BLOCK, BLOCK), BF16) for _ in others]
-        + [table],
-        [me, idx, first_part, first_other, last_part, last_other, self_sums, *start_in],
+        functools.partial(pair_tile_body, dims),
+        [sds((slots, 2 * BLOCK, BLOCK), BF16), sds((capacity, 2 * BLOCK, BLOCK), BF16), table]
+        + [sds((per_core * BLOCK + picked, BLOCK), F32) for _ in others],
+        [me, idx, pair_part, pair_other, self_sums, values],
         smem_in=(0, 1),
-        any_in=range(7, 6 + row_count),
-    )
-    near_tiles, home_tiles, tile_sends = tiles[0], tiles[1], tiles[2:-1]
-    degree_terms = pair_sum(tiles[-1], ("tiles", "rows"))
-    sent = [shift_by(tile_sends[k - 1], "rows", row_count, k) for k in others]
-    shared = [shift_by(tile, "cols", core_count, 1) for tile in sent]
-
-    dims = (row_count, capacity, per_core, blocks_here, tile_count)
-    tile_args = [near_tiles, home_tiles, *sent, *shared, self_tiles]
+    )
+    near_tiles, home_tiles, degrees, sends = tiles[0], tiles[1], tiles[2], tiles[3:]
+    mine, other = pair_sum(degrees, ("tiles",))
+    degree_terms = row_terms(mine + other, row_count)
+    sent = [shift_by(sends[k - 1], "rows", row_count, k) for k in others]
+    shared = [shift_by(message, "cols", core_count, 1) for message in sent]
+
+    tile_args = [near_tiles, home_tiles, self_tiles, *sent, *shared]
     block_shape = sds((own_cols, rows_here), F32)
     square = sds((2 * own_cols, 2 * own_cols), F32)
     folded_square = sds((own_cols, 4 * own_cols), F32)
@@ -498,13 +493,13 @@
     part, degree, inverse = call(
         functools.partial(first_apply_body, dims),
         [block_shape, table, table],
-        [me, idx, *degree_terms, values, *start_in, *tile_args],
+        [me, idx, *degree_terms, values, *tile_args],
         smem_in=(0, 1),
     )
     mine, other = pair_sum(part, ("tiles",))
     first = call(
         functools.partial(mapped_body, row_count, capacity, blocks_here),
-        [block_shape] + [sds((own_cols, 2 * capacity * BLOCK), F32) for _ in others],
+        [block_shape] + [sds((picked, BLOCK), F32) for _ in others],
         [me, idx, inverse, mine, other],
         smem_in=(0, 1),
     )
@@ -513,20 +508,21 @@
 
     mapped_other = shift_by(mapped, "cols", core_count, 1)
     first_gram = call(gram_body, folded_square, [me, mapped, mapped_other], smem_in=(0,))
-    gram_terms = pair_sum(first_gram, ("rows",))
+    gram_terms = row_terms(first_gram, row_count)
     part = call(
         functools.partial(second_apply_body, dims),
         block_shape,
-        [me, idx, inverse, mapped, *received, *tile_args],
+        [me, idx, inverse, first_gram, mapped, *tile_args, *received],
         smem_in=(0, 1),
+        any_in=(3,),
     )
     mine, other = pair_sum(part, ("tiles",))
     second = call(
         functools.partial(last_mapped_body, blocks_here),
         block_shape,
-        [me, inverse, mine, other, gram_terms[0]],
+        [me, inverse, mine, other, *gram_terms[1:]],
         smem_in=(0,),
-        any_in=(4,),
+        any_in=range(4, 3 + row_count),
     )
     second_other = shift_by(second, "cols", core_count, 1)
     factor = call(factor_body, square, [second, *gram_terms], any_in=(0,))
@@ -537,7 +533,7 @@
         smem_in=(0,),
     )
     vectors = call(
-        final_body, block_shape, [me, full, *pair_sum(second_gram, ("rows",))], smem_in=(0,)
+        final_body, block_shape, [me, full, *row_terms(second_gram, row_count)], smem_in=(0,)
     )
     own_degree = lax.dynamic_slice_in_dim(degree, row_index * blocks_here, blocks_here, 0)
     return (vectors.T, own_degree.reshape(rows_here))

time: 114 us -> 110 us (0.965)
  starting transfers between devices: 36.2 us -> 34.6 us
    ppermute x9 -> x3, waiting for transfers between devices: 22.1 us -> 7.31 us  [pair_sum(): lax.ppermute(value, name, [(i, i ^ flip) for i in range(size)])]
    ppermute x23 -> x28, waiting for transfers between devices: 31.7 us -> 46 us  [shift_by(): lax.ppermute(value, axes, [(i, (i + shift) % size) for i in range(size)])]
    ppermute x9 -> x3, starting transfers between devices: 14.5 us -> 4.61 us  [pair_sum(): lax.ppermute(value, name, [(i, i ^ flip) for i in range(size)])]
    ppermute x23 -> x28, starting transfers between devices: 21.7 us -> 30 us  [shift_by(): lax.ppermute(value, axes, [(i, (i + shift) % size) for i in range(size)])]
    pallas_call x15 -> x13, Pallas kernels: 19 us -> 18 us  [call(): pl.pallas_call(body, out_shape=shapes, in_specs=[SMEM if i in smem_in els...]
  transfers between devices with their start and end apart: 32 -> 31, of which waited for: 17 -> 21; matrix products, arithmetic and copies ran while one was open for 1% -> 1% of each run, Pallas kernels for 9% -> 5%
where the time goes in v5:
time: 110 us
  waiting for transfers between devices  53.3 us (48%)
  starting transfers between devices  34.6 us (31%)
  Pallas kernels  18 us (16%)
  local copies, waits for them, and re-layouts  2.7 us (2%)
  between operations  1.41 us (1%)
    ppermute x28, waiting for transfers between devices, shift_by(): lax.ppermute(value, axes, [(i, (i + shift) % size) for i in range(size)])  46 us
    ppermute x28, starting transfers between devices, shift_by(): lax.ppermute(value, axes, [(i, (i + shift) % size) for i in range(size)])  30 us
    pallas_call x13, Pallas kernels, call(): pl.pallas_call(body, out_shape=shapes, in_specs=[SMEM if i in smem_in els...  18 us
    ppermute x3, waiting for transfers between devices, pair_sum(): lax.ppermute(value, name, [(i, i ^ flip) for i in range(size)])  7.31 us
    ppermute x3, starting transfers between devices, pair_sum(): lax.ppermute(value, name, [(i, i ^ flip) for i in range(size)])  4.61 us
  transfers between devices with their start and end apart: 31, of which 21 were waited for; matrix products, arithmetic and copies ran while one was open for 1% of the time, Pallas kernels for 5%

profile of v5, /device:TPU:0, one launch (start us, length us, event | category | flops | bytes accessed | tf_op | source)
XLA Modules:
  0.0 110.1 jit_solution(7238579828246506503)
XLA Ops:
  2.0 5.0 %collective-permute-start.2 = (s32[3,8]{1,0:T(4,128)S(1)}, s32[3,8]{1,0:T(4,128)S(1)}, u32[]{:S(2)}, u32[]{:S(2)}) collective-permute-start(s32[3,8]{1,0:T(4,128)S(1)} %concatenate.3.refs_0_), channel_id=1, source_target_pairs={{0,12},{4,0},{8,4},{12,8},{1,13},{5,1},{9,5},{13,9},{2,14},{6,2},{... | collective-permute-start | bytes 296 | tf_op jit(solution)/shard_map/ppermute | solution.py:399
  8.3 3.2 %collective-permute-done.1.refs_2_ = s32[3,8]{1,0:T(4,128)S(1)} collective-permute-done((s32[3,8]{1,0:T(4,128)S(1)}, s32[3,8]{1,0:T(4,128)S(1)}, u32[]{:S(2)}, u32[]{:S(2)}) %collective-permute-start.1) | collective-permute-done | bytes 128 | tf_op jit(solution)/shard_map/ppermute | solution.py:399
  12.4 1.4 %copy-done = bf16[2048,384]{1,0:T(8,128)(2,1)S(1)} copy-done((bf16[2048,384]{1,0:T(8,128)(2,1)S(1)}, bf16[2048,384]{1,0:T(8,128)(2,1)}, u32[]{:S(2)}) %copy-start) | copy-done | bytes 1572888
  13.8 2.3 %shard_map.59 = (s32[6,8]{1,0:T(8,128)S(1)}, bf16[256,384]{1,0:T(8,128)(2,1)S(1)}, bf16[256,384]{1,0:T(8,128)(2,1)S(1)}, bf16[256,384]{1,0:T(8,128)(2,1)S(1)}) custom-call(s32[3]{0:T(128)S(1)} %pad_add_fusion.me, s32[3,8]{1,0:T(4,128)S(1)} %concatenate.3.refs_0_, s32[3,8]{1,0:T(4,128)S(1)} %collective-permute-done.refs_1_, ...), custom_call_target="tpu_custom_call" | custom-call | tf_op jit(solution)/shard_map/pallas_call | solution.py:26
  17.3 1.9 %collective-permute-start.5 = (bf16[256,384]{1,0:T(8,128)(2,1)S(1)}, bf16[256,384]{1,0:T(8,128)(2,1)S(1)}, u32[]{:S(2)}, u32[]{:S(2)}) collective-permute-start(bf16[256,384]{1,0:T(8,128)(2,1)S(1)} %get-tuple-element.26), channel_id=1, source_target_pairs={{0,4},{4,8},{8,12},{12,0},{1,5},{5,9},{9,13},{13,1},{2,6},{6,10},{... | collective-permute-start | bytes 589832 | tf_op jit(solution)/shard_map/ppermute | solution.py:399
  20.4 2.0 %collective-permute-done.3.refs_0_ = bf16[256,384]{1,0:T(8,128)(2,1)S(1)} collective-permute-done((bf16[256,384]{1,0:T(8,128)(2,1)S(1)}, bf16[256,384]{1,0:T(8,128)(2,1)S(1)}, u32[]{:S(2)}, u32[]{:S(2)}) %collective-permute-start.3) | collective-permute-done | bytes 196640 | tf_op jit(solution)/shard_map/ppermute | solution.py:399
  22.4 10.9 %collective-permute-done.4.refs_1_ = bf16[256,384]{1,0:T(8,128)(2,1)S(1)} collective-permute-done((bf16[256,384]{1,0:T(8,128)(2,1)S(1)}, bf16[256,384]{1,0:T(8,128)(2,1)S(1)}, u32[]{:S(2)}, u32[]{:S(2)}) %collective-permute-start.4) | collective-permute-done | bytes 196640 | tf_op jit(solution)/shard_map/ppermute | solution.py:399
  34.8 1.7 %collective-permute-done.6.other = f32[1024,128]{1,0:T(8,128)S(1)} collective-permute-done((f32[1024,128]{1,0:T(8,128)S(1)}, f32[1024,128]{1,0:T(8,128)S(1)}, u32[]{:S(2)}, u32[]{:S(2)}) %collective-permute-start.6) | collective-permute-done | bytes 524320 | tf_op jit(solution)/shard_map/ppermute | solution.py:399
  36.5 1.4 %shard_map.63 = (bf16[8,256,128]{2,1,0:T(8,128)(2,1)S(1)}, bf16[2,256,128]{2,1,0:T(8,128)(2,1)S(1)}, f32[64,128]{1,0:T(8,128)S(1)}, f32[256,128]{1,0:T(8,128)S(1...) custom-call(s32[3]{0:T(128)S(1)} %pad_add_fusion.me, s32[6,8]{1,0:T(8,128)S(1)} %get-tuple-element.23.idx, ...), custom_call_target="tpu_custom_call" | custom-call | tf_op jit(solution)/shard_map/pallas_call | solution.py:26
  38.4 2.0 %collective-permute-start.13 = (f32[256,128]{1,0:T(8,128)S(1)}, f32[256,128]{1,0:T(8,128)S(1)}, u32[]{:S(2)}, u32[]{:S(2)}) collective-permute-start(f32[256,128]{1,0:T(8,128)S(1)} %get-tuple-element.33), channel_id=1, source_target_pairs={{0,8},{4,12},{8,0},{12,4},{1,9},{5,13},{9,1},{13,5},{2,10},{6,14},... | collective-permute-start | bytes 393224 | tf_op jit(solution)/shard_map/ppermute | solution.py:399
  40.4 2.8 %collective-permute-start.14 = (f32[256,128]{1,0:T(8,128)S(1)}, f32[256,128]{1,0:T(8,128)S(1)}, u32[]{:S(2)}, u32[]{:S(2)}) collective-permute-start(f32[256,128]{1,0:T(8,128)S(1)} %get-tuple-element.34), channel_id=1, source_target_pairs={{0,12},{4,0},{8,4},{12,8},{1,13},{5,1},{9,5},{13,9},{2,14},{6,2},{... | collective-permute-start | bytes 393224 | tf_op jit(solution)/shard_map/ppermute | solution.py:399
  43.2 3.0 %collective-permute-done.12.refs_8_.refs_4_ = f32[256,128]{1,0:T(8,128)S(1)} collective-permute-done((f32[256,128]{1,0:T(8,128)S(1)}, f32[256,128]{1,0:T(8,128)S(1)}, u32[]{:S(2)}, u32[]{:S(2)}) %collective-permute-start.12) | collective-permute-done | bytes 131104 | tf_op jit(solution)/shard_map/ppermute | solution.py:399
  46.2 4.8 %collective-permute-done.13.refs_9_.refs_5_ = f32[256,128]{1,0:T(8,128)S(1)} collective-permute-done((f32[256,128]{1,0:T(8,128)S(1)}, f32[256,128]{1,0:T(8,128)S(1)}, u32[]{:S(2)}, u32[]{:S(2)}) %collective-permute-start.13) | collective-permute-done | bytes 131104 | tf_op jit(solution)/shard_map/ppermute | solution.py:399
  51.6 1.5 %collective-permute-start.8 = (f32[64,128]{1,0:T(8,128)S(1)}, f32[64,128]{1,0:T(8,128)S(1)}, u32[]{:S(2)}, u32[]{:S(2)}) collective-permute-start(f32[64,128]{1,0:T(8,128)S(1)} %get-tuple-element.28), channel_id=1, source_target_pairs={{0,2},{2,0},{1,3},{3,1},{4,6},{6,4},{5,7},{7,5},{8,10},{10,8},{9,1... | collective-permute-start | bytes 98312 | tf_op jit(solution)/shard_map/ppermute | solution.py:413
  53.0 2.4 %collective-permute-done.8 = f32[64,128]{1,0:T(8,128)S(1)} collective-permute-done((f32[64,128]{1,0:T(8,128)S(1)}, f32[64,128]{1,0:T(8,128)S(1)}, u32[]{:S(2)}, u32[]{:S(2)}) %collective-permute-start.8) | collective-permute-done | bytes 32800 | tf_op jit(solution)/shard_map/ppermute | solution.py:413
  55.5 4.1 %collective-permute-start.11 = (f32[64,128]{1,0:T(8,128)S(1)}, f32[64,128]{1,0:T(8,128)S(1)}, u32[]{:S(2)}, u32[]{:S(2)}) collective-permute-start(f32[64,128]{1,0:T(8,128)S(1)} %add.8.refs_0_), channel_id=1, source_target_pairs={{0,12},{4,0},{8,4},{12,8},{1,13},{5,1},{9,5},{13,9},{2,14},{6,2},{... | collective-permute-start | bytes 98312 | tf_op jit(solution)/shard_map/ppermute | solution.py:399
  59.6 1.6 %collective-permute-done.11.refs_3_ = f32[64,128]{1,0:T(8,128)S(1)} collective-permute-done((f32[64,128]{1,0:T(8,128)S(1)}, f32[64,128]{1,0:T(8,128)S(1)}, u32[]{:S(2)}, u32[]{:S(2)}) %collective-permute-start.11) | collective-permute-done | bytes 32800 | tf_op jit(solution)/shard_map/ppermute | solution.py:399
  61.4 3.2 %collective-permute-done.10.refs_2_ = f32[64,128]{1,0:T(8,128)S(1)} collective-permute-done((f32[64,128]{1,0:T(8,128)S(1)}, f32[64,128]{1,0:T(8,128)S(1)}, u32[]{:S(2)}, u32[]{:S(2)}) %collective-permute-start.10) | collective-permute-done | bytes 32800 | tf_op jit(solution)/shard_map/ppermute | solution.py:399
  64.6 2.6 %collective-permute-done.9.refs_1_ = f32[64,128]{1,0:T(8,128)S(1)} collective-permute-done((f32[64,128]{1,0:T(8,128)S(1)}, f32[64,128]{1,0:T(8,128)S(1)}, u32[]{:S(2)}, u32[]{:S(2)}) %collective-permute-start.9) | collective-permute-done | bytes 32800 | tf_op jit(solution)/shard_map/ppermute | solution.py:399
  68.3 1.6 %collective-permute-start.18 = (f32[32,2048]{1,0:T(8,128)S(1)}, f32[32,2048]{1,0:T(8,128)S(1)}, u32[]{:S(2)}, u32[]{:S(2)}) collective-permute-start(f32[32,2048]{1,0:T(8,128)S(1)} %get-tuple-element.36.mine), channel_id=1, source_target_pairs={{0,2},{2,0},{1,3},{3,1},{4,6},{6,4},{5,7},{7,5},{8,10},{10,8},{9,1... | collective-permute-start | bytes 786440 | tf_op jit(solution)/shard_map/ppermute | solution.py:413
  69.8 4.9 %collective-permute-done.18.other = f32[32,2048]{1,0:T(8,128)S(1)} collective-permute-done((f32[32,2048]{1,0:T(8,128)S(1)}, f32[32,2048]{1,0:T(8,128)S(1)}, u32[]{:S(2)}, u32[]{:S(2)}) %collective-permute-start.18) | collective-permute-done | bytes 262176 | tf_op jit(solution)/shard_map/ppermute | solution.py:413
  75.5 2.6 %collective-permute-start.21 = (f32[128,128]{1,0:T(8,128)S(1)}, f32[128,128]{1,0:T(8,128)S(1)}, u32[]{:S(2)}, u32[]{:S(2)}) collective-permute-start(f32[128,128]{1,0:T(8,128)S(1)} %get-tuple-element.39), channel_id=1, source_target_pairs={{0,8},{4,12},{8,0},{12,4},{1,9},{5,13},{9,1},{13,5},{2,10},{6,14},... | collective-permute-start | bytes 196616 | tf_op jit(solution)/shard_map/ppermute | solution.py:399
  80.4 1.9 %collective-permute-done.20.refs_10_ = f32[128,128]{1,0:T(8,128)S(1)} collective-permute-done((f32[128,128]{1,0:T(8,128)S(1)}, f32[128,128]{1,0:T(8,128)S(1)}, u32[]{:S(2)}, u32[]{:S(2)}) %collective-permute-start.20) | collective-permute-done | bytes 65568 | tf_op jit(solution)/shard_map/ppermute | solution.py:399
  82.3 1.8 %collective-permute-done.21.refs_11_ = f32[128,128]{1,0:T(8,128)S(1)} collective-permute-done((f32[128,128]{1,0:T(8,128)S(1)}, f32[128,128]{1,0:T(8,128)S(1)}, u32[]{:S(2)}, u32[]{:S(2)}) %collective-permute-start.21) | collective-permute-done | bytes 65568 | tf_op jit(solution)/shard_map/ppermute | solution.py:399
  85.1 1.6 %collective-permute-start.23 = (f32[32,2048]{1,0:T(8,128)S(1)}, f32[32,2048]{1,0:T(8,128)S(1)}, u32[]{:S(2)}, u32[]{:S(2)}) collective-permute-start(f32[32,2048]{1,0:T(8,128)S(1)} %shard_map.67.mine), channel_id=1, source_target_pairs={{0,2},{2,0},{1,3},{3,1},{4,6},{6,4},{5,7},{7,5},{8,10},{10,8},{9,1... | collective-permute-start | bytes 786440 | tf_op jit(solution)/shard_map/ppermute | solution.py:413
  86.6 2.8 %collective-permute-start.26 = (f32[32,128]{1,0:T(8,128)S(1)}, f32[32,128]{1,0:T(8,128)S(1)}, u32[]{:S(2)}, u32[]{:S(2)}) collective-permute-start(f32[32,128]{1,0:T(8,128)S(1)} %shard_map.66.after.refs_0_), channel_id=1, source_target_pairs={{0,12},{4,0},{8,4},{12,8},{1,13},{5,1},{9,5},{13,9},{2,14},{6,2},{... | collective-permute-start | bytes 49160 | tf_op jit(solution)/shard_map/ppermute | solution.py:399
  90.9 3.2 %collective-permute-done.25.refs_1_.refs_2_ = f32[32,128]{1,0:T(8,128)S(1)} collective-permute-done((f32[32,128]{1,0:T(8,128)S(1)}, f32[32,128]{1,0:T(8,128)S(1)}, u32[]{:S(2)}, u32[]{:S(2)}) %collective-permute-start.25) | collective-permute-done | bytes 16416 | tf_op jit(solution)/shard_map/ppermute | solution.py:399
  95.9 2.3 %shard_map.69.factor = f32[64,64]{1,0:T(8,128)S(1)} custom-call(f32[32,2048]{1,0:T(8,128)S(1)} %shard_map.68.after.own, f32[32,128]{1,0:T(8,128)S(1)} %shard_map.66.after.refs_0_, f32[32,128]{1,0:T(8,128)S(1)} %collective-permute-done.24.refs_0_.refs_1_, f32[32,128]{1,0:T(8,128)S(1)} %collective-permute-done.25.refs_1_.refs_2_, ...), custom_call_target="tpu_custom_call" | custom-call | tf_op jit(solution)/shard_map/pallas_call | solution.py:26
  98.2 1.5 %shard_map.70 = (bf16[192,2048]{1,0:T(8,128)(2,1)S(1)}, f32[32,128]{1,0:T(8,128)S(1)}) custom-call(s32[3]{0:T(128)S(1)} %pad_add_fusion.me, f32[64,64]{1,0:T(8,128)S(1)} %shard_map.69.factor, f32[32,2048]{1,0:T(8,128)S(1)} %shard_map.68.after.own, f32[32,2048]{1,0:T(8,128)S(1)} %collective-permute-done.27.other), custom_call_target="tpu_custom_call" | custom-call | tf_op jit(solution)/shard_map/pallas_call | solution.py:26
  100.7 1.9 %collective-permute-start.28 = (f32[32,128]{1,0:T(8,128)S(1)}, f32[32,128]{1,0:T(8,128)S(1)}, u32[]{:S(2)}, u32[]{:S(2)}) collective-permute-start(f32[32,128]{1,0:T(8,128)S(1)} %get-tuple-element.42.refs_0_), channel_id=1, source_target_pairs={{0,4},{4,8},{8,12},{12,0},{1,5},{5,9},{9,13},{13,1},{2,6},{6,10},{... | collective-permute-start | bytes 49160 | tf_op jit(solution)/shard_map/ppermute | solution.py:399
  103.4 1.9 %collective-permute-done.29.refs_2_ = f32[32,128]{1,0:T(8,128)S(1)} collective-permute-done((f32[32,128]{1,0:T(8,128)S(1)}, f32[32,128]{1,0:T(8,128)S(1)}, u32[]{:S(2)}, u32[]{:S(2)}) %collective-permute-start.29) | collective-permute-done | bytes 16416 | tf_op jit(solution)/shard_map/ppermute | solution.py:399
  106.2 3.8 %shard_map.71 = f32[32,2048]{1,0:T(8,128)} custom-call(s32[3]{0:T(128)S(1)} %pad_add_fusion.me, bf16[192,2048]{1,0:T(8,128)(2,1)S(1)} %get-tuple-element.41.mapped, f32[32,128]{1,0:T(8,128)S(1)} %get-tuple-element.42.refs_0_, f32[32,128]{1,0:T(8,128)S(1)} %collective-permute-done.28.refs_1_, f32[32,128]{1,0:T(8,128)S(1)} %collective-permute-done.29.refs_2_, ...), custom_call_target="tpu_custom_call" | custom-call | tf_op jit(solution)/shard_map/pallas_call | solution.py:26
  (53 shorter events, 18.9 us)
Async XLA Ops:
  2.0 6.4 %collective-permute-start.2 = (s32[3,8]{1,0:T(4,128)S(1)}, s32[3,8]{1,0:T(4,128)S(1)}, u32[]{:S(2)}, u32[]{:S(2)}) collective-permute-start(s32[3,8]{1,0:T(4,128)S(1)} %concatenate.3.refs_0_), channel_id=1, source_target_pairs={{0,12},{4,0},{8,4},{12,8},{1,13},{5,1},{9,5},{13,9},{2,14},{6,2},{... | collective-permute-start | bytes 296 | tf_op jit(solution)/shard_map/ppermute | solution.py:399
  7.0 4.5 %collective-permute-start.1 = (s32[3,8]{1,0:T(4,128)S(1)}, s32[3,8]{1,0:T(4,128)S(1)}, u32[]{:S(2)}, u32[]{:S(2)}) collective-permute-start(s32[3,8]{1,0:T(4,128)S(1)} %concatenate.3.refs_0_), channel_id=1, source_target_pairs={{0,8},{4,12},{8,0},{12,4},{1,9},{5,13},{9,1},{13,5},{2,10},{6,14},... | collective-permute-start | bytes 296 | tf_op jit(solution)/shard_map/ppermute | solution.py:399
  7.0 5.4 %collective-permute-start = (s32[3,8]{1,0:T(4,128)S(1)}, s32[3,8]{1,0:T(4,128)S(1)}, u32[]{:S(2)}, u32[]{:S(2)}) collective-permute-start(s32[3,8]{1,0:T(4,128)S(1)} %concatenate.3.refs_0_), channel_id=1, source_target_pairs={{0,4},{4,8},{8,12},{12,0},{1,5},{5,9},{9,13},{13,1},{2,6},{6,10},{... | collective-permute-start | bytes 296 | tf_op jit(solution)/shard_map/ppermute | solution.py:399
  13.8 5.5 %copy-start.1 = (bf16[2048,384]{1,0:T(8,128)(2,1)S(1)}, bf16[2048,384]{1,0:T(8,128)(2,1)}, u32[]{:S(2)}) copy-start(bf16[2048,384]{1,0:T(8,128)(2,1)} %emb.3) | copy-start | bytes 4718596
  16.1 6.3 %collective-permute-start.3 = (bf16[256,384]{1,0:T(8,128)(2,1)S(1)}, bf16[256,384]{1,0:T(8,128)(2,1)S(1)}, u32[]{:S(2)}, u32[]{:S(2)}) collective-permute-start(bf16[256,384]{1,0:T(8,128)(2,1)S(1)} %get-tuple-element.24), channel_id=1, source_target_pairs={{0,12},{4,0},{8,4},{12,8},{1,13},{5,1},{9,5},{13,9},{2,14},{6,2},{... | collective-permute-start | bytes 589832 | tf_op jit(solution)/shard_map/ppermute | solution.py:399
  16.7 16.7 %collective-permute-start.4 = (bf16[256,384]{1,0:T(8,128)(2,1)S(1)}, bf16[256,384]{1,0:T(8,128)(2,1)S(1)}, u32[]{:S(2)}, u32[]{:S(2)}) collective-permute-start(bf16[256,384]{1,0:T(8,128)(2,1)S(1)} %get-tuple-element.25), channel_id=1, source_target_pairs={{0,8},{4,12},{8,0},{12,4},{1,9},{5,13},{9,1},{13,5},{2,10},{6,14},... | collective-permute-start | bytes 589832 | tf_op jit(solution)/shard_map/ppermute | solution.py:399
  17.3 16.0 %collective-permute-start.5 = (bf16[256,384]{1,0:T(8,128)(2,1)S(1)}, bf16[256,384]{1,0:T(8,128)(2,1)S(1)}, u32[]{:S(2)}, u32[]{:S(2)}) collective-permute-start(bf16[256,384]{1,0:T(8,128)(2,1)S(1)} %get-tuple-element.26), channel_id=1, source_target_pairs={{0,4},{4,8},{8,12},{12,0},{1,5},{5,9},{9,13},{13,1},{2,6},{6,10},{... | collective-permute-start | bytes 589832 | tf_op jit(solution)/shard_map/ppermute | solution.py:399
  20.3 14.3 %collective-permute-start.7 = (f32[1024,128]{1,0:T(8,128)S(1)}, f32[1024,128]{1,0:T(8,128)S(1)}, u32[]{:S(2)}, u32[]{:S(2)}) collective-permute-start(f32[1024,128]{1,0:T(8,128)S(1)} %shard_map.61.mine), channel_id=1, source_target_pairs={{0,1},{1,0},{2,3},{3,2},{4,5},{5,4},{6,7},{7,6},{8,9},{9,8},{10,11... | collective-permute-start | bytes 1572872 | tf_op jit(solution)/shard_map/ppermute | solution.py:399
  34.5 2.0 %collective-permute-start.6 = (f32[1024,128]{1,0:T(8,128)S(1)}, f32[1024,128]{1,0:T(8,128)S(1)}, u32[]{:S(2)}, u32[]{:S(2)}) collective-permute-start(f32[1024,128]{1,0:T(8,128)S(1)} %shard_map.60.mine), channel_id=1, source_target_pairs={{0,1},{1,0},{2,3},{3,2},{4,5},{5,4},{6,7},{7,6},{8,9},{9,8},{10,11... | collective-permute-start | bytes 1572872 | tf_op jit(solution)/shard_map/ppermute | solution.py:399
  37.9 8.3 %collective-permute-start.12 = (f32[256,128]{1,0:T(8,128)S(1)}, f32[256,128]{1,0:T(8,128)S(1)}, u32[]{:S(2)}, u32[]{:S(2)}) collective-permute-start(f32[256,128]{1,0:T(8,128)S(1)} %get-tuple-element.32), channel_id=1, source_target_pairs={{0,4},{4,8},{8,12},{12,0},{1,5},{5,9},{9,13},{13,1},{2,6},{6,10},{... | collective-permute-start | bytes 393224 | tf_op jit(solution)/shard_map/ppermute | solution.py:399
  38.4 12.6 %collective-permute-start.13 = (f32[256,128]{1,0:T(8,128)S(1)}, f32[256,128]{1,0:T(8,128)S(1)}, u32[]{:S(2)}, u32[]{:S(2)}) collective-permute-start(f32[256,128]{1,0:T(8,128)S(1)} %get-tuple-element.33), channel_id=1, source_target_pairs={{0,8},{4,12},{8,0},{12,4},{1,9},{5,13},{9,1},{13,5},{2,10},{6,14},... | collective-permute-start | bytes 393224 | tf_op jit(solution)/shard_map/ppermute | solution.py:399
  40.4 10.6 %collective-permute-start.14 = (f32[256,128]{1,0:T(8,128)S(1)}, f32[256,128]{1,0:T(8,128)S(1)}, u32[]{:S(2)}, u32[]{:S(2)}) collective-permute-start(f32[256,128]{1,0:T(8,128)S(1)} %get-tuple-element.34), channel_id=1, source_target_pairs={{0,12},{4,0},{8,4},{12,8},{1,13},{5,1},{9,5},{13,9},{2,14},{6,2},{... | collective-permute-start | bytes 393224 | tf_op jit(solution)/shard_map/ppermute | solution.py:399
  46.2 21.0 %collective-permute-start.15 = (f32[256,128]{1,0:T(8,128)S(1)}, f32[256,128]{1,0:T(8,128)S(1)}, u32[]{:S(2)}, u32[]{:S(2)}) collective-permute-start(f32[256,128]{1,0:T(8,128)S(1)} %collective-permute-done.12.refs_8_.refs_4_), channel_id=1, source_target_pairs={{0,1},{1,0},{2,3},{3,2},{4,5},{5,4},{6,7},{7,6},{8,9},{9,8},{10,11... | collective-permute-start | bytes 393224 | tf_op jit(solution)/shard_map/ppermute | solution.py:399
  51.0 16.2 %collective-permute-start.16 = (f32[256,128]{1,0:T(8,128)S(1)}, f32[256,128]{1,0:T(8,128)S(1)}, u32[]{:S(2)}, u32[]{:S(2)}) collective-permute-start(f32[256,128]{1,0:T(8,128)S(1)} %collective-permute-done.13.refs_9_.refs_5_), channel_id=1, source_target_pairs={{0,1},{1,0},{2,3},{3,2},{4,5},{5,4},{6,7},{7,6},{8,9},{9,8},{10,11... | collective-permute-start | bytes 393224 | tf_op jit(solution)/shard_map/ppermute | solution.py:399
  51.0 16.2 %collective-permute-start.17 = (f32[256,128]{1,0:T(8,128)S(1)}, f32[256,128]{1,0:T(8,128)S(1)}, u32[]{:S(2)}, u32[]{:S(2)}) collective-permute-start(f32[256,128]{1,0:T(8,128)S(1)} %collective-permute-done.14.refs_10_.refs_6_), channel_id=1, source_target_pairs={{0,1},{1,0},{2,3},{3,2},{4,5},{5,4},{6,7},{7,6},{8,9},{9,8},{10,11... | collective-permute-start | bytes 393224 | tf_op jit(solution)/shard_map/ppermute | solution.py:399
  51.6 3.9 %collective-permute-start.8 = (f32[64,128]{1,0:T(8,128)S(1)}, f32[64,128]{1,0:T(8,128)S(1)}, u32[]{:S(2)}, u32[]{:S(2)}) collective-permute-start(f32[64,128]{1,0:T(8,128)S(1)} %get-tuple-element.28), channel_id=1, source_target_pairs={{0,2},{2,0},{1,3},{3,1},{4,6},{6,4},{5,7},{7,5},{8,10},{10,8},{9,1... | collective-permute-start | bytes 98312 | tf_op jit(solution)/shard_map/ppermute | solution.py:413
  55.5 5.7 %collective-permute-start.11 = (f32[64,128]{1,0:T(8,128)S(1)}, f32[64,128]{1,0:T(8,128)S(1)}, u32[]{:S(2)}, u32[]{:S(2)}) collective-permute-start(f32[64,128]{1,0:T(8,128)S(1)} %add.8.refs_0_), channel_id=1, source_target_pairs={{0,12},{4,0},{8,4},{12,8},{1,13},{5,1},{9,5},{13,9},{2,14},{6,2},{... | collective-permute-start | bytes 98312 | tf_op jit(solution)/shard_map/ppermute | solution.py:399
  59.6 5.0 %collective-permute-start.10 = (f32[64,128]{1,0:T(8,128)S(1)}, f32[64,128]{1,0:T(8,128)S(1)}, u32[]{:S(2)}, u32[]{:S(2)}) collective-permute-start(f32[64,128]{1,0:T(8,128)S(1)} %add.8.refs_0_), channel_id=1, source_target_pairs={{0,8},{4,12},{8,0},{12,4},{1,9},{5,13},{9,1},{13,5},{2,10},{6,14},... | collective-permute-start | bytes 98312 | tf_op jit(solution)/shard_map/ppermute | solution.py:399
  61.2 6.0 %collective-permute-start.9 = (f32[64,128]{1,0:T(8,128)S(1)}, f32[64,128]{1,0:T(8,128)S(1)}, u32[]{:S(2)}, u32[]{:S(2)}) collective-permute-start(f32[64,128]{1,0:T(8,128)S(1)} %add.8.refs_0_), channel_id=1, source_target_pairs={{0,4},{4,8},{8,12},{12,0},{1,5},{5,9},{9,13},{13,1},{2,6},{6,10},{... | collective-permute-start | bytes 98312 | tf_op jit(solution)/shard_map/ppermute | solution.py:399
  68.3 6.4 %collective-permute-start.18 = (f32[32,2048]{1,0:T(8,128)S(1)}, f32[32,2048]{1,0:T(8,128)S(1)}, u32[]{:S(2)}, u32[]{:S(2)}) collective-permute-start(f32[32,2048]{1,0:T(8,128)S(1)} %get-tuple-element.36.mine), channel_id=1, source_target_pairs={{0,2},{2,0},{1,3},{3,1},{4,6},{6,4},{5,7},{7,5},{8,10},{10,8},{9,1... | collective-permute-start | bytes 786440 | tf_op jit(solution)/shard_map/ppermute | solution.py:413
  75.4 4.0 %collective-permute-start.19 = (f32[32,2048]{1,0:T(8,128)S(1)}, f32[32,2048]{1,0:T(8,128)S(1)}, u32[]{:S(2)}, u32[]{:S(2)}) collective-permute-start(f32[32,2048]{1,0:T(8,128)S(1)} %get-tuple-element.37.own.refs_0_), channel_id=1, source_target_pairs={{0,1},{1,0},{2,3},{3,2},{4,5},{5,4},{6,7},{7,6},{8,9},{9,8},{10,11... | collective-permute-start | bytes 786440 | tf_op jit(solution)/shard_map/ppermute | solution.py:399
  75.4 6.8 %collective-permute-start.20 = (f32[128,128]{1,0:T(8,128)S(1)}, f32[128,128]{1,0:T(8,128)S(1)}, u32[]{:S(2)}, u32[]{:S(2)}) collective-permute-start(f32[128,128]{1,0:T(8,128)S(1)} %get-tuple-element.38), channel_id=1, source_target_pairs={{0,4},{4,8},{8,12},{12,0},{1,5},{5,9},{9,13},{13,1},{2,6},{6,10},{... | collective-permute-start | bytes 196616 | tf_op jit(solution)/shard_map/ppermute | solution.py:399
  75.5 8.5 %collective-permute-start.21 = (f32[128,128]{1,0:T(8,128)S(1)}, f32[128,128]{1,0:T(8,128)S(1)}, u32[]{:S(2)}, u32[]{:S(2)}) collective-permute-start(f32[128,128]{1,0:T(8,128)S(1)} %get-tuple-element.39), channel_id=1, source_target_pairs={{0,8},{4,12},{8,0},{12,4},{1,9},{5,13},{9,1},{13,5},{2,10},{6,14},... | collective-permute-start | bytes 196616 | tf_op jit(solution)/shard_map/ppermute | solution.py:399
  78.1 6.0 %collective-permute-start.22 = (f32[128,128]{1,0:T(8,128)S(1)}, f32[128,128]{1,0:T(8,128)S(1)}, u32[]{:S(2)}, u32[]{:S(2)}) collective-permute-start(f32[128,128]{1,0:T(8,128)S(1)} %get-tuple-element.40), channel_id=1, source_target_pairs={{0,12},{4,0},{8,4},{12,8},{1,13},{5,1},{9,5},{13,9},{2,14},{6,2},{... | collective-permute-start | bytes 196616 | tf_op jit(solution)/shard_map/ppermute | solution.py:399
  85.1 10.1 %collective-permute-start.23 = (f32[32,2048]{1,0:T(8,128)S(1)}, f32[32,2048]{1,0:T(8,128)S(1)}, u32[]{:S(2)}, u32[]{:S(2)}) collective-permute-start(f32[32,2048]{1,0:T(8,128)S(1)} %shard_map.67.mine), channel_id=1, source_target_pairs={{0,2},{2,0},{1,3},{3,1},{4,6},{6,4},{5,7},{7,5},{8,10},{10,8},{9,1... | collective-permute-start | bytes 786440 | tf_op jit(solution)/shard_map/ppermute | solution.py:413
  86.6 4.3 %collective-permute-start.26 = (f32[32,128]{1,0:T(8,128)S(1)}, f32[32,128]{1,0:T(8,128)S(1)}, u32[]{:S(2)}, u32[]{:S(2)}) collective-permute-start(f32[32,128]{1,0:T(8,128)S(1)} %shard_map.66.after.refs_0_), channel_id=1, source_target_pairs={{0,12},{4,0},{8,4},{12,8},{1,13},{5,1},{9,5},{13,9},{2,14},{6,2},{... | collective-permute-start | bytes 49160 | tf_op jit(solution)/shard_map/ppermute | solution.py:399
  89.4 4.6 %collective-permute-start.25 = (f32[32,128]{1,0:T(8,128)S(1)}, f32[32,128]{1,0:T(8,128)S(1)}, u32[]{:S(2)}, u32[]{:S(2)}) collective-permute-start(f32[32,128]{1,0:T(8,128)S(1)} %shard_map.66.after.refs_0_), channel_id=1, source_target_pairs={{0,8},{4,12},{8,0},{12,4},{1,9},{5,13},{9,1},{13,5},{2,10},{6,14},... | collective-permute-start | bytes 49160 | tf_op jit(solution)/shard_map/ppermute | solution.py:399
  89.7 5.5 %collective-permute-start.24 = (f32[32,128]{1,0:T(8,128)S(1)}, f32[32,128]{1,0:T(8,128)S(1)}, u32[]{:S(2)}, u32[]{:S(2)}) collective-permute-start(f32[32,128]{1,0:T(8,128)S(1)} %shard_map.66.after.refs_0_), channel_id=1, source_target_pairs={{0,4},{4,8},{8,12},{12,0},{1,5},{5,9},{9,13},{13,1},{2,6},{6,10},{... | collective-permute-start | bytes 49160 | tf_op jit(solution)/shard_map/ppermute | solution.py:399
  95.8 2.4 %collective-permute-start.27 = (f32[32,2048]{1,0:T(8,128)S(1)}, f32[32,2048]{1,0:T(8,128)S(1)}, u32[]{:S(2)}, u32[]{:S(2)}) collective-permute-start(f32[32,2048]{1,0:T(8,128)S(1)} %shard_map.68.after.own), channel_id=1, source_target_pairs={{0,1},{1,0},{2,3},{3,2},{4,5},{5,4},{6,7},{7,6},{8,9},{9,8},{10,11... | collective-permute-start | bytes 786440 | tf_op jit(solution)/shard_map/ppermute | solution.py:399
  99.7 3.7 %collective-permute-start.30 = (f32[32,128]{1,0:T(8,128)S(1)}, f32[32,128]{1,0:T(8,128)S(1)}, u32[]{:S(2)}, u32[]{:S(2)}) collective-permute-start(f32[32,128]{1,0:T(8,128)S(1)} %get-tuple-element.42.refs_0_), channel_id=1, source_target_pairs={{0,12},{4,0},{8,4},{12,8},{1,13},{5,1},{9,5},{13,9},{2,14},{6,2},{... | collective-permute-start | bytes 49160 | tf_op jit(solution)/shard_map/ppermute | solution.py:399
  100.7 4.6 %collective-permute-start.29 = (f32[32,128]{1,0:T(8,128)S(1)}, f32[32,128]{1,0:T(8,128)S(1)}, u32[]{:S(2)}, u32[]{:S(2)}) collective-permute-start(f32[32,128]{1,0:T(8,128)S(1)} %get-tuple-element.42.refs_0_), channel_id=1, source_target_pairs={{0,8},{4,12},{8,0},{12,4},{1,9},{5,13},{9,1},{13,5},{2,10},{6,14},... | collective-permute-start | bytes 49160 | tf_op jit(solution)/shard_map/ppermute | solution.py:399
  100.7 5.5 %collective-permute-start.28 = (f32[32,128]{1,0:T(8,128)S(1)}, f32[32,128]{1,0:T(8,128)S(1)}, u32[]{:S(2)}, u32[]{:S(2)}) collective-permute-start(f32[32,128]{1,0:T(8,128)S(1)} %get-tuple-element.42.refs_0_), channel_id=1, source_target_pairs={{0,4},{4,8},{8,12},{12,0},{1,5},{5,9},{9,13},{13,1},{2,6},{6,10},{... | collective-permute-start | bytes 49160 | tf_op jit(solution)/shard_map/ppermute | solution.py:399
  (2 other events, 4.5 us)

commit v6 on v5

--- a/solution.py
+++ b/solution.py
@@ -13,25 +13,22 @@
 VMEM = pl.BlockSpec(memory_space=pltpu.VMEM)
 SMEM = pl.BlockSpec(memory_space=pltpu.SMEM)
 ANY = pl.BlockSpec(memory_space=pl.ANY)
-HBM = pl.BlockSpec(memory_space=pltpu.HBM)
 F32 = jnp.float32
 BF16 = jnp.bfloat16
 HIGHEST = lax.Precision.HIGHEST
 NT = (((1,), (1,)), ((), ()))
 
 
-def call(body, outs, args, smem_in=(), smem_out=(), any_in=(), hbm_in=(), scratch=()):
+def call(body, outs, args, smem_in=(), smem_out=(), any_in=()):
     single = not isinstance(outs, (list, tuple))
     shapes = [outs] if single else list(outs)
     result = pl.pallas_call(
         body,
         out_shape=shapes,
         in_specs=[
-            SMEM if i in smem_in else ANY if i in any_in else HBM if i in hbm_in else VMEM
-            for i in range(len(args))
+            SMEM if i in smem_in else ANY if i in any_in else VMEM for i in range(len(args))
         ],
         out_specs=[SMEM if i in smem_out else VMEM for i in range(len(shapes))],
-        scratch_shapes=list(scratch),
         compiler_params=pltpu.CompilerParams(vmem_limit_bytes=48 * 2**20),
     )(*args)
     return result[0] if single else result
@@ -133,11 +130,9 @@
 
 def plan_body(dims, me, *refs):
     row_count, capacity, slots, blocks_here = dims
-    lists, (emb_hbm, idx) = refs[:row_count], refs[row_count : row_count + 2]
-    sends, (emb, done) = refs[row_count + 2 : -2], refs[-2:]
+    lists, (emb, after, idx) = refs[:row_count], refs[row_count : row_count + 3]
+    sends = refs[row_count + 3 :]
     row = me[0]
-    copy = pltpu.make_async_copy(emb_hbm, emb, done)
-    copy.start()
 
     def clear(i, carry):
         for line in range(6):
@@ -190,7 +185,6 @@
             return (counts[0] + hit.astype(jnp.int32),)
 
         ranked(lists[k], 1, write_in)
-    copy.wait()
     for k in range(1, row_count):
         for j in range(capacity):
             sends[k - 1][j * BLOCK : (j + 1) * BLOCK, :] = emb[at_block(idx[4, k * capacity + j]), :]
@@ -263,6 +257,14 @@
                     sends[k - 1][inner * BLOCK : (inner + 1) * BLOCK, :] = tile
 
     pick_columns(idx, row_count, capacity, values, sends, per_core * BLOCK)
+
+
+def split_body(row_count, per_core, *refs):
+    others = row_count - 1
+    messages, outs = refs[:others], refs[-others:]
+    for message, out in zip(messages, outs):
+        for inner in range(per_core):
+            out[inner] = pack(message[inner * BLOCK : (inner + 1) * BLOCK, :])
 
 
 def pick_columns(idx, row_count, capacity, source, sends, base):
@@ -311,13 +313,12 @@
                 packed = home_tiles[j]
             else:
                 inner = j % per_core
-                part = slice(inner * BLOCK, (inner + 1) * BLOCK)
                 if j < per_core:
                     place = core * per_core + inner
-                    packed = pack(sent[k - 1][part, :])
+                    packed = sent[k - 1][inner]
                 else:
                     place = (1 - core) * per_core + inner
-                    packed = pack(shared[k - 1][part, :])
+                    packed = shared[k - 1][inner]
                 slot = k * capacity + place
                 values = arrived(k, place)
             add(idx[4, slot], packed, scaled(values, idx[5, slot]))
@@ -328,12 +329,13 @@
     terms, refs = refs[:row_count], refs[row_count:]
     own, near_tiles, home_tiles, self_tiles = refs[:4]
     sent, shared = refs[4 : 3 + row_count], refs[3 + row_count : 2 + 2 * row_count]
+    messages = refs[2 + 2 * row_count : -3]
     out, degree, inverse = refs[-3:]
     total = functools.reduce(lambda total, term: total + term[...], terms[1:], terms[0][...])
     degree[...] = total
     inverse[...] = 1.0 / jnp.sqrt(total)
     apply_tiles(
-        dims, me, idx, inverse, own, sent, per_core * BLOCK, near_tiles, home_tiles, sent, shared, self_tiles, out
+        dims, me, idx, inverse, own, messages, per_core * BLOCK, near_tiles, home_tiles, sent, shared, self_tiles, out
     )
 
 
@@ -403,14 +405,17 @@
     return [value] + [shift_by(value, "rows", row_count, k) for k in range(1, row_count)]
 
 
+def pair_step(value, name, flip):
+    return lax.ppermute(value, name, [(i, i ^ flip) for i in range(lax.axis_size(name))])
+
+
 def pair_sum(value, axes):
     terms = None
     steps = [(name, 1 << bit) for name in axes for bit in range((lax.axis_size(name) - 1).bit_length())]
     for name, flip in steps:
         if terms is not None:
             value = terms[0] + terms[1]
-        size = lax.axis_size(name)
-        terms = (value, lax.ppermute(value, name, [(i, i ^ flip) for i in range(size)]))
+        terms = (value, pair_step(value, name, flip))
     return terms
 
 
@@ -436,24 +441,23 @@
         [pair_list[0], jnp.broadcast_to(pair_count[:, None], (1, slots))], axis=0
     )
     lists = row_terms(own_list, row_count)
-    planned = call(
-        functools.partial(plan_body, (row_count, capacity, slots, blocks_here)),
-        [sds((6, slots), jnp.int32)] + [sds((capacity * BLOCK, half_features), BF16) for _ in others],
-        [me, *lists, embeddings],
-        smem_in=range(1 + row_count),
-        hbm_in=(row_count + 1,),
-        smem_out=(0,),
-        scratch=[pltpu.VMEM(embeddings.shape, BF16), pltpu.SemaphoreType.DMA],
-    )
-    idx, sends = planned[0], planned[1:]
-    far = [shift_by(sends[k - 1], "rows", row_count, -k) for k in others]
-
     self_part = call(
         functools.partial(self_distance_body, own_blocks, tile_count),
         sds((own_blocks * BLOCK, BLOCK), F32),
         [me, embeddings],
         smem_in=(0,),
     )
+    planned = call(
+        functools.partial(plan_body, (row_count, capacity, slots, blocks_here)),
+        [sds((6, slots), jnp.int32)] + [sds((capacity * BLOCK, half_features), BF16) for _ in others],
+        [me, *lists, embeddings, self_part],
+        smem_in=range(1 + row_count),
+        any_in=(row_count + 2,),
+        smem_out=(0,),
+    )
+    idx, sends = planned[0], planned[1:]
+    far = [shift_by(sends[k - 1], "rows", row_count, -k) for k in others]
+
     self_other = shift_by(self_part, "cols", core_count, 1)
     self_tiles, self_sums = call(
         functools.partial(self_tile_body, own_blocks),
@@ -482,8 +486,14 @@
     near_tiles, home_tiles, degrees, sends = tiles[0], tiles[1], tiles[2], tiles[3:]
     mine, other = pair_sum(degrees, ("tiles",))
     degree_terms = row_terms(mine + other, row_count)
-    sent = [shift_by(sends[k - 1], "rows", row_count, k) for k in others]
-    shared = [shift_by(message, "cols", core_count, 1) for message in sent]
+    messages = [shift_by(sends[k - 1], "rows", row_count, k) for k in others]
+    sent = call(
+        functools.partial(split_body, row_count, per_core),
+        [sds((per_core, 2 * BLOCK, BLOCK), BF16) for _ in others],
+        [*messages, *degree_terms],
+        any_in=range(row_count - 1, 2 * row_count - 1),
+    )
+    shared = [shift_by(tile, "cols", core_count, 1) for tile in sent]
 
     tile_args = [near_tiles, home_tiles, self_tiles, *sent, *shared]
     block_shape = sds((own_cols, rows_here), F32)
@@ -493,7 +503,7 @@
     part, degree, inverse = call(
         functools.partial(first_apply_body, dims),
         [block_shape, table, table],
-        [me, idx, *degree_terms, values, *tile_args],
+        [me, idx, *degree_terms, values, *tile_args, *messages],
         smem_in=(0, 1),
     )
     mine, other = pair_sum(part, ("tiles",))
@@ -508,7 +518,9 @@
 
     mapped_other = shift_by(mapped, "cols", core_count, 1)
     first_gram = call(gram_body, folded_square, [me, mapped, mapped_other], smem_in=(0,))
-    gram_terms = row_terms(first_gram, row_count)
+    steps = (row_count - 1).bit_length()
+    for bit in range(steps - 1):
+        first_gram = first_gram + pair_step(first_gram, "rows", 1 << bit)
     part = call(
         functools.partial(second_apply_body, dims),
         block_shape,
@@ -516,13 +528,14 @@
         smem_in=(0, 1),
         any_in=(3,),
     )
+    gram_terms = (first_gram, pair_step(first_gram, "rows", 1 << (steps - 1)))
     mine, other = pair_sum(part, ("tiles",))
     second = call(
         functools.partial(last_mapped_body, blocks_here),
         block_shape,
-        [me, inverse, mine, other, *gram_terms[1:]],
+        [me, inverse, mine, other, gram_terms[1]],
         smem_in=(0,),
-        any_in=range(4, 3 + row_count),
+        any_in=(4,),
     )
     second_other = shift_by(second, "cols", core_count, 1)
     factor = call(factor_body, square, [second, *gram_terms], any_in=(0,))

time: 110 us -> 105 us (0.955)
  waiting for transfers between devices: 53.3 us -> 47.8 us
    ppermute x28 -> x25, waiting for transfers between devices: 46 us -> 29.5 us  [shift_by(): lax.ppermute(value, axes, [(i, (i + shift) % size) for i in range(size)])]
    ppermute x3 -> x5, waiting for transfers between devices: 7.31 us -> 18.3 us  [pair_step(): lax.ppermute(value, name, [(i, i ^ flip) for i in range(lax.axis_size(nam...]
    ppermute x3 -> x5, starting transfers between devices: 4.61 us -> 5.7 us  [pair_step(): lax.ppermute(value, name, [(i, i ^ flip) for i in range(lax.axis_size(nam...]
    ppermute x28 -> x25, starting transfers between devices: 30 us -> 29.1 us  [shift_by(): lax.ppermute(value, axes, [(i, (i + shift) % size) for i in range(size)])]
    pallas_call x13 -> x14, Pallas kernels: 18 us -> 17.9 us  [call(): pl.pallas_call(body, out_shape=shapes, in_specs=[SMEM if i in smem_in els...]
  transfers between devices with their start and end apart: 31 -> 30, of which waited for: 21 -> 17; matrix products, arithmetic and copies ran while one was open for 1% -> 1% of each run, Pallas kernels for 5% -> 6%
where the time goes in v6:
time: 105 us
  waiting for transfers between devices  47.8 us (46%)
  starting transfers between devices  34.8 us (33%)
  Pallas kernels  17.9 us (17%)
  local copies, waits for them, and re-layouts  2.7 us (3%)
  between operations  1.46 us (1%)
    ppermute x25, waiting for transfers between devices, shift_by(): lax.ppermute(value, axes, [(i, (i + shift) % size) for i in range(size)])  29.5 us
    ppermute x25, starting transfers between devices, shift_by(): lax.ppermute(value, axes, [(i, (i + shift) % size) for i in range(size)])  29.1 us
    ppermute x5, waiting for transfers between devices, pair_step(): lax.ppermute(value, name, [(i, i ^ flip) for i in range(lax.axis_size(nam...  18.3 us
    pallas_call x14, Pallas kernels, call(): pl.pallas_call(body, out_shape=shapes, in_specs=[SMEM if i in smem_in els...  17.9 us
    ppermute x5, starting transfers between devices, pair_step(): lax.ppermute(value, name, [(i, i ^ flip) for i in range(lax.axis_size(nam...  5.7 us
  transfers between devices with their start and end apart: 30, of which 17 were waited for; matrix products, arithmetic and copies ran while one was open for 1% of the time, Pallas kernels for 6%

profile of v6, /device:TPU:0, one launch (start us, length us, event | category | flops | bytes accessed | tf_op | source)
XLA Modules:
  0.0 104.8 jit_solution(5005728585414458395)
XLA Ops:
  2.0 5.0 %collective-permute-start.2 = (s32[3,8]{1,0:T(4,128)S(1)}, s32[3,8]{1,0:T(4,128)S(1)}, u32[]{:S(2)}, u32[]{:S(2)}) collective-permute-start(s32[3,8]{1,0:T(4,128)S(1)} %concatenate.3.refs_0_), channel_id=1, source_target_pairs={{0,12},{4,0},{8,4},{12,8},{1,13},{5,1},{9,5},{13,9},{2,14},{6,2},{... | collective-permute-start | bytes 296 | tf_op jit(solution)/shard_map/ppermute | solution.py:401
  8.1 1.4 %copy-done = bf16[2048,384]{1,0:T(8,128)(2,1)S(1)} copy-done((bf16[2048,384]{1,0:T(8,128)(2,1)S(1)}, bf16[2048,384]{1,0:T(8,128)(2,1)}, u32[]{:S(2)}) %copy-start) | copy-done | bytes 1572888
  12.4 2.1 %shard_map.60 = (s32[6,8]{1,0:T(8,128)S(1)}, bf16[256,384]{1,0:T(8,128)(2,1)S(1)}, bf16[256,384]{1,0:T(8,128)(2,1)S(1)}, bf16[256,384]{1,0:T(8,128)(2,1)S(1)}) custom-call(s32[3]{0:T(128)S(1)} %pad_add_fusion.me, s32[3,8]{1,0:T(4,128)S(1)} %concatenate.3.refs_0_, s32[3,8]{1,0:T(4,128)S(1)} %collective-permute-done.refs_1_, ...), custom_call_target="tpu_custom_call" | custom-call | tf_op jit(solution)/shard_map/pallas_call | solution.py:25
  15.6 1.1 %collective-permute-start.4 = (bf16[256,384]{1,0:T(8,128)(2,1)S(1)}, bf16[256,384]{1,0:T(8,128)(2,1)S(1)}, u32[]{:S(2)}, u32[]{:S(2)}) collective-permute-start(bf16[256,384]{1,0:T(8,128)(2,1)S(1)} %get-tuple-element.28), channel_id=1, source_target_pairs={{0,8},{4,12},{8,0},{12,4},{1,9},{5,13},{9,1},{13,5},{2,10},{6,14},... | collective-permute-start | bytes 589832 | tf_op jit(solution)/shard_map/ppermute | solution.py:401
  17.8 3.2 %collective-permute-done.3.refs_0_ = bf16[256,384]{1,0:T(8,128)(2,1)S(1)} collective-permute-done((bf16[256,384]{1,0:T(8,128)(2,1)S(1)}, bf16[256,384]{1,0:T(8,128)(2,1)S(1)}, u32[]{:S(2)}, u32[]{:S(2)}) %collective-permute-start.3) | collective-permute-done | bytes 196640 | tf_op jit(solution)/shard_map/ppermute | solution.py:401
  21.0 12.1 %collective-permute-done.4.refs_1_ = bf16[256,384]{1,0:T(8,128)(2,1)S(1)} collective-permute-done((bf16[256,384]{1,0:T(8,128)(2,1)S(1)}, bf16[256,384]{1,0:T(8,128)(2,1)S(1)}, u32[]{:S(2)}, u32[]{:S(2)}) %collective-permute-start.4) | collective-permute-done | bytes 196640 | tf_op jit(solution)/shard_map/ppermute | solution.py:401
  33.1 1.2 %shard_map.61.mine = f32[1024,128]{1,0:T(8,128)S(1)} custom-call(s32[6,8]{1,0:T(8,128)S(1)} %get-tuple-element.26.idx, bf16[2048,384]{1,0:T(8,128)(2,1)S(1)} %copy-done.1, bf16[256,384]{1,0:T(8,128)(2,1)S(1)} %collective-permute-done.3.refs_0_, bf16[256,384]{1,0:T(8,128)(2,1)S(1)} %collective-permute-done.4.refs_1_, ...), custom_call_target="tpu_custom_call" | custom-call | tf_op jit(solution)/shard_map/pallas_call | solution.py:25
  34.6 1.7 %collective-permute-done.6.other = f32[1024,128]{1,0:T(8,128)S(1)} collective-permute-done((f32[1024,128]{1,0:T(8,128)S(1)}, f32[1024,128]{1,0:T(8,128)S(1)}, u32[]{:S(2)}, u32[]{:S(2)}) %collective-permute-start.6) | collective-permute-done | bytes 524320 | tf_op jit(solution)/shard_map/ppermute | solution.py:401
  36.3 1.4 %shard_map.63 = (bf16[8,256,128]{2,1,0:T(8,128)(2,1)S(1)}, bf16[2,256,128]{2,1,0:T(8,128)(2,1)S(1)}, f32[64,128]{1,0:T(8,128)S(1)}, f32[256,128]{1,0:T(8,128)S(1...) custom-call(s32[3]{0:T(128)S(1)} %pad_add_fusion.me, s32[6,8]{1,0:T(8,128)S(1)} %get-tuple-element.26.idx, ...), custom_call_target="tpu_custom_call" | custom-call | tf_op jit(solution)/shard_map/pallas_call | solution.py:25
  37.8 1.6 %collective-permute-start.13 = (f32[256,128]{1,0:T(8,128)S(1)}, f32[256,128]{1,0:T(8,128)S(1)}, u32[]{:S(2)}, u32[]{:S(2)}) collective-permute-start(f32[256,128]{1,0:T(8,128)S(1)} %get-tuple-element.36), channel_id=1, source_target_pairs={{0,8},{4,12},{8,0},{12,4},{1,9},{5,13},{9,1},{13,5},{2,10},{6,14},... | collective-permute-start | bytes 393224 | tf_op jit(solution)/shard_map/ppermute | solution.py:401
  39.3 2.8 %collective-permute-start.14 = (f32[256,128]{1,0:T(8,128)S(1)}, f32[256,128]{1,0:T(8,128)S(1)}, u32[]{:S(2)}, u32[]{:S(2)}) collective-permute-start(f32[256,128]{1,0:T(8,128)S(1)} %get-tuple-element.37), channel_id=1, source_target_pairs={{0,12},{4,0},{8,4},{12,8},{1,13},{5,1},{9,5},{13,9},{2,14},{6,2},{... | collective-permute-start | bytes 393224 | tf_op jit(solution)/shard_map/ppermute | solution.py:401
  42.2 1.5 %collective-permute-start.8 = (f32[64,128]{1,0:T(8,128)S(1)}, f32[64,128]{1,0:T(8,128)S(1)}, u32[]{:S(2)}, u32[]{:S(2)}) collective-permute-start(f32[64,128]{1,0:T(8,128)S(1)} %get-tuple-element.31), channel_id=1, source_target_pairs={{0,2},{2,0},{1,3},{3,1},{4,6},{6,4},{5,7},{7,5},{8,10},{10,8},{9,1... | collective-permute-start | bytes 98312 | tf_op jit(solution)/shard_map/ppermute | solution.py:409
  43.7 2.4 %collective-permute-done.8 = f32[64,128]{1,0:T(8,128)S(1)} collective-permute-done((f32[64,128]{1,0:T(8,128)S(1)}, f32[64,128]{1,0:T(8,128)S(1)}, u32[]{:S(2)}, u32[]{:S(2)}) %collective-permute-start.8) | collective-permute-done | bytes 32800 | tf_op jit(solution)/shard_map/ppermute | solution.py:409
  46.1 1.5 %collective-permute-start.10 = (f32[64,128]{1,0:T(8,128)S(1)}, f32[64,128]{1,0:T(8,128)S(1)}, u32[]{:S(2)}, u32[]{:S(2)}) collective-permute-start(f32[64,128]{1,0:T(8,128)S(1)} %add.11.refs_3_.refs_0_), channel_id=1, source_target_pairs={{0,8},{4,12},{8,0},{12,4},{1,9},{5,13},{9,1},{13,5},{2,10},{6,14},... | collective-permute-start | bytes 98312 | tf_op jit(solution)/shard_map/ppermute | solution.py:401
  47.6 2.9 %collective-permute-done.11.refs_6_.refs_3_ = f32[64,128]{1,0:T(8,128)S(1)} collective-permute-done((f32[64,128]{1,0:T(8,128)S(1)}, f32[64,128]{1,0:T(8,128)S(1)}, u32[]{:S(2)}, u32[]{:S(2)}) %collective-permute-start.11) | collective-permute-done | bytes 32800 | tf_op jit(solution)/shard_map/ppermute | solution.py:401
  50.5 4.9 %collective-permute-start.9 = (f32[64,128]{1,0:T(8,128)S(1)}, f32[64,128]{1,0:T(8,128)S(1)}, u32[]{:S(2)}, u32[]{:S(2)}) collective-permute-start(f32[64,128]{1,0:T(8,128)S(1)} %add.11.refs_3_.refs_0_), channel_id=1, source_target_pairs={{0,4},{4,8},{8,12},{12,0},{1,5},{5,9},{9,13},{13,1},{2,6},{6,10},{... | collective-permute-start | bytes 98312 | tf_op jit(solution)/shard_map/ppermute | solution.py:401
  55.4 1.6 %collective-permute-done.9.refs_4_.refs_1_ = f32[64,128]{1,0:T(8,128)S(1)} collective-permute-done((f32[64,128]{1,0:T(8,128)S(1)}, f32[64,128]{1,0:T(8,128)S(1)}, u32[]{:S(2)}, u32[]{:S(2)}) %collective-permute-start.9) | collective-permute-done | bytes 32800 | tf_op jit(solution)/shard_map/ppermute | solution.py:401
  59.9 1.6 %collective-permute-start.18 = (f32[32,2048]{1,0:T(8,128)S(1)}, f32[32,2048]{1,0:T(8,128)S(1)}, u32[]{:S(2)}, u32[]{:S(2)}) collective-permute-start(f32[32,2048]{1,0:T(8,128)S(1)} %get-tuple-element.42.mine), channel_id=1, source_target_pairs={{0,2},{2,0},{1,3},{3,1},{4,6},{6,4},{5,7},{7,5},{8,10},{10,8},{9,1... | collective-permute-start | bytes 786440 | tf_op jit(solution)/shard_map/ppermute | solution.py:409
  61.4 6.9 %collective-permute-done.18.other = f32[32,2048]{1,0:T(8,128)S(1)} collective-permute-done((f32[32,2048]{1,0:T(8,128)S(1)}, f32[32,2048]{1,0:T(8,128)S(1)}, u32[]{:S(2)}, u32[]{:S(2)}) %collective-permute-start.18) | collective-permute-done | bytes 262176 | tf_op jit(solution)/shard_map/ppermute | solution.py:409
  69.1 2.4 %collective-permute-start.21 = (f32[128,128]{1,0:T(8,128)S(1)}, f32[128,128]{1,0:T(8,128)S(1)}, u32[]{:S(2)}, u32[]{:S(2)}) collective-permute-start(f32[128,128]{1,0:T(8,128)S(1)} %get-tuple-element.44), channel_id=1, source_target_pairs={{0,4},{4,8},{8,12},{12,0},{1,5},{5,9},{9,13},{13,1},{2,6},{6,10},{... | collective-permute-start | bytes 196616 | tf_op jit(solution)/shard_map/ppermute | solution.py:401
  71.4 2.5 %collective-permute-start.23 = (f32[128,128]{1,0:T(8,128)S(1)}, f32[128,128]{1,0:T(8,128)S(1)}, u32[]{:S(2)}, u32[]{:S(2)}) collective-permute-start(f32[128,128]{1,0:T(8,128)S(1)} %get-tuple-element.46), channel_id=1, source_target_pairs={{0,12},{4,0},{8,4},{12,8},{1,13},{5,1},{9,5},{13,9},{2,14},{6,2},{... | collective-permute-start | bytes 196616 | tf_op jit(solution)/shard_map/ppermute | solution.py:401
  75.0 3.7 %collective-permute-done.20 = f32[32,128]{1,0:T(8,128)S(1)} collective-permute-done((f32[32,128]{1,0:T(8,128)S(1)}, f32[32,128]{1,0:T(8,128)S(1)}, u32[]{:S(2)}, u32[]{:S(2)}) %collective-permute-start.20) | collective-permute-done | bytes 16416 | tf_op jit(solution)/shard_map/ppermute | solution.py:409
  79.8 1.6 %collective-permute-start.24 = (f32[32,2048]{1,0:T(8,128)S(1)}, f32[32,2048]{1,0:T(8,128)S(1)}, u32[]{:S(2)}, u32[]{:S(2)}) collective-permute-start(f32[32,2048]{1,0:T(8,128)S(1)} %shard_map.68.mine), channel_id=1, source_target_pairs={{0,2},{2,0},{1,3},{3,1},{4,6},{6,4},{5,7},{7,5},{8,10},{10,8},{9,1... | collective-permute-start | bytes 786440 | tf_op jit(solution)/shard_map/ppermute | solution.py:409
  82.4 3.6 %collective-permute-done.25.refs_0_.refs_1_ = f32[32,128]{1,0:T(8,128)S(1)} collective-permute-done((f32[32,128]{1,0:T(8,128)S(1)}, f32[32,128]{1,0:T(8,128)S(1)}, u32[]{:S(2)}, u32[]{:S(2)}) %collective-permute-start.25) | collective-permute-done | bytes 16416 | tf_op jit(solution)/shard_map/ppermute | solution.py:409
  86.0 1.7 %collective-permute-done.24.other = f32[32,2048]{1,0:T(8,128)S(1)} collective-permute-done((f32[32,2048]{1,0:T(8,128)S(1)}, f32[32,2048]{1,0:T(8,128)S(1)}, u32[]{:S(2)}, u32[]{:S(2)}) %collective-permute-start.24) | collective-permute-done | bytes 262176 | tf_op jit(solution)/shard_map/ppermute | solution.py:409
  88.3 2.3 %shard_map.70.factor = f32[64,64]{1,0:T(8,128)S(1)} custom-call(f32[32,2048]{1,0:T(8,128)S(1)} %shard_map.69.after.own, f32[32,128]{1,0:T(8,128)S(1)} %add.12.after.refs_0_, f32[32,128]{1,0:T(8,128)S(1)} %collective-permute-done.25.refs_0_.refs_1_), custom_call_target="tpu_custom_call" | custom-call | tf_op jit(solution)/shard_map/pallas_call | solution.py:25
  90.6 1.5 %shard_map.71 = (bf16[192,2048]{1,0:T(8,128)(2,1)S(1)}, f32[32,128]{1,0:T(8,128)S(1)}) custom-call(s32[3]{0:T(128)S(1)} %pad_add_fusion.me, f32[64,64]{1,0:T(8,128)S(1)} %shard_map.70.factor, f32[32,2048]{1,0:T(8,128)S(1)} %shard_map.69.after.own, f32[32,2048]{1,0:T(8,128)S(1)} %collective-permute-done.26.other), custom_call_target="tpu_custom_call" | custom-call | tf_op jit(solution)/shard_map/pallas_call | solution.py:25
  92.2 1.8 %collective-permute-start.29 = (f32[32,128]{1,0:T(8,128)S(1)}, f32[32,128]{1,0:T(8,128)S(1)}, u32[]{:S(2)}, u32[]{:S(2)}) collective-permute-start(f32[32,128]{1,0:T(8,128)S(1)} %get-tuple-element.48.refs_0_), channel_id=1, source_target_pairs={{0,12},{4,0},{8,4},{12,8},{1,13},{5,1},{9,5},{13,9},{2,14},{6,2},{... | collective-permute-start | bytes 49160 | tf_op jit(solution)/shard_map/ppermute | solution.py:401
  94.0 1.4 %collective-permute-start.28 = (f32[32,128]{1,0:T(8,128)S(1)}, f32[32,128]{1,0:T(8,128)S(1)}, u32[]{:S(2)}, u32[]{:S(2)}) collective-permute-start(f32[32,128]{1,0:T(8,128)S(1)} %get-tuple-element.48.refs_0_), channel_id=1, source_target_pairs={{0,8},{4,12},{8,0},{12,4},{1,9},{5,13},{9,1},{13,5},{2,10},{6,14},... | collective-permute-start | bytes 49160 | tf_op jit(solution)/shard_map/ppermute | solution.py:401
  96.0 2.6 %collective-permute-done.28.refs_2_ = f32[32,128]{1,0:T(8,128)S(1)} collective-permute-done((f32[32,128]{1,0:T(8,128)S(1)}, f32[32,128]{1,0:T(8,128)S(1)}, u32[]{:S(2)}, u32[]{:S(2)}) %collective-permute-start.28) | collective-permute-done | bytes 16416 | tf_op jit(solution)/shard_map/ppermute | solution.py:401
  98.6 2.3 %collective-permute-done.27.refs_1_ = f32[32,128]{1,0:T(8,128)S(1)} collective-permute-done((f32[32,128]{1,0:T(8,128)S(1)}, f32[32,128]{1,0:T(8,128)S(1)}, u32[]{:S(2)}, u32[]{:S(2)}) %collective-permute-start.27) | collective-permute-done | bytes 16416 | tf_op jit(solution)/shard_map/ppermute | solution.py:401
  100.9 3.8 %shard_map.72 = f32[32,2048]{1,0:T(8,128)} custom-call(s32[3]{0:T(128)S(1)} %pad_add_fusion.me, bf16[192,2048]{1,0:T(8,128)(2,1)S(1)} %get-tuple-element.47.mapped, f32[32,128]{1,0:T(8,128)S(1)} %get-tuple-element.48.refs_0_, f32[32,128]{1,0:T(8,128)S(1)} %collective-permute-done.27.refs_1_, f32[32,128]{1,0:T(8,128)S(1)} %collective-permute-done.28.refs_2_, ...), custom_call_target="tpu_custom_call" | custom-call | tf_op jit(solution)/shard_map/pallas_call | solution.py:25
  (53 shorter events, 15.2 us)
Async XLA Ops:
  2.0 8.6 %collective-permute-start.2 = (s32[3,8]{1,0:T(4,128)S(1)}, s32[3,8]{1,0:T(4,128)S(1)}, u32[]{:S(2)}, u32[]{:S(2)}) collective-permute-start(s32[3,8]{1,0:T(4,128)S(1)} %concatenate.3.refs_0_), channel_id=1, source_target_pairs={{0,12},{4,0},{8,4},{12,8},{1,13},{5,1},{9,5},{13,9},{2,14},{6,2},{... | collective-permute-start | bytes 296 | tf_op jit(solution)/shard_map/ppermute | solution.py:401
  7.0 4.5 %collective-permute-start.1 = (s32[3,8]{1,0:T(4,128)S(1)}, s32[3,8]{1,0:T(4,128)S(1)}, u32[]{:S(2)}, u32[]{:S(2)}) collective-permute-start(s32[3,8]{1,0:T(4,128)S(1)} %concatenate.3.refs_0_), channel_id=1, source_target_pairs={{0,8},{4,12},{8,0},{12,4},{1,9},{5,13},{9,1},{13,5},{2,10},{6,14},... | collective-permute-start | bytes 296 | tf_op jit(solution)/shard_map/ppermute | solution.py:401
  7.0 5.4 %collective-permute-start = (s32[3,8]{1,0:T(4,128)S(1)}, s32[3,8]{1,0:T(4,128)S(1)}, u32[]{:S(2)}, u32[]{:S(2)}) collective-permute-start(s32[3,8]{1,0:T(4,128)S(1)} %concatenate.3.refs_0_), channel_id=1, source_target_pairs={{0,4},{4,8},{8,12},{12,0},{1,5},{5,9},{9,13},{13,1},{2,6},{6,10},{... | collective-permute-start | bytes 296 | tf_op jit(solution)/shard_map/ppermute | solution.py:401
  10.5 22.6 %copy-start.1 = (bf16[2048,384]{1,0:T(8,128)(2,1)S(1)}, bf16[2048,384]{1,0:T(8,128)(2,1)}, u32[]{:S(2)}) copy-start(bf16[2048,384]{1,0:T(8,128)(2,1)} %emb.3) | copy-start | bytes 4718596
  14.6 6.4 %collective-permute-start.3 = (bf16[256,384]{1,0:T(8,128)(2,1)S(1)}, bf16[256,384]{1,0:T(8,128)(2,1)S(1)}, u32[]{:S(2)}, u32[]{:S(2)}) collective-permute-start(bf16[256,384]{1,0:T(8,128)(2,1)S(1)} %get-tuple-element.27), channel_id=1, source_target_pairs={{0,12},{4,0},{8,4},{12,8},{1,13},{5,1},{9,5},{13,9},{2,14},{6,2},{... | collective-permute-start | bytes 589832 | tf_op jit(solution)/shard_map/ppermute | solution.py:401
  15.6 17.5 %collective-permute-start.4 = (bf16[256,384]{1,0:T(8,128)(2,1)S(1)}, bf16[256,384]{1,0:T(8,128)(2,1)S(1)}, u32[]{:S(2)}, u32[]{:S(2)}) collective-permute-start(bf16[256,384]{1,0:T(8,128)(2,1)S(1)} %get-tuple-element.28), channel_id=1, source_target_pairs={{0,8},{4,12},{8,0},{12,4},{1,9},{5,13},{9,1},{13,5},{2,10},{6,14},... | collective-permute-start | bytes 589832 | tf_op jit(solution)/shard_map/ppermute | solution.py:401
  16.7 16.4 %collective-permute-start.5 = (bf16[256,384]{1,0:T(8,128)(2,1)S(1)}, bf16[256,384]{1,0:T(8,128)(2,1)S(1)}, u32[]{:S(2)}, u32[]{:S(2)}) collective-permute-start(bf16[256,384]{1,0:T(8,128)(2,1)S(1)} %get-tuple-element.29), channel_id=1, source_target_pairs={{0,4},{4,8},{8,12},{12,0},{1,5},{5,9},{9,13},{13,1},{2,6},{6,10},{... | collective-permute-start | bytes 589832 | tf_op jit(solution)/shard_map/ppermute | solution.py:401
  17.8 16.6 %collective-permute-start.7 = (f32[1024,128]{1,0:T(8,128)S(1)}, f32[1024,128]{1,0:T(8,128)S(1)}, u32[]{:S(2)}, u32[]{:S(2)}) collective-permute-start(f32[1024,128]{1,0:T(8,128)S(1)} %shard_map.59.refs_5_.mine), channel_id=1, source_target_pairs={{0,1},{1,0},{2,3},{3,2},{4,5},{5,4},{6,7},{7,6},{8,9},{9,8},{10,11... | collective-permute-start | bytes 1572872 | tf_op jit(solution)/shard_map/ppermute | solution.py:401
  33.1 3.1 %copy-start.2 = (f32[2048,32]{0,1:T(8,128)S(1)}, f32[2048,32]{0,1:T(8,128)}, u32[]{:S(2)}) copy-start(f32[2048,32]{0,1:T(8,128)} %param.5) | copy-start | bytes 786436
  34.3 2.0 %collective-permute-start.6 = (f32[1024,128]{1,0:T(8,128)S(1)}, f32[1024,128]{1,0:T(8,128)S(1)}, u32[]{:S(2)}, u32[]{:S(2)}) collective-permute-start(f32[1024,128]{1,0:T(8,128)S(1)} %shard_map.61.mine), channel_id=1, source_target_pairs={{0,1},{1,0},{2,3},{3,2},{4,5},{5,4},{6,7},{7,6},{8,9},{9,8},{10,11... | collective-permute-start | bytes 1572872 | tf_op jit(solution)/shard_map/ppermute | solution.py:401
  37.7 19.3 %collective-permute-start.12 = (f32[256,128]{1,0:T(8,128)S(1)}, f32[256,128]{1,0:T(8,128)S(1)}, u32[]{:S(2)}, u32[]{:S(2)}) collective-permute-start(f32[256,128]{1,0:T(8,128)S(1)} %get-tuple-element.35), channel_id=1, source_target_pairs={{0,4},{4,8},{8,12},{12,0},{1,5},{5,9},{9,13},{13,1},{2,6},{6,10},{... | collective-permute-start | bytes 393224 | tf_op jit(solution)/shard_map/ppermute | solution.py:401
  37.8 19.2 %collective-permute-start.13 = (f32[256,128]{1,0:T(8,128)S(1)}, f32[256,128]{1,0:T(8,128)S(1)}, u32[]{:S(2)}, u32[]{:S(2)}) collective-permute-start(f32[256,128]{1,0:T(8,128)S(1)} %get-tuple-element.36), channel_id=1, source_target_pairs={{0,8},{4,12},{8,0},{12,4},{1,9},{5,13},{9,1},{13,5},{2,10},{6,14},... | collective-permute-start | bytes 393224 | tf_op jit(solution)/shard_map/ppermute | solution.py:401
  39.3 17.7 %collective-permute-start.14 = (f32[256,128]{1,0:T(8,128)S(1)}, f32[256,128]{1,0:T(8,128)S(1)}, u32[]{:S(2)}, u32[]{:S(2)}) collective-permute-start(f32[256,128]{1,0:T(8,128)S(1)} %get-tuple-element.37), channel_id=1, source_target_pairs={{0,12},{4,0},{8,4},{12,8},{1,13},{5,1},{9,5},{13,9},{2,14},{6,2},{... | collective-permute-start | bytes 393224 | tf_op jit(solution)/shard_map/ppermute | solution.py:401
  42.2 3.9 %collective-permute-start.8 = (f32[64,128]{1,0:T(8,128)S(1)}, f32[64,128]{1,0:T(8,128)S(1)}, u32[]{:S(2)}, u32[]{:S(2)}) collective-permute-start(f32[64,128]{1,0:T(8,128)S(1)} %get-tuple-element.31), channel_id=1, source_target_pairs={{0,2},{2,0},{1,3},{3,1},{4,6},{6,4},{5,7},{7,5},{8,10},{10,8},{9,1... | collective-permute-start | bytes 98312 | tf_op jit(solution)/shard_map/ppermute | solution.py:409
  46.1 4.4 %collective-permute-start.11 = (f32[64,128]{1,0:T(8,128)S(1)}, f32[64,128]{1,0:T(8,128)S(1)}, u32[]{:S(2)}, u32[]{:S(2)}) collective-permute-start(f32[64,128]{1,0:T(8,128)S(1)} %add.11.refs_3_.refs_0_), channel_id=1, source_target_pairs={{0,12},{4,0},{8,4},{12,8},{1,13},{5,1},{9,5},{13,9},{2,14},{6,2},{... | collective-permute-start | bytes 98312 | tf_op jit(solution)/shard_map/ppermute | solution.py:401
  46.1 9.3 %collective-permute-start.10 = (f32[64,128]{1,0:T(8,128)S(1)}, f32[64,128]{1,0:T(8,128)S(1)}, u32[]{:S(2)}, u32[]{:S(2)}) collective-permute-start(f32[64,128]{1,0:T(8,128)S(1)} %add.11.refs_3_.refs_0_), channel_id=1, source_target_pairs={{0,8},{4,12},{8,0},{12,4},{1,9},{5,13},{9,1},{13,5},{2,10},{6,14},... | collective-permute-start | bytes 98312 | tf_op jit(solution)/shard_map/ppermute | solution.py:401
  50.5 6.5 %collective-permute-start.9 = (f32[64,128]{1,0:T(8,128)S(1)}, f32[64,128]{1,0:T(8,128)S(1)}, u32[]{:S(2)}, u32[]{:S(2)}) collective-permute-start(f32[64,128]{1,0:T(8,128)S(1)} %add.11.refs_3_.refs_0_), channel_id=1, source_target_pairs={{0,4},{4,8},{8,12},{12,0},{1,5},{5,9},{9,13},{13,1},{2,6},{6,10},{... | collective-permute-start | bytes 98312 | tf_op jit(solution)/shard_map/ppermute | solution.py:401
  57.0 1.3 %collective-permute-start.15 = (bf16[1,256,128]{2,1,0:T(8,128)(2,1)S(1)}, bf16[1,256,128]{2,1,0:T(8,128)(2,1)S(1)}, u32[]{:S(2)}, u32[]{:S(2)}) collective-permute-start(bf16[1,256,128]{2,1,0:T(8,128)(2,1)S(1)} %get-tuple-element.38.refs_8_.refs_4_), channel_id=1, source_target_pairs={{0,1},{1,0},{2,3},{3,2},{4,5},{5,4},{6,7},{7,6},{8,9},{9,8},{10,11... | collective-permute-start | bytes 196616 | tf_op jit(solution)/shard_map/ppermute | solution.py:401
  57.1 1.4 %collective-permute-start.16 = (bf16[1,256,128]{2,1,0:T(8,128)(2,1)S(1)}, bf16[1,256,128]{2,1,0:T(8,128)(2,1)S(1)}, u32[]{:S(2)}, u32[]{:S(2)}) collective-permute-start(bf16[1,256,128]{2,1,0:T(8,128)(2,1)S(1)} %get-tuple-element.39.refs_9_.refs_5_), channel_id=1, source_target_pairs={{0,1},{1,0},{2,3},{3,2},{4,5},{5,4},{6,7},{7,6},{8,9},{9,8},{10,11... | collective-permute-start | bytes 196616 | tf_op jit(solution)/shard_map/ppermute | solution.py:401
  57.6 1.3 %collective-permute-start.17 = (bf16[1,256,128]{2,1,0:T(8,128)(2,1)S(1)}, bf16[1,256,128]{2,1,0:T(8,128)(2,1)S(1)}, u32[]{:S(2)}, u32[]{:S(2)}) collective-permute-start(bf16[1,256,128]{2,1,0:T(8,128)(2,1)S(1)} %get-tuple-element.40.refs_10_.refs_6_), channel_id=1, source_target_pairs={{0,1},{1,0},{2,3},{3,2},{4,5},{5,4},{6,7},{7,6},{8,9},{9,8},{10,11... | collective-permute-start | bytes 196616 | tf_op jit(solution)/shard_map/ppermute | solution.py:401
  59.9 8.4 %collective-permute-start.18 = (f32[32,2048]{1,0:T(8,128)S(1)}, f32[32,2048]{1,0:T(8,128)S(1)}, u32[]{:S(2)}, u32[]{:S(2)}) collective-permute-start(f32[32,2048]{1,0:T(8,128)S(1)} %get-tuple-element.42.mine), channel_id=1, source_target_pairs={{0,2},{2,0},{1,3},{3,1},{4,6},{6,4},{5,7},{7,5},{8,10},{10,8},{9,1... | collective-permute-start | bytes 786440 | tf_op jit(solution)/shard_map/ppermute | solution.py:409
  69.0 4.9 %collective-permute-start.19 = (f32[32,2048]{1,0:T(8,128)S(1)}, f32[32,2048]{1,0:T(8,128)S(1)}, u32[]{:S(2)}, u32[]{:S(2)}) collective-permute-start(f32[32,2048]{1,0:T(8,128)S(1)} %get-tuple-element.43.own.refs_0_), channel_id=1, source_target_pairs={{0,1},{1,0},{2,3},{3,2},{4,5},{5,4},{6,7},{7,6},{8,9},{9,8},{10,11... | collective-permute-start | bytes 786440 | tf_op jit(solution)/shard_map/ppermute | solution.py:401
  69.1 9.7 %collective-permute-start.21 = (f32[128,128]{1,0:T(8,128)S(1)}, f32[128,128]{1,0:T(8,128)S(1)}, u32[]{:S(2)}, u32[]{:S(2)}) collective-permute-start(f32[128,128]{1,0:T(8,128)S(1)} %get-tuple-element.44), channel_id=1, source_target_pairs={{0,4},{4,8},{8,12},{12,0},{1,5},{5,9},{9,13},{13,1},{2,6},{6,10},{... | collective-permute-start | bytes 196616 | tf_op jit(solution)/shard_map/ppermute | solution.py:401
  71.4 7.3 %collective-permute-start.22 = (f32[128,128]{1,0:T(8,128)S(1)}, f32[128,128]{1,0:T(8,128)S(1)}, u32[]{:S(2)}, u32[]{:S(2)}) collective-permute-start(f32[128,128]{1,0:T(8,128)S(1)} %get-tuple-element.45), channel_id=1, source_target_pairs={{0,8},{4,12},{8,0},{12,4},{1,9},{5,13},{9,1},{13,5},{2,10},{6,14},... | collective-permute-start | bytes 196616 | tf_op jit(solution)/shard_map/ppermute | solution.py:401
  71.4 7.3 %collective-permute-start.23 = (f32[128,128]{1,0:T(8,128)S(1)}, f32[128,128]{1,0:T(8,128)S(1)}, u32[]{:S(2)}, u32[]{:S(2)}) collective-permute-start(f32[128,128]{1,0:T(8,128)S(1)} %get-tuple-element.46), channel_id=1, source_target_pairs={{0,12},{4,0},{8,4},{12,8},{1,13},{5,1},{9,5},{13,9},{2,14},{6,2},{... | collective-permute-start | bytes 196616 | tf_op jit(solution)/shard_map/ppermute | solution.py:401
  75.0 3.8 %collective-permute-start.20 = (f32[32,128]{1,0:T(8,128)S(1)}, f32[32,128]{1,0:T(8,128)S(1)}, u32[]{:S(2)}, u32[]{:S(2)}) collective-permute-start(f32[32,128]{1,0:T(8,128)S(1)} %shard_map.67), channel_id=1, source_target_pairs={{0,4},{4,0},{8,12},{12,8},{1,5},{5,1},{9,13},{13,9},{2,6},{6,2},{1... | collective-permute-start | bytes 49160 | tf_op jit(solution)/shard_map/ppermute | solution.py:409
  79.8 7.9 %collective-permute-start.24 = (f32[32,2048]{1,0:T(8,128)S(1)}, f32[32,2048]{1,0:T(8,128)S(1)}, u32[]{:S(2)}, u32[]{:S(2)}) collective-permute-start(f32[32,2048]{1,0:T(8,128)S(1)} %shard_map.68.mine), channel_id=1, source_target_pairs={{0,2},{2,0},{1,3},{3,1},{4,6},{6,4},{5,7},{7,5},{8,10},{10,8},{9,1... | collective-permute-start | bytes 786440 | tf_op jit(solution)/shard_map/ppermute | solution.py:409
  81.3 4.6 %collective-permute-start.25 = (f32[32,128]{1,0:T(8,128)S(1)}, f32[32,128]{1,0:T(8,128)S(1)}, u32[]{:S(2)}, u32[]{:S(2)}) collective-permute-start(f32[32,128]{1,0:T(8,128)S(1)} %add.12.after.refs_0_), channel_id=1, source_target_pairs={{0,8},{4,12},{8,0},{12,4},{1,9},{5,13},{9,1},{13,5},{2,10},{6,14},... | collective-permute-start | bytes 49160 | tf_op jit(solution)/shard_map/ppermute | solution.py:409
  88.2 2.4 %collective-permute-start.26 = (f32[32,2048]{1,0:T(8,128)S(1)}, f32[32,2048]{1,0:T(8,128)S(1)}, u32[]{:S(2)}, u32[]{:S(2)}) collective-permute-start(f32[32,2048]{1,0:T(8,128)S(1)} %shard_map.69.after.own), channel_id=1, source_target_pairs={{0,1},{1,0},{2,3},{3,2},{4,5},{5,4},{6,7},{7,6},{8,9},{9,8},{10,11... | collective-permute-start | bytes 786440 | tf_op jit(solution)/shard_map/ppermute | solution.py:401
  92.2 3.9 %collective-permute-start.29 = (f32[32,128]{1,0:T(8,128)S(1)}, f32[32,128]{1,0:T(8,128)S(1)}, u32[]{:S(2)}, u32[]{:S(2)}) collective-permute-start(f32[32,128]{1,0:T(8,128)S(1)} %get-tuple-element.48.refs_0_), channel_id=1, source_target_pairs={{0,12},{4,0},{8,4},{12,8},{1,13},{5,1},{9,5},{13,9},{2,14},{6,2},{... | collective-permute-start | bytes 49160 | tf_op jit(solution)/shard_map/ppermute | solution.py:401
  94.0 4.6 %collective-permute-start.28 = (f32[32,128]{1,0:T(8,128)S(1)}, f32[32,128]{1,0:T(8,128)S(1)}, u32[]{:S(2)}, u32[]{:S(2)}) collective-permute-start(f32[32,128]{1,0:T(8,128)S(1)} %get-tuple-element.48.refs_0_), channel_id=1, source_target_pairs={{0,8},{4,12},{8,0},{12,4},{1,9},{5,13},{9,1},{13,5},{2,10},{6,14},... | collective-permute-start | bytes 49160 | tf_op jit(solution)/shard_map/ppermute | solution.py:401
  95.4 5.5 %collective-permute-start.27 = (f32[32,128]{1,0:T(8,128)S(1)}, f32[32,128]{1,0:T(8,128)S(1)}, u32[]{:S(2)}, u32[]{:S(2)}) collective-permute-start(f32[32,128]{1,0:T(8,128)S(1)} %get-tuple-element.48.refs_0_), channel_id=1, source_target_pairs={{0,4},{4,8},{8,12},{12,0},{1,5},{5,9},{9,13},{13,1},{2,6},{6,10},{... | collective-permute-start | bytes 49160 | tf_op jit(solution)/shard_map/ppermute | solution.py:401
  (1 other events, 1.4 us)

commit v7 on v6

--- a/solution.py
+++ b/solution.py
@@ -92,7 +92,7 @@
     return (product3[2 * m :] + product3[m : 2 * m]) + product3[:m]
 
 
-def lower_inverse(matrix, step=4):
+def lower_inverse(matrix, step=8):
     n = matrix.shape[0]
     state = jnp.concatenate([matrix, eye_mask(n).astype(F32)], axis=1)
     done = []
@@ -326,12 +326,12 @@
 
 def first_apply_body(dims, me, idx, *refs):
     row_count, per_core = dims[0], dims[2]
-    terms, refs = refs[:row_count], refs[row_count:]
+    terms, refs = refs[:2], refs[2:]
     own, near_tiles, home_tiles, self_tiles = refs[:4]
     sent, shared = refs[4 : 3 + row_count], refs[3 + row_count : 2 + 2 * row_count]
     messages = refs[2 + 2 * row_count : -3]
     out, degree, inverse = refs[-3:]
-    total = functools.reduce(lambda total, term: total + term[...], terms[1:], terms[0][...])
+    total = terms[0][...] + terms[1][...]
     degree[...] = total
     inverse[...] = 1.0 / jnp.sqrt(total)
     apply_tiles(
@@ -385,7 +385,7 @@
 def second_gram_body(me, factor, own, other, mapped, out):
     full = both_columns(me[2], own[...], other[...])
     parts = thirds(times(factor[...], thirds(full)))
-    mapped[...] = parts
+    mapped[...] = parts[: mapped.shape[0]]
     out[...] = folded(gram(parts))
 
 
@@ -394,7 +394,11 @@
     factor = lower_inverse(unfolded(refs[:-1]))
     own_cols = out.shape[0]
     part = jnp.where(me[2] == 0, factor[:own_cols], factor[own_cols:])
-    out[...] = times(part, mapped[...])
+    left = jnp.concatenate(halves(part), axis=0)
+    both = jnp.dot(
+        jnp.concatenate([left, left], axis=1), mapped[...], preferred_element_type=F32
+    )
+    out[...] = both[own_cols:] + both[:own_cols]
 
 
 def shift_by(value, axes, size, shift):
@@ -484,14 +488,14 @@
         smem_in=(0, 1),
     )
     near_tiles, home_tiles, degrees, sends = tiles[0], tiles[1], tiles[2], tiles[3:]
-    mine, other = pair_sum(degrees, ("tiles",))
-    degree_terms = row_terms(mine + other, row_count)
+    degrees = functools.reduce(jnp.add, row_terms(degrees, row_count))
+    degree_terms = pair_sum(degrees, ("tiles",))
     messages = [shift_by(sends[k - 1], "rows", row_count, k) for k in others]
     sent = call(
         functools.partial(split_body, row_count, per_core),
         [sds((per_core, 2 * BLOCK, BLOCK), BF16) for _ in others],
         [*messages, *degree_terms],
-        any_in=range(row_count - 1, 2 * row_count - 1),
+        any_in=(row_count - 1, row_count),
     )
     shared = [shift_by(tile, "cols", core_count, 1) for tile in sent]
 
@@ -541,7 +545,7 @@
     factor = call(factor_body, square, [second, *gram_terms], any_in=(0,))
     full, second_gram = call(
         second_gram_body,
-        [sds((6 * own_cols, rows_here), BF16), folded_square],
+        [sds((4 * own_cols, rows_here), BF16), folded_square],
         [me, factor, second, second_other],
         smem_in=(0,),
     )

time: 105 us -> 101 us (0.962)
  starting transfers between devices: 34.8 us -> 32.5 us
    ppermute x25, starting transfers between devices: 29.1 us -> 26.4 us  [shift_by(): lax.ppermute(value, axes, [(i, (i + shift) % size) for i in range(size)])]
  transfers between devices with their start and end apart: 30 -> 30, of which waited for: 17 -> 17; matrix products, arithmetic and copies ran while one was open for 1% -> 1% of each run, Pallas kernels for 6% -> 5%
where the time goes in v7:
time: 101 us
  waiting for transfers between devices  46.8 us (46%)
  starting transfers between devices  32.5 us (32%)
  Pallas kernels  17.1 us (17%)
  local copies, waits for them, and re-layouts  2.7 us (3%)
  between operations  1.46 us (1%)
    ppermute x25, waiting for transfers between devices, shift_by(): lax.ppermute(value, axes, [(i, (i + shift) % size) for i in range(size)])  28.9 us
    ppermute x25, starting transfers between devices, shift_by(): lax.ppermute(value, axes, [(i, (i + shift) % size) for i in range(size)])  26.4 us
    ppermute x5, waiting for transfers between devices, pair_step(): lax.ppermute(value, name, [(i, i ^ flip) for i in range(lax.axis_size(nam...  17.9 us
    pallas_call x14, Pallas kernels, call(): pl.pallas_call(body, out_shape=shapes, in_specs=[SMEM if i in smem_in els...  17.1 us
    ppermute x5, starting transfers between devices, pair_step(): lax.ppermute(value, name, [(i, i ^ flip) for i in range(lax.axis_size(nam...  6.12 us
  transfers between devices with their start and end apart: 30, of which 17 were waited for; matrix products, arithmetic and copies ran while one was open for 1% of the time, Pallas kernels for 5%

profile of v7, /device:TPU:0, one launch (start us, length us, event | category | flops | bytes accessed | tf_op | source)
XLA Modules:
  0.0 100.6 jit_solution(9051673905170441131)
XLA Ops:
  2.0 5.0 %collective-permute-start.2 = (s32[3,8]{1,0:T(4,128)S(1)}, s32[3,8]{1,0:T(4,128)S(1)}, u32[]{:S(2)}, u32[]{:S(2)}) collective-permute-start(s32[3,8]{1,0:T(4,128)S(1)} %concatenate.3.refs_0_), channel_id=1, source_target_pairs={{0,12},{4,0},{8,4},{12,8},{1,13},{5,1},{9,5},{13,9},{2,14},{6,2},{... | collective-permute-start | bytes 296 | tf_op jit(solution)/shard_map/ppermute | solution.py:405
  8.1 1.4 %copy-done = bf16[2048,384]{1,0:T(8,128)(2,1)S(1)} copy-done((bf16[2048,384]{1,0:T(8,128)(2,1)S(1)}, bf16[2048,384]{1,0:T(8,128)(2,1)}, u32[]{:S(2)}) %copy-start) | copy-done | bytes 1572888
  12.4 2.1 %shard_map.60 = (s32[6,8]{1,0:T(8,128)S(1)}, bf16[256,384]{1,0:T(8,128)(2,1)S(1)}, bf16[256,384]{1,0:T(8,128)(2,1)S(1)}, bf16[256,384]{1,0:T(8,128)(2,1)S(1)}) custom-call(s32[3]{0:T(128)S(1)} %pad_add_fusion.me, s32[3,8]{1,0:T(4,128)S(1)} %concatenate.3.refs_0_, s32[3,8]{1,0:T(4,128)S(1)} %collective-permute-done.refs_1_, ...), custom_call_target="tpu_custom_call" | custom-call | tf_op jit(solution)/shard_map/pallas_call | solution.py:25
  15.6 1.1 %collective-permute-start.4 = (bf16[256,384]{1,0:T(8,128)(2,1)S(1)}, bf16[256,384]{1,0:T(8,128)(2,1)S(1)}, u32[]{:S(2)}, u32[]{:S(2)}) collective-permute-start(bf16[256,384]{1,0:T(8,128)(2,1)S(1)} %get-tuple-element.28), channel_id=1, source_target_pairs={{0,8},{4,12},{8,0},{12,4},{1,9},{5,13},{9,1},{13,5},{2,10},{6,14},... | collective-permute-start | bytes 589832 | tf_op jit(solution)/shard_map/ppermute | solution.py:405
  17.8 3.2 %collective-permute-done.3.refs_0_ = bf16[256,384]{1,0:T(8,128)(2,1)S(1)} collective-permute-done((bf16[256,384]{1,0:T(8,128)(2,1)S(1)}, bf16[256,384]{1,0:T(8,128)(2,1)S(1)}, u32[]{:S(2)}, u32[]{:S(2)}) %collective-permute-start.3) | collective-permute-done | bytes 196640 | tf_op jit(solution)/shard_map/ppermute | solution.py:405
  21.0 12.1 %collective-permute-done.4.refs_1_ = bf16[256,384]{1,0:T(8,128)(2,1)S(1)} collective-permute-done((bf16[256,384]{1,0:T(8,128)(2,1)S(1)}, bf16[256,384]{1,0:T(8,128)(2,1)S(1)}, u32[]{:S(2)}, u32[]{:S(2)}) %collective-permute-start.4) | collective-permute-done | bytes 196640 | tf_op jit(solution)/shard_map/ppermute | solution.py:405
  33.1 1.2 %shard_map.61.mine = f32[1024,128]{1,0:T(8,128)S(1)} custom-call(s32[6,8]{1,0:T(8,128)S(1)} %get-tuple-element.26.idx, bf16[2048,384]{1,0:T(8,128)(2,1)S(1)} %copy-done.1, bf16[256,384]{1,0:T(8,128)(2,1)S(1)} %collective-permute-done.3.refs_0_, bf16[256,384]{1,0:T(8,128)(2,1)S(1)} %collective-permute-done.4.refs_1_, ...), custom_call_target="tpu_custom_call" | custom-call | tf_op jit(solution)/shard_map/pallas_call | solution.py:25
  34.6 1.7 %collective-permute-done.6.other = f32[1024,128]{1,0:T(8,128)S(1)} collective-permute-done((f32[1024,128]{1,0:T(8,128)S(1)}, f32[1024,128]{1,0:T(8,128)S(1)}, u32[]{:S(2)}, u32[]{:S(2)}) %collective-permute-start.6) | collective-permute-done | bytes 524320 | tf_op jit(solution)/shard_map/ppermute | solution.py:405
  36.3 1.4 %shard_map.63 = (bf16[8,256,128]{2,1,0:T(8,128)(2,1)S(1)}, bf16[2,256,128]{2,1,0:T(8,128)(2,1)S(1)}, f32[64,128]{1,0:T(8,128)S(1)}, f32[256,128]{1,0:T(8,128)S(1...) custom-call(s32[3]{0:T(128)S(1)} %pad_add_fusion.me, s32[6,8]{1,0:T(8,128)S(1)} %get-tuple-element.26.idx, ...), custom_call_target="tpu_custom_call" | custom-call | tf_op jit(solution)/shard_map/pallas_call | solution.py:25
  37.8 1.5 %collective-permute-start.9 = (f32[64,128]{1,0:T(8,128)S(1)}, f32[64,128]{1,0:T(8,128)S(1)}, u32[]{:S(2)}, u32[]{:S(2)}) collective-permute-start(f32[64,128]{1,0:T(8,128)S(1)} %get-tuple-element.31), channel_id=1, source_target_pairs={{0,8},{4,12},{8,0},{12,4},{1,9},{5,13},{9,1},{13,5},{2,10},{6,14},... | collective-permute-start | bytes 98312 | tf_op jit(solution)/shard_map/ppermute | solution.py:405
  39.3 1.9 %collective-permute-start.8 = (f32[64,128]{1,0:T(8,128)S(1)}, f32[64,128]{1,0:T(8,128)S(1)}, u32[]{:S(2)}, u32[]{:S(2)}) collective-permute-start(f32[64,128]{1,0:T(8,128)S(1)} %get-tuple-element.31), channel_id=1, source_target_pairs={{0,4},{4,8},{8,12},{12,0},{1,5},{5,9},{9,13},{13,1},{2,6},{6,10},{... | collective-permute-start | bytes 98312 | tf_op jit(solution)/shard_map/ppermute | solution.py:405
  41.3 2.4 %collective-permute-start.13 = (f32[256,128]{1,0:T(8,128)S(1)}, f32[256,128]{1,0:T(8,128)S(1)}, u32[]{:S(2)}, u32[]{:S(2)}) collective-permute-start(f32[256,128]{1,0:T(8,128)S(1)} %get-tuple-element.36), channel_id=1, source_target_pairs={{0,8},{4,12},{8,0},{12,4},{1,9},{5,13},{9,1},{13,5},{2,10},{6,14},... | collective-permute-start | bytes 393224 | tf_op jit(solution)/shard_map/ppermute | solution.py:405
  43.7 1.9 %collective-permute-start.14 = (f32[256,128]{1,0:T(8,128)S(1)}, f32[256,128]{1,0:T(8,128)S(1)}, u32[]{:S(2)}, u32[]{:S(2)}) collective-permute-start(f32[256,128]{1,0:T(8,128)S(1)} %get-tuple-element.37), channel_id=1, source_target_pairs={{0,12},{4,0},{8,4},{12,8},{1,13},{5,1},{9,5},{13,9},{2,14},{6,2},{... | collective-permute-start | bytes 393224 | tf_op jit(solution)/shard_map/ppermute | solution.py:405
  45.7 1.6 %collective-permute-start.11 = (f32[64,128]{1,0:T(8,128)S(1)}, f32[64,128]{1,0:T(8,128)S(1)}, u32[]{:S(2)}, u32[]{:S(2)}) collective-permute-start(f32[64,128]{1,0:T(8,128)S(1)} %add_add_fusion.refs_3_.refs_0_), channel_id=1, source_target_pairs={{0,2},{2,0},{1,3},{3,1},{4,6},{6,4},{5,7},{7,5},{8,10},{10,8},{9,1... | collective-permute-start | bytes 98312 | tf_op jit(solution)/shard_map/ppermute | solution.py:413
  47.2 2.4 %collective-permute-done.11.refs_4_.refs_1_ = f32[64,128]{1,0:T(8,128)S(1)} collective-permute-done((f32[64,128]{1,0:T(8,128)S(1)}, f32[64,128]{1,0:T(8,128)S(1)}, u32[]{:S(2)}, u32[]{:S(2)}) %collective-permute-start.11) | collective-permute-done | bytes 32800 | tf_op jit(solution)/shard_map/ppermute | solution.py:413
  49.6 3.9 %collective-permute-done.13.refs_1_.refs_13_ = f32[256,128]{1,0:T(8,128)S(1)} collective-permute-done((f32[256,128]{1,0:T(8,128)S(1)}, f32[256,128]{1,0:T(8,128)S(1)}, u32[]{:S(2)}, u32[]{:S(2)}) %collective-permute-start.13) | collective-permute-done | bytes 131104 | tf_op jit(solution)/shard_map/ppermute | solution.py:405
  56.4 1.6 %collective-permute-start.18 = (f32[32,2048]{1,0:T(8,128)S(1)}, f32[32,2048]{1,0:T(8,128)S(1)}, u32[]{:S(2)}, u32[]{:S(2)}) collective-permute-start(f32[32,2048]{1,0:T(8,128)S(1)} %get-tuple-element.42.mine), channel_id=1, source_target_pairs={{0,2},{2,0},{1,3},{3,1},{4,6},{6,4},{5,7},{7,5},{8,10},{10,8},{9,1... | collective-permute-start | bytes 786440 | tf_op jit(solution)/shard_map/ppermute | solution.py:413
  57.9 6.9 %collective-permute-done.18.other = f32[32,2048]{1,0:T(8,128)S(1)} collective-permute-done((f32[32,2048]{1,0:T(8,128)S(1)}, f32[32,2048]{1,0:T(8,128)S(1)}, u32[]{:S(2)}, u32[]{:S(2)}) %collective-permute-start.18) | collective-permute-done | bytes 262176 | tf_op jit(solution)/shard_map/ppermute | solution.py:413
  65.6 2.9 %collective-permute-start.21 = (f32[128,128]{1,0:T(8,128)S(1)}, f32[128,128]{1,0:T(8,128)S(1)}, u32[]{:S(2)}, u32[]{:S(2)}) collective-permute-start(f32[128,128]{1,0:T(8,128)S(1)} %get-tuple-element.44), channel_id=1, source_target_pairs={{0,4},{4,8},{8,12},{12,0},{1,5},{5,9},{9,13},{13,1},{2,6},{6,10},{... | collective-permute-start | bytes 196616 | tf_op jit(solution)/shard_map/ppermute | solution.py:405
  68.5 1.3 %collective-permute-start.22 = (f32[128,128]{1,0:T(8,128)S(1)}, f32[128,128]{1,0:T(8,128)S(1)}, u32[]{:S(2)}, u32[]{:S(2)}) collective-permute-start(f32[128,128]{1,0:T(8,128)S(1)} %get-tuple-element.45), channel_id=1, source_target_pairs={{0,8},{4,12},{8,0},{12,4},{1,9},{5,13},{9,1},{13,5},{2,10},{6,14},... | collective-permute-start | bytes 196616 | tf_op jit(solution)/shard_map/ppermute | solution.py:405
  69.8 1.1 %collective-permute-start.23 = (f32[128,128]{1,0:T(8,128)S(1)}, f32[128,128]{1,0:T(8,128)S(1)}, u32[]{:S(2)}, u32[]{:S(2)}) collective-permute-start(f32[128,128]{1,0:T(8,128)S(1)} %get-tuple-element.46), channel_id=1, source_target_pairs={{0,12},{4,0},{8,4},{12,8},{1,13},{5,1},{9,5},{13,9},{2,14},{6,2},{... | collective-permute-start | bytes 196616 | tf_op jit(solution)/shard_map/ppermute | solution.py:405
  71.0 1.1 %shard_map.67 = f32[32,128]{1,0:T(8,128)S(1)} custom-call(s32[3]{0:T(128)S(1)} %pad_add_fusion.me, f32[32,2048]{1,0:T(8,128)S(1)} %get-tuple-element.43.own.refs_0_, f32[32,2048]{1,0:T(8,128)S(1)} %collective-permute-done.19.other), custom_call_target="tpu_custom_call" | custom-call | tf_op jit(solution)/shard_map/pallas_call | solution.py:25
  73.0 2.8 %collective-permute-done.20 = f32[32,128]{1,0:T(8,128)S(1)} collective-permute-done((f32[32,128]{1,0:T(8,128)S(1)}, f32[32,128]{1,0:T(8,128)S(1)}, u32[]{:S(2)}, u32[]{:S(2)}) %collective-permute-start.20) | collective-permute-done | bytes 16416 | tf_op jit(solution)/shard_map/ppermute | solution.py:413
  76.9 1.6 %collective-permute-start.24 = (f32[32,2048]{1,0:T(8,128)S(1)}, f32[32,2048]{1,0:T(8,128)S(1)}, u32[]{:S(2)}, u32[]{:S(2)}) collective-permute-start(f32[32,2048]{1,0:T(8,128)S(1)} %shard_map.68.mine), channel_id=1, source_target_pairs={{0,2},{2,0},{1,3},{3,1},{4,6},{6,4},{5,7},{7,5},{8,10},{10,8},{9,1... | collective-permute-start | bytes 786440 | tf_op jit(solution)/shard_map/ppermute | solution.py:413
  78.9 4.1 %collective-permute-done.25.refs_0_.refs_1_ = f32[32,128]{1,0:T(8,128)S(1)} collective-permute-done((f32[32,128]{1,0:T(8,128)S(1)}, f32[32,128]{1,0:T(8,128)S(1)}, u32[]{:S(2)}, u32[]{:S(2)}) %collective-permute-start.25) | collective-permute-done | bytes 16416 | tf_op jit(solution)/shard_map/ppermute | solution.py:413
  83.1 1.6 %collective-permute-done.24.other = f32[32,2048]{1,0:T(8,128)S(1)} collective-permute-done((f32[32,2048]{1,0:T(8,128)S(1)}, f32[32,2048]{1,0:T(8,128)S(1)}, u32[]{:S(2)}, u32[]{:S(2)}) %collective-permute-start.24) | collective-permute-done | bytes 262176 | tf_op jit(solution)/shard_map/ppermute | solution.py:413
  85.3 1.9 %shard_map.70.factor = f32[64,64]{1,0:T(8,128)S(1)} custom-call(f32[32,2048]{1,0:T(8,128)S(1)} %shard_map.69.after.own, f32[32,128]{1,0:T(8,128)S(1)} %add.20.after.refs_0_, f32[32,128]{1,0:T(8,128)S(1)} %collective-permute-done.25.refs_0_.refs_1_), custom_call_target="tpu_custom_call" | custom-call | tf_op jit(solution)/shard_map/pallas_call | solution.py:25
  87.3 1.5 %shard_map.71 = (bf16[128,2048]{1,0:T(8,128)(2,1)S(1)}, f32[32,128]{1,0:T(8,128)S(1)}) custom-call(s32[3]{0:T(128)S(1)} %pad_add_fusion.me, f32[64,64]{1,0:T(8,128)S(1)} %shard_map.70.factor, f32[32,2048]{1,0:T(8,128)S(1)} %shard_map.69.after.own, f32[32,2048]{1,0:T(8,128)S(1)} %collective-permute-done.26.other), custom_call_target="tpu_custom_call" | custom-call | tf_op jit(solution)/shard_map/pallas_call | solution.py:25
  88.8 1.8 %collective-permute-start.29 = (f32[32,128]{1,0:T(8,128)S(1)}, f32[32,128]{1,0:T(8,128)S(1)}, u32[]{:S(2)}, u32[]{:S(2)}) collective-permute-start(f32[32,128]{1,0:T(8,128)S(1)} %get-tuple-element.48.refs_0_), channel_id=1, source_target_pairs={{0,12},{4,0},{8,4},{12,8},{1,13},{5,1},{9,5},{13,9},{2,14},{6,2},{... | collective-permute-start | bytes 49160 | tf_op jit(solution)/shard_map/ppermute | solution.py:405
  92.5 2.7 %collective-permute-done.28.refs_2_ = f32[32,128]{1,0:T(8,128)S(1)} collective-permute-done((f32[32,128]{1,0:T(8,128)S(1)}, f32[32,128]{1,0:T(8,128)S(1)}, u32[]{:S(2)}, u32[]{:S(2)}) %collective-permute-start.28) | collective-permute-done | bytes 16416 | tf_op jit(solution)/shard_map/ppermute | solution.py:405
  95.2 2.0 %collective-permute-done.27.refs_1_ = f32[32,128]{1,0:T(8,128)S(1)} collective-permute-done((f32[32,128]{1,0:T(8,128)S(1)}, f32[32,128]{1,0:T(8,128)S(1)}, u32[]{:S(2)}, u32[]{:S(2)}) %collective-permute-start.27) | collective-permute-done | bytes 16416 | tf_op jit(solution)/shard_map/ppermute | solution.py:405
  97.2 3.4 %shard_map.72 = f32[32,2048]{1,0:T(8,128)} custom-call(s32[3]{0:T(128)S(1)} %pad_add_fusion.me, bf16[128,2048]{1,0:T(8,128)(2,1)S(1)} %get-tuple-element.47.mapped, f32[32,128]{1,0:T(8,128)S(1)} %get-tuple-element.48.refs_0_, f32[32,128]{1,0:T(8,128)S(1)} %collective-permute-done.27.refs_1_, f32[32,128]{1,0:T(8,128)S(1)} %collective-permute-done.28.refs_2_, ...), custom_call_target="tpu_custom_call" | custom-call | tf_op jit(solution)/shard_map/pallas_call | solution.py:25
  (53 shorter events, 15.7 us)
Async XLA Ops:
  2.0 8.6 %collective-permute-start.2 = (s32[3,8]{1,0:T(4,128)S(1)}, s32[3,8]{1,0:T(4,128)S(1)}, u32[]{:S(2)}, u32[]{:S(2)}) collective-permute-start(s32[3,8]{1,0:T(4,128)S(1)} %concatenate.3.refs_0_), channel_id=1, source_target_pairs={{0,12},{4,0},{8,4},{12,8},{1,13},{5,1},{9,5},{13,9},{2,14},{6,2},{... | collective-permute-start | bytes 296 | tf_op jit(solution)/shard_map/ppermute | solution.py:405
  7.0 4.5 %collective-permute-start.1 = (s32[3,8]{1,0:T(4,128)S(1)}, s32[3,8]{1,0:T(4,128)S(1)}, u32[]{:S(2)}, u32[]{:S(2)}) collective-permute-start(s32[3,8]{1,0:T(4,128)S(1)} %concatenate.3.refs_0_), channel_id=1, source_target_pairs={{0,8},{4,12},{8,0},{12,4},{1,9},{5,13},{9,1},{13,5},{2,10},{6,14},... | collective-permute-start | bytes 296 | tf_op jit(solution)/shard_map/ppermute | solution.py:405
  7.0 5.4 %collective-permute-start = (s32[3,8]{1,0:T(4,128)S(1)}, s32[3,8]{1,0:T(4,128)S(1)}, u32[]{:S(2)}, u32[]{:S(2)}) collective-permute-start(s32[3,8]{1,0:T(4,128)S(1)} %concatenate.3.refs_0_), channel_id=1, source_target_pairs={{0,4},{4,8},{8,12},{12,0},{1,5},{5,9},{9,13},{13,1},{2,6},{6,10},{... | collective-permute-start | bytes 296 | tf_op jit(solution)/shard_map/ppermute | solution.py:405
  10.5 22.6 %copy-start.1 = (bf16[2048,384]{1,0:T(8,128)(2,1)S(1)}, bf16[2048,384]{1,0:T(8,128)(2,1)}, u32[]{:S(2)}) copy-start(bf16[2048,384]{1,0:T(8,128)(2,1)} %emb.3) | copy-start | bytes 4718596
  14.6 6.4 %collective-permute-start.3 = (bf16[256,384]{1,0:T(8,128)(2,1)S(1)}, bf16[256,384]{1,0:T(8,128)(2,1)S(1)}, u32[]{:S(2)}, u32[]{:S(2)}) collective-permute-start(bf16[256,384]{1,0:T(8,128)(2,1)S(1)} %get-tuple-element.27), channel_id=1, source_target_pairs={{0,12},{4,0},{8,4},{12,8},{1,13},{5,1},{9,5},{13,9},{2,14},{6,2},{... | collective-permute-start | bytes 589832 | tf_op jit(solution)/shard_map/ppermute | solution.py:405
  15.6 17.5 %collective-permute-start.4 = (bf16[256,384]{1,0:T(8,128)(2,1)S(1)}, bf16[256,384]{1,0:T(8,128)(2,1)S(1)}, u32[]{:S(2)}, u32[]{:S(2)}) collective-permute-start(bf16[256,384]{1,0:T(8,128)(2,1)S(1)} %get-tuple-element.28), channel_id=1, source_target_pairs={{0,8},{4,12},{8,0},{12,4},{1,9},{5,13},{9,1},{13,5},{2,10},{6,14},... | collective-permute-start | bytes 589832 | tf_op jit(solution)/shard_map/ppermute | solution.py:405
  16.7 16.4 %collective-permute-start.5 = (bf16[256,384]{1,0:T(8,128)(2,1)S(1)}, bf16[256,384]{1,0:T(8,128)(2,1)S(1)}, u32[]{:S(2)}, u32[]{:S(2)}) collective-permute-start(bf16[256,384]{1,0:T(8,128)(2,1)S(1)} %get-tuple-element.29), channel_id=1, source_target_pairs={{0,4},{4,8},{8,12},{12,0},{1,5},{5,9},{9,13},{13,1},{2,6},{6,10},{... | collective-permute-start | bytes 589832 | tf_op jit(solution)/shard_map/ppermute | solution.py:405
  17.8 16.6 %collective-permute-start.7 = (f32[1024,128]{1,0:T(8,128)S(1)}, f32[1024,128]{1,0:T(8,128)S(1)}, u32[]{:S(2)}, u32[]{:S(2)}) collective-permute-start(f32[1024,128]{1,0:T(8,128)S(1)} %shard_map.59.refs_5_.mine), channel_id=1, source_target_pairs={{0,1},{1,0},{2,3},{3,2},{4,5},{5,4},{6,7},{7,6},{8,9},{9,8},{10,11... | collective-permute-start | bytes 1572872 | tf_op jit(solution)/shard_map/ppermute | solution.py:405
  33.1 3.1 %copy-start.2 = (f32[2048,32]{0,1:T(8,128)S(1)}, f32[2048,32]{0,1:T(8,128)}, u32[]{:S(2)}) copy-start(f32[2048,32]{0,1:T(8,128)} %param.5) | copy-start | bytes 786436
  34.3 2.0 %collective-permute-start.6 = (f32[1024,128]{1,0:T(8,128)S(1)}, f32[1024,128]{1,0:T(8,128)S(1)}, u32[]{:S(2)}, u32[]{:S(2)}) collective-permute-start(f32[1024,128]{1,0:T(8,128)S(1)} %shard_map.61.mine), channel_id=1, source_target_pairs={{0,1},{1,0},{2,3},{3,2},{4,5},{5,4},{6,7},{7,6},{8,9},{9,8},{10,11... | collective-permute-start | bytes 1572872 | tf_op jit(solution)/shard_map/ppermute | solution.py:405
  37.7 6.0 %collective-permute-start.10 = (f32[64,128]{1,0:T(8,128)S(1)}, f32[64,128]{1,0:T(8,128)S(1)}, u32[]{:S(2)}, u32[]{:S(2)}) collective-permute-start(f32[64,128]{1,0:T(8,128)S(1)} %get-tuple-element.31), channel_id=1, source_target_pairs={{0,12},{4,0},{8,4},{12,8},{1,13},{5,1},{9,5},{13,9},{2,14},{6,2},{... | collective-permute-start | bytes 98312 | tf_op jit(solution)/shard_map/ppermute | solution.py:405
  37.8 7.9 %collective-permute-start.9 = (f32[64,128]{1,0:T(8,128)S(1)}, f32[64,128]{1,0:T(8,128)S(1)}, u32[]{:S(2)}, u32[]{:S(2)}) collective-permute-start(f32[64,128]{1,0:T(8,128)S(1)} %get-tuple-element.31), channel_id=1, source_target_pairs={{0,8},{4,12},{8,0},{12,4},{1,9},{5,13},{9,1},{13,5},{2,10},{6,14},... | collective-permute-start | bytes 98312 | tf_op jit(solution)/shard_map/ppermute | solution.py:405
  39.3 6.3 %collective-permute-start.8 = (f32[64,128]{1,0:T(8,128)S(1)}, f32[64,128]{1,0:T(8,128)S(1)}, u32[]{:S(2)}, u32[]{:S(2)}) collective-permute-start(f32[64,128]{1,0:T(8,128)S(1)} %get-tuple-element.31), channel_id=1, source_target_pairs={{0,4},{4,8},{8,12},{12,0},{1,5},{5,9},{9,13},{13,1},{2,6},{6,10},{... | collective-permute-start | bytes 98312 | tf_op jit(solution)/shard_map/ppermute | solution.py:405
  41.3 8.4 %collective-permute-start.12 = (f32[256,128]{1,0:T(8,128)S(1)}, f32[256,128]{1,0:T(8,128)S(1)}, u32[]{:S(2)}, u32[]{:S(2)}) collective-permute-start(f32[256,128]{1,0:T(8,128)S(1)} %get-tuple-element.35), channel_id=1, source_target_pairs={{0,4},{4,8},{8,12},{12,0},{1,5},{5,9},{9,13},{13,1},{2,6},{6,10},{... | collective-permute-start | bytes 393224 | tf_op jit(solution)/shard_map/ppermute | solution.py:405
  41.3 12.2 %collective-permute-start.13 = (f32[256,128]{1,0:T(8,128)S(1)}, f32[256,128]{1,0:T(8,128)S(1)}, u32[]{:S(2)}, u32[]{:S(2)}) collective-permute-start(f32[256,128]{1,0:T(8,128)S(1)} %get-tuple-element.36), channel_id=1, source_target_pairs={{0,8},{4,12},{8,0},{12,4},{1,9},{5,13},{9,1},{13,5},{2,10},{6,14},... | collective-permute-start | bytes 393224 | tf_op jit(solution)/shard_map/ppermute | solution.py:405
  43.7 9.8 %collective-permute-start.14 = (f32[256,128]{1,0:T(8,128)S(1)}, f32[256,128]{1,0:T(8,128)S(1)}, u32[]{:S(2)}, u32[]{:S(2)}) collective-permute-start(f32[256,128]{1,0:T(8,128)S(1)} %get-tuple-element.37), channel_id=1, source_target_pairs={{0,12},{4,0},{8,4},{12,8},{1,13},{5,1},{9,5},{13,9},{2,14},{6,2},{... | collective-permute-start | bytes 393224 | tf_op jit(solution)/shard_map/ppermute | solution.py:405
  45.7 4.0 %collective-permute-start.11 = (f32[64,128]{1,0:T(8,128)S(1)}, f32[64,128]{1,0:T(8,128)S(1)}, u32[]{:S(2)}, u32[]{:S(2)}) collective-permute-start(f32[64,128]{1,0:T(8,128)S(1)} %add_add_fusion.refs_3_.refs_0_), channel_id=1, source_target_pairs={{0,2},{2,0},{1,3},{3,1},{4,6},{6,4},{5,7},{7,5},{8,10},{10,8},{9,1... | collective-permute-start | bytes 98312 | tf_op jit(solution)/shard_map/ppermute | solution.py:413
  53.6 1.3 %collective-permute-start.15 = (bf16[1,256,128]{2,1,0:T(8,128)(2,1)S(1)}, bf16[1,256,128]{2,1,0:T(8,128)(2,1)S(1)}, u32[]{:S(2)}, u32[]{:S(2)}) collective-permute-start(bf16[1,256,128]{2,1,0:T(8,128)(2,1)S(1)} %get-tuple-element.38.refs_6_.refs_4_), channel_id=1, source_target_pairs={{0,1},{1,0},{2,3},{3,2},{4,5},{5,4},{6,7},{7,6},{8,9},{9,8},{10,11... | collective-permute-start | bytes 196616 | tf_op jit(solution)/shard_map/ppermute | solution.py:405
  53.6 1.4 %collective-permute-start.16 = (bf16[1,256,128]{2,1,0:T(8,128)(2,1)S(1)}, bf16[1,256,128]{2,1,0:T(8,128)(2,1)S(1)}, u32[]{:S(2)}, u32[]{:S(2)}) collective-permute-start(bf16[1,256,128]{2,1,0:T(8,128)(2,1)S(1)} %get-tuple-element.39.refs_7_.refs_5_), channel_id=1, source_target_pairs={{0,1},{1,0},{2,3},{3,2},{4,5},{5,4},{6,7},{7,6},{8,9},{9,8},{10,11... | collective-permute-start | bytes 196616 | tf_op jit(solution)/shard_map/ppermute | solution.py:405
  54.1 1.3 %collective-permute-start.17 = (bf16[1,256,128]{2,1,0:T(8,128)(2,1)S(1)}, bf16[1,256,128]{2,1,0:T(8,128)(2,1)S(1)}, u32[]{:S(2)}, u32[]{:S(2)}) collective-permute-start(bf16[1,256,128]{2,1,0:T(8,128)(2,1)S(1)} %get-tuple-element.40.refs_8_.refs_6_), channel_id=1, source_target_pairs={{0,1},{1,0},{2,3},{3,2},{4,5},{5,4},{6,7},{7,6},{8,9},{9,8},{10,11... | collective-permute-start | bytes 196616 | tf_op jit(solution)/shard_map/ppermute | solution.py:405
  56.4 8.4 %collective-permute-start.18 = (f32[32,2048]{1,0:T(8,128)S(1)}, f32[32,2048]{1,0:T(8,128)S(1)}, u32[]{:S(2)}, u32[]{:S(2)}) collective-permute-start(f32[32,2048]{1,0:T(8,128)S(1)} %get-tuple-element.42.mine), channel_id=1, source_target_pairs={{0,2},{2,0},{1,3},{3,1},{4,6},{6,4},{5,7},{7,5},{8,10},{10,8},{9,1... | collective-permute-start | bytes 786440 | tf_op jit(solution)/shard_map/ppermute | solution.py:413
  65.5 5.5 %collective-permute-start.19 = (f32[32,2048]{1,0:T(8,128)S(1)}, f32[32,2048]{1,0:T(8,128)S(1)}, u32[]{:S(2)}, u32[]{:S(2)}) collective-permute-start(f32[32,2048]{1,0:T(8,128)S(1)} %get-tuple-element.43.own.refs_0_), channel_id=1, source_target_pairs={{0,1},{1,0},{2,3},{3,2},{4,5},{5,4},{6,7},{7,6},{8,9},{9,8},{10,11... | collective-permute-start | bytes 786440 | tf_op jit(solution)/shard_map/ppermute | solution.py:405
  65.6 10.3 %collective-permute-start.21 = (f32[128,128]{1,0:T(8,128)S(1)}, f32[128,128]{1,0:T(8,128)S(1)}, u32[]{:S(2)}, u32[]{:S(2)}) collective-permute-start(f32[128,128]{1,0:T(8,128)S(1)} %get-tuple-element.44), channel_id=1, source_target_pairs={{0,4},{4,8},{8,12},{12,0},{1,5},{5,9},{9,13},{13,1},{2,6},{6,10},{... | collective-permute-start | bytes 196616 | tf_op jit(solution)/shard_map/ppermute | solution.py:405
  68.5 7.3 %collective-permute-start.22 = (f32[128,128]{1,0:T(8,128)S(1)}, f32[128,128]{1,0:T(8,128)S(1)}, u32[]{:S(2)}, u32[]{:S(2)}) collective-permute-start(f32[128,128]{1,0:T(8,128)S(1)} %get-tuple-element.45), channel_id=1, source_target_pairs={{0,8},{4,12},{8,0},{12,4},{1,9},{5,13},{9,1},{13,5},{2,10},{6,14},... | collective-permute-start | bytes 196616 | tf_op jit(solution)/shard_map/ppermute | solution.py:405
  69.8 6.0 %collective-permute-start.23 = (f32[128,128]{1,0:T(8,128)S(1)}, f32[128,128]{1,0:T(8,128)S(1)}, u32[]{:S(2)}, u32[]{:S(2)}) collective-permute-start(f32[128,128]{1,0:T(8,128)S(1)} %get-tuple-element.46), channel_id=1, source_target_pairs={{0,12},{4,0},{8,4},{12,8},{1,13},{5,1},{9,5},{13,9},{2,14},{6,2},{... | collective-permute-start | bytes 196616 | tf_op jit(solution)/shard_map/ppermute | solution.py:405
  72.1 3.8 %collective-permute-start.20 = (f32[32,128]{1,0:T(8,128)S(1)}, f32[32,128]{1,0:T(8,128)S(1)}, u32[]{:S(2)}, u32[]{:S(2)}) collective-permute-start(f32[32,128]{1,0:T(8,128)S(1)} %shard_map.67), channel_id=1, source_target_pairs={{0,4},{4,0},{8,12},{12,8},{1,5},{5,1},{9,13},{13,9},{2,6},{6,2},{1... | collective-permute-start | bytes 49160 | tf_op jit(solution)/shard_map/ppermute | solution.py:413
  76.9 7.8 %collective-permute-start.24 = (f32[32,2048]{1,0:T(8,128)S(1)}, f32[32,2048]{1,0:T(8,128)S(1)}, u32[]{:S(2)}, u32[]{:S(2)}) collective-permute-start(f32[32,2048]{1,0:T(8,128)S(1)} %shard_map.68.mine), channel_id=1, source_target_pairs={{0,2},{2,0},{1,3},{3,1},{4,6},{6,4},{5,7},{7,5},{8,10},{10,8},{9,1... | collective-permute-start | bytes 786440 | tf_op jit(solution)/shard_map/ppermute | solution.py:413
  78.4 4.6 %collective-permute-start.25 = (f32[32,128]{1,0:T(8,128)S(1)}, f32[32,128]{1,0:T(8,128)S(1)}, u32[]{:S(2)}, u32[]{:S(2)}) collective-permute-start(f32[32,128]{1,0:T(8,128)S(1)} %add.20.after.refs_0_), channel_id=1, source_target_pairs={{0,8},{4,12},{8,0},{12,4},{1,9},{5,13},{9,1},{13,5},{2,10},{6,14},... | collective-permute-start | bytes 49160 | tf_op jit(solution)/shard_map/ppermute | solution.py:413
  85.2 2.0 %collective-permute-start.26 = (f32[32,2048]{1,0:T(8,128)S(1)}, f32[32,2048]{1,0:T(8,128)S(1)}, u32[]{:S(2)}, u32[]{:S(2)}) collective-permute-start(f32[32,2048]{1,0:T(8,128)S(1)} %shard_map.69.after.own), channel_id=1, source_target_pairs={{0,1},{1,0},{2,3},{3,2},{4,5},{5,4},{6,7},{7,6},{8,9},{9,8},{10,11... | collective-permute-start | bytes 786440 | tf_op jit(solution)/shard_map/ppermute | solution.py:405
  88.8 3.7 %collective-permute-start.29 = (f32[32,128]{1,0:T(8,128)S(1)}, f32[32,128]{1,0:T(8,128)S(1)}, u32[]{:S(2)}, u32[]{:S(2)}) collective-permute-start(f32[32,128]{1,0:T(8,128)S(1)} %get-tuple-element.48.refs_0_), channel_id=1, source_target_pairs={{0,12},{4,0},{8,4},{12,8},{1,13},{5,1},{9,5},{13,9},{2,14},{6,2},{... | collective-permute-start | bytes 49160 | tf_op jit(solution)/shard_map/ppermute | solution.py:405
  90.6 4.6 %collective-permute-start.28 = (f32[32,128]{1,0:T(8,128)S(1)}, f32[32,128]{1,0:T(8,128)S(1)}, u32[]{:S(2)}, u32[]{:S(2)}) collective-permute-start(f32[32,128]{1,0:T(8,128)S(1)} %get-tuple-element.48.refs_0_), channel_id=1, source_target_pairs={{0,8},{4,12},{8,0},{12,4},{1,9},{5,13},{9,1},{13,5},{2,10},{6,14},... | collective-permute-start | bytes 49160 | tf_op jit(solution)/shard_map/ppermute | solution.py:405
  91.7 5.5 %collective-permute-start.27 = (f32[32,128]{1,0:T(8,128)S(1)}, f32[32,128]{1,0:T(8,128)S(1)}, u32[]{:S(2)}, u32[]{:S(2)}) collective-permute-start(f32[32,128]{1,0:T(8,128)S(1)} %get-tuple-element.48.refs_0_), channel_id=1, source_target_pairs={{0,4},{4,8},{8,12},{12,0},{1,5},{5,9},{9,13},{13,1},{2,6},{6,10},{... | collective-permute-start | bytes 49160 | tf_op jit(solution)/shard_map/ppermute | solution.py:405
  (1 other events, 1.4 us)

commit v8 on v7

--- a/solution.py
+++ b/solution.py
@@ -9,6 +9,8 @@
 
 BLOCK = 128
 kernel_gamma = 14.0
+CODE_TOP = 32767.0
+CODE_ROWS = 16
 
 VMEM = pl.BlockSpec(memory_space=pltpu.VMEM)
 SMEM = pl.BlockSpec(memory_space=pltpu.SMEM)
@@ -19,7 +21,7 @@
 NT = (((1,), (1,)), ((), ()))
 
 
-def call(body, outs, args, smem_in=(), smem_out=(), any_in=()):
+def call(body, outs, args, smem_in=(), smem_out=(), any_in=(), scratch=()):
     single = not isinstance(outs, (list, tuple))
     shapes = [outs] if single else list(outs)
     result = pl.pallas_call(
@@ -29,6 +31,7 @@
             SMEM if i in smem_in else ANY if i in any_in else VMEM for i in range(len(args))
         ],
         out_specs=[SMEM if i in smem_out else VMEM for i in range(len(shapes))],
+        scratch_shapes=list(scratch),
         compiler_params=pltpu.CompilerParams(vmem_limit_bytes=48 * 2**20),
     )(*args)
     return result[0] if single else result
@@ -56,6 +59,36 @@
 
 def pack(tile):
     return jnp.concatenate(halves(tile), axis=0)
+
+
+def encode(values):
+    most = jnp.max(jnp.abs(values), axis=0, keepdims=True)
+    power = jnp.floor(jnp.log2(jnp.maximum(most, 1e-30))) + 1.0
+    steps = jnp.floor(values * (CODE_TOP * jnp.exp2(-power)) + 0.5)
+    steps = jnp.minimum(jnp.maximum(steps, -CODE_TOP), CODE_TOP)
+    return steps.astype(jnp.int32).astype(jnp.int16), power
+
+
+def decode(steps, power):
+    return steps.astype(jnp.int32).astype(F32) * (jnp.exp2(power) * (1.0 / CODE_TOP))
+
+
+def as_rows(powers, count):
+    rows = jnp.concatenate([*powers, jnp.zeros((count - len(powers), BLOCK), F32)], axis=0)
+    return rows.astype(jnp.int32).astype(jnp.int16)
+
+
+def power_rows(rows):
+    return rows.astype(jnp.int32).astype(F32)
+
+
+def row_at(rows, place):
+    if isinstance(place, int):
+        return rows[place : place + 1, :]
+    line = rows[:1, :]
+    for i in range(1, rows.shape[0]):
+        line = jnp.where(place == i, rows[i : i + 1, :], line)
+    return line
 
 
 def product(packed, values):
@@ -226,7 +259,8 @@
         sums[i : i + 1, :] = jnp.sum(tile, axis=0, keepdims=True)
 
 
-def pair_tile_body(dims, me, idx, mine, other, self_sums, values, near_tiles, home_tiles, table, *sends):
+def pair_tile_body(dims, me, idx, mine, other, self_sums, values, near_tiles, home_tiles, table, *refs):
+    sends, (codes, powers) = refs[:-2], refs[-2:]
     row_count, capacity, per_core, blocks_here, tile_count = dims
     row, tile_index, core = me[0], me[1], me[2]
     table[...] = jnp.zeros(table.shape, F32)
@@ -237,7 +271,9 @@
         place = pl.ds(block, 1)
         table[place, :] = table[place, :] + line
 
+    encode_blocks(values, codes, powers)
     for k in range(row_count):
+        tiles = []
         for j in range(capacity):
             slot = k * capacity + j
             part = slice(slot * BLOCK, (slot + 1) * BLOCK)
@@ -249,33 +285,44 @@
             add(idx[1, slot], jnp.sum(tile, axis=0, keepdims=True))
             if k == 0:
                 home_tiles[j] = pack(tile)
-            else:
-
-                @pl.when(core == j // per_core)
-                def _():
-                    inner = j % per_core
-                    sends[k - 1][inner * BLOCK : (inner + 1) * BLOCK, :] = tile
-
-    pick_columns(idx, row_count, capacity, values, sends, per_core * BLOCK)
+            tiles.append(tile)
+        if k > 0:
+            lines = []
+            for inner in range(per_core):
+                tile = jnp.where(core == 0, tiles[inner], tiles[per_core + inner])
+                steps, power = encode(tile)
+                sends[k - 1][inner * BLOCK : (inner + 1) * BLOCK, :] = steps
+                lines.append(power)
+            pick_columns(idx, k, row_count, capacity, codes, powers, sends[k - 1], per_core * BLOCK, lines)
+
+
+def encode_blocks(values, codes, powers):
+    for b in range(powers.shape[0]):
+        part = slice(b * BLOCK, (b + 1) * BLOCK)
+        steps, power = encode(values[:, part])
+        codes[:, part] = steps
+        powers[b : b + 1, :] = power
 
 
 def split_body(row_count, per_core, *refs):
     others = row_count - 1
     messages, outs = refs[:others], refs[-others:]
     for message, out in zip(messages, outs):
+        powers = power_rows(message[message.shape[0] - CODE_ROWS :, :])
         for inner in range(per_core):
-            out[inner] = pack(message[inner * BLOCK : (inner + 1) * BLOCK, :])
-
-
-def pick_columns(idx, row_count, capacity, source, sends, base):
-    count = source.shape[0]
-    for k in range(1, row_count):
-        back = row_count - k
-        blocks = [idx[0, k * capacity + j] for j in range(capacity)]
-        blocks += [idx[4, back * capacity + j] for j in range(capacity)]
-        for place, block in enumerate(blocks):
-            rows = slice(base + place * count, base + (place + 1) * count)
-            sends[k - 1][rows, :] = source[:, at_block(block)]
+            steps = message[inner * BLOCK : (inner + 1) * BLOCK, :]
+            out[inner] = pack(decode(steps, powers[inner : inner + 1, :]))
+
+
+def pick_columns(idx, k, row_count, capacity, codes, powers, send, base, lines):
+    count = codes.shape[0]
+    back = row_count - k
+    blocks = [idx[0, k * capacity + j] for j in range(capacity)]
+    blocks += [idx[4, back * capacity + j] for j in range(capacity)]
+    for place, block in enumerate(blocks):
+        send[base + place * count : base + (place + 1) * count, :] = codes[:, at_block(block)]
+        lines.append(powers[pl.ds(block, 1), :])
+    send[base + len(blocks) * count :, :] = as_rows(lines, CODE_ROWS)
 
 
 def apply_tiles(dims, me, idx, inverse, own, received, base, near_tiles, home_tiles, sent, shared, self_tiles, out):
@@ -291,8 +338,13 @@
         place = at_block(block)
         out[:, place] = out[:, place] + product(packed, values)
 
+    lines = [power_rows(message[message.shape[0] - CODE_ROWS :, :]) for message in received]
+    first_line = base // BLOCK
+
     def arrived(k, place):
-        return received[k - 1][pl.ds(pl.multiple_of(base + place * count, 8), count), :]
+        steps = received[k - 1][pl.ds(pl.multiple_of(base + place * count, CODE_ROWS), count), :]
+        rows = lines[k - 1][first_line : first_line + 2 * capacity, :]
+        return decode(steps, row_at(rows, place))
 
     for i in range(blocks_here // tile_count):
         block = i * tile_count + tile_index
@@ -324,19 +376,30 @@
             add(idx[4, slot], packed, scaled(values, idx[5, slot]))
 
 
-def first_apply_body(dims, me, idx, *refs):
+def first_apply_body(dims, coded, me, idx, *refs):
     row_count, per_core = dims[0], dims[2]
     terms, refs = refs[:2], refs[2:]
     own, near_tiles, home_tiles, self_tiles = refs[:4]
     sent, shared = refs[4 : 3 + row_count], refs[3 + row_count : 2 + 2 * row_count]
-    messages = refs[2 + 2 * row_count : -3]
-    out, degree, inverse = refs[-3:]
+    messages = refs[2 + 2 * row_count : -4]
+    out, degree, inverse, total_out = refs[-4:]
     total = terms[0][...] + terms[1][...]
     degree[...] = total
     inverse[...] = 1.0 / jnp.sqrt(total)
     apply_tiles(
-        dims, me, idx, inverse, own, messages, per_core * BLOCK, near_tiles, home_tiles, sent, shared, self_tiles, out
-    )
+        dims, me, idx, inverse, own, messages, per_core * BLOCK, near_tiles, home_tiles, sent, shared, self_tiles, total_out
+    )
+    if not coded:
+        out[...] = total_out[...]
+        return
+    lines = []
+    blocks_here = dims[3]
+    for b in range(blocks_here):
+        part = slice(b * BLOCK, (b + 1) * BLOCK)
+        steps, power = encode(total_out[:, part])
+        out[:, part] = steps
+        lines.append(power)
+    out[:, blocks_here * BLOCK :] = as_rows(lines, out.shape[0])
 
 
 def second_apply_body(dims, me, idx, inverse, after, *refs):
@@ -347,20 +410,31 @@
     apply_tiles(dims, me, idx, inverse, own, received, 0, near_tiles, home_tiles, sent, shared, self_tiles, out)
 
 
-def scale_rows(me, blocks_here, inverse, mine, other, out):
+def mapped_body(dims, coded, me, idx, inverse, mine, other, out, *refs):
+    row_count, capacity, per_core, blocks_here, tile_count = dims
+    sends, (codes, powers) = refs[:-2], refs[-2:]
+    if coded:
+        tail = blocks_here * BLOCK
+        my_powers, other_powers = power_rows(mine[:, tail:]), power_rows(other[:, tail:])
+    for b in range(blocks_here):
+        part = slice(b * BLOCK, (b + 1) * BLOCK)
+        row = inverse[pl.ds(me[0] * blocks_here + b, 1), :]
+        if coded:
+            line = slice(b, b + 1)
+            value = decode(mine[:, part], my_powers[line]) + decode(other[:, part], other_powers[line])
+        else:
+            value = mine[:, part] + other[:, part]
+        out[:, part] = value * row
+    encode_blocks(out, codes, powers)
+    for k in range(1, row_count):
+        pick_columns(idx, k, row_count, capacity, codes, powers, sends[k - 1], 0, [])
+
+
+def last_mapped_body(blocks_here, me, inverse, mine, other, after, out):
     for b in range(blocks_here):
         part = slice(b * BLOCK, (b + 1) * BLOCK)
         row = inverse[pl.ds(me[0] * blocks_here + b, 1), :]
         out[:, part] = (mine[:, part] + other[:, part]) * row
-
-
-def mapped_body(row_count, capacity, blocks_here, me, idx, inverse, mine, other, out, *sends):
-    scale_rows(me, blocks_here, inverse, mine, other, out)
-    pick_columns(idx, row_count, capacity, out, sends, 0)
-
-
-def last_mapped_body(blocks_here, me, inverse, mine, other, *refs):
-    scale_rows(me, blocks_here, inverse, mine, other, refs[-1])
 
 
 def folded(square):
@@ -480,12 +554,15 @@
     dims = (row_count, capacity, per_core, blocks_here, tile_count)
     table = sds((block_count, BLOCK), F32)
     picked = 2 * capacity * own_cols
+    code_scratch = [pltpu.VMEM((own_cols, rows_here), jnp.int16), pltpu.VMEM((blocks_here, BLOCK), F32)]
+    coded = tile_count == 2
     tiles = call(
         functools.partial(pair_tile_body, dims),
         [sds((slots, 2 * BLOCK, BLOCK), BF16), sds((capacity, 2 * BLOCK, BLOCK), BF16), table]
-        + [sds((per_core * BLOCK + picked, BLOCK), F32) for _ in others],
+        + [sds((per_core * BLOCK + picked + CODE_ROWS, BLOCK), jnp.int16) for _ in others],
         [me, idx, pair_part, pair_other, self_sums, values],
         smem_in=(0, 1),
+        scratch=code_scratch,
     )
     near_tiles, home_tiles, degrees, sends = tiles[0], tiles[1], tiles[2], tiles[3:]
     degrees = functools.reduce(jnp.add, row_terms(degrees, row_count))
@@ -505,17 +582,19 @@
     folded_square = sds((own_cols, 4 * own_cols), F32)
 
     part, degree, inverse = call(
-        functools.partial(first_apply_body, dims),
-        [block_shape, table, table],
+        functools.partial(first_apply_body, dims, coded),
+        [sds((own_cols, rows_here + BLOCK), jnp.int16) if coded else block_shape, table, table],
         [me, idx, *degree_terms, values, *tile_args, *messages],
         smem_in=(0, 1),
+        scratch=[pltpu.VMEM((own_cols, rows_here), F32)],
     )
     mine, other = pair_sum(part, ("tiles",))
     first = call(
-        functools.partial(mapped_body, row_count, capacity, blocks_here),
-        [block_shape] + [sds((picked, BLOCK), F32) for _ in others],
+        functools.partial(mapped_body, dims, coded),
+        [block_shape] + [sds((picked + CODE_ROWS, BLOCK), jnp.int16) for _ in others],
         [me, idx, inverse, mine, other],
         smem_in=(0, 1),
+        scratch=code_scratch,
     )
     mapped, sends = first[0], first[1:]
     received = [shift_by(sends[k - 1], "rows", row_count, k) for k in others]

time: 101 us -> 91.7 us (0.908)
  waiting for transfers between devices: 46.8 us -> 37.3 us
    ppermute x25, waiting for transfers between devices: 28.9 us -> 24 us  [shift_by(): lax.ppermute(value, axes, [(i, (i + shift) % size) for i in range(size)])]
    ppermute x5, waiting for transfers between devices: 17.9 us -> 13.3 us  [pair_step(): lax.ppermute(value, name, [(i, i ^ flip) for i in range(lax.axis_size(nam...]
  transfers between devices with their start and end apart: 30 -> 30, of which waited for: 17 -> 15; matrix products, arithmetic and copies ran while one was open for 1% -> 1% of each run, Pallas kernels for 5% -> 6%
where the time goes in v8:
time: 91.7 us; the launch traced here: 91.5 us
  waiting for transfers between devices  37.3 us (41%)
  starting transfers between devices  33 us (36%)
  Pallas kernels  17 us (19%)
  local copies, waits for them, and re-layouts  2.7 us (3%)
  between operations  1.46 us (2%)
    ppermute x25, starting transfers between devices, shift_by(): lax.ppermute(value, axes, [(i, (i + shift) % size) for i in range(size)])  26 us
    ppermute x25, waiting for transfers between devices, shift_by(): lax.ppermute(value, axes, [(i, (i + shift) % size) for i in range(size)])  24 us
    pallas_call x14, Pallas kernels, call(): pl.pallas_call(body, out_shape=shapes, in_specs=[SMEM if i in smem_in els...  17 us
    ppermute x5, waiting for transfers between devices, pair_step(): lax.ppermute(value, name, [(i, i ^ flip) for i in range(lax.axis_size(nam...  13.3 us
    ppermute x5, starting transfers between devices, pair_step(): lax.ppermute(value, name, [(i, i ^ flip) for i in range(lax.axis_size(nam...  7 us
  transfers between devices with their start and end apart: 30, of which 15 were waited for; matrix products, arithmetic and copies ran while one was open for 1% of the time, Pallas kernels for 6%

profile of v8, /device:TPU:0, one launch (start us, length us, event | category | flops | bytes accessed | tf_op | source)
XLA Modules:
  0.0 91.5 jit_solution(1361591676433875405)
XLA Ops:
  2.0 5.0 %collective-permute-start.2 = (s32[3,8]{1,0:T(4,128)S(1)}, s32[3,8]{1,0:T(4,128)S(1)}, u32[]{:S(2)}, u32[]{:S(2)}) collective-permute-start(s32[3,8]{1,0:T(4,128)S(1)} %concatenate.3.refs_0_), channel_id=1, source_target_pairs={{0,12},{4,0},{8,4},{12,8},{1,13},{5,1},{9,5},{13,9},{2,14},{6,2},{... | collective-permute-start | bytes 296 | tf_op jit(solution)/shard_map/ppermute | solution.py:479
  8.1 1.4 %copy-done = bf16[2048,384]{1,0:T(8,128)(2,1)S(1)} copy-done((bf16[2048,384]{1,0:T(8,128)(2,1)S(1)}, bf16[2048,384]{1,0:T(8,128)(2,1)}, u32[]{:S(2)}) %copy-start) | copy-done | bytes 1572888
  12.4 2.1 %shard_map.60 = (s32[6,8]{1,0:T(8,128)S(1)}, bf16[256,384]{1,0:T(8,128)(2,1)S(1)}, bf16[256,384]{1,0:T(8,128)(2,1)S(1)}, bf16[256,384]{1,0:T(8,128)(2,1)S(1)}) custom-call(s32[3]{0:T(128)S(1)} %pad_add_fusion.me, s32[3,8]{1,0:T(4,128)S(1)} %concatenate.3.refs_0_, s32[3,8]{1,0:T(4,128)S(1)} %collective-permute-done.refs_1_, ...), custom_call_target="tpu_custom_call" | custom-call | tf_op jit(solution)/shard_map/pallas_call | solution.py:27
  15.6 1.1 %collective-permute-start.4 = (bf16[256,384]{1,0:T(8,128)(2,1)S(1)}, bf16[256,384]{1,0:T(8,128)(2,1)S(1)}, u32[]{:S(2)}, u32[]{:S(2)}) collective-permute-start(bf16[256,384]{1,0:T(8,128)(2,1)S(1)} %get-tuple-element.28), channel_id=1, source_target_pairs={{0,8},{4,12},{8,0},{12,4},{1,9},{5,13},{9,1},{13,5},{2,10},{6,14},... | collective-permute-start | bytes 589832 | tf_op jit(solution)/shard_map/ppermute | solution.py:479
  17.8 3.2 %collective-permute-done.3.refs_0_ = bf16[256,384]{1,0:T(8,128)(2,1)S(1)} collective-permute-done((bf16[256,384]{1,0:T(8,128)(2,1)S(1)}, bf16[256,384]{1,0:T(8,128)(2,1)S(1)}, u32[]{:S(2)}, u32[]{:S(2)}) %collective-permute-start.3) | collective-permute-done | bytes 196640 | tf_op jit(solution)/shard_map/ppermute | solution.py:479
  21.0 12.1 %collective-permute-done.4.refs_1_ = bf16[256,384]{1,0:T(8,128)(2,1)S(1)} collective-permute-done((bf16[256,384]{1,0:T(8,128)(2,1)S(1)}, bf16[256,384]{1,0:T(8,128)(2,1)S(1)}, u32[]{:S(2)}, u32[]{:S(2)}) %collective-permute-start.4) | collective-permute-done | bytes 196640 | tf_op jit(solution)/shard_map/ppermute | solution.py:479
  33.1 1.2 %shard_map.61.mine = f32[1024,128]{1,0:T(8,128)S(1)} custom-call(s32[6,8]{1,0:T(8,128)S(1)} %get-tuple-element.26.idx, bf16[2048,384]{1,0:T(8,128)(2,1)S(1)} %copy-done.1, bf16[256,384]{1,0:T(8,128)(2,1)S(1)} %collective-permute-done.3.refs_0_, bf16[256,384]{1,0:T(8,128)(2,1)S(1)} %collective-permute-done.4.refs_1_, ...), custom_call_target="tpu_custom_call" | custom-call | tf_op jit(solution)/shard_map/pallas_call | solution.py:27
  34.6 1.7 %collective-permute-done.6.other = f32[1024,128]{1,0:T(8,128)S(1)} collective-permute-done((f32[1024,128]{1,0:T(8,128)S(1)}, f32[1024,128]{1,0:T(8,128)S(1)}, u32[]{:S(2)}, u32[]{:S(2)}) %collective-permute-start.6) | collective-permute-done | bytes 524320 | tf_op jit(solution)/shard_map/ppermute | solution.py:479
  37.4 1.6 %collective-permute-start.9 = (f32[64,128]{1,0:T(8,128)S(1)}, f32[64,128]{1,0:T(8,128)S(1)}, u32[]{:S(2)}, u32[]{:S(2)}) collective-permute-start(f32[64,128]{1,0:T(8,128)S(1)} %get-tuple-element.31), channel_id=1, source_target_pairs={{0,8},{4,12},{8,0},{12,4},{1,9},{5,13},{9,1},{13,5},{2,10},{6,14},... | collective-permute-start | bytes 98312 | tf_op jit(solution)/shard_map/ppermute | solution.py:479
  38.9 1.9 %collective-permute-start.8 = (f32[64,128]{1,0:T(8,128)S(1)}, f32[64,128]{1,0:T(8,128)S(1)}, u32[]{:S(2)}, u32[]{:S(2)}) collective-permute-start(f32[64,128]{1,0:T(8,128)S(1)} %get-tuple-element.31), channel_id=1, source_target_pairs={{0,4},{4,8},{8,12},{12,0},{1,5},{5,9},{9,13},{13,1},{2,6},{6,10},{... | collective-permute-start | bytes 98312 | tf_op jit(solution)/shard_map/ppermute | solution.py:479
  40.9 2.4 %collective-permute-start.13 = (s16[272,128]{1,0:T(8,128)(2,1)S(1)}, s16[272,128]{1,0:T(8,128)(2,1)S(1)}, u32[]{:S(2)}, u32[]{:S(2)}) collective-permute-start(s16[272,128]{1,0:T(8,128)(2,1)S(1)} %get-tuple-element.36), channel_id=1, source_target_pairs={{0,8},{4,12},{8,0},{12,4},{1,9},{5,13},{9,1},{13,5},{2,10},{6,14},... | collective-permute-start | bytes 208904 | tf_op jit(solution)/shard_map/ppermute | solution.py:479
  43.3 1.9 %collective-permute-start.14 = (s16[272,128]{1,0:T(8,128)(2,1)S(1)}, s16[272,128]{1,0:T(8,128)(2,1)S(1)}, u32[]{:S(2)}, u32[]{:S(2)}) collective-permute-start(s16[272,128]{1,0:T(8,128)(2,1)S(1)} %get-tuple-element.37), channel_id=1, source_target_pairs={{0,12},{4,0},{8,4},{12,8},{1,13},{5,1},{9,5},{13,9},{2,14},{6,2},{... | collective-permute-start | bytes 208904 | tf_op jit(solution)/shard_map/ppermute | solution.py:479
  45.3 1.5 %collective-permute-start.11 = (f32[64,128]{1,0:T(8,128)S(1)}, f32[64,128]{1,0:T(8,128)S(1)}, u32[]{:S(2)}, u32[]{:S(2)}) collective-permute-start(f32[64,128]{1,0:T(8,128)S(1)} %add_add_fusion.refs_3_.refs_0_), channel_id=1, source_target_pairs={{0,2},{2,0},{1,3},{3,1},{4,6},{6,4},{5,7},{7,5},{8,10},{10,8},{9,1... | collective-permute-start | bytes 98312 | tf_op jit(solution)/shard_map/ppermute | solution.py:487
  46.8 2.4 %collective-permute-done.11.refs_4_.refs_1_ = f32[64,128]{1,0:T(8,128)S(1)} collective-permute-done((f32[64,128]{1,0:T(8,128)S(1)}, f32[64,128]{1,0:T(8,128)S(1)}, u32[]{:S(2)}, u32[]{:S(2)}) %collective-permute-start.11) | collective-permute-done | bytes 32800 | tf_op jit(solution)/shard_map/ppermute | solution.py:487
  51.2 1.1 %shard_map.65 = (s16[32,2176]{1,0:T(8,128)(2,1)S(1)}, f32[64,128]{1,0:T(8,128)S(1)}, f32[64,128]{1,0:T(8,128)S(1)}) custom-call(s32[3]{0:T(128)S(1)} %pad_add_fusion.me, s32[6,8]{1,0:T(8,128)S(1)} %get-tuple-element.26.idx, f32[64,128]{1,0:T(8,128)S(1)} %add_add_fusion.refs_3_.refs_0_, f32[64,128]{1,0:T(8,128)S(1)} %collective-permute-done.11.refs_4_.refs_1_, ...), custom_call_target="tpu_custom_call" | custom-call | tf_op jit(solution)/shard_map/pallas_call | solution.py:27
  52.3 1.5 %collective-permute-start.18 = (s16[32,2176]{1,0:T(8,128)(2,1)S(1)}, s16[32,2176]{1,0:T(8,128)(2,1)S(1)}, u32[]{:S(2)}, u32[]{:S(2)}) collective-permute-start(s16[32,2176]{1,0:T(8,128)(2,1)S(1)} %get-tuple-element.42.mine), channel_id=1, source_target_pairs={{0,2},{2,0},{1,3},{3,1},{4,6},{6,4},{5,7},{7,5},{8,10},{10,8},{9,1... | collective-permute-start | bytes 417800 | tf_op jit(solution)/shard_map/ppermute | solution.py:487
  53.8 4.2 %collective-permute-done.18.other = s16[32,2176]{1,0:T(8,128)(2,1)S(1)} collective-permute-done((s16[32,2176]{1,0:T(8,128)(2,1)S(1)}, s16[32,2176]{1,0:T(8,128)(2,1)S(1)}, u32[]{:S(2)}, u32[]{:S(2)}) %collective-permute-start.18) | collective-permute-done | bytes 139296 | tf_op jit(solution)/shard_map/ppermute | solution.py:487
  59.0 1.6 %collective-permute-start.21 = (s16[144,128]{1,0:T(8,128)(2,1)S(1)}, s16[144,128]{1,0:T(8,128)(2,1)S(1)}, u32[]{:S(2)}, u32[]{:S(2)}) collective-permute-start(s16[144,128]{1,0:T(8,128)(2,1)S(1)} %get-tuple-element.44), channel_id=1, source_target_pairs={{0,4},{4,8},{8,12},{12,0},{1,5},{5,9},{9,13},{13,1},{2,6},{6,10},{... | collective-permute-start | bytes 110600 | tf_op jit(solution)/shard_map/ppermute | solution.py:479
  60.6 1.8 %collective-permute-start.22 = (s16[144,128]{1,0:T(8,128)(2,1)S(1)}, s16[144,128]{1,0:T(8,128)(2,1)S(1)}, u32[]{:S(2)}, u32[]{:S(2)}) collective-permute-start(s16[144,128]{1,0:T(8,128)(2,1)S(1)} %get-tuple-element.45), channel_id=1, source_target_pairs={{0,8},{4,12},{8,0},{12,4},{1,9},{5,13},{9,1},{13,5},{2,10},{6,14},... | collective-permute-start | bytes 110600 | tf_op jit(solution)/shard_map/ppermute | solution.py:479
  62.4 1.1 %collective-permute-start.23 = (s16[144,128]{1,0:T(8,128)(2,1)S(1)}, s16[144,128]{1,0:T(8,128)(2,1)S(1)}, u32[]{:S(2)}, u32[]{:S(2)}) collective-permute-start(s16[144,128]{1,0:T(8,128)(2,1)S(1)} %get-tuple-element.46), channel_id=1, source_target_pairs={{0,12},{4,0},{8,4},{12,8},{1,13},{5,1},{9,5},{13,9},{2,14},{6,2},{... | collective-permute-start | bytes 110600 | tf_op jit(solution)/shard_map/ppermute | solution.py:479
  63.5 1.1 %shard_map.67 = f32[32,128]{1,0:T(8,128)S(1)} custom-call(s32[3]{0:T(128)S(1)} %pad_add_fusion.me, f32[32,2048]{1,0:T(8,128)S(1)} %get-tuple-element.43.own.refs_0_, f32[32,2048]{1,0:T(8,128)S(1)} %collective-permute-done.19.other), custom_call_target="tpu_custom_call" | custom-call | tf_op jit(solution)/shard_map/pallas_call | solution.py:27
  65.5 2.8 %collective-permute-done.20 = f32[32,128]{1,0:T(8,128)S(1)} collective-permute-done((f32[32,128]{1,0:T(8,128)S(1)}, f32[32,128]{1,0:T(8,128)S(1)}, u32[]{:S(2)}, u32[]{:S(2)}) %collective-permute-start.20) | collective-permute-done | bytes 16416 | tf_op jit(solution)/shard_map/ppermute | solution.py:487
  69.4 1.5 %collective-permute-start.24 = (f32[32,2048]{1,0:T(8,128)S(1)}, f32[32,2048]{1,0:T(8,128)S(1)}, u32[]{:S(2)}, u32[]{:S(2)}) collective-permute-start(f32[32,2048]{1,0:T(8,128)S(1)} %shard_map.68.mine), channel_id=1, source_target_pairs={{0,2},{2,0},{1,3},{3,1},{4,6},{6,4},{5,7},{7,5},{8,10},{10,8},{9,1... | collective-permute-start | bytes 786440 | tf_op jit(solution)/shard_map/ppermute | solution.py:487
  70.9 1.4 %collective-permute-start.25 = (f32[32,128]{1,0:T(8,128)S(1)}, f32[32,128]{1,0:T(8,128)S(1)}, u32[]{:S(2)}, u32[]{:S(2)}) collective-permute-start(f32[32,128]{1,0:T(8,128)S(1)} %add.20.after.refs_0_), channel_id=1, source_target_pairs={{0,8},{4,12},{8,0},{12,4},{1,9},{5,13},{9,1},{13,5},{2,10},{6,14},... | collective-permute-start | bytes 49160 | tf_op jit(solution)/shard_map/ppermute | solution.py:487
  72.3 3.2 %collective-permute-done.25.after.refs_1_ = f32[32,128]{1,0:T(8,128)S(1)} collective-permute-done((f32[32,128]{1,0:T(8,128)S(1)}, f32[32,128]{1,0:T(8,128)S(1)}, u32[]{:S(2)}, u32[]{:S(2)}) %collective-permute-start.25) | collective-permute-done | bytes 16416 | tf_op jit(solution)/shard_map/ppermute | solution.py:487
  76.8 1.9 %shard_map.70.factor = f32[64,64]{1,0:T(8,128)S(1)} custom-call(f32[32,2048]{1,0:T(8,128)S(1)} %shard_map.69.after.own, f32[32,128]{1,0:T(8,128)S(1)} %add.20.after.refs_0_, f32[32,128]{1,0:T(8,128)S(1)} %collective-permute-done.25.after.refs_1_), custom_call_target="tpu_custom_call" | custom-call | tf_op jit(solution)/shard_map/pallas_call | solution.py:27
  78.7 1.5 %shard_map.71 = (bf16[128,2048]{1,0:T(8,128)(2,1)S(1)}, f32[32,128]{1,0:T(8,128)S(1)}) custom-call(s32[3]{0:T(128)S(1)} %pad_add_fusion.me, f32[64,64]{1,0:T(8,128)S(1)} %shard_map.70.factor, f32[32,2048]{1,0:T(8,128)S(1)} %shard_map.69.after.own, f32[32,2048]{1,0:T(8,128)S(1)} %collective-permute-done.26.other), custom_call_target="tpu_custom_call" | custom-call | tf_op jit(solution)/shard_map/pallas_call | solution.py:27
  80.2 1.9 %collective-permute-start.29 = (f32[32,128]{1,0:T(8,128)S(1)}, f32[32,128]{1,0:T(8,128)S(1)}, u32[]{:S(2)}, u32[]{:S(2)}) collective-permute-start(f32[32,128]{1,0:T(8,128)S(1)} %get-tuple-element.48.refs_0_), channel_id=1, source_target_pairs={{0,12},{4,0},{8,4},{12,8},{1,13},{5,1},{9,5},{13,9},{2,14},{6,2},{... | collective-permute-start | bytes 49160 | tf_op jit(solution)/shard_map/ppermute | solution.py:479
  82.6 1.0 %collective-permute-start.27 = (f32[32,128]{1,0:T(8,128)S(1)}, f32[32,128]{1,0:T(8,128)S(1)}, u32[]{:S(2)}, u32[]{:S(2)}) collective-permute-start(f32[32,128]{1,0:T(8,128)S(1)} %get-tuple-element.48.refs_0_), channel_id=1, source_target_pairs={{0,4},{4,8},{8,12},{12,0},{1,5},{5,9},{9,13},{13,1},{2,6},{6,10},{... | collective-permute-start | bytes 49160 | tf_op jit(solution)/shard_map/ppermute | solution.py:479
  84.3 2.5 %collective-permute-done.28.refs_2_ = f32[32,128]{1,0:T(8,128)S(1)} collective-permute-done((f32[32,128]{1,0:T(8,128)S(1)}, f32[32,128]{1,0:T(8,128)S(1)}, u32[]{:S(2)}, u32[]{:S(2)}) %collective-permute-start.28) | collective-permute-done | bytes 16416 | tf_op jit(solution)/shard_map/ppermute | solution.py:479
  86.7 1.4 %collective-permute-done.27.refs_1_ = f32[32,128]{1,0:T(8,128)S(1)} collective-permute-done((f32[32,128]{1,0:T(8,128)S(1)}, f32[32,128]{1,0:T(8,128)S(1)}, u32[]{:S(2)}, u32[]{:S(2)}) %collective-permute-start.27) | collective-permute-done | bytes 16416 | tf_op jit(solution)/shard_map/ppermute | solution.py:479
  88.2 3.4 %shard_map.72 = f32[32,2048]{1,0:T(8,128)} custom-call(s32[3]{0:T(128)S(1)} %pad_add_fusion.me, bf16[128,2048]{1,0:T(8,128)(2,1)S(1)} %get-tuple-element.47.mapped, f32[32,128]{1,0:T(8,128)S(1)} %get-tuple-element.48.refs_0_, f32[32,128]{1,0:T(8,128)S(1)} %collective-permute-done.27.refs_1_, f32[32,128]{1,0:T(8,128)S(1)} %collective-permute-done.28.refs_2_, ...), custom_call_target="tpu_custom_call" | custom-call | tf_op jit(solution)/shard_map/pallas_call | solution.py:27
  (53 shorter events, 15.2 us)
Async XLA Ops:
  2.0 8.6 %collective-permute-start.2 = (s32[3,8]{1,0:T(4,128)S(1)}, s32[3,8]{1,0:T(4,128)S(1)}, u32[]{:S(2)}, u32[]{:S(2)}) collective-permute-start(s32[3,8]{1,0:T(4,128)S(1)} %concatenate.3.refs_0_), channel_id=1, source_target_pairs={{0,12},{4,0},{8,4},{12,8},{1,13},{5,1},{9,5},{13,9},{2,14},{6,2},{... | collective-permute-start | bytes 296 | tf_op jit(solution)/shard_map/ppermute | solution.py:479
  7.0 4.5 %collective-permute-start.1 = (s32[3,8]{1,0:T(4,128)S(1)}, s32[3,8]{1,0:T(4,128)S(1)}, u32[]{:S(2)}, u32[]{:S(2)}) collective-permute-start(s32[3,8]{1,0:T(4,128)S(1)} %concatenate.3.refs_0_), channel_id=1, source_target_pairs={{0,8},{4,12},{8,0},{12,4},{1,9},{5,13},{9,1},{13,5},{2,10},{6,14},... | collective-permute-start | bytes 296 | tf_op jit(solution)/shard_map/ppermute | solution.py:479
  7.0 5.4 %collective-permute-start = (s32[3,8]{1,0:T(4,128)S(1)}, s32[3,8]{1,0:T(4,128)S(1)}, u32[]{:S(2)}, u32[]{:S(2)}) collective-permute-start(s32[3,8]{1,0:T(4,128)S(1)} %concatenate.3.refs_0_), channel_id=1, source_target_pairs={{0,4},{4,8},{8,12},{12,0},{1,5},{5,9},{9,13},{13,1},{2,6},{6,10},{... | collective-permute-start | bytes 296 | tf_op jit(solution)/shard_map/ppermute | solution.py:479
  10.5 22.6 %copy-start.1 = (bf16[2048,384]{1,0:T(8,128)(2,1)S(1)}, bf16[2048,384]{1,0:T(8,128)(2,1)}, u32[]{:S(2)}) copy-start(bf16[2048,384]{1,0:T(8,128)(2,1)} %emb.3) | copy-start | bytes 4718596
  14.6 6.4 %collective-permute-start.3 = (bf16[256,384]{1,0:T(8,128)(2,1)S(1)}, bf16[256,384]{1,0:T(8,128)(2,1)S(1)}, u32[]{:S(2)}, u32[]{:S(2)}) collective-permute-start(bf16[256,384]{1,0:T(8,128)(2,1)S(1)} %get-tuple-element.27), channel_id=1, source_target_pairs={{0,12},{4,0},{8,4},{12,8},{1,13},{5,1},{9,5},{13,9},{2,14},{6,2},{... | collective-permute-start | bytes 589832 | tf_op jit(solution)/shard_map/ppermute | solution.py:479
  15.6 17.5 %collective-permute-start.4 = (bf16[256,384]{1,0:T(8,128)(2,1)S(1)}, bf16[256,384]{1,0:T(8,128)(2,1)S(1)}, u32[]{:S(2)}, u32[]{:S(2)}) collective-permute-start(bf16[256,384]{1,0:T(8,128)(2,1)S(1)} %get-tuple-element.28), channel_id=1, source_target_pairs={{0,8},{4,12},{8,0},{12,4},{1,9},{5,13},{9,1},{13,5},{2,10},{6,14},... | collective-permute-start | bytes 589832 | tf_op jit(solution)/shard_map/ppermute | solution.py:479
  16.7 16.4 %collective-permute-start.5 = (bf16[256,384]{1,0:T(8,128)(2,1)S(1)}, bf16[256,384]{1,0:T(8,128)(2,1)S(1)}, u32[]{:S(2)}, u32[]{:S(2)}) collective-permute-start(bf16[256,384]{1,0:T(8,128)(2,1)S(1)} %get-tuple-element.29), channel_id=1, source_target_pairs={{0,4},{4,8},{8,12},{12,0},{1,5},{5,9},{9,13},{13,1},{2,6},{6,10},{... | collective-permute-start | bytes 589832 | tf_op jit(solution)/shard_map/ppermute | solution.py:479
  17.8 16.6 %collective-permute-start.7 = (f32[1024,128]{1,0:T(8,128)S(1)}, f32[1024,128]{1,0:T(8,128)S(1)}, u32[]{:S(2)}, u32[]{:S(2)}) collective-permute-start(f32[1024,128]{1,0:T(8,128)S(1)} %shard_map.59.refs_5_.mine), channel_id=1, source_target_pairs={{0,1},{1,0},{2,3},{3,2},{4,5},{5,4},{6,7},{7,6},{8,9},{9,8},{10,11... | collective-permute-start | bytes 1572872 | tf_op jit(solution)/shard_map/ppermute | solution.py:479
  33.1 3.1 %copy-start.2 = (f32[2048,32]{0,1:T(8,128)S(1)}, f32[2048,32]{0,1:T(8,128)}, u32[]{:S(2)}) copy-start(f32[2048,32]{0,1:T(8,128)} %param.5) | copy-start | bytes 786436
  34.3 2.0 %collective-permute-start.6 = (f32[1024,128]{1,0:T(8,128)S(1)}, f32[1024,128]{1,0:T(8,128)S(1)}, u32[]{:S(2)}, u32[]{:S(2)}) collective-permute-start(f32[1024,128]{1,0:T(8,128)S(1)} %shard_map.61.mine), channel_id=1, source_target_pairs={{0,1},{1,0},{2,3},{3,2},{4,5},{5,4},{6,7},{7,6},{8,9},{9,8},{10,11... | collective-permute-start | bytes 1572872 | tf_op jit(solution)/shard_map/ppermute | solution.py:479
  37.3 6.0 %collective-permute-start.10 = (f32[64,128]{1,0:T(8,128)S(1)}, f32[64,128]{1,0:T(8,128)S(1)}, u32[]{:S(2)}, u32[]{:S(2)}) collective-permute-start(f32[64,128]{1,0:T(8,128)S(1)} %get-tuple-element.31), channel_id=1, source_target_pairs={{0,12},{4,0},{8,4},{12,8},{1,13},{5,1},{9,5},{13,9},{2,14},{6,2},{... | collective-permute-start | bytes 98312 | tf_op jit(solution)/shard_map/ppermute | solution.py:479
  37.4 7.9 %collective-permute-start.9 = (f32[64,128]{1,0:T(8,128)S(1)}, f32[64,128]{1,0:T(8,128)S(1)}, u32[]{:S(2)}, u32[]{:S(2)}) collective-permute-start(f32[64,128]{1,0:T(8,128)S(1)} %get-tuple-element.31), channel_id=1, source_target_pairs={{0,8},{4,12},{8,0},{12,4},{1,9},{5,13},{9,1},{13,5},{2,10},{6,14},... | collective-permute-start | bytes 98312 | tf_op jit(solution)/shard_map/ppermute | solution.py:479
  38.9 6.3 %collective-permute-start.8 = (f32[64,128]{1,0:T(8,128)S(1)}, f32[64,128]{1,0:T(8,128)S(1)}, u32[]{:S(2)}, u32[]{:S(2)}) collective-permute-start(f32[64,128]{1,0:T(8,128)S(1)} %get-tuple-element.31), channel_id=1, source_target_pairs={{0,4},{4,8},{8,12},{12,0},{1,5},{5,9},{9,13},{13,1},{2,6},{6,10},{... | collective-permute-start | bytes 98312 | tf_op jit(solution)/shard_map/ppermute | solution.py:479
  40.9 8.4 %collective-permute-start.12 = (s16[272,128]{1,0:T(8,128)(2,1)S(1)}, s16[272,128]{1,0:T(8,128)(2,1)S(1)}, u32[]{:S(2)}, u32[]{:S(2)}) collective-permute-start(s16[272,128]{1,0:T(8,128)(2,1)S(1)} %get-tuple-element.35), channel_id=1, source_target_pairs={{0,4},{4,8},{8,12},{12,0},{1,5},{5,9},{9,13},{13,1},{2,6},{6,10},{... | collective-permute-start | bytes 208904 | tf_op jit(solution)/shard_map/ppermute | solution.py:479
  40.9 8.3 %collective-permute-start.13 = (s16[272,128]{1,0:T(8,128)(2,1)S(1)}, s16[272,128]{1,0:T(8,128)(2,1)S(1)}, u32[]{:S(2)}, u32[]{:S(2)}) collective-permute-start(s16[272,128]{1,0:T(8,128)(2,1)S(1)} %get-tuple-element.36), channel_id=1, source_target_pairs={{0,8},{4,12},{8,0},{12,4},{1,9},{5,13},{9,1},{13,5},{2,10},{6,14},... | collective-permute-start | bytes 208904 | tf_op jit(solution)/shard_map/ppermute | solution.py:479
  43.3 5.9 %collective-permute-start.14 = (s16[272,128]{1,0:T(8,128)(2,1)S(1)}, s16[272,128]{1,0:T(8,128)(2,1)S(1)}, u32[]{:S(2)}, u32[]{:S(2)}) collective-permute-start(s16[272,128]{1,0:T(8,128)(2,1)S(1)} %get-tuple-element.37), channel_id=1, source_target_pairs={{0,12},{4,0},{8,4},{12,8},{1,13},{5,1},{9,5},{13,9},{2,14},{6,2},{... | collective-permute-start | bytes 208904 | tf_op jit(solution)/shard_map/ppermute | solution.py:479
  45.3 4.0 %collective-permute-start.11 = (f32[64,128]{1,0:T(8,128)S(1)}, f32[64,128]{1,0:T(8,128)S(1)}, u32[]{:S(2)}, u32[]{:S(2)}) collective-permute-start(f32[64,128]{1,0:T(8,128)S(1)} %add_add_fusion.refs_3_.refs_0_), channel_id=1, source_target_pairs={{0,2},{2,0},{1,3},{3,1},{4,6},{6,4},{5,7},{7,5},{8,10},{10,8},{9,1... | collective-permute-start | bytes 98312 | tf_op jit(solution)/shard_map/ppermute | solution.py:487
  49.3 1.3 %collective-permute-start.15 = (bf16[1,256,128]{2,1,0:T(8,128)(2,1)S(1)}, bf16[1,256,128]{2,1,0:T(8,128)(2,1)S(1)}, u32[]{:S(2)}, u32[]{:S(2)}) collective-permute-start(bf16[1,256,128]{2,1,0:T(8,128)(2,1)S(1)} %get-tuple-element.38.refs_6_.refs_4_), channel_id=1, source_target_pairs={{0,1},{1,0},{2,3},{3,2},{4,5},{5,4},{6,7},{7,6},{8,9},{9,8},{10,11... | collective-permute-start | bytes 196616 | tf_op jit(solution)/shard_map/ppermute | solution.py:479
  49.4 1.4 %collective-permute-start.16 = (bf16[1,256,128]{2,1,0:T(8,128)(2,1)S(1)}, bf16[1,256,128]{2,1,0:T(8,128)(2,1)S(1)}, u32[]{:S(2)}, u32[]{:S(2)}) collective-permute-start(bf16[1,256,128]{2,1,0:T(8,128)(2,1)S(1)} %get-tuple-element.39.refs_7_.refs_5_), channel_id=1, source_target_pairs={{0,1},{1,0},{2,3},{3,2},{4,5},{5,4},{6,7},{7,6},{8,9},{9,8},{10,11... | collective-permute-start | bytes 196616 | tf_op jit(solution)/shard_map/ppermute | solution.py:479
  49.9 1.3 %collective-permute-start.17 = (bf16[1,256,128]{2,1,0:T(8,128)(2,1)S(1)}, bf16[1,256,128]{2,1,0:T(8,128)(2,1)S(1)}, u32[]{:S(2)}, u32[]{:S(2)}) collective-permute-start(bf16[1,256,128]{2,1,0:T(8,128)(2,1)S(1)} %get-tuple-element.40.refs_8_.refs_6_), channel_id=1, source_target_pairs={{0,1},{1,0},{2,3},{3,2},{4,5},{5,4},{6,7},{7,6},{8,9},{9,8},{10,11... | collective-permute-start | bytes 196616 | tf_op jit(solution)/shard_map/ppermute | solution.py:479
  52.3 5.8 %collective-permute-start.18 = (s16[32,2176]{1,0:T(8,128)(2,1)S(1)}, s16[32,2176]{1,0:T(8,128)(2,1)S(1)}, u32[]{:S(2)}, u32[]{:S(2)}) collective-permute-start(s16[32,2176]{1,0:T(8,128)(2,1)S(1)} %get-tuple-element.42.mine), channel_id=1, source_target_pairs={{0,2},{2,0},{1,3},{3,1},{4,6},{6,4},{5,7},{7,5},{8,10},{10,8},{9,1... | collective-permute-start | bytes 417800 | tf_op jit(solution)/shard_map/ppermute | solution.py:487
  58.9 4.6 %collective-permute-start.19 = (f32[32,2048]{1,0:T(8,128)S(1)}, f32[32,2048]{1,0:T(8,128)S(1)}, u32[]{:S(2)}, u32[]{:S(2)}) collective-permute-start(f32[32,2048]{1,0:T(8,128)S(1)} %get-tuple-element.43.own.refs_0_), channel_id=1, source_target_pairs={{0,1},{1,0},{2,3},{3,2},{4,5},{5,4},{6,7},{7,6},{8,9},{9,8},{10,11... | collective-permute-start | bytes 786440 | tf_op jit(solution)/shard_map/ppermute | solution.py:479
  59.0 9.3 %collective-permute-start.21 = (s16[144,128]{1,0:T(8,128)(2,1)S(1)}, s16[144,128]{1,0:T(8,128)(2,1)S(1)}, u32[]{:S(2)}, u32[]{:S(2)}) collective-permute-start(s16[144,128]{1,0:T(8,128)(2,1)S(1)} %get-tuple-element.44), channel_id=1, source_target_pairs={{0,4},{4,8},{8,12},{12,0},{1,5},{5,9},{9,13},{13,1},{2,6},{6,10},{... | collective-permute-start | bytes 110600 | tf_op jit(solution)/shard_map/ppermute | solution.py:479
  60.6 7.8 %collective-permute-start.22 = (s16[144,128]{1,0:T(8,128)(2,1)S(1)}, s16[144,128]{1,0:T(8,128)(2,1)S(1)}, u32[]{:S(2)}, u32[]{:S(2)}) collective-permute-start(s16[144,128]{1,0:T(8,128)(2,1)S(1)} %get-tuple-element.45), channel_id=1, source_target_pairs={{0,8},{4,12},{8,0},{12,4},{1,9},{5,13},{9,1},{13,5},{2,10},{6,14},... | collective-permute-start | bytes 110600 | tf_op jit(solution)/shard_map/ppermute | solution.py:479
  62.4 6.0 %collective-permute-start.23 = (s16[144,128]{1,0:T(8,128)(2,1)S(1)}, s16[144,128]{1,0:T(8,128)(2,1)S(1)}, u32[]{:S(2)}, u32[]{:S(2)}) collective-permute-start(s16[144,128]{1,0:T(8,128)(2,1)S(1)} %get-tuple-element.46), channel_id=1, source_target_pairs={{0,12},{4,0},{8,4},{12,8},{1,13},{5,1},{9,5},{13,9},{2,14},{6,2},{... | collective-permute-start | bytes 110600 | tf_op jit(solution)/shard_map/ppermute | solution.py:479
  64.5 3.8 %collective-permute-start.20 = (f32[32,128]{1,0:T(8,128)S(1)}, f32[32,128]{1,0:T(8,128)S(1)}, u32[]{:S(2)}, u32[]{:S(2)}) collective-permute-start(f32[32,128]{1,0:T(8,128)S(1)} %shard_map.67), channel_id=1, source_target_pairs={{0,4},{4,0},{8,12},{12,8},{1,5},{5,1},{9,13},{13,9},{2,6},{6,2},{1... | collective-permute-start | bytes 49160 | tf_op jit(solution)/shard_map/ppermute | solution.py:487
  69.4 6.7 %collective-permute-start.24 = (f32[32,2048]{1,0:T(8,128)S(1)}, f32[32,2048]{1,0:T(8,128)S(1)}, u32[]{:S(2)}, u32[]{:S(2)}) collective-permute-start(f32[32,2048]{1,0:T(8,128)S(1)} %shard_map.68.mine), channel_id=1, source_target_pairs={{0,2},{2,0},{1,3},{3,1},{4,6},{6,4},{5,7},{7,5},{8,10},{10,8},{9,1... | collective-permute-start | bytes 786440 | tf_op jit(solution)/shard_map/ppermute | solution.py:487
  70.9 4.6 %collective-permute-start.25 = (f32[32,128]{1,0:T(8,128)S(1)}, f32[32,128]{1,0:T(8,128)S(1)}, u32[]{:S(2)}, u32[]{:S(2)}) collective-permute-start(f32[32,128]{1,0:T(8,128)S(1)} %add.20.after.refs_0_), channel_id=1, source_target_pairs={{0,8},{4,12},{8,0},{12,4},{1,9},{5,13},{9,1},{13,5},{2,10},{6,14},... | collective-permute-start | bytes 49160 | tf_op jit(solution)/shard_map/ppermute | solution.py:487
  76.7 2.0 %collective-permute-start.26 = (f32[32,2048]{1,0:T(8,128)S(1)}, f32[32,2048]{1,0:T(8,128)S(1)}, u32[]{:S(2)}, u32[]{:S(2)}) collective-permute-start(f32[32,2048]{1,0:T(8,128)S(1)} %shard_map.69.after.own), channel_id=1, source_target_pairs={{0,1},{1,0},{2,3},{3,2},{4,5},{5,4},{6,7},{7,6},{8,9},{9,8},{10,11... | collective-permute-start | bytes 786440 | tf_op jit(solution)/shard_map/ppermute | solution.py:479
  80.2 4.1 %collective-permute-start.29 = (f32[32,128]{1,0:T(8,128)S(1)}, f32[32,128]{1,0:T(8,128)S(1)}, u32[]{:S(2)}, u32[]{:S(2)}) collective-permute-start(f32[32,128]{1,0:T(8,128)S(1)} %get-tuple-element.48.refs_0_), channel_id=1, source_target_pairs={{0,12},{4,0},{8,4},{12,8},{1,13},{5,1},{9,5},{13,9},{2,14},{6,2},{... | collective-permute-start | bytes 49160 | tf_op jit(solution)/shard_map/ppermute | solution.py:479
  82.1 4.6 %collective-permute-start.28 = (f32[32,128]{1,0:T(8,128)S(1)}, f32[32,128]{1,0:T(8,128)S(1)}, u32[]{:S(2)}, u32[]{:S(2)}) collective-permute-start(f32[32,128]{1,0:T(8,128)S(1)} %get-tuple-element.48.refs_0_), channel_id=1, source_target_pairs={{0,8},{4,12},{8,0},{12,4},{1,9},{5,13},{9,1},{13,5},{2,10},{6,14},... | collective-permute-start | bytes 49160 | tf_op jit(solution)/shard_map/ppermute | solution.py:479
  82.6 5.5 %collective-permute-start.27 = (f32[32,128]{1,0:T(8,128)S(1)}, f32[32,128]{1,0:T(8,128)S(1)}, u32[]{:S(2)}, u32[]{:S(2)}) collective-permute-start(f32[32,128]{1,0:T(8,128)S(1)} %get-tuple-element.48.refs_0_), channel_id=1, source_target_pairs={{0,4},{4,8},{8,12},{12,0},{1,5},{5,9},{9,13},{13,1},{2,6},{6,10},{... | collective-permute-start | bytes 49160 | tf_op jit(solution)/shard_map/ppermute | solution.py:479
  (1 other events, 1.4 us)

commit v9 on v8

--- a/solution.py
+++ b/solution.py
@@ -10,6 +10,7 @@
 BLOCK = 128
 kernel_gamma = 14.0
 CODE_TOP = 32767.0
+PART_TOP = 16384.0
 CODE_ROWS = 16
 
 VMEM = pl.BlockSpec(memory_space=pltpu.VMEM)
@@ -21,7 +22,7 @@
 NT = (((1,), (1,)), ((), ()))
 
 
-def call(body, outs, args, smem_in=(), smem_out=(), any_in=(), scratch=()):
+def call(body, outs, args, smem_in=(), smem_out=(), any_in=(), scratch=(), cost=0):
     single = not isinstance(outs, (list, tuple))
     shapes = [outs] if single else list(outs)
     result = pl.pallas_call(
@@ -32,6 +33,11 @@
         ],
         out_specs=[SMEM if i in smem_out else VMEM for i in range(len(shapes))],
         scratch_shapes=list(scratch),
+        cost_estimate=pl.CostEstimate(
+            flops=cost * 10**9, bytes_accessed=cost * 10**6, transcendentals=0
+        )
+        if cost
+        else None,
         compiler_params=pltpu.CompilerParams(vmem_limit_bytes=48 * 2**20),
     )(*args)
     return result[0] if single else result
@@ -61,25 +67,34 @@
     return jnp.concatenate(halves(tile), axis=0)
 
 
+def scale_of(power, part):
+    return jnp.exp2(power) * (part * (1.0 / PART_TOP))
+
+
 def encode(values):
-    most = jnp.max(jnp.abs(values), axis=0, keepdims=True)
-    power = jnp.floor(jnp.log2(jnp.maximum(most, 1e-30))) + 1.0
-    steps = jnp.floor(values * (CODE_TOP * jnp.exp2(-power)) + 0.5)
+    most = jnp.maximum(jnp.max(jnp.abs(values), axis=0, keepdims=True), 1e-30)
+    power = jnp.floor(jnp.log2(most)) + 1.0
+    part = jnp.floor(most * jnp.exp2(-power) * PART_TOP) + 1.0
+    steps = jnp.floor(values * (CODE_TOP / scale_of(power, part)) + 0.5)
     steps = jnp.minimum(jnp.maximum(steps, -CODE_TOP), CODE_TOP)
-    return steps.astype(jnp.int32).astype(jnp.int16), power
-
-
-def decode(steps, power):
-    return steps.astype(jnp.int32).astype(F32) * (jnp.exp2(power) * (1.0 / CODE_TOP))
-
-
-def as_rows(powers, count):
-    rows = jnp.concatenate([*powers, jnp.zeros((count - len(powers), BLOCK), F32)], axis=0)
+    return steps.astype(jnp.int32).astype(jnp.int16), power, part
+
+
+def decode(steps, scale):
+    return steps.astype(jnp.int32).astype(F32) * (scale * (1.0 / CODE_TOP))
+
+
+def as_rows(powers, parts, count):
+    fill = jnp.zeros((count // 2 - len(powers), BLOCK), F32)
+    fill = [fill] if fill.shape[0] else []
+    rows = jnp.concatenate([*powers, *fill, *parts, *fill], axis=0)
     return rows.astype(jnp.int32).astype(jnp.int16)
 
 
-def power_rows(rows):
-    return rows.astype(jnp.int32).astype(F32)
+def scale_rows(rows):
+    rows = rows.astype(jnp.int32).astype(F32)
+    half = rows.shape[0] // 2
+    return scale_of(rows[:half], rows[half:])
 
 
 def row_at(rows, place):
@@ -167,12 +182,9 @@
     sends = refs[row_count + 3 :]
     row = me[0]
 
-    def clear(i, carry):
-        for line in range(6):
+    for i in range(slots):
+        for line in (0, 1, 2, 4, 5):
             idx[line, i] = 0
-        return carry
-
-    lax.fori_loop(0, slots, clear, 0)
 
     def ranked(listed, want, write):
         count = listed[2, 0]
@@ -182,7 +194,12 @@
             far = listed[1, s]
             return write(s, near, far, far // blocks_here, s < count, counts)
 
-        lax.fori_loop(0, slots, step, (0,) * want)
+        if slots <= 8:
+            counts = (0,) * want
+            for s in range(slots):
+                counts = step(s, counts)
+        else:
+            lax.fori_loop(0, slots, step, (0,) * want)
 
     def write_own(s, near, far, owner, live, counts):
         shift = lax.rem(owner - row + row_count, row_count)
@@ -196,7 +213,6 @@
             idx[0, slot] = near - row * blocks_here
             idx[1, slot] = far
             idx[2, slot] = 1
-            idx[3, slot] = s
 
         return tuple(
             counts[k] + (live & (shift == k)).astype(jnp.int32) for k in range(row_count)
@@ -259,8 +275,7 @@
         sums[i : i + 1, :] = jnp.sum(tile, axis=0, keepdims=True)
 
 
-def pair_tile_body(dims, me, idx, mine, other, self_sums, values, near_tiles, home_tiles, table, *refs):
-    sends, (codes, powers) = refs[:-2], refs[-2:]
+def pair_tile_body(dims, me, idx, mine, other, self_sums, near_tiles, home_tiles, table, *chosen):
     row_count, capacity, per_core, blocks_here, tile_count = dims
     row, tile_index, core = me[0], me[1], me[2]
     table[...] = jnp.zeros(table.shape, F32)
@@ -271,7 +286,6 @@
         place = pl.ds(block, 1)
         table[place, :] = table[place, :] + line
 
-    encode_blocks(values, codes, powers)
     for k in range(row_count):
         tiles = []
         for j in range(capacity):
@@ -287,42 +301,58 @@
                 home_tiles[j] = pack(tile)
             tiles.append(tile)
         if k > 0:
-            lines = []
             for inner in range(per_core):
-                tile = jnp.where(core == 0, tiles[inner], tiles[per_core + inner])
-                steps, power = encode(tile)
-                sends[k - 1][inner * BLOCK : (inner + 1) * BLOCK, :] = steps
-                lines.append(power)
-            pick_columns(idx, k, row_count, capacity, codes, powers, sends[k - 1], per_core * BLOCK, lines)
-
-
-def encode_blocks(values, codes, powers):
+                part = slice(inner * BLOCK, (inner + 1) * BLOCK)
+                chosen[k - 1][part, :] = jnp.where(core == 0, tiles[inner], tiles[per_core + inner])
+
+
+def encode_blocks(values, codes, powers, parts):
     for b in range(powers.shape[0]):
-        part = slice(b * BLOCK, (b + 1) * BLOCK)
-        steps, power = encode(values[:, part])
-        codes[:, part] = steps
+        at = slice(b * BLOCK, (b + 1) * BLOCK)
+        steps, power, part = encode(values[:, at])
+        codes[:, at] = steps
         powers[b : b + 1, :] = power
+        parts[b : b + 1, :] = part
+
+
+def start_body(values, codes, powers, parts):
+    encode_blocks(values, codes, powers, parts)
+
+
+def message_body(dims, idx, codes, powers, parts, *refs):
+    row_count, capacity, per_core, blocks_here, tile_count = dims
+    chosen, sends = refs[: row_count - 1], refs[row_count - 1 :]
+    for k in range(1, row_count):
+        lines = ([], [])
+        for inner in range(per_core):
+            at = slice(inner * BLOCK, (inner + 1) * BLOCK)
+            steps, power, part = encode(chosen[k - 1][at, :])
+            sends[k - 1][at, :] = steps
+            lines[0].append(power)
+            lines[1].append(part)
+        pick_columns(idx, k, row_count, capacity, codes, powers, parts, sends[k - 1], per_core * BLOCK, lines)
 
 
 def split_body(row_count, per_core, *refs):
     others = row_count - 1
     messages, outs = refs[:others], refs[-others:]
     for message, out in zip(messages, outs):
-        powers = power_rows(message[message.shape[0] - CODE_ROWS :, :])
+        scales = scale_rows(message[message.shape[0] - CODE_ROWS :, :])
         for inner in range(per_core):
             steps = message[inner * BLOCK : (inner + 1) * BLOCK, :]
-            out[inner] = pack(decode(steps, powers[inner : inner + 1, :]))
-
-
-def pick_columns(idx, k, row_count, capacity, codes, powers, send, base, lines):
+            out[inner] = pack(decode(steps, scales[inner : inner + 1, :]))
+
+
+def pick_columns(idx, k, row_count, capacity, codes, powers, parts, send, base, lines):
     count = codes.shape[0]
     back = row_count - k
     blocks = [idx[0, k * capacity + j] for j in range(capacity)]
     blocks += [idx[4, back * capacity + j] for j in range(capacity)]
     for place, block in enumerate(blocks):
         send[base + place * count : base + (place + 1) * count, :] = codes[:, at_block(block)]
-        lines.append(powers[pl.ds(block, 1), :])
-    send[base + len(blocks) * count :, :] = as_rows(lines, CODE_ROWS)
+        lines[0].append(powers[pl.ds(block, 1), :])
+        lines[1].append(parts[pl.ds(block, 1), :])
+    send[base + len(blocks) * count :, :] = as_rows(*lines, CODE_ROWS)
 
 
 def apply_tiles(dims, me, idx, inverse, own, received, base, near_tiles, home_tiles, sent, shared, self_tiles, out):
@@ -338,7 +368,7 @@
         place = at_block(block)
         out[:, place] = out[:, place] + product(packed, values)
 
-    lines = [power_rows(message[message.shape[0] - CODE_ROWS :, :]) for message in received]
+    lines = [scale_rows(message[message.shape[0] - CODE_ROWS :, :]) for message in received]
     first_line = base // BLOCK
 
     def arrived(k, place):
@@ -378,12 +408,12 @@
 
 def first_apply_body(dims, coded, me, idx, *refs):
     row_count, per_core = dims[0], dims[2]
-    terms, refs = refs[:2], refs[2:]
+    terms, refs = refs[:row_count], refs[row_count:]
     own, near_tiles, home_tiles, self_tiles = refs[:4]
     sent, shared = refs[4 : 3 + row_count], refs[3 + row_count : 2 + 2 * row_count]
     messages = refs[2 + 2 * row_count : -4]
     out, degree, inverse, total_out = refs[-4:]
-    total = terms[0][...] + terms[1][...]
+    total = functools.reduce(lambda total, term: total + term[...], terms[1:], terms[0][...])
     degree[...] = total
     inverse[...] = 1.0 / jnp.sqrt(total)
     apply_tiles(
@@ -392,14 +422,15 @@
     if not coded:
         out[...] = total_out[...]
         return
-    lines = []
+    lines = ([], [])
     blocks_here = dims[3]
     for b in range(blocks_here):
-        part = slice(b * BLOCK, (b + 1) * BLOCK)
-        steps, power = encode(total_out[:, part])
-        out[:, part] = steps
-        lines.append(power)
-    out[:, blocks_here * BLOCK :] = as_rows(lines, out.shape[0])
+        at = slice(b * BLOCK, (b + 1) * BLOCK)
+        steps, power, part = encode(total_out[:, at])
+        out[:, at] = steps
+        lines[0].append(power)
+        lines[1].append(part)
+    out[:, blocks_here * BLOCK :] = as_rows(*lines, out.shape[0])
 
 
 def second_apply_body(dims, me, idx, inverse, after, *refs):
@@ -412,22 +443,22 @@
 
 def mapped_body(dims, coded, me, idx, inverse, mine, other, out, *refs):
     row_count, capacity, per_core, blocks_here, tile_count = dims
-    sends, (codes, powers) = refs[:-2], refs[-2:]
+    sends, (codes, powers, parts) = refs[:-3], refs[-3:]
     if coded:
         tail = blocks_here * BLOCK
-        my_powers, other_powers = power_rows(mine[:, tail:]), power_rows(other[:, tail:])
+        my_scales, other_scales = scale_rows(mine[:, tail:]), scale_rows(other[:, tail:])
     for b in range(blocks_here):
         part = slice(b * BLOCK, (b + 1) * BLOCK)
         row = inverse[pl.ds(me[0] * blocks_here + b, 1), :]
         if coded:
             line = slice(b, b + 1)
-            value = decode(mine[:, part], my_powers[line]) + decode(other[:, part], other_powers[line])
+            value = decode(mine[:, part], my_scales[line]) + decode(other[:, part], other_scales[line])
         else:
             value = mine[:, part] + other[:, part]
         out[:, part] = value * row
-    encode_blocks(out, codes, powers)
+    encode_blocks(out, codes, powers, parts)
     for k in range(1, row_count):
-        pick_columns(idx, k, row_count, capacity, codes, powers, sends[k - 1], 0, [])
+        pick_columns(idx, k, row_count, capacity, codes, powers, parts, sends[k - 1], 0, ([], []))
 
 
 def last_mapped_body(blocks_here, me, inverse, mine, other, after, out):
@@ -542,6 +573,11 @@
         [sds((own_blocks, 2 * BLOCK, BLOCK), BF16), sds((own_blocks, BLOCK), F32)],
         [self_part, self_other],
     )
+    values = start.T
+    code_shapes = [((own_cols, rows_here), jnp.int16), ((blocks_here, BLOCK), F32), ((blocks_here, BLOCK), F32)]
+    start_codes = call(start_body, [sds(*shape) for shape in code_shapes], [values])
+    code_scratch = [pltpu.VMEM(*shape) for shape in code_shapes]
+    coded = tile_count == 2
     pair_part = call(
         functools.partial(pair_distance_body, row_count, capacity),
         sds((slots * BLOCK, BLOCK), F32),
@@ -550,29 +586,32 @@
     )
     pair_other = shift_by(pair_part, "cols", core_count, 1)
 
-    values = start.T
     dims = (row_count, capacity, per_core, blocks_here, tile_count)
     table = sds((block_count, BLOCK), F32)
     picked = 2 * capacity * own_cols
-    code_scratch = [pltpu.VMEM((own_cols, rows_here), jnp.int16), pltpu.VMEM((blocks_here, BLOCK), F32)]
-    coded = tile_count == 2
     tiles = call(
         functools.partial(pair_tile_body, dims),
         [sds((slots, 2 * BLOCK, BLOCK), BF16), sds((capacity, 2 * BLOCK, BLOCK), BF16), table]
-        + [sds((per_core * BLOCK + picked + CODE_ROWS, BLOCK), jnp.int16) for _ in others],
-        [me, idx, pair_part, pair_other, self_sums, values],
+        + [sds((per_core * BLOCK, BLOCK), F32) for _ in others],
+        [me, idx, pair_part, pair_other, self_sums],
         smem_in=(0, 1),
-        scratch=code_scratch,
-    )
-    near_tiles, home_tiles, degrees, sends = tiles[0], tiles[1], tiles[2], tiles[3:]
-    degrees = functools.reduce(jnp.add, row_terms(degrees, row_count))
-    degree_terms = pair_sum(degrees, ("tiles",))
+    )
+    near_tiles, home_tiles, degrees, chosen = tiles[0], tiles[1], tiles[2], tiles[3:]
+    mine, other = pair_sum(degrees, ("tiles",))
+    degree_terms = row_terms(mine + other, row_count)
+    sends = call(
+        functools.partial(message_body, dims),
+        [sds((per_core * BLOCK + picked + CODE_ROWS, BLOCK), jnp.int16) for _ in others],
+        [idx, *start_codes, *chosen],
+        smem_in=(0,),
+        cost=3,
+    )
     messages = [shift_by(sends[k - 1], "rows", row_count, k) for k in others]
     sent = call(
         functools.partial(split_body, row_count, per_core),
         [sds((per_core, 2 * BLOCK, BLOCK), BF16) for _ in others],
         [*messages, *degree_terms],
-        any_in=(row_count - 1, row_count),
+        any_in=range(row_count - 1, 2 * row_count - 1),
     )
     shared = [shift_by(tile, "cols", core_count, 1) for tile in sent]
 
@@ -601,9 +640,6 @@
 
     mapped_other = shift_by(mapped, "cols", core_count, 1)
     first_gram = call(gram_body, folded_square, [me, mapped, mapped_other], smem_in=(0,))
-    steps = (row_count - 1).bit_length()
-    for bit in range(steps - 1):
-        first_gram = first_gram + pair_step(first_gram, "rows", 1 << bit)
     part = call(
         functools.partial(second_apply_body, dims),
         block_shape,
@@ -611,7 +647,7 @@
         smem_in=(0, 1),
         any_in=(3,),
     )
-    gram_terms = (first_gram, pair_step(first_gram, "rows", 1 << (steps - 1)))
+    gram_terms = pair_sum(first_gram, ("rows",))
     mine, other = pair_sum(part, ("tiles",))
     second = call(
         functools.partial(last_mapped_body, blocks_here),

time: 91.7 us -> 96.5 us (1.052)
  waiting for transfers between devices: 37.3 us -> 43.3 us
  starting transfers between devices: 33 us -> 31.3 us
    ppermute x25, waiting for transfers between devices: 24 us -> 32.1 us  [shift_by(): lax.ppermute(value, axes, [(i, (i + shift) % size) for i in range(size)])]
    ppermute x5, waiting for transfers between devices: 13.3 us -> 11.3 us  [pair_step(): lax.ppermute(value, name, [(i, i ^ flip) for i in range(lax.axis_size(nam...]
    ppermute x5, starting transfers between devices: 7 us -> 5.04 us  [pair_step(): lax.ppermute(value, name, [(i, i ^ flip) for i in range(lax.axis_size(nam...]
    pallas_call x14 -> x16, Pallas kernels: 17 us -> 17.4 us  [call(): pl.pallas_call(body, out_shape=shapes, in_specs=[SMEM if i in smem_in els...]
  transfers between devices with their start and end apart: 30 -> 30, of which waited for: 15 -> 18; matrix products, arithmetic and copies ran while one was open for 1% -> 1% of each run, Pallas kernels for 6% -> 6%
where the time goes in v9:
time: 96.5 us; the launch traced here: 96.3 us
  waiting for transfers between devices  43.3 us (45%)
  starting transfers between devices  31.3 us (32%)
  Pallas kernels  17.4 us (18%)
  local copies, waits for them, and re-layouts  2.71 us (3%)
  between operations  1.46 us (2%)
    ppermute x25, waiting for transfers between devices, shift_by(): lax.ppermute(value, axes, [(i, (i + shift) % size) for i in range(size)])  32.1 us
    ppermute x25, starting transfers between devices, shift_by(): lax.ppermute(value, axes, [(i, (i + shift) % size) for i in range(size)])  26.3 us
    pallas_call x16, Pallas kernels, call(): pl.pallas_call(body, out_shape=shapes, in_specs=[SMEM if i in smem_in els...  17.4 us
    ppermute x5, waiting for transfers between devices, pair_step(): lax.ppermute(value, name, [(i, i ^ flip) for i in range(lax.axis_size(nam...  11.3 us
    ppermute x5, starting transfers between devices, pair_step(): lax.ppermute(value, name, [(i, i ^ flip) for i in range(lax.axis_size(nam...  5.04 us
  transfers between devices with their start and end apart: 30, of which 18 were waited for; matrix products, arithmetic and copies ran while one was open for 1% of the time, Pallas kernels for 6%

profile of v9, /device:TPU:0, one launch (start us, length us, event | category | flops | bytes accessed | tf_op | source)
XLA Modules:
  0.0 96.3 jit_solution(3833605902170747712)
XLA Ops:
  2.0 5.0 %collective-permute-start.2 = (s32[3,8]{1,0:T(4,128)S(1)}, s32[3,8]{1,0:T(4,128)S(1)}, u32[]{:S(2)}, u32[]{:S(2)}) collective-permute-start(s32[3,8]{1,0:T(4,128)S(1)} %concatenate.3.refs_0_), channel_id=1, source_target_pairs={{0,12},{4,0},{8,4},{12,8},{1,13},{5,1},{9,5},{13,9},{2,14},{6,2},{... | collective-permute-start | bytes 296 | tf_op jit(solution)/shard_map/ppermute | solution.py:510
  8.1 1.4 %copy-done = bf16[2048,384]{1,0:T(8,128)(2,1)S(1)} copy-done((bf16[2048,384]{1,0:T(8,128)(2,1)S(1)}, bf16[2048,384]{1,0:T(8,128)(2,1)}, u32[]{:S(2)}) %copy-start) | copy-done | bytes 1572888
  12.4 1.8 %shard_map.60 = (s32[6,8]{1,0:T(8,128)S(1)}, bf16[256,384]{1,0:T(8,128)(2,1)S(1)}, bf16[256,384]{1,0:T(8,128)(2,1)S(1)}, bf16[256,384]{1,0:T(8,128)(2,1)S(1)}) custom-call(s32[3]{0:T(128)S(1)} %pad_add_fusion.me, s32[3,8]{1,0:T(4,128)S(1)} %concatenate.3.refs_0_, s32[3,8]{1,0:T(4,128)S(1)} %collective-permute-done.refs_1_, ...), custom_call_target="tpu_custom_call" | custom-call | tf_op jit(solution)/shard_map/pallas_call | solution.py:28
  14.2 1.0 %collective-permute-start.3 = (bf16[256,384]{1,0:T(8,128)(2,1)S(1)}, bf16[256,384]{1,0:T(8,128)(2,1)S(1)}, u32[]{:S(2)}, u32[]{:S(2)}) collective-permute-start(bf16[256,384]{1,0:T(8,128)(2,1)S(1)} %get-tuple-element.33), channel_id=1, source_target_pairs={{0,12},{4,0},{8,4},{12,8},{1,13},{5,1},{9,5},{13,9},{2,14},{6,2},{... | collective-permute-start | bytes 589832 | tf_op jit(solution)/shard_map/ppermute | solution.py:510
  15.3 1.1 %collective-permute-start.4 = (bf16[256,384]{1,0:T(8,128)(2,1)S(1)}, bf16[256,384]{1,0:T(8,128)(2,1)S(1)}, u32[]{:S(2)}, u32[]{:S(2)}) collective-permute-start(bf16[256,384]{1,0:T(8,128)(2,1)S(1)} %get-tuple-element.34), channel_id=1, source_target_pairs={{0,8},{4,12},{8,0},{12,4},{1,9},{5,13},{9,1},{13,5},{2,10},{6,14},... | collective-permute-start | bytes 589832 | tf_op jit(solution)/shard_map/ppermute | solution.py:510
  17.4 3.2 %collective-permute-done.3.refs_0_ = bf16[256,384]{1,0:T(8,128)(2,1)S(1)} collective-permute-done((bf16[256,384]{1,0:T(8,128)(2,1)S(1)}, bf16[256,384]{1,0:T(8,128)(2,1)S(1)}, u32[]{:S(2)}, u32[]{:S(2)}) %collective-permute-start.3) | collective-permute-done | bytes 196640 | tf_op jit(solution)/shard_map/ppermute | solution.py:510
  20.7 12.1 %collective-permute-done.4.refs_1_ = bf16[256,384]{1,0:T(8,128)(2,1)S(1)} collective-permute-done((bf16[256,384]{1,0:T(8,128)(2,1)S(1)}, bf16[256,384]{1,0:T(8,128)(2,1)S(1)}, u32[]{:S(2)}, u32[]{:S(2)}) %collective-permute-start.4) | collective-permute-done | bytes 196640 | tf_op jit(solution)/shard_map/ppermute | solution.py:510
  32.8 1.2 %shard_map.61.mine = f32[1024,128]{1,0:T(8,128)S(1)} custom-call(s32[6,8]{1,0:T(8,128)S(1)} %get-tuple-element.32.idx, bf16[2048,384]{1,0:T(8,128)(2,1)S(1)} %copy-done.1, bf16[256,384]{1,0:T(8,128)(2,1)S(1)} %collective-permute-done.3.refs_0_, bf16[256,384]{1,0:T(8,128)(2,1)S(1)} %collective-permute-done.4.refs_1_, ...), custom_call_target="tpu_custom_call" | custom-call | tf_op jit(solution)/shard_map/pallas_call | solution.py:28
  34.4 1.5 %collective-permute-done.6.other = f32[1024,128]{1,0:T(8,128)S(1)} collective-permute-done((f32[1024,128]{1,0:T(8,128)S(1)}, f32[1024,128]{1,0:T(8,128)S(1)}, u32[]{:S(2)}, u32[]{:S(2)}) %collective-permute-start.6) | collective-permute-done | bytes 524320 | tf_op jit(solution)/shard_map/ppermute | solution.py:510
  36.8 1.6 %collective-permute-start.8 = (f32[64,128]{1,0:T(8,128)S(1)}, f32[64,128]{1,0:T(8,128)S(1)}, u32[]{:S(2)}, u32[]{:S(2)}) collective-permute-start(f32[64,128]{1,0:T(8,128)S(1)} %get-tuple-element.37), channel_id=1, source_target_pairs={{0,2},{2,0},{1,3},{3,1},{4,6},{6,4},{5,7},{7,5},{8,10},{10,8},{9,1... | collective-permute-start | bytes 98312 | tf_op jit(solution)/shard_map/ppermute | solution.py:518
  39.2 1.6 %collective-permute-start.13 = (s16[272,128]{1,0:T(8,128)(2,1)S(1)}, s16[272,128]{1,0:T(8,128)(2,1)S(1)}, u32[]{:S(2)}, u32[]{:S(2)}) collective-permute-start(s16[272,128]{1,0:T(8,128)(2,1)S(1)} %get-tuple-element.48), channel_id=1, source_target_pairs={{0,8},{4,12},{8,0},{12,4},{1,9},{5,13},{9,1},{13,5},{2,10},{6,14},... | collective-permute-start | bytes 208904 | tf_op jit(solution)/shard_map/ppermute | solution.py:510
  40.7 2.8 %collective-permute-start.14 = (s16[272,128]{1,0:T(8,128)(2,1)S(1)}, s16[272,128]{1,0:T(8,128)(2,1)S(1)}, u32[]{:S(2)}, u32[]{:S(2)}) collective-permute-start(s16[272,128]{1,0:T(8,128)(2,1)S(1)} %get-tuple-element.49), channel_id=1, source_target_pairs={{0,12},{4,0},{8,4},{12,8},{1,13},{5,1},{9,5},{13,9},{2,14},{6,2},{... | collective-permute-start | bytes 208904 | tf_op jit(solution)/shard_map/ppermute | solution.py:510
  43.7 1.5 %collective-permute-start.10 = (f32[64,128]{1,0:T(8,128)S(1)}, f32[64,128]{1,0:T(8,128)S(1)}, u32[]{:S(2)}, u32[]{:S(2)}) collective-permute-start(f32[64,128]{1,0:T(8,128)S(1)} %add.11.refs_3_.refs_0_), channel_id=1, source_target_pairs={{0,8},{4,12},{8,0},{12,4},{1,9},{5,13},{9,1},{13,5},{2,10},{6,14},... | collective-permute-start | bytes 98312 | tf_op jit(solution)/shard_map/ppermute | solution.py:510
  45.1 2.6 %collective-permute-done.11.refs_6_.refs_3_ = f32[64,128]{1,0:T(8,128)S(1)} collective-permute-done((f32[64,128]{1,0:T(8,128)S(1)}, f32[64,128]{1,0:T(8,128)S(1)}, u32[]{:S(2)}, u32[]{:S(2)}) %collective-permute-start.11) | collective-permute-done | bytes 32800 | tf_op jit(solution)/shard_map/ppermute | solution.py:510
  47.7 3.2 %collective-permute-start.9 = (f32[64,128]{1,0:T(8,128)S(1)}, f32[64,128]{1,0:T(8,128)S(1)}, u32[]{:S(2)}, u32[]{:S(2)}) collective-permute-start(f32[64,128]{1,0:T(8,128)S(1)} %add.11.refs_3_.refs_0_), channel_id=1, source_target_pairs={{0,4},{4,8},{8,12},{12,0},{1,5},{5,9},{9,13},{13,1},{2,6},{6,10},{... | collective-permute-start | bytes 98312 | tf_op jit(solution)/shard_map/ppermute | solution.py:510
  50.9 2.5 %collective-permute-done.9.refs_4_.refs_1_ = f32[64,128]{1,0:T(8,128)S(1)} collective-permute-done((f32[64,128]{1,0:T(8,128)S(1)}, f32[64,128]{1,0:T(8,128)S(1)}, u32[]{:S(2)}, u32[]{:S(2)}) %collective-permute-start.9) | collective-permute-done | bytes 32800 | tf_op jit(solution)/shard_map/ppermute | solution.py:510
  55.4 1.1 %shard_map.67 = (s16[32,2176]{1,0:T(8,128)(2,1)S(1)}, f32[64,128]{1,0:T(8,128)S(1)}, f32[64,128]{1,0:T(8,128)S(1)}) custom-call(s32[3]{0:T(128)S(1)} %pad_add_fusion.me, s32[6,8]{1,0:T(8,128)S(1)} %get-tuple-element.32.idx, f32[64,128]{1,0:T(8,128)S(1)} %add.11.refs_3_.refs_0_, f32[64,128]{1,0:T(8,128)S(1)} %collective-permute-done.9.refs_4_.refs_1_, ...), custom_call_target="tpu_custom_call" | custom-call | tf_op jit(solution)/shard_map/pallas_call | solution.py:28
  57.1 5.2 %collective-permute-done.18.other = s16[32,2176]{1,0:T(8,128)(2,1)S(1)} collective-permute-done((s16[32,2176]{1,0:T(8,128)(2,1)S(1)}, s16[32,2176]{1,0:T(8,128)(2,1)S(1)}, u32[]{:S(2)}, u32[]{:S(2)}) %collective-permute-start.18) | collective-permute-done | bytes 139296 | tf_op jit(solution)/shard_map/ppermute | solution.py:518
  63.2 1.5 %collective-permute-start.20 = (s16[144,128]{1,0:T(8,128)(2,1)S(1)}, s16[144,128]{1,0:T(8,128)(2,1)S(1)}, u32[]{:S(2)}, u32[]{:S(2)}) collective-permute-start(s16[144,128]{1,0:T(8,128)(2,1)S(1)} %get-tuple-element.56), channel_id=1, source_target_pairs={{0,4},{4,8},{8,12},{12,0},{1,5},{5,9},{9,13},{13,1},{2,6},{6,10},{... | collective-permute-start | bytes 110600 | tf_op jit(solution)/shard_map/ppermute | solution.py:510
  64.7 2.5 %collective-permute-start.22 = (s16[144,128]{1,0:T(8,128)(2,1)S(1)}, s16[144,128]{1,0:T(8,128)(2,1)S(1)}, u32[]{:S(2)}, u32[]{:S(2)}) collective-permute-start(s16[144,128]{1,0:T(8,128)(2,1)S(1)} %get-tuple-element.58), channel_id=1, source_target_pairs={{0,12},{4,0},{8,4},{12,8},{1,13},{5,1},{9,5},{13,9},{2,14},{6,2},{... | collective-permute-start | bytes 110600 | tf_op jit(solution)/shard_map/ppermute | solution.py:510
  67.1 1.1 %shard_map.69.after = f32[32,128]{1,0:T(8,128)S(1)} custom-call(s32[3]{0:T(128)S(1)} %pad_add_fusion.me, f32[32,2048]{1,0:T(8,128)S(1)} %get-tuple-element.55.own.refs_0_, f32[32,2048]{1,0:T(8,128)S(1)} %collective-permute-done.19.other), custom_call_target="tpu_custom_call" | custom-call | tf_op jit(solution)/shard_map/pallas_call | solution.py:28
  68.2 1.2 %collective-permute-done.20.refs_10_ = s16[144,128]{1,0:T(8,128)(2,1)S(1)} collective-permute-done((s16[144,128]{1,0:T(8,128)(2,1)S(1)}, s16[144,128]{1,0:T(8,128)(2,1)S(1)}, u32[]{:S(2)}, u32[]{:S(2)}) %collective-permute-start.20) | collective-permute-done | bytes 36896 | tf_op jit(solution)/shard_map/ppermute | solution.py:510
  69.4 1.2 %collective-permute-done.21.refs_11_ = s16[144,128]{1,0:T(8,128)(2,1)S(1)} collective-permute-done((s16[144,128]{1,0:T(8,128)(2,1)S(1)}, s16[144,128]{1,0:T(8,128)(2,1)S(1)}, u32[]{:S(2)}, u32[]{:S(2)}) %collective-permute-start.21) | collective-permute-done | bytes 36896 | tf_op jit(solution)/shard_map/ppermute | solution.py:510
  72.2 1.3 %collective-permute-start.24 = (f32[32,128]{1,0:T(8,128)S(1)}, f32[32,128]{1,0:T(8,128)S(1)}, u32[]{:S(2)}, u32[]{:S(2)}) collective-permute-start(f32[32,128]{1,0:T(8,128)S(1)} %shard_map.69.after), channel_id=1, source_target_pairs={{0,4},{4,0},{8,12},{12,8},{1,5},{5,1},{9,13},{13,9},{2,6},{6,2},{1... | collective-permute-start | bytes 49160 | tf_op jit(solution)/shard_map/ppermute | solution.py:518
  73.4 2.5 %collective-permute-done.24 = f32[32,128]{1,0:T(8,128)S(1)} collective-permute-done((f32[32,128]{1,0:T(8,128)S(1)}, f32[32,128]{1,0:T(8,128)S(1)}, u32[]{:S(2)}, u32[]{:S(2)}) %collective-permute-start.24) | collective-permute-done | bytes 16416 | tf_op jit(solution)/shard_map/ppermute | solution.py:518
  76.9 3.6 %collective-permute-done.25.after.refs_1_ = f32[32,128]{1,0:T(8,128)S(1)} collective-permute-done((f32[32,128]{1,0:T(8,128)S(1)}, f32[32,128]{1,0:T(8,128)S(1)}, u32[]{:S(2)}, u32[]{:S(2)}) %collective-permute-start.25) | collective-permute-done | bytes 16416 | tf_op jit(solution)/shard_map/ppermute | solution.py:518
  81.2 1.9 %shard_map.72.factor = f32[64,64]{1,0:T(8,128)S(1)} custom-call(f32[32,2048]{1,0:T(8,128)S(1)} %shard_map.71.after.own, f32[32,128]{1,0:T(8,128)S(1)} %add.12.refs_0_, f32[32,128]{1,0:T(8,128)S(1)} %collective-permute-done.25.after.refs_1_), custom_call_target="tpu_custom_call" | custom-call | tf_op jit(solution)/shard_map/pallas_call | solution.py:28
  83.1 1.5 %shard_map.73 = (bf16[128,2048]{1,0:T(8,128)(2,1)S(1)}, f32[32,128]{1,0:T(8,128)S(1)}) custom-call(s32[3]{0:T(128)S(1)} %pad_add_fusion.me, f32[64,64]{1,0:T(8,128)S(1)} %shard_map.72.factor, f32[32,2048]{1,0:T(8,128)S(1)} %shard_map.71.after.own, f32[32,2048]{1,0:T(8,128)S(1)} %collective-permute-done.26.other), custom_call_target="tpu_custom_call" | custom-call | tf_op jit(solution)/shard_map/pallas_call | solution.py:28
  84.6 2.3 %collective-permute-start.29 = (f32[32,128]{1,0:T(8,128)S(1)}, f32[32,128]{1,0:T(8,128)S(1)}, u32[]{:S(2)}, u32[]{:S(2)}) collective-permute-start(f32[32,128]{1,0:T(8,128)S(1)} %get-tuple-element.60.refs_0_), channel_id=1, source_target_pairs={{0,12},{4,0},{8,4},{12,8},{1,13},{5,1},{9,5},{13,9},{2,14},{6,2},{... | collective-permute-start | bytes 49160 | tf_op jit(solution)/shard_map/ppermute | solution.py:510
  88.4 3.2 %collective-permute-done.28.refs_2_ = f32[32,128]{1,0:T(8,128)S(1)} collective-permute-done((f32[32,128]{1,0:T(8,128)S(1)}, f32[32,128]{1,0:T(8,128)S(1)}, u32[]{:S(2)}, u32[]{:S(2)}) %collective-permute-start.28) | collective-permute-done | bytes 16416 | tf_op jit(solution)/shard_map/ppermute | solution.py:510
  91.6 1.3 %collective-permute-done.27.refs_1_ = f32[32,128]{1,0:T(8,128)S(1)} collective-permute-done((f32[32,128]{1,0:T(8,128)S(1)}, f32[32,128]{1,0:T(8,128)S(1)}, u32[]{:S(2)}, u32[]{:S(2)}) %collective-permute-start.27) | collective-permute-done | bytes 16416 | tf_op jit(solution)/shard_map/ppermute | solution.py:510
  92.9 3.4 %shard_map.74 = f32[32,2048]{1,0:T(8,128)} custom-call(s32[3]{0:T(128)S(1)} %pad_add_fusion.me, bf16[128,2048]{1,0:T(8,128)(2,1)S(1)} %get-tuple-element.59.mapped, f32[32,128]{1,0:T(8,128)S(1)} %get-tuple-element.60.refs_0_, f32[32,128]{1,0:T(8,128)S(1)} %collective-permute-done.27.refs_1_, f32[32,128]{1,0:T(8,128)S(1)} %collective-permute-done.28.refs_2_, ...), custom_call_target="tpu_custom_call" | custom-call | tf_op jit(solution)/shard_map/pallas_call | solution.py:28
  (55 shorter events, 15.9 us)
Async XLA Ops:
  2.0 8.6 %collective-permute-start.2 = (s32[3,8]{1,0:T(4,128)S(1)}, s32[3,8]{1,0:T(4,128)S(1)}, u32[]{:S(2)}, u32[]{:S(2)}) collective-permute-start(s32[3,8]{1,0:T(4,128)S(1)} %concatenate.3.refs_0_), channel_id=1, source_target_pairs={{0,12},{4,0},{8,4},{12,8},{1,13},{5,1},{9,5},{13,9},{2,14},{6,2},{... | collective-permute-start | bytes 296 | tf_op jit(solution)/shard_map/ppermute | solution.py:510
  7.0 4.5 %collective-permute-start.1 = (s32[3,8]{1,0:T(4,128)S(1)}, s32[3,8]{1,0:T(4,128)S(1)}, u32[]{:S(2)}, u32[]{:S(2)}) collective-permute-start(s32[3,8]{1,0:T(4,128)S(1)} %concatenate.3.refs_0_), channel_id=1, source_target_pairs={{0,8},{4,12},{8,0},{12,4},{1,9},{5,13},{9,1},{13,5},{2,10},{6,14},... | collective-permute-start | bytes 296 | tf_op jit(solution)/shard_map/ppermute | solution.py:510
  7.0 5.4 %collective-permute-start = (s32[3,8]{1,0:T(4,128)S(1)}, s32[3,8]{1,0:T(4,128)S(1)}, u32[]{:S(2)}, u32[]{:S(2)}) collective-permute-start(s32[3,8]{1,0:T(4,128)S(1)} %concatenate.3.refs_0_), channel_id=1, source_target_pairs={{0,4},{4,8},{8,12},{12,0},{1,5},{5,9},{9,13},{13,1},{2,6},{6,10},{... | collective-permute-start | bytes 296 | tf_op jit(solution)/shard_map/ppermute | solution.py:510
  10.5 22.3 %copy-start.1 = (bf16[2048,384]{1,0:T(8,128)(2,1)S(1)}, bf16[2048,384]{1,0:T(8,128)(2,1)}, u32[]{:S(2)}) copy-start(bf16[2048,384]{1,0:T(8,128)(2,1)} %emb.3) | copy-start | bytes 4718596
  14.2 19.8 %copy-start.2 = (f32[2048,32]{0,1:T(8,128)S(1)}, f32[2048,32]{0,1:T(8,128)}, u32[]{:S(2)}) copy-start(f32[2048,32]{0,1:T(8,128)} %param.5) | copy-start | bytes 786436
  14.2 6.4 %collective-permute-start.3 = (bf16[256,384]{1,0:T(8,128)(2,1)S(1)}, bf16[256,384]{1,0:T(8,128)(2,1)S(1)}, u32[]{:S(2)}, u32[]{:S(2)}) collective-permute-start(bf16[256,384]{1,0:T(8,128)(2,1)S(1)} %get-tuple-element.33), channel_id=1, source_target_pairs={{0,12},{4,0},{8,4},{12,8},{1,13},{5,1},{9,5},{13,9},{2,14},{6,2},{... | collective-permute-start | bytes 589832 | tf_op jit(solution)/shard_map/ppermute | solution.py:510
  15.3 17.5 %collective-permute-start.4 = (bf16[256,384]{1,0:T(8,128)(2,1)S(1)}, bf16[256,384]{1,0:T(8,128)(2,1)S(1)}, u32[]{:S(2)}, u32[]{:S(2)}) collective-permute-start(bf16[256,384]{1,0:T(8,128)(2,1)S(1)} %get-tuple-element.34), channel_id=1, source_target_pairs={{0,8},{4,12},{8,0},{12,4},{1,9},{5,13},{9,1},{13,5},{2,10},{6,14},... | collective-permute-start | bytes 589832 | tf_op jit(solution)/shard_map/ppermute | solution.py:510
  16.4 16.4 %collective-permute-start.5 = (bf16[256,384]{1,0:T(8,128)(2,1)S(1)}, bf16[256,384]{1,0:T(8,128)(2,1)S(1)}, u32[]{:S(2)}, u32[]{:S(2)}) collective-permute-start(bf16[256,384]{1,0:T(8,128)(2,1)S(1)} %get-tuple-element.35), channel_id=1, source_target_pairs={{0,4},{4,8},{8,12},{12,0},{1,5},{5,9},{9,13},{13,1},{2,6},{6,10},{... | collective-permute-start | bytes 589832 | tf_op jit(solution)/shard_map/ppermute | solution.py:510
  17.4 16.8 %collective-permute-start.7 = (f32[1024,128]{1,0:T(8,128)S(1)}, f32[1024,128]{1,0:T(8,128)S(1)}, u32[]{:S(2)}, u32[]{:S(2)}) collective-permute-start(f32[1024,128]{1,0:T(8,128)S(1)} %shard_map.59.refs_5_.mine), channel_id=1, source_target_pairs={{0,1},{1,0},{2,3},{3,2},{4,5},{5,4},{6,7},{7,6},{8,9},{9,8},{10,11... | collective-permute-start | bytes 1572872 | tf_op jit(solution)/shard_map/ppermute | solution.py:510
  34.0 2.0 %collective-permute-start.6 = (f32[1024,128]{1,0:T(8,128)S(1)}, f32[1024,128]{1,0:T(8,128)S(1)}, u32[]{:S(2)}, u32[]{:S(2)}) collective-permute-start(f32[1024,128]{1,0:T(8,128)S(1)} %shard_map.61.mine), channel_id=1, source_target_pairs={{0,1},{1,0},{2,3},{3,2},{4,5},{5,4},{6,7},{7,6},{8,9},{9,8},{10,11... | collective-permute-start | bytes 1572872 | tf_op jit(solution)/shard_map/ppermute | solution.py:510
  36.8 6.7 %collective-permute-start.8 = (f32[64,128]{1,0:T(8,128)S(1)}, f32[64,128]{1,0:T(8,128)S(1)}, u32[]{:S(2)}, u32[]{:S(2)}) collective-permute-start(f32[64,128]{1,0:T(8,128)S(1)} %get-tuple-element.37), channel_id=1, source_target_pairs={{0,2},{2,0},{1,3},{3,1},{4,6},{6,4},{5,7},{7,5},{8,10},{10,8},{9,1... | collective-permute-start | bytes 98312 | tf_op jit(solution)/shard_map/ppermute | solution.py:518
  39.1 14.4 %collective-permute-start.12 = (s16[272,128]{1,0:T(8,128)(2,1)S(1)}, s16[272,128]{1,0:T(8,128)(2,1)S(1)}, u32[]{:S(2)}, u32[]{:S(2)}) collective-permute-start(s16[272,128]{1,0:T(8,128)(2,1)S(1)} %get-tuple-element.47), channel_id=1, source_target_pairs={{0,4},{4,8},{8,12},{12,0},{1,5},{5,9},{9,13},{13,1},{2,6},{6,10},{... | collective-permute-start | bytes 208904 | tf_op jit(solution)/shard_map/ppermute | solution.py:510
  39.2 14.3 %collective-permute-start.13 = (s16[272,128]{1,0:T(8,128)(2,1)S(1)}, s16[272,128]{1,0:T(8,128)(2,1)S(1)}, u32[]{:S(2)}, u32[]{:S(2)}) collective-permute-start(s16[272,128]{1,0:T(8,128)(2,1)S(1)} %get-tuple-element.48), channel_id=1, source_target_pairs={{0,8},{4,12},{8,0},{12,4},{1,9},{5,13},{9,1},{13,5},{2,10},{6,14},... | collective-permute-start | bytes 208904 | tf_op jit(solution)/shard_map/ppermute | solution.py:510
  40.7 12.7 %collective-permute-start.14 = (s16[272,128]{1,0:T(8,128)(2,1)S(1)}, s16[272,128]{1,0:T(8,128)(2,1)S(1)}, u32[]{:S(2)}, u32[]{:S(2)}) collective-permute-start(s16[272,128]{1,0:T(8,128)(2,1)S(1)} %get-tuple-element.49), channel_id=1, source_target_pairs={{0,12},{4,0},{8,4},{12,8},{1,13},{5,1},{9,5},{13,9},{2,14},{6,2},{... | collective-permute-start | bytes 208904 | tf_op jit(solution)/shard_map/ppermute | solution.py:510
  43.6 4.2 %collective-permute-start.11 = (f32[64,128]{1,0:T(8,128)S(1)}, f32[64,128]{1,0:T(8,128)S(1)}, u32[]{:S(2)}, u32[]{:S(2)}) collective-permute-start(f32[64,128]{1,0:T(8,128)S(1)} %add.11.refs_3_.refs_0_), channel_id=1, source_target_pairs={{0,12},{4,0},{8,4},{12,8},{1,13},{5,1},{9,5},{13,9},{2,14},{6,2},{... | collective-permute-start | bytes 98312 | tf_op jit(solution)/shard_map/ppermute | solution.py:510
  43.7 7.3 %collective-permute-start.10 = (f32[64,128]{1,0:T(8,128)S(1)}, f32[64,128]{1,0:T(8,128)S(1)}, u32[]{:S(2)}, u32[]{:S(2)}) collective-permute-start(f32[64,128]{1,0:T(8,128)S(1)} %add.11.refs_3_.refs_0_), channel_id=1, source_target_pairs={{0,8},{4,12},{8,0},{12,4},{1,9},{5,13},{9,1},{13,5},{2,10},{6,14},... | collective-permute-start | bytes 98312 | tf_op jit(solution)/shard_map/ppermute | solution.py:510
  47.7 5.7 %collective-permute-start.9 = (f32[64,128]{1,0:T(8,128)S(1)}, f32[64,128]{1,0:T(8,128)S(1)}, u32[]{:S(2)}, u32[]{:S(2)}) collective-permute-start(f32[64,128]{1,0:T(8,128)S(1)} %add.11.refs_3_.refs_0_), channel_id=1, source_target_pairs={{0,4},{4,8},{8,12},{12,0},{1,5},{5,9},{9,13},{13,1},{2,6},{6,10},{... | collective-permute-start | bytes 98312 | tf_op jit(solution)/shard_map/ppermute | solution.py:510
  53.5 1.3 %collective-permute-start.15 = (bf16[1,256,128]{2,1,0:T(8,128)(2,1)S(1)}, bf16[1,256,128]{2,1,0:T(8,128)(2,1)S(1)}, u32[]{:S(2)}, u32[]{:S(2)}) collective-permute-start(bf16[1,256,128]{2,1,0:T(8,128)(2,1)S(1)} %get-tuple-element.50.refs_8_.refs_4_), channel_id=1, source_target_pairs={{0,1},{1,0},{2,3},{3,2},{4,5},{5,4},{6,7},{7,6},{8,9},{9,8},{10,11... | collective-permute-start | bytes 196616 | tf_op jit(solution)/shard_map/ppermute | solution.py:510
  53.6 1.4 %collective-permute-start.16 = (bf16[1,256,128]{2,1,0:T(8,128)(2,1)S(1)}, bf16[1,256,128]{2,1,0:T(8,128)(2,1)S(1)}, u32[]{:S(2)}, u32[]{:S(2)}) collective-permute-start(bf16[1,256,128]{2,1,0:T(8,128)(2,1)S(1)} %get-tuple-element.51.refs_9_.refs_5_), channel_id=1, source_target_pairs={{0,1},{1,0},{2,3},{3,2},{4,5},{5,4},{6,7},{7,6},{8,9},{9,8},{10,11... | collective-permute-start | bytes 196616 | tf_op jit(solution)/shard_map/ppermute | solution.py:510
  54.1 1.3 %collective-permute-start.17 = (bf16[1,256,128]{2,1,0:T(8,128)(2,1)S(1)}, bf16[1,256,128]{2,1,0:T(8,128)(2,1)S(1)}, u32[]{:S(2)}, u32[]{:S(2)}) collective-permute-start(bf16[1,256,128]{2,1,0:T(8,128)(2,1)S(1)} %get-tuple-element.52.refs_10_.refs_6_), channel_id=1, source_target_pairs={{0,1},{1,0},{2,3},{3,2},{4,5},{5,4},{6,7},{7,6},{8,9},{9,8},{10,11... | collective-permute-start | bytes 196616 | tf_op jit(solution)/shard_map/ppermute | solution.py:510
  56.5 5.8 %collective-permute-start.18 = (s16[32,2176]{1,0:T(8,128)(2,1)S(1)}, s16[32,2176]{1,0:T(8,128)(2,1)S(1)}, u32[]{:S(2)}, u32[]{:S(2)}) collective-permute-start(s16[32,2176]{1,0:T(8,128)(2,1)S(1)} %get-tuple-element.54.mine), channel_id=1, source_target_pairs={{0,2},{2,0},{1,3},{3,1},{4,6},{6,4},{5,7},{7,5},{8,10},{10,8},{9,1... | collective-permute-start | bytes 417800 | tf_op jit(solution)/shard_map/ppermute | solution.py:518
  63.1 4.0 %collective-permute-start.19 = (f32[32,2048]{1,0:T(8,128)S(1)}, f32[32,2048]{1,0:T(8,128)S(1)}, u32[]{:S(2)}, u32[]{:S(2)}) collective-permute-start(f32[32,2048]{1,0:T(8,128)S(1)} %get-tuple-element.55.own.refs_0_), channel_id=1, source_target_pairs={{0,1},{1,0},{2,3},{3,2},{4,5},{5,4},{6,7},{7,6},{8,9},{9,8},{10,11... | collective-permute-start | bytes 786440 | tf_op jit(solution)/shard_map/ppermute | solution.py:510
  63.2 6.2 %collective-permute-start.20 = (s16[144,128]{1,0:T(8,128)(2,1)S(1)}, s16[144,128]{1,0:T(8,128)(2,1)S(1)}, u32[]{:S(2)}, u32[]{:S(2)}) collective-permute-start(s16[144,128]{1,0:T(8,128)(2,1)S(1)} %get-tuple-element.56), channel_id=1, source_target_pairs={{0,4},{4,8},{8,12},{12,0},{1,5},{5,9},{9,13},{13,1},{2,6},{6,10},{... | collective-permute-start | bytes 110600 | tf_op jit(solution)/shard_map/ppermute | solution.py:510
  64.7 5.9 %collective-permute-start.21 = (s16[144,128]{1,0:T(8,128)(2,1)S(1)}, s16[144,128]{1,0:T(8,128)(2,1)S(1)}, u32[]{:S(2)}, u32[]{:S(2)}) collective-permute-start(s16[144,128]{1,0:T(8,128)(2,1)S(1)} %get-tuple-element.57), channel_id=1, source_target_pairs={{0,8},{4,12},{8,0},{12,4},{1,9},{5,13},{9,1},{13,5},{2,10},{6,14},... | collective-permute-start | bytes 110600 | tf_op jit(solution)/shard_map/ppermute | solution.py:510
  64.7 5.9 %collective-permute-start.22 = (s16[144,128]{1,0:T(8,128)(2,1)S(1)}, s16[144,128]{1,0:T(8,128)(2,1)S(1)}, u32[]{:S(2)}, u32[]{:S(2)}) collective-permute-start(s16[144,128]{1,0:T(8,128)(2,1)S(1)} %get-tuple-element.58), channel_id=1, source_target_pairs={{0,12},{4,0},{8,4},{12,8},{1,13},{5,1},{9,5},{13,9},{2,14},{6,2},{... | collective-permute-start | bytes 110600 | tf_op jit(solution)/shard_map/ppermute | solution.py:510
  71.6 9.0 %collective-permute-start.23 = (f32[32,2048]{1,0:T(8,128)S(1)}, f32[32,2048]{1,0:T(8,128)S(1)}, u32[]{:S(2)}, u32[]{:S(2)}) collective-permute-start(f32[32,2048]{1,0:T(8,128)S(1)} %shard_map.70.mine), channel_id=1, source_target_pairs={{0,2},{2,0},{1,3},{3,1},{4,6},{6,4},{5,7},{7,5},{8,10},{10,8},{9,1... | collective-permute-start | bytes 786440 | tf_op jit(solution)/shard_map/ppermute | solution.py:518
  72.2 3.7 %collective-permute-start.24 = (f32[32,128]{1,0:T(8,128)S(1)}, f32[32,128]{1,0:T(8,128)S(1)}, u32[]{:S(2)}, u32[]{:S(2)}) collective-permute-start(f32[32,128]{1,0:T(8,128)S(1)} %shard_map.69.after), channel_id=1, source_target_pairs={{0,4},{4,0},{8,12},{12,8},{1,5},{5,1},{9,13},{13,9},{2,6},{6,2},{1... | collective-permute-start | bytes 49160 | tf_op jit(solution)/shard_map/ppermute | solution.py:518
  75.9 4.6 %collective-permute-start.25 = (f32[32,128]{1,0:T(8,128)S(1)}, f32[32,128]{1,0:T(8,128)S(1)}, u32[]{:S(2)}, u32[]{:S(2)}) collective-permute-start(f32[32,128]{1,0:T(8,128)S(1)} %add.12.refs_0_), channel_id=1, source_target_pairs={{0,8},{4,12},{8,0},{12,4},{1,9},{5,13},{9,1},{13,5},{2,10},{6,14},... | collective-permute-start | bytes 49160 | tf_op jit(solution)/shard_map/ppermute | solution.py:518
  81.1 2.0 %collective-permute-start.26 = (f32[32,2048]{1,0:T(8,128)S(1)}, f32[32,2048]{1,0:T(8,128)S(1)}, u32[]{:S(2)}, u32[]{:S(2)}) collective-permute-start(f32[32,2048]{1,0:T(8,128)S(1)} %shard_map.71.after.own), channel_id=1, source_target_pairs={{0,1},{1,0},{2,3},{3,2},{4,5},{5,4},{6,7},{7,6},{8,9},{9,8},{10,11... | collective-permute-start | bytes 786440 | tf_op jit(solution)/shard_map/ppermute | solution.py:510
  84.6 3.8 %collective-permute-start.29 = (f32[32,128]{1,0:T(8,128)S(1)}, f32[32,128]{1,0:T(8,128)S(1)}, u32[]{:S(2)}, u32[]{:S(2)}) collective-permute-start(f32[32,128]{1,0:T(8,128)S(1)} %get-tuple-element.60.refs_0_), channel_id=1, source_target_pairs={{0,12},{4,0},{8,4},{12,8},{1,13},{5,1},{9,5},{13,9},{2,14},{6,2},{... | collective-permute-start | bytes 49160 | tf_op jit(solution)/shard_map/ppermute | solution.py:510
  87.0 4.6 %collective-permute-start.28 = (f32[32,128]{1,0:T(8,128)S(1)}, f32[32,128]{1,0:T(8,128)S(1)}, u32[]{:S(2)}, u32[]{:S(2)}) collective-permute-start(f32[32,128]{1,0:T(8,128)S(1)} %get-tuple-element.60.refs_0_), channel_id=1, source_target_pairs={{0,8},{4,12},{8,0},{12,4},{1,9},{5,13},{9,1},{13,5},{2,10},{6,14},... | collective-permute-start | bytes 49160 | tf_op jit(solution)/shard_map/ppermute | solution.py:510
  87.4 5.5 %collective-permute-start.27 = (f32[32,128]{1,0:T(8,128)S(1)}, f32[32,128]{1,0:T(8,128)S(1)}, u32[]{:S(2)}, u32[]{:S(2)}) collective-permute-start(f32[32,128]{1,0:T(8,128)S(1)} %get-tuple-element.60.refs_0_), channel_id=1, source_target_pairs={{0,4},{4,8},{8,12},{12,0},{1,5},{5,9},{9,13},{13,1},{2,6},{6,10},{... | collective-permute-start | bytes 49160 | tf_op jit(solution)/shard_map/ppermute | solution.py:510
  (1 other events, 1.4 us)

commit v10 on v9

--- a/solution.py
+++ b/solution.py
@@ -22,7 +22,7 @@
 NT = (((1,), (1,)), ((), ()))
 
 
-def call(body, outs, args, smem_in=(), smem_out=(), any_in=(), scratch=(), cost=0):
+def call(body, outs, args, smem_in=(), smem_out=(), any_in=(), scratch=()):
     single = not isinstance(outs, (list, tuple))
     shapes = [outs] if single else list(outs)
     result = pl.pallas_call(
@@ -33,11 +33,6 @@
         ],
         out_specs=[SMEM if i in smem_out else VMEM for i in range(len(shapes))],
         scratch_shapes=list(scratch),
-        cost_estimate=pl.CostEstimate(
-            flops=cost * 10**9, bytes_accessed=cost * 10**6, transcendentals=0
-        )
-        if cost
-        else None,
         compiler_params=pltpu.CompilerParams(vmem_limit_bytes=48 * 2**20),
     )(*args)
     return result[0] if single else result
@@ -275,7 +270,7 @@
         sums[i : i + 1, :] = jnp.sum(tile, axis=0, keepdims=True)
 
 
-def pair_tile_body(dims, me, idx, mine, other, self_sums, near_tiles, home_tiles, table, *chosen):
+def pair_tile_body(dims, me, idx, mine, other, self_sums, codes, powers, parts, near_tiles, home_tiles, table, *sends):
     row_count, capacity, per_core, blocks_here, tile_count = dims
     row, tile_index, core = me[0], me[1], me[2]
     table[...] = jnp.zeros(table.shape, F32)
@@ -301,9 +296,14 @@
                 home_tiles[j] = pack(tile)
             tiles.append(tile)
         if k > 0:
+            lines = ([], [])
             for inner in range(per_core):
-                part = slice(inner * BLOCK, (inner + 1) * BLOCK)
-                chosen[k - 1][part, :] = jnp.where(core == 0, tiles[inner], tiles[per_core + inner])
+                at = slice(inner * BLOCK, (inner + 1) * BLOCK)
+                steps, power, part = encode(jnp.where(core == 0, tiles[inner], tiles[per_core + inner]))
+                sends[k - 1][at, :] = steps
+                lines[0].append(power)
+                lines[1].append(part)
+            pick_columns(idx, k, row_count, capacity, codes, powers, parts, sends[k - 1], per_core * BLOCK, lines)
 
 
 def encode_blocks(values, codes, powers, parts):
@@ -317,20 +317,6 @@
 
 def start_body(values, codes, powers, parts):
     encode_blocks(values, codes, powers, parts)
-
-
-def message_body(dims, idx, codes, powers, parts, *refs):
-    row_count, capacity, per_core, blocks_here, tile_count = dims
-    chosen, sends = refs[: row_count - 1], refs[row_count - 1 :]
-    for k in range(1, row_count):
-        lines = ([], [])
-        for inner in range(per_core):
-            at = slice(inner * BLOCK, (inner + 1) * BLOCK)
-            steps, power, part = encode(chosen[k - 1][at, :])
-            sends[k - 1][at, :] = steps
-            lines[0].append(power)
-            lines[1].append(part)
-        pick_columns(idx, k, row_count, capacity, codes, powers, parts, sends[k - 1], per_core * BLOCK, lines)
 
 
 def split_body(row_count, per_core, *refs):
@@ -408,64 +394,72 @@
 
 def first_apply_body(dims, coded, me, idx, *refs):
     row_count, per_core = dims[0], dims[2]
-    terms, refs = refs[:row_count], refs[row_count:]
+    terms, refs = refs[:2], refs[2:]
     own, near_tiles, home_tiles, self_tiles = refs[:4]
     sent, shared = refs[4 : 3 + row_count], refs[3 + row_count : 2 + 2 * row_count]
     messages = refs[2 + 2 * row_count : -4]
     out, degree, inverse, total_out = refs[-4:]
-    total = functools.reduce(lambda total, term: total + term[...], terms[1:], terms[0][...])
+    total = terms[0][...] + terms[1][...]
     degree[...] = total
     inverse[...] = 1.0 / jnp.sqrt(total)
     apply_tiles(
         dims, me, idx, inverse, own, messages, per_core * BLOCK, near_tiles, home_tiles, sent, shared, self_tiles, total_out
     )
+    put_sum(coded, total_out, out)
+
+
+def put_sum(coded, total, out):
     if not coded:
-        out[...] = total_out[...]
+        out[...] = total[...]
         return
     lines = ([], [])
-    blocks_here = dims[3]
+    blocks_here = total.shape[1] // BLOCK
     for b in range(blocks_here):
         at = slice(b * BLOCK, (b + 1) * BLOCK)
-        steps, power, part = encode(total_out[:, at])
+        steps, power, part = encode(total[:, at])
         out[:, at] = steps
         lines[0].append(power)
         lines[1].append(part)
     out[:, blocks_here * BLOCK :] = as_rows(*lines, out.shape[0])
 
 
-def second_apply_body(dims, me, idx, inverse, after, *refs):
-    row_count = dims[0]
-    own, near_tiles, home_tiles, self_tiles = refs[:4]
-    sent, shared = refs[4 : 3 + row_count], refs[3 + row_count : 2 + 2 * row_count]
-    received, out = refs[2 + 2 * row_count : -1], refs[-1]
-    apply_tiles(dims, me, idx, inverse, own, received, 0, near_tiles, home_tiles, sent, shared, self_tiles, out)
-
-
-def mapped_body(dims, coded, me, idx, inverse, mine, other, out, *refs):
-    row_count, capacity, per_core, blocks_here, tile_count = dims
-    sends, (codes, powers, parts) = refs[:-3], refs[-3:]
+def take_sum(coded, me, blocks_here, inverse, mine, other, out):
     if coded:
         tail = blocks_here * BLOCK
         my_scales, other_scales = scale_rows(mine[:, tail:]), scale_rows(other[:, tail:])
     for b in range(blocks_here):
-        part = slice(b * BLOCK, (b + 1) * BLOCK)
+        at = slice(b * BLOCK, (b + 1) * BLOCK)
         row = inverse[pl.ds(me[0] * blocks_here + b, 1), :]
         if coded:
             line = slice(b, b + 1)
-            value = decode(mine[:, part], my_scales[line]) + decode(other[:, part], other_scales[line])
+            value = decode(mine[:, at], my_scales[line]) + decode(other[:, at], other_scales[line])
         else:
-            value = mine[:, part] + other[:, part]
-        out[:, part] = value * row
+            value = mine[:, at] + other[:, at]
+        out[:, at] = value * row
+
+
+def second_apply_body(dims, coded, me, idx, inverse, after, *refs):
+    row_count = dims[0]
+    own, near_tiles, home_tiles, self_tiles = refs[:4]
+    sent, shared = refs[4 : 3 + row_count], refs[3 + row_count : 2 + 2 * row_count]
+    received, (out, total_out) = refs[2 + 2 * row_count : -2], refs[-2:]
+    apply_tiles(
+        dims, me, idx, inverse, own, received, 0, near_tiles, home_tiles, sent, shared, self_tiles, total_out
+    )
+    put_sum(coded, total_out, out)
+
+
+def mapped_body(dims, coded, me, idx, inverse, mine, other, out, *refs):
+    row_count, capacity, per_core, blocks_here, tile_count = dims
+    sends, (codes, powers, parts) = refs[:-3], refs[-3:]
+    take_sum(coded, me, blocks_here, inverse, mine, other, out)
     encode_blocks(out, codes, powers, parts)
     for k in range(1, row_count):
         pick_columns(idx, k, row_count, capacity, codes, powers, parts, sends[k - 1], 0, ([], []))
 
 
-def last_mapped_body(blocks_here, me, inverse, mine, other, after, out):
-    for b in range(blocks_here):
-        part = slice(b * BLOCK, (b + 1) * BLOCK)
-        row = inverse[pl.ds(me[0] * blocks_here + b, 1), :]
-        out[:, part] = (mine[:, part] + other[:, part]) * row
+def last_mapped_body(blocks_here, coded, me, inverse, mine, other, after, out):
+    take_sum(coded, me, blocks_here, inverse, mine, other, out)
 
 
 def folded(square):
@@ -592,37 +586,31 @@
     tiles = call(
         functools.partial(pair_tile_body, dims),
         [sds((slots, 2 * BLOCK, BLOCK), BF16), sds((capacity, 2 * BLOCK, BLOCK), BF16), table]
-        + [sds((per_core * BLOCK, BLOCK), F32) for _ in others],
-        [me, idx, pair_part, pair_other, self_sums],
+        + [sds((per_core * BLOCK + picked + CODE_ROWS, BLOCK), jnp.int16) for _ in others],
+        [me, idx, pair_part, pair_other, self_sums, *start_codes],
         smem_in=(0, 1),
     )
-    near_tiles, home_tiles, degrees, chosen = tiles[0], tiles[1], tiles[2], tiles[3:]
-    mine, other = pair_sum(degrees, ("tiles",))
-    degree_terms = row_terms(mine + other, row_count)
-    sends = call(
-        functools.partial(message_body, dims),
-        [sds((per_core * BLOCK + picked + CODE_ROWS, BLOCK), jnp.int16) for _ in others],
-        [idx, *start_codes, *chosen],
-        smem_in=(0,),
-        cost=3,
-    )
+    near_tiles, home_tiles, degrees, sends = tiles[0], tiles[1], tiles[2], tiles[3:]
+    degrees = functools.reduce(jnp.add, row_terms(degrees, row_count))
+    degree_terms = pair_sum(degrees, ("tiles",))
     messages = [shift_by(sends[k - 1], "rows", row_count, k) for k in others]
     sent = call(
         functools.partial(split_body, row_count, per_core),
         [sds((per_core, 2 * BLOCK, BLOCK), BF16) for _ in others],
-        [*messages, *degree_terms],
-        any_in=range(row_count - 1, 2 * row_count - 1),
+        [*messages, degree_terms[1]],
+        any_in=(row_count - 1,),
     )
     shared = [shift_by(tile, "cols", core_count, 1) for tile in sent]
 
     tile_args = [near_tiles, home_tiles, self_tiles, *sent, *shared]
     block_shape = sds((own_cols, rows_here), F32)
+    sum_shape = sds((own_cols, rows_here + BLOCK), jnp.int16) if coded else block_shape
     square = sds((2 * own_cols, 2 * own_cols), F32)
     folded_square = sds((own_cols, 4 * own_cols), F32)
 
     part, degree, inverse = call(
         functools.partial(first_apply_body, dims, coded),
-        [sds((own_cols, rows_here + BLOCK), jnp.int16) if coded else block_shape, table, table],
+        [sum_shape, table, table],
         [me, idx, *degree_terms, values, *tile_args, *messages],
         smem_in=(0, 1),
         scratch=[pltpu.VMEM((own_cols, rows_here), F32)],
@@ -640,17 +628,21 @@
 
     mapped_other = shift_by(mapped, "cols", core_count, 1)
     first_gram = call(gram_body, folded_square, [me, mapped, mapped_other], smem_in=(0,))
+    steps = (row_count - 1).bit_length()
+    for bit in range(steps - 1):
+        first_gram = first_gram + pair_step(first_gram, "rows", 1 << bit)
     part = call(
-        functools.partial(second_apply_body, dims),
-        block_shape,
+        functools.partial(second_apply_body, dims, coded),
+        sum_shape,
         [me, idx, inverse, first_gram, mapped, *tile_args, *received],
         smem_in=(0, 1),
         any_in=(3,),
-    )
-    gram_terms = pair_sum(first_gram, ("rows",))
+        scratch=[pltpu.VMEM((own_cols, rows_here), F32)],
+    )
+    gram_terms = (first_gram, pair_step(first_gram, "rows", 1 << (steps - 1)))
     mine, other = pair_sum(part, ("tiles",))
     second = call(
-        functools.partial(last_mapped_body, blocks_here),
+        functools.partial(last_mapped_body, blocks_here, coded),
         block_shape,
         [me, inverse, mine, other, gram_terms[1]],
         smem_in=(0,),

time: 96.5 us -> 90.9 us (0.942)
  waiting for transfers between devices: 43.3 us -> 36.6 us
  starting transfers between devices: 31.3 us -> 33 us
    ppermute x25, waiting for transfers between devices: 32.1 us -> 23.9 us  [shift_by(): lax.ppermute(value, axes, [(i, (i + shift) % size) for i in range(size)])]
    ppermute x5, starting transfers between devices: 5.04 us -> 7 us  [pair_step(): lax.ppermute(value, name, [(i, i ^ flip) for i in range(lax.axis_size(nam...]
    ppermute x5, waiting for transfers between devices: 11.3 us -> 12.7 us  [pair_step(): lax.ppermute(value, name, [(i, i ^ flip) for i in range(lax.axis_size(nam...]
    pallas_call x16 -> x15, Pallas kernels: 17.4 us -> 16.9 us  [call(): pl.pallas_call(body, out_shape=shapes, in_specs=[SMEM if i in smem_in els...]
  transfers between devices with their start and end apart: 30 -> 30, of which waited for: 18 -> 14; matrix products, arithmetic and copies ran while one was open for 1% -> 1% of each run, Pallas kernels for 6% -> 6%
where the time goes in v10:
time: 90.9 us; the launch traced here: 90.8 us
  waiting for transfers between devices  36.6 us (40%)
  starting transfers between devices  33 us (36%)
  Pallas kernels  16.9 us (19%)
  local copies, waits for them, and re-layouts  2.71 us (3%)
  between operations  1.47 us (2%)
    ppermute x25, starting transfers between devices, shift_by(): lax.ppermute(value, axes, [(i, (i + shift) % size) for i in range(size)])  26 us
    ppermute x25, waiting for transfers between devices, shift_by(): lax.ppermute(value, axes, [(i, (i + shift) % size) for i in range(size)])  23.9 us
    pallas_call x15, Pallas kernels, call(): pl.pallas_call(body, out_shape=shapes, in_specs=[SMEM if i in smem_in els...  16.9 us
    ppermute x5, waiting for transfers between devices, pair_step(): lax.ppermute(value, name, [(i, i ^ flip) for i in range(lax.axis_size(nam...  12.7 us
    ppermute x5, starting transfers between devices, pair_step(): lax.ppermute(value, name, [(i, i ^ flip) for i in range(lax.axis_size(nam...  7 us
  transfers between devices with their start and end apart: 30, of which 14 were waited for; matrix products, arithmetic and copies ran while one was open for 1% of the time, Pallas kernels for 6%

profile of v10, /device:TPU:0, one launch (start us, length us, event | category | flops | bytes accessed | tf_op | source)
XLA Modules:
  0.0 90.8 jit_solution(10340658812950771747)
XLA Ops:
  2.0 5.0 %collective-permute-start.2 = (s32[3,8]{1,0:T(4,128)S(1)}, s32[3,8]{1,0:T(4,128)S(1)}, u32[]{:S(2)}, u32[]{:S(2)}) collective-permute-start(s32[3,8]{1,0:T(4,128)S(1)} %concatenate.3.refs_0_), channel_id=1, source_target_pairs={{0,12},{4,0},{8,4},{12,8},{1,13},{5,1},{9,5},{13,9},{2,14},{6,2},{... | collective-permute-start | bytes 296 | tf_op jit(solution)/shard_map/ppermute | solution.py:504
  8.1 1.4 %copy-done = bf16[2048,384]{1,0:T(8,128)(2,1)S(1)} copy-done((bf16[2048,384]{1,0:T(8,128)(2,1)S(1)}, bf16[2048,384]{1,0:T(8,128)(2,1)}, u32[]{:S(2)}) %copy-start) | copy-done | bytes 1572888
  12.4 1.8 %shard_map.60 = (s32[6,8]{1,0:T(8,128)S(1)}, bf16[256,384]{1,0:T(8,128)(2,1)S(1)}, bf16[256,384]{1,0:T(8,128)(2,1)S(1)}, bf16[256,384]{1,0:T(8,128)(2,1)S(1)}) custom-call(s32[3]{0:T(128)S(1)} %pad_add_fusion.me, s32[3,8]{1,0:T(4,128)S(1)} %concatenate.3.refs_0_, s32[3,8]{1,0:T(4,128)S(1)} %collective-permute-done.refs_1_, ...), custom_call_target="tpu_custom_call" | custom-call | tf_op jit(solution)/shard_map/pallas_call | solution.py:28
  15.3 1.1 %collective-permute-start.4 = (bf16[256,384]{1,0:T(8,128)(2,1)S(1)}, bf16[256,384]{1,0:T(8,128)(2,1)S(1)}, u32[]{:S(2)}, u32[]{:S(2)}) collective-permute-start(bf16[256,384]{1,0:T(8,128)(2,1)S(1)} %get-tuple-element.31), channel_id=1, source_target_pairs={{0,8},{4,12},{8,0},{12,4},{1,9},{5,13},{9,1},{13,5},{2,10},{6,14},... | collective-permute-start | bytes 589832 | tf_op jit(solution)/shard_map/ppermute | solution.py:504
  17.4 3.2 %collective-permute-done.3.refs_0_ = bf16[256,384]{1,0:T(8,128)(2,1)S(1)} collective-permute-done((bf16[256,384]{1,0:T(8,128)(2,1)S(1)}, bf16[256,384]{1,0:T(8,128)(2,1)S(1)}, u32[]{:S(2)}, u32[]{:S(2)}) %collective-permute-start.3) | collective-permute-done | bytes 196640 | tf_op jit(solution)/shard_map/ppermute | solution.py:504
  20.7 12.1 %collective-permute-done.4.refs_1_ = bf16[256,384]{1,0:T(8,128)(2,1)S(1)} collective-permute-done((bf16[256,384]{1,0:T(8,128)(2,1)S(1)}, bf16[256,384]{1,0:T(8,128)(2,1)S(1)}, u32[]{:S(2)}, u32[]{:S(2)}) %collective-permute-start.4) | collective-permute-done | bytes 196640 | tf_op jit(solution)/shard_map/ppermute | solution.py:504
  32.8 1.2 %shard_map.61.mine = f32[1024,128]{1,0:T(8,128)S(1)} custom-call(s32[6,8]{1,0:T(8,128)S(1)} %get-tuple-element.29.idx, bf16[2048,384]{1,0:T(8,128)(2,1)S(1)} %copy-done.1, bf16[256,384]{1,0:T(8,128)(2,1)S(1)} %collective-permute-done.3.refs_0_, bf16[256,384]{1,0:T(8,128)(2,1)S(1)} %collective-permute-done.4.refs_1_, ...), custom_call_target="tpu_custom_call" | custom-call | tf_op jit(solution)/shard_map/pallas_call | solution.py:28
  34.4 1.5 %collective-permute-done.6.other = f32[1024,128]{1,0:T(8,128)S(1)} collective-permute-done((f32[1024,128]{1,0:T(8,128)S(1)}, f32[1024,128]{1,0:T(8,128)S(1)}, u32[]{:S(2)}, u32[]{:S(2)}) %collective-permute-start.6) | collective-permute-done | bytes 524320 | tf_op jit(solution)/shard_map/ppermute | solution.py:504
  37.0 1.6 %collective-permute-start.9 = (f32[64,128]{1,0:T(8,128)S(1)}, f32[64,128]{1,0:T(8,128)S(1)}, u32[]{:S(2)}, u32[]{:S(2)}) collective-permute-start(f32[64,128]{1,0:T(8,128)S(1)} %get-tuple-element.37), channel_id=1, source_target_pairs={{0,8},{4,12},{8,0},{12,4},{1,9},{5,13},{9,1},{13,5},{2,10},{6,14},... | collective-permute-start | bytes 98312 | tf_op jit(solution)/shard_map/ppermute | solution.py:504
  38.5 1.9 %collective-permute-start.8 = (f32[64,128]{1,0:T(8,128)S(1)}, f32[64,128]{1,0:T(8,128)S(1)}, u32[]{:S(2)}, u32[]{:S(2)}) collective-permute-start(f32[64,128]{1,0:T(8,128)S(1)} %get-tuple-element.37), channel_id=1, source_target_pairs={{0,4},{4,8},{8,12},{12,0},{1,5},{5,9},{9,13},{13,1},{2,6},{6,10},{... | collective-permute-start | bytes 98312 | tf_op jit(solution)/shard_map/ppermute | solution.py:504
  40.5 2.4 %collective-permute-start.13 = (s16[272,128]{1,0:T(8,128)(2,1)S(1)}, s16[272,128]{1,0:T(8,128)(2,1)S(1)}, u32[]{:S(2)}, u32[]{:S(2)}) collective-permute-start(s16[272,128]{1,0:T(8,128)(2,1)S(1)} %get-tuple-element.42), channel_id=1, source_target_pairs={{0,8},{4,12},{8,0},{12,4},{1,9},{5,13},{9,1},{13,5},{2,10},{6,14},... | collective-permute-start | bytes 208904 | tf_op jit(solution)/shard_map/ppermute | solution.py:504
  42.9 1.9 %collective-permute-start.14 = (s16[272,128]{1,0:T(8,128)(2,1)S(1)}, s16[272,128]{1,0:T(8,128)(2,1)S(1)}, u32[]{:S(2)}, u32[]{:S(2)}) collective-permute-start(s16[272,128]{1,0:T(8,128)(2,1)S(1)} %get-tuple-element.43), channel_id=1, source_target_pairs={{0,12},{4,0},{8,4},{12,8},{1,13},{5,1},{9,5},{13,9},{2,14},{6,2},{... | collective-permute-start | bytes 208904 | tf_op jit(solution)/shard_map/ppermute | solution.py:504
  44.9 1.6 %collective-permute-start.11 = (f32[64,128]{1,0:T(8,128)S(1)}, f32[64,128]{1,0:T(8,128)S(1)}, u32[]{:S(2)}, u32[]{:S(2)}) collective-permute-start(f32[64,128]{1,0:T(8,128)S(1)} %add_add_fusion.refs_0_), channel_id=1, source_target_pairs={{0,2},{2,0},{1,3},{3,1},{4,6},{6,4},{5,7},{7,5},{8,10},{10,8},{9,1... | collective-permute-start | bytes 98312 | tf_op jit(solution)/shard_map/ppermute | solution.py:512
  46.4 2.4 %collective-permute-done.11.refs_3_.refs_1_ = f32[64,128]{1,0:T(8,128)S(1)} collective-permute-done((f32[64,128]{1,0:T(8,128)S(1)}, f32[64,128]{1,0:T(8,128)S(1)}, u32[]{:S(2)}, u32[]{:S(2)}) %collective-permute-start.11) | collective-permute-done | bytes 32800 | tf_op jit(solution)/shard_map/ppermute | solution.py:512
  50.7 1.1 %shard_map.66 = (s16[32,2176]{1,0:T(8,128)(2,1)S(1)}, f32[64,128]{1,0:T(8,128)S(1)}, f32[64,128]{1,0:T(8,128)S(1)}) custom-call(s32[3]{0:T(128)S(1)} %pad_add_fusion.me, s32[6,8]{1,0:T(8,128)S(1)} %get-tuple-element.29.idx, f32[64,128]{1,0:T(8,128)S(1)} %add_add_fusion.refs_0_, f32[64,128]{1,0:T(8,128)S(1)} %collective-permute-done.11.refs_3_.refs_1_, ...), custom_call_target="tpu_custom_call" | custom-call | tf_op jit(solution)/shard_map/pallas_call | solution.py:28
  51.9 1.6 %collective-permute-start.18 = (s16[32,2176]{1,0:T(8,128)(2,1)S(1)}, s16[32,2176]{1,0:T(8,128)(2,1)S(1)}, u32[]{:S(2)}, u32[]{:S(2)}) collective-permute-start(s16[32,2176]{1,0:T(8,128)(2,1)S(1)} %get-tuple-element.48.mine), channel_id=1, source_target_pairs={{0,2},{2,0},{1,3},{3,1},{4,6},{6,4},{5,7},{7,5},{8,10},{10,8},{9,1... | collective-permute-start | bytes 417800 | tf_op jit(solution)/shard_map/ppermute | solution.py:512
  53.4 4.3 %collective-permute-done.18.other = s16[32,2176]{1,0:T(8,128)(2,1)S(1)} collective-permute-done((s16[32,2176]{1,0:T(8,128)(2,1)S(1)}, s16[32,2176]{1,0:T(8,128)(2,1)S(1)}, u32[]{:S(2)}, u32[]{:S(2)}) %collective-permute-start.18) | collective-permute-done | bytes 139296 | tf_op jit(solution)/shard_map/ppermute | solution.py:512
  58.6 1.6 %collective-permute-start.21 = (s16[144,128]{1,0:T(8,128)(2,1)S(1)}, s16[144,128]{1,0:T(8,128)(2,1)S(1)}, u32[]{:S(2)}, u32[]{:S(2)}) collective-permute-start(s16[144,128]{1,0:T(8,128)(2,1)S(1)} %get-tuple-element.50), channel_id=1, source_target_pairs={{0,4},{4,8},{8,12},{12,0},{1,5},{5,9},{9,13},{13,1},{2,6},{6,10},{... | collective-permute-start | bytes 110600 | tf_op jit(solution)/shard_map/ppermute | solution.py:504
  60.2 1.8 %collective-permute-start.22 = (s16[144,128]{1,0:T(8,128)(2,1)S(1)}, s16[144,128]{1,0:T(8,128)(2,1)S(1)}, u32[]{:S(2)}, u32[]{:S(2)}) collective-permute-start(s16[144,128]{1,0:T(8,128)(2,1)S(1)} %get-tuple-element.51), channel_id=1, source_target_pairs={{0,8},{4,12},{8,0},{12,4},{1,9},{5,13},{9,1},{13,5},{2,10},{6,14},... | collective-permute-start | bytes 110600 | tf_op jit(solution)/shard_map/ppermute | solution.py:504
  62.0 1.1 %collective-permute-start.23 = (s16[144,128]{1,0:T(8,128)(2,1)S(1)}, s16[144,128]{1,0:T(8,128)(2,1)S(1)}, u32[]{:S(2)}, u32[]{:S(2)}) collective-permute-start(s16[144,128]{1,0:T(8,128)(2,1)S(1)} %get-tuple-element.52), channel_id=1, source_target_pairs={{0,12},{4,0},{8,4},{12,8},{1,13},{5,1},{9,5},{13,9},{2,14},{6,2},{... | collective-permute-start | bytes 110600 | tf_op jit(solution)/shard_map/ppermute | solution.py:504
  63.1 1.1 %shard_map.68 = f32[32,128]{1,0:T(8,128)S(1)} custom-call(s32[3]{0:T(128)S(1)} %pad_add_fusion.me, f32[32,2048]{1,0:T(8,128)S(1)} %get-tuple-element.49.own.refs_0_, f32[32,2048]{1,0:T(8,128)S(1)} %collective-permute-done.19.other), custom_call_target="tpu_custom_call" | custom-call | tf_op jit(solution)/shard_map/pallas_call | solution.py:28
  65.1 2.8 %collective-permute-done.20 = f32[32,128]{1,0:T(8,128)S(1)} collective-permute-done((f32[32,128]{1,0:T(8,128)S(1)}, f32[32,128]{1,0:T(8,128)S(1)}, u32[]{:S(2)}, u32[]{:S(2)}) %collective-permute-start.20) | collective-permute-done | bytes 16416 | tf_op jit(solution)/shard_map/ppermute | solution.py:512
  68.0 1.2 %shard_map.69.mine = s16[32,2176]{1,0:T(8,128)(2,1)S(1)} custom-call(s32[3]{0:T(128)S(1)} %pad_add_fusion.me, s32[6,8]{1,0:T(8,128)S(1)} %get-tuple-element.29.idx, f32[64,128]{1,0:T(8,128)S(1)} %get-tuple-element.47.inverse, f32[32,128]{1,0:T(8,128)S(1)} %add.20.after.refs_0_, f32[32,2048]{1,0:T(8,128)S(1)} %get-tuple-element.49.own.refs_0_, ...), custom_call_target="tpu_custom_call" | custom-call | tf_op jit(solution)/shard_map/pallas_call | solution.py:28
  69.1 1.6 %collective-permute-start.24 = (s16[32,2176]{1,0:T(8,128)(2,1)S(1)}, s16[32,2176]{1,0:T(8,128)(2,1)S(1)}, u32[]{:S(2)}, u32[]{:S(2)}) collective-permute-start(s16[32,2176]{1,0:T(8,128)(2,1)S(1)} %shard_map.69.mine), channel_id=1, source_target_pairs={{0,2},{2,0},{1,3},{3,1},{4,6},{6,4},{5,7},{7,5},{8,10},{10,8},{9,1... | collective-permute-start | bytes 417800 | tf_op jit(solution)/shard_map/ppermute | solution.py:512
  70.7 1.4 %collective-permute-start.25 = (f32[32,128]{1,0:T(8,128)S(1)}, f32[32,128]{1,0:T(8,128)S(1)}, u32[]{:S(2)}, u32[]{:S(2)}) collective-permute-start(f32[32,128]{1,0:T(8,128)S(1)} %add.20.after.refs_0_), channel_id=1, source_target_pairs={{0,8},{4,12},{8,0},{12,4},{1,9},{5,13},{9,1},{13,5},{2,10},{6,14},... | collective-permute-start | bytes 49160 | tf_op jit(solution)/shard_map/ppermute | solution.py:512
  72.1 3.2 %collective-permute-done.25.after.refs_1_ = f32[32,128]{1,0:T(8,128)S(1)} collective-permute-done((f32[32,128]{1,0:T(8,128)S(1)}, f32[32,128]{1,0:T(8,128)S(1)}, u32[]{:S(2)}, u32[]{:S(2)}) %collective-permute-start.25) | collective-permute-done | bytes 16416 | tf_op jit(solution)/shard_map/ppermute | solution.py:512
  76.0 1.9 %shard_map.71.factor = f32[64,64]{1,0:T(8,128)S(1)} custom-call(f32[32,2048]{1,0:T(8,128)S(1)} %shard_map.70.after.own, f32[32,128]{1,0:T(8,128)S(1)} %add.20.after.refs_0_, f32[32,128]{1,0:T(8,128)S(1)} %collective-permute-done.25.after.refs_1_), custom_call_target="tpu_custom_call" | custom-call | tf_op jit(solution)/shard_map/pallas_call | solution.py:28
  77.9 1.5 %shard_map.72 = (bf16[128,2048]{1,0:T(8,128)(2,1)S(1)}, f32[32,128]{1,0:T(8,128)S(1)}) custom-call(s32[3]{0:T(128)S(1)} %pad_add_fusion.me, f32[64,64]{1,0:T(8,128)S(1)} %shard_map.71.factor, f32[32,2048]{1,0:T(8,128)S(1)} %shard_map.70.after.own, f32[32,2048]{1,0:T(8,128)S(1)} %collective-permute-done.26.other), custom_call_target="tpu_custom_call" | custom-call | tf_op jit(solution)/shard_map/pallas_call | solution.py:28
  79.5 1.5 %collective-permute-start.29 = (f32[32,128]{1,0:T(8,128)S(1)}, f32[32,128]{1,0:T(8,128)S(1)}, u32[]{:S(2)}, u32[]{:S(2)}) collective-permute-start(f32[32,128]{1,0:T(8,128)S(1)} %get-tuple-element.54.refs_0_), channel_id=1, source_target_pairs={{0,12},{4,0},{8,4},{12,8},{1,13},{5,1},{9,5},{13,9},{2,14},{6,2},{... | collective-permute-start | bytes 49160 | tf_op jit(solution)/shard_map/ppermute | solution.py:504
  83.5 2.2 %collective-permute-done.28.refs_2_ = f32[32,128]{1,0:T(8,128)S(1)} collective-permute-done((f32[32,128]{1,0:T(8,128)S(1)}, f32[32,128]{1,0:T(8,128)S(1)}, u32[]{:S(2)}, u32[]{:S(2)}) %collective-permute-start.28) | collective-permute-done | bytes 16416 | tf_op jit(solution)/shard_map/ppermute | solution.py:504
  85.7 1.6 %collective-permute-done.27.refs_1_ = f32[32,128]{1,0:T(8,128)S(1)} collective-permute-done((f32[32,128]{1,0:T(8,128)S(1)}, f32[32,128]{1,0:T(8,128)S(1)}, u32[]{:S(2)}, u32[]{:S(2)}) %collective-permute-start.27) | collective-permute-done | bytes 16416 | tf_op jit(solution)/shard_map/ppermute | solution.py:504
  87.4 3.4 %shard_map.73 = f32[32,2048]{1,0:T(8,128)} custom-call(s32[3]{0:T(128)S(1)} %pad_add_fusion.me, bf16[128,2048]{1,0:T(8,128)(2,1)S(1)} %get-tuple-element.53.mapped, f32[32,128]{1,0:T(8,128)S(1)} %get-tuple-element.54.refs_0_, f32[32,128]{1,0:T(8,128)S(1)} %collective-permute-done.27.refs_1_, f32[32,128]{1,0:T(8,128)S(1)} %collective-permute-done.28.refs_2_, ...), custom_call_target="tpu_custom_call" | custom-call | tf_op jit(solution)/shard_map/pallas_call | solution.py:28
  (54 shorter events, 15.2 us)
Async XLA Ops:
  2.0 8.6 %collective-permute-start.2 = (s32[3,8]{1,0:T(4,128)S(1)}, s32[3,8]{1,0:T(4,128)S(1)}, u32[]{:S(2)}, u32[]{:S(2)}) collective-permute-start(s32[3,8]{1,0:T(4,128)S(1)} %concatenate.3.refs_0_), channel_id=1, source_target_pairs={{0,12},{4,0},{8,4},{12,8},{1,13},{5,1},{9,5},{13,9},{2,14},{6,2},{... | collective-permute-start | bytes 296 | tf_op jit(solution)/shard_map/ppermute | solution.py:504
  7.0 4.5 %collective-permute-start.1 = (s32[3,8]{1,0:T(4,128)S(1)}, s32[3,8]{1,0:T(4,128)S(1)}, u32[]{:S(2)}, u32[]{:S(2)}) collective-permute-start(s32[3,8]{1,0:T(4,128)S(1)} %concatenate.3.refs_0_), channel_id=1, source_target_pairs={{0,8},{4,12},{8,0},{12,4},{1,9},{5,13},{9,1},{13,5},{2,10},{6,14},... | collective-permute-start | bytes 296 | tf_op jit(solution)/shard_map/ppermute | solution.py:504
  7.0 5.4 %collective-permute-start = (s32[3,8]{1,0:T(4,128)S(1)}, s32[3,8]{1,0:T(4,128)S(1)}, u32[]{:S(2)}, u32[]{:S(2)}) collective-permute-start(s32[3,8]{1,0:T(4,128)S(1)} %concatenate.3.refs_0_), channel_id=1, source_target_pairs={{0,4},{4,8},{8,12},{12,0},{1,5},{5,9},{9,13},{13,1},{2,6},{6,10},{... | collective-permute-start | bytes 296 | tf_op jit(solution)/shard_map/ppermute | solution.py:504
  10.5 22.3 %copy-start.1 = (bf16[2048,384]{1,0:T(8,128)(2,1)S(1)}, bf16[2048,384]{1,0:T(8,128)(2,1)}, u32[]{:S(2)}) copy-start(bf16[2048,384]{1,0:T(8,128)(2,1)} %emb.3) | copy-start | bytes 4718596
  14.2 19.8 %copy-start.2 = (f32[2048,32]{0,1:T(8,128)S(1)}, f32[2048,32]{0,1:T(8,128)}, u32[]{:S(2)}) copy-start(f32[2048,32]{0,1:T(8,128)} %param.5) | copy-start | bytes 786436
  14.2 6.4 %collective-permute-start.3 = (bf16[256,384]{1,0:T(8,128)(2,1)S(1)}, bf16[256,384]{1,0:T(8,128)(2,1)S(1)}, u32[]{:S(2)}, u32[]{:S(2)}) collective-permute-start(bf16[256,384]{1,0:T(8,128)(2,1)S(1)} %get-tuple-element.30), channel_id=1, source_target_pairs={{0,12},{4,0},{8,4},{12,8},{1,13},{5,1},{9,5},{13,9},{2,14},{6,2},{... | collective-permute-start | bytes 589832 | tf_op jit(solution)/shard_map/ppermute | solution.py:504
  15.3 17.5 %collective-permute-start.4 = (bf16[256,384]{1,0:T(8,128)(2,1)S(1)}, bf16[256,384]{1,0:T(8,128)(2,1)S(1)}, u32[]{:S(2)}, u32[]{:S(2)}) collective-permute-start(bf16[256,384]{1,0:T(8,128)(2,1)S(1)} %get-tuple-element.31), channel_id=1, source_target_pairs={{0,8},{4,12},{8,0},{12,4},{1,9},{5,13},{9,1},{13,5},{2,10},{6,14},... | collective-permute-start | bytes 589832 | tf_op jit(solution)/shard_map/ppermute | solution.py:504
  16.4 16.4 %collective-permute-start.5 = (bf16[256,384]{1,0:T(8,128)(2,1)S(1)}, bf16[256,384]{1,0:T(8,128)(2,1)S(1)}, u32[]{:S(2)}, u32[]{:S(2)}) collective-permute-start(bf16[256,384]{1,0:T(8,128)(2,1)S(1)} %get-tuple-element.32), channel_id=1, source_target_pairs={{0,4},{4,8},{8,12},{12,0},{1,5},{5,9},{9,13},{13,1},{2,6},{6,10},{... | collective-permute-start | bytes 589832 | tf_op jit(solution)/shard_map/ppermute | solution.py:504
  17.4 16.8 %collective-permute-start.7 = (f32[1024,128]{1,0:T(8,128)S(1)}, f32[1024,128]{1,0:T(8,128)S(1)}, u32[]{:S(2)}, u32[]{:S(2)}) collective-permute-start(f32[1024,128]{1,0:T(8,128)S(1)} %shard_map.59.refs_5_.mine), channel_id=1, source_target_pairs={{0,1},{1,0},{2,3},{3,2},{4,5},{5,4},{6,7},{7,6},{8,9},{9,8},{10,11... | collective-permute-start | bytes 1572872 | tf_op jit(solution)/shard_map/ppermute | solution.py:504
  34.0 2.0 %collective-permute-start.6 = (f32[1024,128]{1,0:T(8,128)S(1)}, f32[1024,128]{1,0:T(8,128)S(1)}, u32[]{:S(2)}, u32[]{:S(2)}) collective-permute-start(f32[1024,128]{1,0:T(8,128)S(1)} %shard_map.61.mine), channel_id=1, source_target_pairs={{0,1},{1,0},{2,3},{3,2},{4,5},{5,4},{6,7},{7,6},{8,9},{9,8},{10,11... | collective-permute-start | bytes 1572872 | tf_op jit(solution)/shard_map/ppermute | solution.py:504
  36.9 6.0 %collective-permute-start.10 = (f32[64,128]{1,0:T(8,128)S(1)}, f32[64,128]{1,0:T(8,128)S(1)}, u32[]{:S(2)}, u32[]{:S(2)}) collective-permute-start(f32[64,128]{1,0:T(8,128)S(1)} %get-tuple-element.37), channel_id=1, source_target_pairs={{0,12},{4,0},{8,4},{12,8},{1,13},{5,1},{9,5},{13,9},{2,14},{6,2},{... | collective-permute-start | bytes 98312 | tf_op jit(solution)/shard_map/ppermute | solution.py:504
  37.0 7.9 %collective-permute-start.9 = (f32[64,128]{1,0:T(8,128)S(1)}, f32[64,128]{1,0:T(8,128)S(1)}, u32[]{:S(2)}, u32[]{:S(2)}) collective-permute-start(f32[64,128]{1,0:T(8,128)S(1)} %get-tuple-element.37), channel_id=1, source_target_pairs={{0,8},{4,12},{8,0},{12,4},{1,9},{5,13},{9,1},{13,5},{2,10},{6,14},... | collective-permute-start | bytes 98312 | tf_op jit(solution)/shard_map/ppermute | solution.py:504
  38.5 6.3 %collective-permute-start.8 = (f32[64,128]{1,0:T(8,128)S(1)}, f32[64,128]{1,0:T(8,128)S(1)}, u32[]{:S(2)}, u32[]{:S(2)}) collective-permute-start(f32[64,128]{1,0:T(8,128)S(1)} %get-tuple-element.37), channel_id=1, source_target_pairs={{0,4},{4,8},{8,12},{12,0},{1,5},{5,9},{9,13},{13,1},{2,6},{6,10},{... | collective-permute-start | bytes 98312 | tf_op jit(solution)/shard_map/ppermute | solution.py:504
  40.5 8.4 %collective-permute-start.12 = (s16[272,128]{1,0:T(8,128)(2,1)S(1)}, s16[272,128]{1,0:T(8,128)(2,1)S(1)}, u32[]{:S(2)}, u32[]{:S(2)}) collective-permute-start(s16[272,128]{1,0:T(8,128)(2,1)S(1)} %get-tuple-element.41), channel_id=1, source_target_pairs={{0,4},{4,8},{8,12},{12,0},{1,5},{5,9},{9,13},{13,1},{2,6},{6,10},{... | collective-permute-start | bytes 208904 | tf_op jit(solution)/shard_map/ppermute | solution.py:504
  40.5 8.3 %collective-permute-start.13 = (s16[272,128]{1,0:T(8,128)(2,1)S(1)}, s16[272,128]{1,0:T(8,128)(2,1)S(1)}, u32[]{:S(2)}, u32[]{:S(2)}) collective-permute-start(s16[272,128]{1,0:T(8,128)(2,1)S(1)} %get-tuple-element.42), channel_id=1, source_target_pairs={{0,8},{4,12},{8,0},{12,4},{1,9},{5,13},{9,1},{13,5},{2,10},{6,14},... | collective-permute-start | bytes 208904 | tf_op jit(solution)/shard_map/ppermute | solution.py:504
  42.9 5.9 %collective-permute-start.14 = (s16[272,128]{1,0:T(8,128)(2,1)S(1)}, s16[272,128]{1,0:T(8,128)(2,1)S(1)}, u32[]{:S(2)}, u32[]{:S(2)}) collective-permute-start(s16[272,128]{1,0:T(8,128)(2,1)S(1)} %get-tuple-element.43), channel_id=1, source_target_pairs={{0,12},{4,0},{8,4},{12,8},{1,13},{5,1},{9,5},{13,9},{2,14},{6,2},{... | collective-permute-start | bytes 208904 | tf_op jit(solution)/shard_map/ppermute | solution.py:504
  44.9 4.0 %collective-permute-start.11 = (f32[64,128]{1,0:T(8,128)S(1)}, f32[64,128]{1,0:T(8,128)S(1)}, u32[]{:S(2)}, u32[]{:S(2)}) collective-permute-start(f32[64,128]{1,0:T(8,128)S(1)} %add_add_fusion.refs_0_), channel_id=1, source_target_pairs={{0,2},{2,0},{1,3},{3,1},{4,6},{6,4},{5,7},{7,5},{8,10},{10,8},{9,1... | collective-permute-start | bytes 98312 | tf_op jit(solution)/shard_map/ppermute | solution.py:512
  48.9 1.3 %collective-permute-start.15 = (bf16[1,256,128]{2,1,0:T(8,128)(2,1)S(1)}, bf16[1,256,128]{2,1,0:T(8,128)(2,1)S(1)}, u32[]{:S(2)}, u32[]{:S(2)}) collective-permute-start(bf16[1,256,128]{2,1,0:T(8,128)(2,1)S(1)} %get-tuple-element.44.refs_6_.refs_4_), channel_id=1, source_target_pairs={{0,1},{1,0},{2,3},{3,2},{4,5},{5,4},{6,7},{7,6},{8,9},{9,8},{10,11... | collective-permute-start | bytes 196616 | tf_op jit(solution)/shard_map/ppermute | solution.py:504
  49.0 1.4 %collective-permute-start.16 = (bf16[1,256,128]{2,1,0:T(8,128)(2,1)S(1)}, bf16[1,256,128]{2,1,0:T(8,128)(2,1)S(1)}, u32[]{:S(2)}, u32[]{:S(2)}) collective-permute-start(bf16[1,256,128]{2,1,0:T(8,128)(2,1)S(1)} %get-tuple-element.45.refs_7_.refs_5_), channel_id=1, source_target_pairs={{0,1},{1,0},{2,3},{3,2},{4,5},{5,4},{6,7},{7,6},{8,9},{9,8},{10,11... | collective-permute-start | bytes 196616 | tf_op jit(solution)/shard_map/ppermute | solution.py:504
  49.5 1.3 %collective-permute-start.17 = (bf16[1,256,128]{2,1,0:T(8,128)(2,1)S(1)}, bf16[1,256,128]{2,1,0:T(8,128)(2,1)S(1)}, u32[]{:S(2)}, u32[]{:S(2)}) collective-permute-start(bf16[1,256,128]{2,1,0:T(8,128)(2,1)S(1)} %get-tuple-element.46.refs_8_.refs_6_), channel_id=1, source_target_pairs={{0,1},{1,0},{2,3},{3,2},{4,5},{5,4},{6,7},{7,6},{8,9},{9,8},{10,11... | collective-permute-start | bytes 196616 | tf_op jit(solution)/shard_map/ppermute | solution.py:504
  51.9 5.8 %collective-permute-start.18 = (s16[32,2176]{1,0:T(8,128)(2,1)S(1)}, s16[32,2176]{1,0:T(8,128)(2,1)S(1)}, u32[]{:S(2)}, u32[]{:S(2)}) collective-permute-start(s16[32,2176]{1,0:T(8,128)(2,1)S(1)} %get-tuple-element.48.mine), channel_id=1, source_target_pairs={{0,2},{2,0},{1,3},{3,1},{4,6},{6,4},{5,7},{7,5},{8,10},{10,8},{9,1... | collective-permute-start | bytes 417800 | tf_op jit(solution)/shard_map/ppermute | solution.py:512
  58.5 4.6 %collective-permute-start.19 = (f32[32,2048]{1,0:T(8,128)S(1)}, f32[32,2048]{1,0:T(8,128)S(1)}, u32[]{:S(2)}, u32[]{:S(2)}) collective-permute-start(f32[32,2048]{1,0:T(8,128)S(1)} %get-tuple-element.49.own.refs_0_), channel_id=1, source_target_pairs={{0,1},{1,0},{2,3},{3,2},{4,5},{5,4},{6,7},{7,6},{8,9},{9,8},{10,11... | collective-permute-start | bytes 786440 | tf_op jit(solution)/shard_map/ppermute | solution.py:504
  58.6 9.3 %collective-permute-start.21 = (s16[144,128]{1,0:T(8,128)(2,1)S(1)}, s16[144,128]{1,0:T(8,128)(2,1)S(1)}, u32[]{:S(2)}, u32[]{:S(2)}) collective-permute-start(s16[144,128]{1,0:T(8,128)(2,1)S(1)} %get-tuple-element.50), channel_id=1, source_target_pairs={{0,4},{4,8},{8,12},{12,0},{1,5},{5,9},{9,13},{13,1},{2,6},{6,10},{... | collective-permute-start | bytes 110600 | tf_op jit(solution)/shard_map/ppermute | solution.py:504
  60.2 7.8 %collective-permute-start.22 = (s16[144,128]{1,0:T(8,128)(2,1)S(1)}, s16[144,128]{1,0:T(8,128)(2,1)S(1)}, u32[]{:S(2)}, u32[]{:S(2)}) collective-permute-start(s16[144,128]{1,0:T(8,128)(2,1)S(1)} %get-tuple-element.51), channel_id=1, source_target_pairs={{0,8},{4,12},{8,0},{12,4},{1,9},{5,13},{9,1},{13,5},{2,10},{6,14},... | collective-permute-start | bytes 110600 | tf_op jit(solution)/shard_map/ppermute | solution.py:504
  62.0 6.0 %collective-permute-start.23 = (s16[144,128]{1,0:T(8,128)(2,1)S(1)}, s16[144,128]{1,0:T(8,128)(2,1)S(1)}, u32[]{:S(2)}, u32[]{:S(2)}) collective-permute-start(s16[144,128]{1,0:T(8,128)(2,1)S(1)} %get-tuple-element.52), channel_id=1, source_target_pairs={{0,12},{4,0},{8,4},{12,8},{1,13},{5,1},{9,5},{13,9},{2,14},{6,2},{... | collective-permute-start | bytes 110600 | tf_op jit(solution)/shard_map/ppermute | solution.py:504
  64.2 3.8 %collective-permute-start.20 = (f32[32,128]{1,0:T(8,128)S(1)}, f32[32,128]{1,0:T(8,128)S(1)}, u32[]{:S(2)}, u32[]{:S(2)}) collective-permute-start(f32[32,128]{1,0:T(8,128)S(1)} %shard_map.68), channel_id=1, source_target_pairs={{0,4},{4,0},{8,12},{12,8},{1,5},{5,1},{9,13},{13,9},{2,6},{6,2},{1... | collective-permute-start | bytes 49160 | tf_op jit(solution)/shard_map/ppermute | solution.py:512
  69.1 6.2 %collective-permute-start.24 = (s16[32,2176]{1,0:T(8,128)(2,1)S(1)}, s16[32,2176]{1,0:T(8,128)(2,1)S(1)}, u32[]{:S(2)}, u32[]{:S(2)}) collective-permute-start(s16[32,2176]{1,0:T(8,128)(2,1)S(1)} %shard_map.69.mine), channel_id=1, source_target_pairs={{0,2},{2,0},{1,3},{3,1},{4,6},{6,4},{5,7},{7,5},{8,10},{10,8},{9,1... | collective-permute-start | bytes 417800 | tf_op jit(solution)/shard_map/ppermute | solution.py:512
  70.7 4.6 %collective-permute-start.25 = (f32[32,128]{1,0:T(8,128)S(1)}, f32[32,128]{1,0:T(8,128)S(1)}, u32[]{:S(2)}, u32[]{:S(2)}) collective-permute-start(f32[32,128]{1,0:T(8,128)S(1)} %add.20.after.refs_0_), channel_id=1, source_target_pairs={{0,8},{4,12},{8,0},{12,4},{1,9},{5,13},{9,1},{13,5},{2,10},{6,14},... | collective-permute-start | bytes 49160 | tf_op jit(solution)/shard_map/ppermute | solution.py:512
  75.9 2.0 %collective-permute-start.26 = (f32[32,2048]{1,0:T(8,128)S(1)}, f32[32,2048]{1,0:T(8,128)S(1)}, u32[]{:S(2)}, u32[]{:S(2)}) collective-permute-start(f32[32,2048]{1,0:T(8,128)S(1)} %shard_map.70.after.own), channel_id=1, source_target_pairs={{0,1},{1,0},{2,3},{3,2},{4,5},{5,4},{6,7},{7,6},{8,9},{9,8},{10,11... | collective-permute-start | bytes 786440 | tf_op jit(solution)/shard_map/ppermute | solution.py:504
  79.5 4.1 %collective-permute-start.29 = (f32[32,128]{1,0:T(8,128)S(1)}, f32[32,128]{1,0:T(8,128)S(1)}, u32[]{:S(2)}, u32[]{:S(2)}) collective-permute-start(f32[32,128]{1,0:T(8,128)S(1)} %get-tuple-element.54.refs_0_), channel_id=1, source_target_pairs={{0,12},{4,0},{8,4},{12,8},{1,13},{5,1},{9,5},{13,9},{2,14},{6,2},{... | collective-permute-start | bytes 49160 | tf_op jit(solution)/shard_map/ppermute | solution.py:504
  80.9 4.8 %collective-permute-start.28 = (f32[32,128]{1,0:T(8,128)S(1)}, f32[32,128]{1,0:T(8,128)S(1)}, u32[]{:S(2)}, u32[]{:S(2)}) collective-permute-start(f32[32,128]{1,0:T(8,128)S(1)} %get-tuple-element.54.refs_0_), channel_id=1, source_target_pairs={{0,8},{4,12},{8,0},{12,4},{1,9},{5,13},{9,1},{13,5},{2,10},{6,14},... | collective-permute-start | bytes 49160 | tf_op jit(solution)/shard_map/ppermute | solution.py:504
  81.8 5.5 %collective-permute-start.27 = (f32[32,128]{1,0:T(8,128)S(1)}, f32[32,128]{1,0:T(8,128)S(1)}, u32[]{:S(2)}, u32[]{:S(2)}) collective-permute-start(f32[32,128]{1,0:T(8,128)S(1)} %get-tuple-element.54.refs_0_), channel_id=1, source_target_pairs={{0,4},{4,8},{8,12},{12,0},{1,5},{5,9},{9,13},{13,1},{2,6},{6,10},{... | collective-permute-start | bytes 49160 | tf_op jit(solution)/shard_map/ppermute | solution.py:504
  (1 other events, 1.4 us)

commit v11 on v10

--- a/solution.py
+++ b/solution.py
@@ -127,12 +127,10 @@
 
 
 def times(left, parts):
-    left = thirds(left)
-    m = left.shape[0] // 3
-    product3 = jnp.dot(
-        jnp.concatenate([left, left, left], axis=1), parts, preferred_element_type=F32
-    )
-    return (product3[2 * m :] + product3[m : 2 * m]) + product3[:m]
+    m = left.shape[0]
+    left = jnp.concatenate(halves(left), axis=0)
+    both = jnp.dot(jnp.concatenate([left, left], axis=1), parts, preferred_element_type=F32)
+    return both[m:] + both[:m]
 
 
 def lower_inverse(matrix, step=8):
@@ -234,10 +232,12 @@
             sends[k - 1][j * BLOCK : (j + 1) * BLOCK, :] = emb[at_block(idx[4, k * capacity + j]), :]
 
 
-def partial_distance(left, right):
+def squares(block):
+    return jnp.sum(jnp.square(block.astype(F32)), axis=1, keepdims=True)
+
+
+def partial_distance(left, right, left_sq, right_sq):
     inner = lax.dot_general(left, right, NT, preferred_element_type=F32)
-    left_sq = jnp.sum(jnp.square(left.astype(F32)), axis=1, keepdims=True)
-    right_sq = jnp.sum(jnp.square(right.astype(F32)), axis=1, keepdims=True)
     right_row = jnp.sum(jnp.where(eye_mask(BLOCK), right_sq, 0.0), axis=0, keepdims=True)
     return left_sq + right_row - 2.0 * inner
 
@@ -245,20 +245,31 @@
 def self_distance_body(own_blocks, tile_count, me, emb, out):
     for i in range(own_blocks):
         block = emb[at_block(i * tile_count + me[1]), :]
-        out[i * BLOCK : (i + 1) * BLOCK, :] = partial_distance(block, block)
-
-
-def pair_distance_body(row_count, capacity, idx, emb, *refs):
+        block_sq = squares(block)
+        out[i * BLOCK : (i + 1) * BLOCK, :] = partial_distance(block, block, block_sq, block_sq)
+
+
+def squares_body(emb, after, out):
+    for b in range(out.shape[0] // BLOCK):
+        part = slice(b * BLOCK, (b + 1) * BLOCK)
+        out[part, :] = jnp.broadcast_to(squares(emb[part, :]), (BLOCK, BLOCK))
+
+
+def pair_distance_body(row_count, capacity, idx, emb, own_squares, *refs):
     out = refs[-1]
     for k in range(row_count):
         for j in range(capacity):
             slot = k * capacity + j
             left = emb[at_block(idx[0, slot]), :]
+            left_sq = own_squares[at_block(idx[0, slot]), :]
             if k == 0:
                 right = emb[at_block(idx[4, j]), :]
+                right_sq = own_squares[at_block(idx[4, j]), :]
             else:
                 right = refs[k - 1][j * BLOCK : (j + 1) * BLOCK, :]
-            out[slot * BLOCK : (slot + 1) * BLOCK, :] = partial_distance(left, right)
+                right_sq = squares(right)
+            part = slice(slot * BLOCK, (slot + 1) * BLOCK)
+            out[part, :] = partial_distance(left, right, left_sq, right_sq)
 
 
 def self_tile_body(own_blocks, mine, other, packed, sums):
@@ -341,71 +352,92 @@
     send[base + len(blocks) * count :, :] = as_rows(*lines, CODE_ROWS)
 
 
-def apply_tiles(dims, me, idx, inverse, own, received, base, near_tiles, home_tiles, sent, shared, self_tiles, out):
+def add_product(out, block, packed, values):
+    place = at_block(block)
+    out[:, place] = out[:, place] + product(packed, values)
+
+
+def apply_own(dims, me, idx, inverse, own, near_tiles, home_tiles, self_tiles, out):
     row_count, capacity, per_core, blocks_here, tile_count = dims
-    row, tile_index, core = me[0], me[1], me[2]
+    row, tile_index = me[0], me[1]
+    out[...] = jnp.zeros(out.shape, F32)
+
+    def scaled(block):
+        return own[:, at_block(block)] * inverse[pl.ds(row * blocks_here + block, 1), :]
+
+    for i in range(blocks_here // tile_count):
+        block = i * tile_count + tile_index
+        add_product(out, block, self_tiles[i], scaled(block))
+    for j in range(capacity):
+        add_product(out, idx[0, j], near_tiles[j], scaled(idx[4, j]))
+        add_product(out, idx[4, j], home_tiles[j], scaled(idx[0, j]))
+
+
+def apply_far(dims, me, idx, inverse, received, base, near_tiles, sent, shared, out):
+    row_count, capacity, per_core, blocks_here, tile_count = dims
+    core = me[2]
     count = out.shape[0]
-    out[...] = jnp.zeros(out.shape, F32)
-
-    def scaled(values, block):
-        return values * inverse[pl.ds(block, 1), :]
-
-    def add(block, packed, values):
-        place = at_block(block)
-        out[:, place] = out[:, place] + product(packed, values)
-
     lines = [scale_rows(message[message.shape[0] - CODE_ROWS :, :]) for message in received]
     first_line = base // BLOCK
 
-    def arrived(k, place):
+    def arrived(k, place, block):
         steps = received[k - 1][pl.ds(pl.multiple_of(base + place * count, CODE_ROWS), count), :]
         rows = lines[k - 1][first_line : first_line + 2 * capacity, :]
-        return decode(steps, row_at(rows, place))
-
-    for i in range(blocks_here // tile_count):
-        block = i * tile_count + tile_index
-        add(block, self_tiles[i], scaled(own[:, at_block(block)], row * blocks_here + block))
-    for k in range(row_count):
+        return decode(steps, row_at(rows, place) * inverse[pl.ds(block, 1), :])
+
+    for k in range(1, row_count):
         for j in range(capacity):
             slot = k * capacity + j
-            if k == 0:
-                values = own[:, at_block(idx[4, j])]
+            values = arrived(row_count - k, capacity + j, idx[1, slot])
+            add_product(out, idx[0, slot], near_tiles[slot], values)
+            inner = j % per_core
+            if j < per_core:
+                place = core * per_core + inner
+                packed = sent[k - 1][inner]
             else:
-                values = arrived(row_count - k, capacity + j)
-            add(idx[0, slot], near_tiles[slot], scaled(values, idx[1, slot]))
-    for k in range(row_count):
-        for j in range(capacity):
-            if k == 0:
-                slot = j
-                values = own[:, at_block(idx[0, j])]
-                packed = home_tiles[j]
-            else:
-                inner = j % per_core
-                if j < per_core:
-                    place = core * per_core + inner
-                    packed = sent[k - 1][inner]
-                else:
-                    place = (1 - core) * per_core + inner
-                    packed = shared[k - 1][inner]
-                slot = k * capacity + place
-                values = arrived(k, place)
-            add(idx[4, slot], packed, scaled(values, idx[5, slot]))
-
-
-def first_apply_body(dims, coded, me, idx, *refs):
-    row_count, per_core = dims[0], dims[2]
-    terms, refs = refs[:2], refs[2:]
-    own, near_tiles, home_tiles, self_tiles = refs[:4]
-    sent, shared = refs[4 : 3 + row_count], refs[3 + row_count : 2 + 2 * row_count]
-    messages = refs[2 + 2 * row_count : -4]
-    out, degree, inverse, total_out = refs[-4:]
-    total = terms[0][...] + terms[1][...]
+                place = (1 - core) * per_core + inner
+                packed = shared[k - 1][inner]
+            slot = k * capacity + place
+            add_product(out, idx[4, slot], packed, arrived(k, place, idx[5, slot]))
+
+
+def first_own_body(dims, me, idx, mine, other, own, near_tiles, home_tiles, self_tiles, out, degree, inverse):
+    total = mine[...] + other[...]
     degree[...] = total
     inverse[...] = 1.0 / jnp.sqrt(total)
-    apply_tiles(
-        dims, me, idx, inverse, own, messages, per_core * BLOCK, near_tiles, home_tiles, sent, shared, self_tiles, total_out
-    )
-    put_sum(coded, total_out, out)
+    apply_own(dims, me, idx, inverse, own, near_tiles, home_tiles, self_tiles, out)
+
+
+def first_far_body(dims, coded, me, idx, inverse, started, near_tiles, *refs):
+    row_count, per_core = dims[0], dims[2]
+    others = row_count - 1
+    sent, shared, messages = refs[:others], refs[others : 2 * others], refs[2 * others : 3 * others]
+    out, total = refs[3 * others :]
+    total[...] = started[...]
+    apply_far(dims, me, idx, inverse, messages, per_core * BLOCK, near_tiles, sent, shared, total)
+    put_sum(coded, total, out)
+
+
+def second_apply_body(dims, me, idx, inverse, after, own, home_tiles, self_tiles, near_tiles, *refs):
+    others = dims[0] - 1
+    sent, shared, received = refs[:others], refs[others : 2 * others], refs[2 * others : 3 * others]
+    out = refs[-1]
+    apply_own(dims, me, idx, inverse, own, near_tiles, home_tiles, self_tiles, out)
+    apply_far(dims, me, idx, inverse, received, 0, near_tiles, sent, shared, out)
+
+
+def gate_body(value, after, out):
+    pass
+
+
+def gate(value, after):
+    return pl.pallas_call(
+        gate_body,
+        out_shape=sds(value.shape, value.dtype),
+        in_specs=[ANY, ANY],
+        out_specs=ANY,
+        input_output_aliases={0: 0},
+    )(value, after)
 
 
 def put_sum(coded, total, out):
@@ -438,17 +470,6 @@
         out[:, at] = value * row
 
 
-def second_apply_body(dims, coded, me, idx, inverse, after, *refs):
-    row_count = dims[0]
-    own, near_tiles, home_tiles, self_tiles = refs[:4]
-    sent, shared = refs[4 : 3 + row_count], refs[3 + row_count : 2 + 2 * row_count]
-    received, (out, total_out) = refs[2 + 2 * row_count : -2], refs[-2:]
-    apply_tiles(
-        dims, me, idx, inverse, own, received, 0, near_tiles, home_tiles, sent, shared, self_tiles, total_out
-    )
-    put_sum(coded, total_out, out)
-
-
 def mapped_body(dims, coded, me, idx, inverse, mine, other, out, *refs):
     row_count, capacity, per_core, blocks_here, tile_count = dims
     sends, (codes, powers, parts) = refs[:-3], refs[-3:]
@@ -458,8 +479,8 @@
         pick_columns(idx, k, row_count, capacity, codes, powers, parts, sends[k - 1], 0, ([], []))
 
 
-def last_mapped_body(blocks_here, coded, me, inverse, mine, other, after, out):
-    take_sum(coded, me, blocks_here, inverse, mine, other, out)
+def last_mapped_body(blocks_here, me, inverse, mine, other, after, out):
+    take_sum(False, me, blocks_here, inverse, mine, other, out)
 
 
 def folded(square):
@@ -483,7 +504,7 @@
 
 def second_gram_body(me, factor, own, other, mapped, out):
     full = both_columns(me[2], own[...], other[...])
-    parts = thirds(times(factor[...], thirds(full)))
+    parts = thirds(times(factor[...], pack(full)))
     mapped[...] = parts[: mapped.shape[0]]
     out[...] = folded(gram(parts))
 
@@ -493,11 +514,7 @@
     factor = lower_inverse(unfolded(refs[:-1]))
     own_cols = out.shape[0]
     part = jnp.where(me[2] == 0, factor[:own_cols], factor[own_cols:])
-    left = jnp.concatenate(halves(part), axis=0)
-    both = jnp.dot(
-        jnp.concatenate([left, left], axis=1), mapped[...], preferred_element_type=F32
-    )
-    out[...] = both[own_cols:] + both[:own_cols]
+    out[...] = times(part, mapped[...])
 
 
 def shift_by(value, axes, size, shift):
@@ -572,10 +589,11 @@
     start_codes = call(start_body, [sds(*shape) for shape in code_shapes], [values])
     code_scratch = [pltpu.VMEM(*shape) for shape in code_shapes]
     coded = tile_count == 2
+    own_squares = call(squares_body, sds((rows_here, BLOCK), F32), [embeddings, idx], any_in=(1,))
     pair_part = call(
         functools.partial(pair_distance_body, row_count, capacity),
         sds((slots * BLOCK, BLOCK), F32),
-        [idx, embeddings, *far],
+        [idx, embeddings, own_squares, *far],
         smem_in=(0,),
     )
     pair_other = shift_by(pair_part, "cols", core_count, 1)
@@ -602,16 +620,21 @@
     )
     shared = [shift_by(tile, "cols", core_count, 1) for tile in sent]
 
-    tile_args = [near_tiles, home_tiles, self_tiles, *sent, *shared]
     block_shape = sds((own_cols, rows_here), F32)
     sum_shape = sds((own_cols, rows_here + BLOCK), jnp.int16) if coded else block_shape
     square = sds((2 * own_cols, 2 * own_cols), F32)
     folded_square = sds((own_cols, 4 * own_cols), F32)
 
-    part, degree, inverse = call(
-        functools.partial(first_apply_body, dims, coded),
-        [sum_shape, table, table],
-        [me, idx, *degree_terms, values, *tile_args, *messages],
+    started, degree, inverse = call(
+        functools.partial(first_own_body, dims),
+        [block_shape, table, table],
+        [me, idx, *degree_terms, values, near_tiles, home_tiles, self_tiles],
+        smem_in=(0, 1),
+    )
+    part = call(
+        functools.partial(first_far_body, dims, coded),
+        sum_shape,
+        [me, idx, inverse, started, near_tiles, *sent, *shared, *messages],
         smem_in=(0, 1),
         scratch=[pltpu.VMEM((own_cols, rows_here), F32)],
     )
@@ -628,21 +651,21 @@
 
     mapped_other = shift_by(mapped, "cols", core_count, 1)
     first_gram = call(gram_body, folded_square, [me, mapped, mapped_other], smem_in=(0,))
+    part = call(
+        functools.partial(second_apply_body, dims),
+        block_shape,
+        [me, idx, inverse, first_gram, mapped, home_tiles, self_tiles, near_tiles, *sent, *shared, *received],
+        smem_in=(0, 1),
+        any_in=(3,),
+    )
     steps = (row_count - 1).bit_length()
     for bit in range(steps - 1):
         first_gram = first_gram + pair_step(first_gram, "rows", 1 << bit)
-    part = call(
-        functools.partial(second_apply_body, dims, coded),
-        sum_shape,
-        [me, idx, inverse, first_gram, mapped, *tile_args, *received],
-        smem_in=(0, 1),
-        any_in=(3,),
-        scratch=[pltpu.VMEM((own_cols, rows_here), F32)],
-    )
+    part = gate(part, first_gram)
     gram_terms = (first_gram, pair_step(first_gram, "rows", 1 << (steps - 1)))
     mine, other = pair_sum(part, ("tiles",))
     second = call(
-        functools.partial(last_mapped_body, blocks_here, coded),
+        functools.partial(last_mapped_body, blocks_here),
         block_shape,
         [me, inverse, mine, other, gram_terms[1]],
         smem_in=(0,),

time: 90.9 us -> 91.4 us (level)
  waiting for transfers between devices: 36.6 us -> 32 us
  local copies, waits for them, and re-layouts: 2.71 us -> 5.06 us
  starting transfers between devices: 33 us -> 34.2 us
    ppermute x25, waiting for transfers between devices: 23.9 us -> 20.1 us  [shift_by(): lax.ppermute(value, axes, [(i, (i + shift) % size) for i in range(size)])]
    unnamed x6 -> x12, local copies, waits for them, and re-layouts: 1.42 us -> 3.78 us
    ppermute x25, starting transfers between devices: 26 us -> 27.6 us  [shift_by(): lax.ppermute(value, axes, [(i, (i + shift) % size) for i in range(size)])]
    pallas_call x15 -> x17, Pallas kernels: 16.9 us -> 17.6 us  [call(): pl.pallas_call(body, out_shape=shapes, in_specs=[SMEM if i in smem_in els...]
  transfers between devices with their start and end apart: 30 -> 30, of which waited for: 14 -> 14; matrix products, arithmetic and copies ran while one was open for 1% -> 1% of each run, Pallas kernels for 6% -> 8%
where the time goes in v11:
time: 91.4 us; the launch traced here: 91.1 us
  starting transfers between devices  34.2 us (37%)
  waiting for transfers between devices  32 us (35%)
  Pallas kernels  17.6 us (19%)
  local copies, waits for them, and re-layouts  5.06 us (6%)
  between operations  1.49 us (2%)
    ppermute x25, starting transfers between devices, shift_by(): lax.ppermute(value, axes, [(i, (i + shift) % size) for i in range(size)])  27.6 us
    ppermute x25, waiting for transfers between devices, shift_by(): lax.ppermute(value, axes, [(i, (i + shift) % size) for i in range(size)])  20.1 us
    pallas_call x17, Pallas kernels, call(): pl.pallas_call(body, out_shape=shapes, in_specs=[SMEM if i in smem_in els...  17.6 us
    ppermute x5, waiting for transfers between devices, pair_step(): lax.ppermute(value, name, [(i, i ^ flip) for i in range(lax.axis_size(nam...  11.9 us
    ppermute x5, starting transfers between devices, pair_step(): lax.ppermute(value, name, [(i, i ^ flip) for i in range(lax.axis_size(nam...  6.56 us
    unnamed x12, local copies, waits for them, and re-layouts  3.78 us
  transfers between devices with their start and end apart: 30, of which 14 were waited for; matrix products, arithmetic and copies ran while one was open for 1% of the time, Pallas kernels for 8%

profile of v11, /device:TPU:0, one launch (start us, length us, event | category | flops | bytes accessed | tf_op | source)
XLA Modules:
  0.0 91.1 jit_solution(3910009065451503622)
XLA Ops:
  2.0 3.0 %collective-permute-start = (s32[3,8]{1,0:T(4,128)S(1)}, s32[3,8]{1,0:T(4,128)S(1)}, u32[]{:S(2)}, u32[]{:S(2)}) collective-permute-start(s32[3,8]{1,0:T(4,128)S(1)} %concatenate.3.refs_0_), channel_id=1, source_target_pairs={{0,4},{4,8},{8,12},{12,0},{1,5},{5,9},{9,13},{13,1},{2,6},{6,10},{... | collective-permute-start | bytes 296 | tf_op jit(solution)/shard_map/ppermute | solution.py:521
  5.0 2.6 %collective-permute-start.1 = (s32[3,8]{1,0:T(4,128)S(1)}, s32[3,8]{1,0:T(4,128)S(1)}, u32[]{:S(2)}, u32[]{:S(2)}) collective-permute-start(s32[3,8]{1,0:T(4,128)S(1)} %concatenate.3.refs_0_), channel_id=1, source_target_pairs={{0,8},{4,12},{8,0},{12,4},{1,9},{5,13},{9,1},{13,5},{2,10},{6,14},... | collective-permute-start | bytes 296 | tf_op jit(solution)/shard_map/ppermute | solution.py:521
  7.6 1.3 %collective-permute-start.2 = (s32[3,8]{1,0:T(4,128)S(1)}, s32[3,8]{1,0:T(4,128)S(1)}, u32[]{:S(2)}, u32[]{:S(2)}) collective-permute-start(s32[3,8]{1,0:T(4,128)S(1)} %concatenate.3.refs_0_), channel_id=1, source_target_pairs={{0,12},{4,0},{8,4},{12,8},{1,13},{5,1},{9,5},{13,9},{2,14},{6,2},{... | collective-permute-start | bytes 296 | tf_op jit(solution)/shard_map/ppermute | solution.py:521
  9.0 1.4 %copy-done = bf16[2048,384]{1,0:T(8,128)(2,1)S(1)} copy-done((bf16[2048,384]{1,0:T(8,128)(2,1)S(1)}, bf16[2048,384]{1,0:T(8,128)(2,1)}, u32[]{:S(2)}) %copy-start) | copy-done | bytes 1572888
  11.5 1.8 %shard_map.60 = (s32[6,8]{1,0:T(8,128)S(1)}, bf16[256,384]{1,0:T(8,128)(2,1)S(1)}, bf16[256,384]{1,0:T(8,128)(2,1)S(1)}, bf16[256,384]{1,0:T(8,128)(2,1)S(1)}) custom-call(s32[3]{0:T(128)S(1)} %pad_add_fusion.me, s32[3,8]{1,0:T(4,128)S(1)} %concatenate.3.refs_0_, s32[3,8]{1,0:T(4,128)S(1)} %collective-permute-done.refs_1_, ...), custom_call_target="tpu_custom_call" | custom-call | tf_op jit(solution)/shard_map/pallas_call | solution.py:28
  13.3 2.9 %collective-permute-start.3 = (bf16[256,384]{1,0:T(8,128)(2,1)S(1)}, bf16[256,384]{1,0:T(8,128)(2,1)S(1)}, u32[]{:S(2)}, u32[]{:S(2)}) collective-permute-start(bf16[256,384]{1,0:T(8,128)(2,1)S(1)} %get-tuple-element.30), channel_id=1, source_target_pairs={{0,12},{4,0},{8,4},{12,8},{1,13},{5,1},{9,5},{13,9},{2,14},{6,2},{... | collective-permute-start | bytes 589832 | tf_op jit(solution)/shard_map/ppermute | solution.py:521
  17.2 4.4 %collective-permute-done.3.refs_0_ = bf16[256,384]{1,0:T(8,128)(2,1)S(1)} collective-permute-done((bf16[256,384]{1,0:T(8,128)(2,1)S(1)}, bf16[256,384]{1,0:T(8,128)(2,1)S(1)}, u32[]{:S(2)}, u32[]{:S(2)}) %collective-permute-start.3) | collective-permute-done | bytes 196640 | tf_op jit(solution)/shard_map/ppermute | solution.py:521
  21.6 10.3 %collective-permute-done.4.refs_1_ = bf16[256,384]{1,0:T(8,128)(2,1)S(1)} collective-permute-done((bf16[256,384]{1,0:T(8,128)(2,1)S(1)}, bf16[256,384]{1,0:T(8,128)(2,1)S(1)}, u32[]{:S(2)}, u32[]{:S(2)}) %collective-permute-start.4) | collective-permute-done | bytes 196640 | tf_op jit(solution)/shard_map/ppermute | solution.py:521
  33.4 1.5 %collective-permute-done.6.other = f32[1024,128]{1,0:T(8,128)S(1)} collective-permute-done((f32[1024,128]{1,0:T(8,128)S(1)}, f32[1024,128]{1,0:T(8,128)S(1)}, u32[]{:S(2)}, u32[]{:S(2)}) %collective-permute-start.6) | collective-permute-done | bytes 524320 | tf_op jit(solution)/shard_map/ppermute | solution.py:521
  36.0 2.0 %collective-permute-start.8 = (f32[64,128]{1,0:T(8,128)S(1)}, f32[64,128]{1,0:T(8,128)S(1)}, u32[]{:S(2)}, u32[]{:S(2)}) collective-permute-start(f32[64,128]{1,0:T(8,128)S(1)} %get-tuple-element.37), channel_id=1, source_target_pairs={{0,4},{4,8},{8,12},{12,0},{1,5},{5,9},{9,13},{13,1},{2,6},{6,10},{... | collective-permute-start | bytes 98312 | tf_op jit(solution)/shard_map/ppermute | solution.py:521
  38.0 2.0 %collective-permute-start.9 = (f32[64,128]{1,0:T(8,128)S(1)}, f32[64,128]{1,0:T(8,128)S(1)}, u32[]{:S(2)}, u32[]{:S(2)}) collective-permute-start(f32[64,128]{1,0:T(8,128)S(1)} %get-tuple-element.37), channel_id=1, source_target_pairs={{0,8},{4,12},{8,0},{12,4},{1,9},{5,13},{9,1},{13,5},{2,10},{6,14},... | collective-permute-start | bytes 98312 | tf_op jit(solution)/shard_map/ppermute | solution.py:521
  40.4 1.1 %collective-permute-start.13 = (s16[272,128]{1,0:T(8,128)(2,1)S(1)}, s16[272,128]{1,0:T(8,128)(2,1)S(1)}, u32[]{:S(2)}, u32[]{:S(2)}) collective-permute-start(s16[272,128]{1,0:T(8,128)(2,1)S(1)} %get-tuple-element.44), channel_id=1, source_target_pairs={{0,8},{4,12},{8,0},{12,4},{1,9},{5,13},{9,1},{13,5},{2,10},{6,14},... | collective-permute-start | bytes 208904 | tf_op jit(solution)/shard_map/ppermute | solution.py:521
  41.5 2.3 %collective-permute-start.14 = (s16[272,128]{1,0:T(8,128)(2,1)S(1)}, s16[272,128]{1,0:T(8,128)(2,1)S(1)}, u32[]{:S(2)}, u32[]{:S(2)}) collective-permute-start(s16[272,128]{1,0:T(8,128)(2,1)S(1)} %get-tuple-element.45), channel_id=1, source_target_pairs={{0,12},{4,0},{8,4},{12,8},{1,13},{5,1},{9,5},{13,9},{2,14},{6,2},{... | collective-permute-start | bytes 208904 | tf_op jit(solution)/shard_map/ppermute | solution.py:521
  43.9 1.5 %collective-permute-start.11 = (f32[64,128]{1,0:T(8,128)S(1)}, f32[64,128]{1,0:T(8,128)S(1)}, u32[]{:S(2)}, u32[]{:S(2)}) collective-permute-start(f32[64,128]{1,0:T(8,128)S(1)} %add_add_fusion.mine), channel_id=1, source_target_pairs={{0,2},{2,0},{1,3},{3,1},{4,6},{6,4},{5,7},{7,5},{8,10},{10,8},{9,1... | collective-permute-start | bytes 98312 | tf_op jit(solution)/shard_map/ppermute | solution.py:529
  45.4 2.4 %collective-permute-done.11.other.refs_3_ = f32[64,128]{1,0:T(8,128)S(1)} collective-permute-done((f32[64,128]{1,0:T(8,128)S(1)}, f32[64,128]{1,0:T(8,128)S(1)}, u32[]{:S(2)}, u32[]{:S(2)}) %collective-permute-start.11) | collective-permute-done | bytes 32800 | tf_op jit(solution)/shard_map/ppermute | solution.py:529
  51.2 1.5 %collective-permute-start.18 = (s16[32,2176]{1,0:T(8,128)(2,1)S(1)}, s16[32,2176]{1,0:T(8,128)(2,1)S(1)}, u32[]{:S(2)}, u32[]{:S(2)}) collective-permute-start(s16[32,2176]{1,0:T(8,128)(2,1)S(1)} %shard_map.68.mine), channel_id=1, source_target_pairs={{0,2},{2,0},{1,3},{3,1},{4,6},{6,4},{5,7},{7,5},{8,10},{10,8},{9,1... | collective-permute-start | bytes 417800 | tf_op jit(solution)/shard_map/ppermute | solution.py:529
  52.8 4.3 %collective-permute-done.18.other = s16[32,2176]{1,0:T(8,128)(2,1)S(1)} collective-permute-done((s16[32,2176]{1,0:T(8,128)(2,1)S(1)}, s16[32,2176]{1,0:T(8,128)(2,1)S(1)}, u32[]{:S(2)}, u32[]{:S(2)}) %collective-permute-start.18) | collective-permute-done | bytes 139296 | tf_op jit(solution)/shard_map/ppermute | solution.py:529
  58.0 1.5 %collective-permute-start.20 = (s16[144,128]{1,0:T(8,128)(2,1)S(1)}, s16[144,128]{1,0:T(8,128)(2,1)S(1)}, u32[]{:S(2)}, u32[]{:S(2)}) collective-permute-start(s16[144,128]{1,0:T(8,128)(2,1)S(1)} %get-tuple-element.50), channel_id=1, source_target_pairs={{0,4},{4,8},{8,12},{12,0},{1,5},{5,9},{9,13},{13,1},{2,6},{6,10},{... | collective-permute-start | bytes 110600 | tf_op jit(solution)/shard_map/ppermute | solution.py:521
  59.4 1.6 %collective-permute-start.21 = (s16[144,128]{1,0:T(8,128)(2,1)S(1)}, s16[144,128]{1,0:T(8,128)(2,1)S(1)}, u32[]{:S(2)}, u32[]{:S(2)}) collective-permute-start(s16[144,128]{1,0:T(8,128)(2,1)S(1)} %get-tuple-element.51), channel_id=1, source_target_pairs={{0,8},{4,12},{8,0},{12,4},{1,9},{5,13},{9,1},{13,5},{2,10},{6,14},... | collective-permute-start | bytes 110600 | tf_op jit(solution)/shard_map/ppermute | solution.py:521
  61.1 1.4 %collective-permute-start.22 = (s16[144,128]{1,0:T(8,128)(2,1)S(1)}, s16[144,128]{1,0:T(8,128)(2,1)S(1)}, u32[]{:S(2)}, u32[]{:S(2)}) collective-permute-start(s16[144,128]{1,0:T(8,128)(2,1)S(1)} %get-tuple-element.52), channel_id=1, source_target_pairs={{0,12},{4,0},{8,4},{12,8},{1,13},{5,1},{9,5},{13,9},{2,14},{6,2},{... | collective-permute-start | bytes 110600 | tf_op jit(solution)/shard_map/ppermute | solution.py:521
  64.2 1.1 %collective-permute-done.21.refs_7_ = s16[144,128]{1,0:T(8,128)(2,1)S(1)} collective-permute-done((s16[144,128]{1,0:T(8,128)(2,1)S(1)}, s16[144,128]{1,0:T(8,128)(2,1)S(1)}, u32[]{:S(2)}, u32[]{:S(2)}) %collective-permute-start.21) | collective-permute-done | bytes 36896 | tf_op jit(solution)/shard_map/ppermute | solution.py:521
  67.9 1.5 %collective-permute-start.24 = (f32[32,2048]{1,0:T(8,128)}, f32[32,2048]{1,0:T(8,128)S(1)}, u32[]{:S(2)}, u32[]{:S(2)}) collective-permute-start(f32[32,2048]{1,0:T(8,128)} %shard_map.72.mine), channel_id=1, source_target_pairs={{0,2},{2,0},{1,3},{3,1},{4,6},{6,4},{5,7},{7,5},{8,10},{10,8},{9,1... | collective-permute-start | bytes 786440 | tf_op jit(solution)/shard_map/ppermute | solution.py:529
  69.4 1.4 %collective-permute-start.25 = (f32[32,128]{1,0:T(8,128)}, f32[32,128]{1,0:T(8,128)S(1)}, u32[]{:S(2)}, u32[]{:S(2)}) collective-permute-start(f32[32,128]{1,0:T(8,128)} %add.20.after.refs_0_), channel_id=1, source_target_pairs={{0,8},{4,12},{8,0},{12,4},{1,9},{5,13},{9,1},{13,5},{2,10},{6,14},... | collective-permute-start | bytes 49160 | tf_op jit(solution)/shard_map/ppermute | solution.py:529
  70.8 3.5 %collective-permute-done.25.after.refs_1_ = f32[32,128]{1,0:T(8,128)S(1)} collective-permute-done((f32[32,128]{1,0:T(8,128)}, f32[32,128]{1,0:T(8,128)S(1)}, u32[]{:S(2)}, u32[]{:S(2)}) %collective-permute-start.25) | collective-permute-done | bytes 16416 | tf_op jit(solution)/shard_map/ppermute | solution.py:529
  74.3 1.7 %collective-permute-done.24.other = f32[32,2048]{1,0:T(8,128)S(1)} collective-permute-done((f32[32,2048]{1,0:T(8,128)}, f32[32,2048]{1,0:T(8,128)S(1)}, u32[]{:S(2)}, u32[]{:S(2)}) %collective-permute-start.24) | collective-permute-done | bytes 262176 | tf_op jit(solution)/shard_map/ppermute | solution.py:529
  78.3 1.9 %shard_map.74.factor = f32[64,64]{1,0:T(8,128)S(1)} custom-call(f32[32,2048]{1,0:T(8,128)S(1)} %shard_map.73.after.own, f32[32,128]{1,0:T(8,128)S(1)} %copy-done.5, f32[32,128]{1,0:T(8,128)S(1)} %collective-permute-done.25.after.refs_1_), custom_call_target="tpu_custom_call" | custom-call | tf_op jit(solution)/shard_map/pallas_call | solution.py:28
  80.3 1.4 %shard_map.75 = (bf16[128,2048]{1,0:T(8,128)(2,1)S(1)}, f32[32,128]{1,0:T(8,128)S(1)}) custom-call(s32[3]{0:T(128)S(1)} %pad_add_fusion.me, f32[64,64]{1,0:T(8,128)S(1)} %shard_map.74.factor, f32[32,2048]{1,0:T(8,128)S(1)} %shard_map.73.after.own, f32[32,2048]{1,0:T(8,128)S(1)} %collective-permute-done.26.other), custom_call_target="tpu_custom_call" | custom-call | tf_op jit(solution)/shard_map/pallas_call | solution.py:28
  81.6 1.2 %collective-permute-start.27 = (f32[32,128]{1,0:T(8,128)S(1)}, f32[32,128]{1,0:T(8,128)S(1)}, u32[]{:S(2)}, u32[]{:S(2)}) collective-permute-start(f32[32,128]{1,0:T(8,128)S(1)} %get-tuple-element.54.refs_0_), channel_id=1, source_target_pairs={{0,4},{4,8},{8,12},{12,0},{1,5},{5,9},{9,13},{13,1},{2,6},{6,10},{... | collective-permute-start | bytes 49160 | tf_op jit(solution)/shard_map/ppermute | solution.py:521
  82.8 1.1 %collective-permute-start.28 = (f32[32,128]{1,0:T(8,128)S(1)}, f32[32,128]{1,0:T(8,128)S(1)}, u32[]{:S(2)}, u32[]{:S(2)}) collective-permute-start(f32[32,128]{1,0:T(8,128)S(1)} %get-tuple-element.54.refs_0_), channel_id=1, source_target_pairs={{0,8},{4,12},{8,0},{12,4},{1,9},{5,13},{9,1},{13,5},{2,10},{6,14},... | collective-permute-start | bytes 49160 | tf_op jit(solution)/shard_map/ppermute | solution.py:521
  84.0 1.5 %collective-permute-start.29 = (f32[32,128]{1,0:T(8,128)S(1)}, f32[32,128]{1,0:T(8,128)S(1)}, u32[]{:S(2)}, u32[]{:S(2)}) collective-permute-start(f32[32,128]{1,0:T(8,128)S(1)} %get-tuple-element.54.refs_0_), channel_id=1, source_target_pairs={{0,12},{4,0},{8,4},{12,8},{1,13},{5,1},{9,5},{13,9},{2,14},{6,2},{... | collective-permute-start | bytes 49160 | tf_op jit(solution)/shard_map/ppermute | solution.py:521
  86.1 1.1 %collective-permute-done.27.refs_1_ = f32[32,128]{1,0:T(8,128)S(1)} collective-permute-done((f32[32,128]{1,0:T(8,128)S(1)}, f32[32,128]{1,0:T(8,128)S(1)}, u32[]{:S(2)}, u32[]{:S(2)}) %collective-permute-start.27) | collective-permute-done | bytes 16416 | tf_op jit(solution)/shard_map/ppermute | solution.py:521
  87.7 3.4 %shard_map.76 = f32[32,2048]{1,0:T(8,128)} custom-call(s32[3]{0:T(128)S(1)} %pad_add_fusion.me, bf16[128,2048]{1,0:T(8,128)(2,1)S(1)} %get-tuple-element.53.mapped, f32[32,128]{1,0:T(8,128)S(1)} %get-tuple-element.54.refs_0_, f32[32,128]{1,0:T(8,128)S(1)} %collective-permute-done.27.refs_1_, f32[32,128]{1,0:T(8,128)S(1)} %collective-permute-done.28.refs_2_, ...), custom_call_target="tpu_custom_call" | custom-call | tf_op jit(solution)/shard_map/pallas_call | solution.py:28
  (63 shorter events, 17.8 us)
Async XLA Ops:
  2.0 9.5 %collective-permute-start = (s32[3,8]{1,0:T(4,128)S(1)}, s32[3,8]{1,0:T(4,128)S(1)}, u32[]{:S(2)}, u32[]{:S(2)}) collective-permute-start(s32[3,8]{1,0:T(4,128)S(1)} %concatenate.3.refs_0_), channel_id=1, source_target_pairs={{0,4},{4,8},{8,12},{12,0},{1,5},{5,9},{9,13},{13,1},{2,6},{6,10},{... | collective-permute-start | bytes 296 | tf_op jit(solution)/shard_map/ppermute | solution.py:521
  5.0 6.5 %collective-permute-start.1 = (s32[3,8]{1,0:T(4,128)S(1)}, s32[3,8]{1,0:T(4,128)S(1)}, u32[]{:S(2)}, u32[]{:S(2)}) collective-permute-start(s32[3,8]{1,0:T(4,128)S(1)} %concatenate.3.refs_0_), channel_id=1, source_target_pairs={{0,8},{4,12},{8,0},{12,4},{1,9},{5,13},{9,1},{13,5},{2,10},{6,14},... | collective-permute-start | bytes 296 | tf_op jit(solution)/shard_map/ppermute | solution.py:521
  7.6 3.9 %collective-permute-start.2 = (s32[3,8]{1,0:T(4,128)S(1)}, s32[3,8]{1,0:T(4,128)S(1)}, u32[]{:S(2)}, u32[]{:S(2)}) collective-permute-start(s32[3,8]{1,0:T(4,128)S(1)} %concatenate.3.refs_0_), channel_id=1, source_target_pairs={{0,12},{4,0},{8,4},{12,8},{1,13},{5,1},{9,5},{13,9},{2,14},{6,2},{... | collective-permute-start | bytes 296 | tf_op jit(solution)/shard_map/ppermute | solution.py:521
  11.4 5.4 %copy-start.1 = (bf16[2048,384]{1,0:T(8,128)(2,1)S(1)}, bf16[2048,384]{1,0:T(8,128)(2,1)}, u32[]{:S(2)}) copy-start(bf16[2048,384]{1,0:T(8,128)(2,1)} %emb.5) | copy-start | bytes 4718596
  13.3 8.3 %collective-permute-start.3 = (bf16[256,384]{1,0:T(8,128)(2,1)S(1)}, bf16[256,384]{1,0:T(8,128)(2,1)S(1)}, u32[]{:S(2)}, u32[]{:S(2)}) collective-permute-start(bf16[256,384]{1,0:T(8,128)(2,1)S(1)} %get-tuple-element.30), channel_id=1, source_target_pairs={{0,12},{4,0},{8,4},{12,8},{1,13},{5,1},{9,5},{13,9},{2,14},{6,2},{... | collective-permute-start | bytes 589832 | tf_op jit(solution)/shard_map/ppermute | solution.py:521
  16.2 15.7 %collective-permute-start.4 = (bf16[256,384]{1,0:T(8,128)(2,1)S(1)}, bf16[256,384]{1,0:T(8,128)(2,1)S(1)}, u32[]{:S(2)}, u32[]{:S(2)}) collective-permute-start(bf16[256,384]{1,0:T(8,128)(2,1)S(1)} %get-tuple-element.31), channel_id=1, source_target_pairs={{0,8},{4,12},{8,0},{12,4},{1,9},{5,13},{9,1},{13,5},{2,10},{6,14},... | collective-permute-start | bytes 589832 | tf_op jit(solution)/shard_map/ppermute | solution.py:521
  16.2 15.7 %collective-permute-start.5 = (bf16[256,384]{1,0:T(8,128)(2,1)S(1)}, bf16[256,384]{1,0:T(8,128)(2,1)S(1)}, u32[]{:S(2)}, u32[]{:S(2)}) collective-permute-start(bf16[256,384]{1,0:T(8,128)(2,1)S(1)} %get-tuple-element.32), channel_id=1, source_target_pairs={{0,4},{4,8},{8,12},{12,0},{1,5},{5,9},{9,13},{13,1},{2,6},{6,10},{... | collective-permute-start | bytes 589832 | tf_op jit(solution)/shard_map/ppermute | solution.py:521
  16.8 16.4 %collective-permute-start.7 = (f32[1024,128]{1,0:T(8,128)S(1)}, f32[1024,128]{1,0:T(8,128)S(1)}, u32[]{:S(2)}, u32[]{:S(2)}) collective-permute-start(f32[1024,128]{1,0:T(8,128)S(1)} %shard_map.59.refs_5_.mine), channel_id=1, source_target_pairs={{0,1},{1,0},{2,3},{3,2},{4,5},{5,4},{6,7},{7,6},{8,9},{9,8},{10,11... | collective-permute-start | bytes 1572872 | tf_op jit(solution)/shard_map/ppermute | solution.py:521
  17.2 15.9 %copy-start.4 = (f32[2048,32]{0,1:T(8,128)S(1)}, f32[2048,32]{0,1:T(8,128)}, u32[]{:S(2)}) copy-start(f32[2048,32]{0,1:T(8,128)} %param.5) | copy-start | bytes 786436
  33.0 2.0 %collective-permute-start.6 = (f32[1024,128]{1,0:T(8,128)S(1)}, f32[1024,128]{1,0:T(8,128)S(1)}, u32[]{:S(2)}, u32[]{:S(2)}) collective-permute-start(f32[1024,128]{1,0:T(8,128)S(1)} %shard_map.62.mine), channel_id=1, source_target_pairs={{0,1},{1,0},{2,3},{3,2},{4,5},{5,4},{6,7},{7,6},{8,9},{9,8},{10,11... | collective-permute-start | bytes 1572872 | tf_op jit(solution)/shard_map/ppermute | solution.py:521
  35.9 5.6 %collective-permute-start.10 = (f32[64,128]{1,0:T(8,128)S(1)}, f32[64,128]{1,0:T(8,128)S(1)}, u32[]{:S(2)}, u32[]{:S(2)}) collective-permute-start(f32[64,128]{1,0:T(8,128)S(1)} %get-tuple-element.37), channel_id=1, source_target_pairs={{0,12},{4,0},{8,4},{12,8},{1,13},{5,1},{9,5},{13,9},{2,14},{6,2},{... | collective-permute-start | bytes 98312 | tf_op jit(solution)/shard_map/ppermute | solution.py:521
  36.0 7.9 %collective-permute-start.8 = (f32[64,128]{1,0:T(8,128)S(1)}, f32[64,128]{1,0:T(8,128)S(1)}, u32[]{:S(2)}, u32[]{:S(2)}) collective-permute-start(f32[64,128]{1,0:T(8,128)S(1)} %get-tuple-element.37), channel_id=1, source_target_pairs={{0,4},{4,8},{8,12},{12,0},{1,5},{5,9},{9,13},{13,1},{2,6},{6,10},{... | collective-permute-start | bytes 98312 | tf_op jit(solution)/shard_map/ppermute | solution.py:521
  38.0 5.9 %collective-permute-start.9 = (f32[64,128]{1,0:T(8,128)S(1)}, f32[64,128]{1,0:T(8,128)S(1)}, u32[]{:S(2)}, u32[]{:S(2)}) collective-permute-start(f32[64,128]{1,0:T(8,128)S(1)} %get-tuple-element.37), channel_id=1, source_target_pairs={{0,8},{4,12},{8,0},{12,4},{1,9},{5,13},{9,1},{13,5},{2,10},{6,14},... | collective-permute-start | bytes 98312 | tf_op jit(solution)/shard_map/ppermute | solution.py:521
  40.0 7.9 %collective-permute-start.12 = (s16[272,128]{1,0:T(8,128)(2,1)S(1)}, s16[272,128]{1,0:T(8,128)(2,1)S(1)}, u32[]{:S(2)}, u32[]{:S(2)}) collective-permute-start(s16[272,128]{1,0:T(8,128)(2,1)S(1)} %get-tuple-element.43), channel_id=1, source_target_pairs={{0,4},{4,8},{8,12},{12,0},{1,5},{5,9},{9,13},{13,1},{2,6},{6,10},{... | collective-permute-start | bytes 208904 | tf_op jit(solution)/shard_map/ppermute | solution.py:521
  40.4 7.9 %collective-permute-start.13 = (s16[272,128]{1,0:T(8,128)(2,1)S(1)}, s16[272,128]{1,0:T(8,128)(2,1)S(1)}, u32[]{:S(2)}, u32[]{:S(2)}) collective-permute-start(s16[272,128]{1,0:T(8,128)(2,1)S(1)} %get-tuple-element.44), channel_id=1, source_target_pairs={{0,8},{4,12},{8,0},{12,4},{1,9},{5,13},{9,1},{13,5},{2,10},{6,14},... | collective-permute-start | bytes 208904 | tf_op jit(solution)/shard_map/ppermute | solution.py:521
  41.5 6.8 %collective-permute-start.14 = (s16[272,128]{1,0:T(8,128)(2,1)S(1)}, s16[272,128]{1,0:T(8,128)(2,1)S(1)}, u32[]{:S(2)}, u32[]{:S(2)}) collective-permute-start(s16[272,128]{1,0:T(8,128)(2,1)S(1)} %get-tuple-element.45), channel_id=1, source_target_pairs={{0,12},{4,0},{8,4},{12,8},{1,13},{5,1},{9,5},{13,9},{2,14},{6,2},{... | collective-permute-start | bytes 208904 | tf_op jit(solution)/shard_map/ppermute | solution.py:521
  43.9 4.0 %collective-permute-start.11 = (f32[64,128]{1,0:T(8,128)S(1)}, f32[64,128]{1,0:T(8,128)S(1)}, u32[]{:S(2)}, u32[]{:S(2)}) collective-permute-start(f32[64,128]{1,0:T(8,128)S(1)} %add_add_fusion.mine), channel_id=1, source_target_pairs={{0,2},{2,0},{1,3},{3,1},{4,6},{6,4},{5,7},{7,5},{8,10},{10,8},{9,1... | collective-permute-start | bytes 98312 | tf_op jit(solution)/shard_map/ppermute | solution.py:529
  48.4 1.5 %collective-permute-start.15 = (bf16[1,256,128]{2,1,0:T(8,128)(2,1)S(1)}, bf16[1,256,128]{2,1,0:T(8,128)(2,1)S(1)}, u32[]{:S(2)}, u32[]{:S(2)}) collective-permute-start(bf16[1,256,128]{2,1,0:T(8,128)(2,1)S(1)} %get-tuple-element.46.refs_0_), channel_id=1, source_target_pairs={{0,1},{1,0},{2,3},{3,2},{4,5},{5,4},{6,7},{7,6},{8,9},{9,8},{10,11... | collective-permute-start | bytes 196616 | tf_op jit(solution)/shard_map/ppermute | solution.py:521
  48.4 1.5 %collective-permute-start.16 = (bf16[1,256,128]{2,1,0:T(8,128)(2,1)S(1)}, bf16[1,256,128]{2,1,0:T(8,128)(2,1)S(1)}, u32[]{:S(2)}, u32[]{:S(2)}) collective-permute-start(bf16[1,256,128]{2,1,0:T(8,128)(2,1)S(1)} %get-tuple-element.47.refs_1_), channel_id=1, source_target_pairs={{0,1},{1,0},{2,3},{3,2},{4,5},{5,4},{6,7},{7,6},{8,9},{9,8},{10,11... | collective-permute-start | bytes 196616 | tf_op jit(solution)/shard_map/ppermute | solution.py:521
  48.9 1.3 %collective-permute-start.17 = (bf16[1,256,128]{2,1,0:T(8,128)(2,1)S(1)}, bf16[1,256,128]{2,1,0:T(8,128)(2,1)S(1)}, u32[]{:S(2)}, u32[]{:S(2)}) collective-permute-start(bf16[1,256,128]{2,1,0:T(8,128)(2,1)S(1)} %get-tuple-element.48.refs_2_), channel_id=1, source_target_pairs={{0,1},{1,0},{2,3},{3,2},{4,5},{5,4},{6,7},{7,6},{8,9},{9,8},{10,11... | collective-permute-start | bytes 196616 | tf_op jit(solution)/shard_map/ppermute | solution.py:521
  51.2 5.8 %collective-permute-start.18 = (s16[32,2176]{1,0:T(8,128)(2,1)S(1)}, s16[32,2176]{1,0:T(8,128)(2,1)S(1)}, u32[]{:S(2)}, u32[]{:S(2)}) collective-permute-start(s16[32,2176]{1,0:T(8,128)(2,1)S(1)} %shard_map.68.mine), channel_id=1, source_target_pairs={{0,2},{2,0},{1,3},{3,1},{4,6},{6,4},{5,7},{7,5},{8,10},{10,8},{9,1... | collective-permute-start | bytes 417800 | tf_op jit(solution)/shard_map/ppermute | solution.py:529
  57.9 4.6 %collective-permute-start.19 = (f32[32,2048]{1,0:T(8,128)S(1)}, f32[32,2048]{1,0:T(8,128)S(1)}, u32[]{:S(2)}, u32[]{:S(2)}) collective-permute-start(f32[32,2048]{1,0:T(8,128)S(1)} %get-tuple-element.49.own), channel_id=1, source_target_pairs={{0,1},{1,0},{2,3},{3,2},{4,5},{5,4},{6,7},{7,6},{8,9},{9,8},{10,11... | collective-permute-start | bytes 786440 | tf_op jit(solution)/shard_map/ppermute | solution.py:521
  58.0 6.2 %collective-permute-start.20 = (s16[144,128]{1,0:T(8,128)(2,1)S(1)}, s16[144,128]{1,0:T(8,128)(2,1)S(1)}, u32[]{:S(2)}, u32[]{:S(2)}) collective-permute-start(s16[144,128]{1,0:T(8,128)(2,1)S(1)} %get-tuple-element.50), channel_id=1, source_target_pairs={{0,4},{4,8},{8,12},{12,0},{1,5},{5,9},{9,13},{13,1},{2,6},{6,10},{... | collective-permute-start | bytes 110600 | tf_op jit(solution)/shard_map/ppermute | solution.py:521
  59.4 5.9 %collective-permute-start.21 = (s16[144,128]{1,0:T(8,128)(2,1)S(1)}, s16[144,128]{1,0:T(8,128)(2,1)S(1)}, u32[]{:S(2)}, u32[]{:S(2)}) collective-permute-start(s16[144,128]{1,0:T(8,128)(2,1)S(1)} %get-tuple-element.51), channel_id=1, source_target_pairs={{0,8},{4,12},{8,0},{12,4},{1,9},{5,13},{9,1},{13,5},{2,10},{6,14},... | collective-permute-start | bytes 110600 | tf_op jit(solution)/shard_map/ppermute | solution.py:521
  61.1 4.6 %collective-permute-start.22 = (s16[144,128]{1,0:T(8,128)(2,1)S(1)}, s16[144,128]{1,0:T(8,128)(2,1)S(1)}, u32[]{:S(2)}, u32[]{:S(2)}) collective-permute-start(s16[144,128]{1,0:T(8,128)(2,1)S(1)} %get-tuple-element.52), channel_id=1, source_target_pairs={{0,12},{4,0},{8,4},{12,8},{1,13},{5,1},{9,5},{13,9},{2,14},{6,2},{... | collective-permute-start | bytes 110600 | tf_op jit(solution)/shard_map/ppermute | solution.py:521
  63.6 3.8 %collective-permute-start.23 = (f32[32,128]{1,0:T(8,128)S(1)}, f32[32,128]{1,0:T(8,128)S(1)}, u32[]{:S(2)}, u32[]{:S(2)}) collective-permute-start(f32[32,128]{1,0:T(8,128)S(1)} %shard_map.70.after), channel_id=1, source_target_pairs={{0,4},{4,0},{8,12},{12,8},{1,5},{5,1},{9,13},{13,9},{2,6},{6,2},{1... | collective-permute-start | bytes 49160 | tf_op jit(solution)/shard_map/ppermute | solution.py:529
  67.9 8.1 %collective-permute-start.24 = (f32[32,2048]{1,0:T(8,128)}, f32[32,2048]{1,0:T(8,128)S(1)}, u32[]{:S(2)}, u32[]{:S(2)}) collective-permute-start(f32[32,2048]{1,0:T(8,128)} %shard_map.72.mine), channel_id=1, source_target_pairs={{0,2},{2,0},{1,3},{3,1},{4,6},{6,4},{5,7},{7,5},{8,10},{10,8},{9,1... | collective-permute-start | bytes 786440 | tf_op jit(solution)/shard_map/ppermute | solution.py:529
  69.4 4.8 %collective-permute-start.25 = (f32[32,128]{1,0:T(8,128)}, f32[32,128]{1,0:T(8,128)S(1)}, u32[]{:S(2)}, u32[]{:S(2)}) collective-permute-start(f32[32,128]{1,0:T(8,128)} %add.20.after.refs_0_), channel_id=1, source_target_pairs={{0,8},{4,12},{8,0},{12,4},{1,9},{5,13},{9,1},{13,5},{2,10},{6,14},... | collective-permute-start | bytes 49160 | tf_op jit(solution)/shard_map/ppermute | solution.py:529
  77.5 2.7 %collective-permute-start.26 = (f32[32,2048]{1,0:T(8,128)S(1)}, f32[32,2048]{1,0:T(8,128)S(1)}, u32[]{:S(2)}, u32[]{:S(2)}) collective-permute-start(f32[32,2048]{1,0:T(8,128)S(1)} %shard_map.73.after.own), channel_id=1, source_target_pairs={{0,1},{1,0},{2,3},{3,2},{4,5},{5,4},{6,7},{7,6},{8,9},{9,8},{10,11... | collective-permute-start | bytes 786440 | tf_op jit(solution)/shard_map/ppermute | solution.py:521
  81.6 5.6 %collective-permute-start.27 = (f32[32,128]{1,0:T(8,128)S(1)}, f32[32,128]{1,0:T(8,128)S(1)}, u32[]{:S(2)}, u32[]{:S(2)}) collective-permute-start(f32[32,128]{1,0:T(8,128)S(1)} %get-tuple-element.54.refs_0_), channel_id=1, source_target_pairs={{0,4},{4,8},{8,12},{12,0},{1,5},{5,9},{9,13},{13,1},{2,6},{6,10},{... | collective-permute-start | bytes 49160 | tf_op jit(solution)/shard_map/ppermute | solution.py:521
  82.8 4.8 %collective-permute-start.28 = (f32[32,128]{1,0:T(8,128)S(1)}, f32[32,128]{1,0:T(8,128)S(1)}, u32[]{:S(2)}, u32[]{:S(2)}) collective-permute-start(f32[32,128]{1,0:T(8,128)S(1)} %get-tuple-element.54.refs_0_), channel_id=1, source_target_pairs={{0,8},{4,12},{8,0},{12,4},{1,9},{5,13},{9,1},{13,5},{2,10},{6,14},... | collective-permute-start | bytes 49160 | tf_op jit(solution)/shard_map/ppermute | solution.py:521
  84.0 3.8 %collective-permute-start.29 = (f32[32,128]{1,0:T(8,128)S(1)}, f32[32,128]{1,0:T(8,128)S(1)}, u32[]{:S(2)}, u32[]{:S(2)}) collective-permute-start(f32[32,128]{1,0:T(8,128)S(1)} %get-tuple-element.54.refs_0_), channel_id=1, source_target_pairs={{0,12},{4,0},{8,4},{12,8},{1,13},{5,1},{9,5},{13,9},{2,14},{6,2},{... | collective-permute-start | bytes 49160 | tf_op jit(solution)/shard_map/ppermute | solution.py:521
  (4 other events, 3.8 us)

commit v12 on v11

--- a/solution.py
+++ b/solution.py
@@ -116,11 +116,12 @@
     return jnp.concatenate([high, middle, low], axis=0)
 
 
-def gram(parts):
+def gram(parts, n):
     cross = lax.dot_general(parts, parts, NT, preferred_element_type=F32)
-    n = parts.shape[0] // 3
+    count = parts.shape[0] // n
+    pairs = sorted(((i, j) for i in range(count) for j in range(count)), key=lambda p: -p[0] - p[1])
     total = None
-    for i, j in ((2, 2), (1, 2), (2, 1), (0, 2), (2, 0), (1, 1), (0, 1), (1, 0), (0, 0)):
+    for i, j in pairs:
         piece = cross[i * n : (i + 1) * n, j * n : (j + 1) * n]
         total = piece if total is None else total + piece
     return total
@@ -148,7 +149,10 @@
         lines = [state[base + i : base + i + 1, :] for i in range(step)]
         pivot = [[columns[k][base + i : base + i + 1, :] for k in range(step)] for i in range(step)]
         for i in range(step):
-            reciprocal = 1.0 / pivot[i][i]
+            if i % 2 == 0:
+                first, cross, second = pivot[i][i], pivot[i][i + 1], pivot[i + 1][i + 1]
+                reciprocals = (1.0 / first, first / (first * second - cross * cross))
+            reciprocal = reciprocals[i % 2]
             scaled = lines[i] * reciprocal
             ratio = [pivot[i][k] * reciprocal for k in range(step)]
             for k in range(i + 1, step):
@@ -426,18 +430,8 @@
     apply_far(dims, me, idx, inverse, received, 0, near_tiles, sent, shared, out)
 
 
-def gate_body(value, after, out):
-    pass
-
-
-def gate(value, after):
-    return pl.pallas_call(
-        gate_body,
-        out_shape=sds(value.shape, value.dtype),
-        in_specs=[ANY, ANY],
-        out_specs=ANY,
-        input_output_aliases={0: 0},
-    )(value, after)
+def send_sum_body(coded, total, after, out):
+    put_sum(coded, total, out)
 
 
 def put_sum(coded, total, out):
@@ -479,8 +473,8 @@
         pick_columns(idx, k, row_count, capacity, codes, powers, parts, sends[k - 1], 0, ([], []))
 
 
-def last_mapped_body(blocks_here, me, inverse, mine, other, after, out):
-    take_sum(False, me, blocks_here, inverse, mine, other, out)
+def last_mapped_body(blocks_here, coded, me, inverse, mine, other, after, out):
+    take_sum(coded, me, blocks_here, inverse, mine, other, out)
 
 
 def folded(square):
@@ -495,7 +489,8 @@
 
 
 def gram_body(me, own, other, out):
-    out[...] = folded(gram(thirds(both_columns(me[2], own[...], other[...]))))
+    full = both_columns(me[2], own[...], other[...])
+    out[...] = folded(gram(pack(full), full.shape[0]))
 
 
 def factor_body(after, *refs):
@@ -506,7 +501,7 @@
     full = both_columns(me[2], own[...], other[...])
     parts = thirds(times(factor[...], pack(full)))
     mapped[...] = parts[: mapped.shape[0]]
-    out[...] = folded(gram(parts))
+    out[...] = folded(gram(parts, full.shape[0]))
 
 
 def final_body(me, mapped, *refs):
@@ -661,11 +656,11 @@
     steps = (row_count - 1).bit_length()
     for bit in range(steps - 1):
         first_gram = first_gram + pair_step(first_gram, "rows", 1 << bit)
-    part = gate(part, first_gram)
+    part = call(functools.partial(send_sum_body, coded), sum_shape, [part, first_gram])
     gram_terms = (first_gram, pair_step(first_gram, "rows", 1 << (steps - 1)))
     mine, other = pair_sum(part, ("tiles",))
     second = call(
-        functools.partial(last_mapped_body, blocks_here),
+        functools.partial(last_mapped_body, blocks_here, coded),
         block_shape,
         [me, inverse, mine, other, gram_terms[1]],
         smem_in=(0,),

time: 91.4 us -> 87.3 us (0.955)
  local copies, waits for them, and re-layouts: 5.06 us -> 2.71 us
  waiting for transfers between devices: 32 us -> 30.8 us
    unnamed x12 -> x6, local copies, waits for them, and re-layouts: 3.78 us -> 1.42 us
    ppermute x5, waiting for transfers between devices: 11.9 us -> 10.7 us  [pair_step(): lax.ppermute(value, name, [(i, i ^ flip) for i in range(lax.axis_size(nam...]
    pallas_call x17 -> x18, Pallas kernels: 17.6 us -> 17.4 us  [call(): pl.pallas_call(body, out_shape=shapes, in_specs=[SMEM if i in smem_in els...]
where the time goes in v12:
time: 87.3 us; the launch traced here: 87.1 us
  starting transfers between devices  34.7 us (40%)
  waiting for transfers between devices  30.8 us (35%)
  Pallas kernels  17.4 us (20%)
  local copies, waits for them, and re-layouts  2.71 us (3%)
  between operations  1.48 us (2%)
    ppermute x25, starting transfers between devices, shift_by(): lax.ppermute(value, axes, [(i, (i + shift) % size) for i in range(size)])  28 us
    ppermute x25, waiting for transfers between devices, shift_by(): lax.ppermute(value, axes, [(i, (i + shift) % size) for i in range(size)])  20.1 us
    pallas_call x18, Pallas kernels, call(): pl.pallas_call(body, out_shape=shapes, in_specs=[SMEM if i in smem_in els...  17.4 us
    ppermute x5, waiting for transfers between devices, pair_step(): lax.ppermute(value, name, [(i, i ^ flip) for i in range(lax.axis_size(nam...  10.7 us
    ppermute x5, starting transfers between devices, pair_step(): lax.ppermute(value, name, [(i, i ^ flip) for i in range(lax.axis_size(nam...  6.68 us
  transfers between devices with their start and end apart: 30, of which 14 were waited for; matrix products, arithmetic and copies ran while one was open for 1% of the time, Pallas kernels for 8%

profile of v12, /device:TPU:0, one launch (start us, length us, event | category | flops | bytes accessed | tf_op | source)
XLA Modules:
  0.0 87.1 jit_solution(17256508412432763475)
XLA Ops:
  2.0 3.0 %collective-permute-start = (s32[3,8]{1,0:T(4,128)S(1)}, s32[3,8]{1,0:T(4,128)S(1)}, u32[]{:S(2)}, u32[]{:S(2)}) collective-permute-start(s32[3,8]{1,0:T(4,128)S(1)} %concatenate.3.refs_0_), channel_id=1, source_target_pairs={{0,4},{4,8},{8,12},{12,0},{1,5},{5,9},{9,13},{13,1},{2,6},{6,10},{... | collective-permute-start | bytes 296 | tf_op jit(solution)/shard_map/ppermute | solution.py:516
  5.0 2.6 %collective-permute-start.1 = (s32[3,8]{1,0:T(4,128)S(1)}, s32[3,8]{1,0:T(4,128)S(1)}, u32[]{:S(2)}, u32[]{:S(2)}) collective-permute-start(s32[3,8]{1,0:T(4,128)S(1)} %concatenate.3.refs_0_), channel_id=1, source_target_pairs={{0,8},{4,12},{8,0},{12,4},{1,9},{5,13},{9,1},{13,5},{2,10},{6,14},... | collective-permute-start | bytes 296 | tf_op jit(solution)/shard_map/ppermute | solution.py:516
  7.6 1.3 %collective-permute-start.2 = (s32[3,8]{1,0:T(4,128)S(1)}, s32[3,8]{1,0:T(4,128)S(1)}, u32[]{:S(2)}, u32[]{:S(2)}) collective-permute-start(s32[3,8]{1,0:T(4,128)S(1)} %concatenate.3.refs_0_), channel_id=1, source_target_pairs={{0,12},{4,0},{8,4},{12,8},{1,13},{5,1},{9,5},{13,9},{2,14},{6,2},{... | collective-permute-start | bytes 296 | tf_op jit(solution)/shard_map/ppermute | solution.py:516
  9.0 1.4 %copy-done = bf16[2048,384]{1,0:T(8,128)(2,1)S(1)} copy-done((bf16[2048,384]{1,0:T(8,128)(2,1)S(1)}, bf16[2048,384]{1,0:T(8,128)(2,1)}, u32[]{:S(2)}) %copy-start) | copy-done | bytes 1572888
  10.4 1.0 %shard_map.59.refs_5_.mine = f32[1024,128]{1,0:T(8,128)S(1)} custom-call(s32[3]{0:T(128)S(1)} %pad_add_fusion.me, bf16[2048,384]{1,0:T(8,128)(2,1)S(1)} %copy-done), custom_call_target="tpu_custom_call" | custom-call | tf_op jit(solution)/shard_map/pallas_call | solution.py:28
  11.5 1.8 %shard_map.60 = (s32[6,8]{1,0:T(8,128)S(1)}, bf16[256,384]{1,0:T(8,128)(2,1)S(1)}, bf16[256,384]{1,0:T(8,128)(2,1)S(1)}, bf16[256,384]{1,0:T(8,128)(2,1)S(1)}) custom-call(s32[3]{0:T(128)S(1)} %pad_add_fusion.me, s32[3,8]{1,0:T(4,128)S(1)} %concatenate.3.refs_0_, s32[3,8]{1,0:T(4,128)S(1)} %collective-permute-done.refs_1_, ...), custom_call_target="tpu_custom_call" | custom-call | tf_op jit(solution)/shard_map/pallas_call | solution.py:28
  13.3 2.9 %collective-permute-start.3 = (bf16[256,384]{1,0:T(8,128)(2,1)S(1)}, bf16[256,384]{1,0:T(8,128)(2,1)S(1)}, u32[]{:S(2)}, u32[]{:S(2)}) collective-permute-start(bf16[256,384]{1,0:T(8,128)(2,1)S(1)} %get-tuple-element.30), channel_id=1, source_target_pairs={{0,12},{4,0},{8,4},{12,8},{1,13},{5,1},{9,5},{13,9},{2,14},{6,2},{... | collective-permute-start | bytes 589832 | tf_op jit(solution)/shard_map/ppermute | solution.py:516
  17.2 4.4 %collective-permute-done.3.refs_0_ = bf16[256,384]{1,0:T(8,128)(2,1)S(1)} collective-permute-done((bf16[256,384]{1,0:T(8,128)(2,1)S(1)}, bf16[256,384]{1,0:T(8,128)(2,1)S(1)}, u32[]{:S(2)}, u32[]{:S(2)}) %collective-permute-start.3) | collective-permute-done | bytes 196640 | tf_op jit(solution)/shard_map/ppermute | solution.py:516
  21.6 10.3 %collective-permute-done.4.refs_1_ = bf16[256,384]{1,0:T(8,128)(2,1)S(1)} collective-permute-done((bf16[256,384]{1,0:T(8,128)(2,1)S(1)}, bf16[256,384]{1,0:T(8,128)(2,1)S(1)}, u32[]{:S(2)}, u32[]{:S(2)}) %collective-permute-start.4) | collective-permute-done | bytes 196640 | tf_op jit(solution)/shard_map/ppermute | solution.py:516
  31.9 1.1 %shard_map.62.mine = f32[1024,128]{1,0:T(8,128)S(1)} custom-call(s32[6,8]{1,0:T(8,128)S(1)} %get-tuple-element.29.after.idx, bf16[2048,384]{1,0:T(8,128)(2,1)S(1)} %copy-done.1, f32[2048,128]{1,0:T(8,128)S(1)} %shard_map.61.own_squares, bf16[256,384]{1,0:T(8,128)(2,1)S(1)} %collective-permute-done.3.refs_0_, ...), custom_call_target="tpu_custom_call" | custom-call | tf_op jit(solution)/shard_map/pallas_call | solution.py:28
  33.4 1.5 %collective-permute-done.6.other = f32[1024,128]{1,0:T(8,128)S(1)} collective-permute-done((f32[1024,128]{1,0:T(8,128)S(1)}, f32[1024,128]{1,0:T(8,128)S(1)}, u32[]{:S(2)}, u32[]{:S(2)}) %collective-permute-start.6) | collective-permute-done | bytes 524320 | tf_op jit(solution)/shard_map/ppermute | solution.py:516
  36.0 2.0 %collective-permute-start.8 = (f32[64,128]{1,0:T(8,128)S(1)}, f32[64,128]{1,0:T(8,128)S(1)}, u32[]{:S(2)}, u32[]{:S(2)}) collective-permute-start(f32[64,128]{1,0:T(8,128)S(1)} %get-tuple-element.37), channel_id=1, source_target_pairs={{0,4},{4,8},{8,12},{12,0},{1,5},{5,9},{9,13},{13,1},{2,6},{6,10},{... | collective-permute-start | bytes 98312 | tf_op jit(solution)/shard_map/ppermute | solution.py:516
  38.0 2.0 %collective-permute-start.9 = (f32[64,128]{1,0:T(8,128)S(1)}, f32[64,128]{1,0:T(8,128)S(1)}, u32[]{:S(2)}, u32[]{:S(2)}) collective-permute-start(f32[64,128]{1,0:T(8,128)S(1)} %get-tuple-element.37), channel_id=1, source_target_pairs={{0,8},{4,12},{8,0},{12,4},{1,9},{5,13},{9,1},{13,5},{2,10},{6,14},... | collective-permute-start | bytes 98312 | tf_op jit(solution)/shard_map/ppermute | solution.py:516
  40.4 1.1 %collective-permute-start.13 = (s16[272,128]{1,0:T(8,128)(2,1)S(1)}, s16[272,128]{1,0:T(8,128)(2,1)S(1)}, u32[]{:S(2)}, u32[]{:S(2)}) collective-permute-start(s16[272,128]{1,0:T(8,128)(2,1)S(1)} %get-tuple-element.44), channel_id=1, source_target_pairs={{0,8},{4,12},{8,0},{12,4},{1,9},{5,13},{9,1},{13,5},{2,10},{6,14},... | collective-permute-start | bytes 208904 | tf_op jit(solution)/shard_map/ppermute | solution.py:516
  41.5 2.3 %collective-permute-start.14 = (s16[272,128]{1,0:T(8,128)(2,1)S(1)}, s16[272,128]{1,0:T(8,128)(2,1)S(1)}, u32[]{:S(2)}, u32[]{:S(2)}) collective-permute-start(s16[272,128]{1,0:T(8,128)(2,1)S(1)} %get-tuple-element.45), channel_id=1, source_target_pairs={{0,12},{4,0},{8,4},{12,8},{1,13},{5,1},{9,5},{13,9},{2,14},{6,2},{... | collective-permute-start | bytes 208904 | tf_op jit(solution)/shard_map/ppermute | solution.py:516
  43.9 1.5 %collective-permute-start.11 = (f32[64,128]{1,0:T(8,128)S(1)}, f32[64,128]{1,0:T(8,128)S(1)}, u32[]{:S(2)}, u32[]{:S(2)}) collective-permute-start(f32[64,128]{1,0:T(8,128)S(1)} %add_add_fusion.mine), channel_id=1, source_target_pairs={{0,2},{2,0},{1,3},{3,1},{4,6},{6,4},{5,7},{7,5},{8,10},{10,8},{9,1... | collective-permute-start | bytes 98312 | tf_op jit(solution)/shard_map/ppermute | solution.py:524
  45.4 2.4 %collective-permute-done.11.other.refs_3_ = f32[64,128]{1,0:T(8,128)S(1)} collective-permute-done((f32[64,128]{1,0:T(8,128)S(1)}, f32[64,128]{1,0:T(8,128)S(1)}, u32[]{:S(2)}, u32[]{:S(2)}) %collective-permute-start.11) | collective-permute-done | bytes 32800 | tf_op jit(solution)/shard_map/ppermute | solution.py:524
  50.2 1.0 %shard_map.68.mine = s16[32,2176]{1,0:T(8,128)(2,1)S(1)} custom-call(s32[3]{0:T(128)S(1)} %pad_add_fusion.me, s32[6,8]{1,0:T(8,128)S(1)} %get-tuple-element.29.after.idx, f32[64,128]{1,0:T(8,128)S(1)} %get-tuple-element.41.inverse, f32[32,2048]{1,0:T(8,128)S(1)} %get-tuple-element.42.started, bf16[8,256,128]{2,1,0:T(8,128)(2,1)S(1)} %get-tuple-element.38.near_tiles, ...), custom_call_target="tpu_custom_call" | custom-call | tf_op jit(solution)/shard_map/pallas_call | solution.py:28
  51.2 1.6 %collective-permute-start.18 = (s16[32,2176]{1,0:T(8,128)(2,1)S(1)}, s16[32,2176]{1,0:T(8,128)(2,1)S(1)}, u32[]{:S(2)}, u32[]{:S(2)}) collective-permute-start(s16[32,2176]{1,0:T(8,128)(2,1)S(1)} %shard_map.68.mine), channel_id=1, source_target_pairs={{0,2},{2,0},{1,3},{3,1},{4,6},{6,4},{5,7},{7,5},{8,10},{10,8},{9,1... | collective-permute-start | bytes 417800 | tf_op jit(solution)/shard_map/ppermute | solution.py:524
  52.8 4.3 %collective-permute-done.18.other = s16[32,2176]{1,0:T(8,128)(2,1)S(1)} collective-permute-done((s16[32,2176]{1,0:T(8,128)(2,1)S(1)}, s16[32,2176]{1,0:T(8,128)(2,1)S(1)}, u32[]{:S(2)}, u32[]{:S(2)}) %collective-permute-start.18) | collective-permute-done | bytes 139296 | tf_op jit(solution)/shard_map/ppermute | solution.py:524
  58.0 1.5 %collective-permute-start.20 = (s16[144,128]{1,0:T(8,128)(2,1)S(1)}, s16[144,128]{1,0:T(8,128)(2,1)S(1)}, u32[]{:S(2)}, u32[]{:S(2)}) collective-permute-start(s16[144,128]{1,0:T(8,128)(2,1)S(1)} %get-tuple-element.50), channel_id=1, source_target_pairs={{0,4},{4,8},{8,12},{12,0},{1,5},{5,9},{9,13},{13,1},{2,6},{6,10},{... | collective-permute-start | bytes 110600 | tf_op jit(solution)/shard_map/ppermute | solution.py:516
  59.4 1.6 %collective-permute-start.21 = (s16[144,128]{1,0:T(8,128)(2,1)S(1)}, s16[144,128]{1,0:T(8,128)(2,1)S(1)}, u32[]{:S(2)}, u32[]{:S(2)}) collective-permute-start(s16[144,128]{1,0:T(8,128)(2,1)S(1)} %get-tuple-element.51), channel_id=1, source_target_pairs={{0,8},{4,12},{8,0},{12,4},{1,9},{5,13},{9,1},{13,5},{2,10},{6,14},... | collective-permute-start | bytes 110600 | tf_op jit(solution)/shard_map/ppermute | solution.py:516
  61.0 1.4 %collective-permute-start.22 = (s16[144,128]{1,0:T(8,128)(2,1)S(1)}, s16[144,128]{1,0:T(8,128)(2,1)S(1)}, u32[]{:S(2)}, u32[]{:S(2)}) collective-permute-start(s16[144,128]{1,0:T(8,128)(2,1)S(1)} %get-tuple-element.52), channel_id=1, source_target_pairs={{0,12},{4,0},{8,4},{12,8},{1,13},{5,1},{9,5},{13,9},{2,14},{6,2},{... | collective-permute-start | bytes 110600 | tf_op jit(solution)/shard_map/ppermute | solution.py:516
  64.1 1.2 %collective-permute-done.21.refs_7_ = s16[144,128]{1,0:T(8,128)(2,1)S(1)} collective-permute-done((s16[144,128]{1,0:T(8,128)(2,1)S(1)}, s16[144,128]{1,0:T(8,128)(2,1)S(1)}, u32[]{:S(2)}, u32[]{:S(2)}) %collective-permute-start.21) | collective-permute-done | bytes 36896 | tf_op jit(solution)/shard_map/ppermute | solution.py:516
  67.4 1.6 %collective-permute-start.24 = (s16[32,2176]{1,0:T(8,128)(2,1)S(1)}, s16[32,2176]{1,0:T(8,128)(2,1)S(1)}, u32[]{:S(2)}, u32[]{:S(2)}) collective-permute-start(s16[32,2176]{1,0:T(8,128)(2,1)S(1)} %shard_map.72.mine), channel_id=1, source_target_pairs={{0,2},{2,0},{1,3},{3,1},{4,6},{6,4},{5,7},{7,5},{8,10},{10,8},{9,1... | collective-permute-start | bytes 417800 | tf_op jit(solution)/shard_map/ppermute | solution.py:524
  69.0 1.4 %collective-permute-start.25 = (f32[32,128]{1,0:T(8,128)S(1)}, f32[32,128]{1,0:T(8,128)S(1)}, u32[]{:S(2)}, u32[]{:S(2)}) collective-permute-start(f32[32,128]{1,0:T(8,128)S(1)} %add.20.after.refs_0_), channel_id=1, source_target_pairs={{0,8},{4,12},{8,0},{12,4},{1,9},{5,13},{9,1},{13,5},{2,10},{6,14},... | collective-permute-start | bytes 49160 | tf_op jit(solution)/shard_map/ppermute | solution.py:524
  70.3 3.4 %collective-permute-done.25.after.refs_1_ = f32[32,128]{1,0:T(8,128)S(1)} collective-permute-done((f32[32,128]{1,0:T(8,128)S(1)}, f32[32,128]{1,0:T(8,128)S(1)}, u32[]{:S(2)}, u32[]{:S(2)}) %collective-permute-start.25) | collective-permute-done | bytes 16416 | tf_op jit(solution)/shard_map/ppermute | solution.py:524
  74.5 1.7 %shard_map.74.factor = f32[64,64]{1,0:T(8,128)S(1)} custom-call(f32[32,2048]{1,0:T(8,128)S(1)} %shard_map.73.after.own, f32[32,128]{1,0:T(8,128)S(1)} %add.20.after.refs_0_, f32[32,128]{1,0:T(8,128)S(1)} %collective-permute-done.25.after.refs_1_), custom_call_target="tpu_custom_call" | custom-call | tf_op jit(solution)/shard_map/pallas_call | solution.py:28
  76.2 1.4 %shard_map.75 = (bf16[128,2048]{1,0:T(8,128)(2,1)S(1)}, f32[32,128]{1,0:T(8,128)S(1)}) custom-call(s32[3]{0:T(128)S(1)} %pad_add_fusion.me, f32[64,64]{1,0:T(8,128)S(1)} %shard_map.74.factor, f32[32,2048]{1,0:T(8,128)S(1)} %shard_map.73.after.own, f32[32,2048]{1,0:T(8,128)S(1)} %collective-permute-done.26.other), custom_call_target="tpu_custom_call" | custom-call | tf_op jit(solution)/shard_map/pallas_call | solution.py:28
  78.1 2.1 %collective-permute-start.28 = (f32[32,128]{1,0:T(8,128)S(1)}, f32[32,128]{1,0:T(8,128)S(1)}, u32[]{:S(2)}, u32[]{:S(2)}) collective-permute-start(f32[32,128]{1,0:T(8,128)S(1)} %get-tuple-element.54.refs_0_), channel_id=1, source_target_pairs={{0,8},{4,12},{8,0},{12,4},{1,9},{5,13},{9,1},{13,5},{2,10},{6,14},... | collective-permute-start | bytes 49160 | tf_op jit(solution)/shard_map/ppermute | solution.py:516
  80.2 1.6 %collective-permute-start.29 = (f32[32,128]{1,0:T(8,128)S(1)}, f32[32,128]{1,0:T(8,128)S(1)}, u32[]{:S(2)}, u32[]{:S(2)}) collective-permute-start(f32[32,128]{1,0:T(8,128)S(1)} %get-tuple-element.54.refs_0_), channel_id=1, source_target_pairs={{0,12},{4,0},{8,4},{12,8},{1,13},{5,1},{9,5},{13,9},{2,14},{6,2},{... | collective-permute-start | bytes 49160 | tf_op jit(solution)/shard_map/ppermute | solution.py:516
  83.9 3.2 %shard_map.76 = f32[32,2048]{1,0:T(8,128)} custom-call(s32[3]{0:T(128)S(1)} %pad_add_fusion.me, bf16[128,2048]{1,0:T(8,128)(2,1)S(1)} %get-tuple-element.53.mapped, f32[32,128]{1,0:T(8,128)S(1)} %get-tuple-element.54.refs_0_, f32[32,128]{1,0:T(8,128)S(1)} %collective-permute-done.27.refs_1_, f32[32,128]{1,0:T(8,128)S(1)} %collective-permute-done.28.refs_2_, ...), custom_call_target="tpu_custom_call" | custom-call | tf_op jit(solution)/shard_map/pallas_call | solution.py:28
  (57 shorter events, 13.9 us)
Async XLA Ops:
  2.0 9.5 %collective-permute-start = (s32[3,8]{1,0:T(4,128)S(1)}, s32[3,8]{1,0:T(4,128)S(1)}, u32[]{:S(2)}, u32[]{:S(2)}) collective-permute-start(s32[3,8]{1,0:T(4,128)S(1)} %concatenate.3.refs_0_), channel_id=1, source_target_pairs={{0,4},{4,8},{8,12},{12,0},{1,5},{5,9},{9,13},{13,1},{2,6},{6,10},{... | collective-permute-start | bytes 296 | tf_op jit(solution)/shard_map/ppermute | solution.py:516
  5.0 6.5 %collective-permute-start.1 = (s32[3,8]{1,0:T(4,128)S(1)}, s32[3,8]{1,0:T(4,128)S(1)}, u32[]{:S(2)}, u32[]{:S(2)}) collective-permute-start(s32[3,8]{1,0:T(4,128)S(1)} %concatenate.3.refs_0_), channel_id=1, source_target_pairs={{0,8},{4,12},{8,0},{12,4},{1,9},{5,13},{9,1},{13,5},{2,10},{6,14},... | collective-permute-start | bytes 296 | tf_op jit(solution)/shard_map/ppermute | solution.py:516
  7.6 3.9 %collective-permute-start.2 = (s32[3,8]{1,0:T(4,128)S(1)}, s32[3,8]{1,0:T(4,128)S(1)}, u32[]{:S(2)}, u32[]{:S(2)}) collective-permute-start(s32[3,8]{1,0:T(4,128)S(1)} %concatenate.3.refs_0_), channel_id=1, source_target_pairs={{0,12},{4,0},{8,4},{12,8},{1,13},{5,1},{9,5},{13,9},{2,14},{6,2},{... | collective-permute-start | bytes 296 | tf_op jit(solution)/shard_map/ppermute | solution.py:516
  11.4 5.4 %copy-start.1 = (bf16[2048,384]{1,0:T(8,128)(2,1)S(1)}, bf16[2048,384]{1,0:T(8,128)(2,1)}, u32[]{:S(2)}) copy-start(bf16[2048,384]{1,0:T(8,128)(2,1)} %emb.5) | copy-start | bytes 4718596
  13.3 8.3 %collective-permute-start.3 = (bf16[256,384]{1,0:T(8,128)(2,1)S(1)}, bf16[256,384]{1,0:T(8,128)(2,1)S(1)}, u32[]{:S(2)}, u32[]{:S(2)}) collective-permute-start(bf16[256,384]{1,0:T(8,128)(2,1)S(1)} %get-tuple-element.30), channel_id=1, source_target_pairs={{0,12},{4,0},{8,4},{12,8},{1,13},{5,1},{9,5},{13,9},{2,14},{6,2},{... | collective-permute-start | bytes 589832 | tf_op jit(solution)/shard_map/ppermute | solution.py:516
  16.2 15.7 %collective-permute-start.4 = (bf16[256,384]{1,0:T(8,128)(2,1)S(1)}, bf16[256,384]{1,0:T(8,128)(2,1)S(1)}, u32[]{:S(2)}, u32[]{:S(2)}) collective-permute-start(bf16[256,384]{1,0:T(8,128)(2,1)S(1)} %get-tuple-element.31), channel_id=1, source_target_pairs={{0,8},{4,12},{8,0},{12,4},{1,9},{5,13},{9,1},{13,5},{2,10},{6,14},... | collective-permute-start | bytes 589832 | tf_op jit(solution)/shard_map/ppermute | solution.py:516
  16.2 15.7 %collective-permute-start.5 = (bf16[256,384]{1,0:T(8,128)(2,1)S(1)}, bf16[256,384]{1,0:T(8,128)(2,1)S(1)}, u32[]{:S(2)}, u32[]{:S(2)}) collective-permute-start(bf16[256,384]{1,0:T(8,128)(2,1)S(1)} %get-tuple-element.32), channel_id=1, source_target_pairs={{0,4},{4,8},{8,12},{12,0},{1,5},{5,9},{9,13},{13,1},{2,6},{6,10},{... | collective-permute-start | bytes 589832 | tf_op jit(solution)/shard_map/ppermute | solution.py:516
  16.8 16.4 %collective-permute-start.7 = (f32[1024,128]{1,0:T(8,128)S(1)}, f32[1024,128]{1,0:T(8,128)S(1)}, u32[]{:S(2)}, u32[]{:S(2)}) collective-permute-start(f32[1024,128]{1,0:T(8,128)S(1)} %shard_map.59.refs_5_.mine), channel_id=1, source_target_pairs={{0,1},{1,0},{2,3},{3,2},{4,5},{5,4},{6,7},{7,6},{8,9},{9,8},{10,11... | collective-permute-start | bytes 1572872 | tf_op jit(solution)/shard_map/ppermute | solution.py:516
  17.2 15.9 %copy-start.2 = (f32[2048,32]{0,1:T(8,128)S(1)}, f32[2048,32]{0,1:T(8,128)}, u32[]{:S(2)}) copy-start(f32[2048,32]{0,1:T(8,128)} %param.5) | copy-start | bytes 786436
  33.0 2.0 %collective-permute-start.6 = (f32[1024,128]{1,0:T(8,128)S(1)}, f32[1024,128]{1,0:T(8,128)S(1)}, u32[]{:S(2)}, u32[]{:S(2)}) collective-permute-start(f32[1024,128]{1,0:T(8,128)S(1)} %shard_map.62.mine), channel_id=1, source_target_pairs={{0,1},{1,0},{2,3},{3,2},{4,5},{5,4},{6,7},{7,6},{8,9},{9,8},{10,11... | collective-permute-start | bytes 1572872 | tf_op jit(solution)/shard_map/ppermute | solution.py:516
  35.9 5.6 %collective-permute-start.10 = (f32[64,128]{1,0:T(8,128)S(1)}, f32[64,128]{1,0:T(8,128)S(1)}, u32[]{:S(2)}, u32[]{:S(2)}) collective-permute-start(f32[64,128]{1,0:T(8,128)S(1)} %get-tuple-element.37), channel_id=1, source_target_pairs={{0,12},{4,0},{8,4},{12,8},{1,13},{5,1},{9,5},{13,9},{2,14},{6,2},{... | collective-permute-start | bytes 98312 | tf_op jit(solution)/shard_map/ppermute | solution.py:516
  36.0 7.9 %collective-permute-start.8 = (f32[64,128]{1,0:T(8,128)S(1)}, f32[64,128]{1,0:T(8,128)S(1)}, u32[]{:S(2)}, u32[]{:S(2)}) collective-permute-start(f32[64,128]{1,0:T(8,128)S(1)} %get-tuple-element.37), channel_id=1, source_target_pairs={{0,4},{4,8},{8,12},{12,0},{1,5},{5,9},{9,13},{13,1},{2,6},{6,10},{... | collective-permute-start | bytes 98312 | tf_op jit(solution)/shard_map/ppermute | solution.py:516
  38.0 5.9 %collective-permute-start.9 = (f32[64,128]{1,0:T(8,128)S(1)}, f32[64,128]{1,0:T(8,128)S(1)}, u32[]{:S(2)}, u32[]{:S(2)}) collective-permute-start(f32[64,128]{1,0:T(8,128)S(1)} %get-tuple-element.37), channel_id=1, source_target_pairs={{0,8},{4,12},{8,0},{12,4},{1,9},{5,13},{9,1},{13,5},{2,10},{6,14},... | collective-permute-start | bytes 98312 | tf_op jit(solution)/shard_map/ppermute | solution.py:516
  40.0 7.9 %collective-permute-start.12 = (s16[272,128]{1,0:T(8,128)(2,1)S(1)}, s16[272,128]{1,0:T(8,128)(2,1)S(1)}, u32[]{:S(2)}, u32[]{:S(2)}) collective-permute-start(s16[272,128]{1,0:T(8,128)(2,1)S(1)} %get-tuple-element.43), channel_id=1, source_target_pairs={{0,4},{4,8},{8,12},{12,0},{1,5},{5,9},{9,13},{13,1},{2,6},{6,10},{... | collective-permute-start | bytes 208904 | tf_op jit(solution)/shard_map/ppermute | solution.py:516
  40.4 7.9 %collective-permute-start.13 = (s16[272,128]{1,0:T(8,128)(2,1)S(1)}, s16[272,128]{1,0:T(8,128)(2,1)S(1)}, u32[]{:S(2)}, u32[]{:S(2)}) collective-permute-start(s16[272,128]{1,0:T(8,128)(2,1)S(1)} %get-tuple-element.44), channel_id=1, source_target_pairs={{0,8},{4,12},{8,0},{12,4},{1,9},{5,13},{9,1},{13,5},{2,10},{6,14},... | collective-permute-start | bytes 208904 | tf_op jit(solution)/shard_map/ppermute | solution.py:516
  41.5 6.8 %collective-permute-start.14 = (s16[272,128]{1,0:T(8,128)(2,1)S(1)}, s16[272,128]{1,0:T(8,128)(2,1)S(1)}, u32[]{:S(2)}, u32[]{:S(2)}) collective-permute-start(s16[272,128]{1,0:T(8,128)(2,1)S(1)} %get-tuple-element.45), channel_id=1, source_target_pairs={{0,12},{4,0},{8,4},{12,8},{1,13},{5,1},{9,5},{13,9},{2,14},{6,2},{... | collective-permute-start | bytes 208904 | tf_op jit(solution)/shard_map/ppermute | solution.py:516
  43.9 4.0 %collective-permute-start.11 = (f32[64,128]{1,0:T(8,128)S(1)}, f32[64,128]{1,0:T(8,128)S(1)}, u32[]{:S(2)}, u32[]{:S(2)}) collective-permute-start(f32[64,128]{1,0:T(8,128)S(1)} %add_add_fusion.mine), channel_id=1, source_target_pairs={{0,2},{2,0},{1,3},{3,1},{4,6},{6,4},{5,7},{7,5},{8,10},{10,8},{9,1... | collective-permute-start | bytes 98312 | tf_op jit(solution)/shard_map/ppermute | solution.py:524
  48.4 1.5 %collective-permute-start.15 = (bf16[1,256,128]{2,1,0:T(8,128)(2,1)S(1)}, bf16[1,256,128]{2,1,0:T(8,128)(2,1)S(1)}, u32[]{:S(2)}, u32[]{:S(2)}) collective-permute-start(bf16[1,256,128]{2,1,0:T(8,128)(2,1)S(1)} %get-tuple-element.46.refs_0_), channel_id=1, source_target_pairs={{0,1},{1,0},{2,3},{3,2},{4,5},{5,4},{6,7},{7,6},{8,9},{9,8},{10,11... | collective-permute-start | bytes 196616 | tf_op jit(solution)/shard_map/ppermute | solution.py:516
  48.4 1.5 %collective-permute-start.16 = (bf16[1,256,128]{2,1,0:T(8,128)(2,1)S(1)}, bf16[1,256,128]{2,1,0:T(8,128)(2,1)S(1)}, u32[]{:S(2)}, u32[]{:S(2)}) collective-permute-start(bf16[1,256,128]{2,1,0:T(8,128)(2,1)S(1)} %get-tuple-element.47.refs_1_), channel_id=1, source_target_pairs={{0,1},{1,0},{2,3},{3,2},{4,5},{5,4},{6,7},{7,6},{8,9},{9,8},{10,11... | collective-permute-start | bytes 196616 | tf_op jit(solution)/shard_map/ppermute | solution.py:516
  48.9 1.3 %collective-permute-start.17 = (bf16[1,256,128]{2,1,0:T(8,128)(2,1)S(1)}, bf16[1,256,128]{2,1,0:T(8,128)(2,1)S(1)}, u32[]{:S(2)}, u32[]{:S(2)}) collective-permute-start(bf16[1,256,128]{2,1,0:T(8,128)(2,1)S(1)} %get-tuple-element.48.refs_2_), channel_id=1, source_target_pairs={{0,1},{1,0},{2,3},{3,2},{4,5},{5,4},{6,7},{7,6},{8,9},{9,8},{10,11... | collective-permute-start | bytes 196616 | tf_op jit(solution)/shard_map/ppermute | solution.py:516
  51.2 5.8 %collective-permute-start.18 = (s16[32,2176]{1,0:T(8,128)(2,1)S(1)}, s16[32,2176]{1,0:T(8,128)(2,1)S(1)}, u32[]{:S(2)}, u32[]{:S(2)}) collective-permute-start(s16[32,2176]{1,0:T(8,128)(2,1)S(1)} %shard_map.68.mine), channel_id=1, source_target_pairs={{0,2},{2,0},{1,3},{3,1},{4,6},{6,4},{5,7},{7,5},{8,10},{10,8},{9,1... | collective-permute-start | bytes 417800 | tf_op jit(solution)/shard_map/ppermute | solution.py:524
  57.9 4.6 %collective-permute-start.19 = (f32[32,2048]{1,0:T(8,128)S(1)}, f32[32,2048]{1,0:T(8,128)S(1)}, u32[]{:S(2)}, u32[]{:S(2)}) collective-permute-start(f32[32,2048]{1,0:T(8,128)S(1)} %get-tuple-element.49.own), channel_id=1, source_target_pairs={{0,1},{1,0},{2,3},{3,2},{4,5},{5,4},{6,7},{7,6},{8,9},{9,8},{10,11... | collective-permute-start | bytes 786440 | tf_op jit(solution)/shard_map/ppermute | solution.py:516
  58.0 6.2 %collective-permute-start.20 = (s16[144,128]{1,0:T(8,128)(2,1)S(1)}, s16[144,128]{1,0:T(8,128)(2,1)S(1)}, u32[]{:S(2)}, u32[]{:S(2)}) collective-permute-start(s16[144,128]{1,0:T(8,128)(2,1)S(1)} %get-tuple-element.50), channel_id=1, source_target_pairs={{0,4},{4,8},{8,12},{12,0},{1,5},{5,9},{9,13},{13,1},{2,6},{6,10},{... | collective-permute-start | bytes 110600 | tf_op jit(solution)/shard_map/ppermute | solution.py:516
  59.4 5.9 %collective-permute-start.21 = (s16[144,128]{1,0:T(8,128)(2,1)S(1)}, s16[144,128]{1,0:T(8,128)(2,1)S(1)}, u32[]{:S(2)}, u32[]{:S(2)}) collective-permute-start(s16[144,128]{1,0:T(8,128)(2,1)S(1)} %get-tuple-element.51), channel_id=1, source_target_pairs={{0,8},{4,12},{8,0},{12,4},{1,9},{5,13},{9,1},{13,5},{2,10},{6,14},... | collective-permute-start | bytes 110600 | tf_op jit(solution)/shard_map/ppermute | solution.py:516
  61.0 4.6 %collective-permute-start.22 = (s16[144,128]{1,0:T(8,128)(2,1)S(1)}, s16[144,128]{1,0:T(8,128)(2,1)S(1)}, u32[]{:S(2)}, u32[]{:S(2)}) collective-permute-start(s16[144,128]{1,0:T(8,128)(2,1)S(1)} %get-tuple-element.52), channel_id=1, source_target_pairs={{0,12},{4,0},{8,4},{12,8},{1,13},{5,1},{9,5},{13,9},{2,14},{6,2},{... | collective-permute-start | bytes 110600 | tf_op jit(solution)/shard_map/ppermute | solution.py:516
  63.5 3.8 %collective-permute-start.23 = (f32[32,128]{1,0:T(8,128)S(1)}, f32[32,128]{1,0:T(8,128)S(1)}, u32[]{:S(2)}, u32[]{:S(2)}) collective-permute-start(f32[32,128]{1,0:T(8,128)S(1)} %shard_map.70.after), channel_id=1, source_target_pairs={{0,4},{4,0},{8,12},{12,8},{1,5},{5,1},{9,13},{13,9},{2,6},{6,2},{1... | collective-permute-start | bytes 49160 | tf_op jit(solution)/shard_map/ppermute | solution.py:524
  67.4 6.4 %collective-permute-start.24 = (s16[32,2176]{1,0:T(8,128)(2,1)S(1)}, s16[32,2176]{1,0:T(8,128)(2,1)S(1)}, u32[]{:S(2)}, u32[]{:S(2)}) collective-permute-start(s16[32,2176]{1,0:T(8,128)(2,1)S(1)} %shard_map.72.mine), channel_id=1, source_target_pairs={{0,2},{2,0},{1,3},{3,1},{4,6},{6,4},{5,7},{7,5},{8,10},{10,8},{9,1... | collective-permute-start | bytes 417800 | tf_op jit(solution)/shard_map/ppermute | solution.py:524
  69.0 4.8 %collective-permute-start.25 = (f32[32,128]{1,0:T(8,128)S(1)}, f32[32,128]{1,0:T(8,128)S(1)}, u32[]{:S(2)}, u32[]{:S(2)}) collective-permute-start(f32[32,128]{1,0:T(8,128)S(1)} %add.20.after.refs_0_), channel_id=1, source_target_pairs={{0,8},{4,12},{8,0},{12,4},{1,9},{5,13},{9,1},{13,5},{2,10},{6,14},... | collective-permute-start | bytes 49160 | tf_op jit(solution)/shard_map/ppermute | solution.py:524
  74.4 1.8 %collective-permute-start.26 = (f32[32,2048]{1,0:T(8,128)S(1)}, f32[32,2048]{1,0:T(8,128)S(1)}, u32[]{:S(2)}, u32[]{:S(2)}) collective-permute-start(f32[32,2048]{1,0:T(8,128)S(1)} %shard_map.73.after.own), channel_id=1, source_target_pairs={{0,1},{1,0},{2,3},{3,2},{4,5},{5,4},{6,7},{7,6},{8,9},{9,8},{10,11... | collective-permute-start | bytes 786440 | tf_op jit(solution)/shard_map/ppermute | solution.py:516
  77.6 5.7 %collective-permute-start.27 = (f32[32,128]{1,0:T(8,128)S(1)}, f32[32,128]{1,0:T(8,128)S(1)}, u32[]{:S(2)}, u32[]{:S(2)}) collective-permute-start(f32[32,128]{1,0:T(8,128)S(1)} %get-tuple-element.54.refs_0_), channel_id=1, source_target_pairs={{0,4},{4,8},{8,12},{12,0},{1,5},{5,9},{9,13},{13,1},{2,6},{6,10},{... | collective-permute-start | bytes 49160 | tf_op jit(solution)/shard_map/ppermute | solution.py:516
  78.1 5.2 %collective-permute-start.28 = (f32[32,128]{1,0:T(8,128)S(1)}, f32[32,128]{1,0:T(8,128)S(1)}, u32[]{:S(2)}, u32[]{:S(2)}) collective-permute-start(f32[32,128]{1,0:T(8,128)S(1)} %get-tuple-element.54.refs_0_), channel_id=1, source_target_pairs={{0,8},{4,12},{8,0},{12,4},{1,9},{5,13},{9,1},{13,5},{2,10},{6,14},... | collective-permute-start | bytes 49160 | tf_op jit(solution)/shard_map/ppermute | solution.py:516
  80.2 3.7 %collective-permute-start.29 = (f32[32,128]{1,0:T(8,128)S(1)}, f32[32,128]{1,0:T(8,128)S(1)}, u32[]{:S(2)}, u32[]{:S(2)}) collective-permute-start(f32[32,128]{1,0:T(8,128)S(1)} %get-tuple-element.54.refs_0_), channel_id=1, source_target_pairs={{0,12},{4,0},{8,4},{12,8},{1,13},{5,1},{9,5},{13,9},{2,14},{6,2},{... | collective-permute-start | bytes 49160 | tf_op jit(solution)/shard_map/ppermute | solution.py:516
  (1 other events, 1.4 us)

commit v13 on v12

--- a/solution.py
+++ b/solution.py
@@ -22,7 +22,7 @@
 NT = (((1,), (1,)), ((), ()))
 
 
-def call(body, outs, args, smem_in=(), smem_out=(), any_in=(), scratch=()):
+def call(body, outs, args, smem_in=(), smem_out=(), any_in=(), scratch=(), cost=0):
     single = not isinstance(outs, (list, tuple))
     shapes = [outs] if single else list(outs)
     result = pl.pallas_call(
@@ -33,6 +33,9 @@
         ],
         out_specs=[SMEM if i in smem_out else VMEM for i in range(len(shapes))],
         scratch_shapes=list(scratch),
+        cost_estimate=pl.CostEstimate(flops=cost * 10**9, bytes_accessed=0, transcendentals=0)
+        if cost
+        else None,
         compiler_params=pltpu.CompilerParams(vmem_limit_bytes=48 * 2**20),
     )(*args)
     return result[0] if single else result
@@ -175,8 +178,7 @@
 
 def plan_body(dims, me, *refs):
     row_count, capacity, slots, blocks_here = dims
-    lists, (emb, after, idx) = refs[:row_count], refs[row_count : row_count + 3]
-    sends = refs[row_count + 3 :]
+    lists, idx = refs[:row_count], refs[row_count]
     row = me[0]
 
     for i in range(slots):
@@ -231,6 +233,8 @@
             return (counts[0] + hit.astype(jnp.int32),)
 
         ranked(lists[k], 1, write_in)
+
+def pick_body(row_count, capacity, idx, emb, *sends):
     for k in range(1, row_count):
         for j in range(capacity):
             sends[k - 1][j * BLOCK : (j + 1) * BLOCK, :] = emb[at_block(idx[4, k * capacity + j]), :]
@@ -246,7 +250,7 @@
     return left_sq + right_row - 2.0 * inner
 
 
-def self_distance_body(own_blocks, tile_count, me, emb, out):
+def self_distance_body(own_blocks, tile_count, me, emb, after, out):
     for i in range(own_blocks):
         block = emb[at_block(i * tile_count + me[1]), :]
         block_sq = squares(block)
@@ -556,23 +560,29 @@
         [pair_list[0], jnp.broadcast_to(pair_count[:, None], (1, slots))], axis=0
     )
     lists = row_terms(own_list, row_count)
+    idx = call(
+        functools.partial(plan_body, (row_count, capacity, slots, blocks_here)),
+        sds((6, slots), jnp.int32),
+        [me, *lists],
+        smem_in=range(1 + row_count),
+        smem_out=(0,),
+        cost=3,
+    )
+    sends = call(
+        functools.partial(pick_body, row_count, capacity),
+        [sds((capacity * BLOCK, half_features), BF16) for _ in others],
+        [idx, embeddings],
+        smem_in=(0,),
+    )
+    far = [shift_by(sends[k - 1], "rows", row_count, -k) for k in others]
+
     self_part = call(
         functools.partial(self_distance_body, own_blocks, tile_count),
         sds((own_blocks * BLOCK, BLOCK), F32),
-        [me, embeddings],
+        [me, embeddings, idx],
         smem_in=(0,),
-    )
-    planned = call(
-        functools.partial(plan_body, (row_count, capacity, slots, blocks_here)),
-        [sds((6, slots), jnp.int32)] + [sds((capacity * BLOCK, half_features), BF16) for _ in others],
-        [me, *lists, embeddings, self_part],
-        smem_in=range(1 + row_count),
-        any_in=(row_count + 2,),
-        smem_out=(0,),
-    )
-    idx, sends = planned[0], planned[1:]
-    far = [shift_by(sends[k - 1], "rows", row_count, -k) for k in others]
-
+        any_in=(2,),
+    )
     self_other = shift_by(self_part, "cols", core_count, 1)
     self_tiles, self_sums = call(
         functools.partial(self_tile_body, own_blocks),

time: 87.3 us -> 87.9 us (level)
  local copies, waits for them, and re-layouts: 2.71 us -> 1.29 us
    ppermute x25, starting transfers between devices: 28 us -> 29.6 us  [shift_by(): lax.ppermute(value, axes, [(i, (i + shift) % size) for i in range(size)])]
    unnamed x6 -> x4, local copies, waits for them, and re-layouts: 1.42 us -> 0.01 us
    pallas_call x18 -> x19, Pallas kernels: 17.4 us -> 17.9 us  [call(): pl.pallas_call(body, out_shape=shapes, in_specs=[SMEM if i in smem_in els...]
  transfers between devices with their start and end apart: 30 -> 30, of which waited for: 14 -> 15; matrix products, arithmetic and copies ran while one was open for 1% -> 1% of each run, Pallas kernels for 8% -> 8%
where the time goes in v13:
time: 87.9 us; the launch traced here: 87.8 us
  starting transfers between devices  35.5 us (40%)
  waiting for transfers between devices  31.5 us (36%)
  Pallas kernels  17.9 us (20%)
  between operations  1.47 us (2%)
  local copies, waits for them, and re-layouts  1.29 us (1%)
    ppermute x25, starting transfers between devices, shift_by(): lax.ppermute(value, axes, [(i, (i + shift) % size) for i in range(size)])  29.6 us
    ppermute x25, waiting for transfers between devices, shift_by(): lax.ppermute(value, axes, [(i, (i + shift) % size) for i in range(size)])  20.2 us
    pallas_call x19, Pallas kernels, call(): pl.pallas_call(body, out_shape=shapes, in_specs=[SMEM if i in smem_in els...  17.9 us
    ppermute x5, waiting for transfers between devices, pair_step(): lax.ppermute(value, name, [(i, i ^ flip) for i in range(lax.axis_size(nam...  11.3 us
    ppermute x5, starting transfers between devices, pair_step(): lax.ppermute(value, name, [(i, i ^ flip) for i in range(lax.axis_size(nam...  5.87 us
  transfers between devices with their start and end apart: 30, of which 15 were waited for; matrix products, arithmetic and copies ran while one was open for 1% of the time, Pallas kernels for 8%

profile of v13, /device:TPU:0, one launch (start us, length us, event | category | flops | bytes accessed | tf_op | source)
XLA Modules:
  0.0 87.8 jit_solution(10329327980781169094)
XLA Ops:
  2.0 3.0 %collective-permute-start = (s32[3,8]{1,0:T(4,128)S(1)}, s32[3,8]{1,0:T(4,128)S(1)}, u32[]{:S(2)}, u32[]{:S(2)}) collective-permute-start(s32[3,8]{1,0:T(4,128)S(1)} %concatenate.3.refs_0_), channel_id=1, source_target_pairs={{0,4},{4,8},{8,12},{12,0},{1,5},{5,9},{9,13},{13,1},{2,6},{6,10},{... | collective-permute-start | bytes 296 | tf_op jit(solution)/shard_map/ppermute | solution.py:520
  5.0 2.6 %collective-permute-start.1 = (s32[3,8]{1,0:T(4,128)S(1)}, s32[3,8]{1,0:T(4,128)S(1)}, u32[]{:S(2)}, u32[]{:S(2)}) collective-permute-start(s32[3,8]{1,0:T(4,128)S(1)} %concatenate.3.refs_0_), channel_id=1, source_target_pairs={{0,8},{4,12},{8,0},{12,4},{1,9},{5,13},{9,1},{13,5},{2,10},{6,14},... | collective-permute-start | bytes 296 | tf_op jit(solution)/shard_map/ppermute | solution.py:520
  7.6 1.3 %collective-permute-start.2 = (s32[3,8]{1,0:T(4,128)S(1)}, s32[3,8]{1,0:T(4,128)S(1)}, u32[]{:S(2)}, u32[]{:S(2)}) collective-permute-start(s32[3,8]{1,0:T(4,128)S(1)} %concatenate.3.refs_0_), channel_id=1, source_target_pairs={{0,12},{4,0},{8,4},{12,8},{1,13},{5,1},{9,5},{13,9},{2,14},{6,2},{... | collective-permute-start | bytes 296 | tf_op jit(solution)/shard_map/ppermute | solution.py:520
  9.5 1.7 %collective-permute-done.2.refs_3_ = s32[3,8]{1,0:T(4,128)S(1)} collective-permute-done((s32[3,8]{1,0:T(4,128)S(1)}, s32[3,8]{1,0:T(4,128)S(1)}, u32[]{:S(2)}, u32[]{:S(2)}) %collective-permute-start.2) | collective-permute-done | bytes 128 | tf_op jit(solution)/shard_map/ppermute | solution.py:520
  11.2 1.7 %shard_map.59.after.idx = s32[6,8]{1,0:T(8,128)S(1)} custom-call(s32[3]{0:T(128)S(1)} %pad_add_fusion.me, s32[3,8]{1,0:T(4,128)S(1)} %concatenate.3.refs_0_, s32[3,8]{1,0:T(4,128)S(1)} %collective-permute-done.refs_1_, s32[3,8]{1,0:T(4,128)S(1)} %collective-permute-done.1.refs_2_, s32[3,8]{1,0:T(4,128)S(1)} %collective-permute-done.2.refs_3_), custom_call_target="tpu_custom_call" | custom-call | flops 3000000000 | tf_op jit(solution)/shard_map/pallas_call | solution.py:28
  13.6 3.2 %collective-permute-start.3 = (bf16[256,384]{1,0:T(8,128)(2,1)S(1)}, bf16[256,384]{1,0:T(8,128)(2,1)S(1)}, u32[]{:S(2)}, u32[]{:S(2)}) collective-permute-start(bf16[256,384]{1,0:T(8,128)(2,1)S(1)} %get-tuple-element.28), channel_id=1, source_target_pairs={{0,12},{4,0},{8,4},{12,8},{1,13},{5,1},{9,5},{13,9},{2,14},{6,2},{... | collective-permute-start | bytes 589832 | tf_op jit(solution)/shard_map/ppermute | solution.py:520
  18.9 3.3 %collective-permute-done.3.refs_0_ = bf16[256,384]{1,0:T(8,128)(2,1)S(1)} collective-permute-done((bf16[256,384]{1,0:T(8,128)(2,1)S(1)}, bf16[256,384]{1,0:T(8,128)(2,1)S(1)}, u32[]{:S(2)}, u32[]{:S(2)}) %collective-permute-start.3) | collective-permute-done | bytes 196640 | tf_op jit(solution)/shard_map/ppermute | solution.py:520
  22.2 9.2 %collective-permute-done.4.refs_1_ = bf16[256,384]{1,0:T(8,128)(2,1)S(1)} collective-permute-done((bf16[256,384]{1,0:T(8,128)(2,1)S(1)}, bf16[256,384]{1,0:T(8,128)(2,1)S(1)}, u32[]{:S(2)}, u32[]{:S(2)}) %collective-permute-start.4) | collective-permute-done | bytes 196640 | tf_op jit(solution)/shard_map/ppermute | solution.py:520
  31.4 1.1 %shard_map.62.mine = f32[1024,128]{1,0:T(8,128)S(1)} custom-call(s32[6,8]{1,0:T(8,128)S(1)} %shard_map.59.after.idx, bf16[2048,384]{1,0:T(8,128)(2,1)S(1)} %copy-done, f32[2048,128]{1,0:T(8,128)S(1)} %shard_map.60.own_squares, bf16[256,384]{1,0:T(8,128)(2,1)S(1)} %collective-permute-done.3.refs_0_, bf16[256,384]{1,0:T(8,128)(2,1)S(1)} %collective-permute-done.4.refs_1_, ...), custom_call_target="tpu_custom_call" | custom-call | tf_op jit(solution)/shard_map/pallas_call | solution.py:28
  32.9 1.5 %collective-permute-done.6.other = f32[1024,128]{1,0:T(8,128)S(1)} collective-permute-done((f32[1024,128]{1,0:T(8,128)S(1)}, f32[1024,128]{1,0:T(8,128)S(1)}, u32[]{:S(2)}, u32[]{:S(2)}) %collective-permute-start.6) | collective-permute-done | bytes 524320 | tf_op jit(solution)/shard_map/ppermute | solution.py:520
  36.2 1.2 %collective-permute-start.8 = (f32[64,128]{1,0:T(8,128)S(1)}, f32[64,128]{1,0:T(8,128)S(1)}, u32[]{:S(2)}, u32[]{:S(2)}) collective-permute-start(f32[64,128]{1,0:T(8,128)S(1)} %get-tuple-element.35), channel_id=1, source_target_pairs={{0,4},{4,8},{8,12},{12,0},{1,5},{5,9},{9,13},{13,1},{2,6},{6,10},{... | collective-permute-start | bytes 98312 | tf_op jit(solution)/shard_map/ppermute | solution.py:520
  37.5 3.1 %collective-permute-start.9 = (f32[64,128]{1,0:T(8,128)S(1)}, f32[64,128]{1,0:T(8,128)S(1)}, u32[]{:S(2)}, u32[]{:S(2)}) collective-permute-start(f32[64,128]{1,0:T(8,128)S(1)} %get-tuple-element.35), channel_id=1, source_target_pairs={{0,8},{4,12},{8,0},{12,4},{1,9},{5,13},{9,1},{13,5},{2,10},{6,14},... | collective-permute-start | bytes 98312 | tf_op jit(solution)/shard_map/ppermute | solution.py:520
  40.6 1.5 %collective-permute-start.13 = (s16[272,128]{1,0:T(8,128)(2,1)S(1)}, s16[272,128]{1,0:T(8,128)(2,1)S(1)}, u32[]{:S(2)}, u32[]{:S(2)}) collective-permute-start(s16[272,128]{1,0:T(8,128)(2,1)S(1)} %get-tuple-element.42), channel_id=1, source_target_pairs={{0,8},{4,12},{8,0},{12,4},{1,9},{5,13},{9,1},{13,5},{2,10},{6,14},... | collective-permute-start | bytes 208904 | tf_op jit(solution)/shard_map/ppermute | solution.py:520
  42.1 2.3 %collective-permute-start.14 = (s16[272,128]{1,0:T(8,128)(2,1)S(1)}, s16[272,128]{1,0:T(8,128)(2,1)S(1)}, u32[]{:S(2)}, u32[]{:S(2)}) collective-permute-start(s16[272,128]{1,0:T(8,128)(2,1)S(1)} %get-tuple-element.43), channel_id=1, source_target_pairs={{0,12},{4,0},{8,4},{12,8},{1,13},{5,1},{9,5},{13,9},{2,14},{6,2},{... | collective-permute-start | bytes 208904 | tf_op jit(solution)/shard_map/ppermute | solution.py:520
  44.4 1.6 %collective-permute-start.11 = (f32[64,128]{1,0:T(8,128)S(1)}, f32[64,128]{1,0:T(8,128)S(1)}, u32[]{:S(2)}, u32[]{:S(2)}) collective-permute-start(f32[64,128]{1,0:T(8,128)S(1)} %add_add_fusion.mine), channel_id=1, source_target_pairs={{0,2},{2,0},{1,3},{3,1},{4,6},{6,4},{5,7},{7,5},{8,10},{10,8},{9,1... | collective-permute-start | bytes 98312 | tf_op jit(solution)/shard_map/ppermute | solution.py:528
  46.0 2.4 %collective-permute-done.11.other.refs_3_ = f32[64,128]{1,0:T(8,128)S(1)} collective-permute-done((f32[64,128]{1,0:T(8,128)S(1)}, f32[64,128]{1,0:T(8,128)S(1)}, u32[]{:S(2)}, u32[]{:S(2)}) %collective-permute-start.11) | collective-permute-done | bytes 32800 | tf_op jit(solution)/shard_map/ppermute | solution.py:528
  50.6 1.0 %shard_map.69.mine = s16[32,2176]{1,0:T(8,128)(2,1)S(1)} custom-call(s32[3]{0:T(128)S(1)} %pad_add_fusion.me, s32[6,8]{1,0:T(8,128)S(1)} %shard_map.59.after.idx, f32[64,128]{1,0:T(8,128)S(1)} %get-tuple-element.39.inverse, f32[32,2048]{1,0:T(8,128)S(1)} %get-tuple-element.40.started, bf16[8,256,128]{2,1,0:T(8,128)(2,1)S(1)} %get-tuple-element.36.near_tiles, ...), custom_call_target="tpu_custom_call" | custom-call | tf_op jit(solution)/shard_map/pallas_call | solution.py:28
  51.6 1.6 %collective-permute-start.18 = (s16[32,2176]{1,0:T(8,128)(2,1)S(1)}, s16[32,2176]{1,0:T(8,128)(2,1)S(1)}, u32[]{:S(2)}, u32[]{:S(2)}) collective-permute-start(s16[32,2176]{1,0:T(8,128)(2,1)S(1)} %shard_map.69.mine), channel_id=1, source_target_pairs={{0,2},{2,0},{1,3},{3,1},{4,6},{6,4},{5,7},{7,5},{8,10},{10,8},{9,1... | collective-permute-start | bytes 417800 | tf_op jit(solution)/shard_map/ppermute | solution.py:528
  53.2 4.3 %collective-permute-done.18.other = s16[32,2176]{1,0:T(8,128)(2,1)S(1)} collective-permute-done((s16[32,2176]{1,0:T(8,128)(2,1)S(1)}, s16[32,2176]{1,0:T(8,128)(2,1)S(1)}, u32[]{:S(2)}, u32[]{:S(2)}) %collective-permute-start.18) | collective-permute-done | bytes 139296 | tf_op jit(solution)/shard_map/ppermute | solution.py:528
  58.4 1.4 %collective-permute-start.20 = (s16[144,128]{1,0:T(8,128)(2,1)S(1)}, s16[144,128]{1,0:T(8,128)(2,1)S(1)}, u32[]{:S(2)}, u32[]{:S(2)}) collective-permute-start(s16[144,128]{1,0:T(8,128)(2,1)S(1)} %get-tuple-element.48), channel_id=1, source_target_pairs={{0,4},{4,8},{8,12},{12,0},{1,5},{5,9},{9,13},{13,1},{2,6},{6,10},{... | collective-permute-start | bytes 110600 | tf_op jit(solution)/shard_map/ppermute | solution.py:520
  59.8 1.3 %collective-permute-start.21 = (s16[144,128]{1,0:T(8,128)(2,1)S(1)}, s16[144,128]{1,0:T(8,128)(2,1)S(1)}, u32[]{:S(2)}, u32[]{:S(2)}) collective-permute-start(s16[144,128]{1,0:T(8,128)(2,1)S(1)} %get-tuple-element.49), channel_id=1, source_target_pairs={{0,8},{4,12},{8,0},{12,4},{1,9},{5,13},{9,1},{13,5},{2,10},{6,14},... | collective-permute-start | bytes 110600 | tf_op jit(solution)/shard_map/ppermute | solution.py:520
  61.1 2.0 %collective-permute-start.22 = (s16[144,128]{1,0:T(8,128)(2,1)S(1)}, s16[144,128]{1,0:T(8,128)(2,1)S(1)}, u32[]{:S(2)}, u32[]{:S(2)}) collective-permute-start(s16[144,128]{1,0:T(8,128)(2,1)S(1)} %get-tuple-element.50), channel_id=1, source_target_pairs={{0,12},{4,0},{8,4},{12,8},{1,13},{5,1},{9,5},{13,9},{2,14},{6,2},{... | collective-permute-start | bytes 110600 | tf_op jit(solution)/shard_map/ppermute | solution.py:520
  64.5 1.2 %collective-permute-done.21.refs_7_ = s16[144,128]{1,0:T(8,128)(2,1)S(1)} collective-permute-done((s16[144,128]{1,0:T(8,128)(2,1)S(1)}, s16[144,128]{1,0:T(8,128)(2,1)S(1)}, u32[]{:S(2)}, u32[]{:S(2)}) %collective-permute-start.21) | collective-permute-done | bytes 36896 | tf_op jit(solution)/shard_map/ppermute | solution.py:520
  66.7 1.1 %collective-permute-done.23 = f32[32,128]{1,0:T(8,128)S(1)} collective-permute-done((f32[32,128]{1,0:T(8,128)S(1)}, f32[32,128]{1,0:T(8,128)S(1)}, u32[]{:S(2)}, u32[]{:S(2)}) %collective-permute-start.23) | collective-permute-done | bytes 16416 | tf_op jit(solution)/shard_map/ppermute | solution.py:528
  68.0 1.6 %collective-permute-start.24 = (s16[32,2176]{1,0:T(8,128)(2,1)S(1)}, s16[32,2176]{1,0:T(8,128)(2,1)S(1)}, u32[]{:S(2)}, u32[]{:S(2)}) collective-permute-start(s16[32,2176]{1,0:T(8,128)(2,1)S(1)} %shard_map.73.mine), channel_id=1, source_target_pairs={{0,2},{2,0},{1,3},{3,1},{4,6},{6,4},{5,7},{7,5},{8,10},{10,8},{9,1... | collective-permute-start | bytes 417800 | tf_op jit(solution)/shard_map/ppermute | solution.py:528
  69.6 1.2 %collective-permute-start.25 = (f32[32,128]{1,0:T(8,128)S(1)}, f32[32,128]{1,0:T(8,128)S(1)}, u32[]{:S(2)}, u32[]{:S(2)}) collective-permute-start(f32[32,128]{1,0:T(8,128)S(1)} %add.20.after.refs_0_), channel_id=1, source_target_pairs={{0,8},{4,12},{8,0},{12,4},{1,9},{5,13},{9,1},{13,5},{2,10},{6,14},... | collective-permute-start | bytes 49160 | tf_op jit(solution)/shard_map/ppermute | solution.py:528
  70.7 3.5 %collective-permute-done.25.after.refs_1_ = f32[32,128]{1,0:T(8,128)S(1)} collective-permute-done((f32[32,128]{1,0:T(8,128)S(1)}, f32[32,128]{1,0:T(8,128)S(1)}, u32[]{:S(2)}, u32[]{:S(2)}) %collective-permute-start.25) | collective-permute-done | bytes 16416 | tf_op jit(solution)/shard_map/ppermute | solution.py:528
  74.9 1.7 %shard_map.75.factor = f32[64,64]{1,0:T(8,128)S(1)} custom-call(f32[32,2048]{1,0:T(8,128)S(1)} %shard_map.74.after.own, f32[32,128]{1,0:T(8,128)S(1)} %add.20.after.refs_0_, f32[32,128]{1,0:T(8,128)S(1)} %collective-permute-done.25.after.refs_1_), custom_call_target="tpu_custom_call" | custom-call | tf_op jit(solution)/shard_map/pallas_call | solution.py:28
  76.7 1.4 %shard_map.76 = (bf16[128,2048]{1,0:T(8,128)(2,1)S(1)}, f32[32,128]{1,0:T(8,128)S(1)}) custom-call(s32[3]{0:T(128)S(1)} %pad_add_fusion.me, f32[64,64]{1,0:T(8,128)S(1)} %shard_map.75.factor, f32[32,2048]{1,0:T(8,128)S(1)} %shard_map.74.after.own, f32[32,2048]{1,0:T(8,128)S(1)} %collective-permute-done.26.other), custom_call_target="tpu_custom_call" | custom-call | tf_op jit(solution)/shard_map/pallas_call | solution.py:28
  78.2 2.6 %collective-permute-start.28 = (f32[32,128]{1,0:T(8,128)S(1)}, f32[32,128]{1,0:T(8,128)S(1)}, u32[]{:S(2)}, u32[]{:S(2)}) collective-permute-start(f32[32,128]{1,0:T(8,128)S(1)} %get-tuple-element.52.refs_0_), channel_id=1, source_target_pairs={{0,8},{4,12},{8,0},{12,4},{1,9},{5,13},{9,1},{13,5},{2,10},{6,14},... | collective-permute-start | bytes 49160 | tf_op jit(solution)/shard_map/ppermute | solution.py:520
  80.8 1.3 %collective-permute-start.29 = (f32[32,128]{1,0:T(8,128)S(1)}, f32[32,128]{1,0:T(8,128)S(1)}, u32[]{:S(2)}, u32[]{:S(2)}) collective-permute-start(f32[32,128]{1,0:T(8,128)S(1)} %get-tuple-element.52.refs_0_), channel_id=1, source_target_pairs={{0,12},{4,0},{8,4},{12,8},{1,13},{5,1},{9,5},{13,9},{2,14},{6,2},{... | collective-permute-start | bytes 49160 | tf_op jit(solution)/shard_map/ppermute | solution.py:520
  84.6 3.2 %shard_map.77 = f32[32,2048]{1,0:T(8,128)} custom-call(s32[3]{0:T(128)S(1)} %pad_add_fusion.me, bf16[128,2048]{1,0:T(8,128)(2,1)S(1)} %get-tuple-element.51.mapped, f32[32,128]{1,0:T(8,128)S(1)} %get-tuple-element.52.refs_0_, f32[32,128]{1,0:T(8,128)S(1)} %collective-permute-done.27.refs_1_, f32[32,128]{1,0:T(8,128)S(1)} %collective-permute-done.28.refs_2_, ...), custom_call_target="tpu_custom_call" | custom-call | tf_op jit(solution)/shard_map/pallas_call | solution.py:28
  (56 shorter events, 15.1 us)
Async XLA Ops:
  2.0 7.0 %collective-permute-start = (s32[3,8]{1,0:T(4,128)S(1)}, s32[3,8]{1,0:T(4,128)S(1)}, u32[]{:S(2)}, u32[]{:S(2)}) collective-permute-start(s32[3,8]{1,0:T(4,128)S(1)} %concatenate.3.refs_0_), channel_id=1, source_target_pairs={{0,4},{4,8},{8,12},{12,0},{1,5},{5,9},{9,13},{13,1},{2,6},{6,10},{... | collective-permute-start | bytes 296 | tf_op jit(solution)/shard_map/ppermute | solution.py:520
  5.0 4.5 %collective-permute-start.1 = (s32[3,8]{1,0:T(4,128)S(1)}, s32[3,8]{1,0:T(4,128)S(1)}, u32[]{:S(2)}, u32[]{:S(2)}) collective-permute-start(s32[3,8]{1,0:T(4,128)S(1)} %concatenate.3.refs_0_), channel_id=1, source_target_pairs={{0,8},{4,12},{8,0},{12,4},{1,9},{5,13},{9,1},{13,5},{2,10},{6,14},... | collective-permute-start | bytes 296 | tf_op jit(solution)/shard_map/ppermute | solution.py:520
  7.6 3.6 %collective-permute-start.2 = (s32[3,8]{1,0:T(4,128)S(1)}, s32[3,8]{1,0:T(4,128)S(1)}, u32[]{:S(2)}, u32[]{:S(2)}) collective-permute-start(s32[3,8]{1,0:T(4,128)S(1)} %concatenate.3.refs_0_), channel_id=1, source_target_pairs={{0,12},{4,0},{8,4},{12,8},{1,13},{5,1},{9,5},{13,9},{2,14},{6,2},{... | collective-permute-start | bytes 296 | tf_op jit(solution)/shard_map/ppermute | solution.py:520
  9.0 3.9 %copy-start = (bf16[2048,384]{1,0:T(8,128)(2,1)S(1)}, bf16[2048,384]{1,0:T(8,128)(2,1)}, u32[]{:S(2)}) copy-start(bf16[2048,384]{1,0:T(8,128)(2,1)} %emb.7) | copy-start | bytes 4718596
  13.6 8.6 %collective-permute-start.3 = (bf16[256,384]{1,0:T(8,128)(2,1)S(1)}, bf16[256,384]{1,0:T(8,128)(2,1)S(1)}, u32[]{:S(2)}, u32[]{:S(2)}) collective-permute-start(bf16[256,384]{1,0:T(8,128)(2,1)S(1)} %get-tuple-element.28), channel_id=1, source_target_pairs={{0,12},{4,0},{8,4},{12,8},{1,13},{5,1},{9,5},{13,9},{2,14},{6,2},{... | collective-permute-start | bytes 589832 | tf_op jit(solution)/shard_map/ppermute | solution.py:520
  16.8 14.6 %collective-permute-start.4 = (bf16[256,384]{1,0:T(8,128)(2,1)S(1)}, bf16[256,384]{1,0:T(8,128)(2,1)S(1)}, u32[]{:S(2)}, u32[]{:S(2)}) collective-permute-start(bf16[256,384]{1,0:T(8,128)(2,1)S(1)} %get-tuple-element.29), channel_id=1, source_target_pairs={{0,8},{4,12},{8,0},{12,4},{1,9},{5,13},{9,1},{13,5},{2,10},{6,14},... | collective-permute-start | bytes 589832 | tf_op jit(solution)/shard_map/ppermute | solution.py:520
  16.8 14.6 %collective-permute-start.5 = (bf16[256,384]{1,0:T(8,128)(2,1)S(1)}, bf16[256,384]{1,0:T(8,128)(2,1)S(1)}, u32[]{:S(2)}, u32[]{:S(2)}) collective-permute-start(bf16[256,384]{1,0:T(8,128)(2,1)S(1)} %get-tuple-element.30), channel_id=1, source_target_pairs={{0,4},{4,8},{8,12},{12,0},{1,5},{5,9},{9,13},{13,1},{2,6},{6,10},{... | collective-permute-start | bytes 589832 | tf_op jit(solution)/shard_map/ppermute | solution.py:520
  18.8 13.8 %copy-start.1 = (f32[2048,32]{0,1:T(8,128)S(1)}, f32[2048,32]{0,1:T(8,128)}, u32[]{:S(2)}) copy-start(f32[2048,32]{0,1:T(8,128)} %param.5) | copy-start | bytes 786436
  18.8 13.9 %collective-permute-start.7 = (f32[1024,128]{1,0:T(8,128)S(1)}, f32[1024,128]{1,0:T(8,128)S(1)}, u32[]{:S(2)}, u32[]{:S(2)}) collective-permute-start(f32[1024,128]{1,0:T(8,128)S(1)} %shard_map.63.mine), channel_id=1, source_target_pairs={{0,1},{1,0},{2,3},{3,2},{4,5},{5,4},{6,7},{7,6},{8,9},{9,8},{10,11... | collective-permute-start | bytes 1572872 | tf_op jit(solution)/shard_map/ppermute | solution.py:520
  32.5 2.0 %collective-permute-start.6 = (f32[1024,128]{1,0:T(8,128)S(1)}, f32[1024,128]{1,0:T(8,128)S(1)}, u32[]{:S(2)}, u32[]{:S(2)}) collective-permute-start(f32[1024,128]{1,0:T(8,128)S(1)} %shard_map.62.mine), channel_id=1, source_target_pairs={{0,1},{1,0},{2,3},{3,2},{4,5},{5,4},{6,7},{7,6},{8,9},{9,8},{10,11... | collective-permute-start | bytes 1572872 | tf_op jit(solution)/shard_map/ppermute | solution.py:520
  35.4 6.7 %collective-permute-start.10 = (f32[64,128]{1,0:T(8,128)S(1)}, f32[64,128]{1,0:T(8,128)S(1)}, u32[]{:S(2)}, u32[]{:S(2)}) collective-permute-start(f32[64,128]{1,0:T(8,128)S(1)} %get-tuple-element.35), channel_id=1, source_target_pairs={{0,12},{4,0},{8,4},{12,8},{1,13},{5,1},{9,5},{13,9},{2,14},{6,2},{... | collective-permute-start | bytes 98312 | tf_op jit(solution)/shard_map/ppermute | solution.py:520
  36.2 8.2 %collective-permute-start.8 = (f32[64,128]{1,0:T(8,128)S(1)}, f32[64,128]{1,0:T(8,128)S(1)}, u32[]{:S(2)}, u32[]{:S(2)}) collective-permute-start(f32[64,128]{1,0:T(8,128)S(1)} %get-tuple-element.35), channel_id=1, source_target_pairs={{0,4},{4,8},{8,12},{12,0},{1,5},{5,9},{9,13},{13,1},{2,6},{6,10},{... | collective-permute-start | bytes 98312 | tf_op jit(solution)/shard_map/ppermute | solution.py:520
  37.5 7.0 %collective-permute-start.9 = (f32[64,128]{1,0:T(8,128)S(1)}, f32[64,128]{1,0:T(8,128)S(1)}, u32[]{:S(2)}, u32[]{:S(2)}) collective-permute-start(f32[64,128]{1,0:T(8,128)S(1)} %get-tuple-element.35), channel_id=1, source_target_pairs={{0,8},{4,12},{8,0},{12,4},{1,9},{5,13},{9,1},{13,5},{2,10},{6,14},... | collective-permute-start | bytes 98312 | tf_op jit(solution)/shard_map/ppermute | solution.py:520
  40.6 7.8 %collective-permute-start.12 = (s16[272,128]{1,0:T(8,128)(2,1)S(1)}, s16[272,128]{1,0:T(8,128)(2,1)S(1)}, u32[]{:S(2)}, u32[]{:S(2)}) collective-permute-start(s16[272,128]{1,0:T(8,128)(2,1)S(1)} %get-tuple-element.41), channel_id=1, source_target_pairs={{0,4},{4,8},{8,12},{12,0},{1,5},{5,9},{9,13},{13,1},{2,6},{6,10},{... | collective-permute-start | bytes 208904 | tf_op jit(solution)/shard_map/ppermute | solution.py:520
  40.6 8.1 %collective-permute-start.13 = (s16[272,128]{1,0:T(8,128)(2,1)S(1)}, s16[272,128]{1,0:T(8,128)(2,1)S(1)}, u32[]{:S(2)}, u32[]{:S(2)}) collective-permute-start(s16[272,128]{1,0:T(8,128)(2,1)S(1)} %get-tuple-element.42), channel_id=1, source_target_pairs={{0,8},{4,12},{8,0},{12,4},{1,9},{5,13},{9,1},{13,5},{2,10},{6,14},... | collective-permute-start | bytes 208904 | tf_op jit(solution)/shard_map/ppermute | solution.py:520
  42.1 6.6 %collective-permute-start.14 = (s16[272,128]{1,0:T(8,128)(2,1)S(1)}, s16[272,128]{1,0:T(8,128)(2,1)S(1)}, u32[]{:S(2)}, u32[]{:S(2)}) collective-permute-start(s16[272,128]{1,0:T(8,128)(2,1)S(1)} %get-tuple-element.43), channel_id=1, source_target_pairs={{0,12},{4,0},{8,4},{12,8},{1,13},{5,1},{9,5},{13,9},{2,14},{6,2},{... | collective-permute-start | bytes 208904 | tf_op jit(solution)/shard_map/ppermute | solution.py:520
  44.4 4.0 %collective-permute-start.11 = (f32[64,128]{1,0:T(8,128)S(1)}, f32[64,128]{1,0:T(8,128)S(1)}, u32[]{:S(2)}, u32[]{:S(2)}) collective-permute-start(f32[64,128]{1,0:T(8,128)S(1)} %add_add_fusion.mine), channel_id=1, source_target_pairs={{0,2},{2,0},{1,3},{3,1},{4,6},{6,4},{5,7},{7,5},{8,10},{10,8},{9,1... | collective-permute-start | bytes 98312 | tf_op jit(solution)/shard_map/ppermute | solution.py:528
  48.7 1.5 %collective-permute-start.15 = (bf16[1,256,128]{2,1,0:T(8,128)(2,1)S(1)}, bf16[1,256,128]{2,1,0:T(8,128)(2,1)S(1)}, u32[]{:S(2)}, u32[]{:S(2)}) collective-permute-start(bf16[1,256,128]{2,1,0:T(8,128)(2,1)S(1)} %get-tuple-element.44.refs_0_), channel_id=1, source_target_pairs={{0,1},{1,0},{2,3},{3,2},{4,5},{5,4},{6,7},{7,6},{8,9},{9,8},{10,11... | collective-permute-start | bytes 196616 | tf_op jit(solution)/shard_map/ppermute | solution.py:520
  48.8 1.5 %collective-permute-start.16 = (bf16[1,256,128]{2,1,0:T(8,128)(2,1)S(1)}, bf16[1,256,128]{2,1,0:T(8,128)(2,1)S(1)}, u32[]{:S(2)}, u32[]{:S(2)}) collective-permute-start(bf16[1,256,128]{2,1,0:T(8,128)(2,1)S(1)} %get-tuple-element.45.refs_1_), channel_id=1, source_target_pairs={{0,1},{1,0},{2,3},{3,2},{4,5},{5,4},{6,7},{7,6},{8,9},{9,8},{10,11... | collective-permute-start | bytes 196616 | tf_op jit(solution)/shard_map/ppermute | solution.py:520
  49.3 1.3 %collective-permute-start.17 = (bf16[1,256,128]{2,1,0:T(8,128)(2,1)S(1)}, bf16[1,256,128]{2,1,0:T(8,128)(2,1)S(1)}, u32[]{:S(2)}, u32[]{:S(2)}) collective-permute-start(bf16[1,256,128]{2,1,0:T(8,128)(2,1)S(1)} %get-tuple-element.46.refs_2_), channel_id=1, source_target_pairs={{0,1},{1,0},{2,3},{3,2},{4,5},{5,4},{6,7},{7,6},{8,9},{9,8},{10,11... | collective-permute-start | bytes 196616 | tf_op jit(solution)/shard_map/ppermute | solution.py:520
  51.6 5.8 %collective-permute-start.18 = (s16[32,2176]{1,0:T(8,128)(2,1)S(1)}, s16[32,2176]{1,0:T(8,128)(2,1)S(1)}, u32[]{:S(2)}, u32[]{:S(2)}) collective-permute-start(s16[32,2176]{1,0:T(8,128)(2,1)S(1)} %shard_map.69.mine), channel_id=1, source_target_pairs={{0,2},{2,0},{1,3},{3,1},{4,6},{6,4},{5,7},{7,5},{8,10},{10,8},{9,1... | collective-permute-start | bytes 417800 | tf_op jit(solution)/shard_map/ppermute | solution.py:528
  58.3 4.8 %collective-permute-start.19 = (f32[32,2048]{1,0:T(8,128)S(1)}, f32[32,2048]{1,0:T(8,128)S(1)}, u32[]{:S(2)}, u32[]{:S(2)}) collective-permute-start(f32[32,2048]{1,0:T(8,128)S(1)} %get-tuple-element.47.own), channel_id=1, source_target_pairs={{0,1},{1,0},{2,3},{3,2},{4,5},{5,4},{6,7},{7,6},{8,9},{9,8},{10,11... | collective-permute-start | bytes 786440 | tf_op jit(solution)/shard_map/ppermute | solution.py:520
  58.4 6.1 %collective-permute-start.20 = (s16[144,128]{1,0:T(8,128)(2,1)S(1)}, s16[144,128]{1,0:T(8,128)(2,1)S(1)}, u32[]{:S(2)}, u32[]{:S(2)}) collective-permute-start(s16[144,128]{1,0:T(8,128)(2,1)S(1)} %get-tuple-element.48), channel_id=1, source_target_pairs={{0,4},{4,8},{8,12},{12,0},{1,5},{5,9},{9,13},{13,1},{2,6},{6,10},{... | collective-permute-start | bytes 110600 | tf_op jit(solution)/shard_map/ppermute | solution.py:520
  59.8 6.0 %collective-permute-start.21 = (s16[144,128]{1,0:T(8,128)(2,1)S(1)}, s16[144,128]{1,0:T(8,128)(2,1)S(1)}, u32[]{:S(2)}, u32[]{:S(2)}) collective-permute-start(s16[144,128]{1,0:T(8,128)(2,1)S(1)} %get-tuple-element.49), channel_id=1, source_target_pairs={{0,8},{4,12},{8,0},{12,4},{1,9},{5,13},{9,1},{13,5},{2,10},{6,14},... | collective-permute-start | bytes 110600 | tf_op jit(solution)/shard_map/ppermute | solution.py:520
  61.1 4.6 %collective-permute-start.22 = (s16[144,128]{1,0:T(8,128)(2,1)S(1)}, s16[144,128]{1,0:T(8,128)(2,1)S(1)}, u32[]{:S(2)}, u32[]{:S(2)}) collective-permute-start(s16[144,128]{1,0:T(8,128)(2,1)S(1)} %get-tuple-element.50), channel_id=1, source_target_pairs={{0,12},{4,0},{8,4},{12,8},{1,13},{5,1},{9,5},{13,9},{2,14},{6,2},{... | collective-permute-start | bytes 110600 | tf_op jit(solution)/shard_map/ppermute | solution.py:520
  64.1 3.8 %collective-permute-start.23 = (f32[32,128]{1,0:T(8,128)S(1)}, f32[32,128]{1,0:T(8,128)S(1)}, u32[]{:S(2)}, u32[]{:S(2)}) collective-permute-start(f32[32,128]{1,0:T(8,128)S(1)} %shard_map.71.after), channel_id=1, source_target_pairs={{0,4},{4,0},{8,12},{12,8},{1,5},{5,1},{9,13},{13,9},{2,6},{6,2},{1... | collective-permute-start | bytes 49160 | tf_op jit(solution)/shard_map/ppermute | solution.py:528
  68.0 6.2 %collective-permute-start.24 = (s16[32,2176]{1,0:T(8,128)(2,1)S(1)}, s16[32,2176]{1,0:T(8,128)(2,1)S(1)}, u32[]{:S(2)}, u32[]{:S(2)}) collective-permute-start(s16[32,2176]{1,0:T(8,128)(2,1)S(1)} %shard_map.73.mine), channel_id=1, source_target_pairs={{0,2},{2,0},{1,3},{3,1},{4,6},{6,4},{5,7},{7,5},{8,10},{10,8},{9,1... | collective-permute-start | bytes 417800 | tf_op jit(solution)/shard_map/ppermute | solution.py:528
  69.6 4.6 %collective-permute-start.25 = (f32[32,128]{1,0:T(8,128)S(1)}, f32[32,128]{1,0:T(8,128)S(1)}, u32[]{:S(2)}, u32[]{:S(2)}) collective-permute-start(f32[32,128]{1,0:T(8,128)S(1)} %add.20.after.refs_0_), channel_id=1, source_target_pairs={{0,8},{4,12},{8,0},{12,4},{1,9},{5,13},{9,1},{13,5},{2,10},{6,14},... | collective-permute-start | bytes 49160 | tf_op jit(solution)/shard_map/ppermute | solution.py:528
  74.8 1.8 %collective-permute-start.26 = (f32[32,2048]{1,0:T(8,128)S(1)}, f32[32,2048]{1,0:T(8,128)S(1)}, u32[]{:S(2)}, u32[]{:S(2)}) collective-permute-start(f32[32,2048]{1,0:T(8,128)S(1)} %shard_map.74.after.own), channel_id=1, source_target_pairs={{0,1},{1,0},{2,3},{3,2},{4,5},{5,4},{6,7},{7,6},{8,9},{9,8},{10,11... | collective-permute-start | bytes 786440 | tf_op jit(solution)/shard_map/ppermute | solution.py:520
  78.0 5.7 %collective-permute-start.27 = (f32[32,128]{1,0:T(8,128)S(1)}, f32[32,128]{1,0:T(8,128)S(1)}, u32[]{:S(2)}, u32[]{:S(2)}) collective-permute-start(f32[32,128]{1,0:T(8,128)S(1)} %get-tuple-element.52.refs_0_), channel_id=1, source_target_pairs={{0,4},{4,8},{8,12},{12,0},{1,5},{5,9},{9,13},{13,1},{2,6},{6,10},{... | collective-permute-start | bytes 49160 | tf_op jit(solution)/shard_map/ppermute | solution.py:520
  78.2 5.5 %collective-permute-start.28 = (f32[32,128]{1,0:T(8,128)S(1)}, f32[32,128]{1,0:T(8,128)S(1)}, u32[]{:S(2)}, u32[]{:S(2)}) collective-permute-start(f32[32,128]{1,0:T(8,128)S(1)} %get-tuple-element.52.refs_0_), channel_id=1, source_target_pairs={{0,8},{4,12},{8,0},{12,4},{1,9},{5,13},{9,1},{13,5},{2,10},{6,14},... | collective-permute-start | bytes 49160 | tf_op jit(solution)/shard_map/ppermute | solution.py:520
  80.8 3.7 %collective-permute-start.29 = (f32[32,128]{1,0:T(8,128)S(1)}, f32[32,128]{1,0:T(8,128)S(1)}, u32[]{:S(2)}, u32[]{:S(2)}) collective-permute-start(f32[32,128]{1,0:T(8,128)S(1)} %get-tuple-element.52.refs_0_), channel_id=1, source_target_pairs={{0,12},{4,0},{8,4},{12,8},{1,13},{5,1},{9,5},{13,9},{2,14},{6,2},{... | collective-permute-start | bytes 49160 | tf_op jit(solution)/shard_map/ppermute | solution.py:520

commit v14 on v13

--- a/solution.py
+++ b/solution.py
@@ -22,7 +22,7 @@
 NT = (((1,), (1,)), ((), ()))
 
 
-def call(body, outs, args, smem_in=(), smem_out=(), any_in=(), scratch=(), cost=0):
+def call(body, outs, args, smem_in=(), smem_out=(), any_in=(), scratch=(), vmem=48):
     single = not isinstance(outs, (list, tuple))
     shapes = [outs] if single else list(outs)
     result = pl.pallas_call(
@@ -33,10 +33,7 @@
         ],
         out_specs=[SMEM if i in smem_out else VMEM for i in range(len(shapes))],
         scratch_shapes=list(scratch),
-        cost_estimate=pl.CostEstimate(flops=cost * 10**9, bytes_accessed=0, transcendentals=0)
-        if cost
-        else None,
-        compiler_params=pltpu.CompilerParams(vmem_limit_bytes=48 * 2**20),
+        compiler_params=pltpu.CompilerParams(vmem_limit_bytes=vmem * 2**20),
     )(*args)
     return result[0] if single else result
 
@@ -176,68 +173,77 @@
     )
 
 
-def plan_body(dims, me, *refs):
+def quotient(value, size):
+    if size & (size - 1) == 0:
+        return lax.shift_right_logical(value, jnp.int32(size.bit_length() - 1))
+    return lax.div(value, jnp.int32(size))
+
+
+def remainder(value, size):
+    if size & (size - 1) == 0:
+        return lax.bitwise_and(value, jnp.int32(size - 1))
+    return lax.rem(value, jnp.int32(size))
+
+
+def plan_body(dims, me, lists, emb, idx, *refs):
+    sends, arrived = refs[:-1], refs[-1]
     row_count, capacity, slots, blocks_here = dims
-    lists, idx = refs[:row_count], refs[row_count]
     row = me[0]
-
     for i in range(slots):
         for line in (0, 1, 2, 4, 5):
             idx[line, i] = 0
 
-    def ranked(listed, want, write):
-        count = listed[2, 0]
-
-        def step(s, counts):
-            near = listed[0, s]
-            far = listed[1, s]
-            return write(s, near, far, far // blocks_here, s < count, counts)
-
+    def each(count, step, start):
         if slots <= 8:
-            counts = (0,) * want
             for s in range(slots):
-                counts = step(s, counts)
+                start = step(s, start)
         else:
-            lax.fori_loop(0, slots, step, (0,) * want)
-
-    def write_own(s, near, far, owner, live, counts):
-        shift = lax.rem(owner - row + row_count, row_count)
-        rank = functools.reduce(
-            lambda total, k: total + jnp.where(shift == k, counts[k], 0), range(row_count), 0
-        )
-
-        @pl.when(live)
-        def _():
-            slot = shift * capacity + rank
+            lax.fori_loop(0, slots, step, start)
+
+    for k in range(row_count):
+        source = remainder(row - k + row_count, row_count)
+        live_count = lists[source, 2, 0]
+
+        def step(s, counts, k=k, source=source, live_count=live_count):
+            near = lists[source, 0, s]
+            far = lists[source, 1, s]
+            owner = quotient(far, blocks_here)
+            live = s < live_count
+            hit = live & (owner == row)
+            slot = jnp.where(hit, k * capacity + counts[0], slots)
+            idx[4, slot] = far - row * blocks_here
+            idx[5, slot] = near
+            if k > 0:
+                return (counts[0] + hit.astype(jnp.int32),)
+            shift = remainder(owner - row + row_count, row_count)
+            rank = counts[1]
+            for d in range(1, row_count):
+                rank = jnp.where(shift == d, counts[1 + d], rank)
+            slot = jnp.where(live, shift * capacity + rank, slots)
             idx[0, slot] = near - row * blocks_here
             idx[1, slot] = far
             idx[2, slot] = 1
-
-        return tuple(
-            counts[k] + (live & (shift == k)).astype(jnp.int32) for k in range(row_count)
-        )
-
-    for k in range(row_count):
-        if k == 0:
-            ranked(lists[k], row_count, write_own)
-
-        def write_in(s, near, far, owner, live, counts, k=k):
-            hit = live & (owner == row)
-
-            @pl.when(hit)
-            def _():
-                slot = k * capacity + counts[0]
-                idx[4, slot] = far - row * blocks_here
-                idx[5, slot] = near
-
-            return (counts[0] + hit.astype(jnp.int32),)
-
-        ranked(lists[k], 1, write_in)
-
-def pick_body(row_count, capacity, idx, emb, *sends):
+            more = tuple(
+                counts[1 + d] + (live & (shift == d)).astype(jnp.int32) for d in range(row_count)
+            )
+            return (counts[0] + hit.astype(jnp.int32), *more)
+
+        each(slots, step, (jnp.int32(0),) * (1 + row_count if k == 0 else 1))
+    copies = []
     for k in range(1, row_count):
         for j in range(capacity):
-            sends[k - 1][j * BLOCK : (j + 1) * BLOCK, :] = emb[at_block(idx[4, k * capacity + j]), :]
+            slot = k * capacity + j
+            copies.append(
+                pltpu.make_async_copy(
+                    emb.at[at_block(idx[4, slot]), :],
+                    sends[k - 1].at[j * BLOCK : (j + 1) * BLOCK, :],
+                    arrived.at[slot - capacity],
+                )
+            )
+    for copy in copies:
+        copy.start()
+    for copy in copies:
+        copy.wait()
 
 
 def squares(block):
@@ -520,6 +526,10 @@
     return lax.ppermute(value, axes, [(i, (i + shift) % size) for i in range(size)])
 
 
+def exchange(value):
+    return lax.all_to_all(value, "rows", split_axis=0, concat_axis=0, tiled=True)
+
+
 def row_terms(value, row_count):
     return [value] + [shift_by(value, "rows", row_count, k) for k in range(1, row_count)]
 
@@ -559,21 +569,19 @@
     own_list = jnp.concatenate(
         [pair_list[0], jnp.broadcast_to(pair_count[:, None], (1, slots))], axis=0
     )
-    lists = row_terms(own_list, row_count)
-    idx = call(
+    own_list = jnp.pad(own_list, ((0, 5), (0, BLOCK - slots)))
+    lists = exchange(jnp.broadcast_to(own_list[None], (row_count, 8, BLOCK)))
+    planned = call(
         functools.partial(plan_body, (row_count, capacity, slots, blocks_here)),
-        sds((6, slots), jnp.int32),
-        [me, *lists],
-        smem_in=range(1 + row_count),
+        [sds((6, slots + 1), jnp.int32)] + [sds((capacity * BLOCK, half_features), BF16) for _ in others],
+        [me, lists, embeddings],
+        smem_in=(0, 1),
+        any_in=(2,),
         smem_out=(0,),
-        cost=3,
-    )
-    sends = call(
-        functools.partial(pick_body, row_count, capacity),
-        [sds((capacity * BLOCK, half_features), BF16) for _ in others],
-        [idx, embeddings],
-        smem_in=(0,),
-    )
+        scratch=[pltpu.SemaphoreType.DMA((slots - capacity,))],
+        vmem=53,
+    )
+    idx, sends = planned[0], planned[1:]
     far = [shift_by(sends[k - 1], "rows", row_count, -k) for k in others]
 
     self_part = call(

time: 87.9 us -> 90.9 us (1.034)
  waiting for transfers between devices: 31.5 us -> 34.8 us
  starting transfers between devices: 35.5 us -> 33.8 us
    ppermute x25 -> x22, starting transfers between devices: 29.6 us -> 20.4 us  [shift_by(): lax.ppermute(value, axes, [(i, (i + shift) % size) for i in range(size)])]
    all_to_all x0 -> x1, starting transfers between devices: none -> 6.32 us  [exchange(): lax.all_to_all(value, 'rows', split_axis=0, concat_axis=0, tiled=True)]
    all_to_all x0 -> x1, waiting for transfers between devices: none -> 5.54 us  [exchange(): lax.all_to_all(value, 'rows', split_axis=0, concat_axis=0, tiled=True)]
    ppermute x5, waiting for transfers between devices: 11.3 us -> 9.92 us  [pair_step(): lax.ppermute(value, name, [(i, i ^ flip) for i in range(lax.axis_size(nam...]
    ppermute x5, starting transfers between devices: 5.87 us -> 7.17 us  [pair_step(): lax.ppermute(value, name, [(i, i ^ flip) for i in range(lax.axis_size(nam...]
    ppermute x25 -> x22, waiting for transfers between devices: 20.2 us -> 19.3 us  [shift_by(): lax.ppermute(value, axes, [(i, (i + shift) % size) for i in range(size)])]
    pallas_call x19 -> x18, Pallas kernels: 17.9 us -> 18.4 us  [call(): pl.pallas_call(body, out_shape=shapes, in_specs=[SMEM if i in smem_in els...]
  transfers between devices with their start and end apart: 30 -> 28, of which waited for: 15 -> 14; matrix products, arithmetic and copies ran while one was open for 1% -> 1% of each run, Pallas kernels for 8% -> 8%
where the time goes in v14:
time: 90.9 us; the launch traced here: 90.6 us
  waiting for transfers between devices  34.8 us (38%)
  starting transfers between devices  33.8 us (37%)
  Pallas kernels  18.4 us (20%)
  between operations  1.58 us (2%)
  local copies, waits for them, and re-layouts  1.22 us (1%)
    ppermute x22, starting transfers between devices, shift_by(): lax.ppermute(value, axes, [(i, (i + shift) % size) for i in range(size)])  20.4 us
    ppermute x22, waiting for transfers between devices, shift_by(): lax.ppermute(value, axes, [(i, (i + shift) % size) for i in range(size)])  19.3 us
    pallas_call x18, Pallas kernels, call(): pl.pallas_call(body, out_shape=shapes, in_specs=[SMEM if i in smem_in els...  18.4 us
    ppermute x5, waiting for transfers between devices, pair_step(): lax.ppermute(value, name, [(i, i ^ flip) for i in range(lax.axis_size(nam...  9.92 us
    ppermute x5, starting transfers between devices, pair_step(): lax.ppermute(value, name, [(i, i ^ flip) for i in range(lax.axis_size(nam...  7.17 us
    all_to_all x1, starting transfers between devices, exchange(): lax.all_to_all(value, 'rows', split_axis=0, concat_axis=0, tiled=True)  6.32 us
    all_to_all x1, waiting for transfers between devices, exchange(): lax.all_to_all(value, 'rows', split_axis=0, concat_axis=0, tiled=True)  5.54 us
  transfers between devices with their start and end apart: 28, of which 14 were waited for; matrix products, arithmetic and copies ran while one was open for 1% of the time, Pallas kernels for 8%

profile of v14, /device:TPU:0, one launch (start us, length us, event | category | flops | bytes accessed | tf_op | source)
XLA Modules:
  0.0 90.6 jit_solution(14797866800799403425)
XLA Ops:
  2.7 6.3 %all-to-all-start = ((s32[4,8,128]{2,1,0:T(8,128)}), s32[4,8,128]{2,1,0:T(8,128)S(1)}, u32[]{:S(2)}, u32[]{:S(2)}) async-start(s32[4,8,128]{2,1,0:T(8,128)} %broadcast_in_dim.5), calls=%async_computation | async-start | bytes 32768 | tf_op jit(solution)/shard_map/all_to_all | solution.py:530
  9.1 5.5 %all-to-all-done.lists = s32[4,8,128]{2,1,0:T(8,128)S(1)} async-done(((s32[4,8,128]{2,1,0:T(8,128)}), s32[4,8,128]{2,1,0:T(8,128)S(1)}, u32[]{:S(2)}, u32[]{:S(2)}) %all-to-all-start) | async-done | bytes 16416 | tf_op jit(solution)/shard_map/all_to_all | solution.py:530
  14.6 2.9 %shard_map.59 = (s32[6,9]{1,0:T(8,128)S(1)}, bf16[256,384]{1,0:T(8,128)(2,1)S(1)}, bf16[256,384]{1,0:T(8,128)(2,1)S(1)}, bf16[256,384]{1,0:T(8,128)(2,1)S(1)}) custom-call(s32[3]{0:T(128)S(1)} %pad_add_fusion.me, s32[4,8,128]{2,1,0:T(8,128)S(1)} %all-to-all-done.lists, bf16[2048,384]{1,0:T(8,128)(2,1)} %emb.7), custom_call_target="tpu_custom_call" | custom-call | tf_op jit(solution)/shard_map/pallas_call | solution.py:28
  18.2 1.5 %collective-permute-start.1 = (bf16[256,384]{1,0:T(8,128)(2,1)S(1)}, bf16[256,384]{1,0:T(8,128)(2,1)S(1)}, u32[]{:S(2)}, u32[]{:S(2)}) collective-permute-start(bf16[256,384]{1,0:T(8,128)(2,1)S(1)} %get-tuple-element.31), channel_id=1, source_target_pairs={{0,8},{4,12},{8,0},{12,4},{1,9},{5,13},{9,1},{13,5},{2,10},{6,14},... | collective-permute-start | bytes 589832 | tf_op jit(solution)/shard_map/ppermute | solution.py:526
  20.6 1.0 %shard_map.62.mine = f32[1024,128]{1,0:T(8,128)S(1)} custom-call(s32[3]{0:T(128)S(1)} %pad_add_fusion.me, bf16[2048,384]{1,0:T(8,128)(2,1)S(1)} %copy-done, s32[6,9]{1,0:T(8,128)S(1)} %get-tuple-element.29.after.idx), custom_call_target="tpu_custom_call" | custom-call | tf_op jit(solution)/shard_map/pallas_call | solution.py:28
  21.7 2.2 %collective-permute-done.refs_0_ = bf16[256,384]{1,0:T(8,128)(2,1)S(1)} collective-permute-done((bf16[256,384]{1,0:T(8,128)(2,1)S(1)}, bf16[256,384]{1,0:T(8,128)(2,1)S(1)}, u32[]{:S(2)}, u32[]{:S(2)}) %collective-permute-start) | collective-permute-done | bytes 196640 | tf_op jit(solution)/shard_map/ppermute | solution.py:526
  23.9 11.6 %collective-permute-done.1.refs_1_ = bf16[256,384]{1,0:T(8,128)(2,1)S(1)} collective-permute-done((bf16[256,384]{1,0:T(8,128)(2,1)S(1)}, bf16[256,384]{1,0:T(8,128)(2,1)S(1)}, u32[]{:S(2)}, u32[]{:S(2)}) %collective-permute-start.1) | collective-permute-done | bytes 196640 | tf_op jit(solution)/shard_map/ppermute | solution.py:526
  35.5 1.1 %shard_map.61.mine = f32[1024,128]{1,0:T(8,128)S(1)} custom-call(s32[6,9]{1,0:T(8,128)S(1)} %get-tuple-element.29.after.idx, bf16[2048,384]{1,0:T(8,128)(2,1)S(1)} %copy-done, f32[2048,128]{1,0:T(8,128)S(1)} %shard_map.60.own_squares, bf16[256,384]{1,0:T(8,128)(2,1)S(1)} %collective-permute-done.refs_0_, ...), custom_call_target="tpu_custom_call" | custom-call | tf_op jit(solution)/shard_map/pallas_call | solution.py:28
  37.0 1.5 %collective-permute-done.3.other = f32[1024,128]{1,0:T(8,128)S(1)} collective-permute-done((f32[1024,128]{1,0:T(8,128)S(1)}, f32[1024,128]{1,0:T(8,128)S(1)}, u32[]{:S(2)}, u32[]{:S(2)}) %collective-permute-start.3) | collective-permute-done | bytes 524320 | tf_op jit(solution)/shard_map/ppermute | solution.py:526
  39.6 1.7 %collective-permute-start.6 = (f32[64,128]{1,0:T(8,128)S(1)}, f32[64,128]{1,0:T(8,128)S(1)}, u32[]{:S(2)}, u32[]{:S(2)}) collective-permute-start(f32[64,128]{1,0:T(8,128)S(1)} %get-tuple-element.37), channel_id=1, source_target_pairs={{0,8},{4,12},{8,0},{12,4},{1,9},{5,13},{9,1},{13,5},{2,10},{6,14},... | collective-permute-start | bytes 98312 | tf_op jit(solution)/shard_map/ppermute | solution.py:526
  41.3 2.8 %collective-permute-start.7 = (f32[64,128]{1,0:T(8,128)S(1)}, f32[64,128]{1,0:T(8,128)S(1)}, u32[]{:S(2)}, u32[]{:S(2)}) collective-permute-start(f32[64,128]{1,0:T(8,128)S(1)} %get-tuple-element.37), channel_id=1, source_target_pairs={{0,12},{4,0},{8,4},{12,8},{1,13},{5,1},{9,5},{13,9},{2,14},{6,2},{... | collective-permute-start | bytes 98312 | tf_op jit(solution)/shard_map/ppermute | solution.py:526
  44.1 1.3 %collective-permute-start.10 = (s16[272,128]{1,0:T(8,128)(2,1)S(1)}, s16[272,128]{1,0:T(8,128)(2,1)S(1)}, u32[]{:S(2)}, u32[]{:S(2)}) collective-permute-start(s16[272,128]{1,0:T(8,128)(2,1)S(1)} %get-tuple-element.44), channel_id=1, source_target_pairs={{0,8},{4,12},{8,0},{12,4},{1,9},{5,13},{9,1},{13,5},{2,10},{6,14},... | collective-permute-start | bytes 208904 | tf_op jit(solution)/shard_map/ppermute | solution.py:526
  46.3 1.1 %collective-permute-start.9 = (s16[272,128]{1,0:T(8,128)(2,1)S(1)}, s16[272,128]{1,0:T(8,128)(2,1)S(1)}, u32[]{:S(2)}, u32[]{:S(2)}) collective-permute-start(s16[272,128]{1,0:T(8,128)(2,1)S(1)} %get-tuple-element.43), channel_id=1, source_target_pairs={{0,4},{4,8},{8,12},{12,0},{1,5},{5,9},{9,13},{13,1},{2,6},{6,10},{... | collective-permute-start | bytes 208904 | tf_op jit(solution)/shard_map/ppermute | solution.py:526
  47.5 1.6 %collective-permute-start.8 = (f32[64,128]{1,0:T(8,128)S(1)}, f32[64,128]{1,0:T(8,128)S(1)}, u32[]{:S(2)}, u32[]{:S(2)}) collective-permute-start(f32[64,128]{1,0:T(8,128)S(1)} %add_add_fusion.mine), channel_id=1, source_target_pairs={{0,2},{2,0},{1,3},{3,1},{4,6},{6,4},{5,7},{7,5},{8,10},{10,8},{9,1... | collective-permute-start | bytes 98312 | tf_op jit(solution)/shard_map/ppermute | solution.py:538
  49.0 2.4 %collective-permute-done.8.other.refs_3_ = f32[64,128]{1,0:T(8,128)S(1)} collective-permute-done((f32[64,128]{1,0:T(8,128)S(1)}, f32[64,128]{1,0:T(8,128)S(1)}, u32[]{:S(2)}, u32[]{:S(2)}) %collective-permute-start.8) | collective-permute-done | bytes 32800 | tf_op jit(solution)/shard_map/ppermute | solution.py:538
  51.4 1.1 %collective-permute-done.9.refs_0_.refs_6_ = s16[272,128]{1,0:T(8,128)(2,1)S(1)} collective-permute-done((s16[272,128]{1,0:T(8,128)(2,1)S(1)}, s16[272,128]{1,0:T(8,128)(2,1)S(1)}, u32[]{:S(2)}, u32[]{:S(2)}) %collective-permute-start.9) | collective-permute-done | bytes 69664 | tf_op jit(solution)/shard_map/ppermute | solution.py:526
  54.4 1.0 %shard_map.68.mine = s16[32,2176]{1,0:T(8,128)(2,1)S(1)} custom-call(s32[3]{0:T(128)S(1)} %pad_add_fusion.me, s32[6,9]{1,0:T(8,128)S(1)} %get-tuple-element.29.after.idx, f32[64,128]{1,0:T(8,128)S(1)} %get-tuple-element.41.inverse, f32[32,2048]{1,0:T(8,128)S(1)} %get-tuple-element.42.started, bf16[8,256,128]{2,1,0:T(8,128)(2,1)S(1)} %get-tuple-element.38.near_tiles, ...), custom_call_target="tpu_custom_call" | custom-call | tf_op jit(solution)/shard_map/pallas_call | solution.py:28
  55.4 1.6 %collective-permute-start.15 = (s16[32,2176]{1,0:T(8,128)(2,1)S(1)}, s16[32,2176]{1,0:T(8,128)(2,1)S(1)}, u32[]{:S(2)}, u32[]{:S(2)}) collective-permute-start(s16[32,2176]{1,0:T(8,128)(2,1)S(1)} %shard_map.68.mine), channel_id=1, source_target_pairs={{0,2},{2,0},{1,3},{3,1},{4,6},{6,4},{5,7},{7,5},{8,10},{10,8},{9,1... | collective-permute-start | bytes 417800 | tf_op jit(solution)/shard_map/ppermute | solution.py:538
  57.0 4.3 %collective-permute-done.15.other = s16[32,2176]{1,0:T(8,128)(2,1)S(1)} collective-permute-done((s16[32,2176]{1,0:T(8,128)(2,1)S(1)}, s16[32,2176]{1,0:T(8,128)(2,1)S(1)}, u32[]{:S(2)}, u32[]{:S(2)}) %collective-permute-start.15) | collective-permute-done | bytes 139296 | tf_op jit(solution)/shard_map/ppermute | solution.py:538
  63.0 1.5 %collective-permute-start.18 = (s16[144,128]{1,0:T(8,128)(2,1)S(1)}, s16[144,128]{1,0:T(8,128)(2,1)S(1)}, u32[]{:S(2)}, u32[]{:S(2)}) collective-permute-start(s16[144,128]{1,0:T(8,128)(2,1)S(1)} %get-tuple-element.51), channel_id=1, source_target_pairs={{0,8},{4,12},{8,0},{12,4},{1,9},{5,13},{9,1},{13,5},{2,10},{6,14},... | collective-permute-start | bytes 110600 | tf_op jit(solution)/shard_map/ppermute | solution.py:526
  64.5 1.6 %collective-permute-start.19 = (s16[144,128]{1,0:T(8,128)(2,1)S(1)}, s16[144,128]{1,0:T(8,128)(2,1)S(1)}, u32[]{:S(2)}, u32[]{:S(2)}) collective-permute-start(s16[144,128]{1,0:T(8,128)(2,1)S(1)} %get-tuple-element.52), channel_id=1, source_target_pairs={{0,12},{4,0},{8,4},{12,8},{1,13},{5,1},{9,5},{13,9},{2,14},{6,2},{... | collective-permute-start | bytes 110600 | tf_op jit(solution)/shard_map/ppermute | solution.py:526
  66.1 1.0 %shard_map.70.after = f32[32,128]{1,0:T(8,128)S(1)} custom-call(s32[3]{0:T(128)S(1)} %pad_add_fusion.me, f32[32,2048]{1,0:T(8,128)S(1)} %get-tuple-element.49.own, f32[32,2048]{1,0:T(8,128)S(1)} %collective-permute-done.16.other), custom_call_target="tpu_custom_call" | custom-call | tf_op jit(solution)/shard_map/pallas_call | solution.py:28
  68.4 1.0 %collective-permute-done.18.refs_7_ = s16[144,128]{1,0:T(8,128)(2,1)S(1)} collective-permute-done((s16[144,128]{1,0:T(8,128)(2,1)S(1)}, s16[144,128]{1,0:T(8,128)(2,1)S(1)}, u32[]{:S(2)}, u32[]{:S(2)}) %collective-permute-start.18) | collective-permute-done | bytes 36896 | tf_op jit(solution)/shard_map/ppermute | solution.py:526
  69.3 1.0 %shard_map.71.total = f32[32,2048]{1,0:T(8,128)S(1)} custom-call(s32[3]{0:T(128)S(1)} %pad_add_fusion.me, s32[6,9]{1,0:T(8,128)S(1)} %get-tuple-element.29.after.idx, f32[64,128]{1,0:T(8,128)S(1)} %get-tuple-element.41.inverse, f32[32,128]{1,0:T(8,128)S(1)} %shard_map.70.after, f32[32,2048]{1,0:T(8,128)S(1)} %get-tuple-element.49.own, ...), custom_call_target="tpu_custom_call" | custom-call | tf_op jit(solution)/shard_map/pallas_call | solution.py:28
  71.0 1.6 %collective-permute-start.21 = (s16[32,2176]{1,0:T(8,128)(2,1)S(1)}, s16[32,2176]{1,0:T(8,128)(2,1)S(1)}, u32[]{:S(2)}, u32[]{:S(2)}) collective-permute-start(s16[32,2176]{1,0:T(8,128)(2,1)S(1)} %shard_map.72.mine), channel_id=1, source_target_pairs={{0,2},{2,0},{1,3},{3,1},{4,6},{6,4},{5,7},{7,5},{8,10},{10,8},{9,1... | collective-permute-start | bytes 417800 | tf_op jit(solution)/shard_map/ppermute | solution.py:538
  72.6 2.0 %collective-permute-start.22 = (f32[32,128]{1,0:T(8,128)S(1)}, f32[32,128]{1,0:T(8,128)S(1)}, u32[]{:S(2)}, u32[]{:S(2)}) collective-permute-start(f32[32,128]{1,0:T(8,128)S(1)} %add.22.after.refs_0_), channel_id=1, source_target_pairs={{0,8},{4,12},{8,0},{12,4},{1,9},{5,13},{9,1},{13,5},{2,10},{6,14},... | collective-permute-start | bytes 49160 | tf_op jit(solution)/shard_map/ppermute | solution.py:538
  74.5 2.7 %collective-permute-done.22.after.refs_1_ = f32[32,128]{1,0:T(8,128)S(1)} collective-permute-done((f32[32,128]{1,0:T(8,128)S(1)}, f32[32,128]{1,0:T(8,128)S(1)}, u32[]{:S(2)}, u32[]{:S(2)}) %collective-permute-start.22) | collective-permute-done | bytes 16416 | tf_op jit(solution)/shard_map/ppermute | solution.py:538
  77.9 1.7 %shard_map.74.factor = f32[64,64]{1,0:T(8,128)S(1)} custom-call(f32[32,2048]{1,0:T(8,128)S(1)} %shard_map.73.after.own, f32[32,128]{1,0:T(8,128)S(1)} %add.22.after.refs_0_, f32[32,128]{1,0:T(8,128)S(1)} %collective-permute-done.22.after.refs_1_), custom_call_target="tpu_custom_call" | custom-call | tf_op jit(solution)/shard_map/pallas_call | solution.py:28
  79.7 1.4 %shard_map.75 = (bf16[128,2048]{1,0:T(8,128)(2,1)S(1)}, f32[32,128]{1,0:T(8,128)S(1)}) custom-call(s32[3]{0:T(128)S(1)} %pad_add_fusion.me, f32[64,64]{1,0:T(8,128)S(1)} %shard_map.74.factor, f32[32,2048]{1,0:T(8,128)S(1)} %shard_map.73.after.own, f32[32,2048]{1,0:T(8,128)S(1)} %collective-permute-done.23.other), custom_call_target="tpu_custom_call" | custom-call | tf_op jit(solution)/shard_map/pallas_call | solution.py:28
  81.8 1.9 %collective-permute-start.25 = (f32[32,128]{1,0:T(8,128)S(1)}, f32[32,128]{1,0:T(8,128)S(1)}, u32[]{:S(2)}, u32[]{:S(2)}) collective-permute-start(f32[32,128]{1,0:T(8,128)S(1)} %get-tuple-element.54.refs_0_), channel_id=1, source_target_pairs={{0,8},{4,12},{8,0},{12,4},{1,9},{5,13},{9,1},{13,5},{2,10},{6,14},... | collective-permute-start | bytes 49160 | tf_op jit(solution)/shard_map/ppermute | solution.py:526
  83.6 2.3 %collective-permute-start.26 = (f32[32,128]{1,0:T(8,128)S(1)}, f32[32,128]{1,0:T(8,128)S(1)}, u32[]{:S(2)}, u32[]{:S(2)}) collective-permute-start(f32[32,128]{1,0:T(8,128)S(1)} %get-tuple-element.54.refs_0_), channel_id=1, source_target_pairs={{0,12},{4,0},{8,4},{12,8},{1,13},{5,1},{9,5},{13,9},{2,14},{6,2},{... | collective-permute-start | bytes 49160 | tf_op jit(solution)/shard_map/ppermute | solution.py:526
  87.4 3.2 %shard_map.76 = f32[32,2048]{1,0:T(8,128)} custom-call(s32[3]{0:T(128)S(1)} %pad_add_fusion.me, bf16[128,2048]{1,0:T(8,128)(2,1)S(1)} %get-tuple-element.53.mapped, f32[32,128]{1,0:T(8,128)S(1)} %get-tuple-element.54.refs_0_, f32[32,128]{1,0:T(8,128)S(1)} %collective-permute-done.24.refs_1_, f32[32,128]{1,0:T(8,128)S(1)} %collective-permute-done.25.refs_2_, ...), custom_call_target="tpu_custom_call" | custom-call | tf_op jit(solution)/shard_map/pallas_call | solution.py:28
  (52 shorter events, 13.8 us)
Async XLA Ops:
  0.6 19.6 %copy-start = (bf16[2048,384]{1,0:T(8,128)(2,1)S(1)}, bf16[2048,384]{1,0:T(8,128)(2,1)}, u32[]{:S(2)}) copy-start(bf16[2048,384]{1,0:T(8,128)(2,1)} %emb.7) | copy-start | bytes 4718596
  2.7 11.9 %all-to-all-start = ((s32[4,8,128]{2,1,0:T(8,128)}), s32[4,8,128]{2,1,0:T(8,128)S(1)}, u32[]{:S(2)}, u32[]{:S(2)}) async-start(s32[4,8,128]{2,1,0:T(8,128)} %broadcast_in_dim.5), calls=%async_computation | async-start | bytes 32768 | tf_op jit(solution)/shard_map/all_to_all | solution.py:530
  17.5 6.4 %collective-permute-start = (bf16[256,384]{1,0:T(8,128)(2,1)S(1)}, bf16[256,384]{1,0:T(8,128)(2,1)S(1)}, u32[]{:S(2)}, u32[]{:S(2)}) collective-permute-start(bf16[256,384]{1,0:T(8,128)(2,1)S(1)} %get-tuple-element.30), channel_id=1, source_target_pairs={{0,12},{4,0},{8,4},{12,8},{1,13},{5,1},{9,5},{13,9},{2,14},{6,2},{... | collective-permute-start | bytes 589832 | tf_op jit(solution)/shard_map/ppermute | solution.py:526
  18.2 17.3 %collective-permute-start.1 = (bf16[256,384]{1,0:T(8,128)(2,1)S(1)}, bf16[256,384]{1,0:T(8,128)(2,1)S(1)}, u32[]{:S(2)}, u32[]{:S(2)}) collective-permute-start(bf16[256,384]{1,0:T(8,128)(2,1)S(1)} %get-tuple-element.31), channel_id=1, source_target_pairs={{0,8},{4,12},{8,0},{12,4},{1,9},{5,13},{9,1},{13,5},{2,10},{6,14},... | collective-permute-start | bytes 589832 | tf_op jit(solution)/shard_map/ppermute | solution.py:526
  19.7 15.8 %collective-permute-start.2 = (bf16[256,384]{1,0:T(8,128)(2,1)S(1)}, bf16[256,384]{1,0:T(8,128)(2,1)S(1)}, u32[]{:S(2)}, u32[]{:S(2)}) collective-permute-start(bf16[256,384]{1,0:T(8,128)(2,1)S(1)} %get-tuple-element.32), channel_id=1, source_target_pairs={{0,4},{4,8},{8,12},{12,0},{1,5},{5,9},{9,13},{13,1},{2,6},{6,10},{... | collective-permute-start | bytes 589832 | tf_op jit(solution)/shard_map/ppermute | solution.py:526
  21.6 15.1 %copy-start.1 = (f32[2048,32]{0,1:T(8,128)S(1)}, f32[2048,32]{0,1:T(8,128)}, u32[]{:S(2)}) copy-start(f32[2048,32]{0,1:T(8,128)} %param.5) | copy-start | bytes 786436
  21.6 15.2 %collective-permute-start.4 = (f32[1024,128]{1,0:T(8,128)S(1)}, f32[1024,128]{1,0:T(8,128)S(1)}, u32[]{:S(2)}, u32[]{:S(2)}) collective-permute-start(f32[1024,128]{1,0:T(8,128)S(1)} %shard_map.62.mine), channel_id=1, source_target_pairs={{0,1},{1,0},{2,3},{3,2},{4,5},{5,4},{6,7},{7,6},{8,9},{9,8},{10,11... | collective-permute-start | bytes 1572872 | tf_op jit(solution)/shard_map/ppermute | solution.py:526
  36.6 2.0 %collective-permute-start.3 = (f32[1024,128]{1,0:T(8,128)S(1)}, f32[1024,128]{1,0:T(8,128)S(1)}, u32[]{:S(2)}, u32[]{:S(2)}) collective-permute-start(f32[1024,128]{1,0:T(8,128)S(1)} %shard_map.61.mine), channel_id=1, source_target_pairs={{0,1},{1,0},{2,3},{3,2},{4,5},{5,4},{6,7},{7,6},{8,9},{9,8},{10,11... | collective-permute-start | bytes 1572872 | tf_op jit(solution)/shard_map/ppermute | solution.py:526
  39.5 6.8 %collective-permute-start.5 = (f32[64,128]{1,0:T(8,128)S(1)}, f32[64,128]{1,0:T(8,128)S(1)}, u32[]{:S(2)}, u32[]{:S(2)}) collective-permute-start(f32[64,128]{1,0:T(8,128)S(1)} %get-tuple-element.37), channel_id=1, source_target_pairs={{0,4},{4,8},{8,12},{12,0},{1,5},{5,9},{9,13},{13,1},{2,6},{6,10},{... | collective-permute-start | bytes 98312 | tf_op jit(solution)/shard_map/ppermute | solution.py:526
  39.6 7.9 %collective-permute-start.6 = (f32[64,128]{1,0:T(8,128)S(1)}, f32[64,128]{1,0:T(8,128)S(1)}, u32[]{:S(2)}, u32[]{:S(2)}) collective-permute-start(f32[64,128]{1,0:T(8,128)S(1)} %get-tuple-element.37), channel_id=1, source_target_pairs={{0,8},{4,12},{8,0},{12,4},{1,9},{5,13},{9,1},{13,5},{2,10},{6,14},... | collective-permute-start | bytes 98312 | tf_op jit(solution)/shard_map/ppermute | solution.py:526
  41.3 6.1 %collective-permute-start.7 = (f32[64,128]{1,0:T(8,128)S(1)}, f32[64,128]{1,0:T(8,128)S(1)}, u32[]{:S(2)}, u32[]{:S(2)}) collective-permute-start(f32[64,128]{1,0:T(8,128)S(1)} %get-tuple-element.37), channel_id=1, source_target_pairs={{0,12},{4,0},{8,4},{12,8},{1,13},{5,1},{9,5},{13,9},{2,14},{6,2},{... | collective-permute-start | bytes 98312 | tf_op jit(solution)/shard_map/ppermute | solution.py:526
  44.1 7.3 %collective-permute-start.10 = (s16[272,128]{1,0:T(8,128)(2,1)S(1)}, s16[272,128]{1,0:T(8,128)(2,1)S(1)}, u32[]{:S(2)}, u32[]{:S(2)}) collective-permute-start(s16[272,128]{1,0:T(8,128)(2,1)S(1)} %get-tuple-element.44), channel_id=1, source_target_pairs={{0,8},{4,12},{8,0},{12,4},{1,9},{5,13},{9,1},{13,5},{2,10},{6,14},... | collective-permute-start | bytes 208904 | tf_op jit(solution)/shard_map/ppermute | solution.py:526
  45.4 6.0 %collective-permute-start.11 = (s16[272,128]{1,0:T(8,128)(2,1)S(1)}, s16[272,128]{1,0:T(8,128)(2,1)S(1)}, u32[]{:S(2)}, u32[]{:S(2)}) collective-permute-start(s16[272,128]{1,0:T(8,128)(2,1)S(1)} %get-tuple-element.45), channel_id=1, source_target_pairs={{0,12},{4,0},{8,4},{12,8},{1,13},{5,1},{9,5},{13,9},{2,14},{6,2},{... | collective-permute-start | bytes 208904 | tf_op jit(solution)/shard_map/ppermute | solution.py:526
  46.3 6.2 %collective-permute-start.9 = (s16[272,128]{1,0:T(8,128)(2,1)S(1)}, s16[272,128]{1,0:T(8,128)(2,1)S(1)}, u32[]{:S(2)}, u32[]{:S(2)}) collective-permute-start(s16[272,128]{1,0:T(8,128)(2,1)S(1)} %get-tuple-element.43), channel_id=1, source_target_pairs={{0,4},{4,8},{8,12},{12,0},{1,5},{5,9},{9,13},{13,1},{2,6},{6,10},{... | collective-permute-start | bytes 208904 | tf_op jit(solution)/shard_map/ppermute | solution.py:526
  47.5 4.0 %collective-permute-start.8 = (f32[64,128]{1,0:T(8,128)S(1)}, f32[64,128]{1,0:T(8,128)S(1)}, u32[]{:S(2)}, u32[]{:S(2)}) collective-permute-start(f32[64,128]{1,0:T(8,128)S(1)} %add_add_fusion.mine), channel_id=1, source_target_pairs={{0,2},{2,0},{1,3},{3,1},{4,6},{6,4},{5,7},{7,5},{8,10},{10,8},{9,1... | collective-permute-start | bytes 98312 | tf_op jit(solution)/shard_map/ppermute | solution.py:538
  52.6 1.5 %collective-permute-start.12 = (bf16[1,256,128]{2,1,0:T(8,128)(2,1)S(1)}, bf16[1,256,128]{2,1,0:T(8,128)(2,1)S(1)}, u32[]{:S(2)}, u32[]{:S(2)}) collective-permute-start(bf16[1,256,128]{2,1,0:T(8,128)(2,1)S(1)} %get-tuple-element.46.refs_0_), channel_id=1, source_target_pairs={{0,1},{1,0},{2,3},{3,2},{4,5},{5,4},{6,7},{7,6},{8,9},{9,8},{10,11... | collective-permute-start | bytes 196616 | tf_op jit(solution)/shard_map/ppermute | solution.py:526
  52.7 1.5 %collective-permute-start.13 = (bf16[1,256,128]{2,1,0:T(8,128)(2,1)S(1)}, bf16[1,256,128]{2,1,0:T(8,128)(2,1)S(1)}, u32[]{:S(2)}, u32[]{:S(2)}) collective-permute-start(bf16[1,256,128]{2,1,0:T(8,128)(2,1)S(1)} %get-tuple-element.47.refs_1_), channel_id=1, source_target_pairs={{0,1},{1,0},{2,3},{3,2},{4,5},{5,4},{6,7},{7,6},{8,9},{9,8},{10,11... | collective-permute-start | bytes 196616 | tf_op jit(solution)/shard_map/ppermute | solution.py:526
  53.2 1.3 %collective-permute-start.14 = (bf16[1,256,128]{2,1,0:T(8,128)(2,1)S(1)}, bf16[1,256,128]{2,1,0:T(8,128)(2,1)S(1)}, u32[]{:S(2)}, u32[]{:S(2)}) collective-permute-start(bf16[1,256,128]{2,1,0:T(8,128)(2,1)S(1)} %get-tuple-element.48.refs_2_), channel_id=1, source_target_pairs={{0,1},{1,0},{2,3},{3,2},{4,5},{5,4},{6,7},{7,6},{8,9},{9,8},{10,11... | collective-permute-start | bytes 196616 | tf_op jit(solution)/shard_map/ppermute | solution.py:526
  55.4 5.8 %collective-permute-start.15 = (s16[32,2176]{1,0:T(8,128)(2,1)S(1)}, s16[32,2176]{1,0:T(8,128)(2,1)S(1)}, u32[]{:S(2)}, u32[]{:S(2)}) collective-permute-start(s16[32,2176]{1,0:T(8,128)(2,1)S(1)} %shard_map.68.mine), channel_id=1, source_target_pairs={{0,2},{2,0},{1,3},{3,1},{4,6},{6,4},{5,7},{7,5},{8,10},{10,8},{9,1... | collective-permute-start | bytes 417800 | tf_op jit(solution)/shard_map/ppermute | solution.py:538
  62.1 4.0 %collective-permute-start.16 = (f32[32,2048]{1,0:T(8,128)S(1)}, f32[32,2048]{1,0:T(8,128)S(1)}, u32[]{:S(2)}, u32[]{:S(2)}) collective-permute-start(f32[32,2048]{1,0:T(8,128)S(1)} %get-tuple-element.49.own), channel_id=1, source_target_pairs={{0,1},{1,0},{2,3},{3,2},{4,5},{5,4},{6,7},{7,6},{8,9},{9,8},{10,11... | collective-permute-start | bytes 786440 | tf_op jit(solution)/shard_map/ppermute | solution.py:526
  62.2 6.2 %collective-permute-start.17 = (s16[144,128]{1,0:T(8,128)(2,1)S(1)}, s16[144,128]{1,0:T(8,128)(2,1)S(1)}, u32[]{:S(2)}, u32[]{:S(2)}) collective-permute-start(s16[144,128]{1,0:T(8,128)(2,1)S(1)} %get-tuple-element.50), channel_id=1, source_target_pairs={{0,4},{4,8},{8,12},{12,0},{1,5},{5,9},{9,13},{13,1},{2,6},{6,10},{... | collective-permute-start | bytes 110600 | tf_op jit(solution)/shard_map/ppermute | solution.py:526
  63.0 6.3 %collective-permute-start.18 = (s16[144,128]{1,0:T(8,128)(2,1)S(1)}, s16[144,128]{1,0:T(8,128)(2,1)S(1)}, u32[]{:S(2)}, u32[]{:S(2)}) collective-permute-start(s16[144,128]{1,0:T(8,128)(2,1)S(1)} %get-tuple-element.51), channel_id=1, source_target_pairs={{0,8},{4,12},{8,0},{12,4},{1,9},{5,13},{9,1},{13,5},{2,10},{6,14},... | collective-permute-start | bytes 110600 | tf_op jit(solution)/shard_map/ppermute | solution.py:526
  64.5 4.8 %collective-permute-start.19 = (s16[144,128]{1,0:T(8,128)(2,1)S(1)}, s16[144,128]{1,0:T(8,128)(2,1)S(1)}, u32[]{:S(2)}, u32[]{:S(2)}) collective-permute-start(s16[144,128]{1,0:T(8,128)(2,1)S(1)} %get-tuple-element.52), channel_id=1, source_target_pairs={{0,12},{4,0},{8,4},{12,8},{1,13},{5,1},{9,5},{13,9},{2,14},{6,2},{... | collective-permute-start | bytes 110600 | tf_op jit(solution)/shard_map/ppermute | solution.py:526
  67.1 3.8 %collective-permute-start.20 = (f32[32,128]{1,0:T(8,128)S(1)}, f32[32,128]{1,0:T(8,128)S(1)}, u32[]{:S(2)}, u32[]{:S(2)}) collective-permute-start(f32[32,128]{1,0:T(8,128)S(1)} %shard_map.70.after), channel_id=1, source_target_pairs={{0,4},{4,0},{8,12},{12,8},{1,5},{5,1},{9,13},{13,9},{2,6},{6,2},{1... | collective-permute-start | bytes 49160 | tf_op jit(solution)/shard_map/ppermute | solution.py:538
  71.0 6.2 %collective-permute-start.21 = (s16[32,2176]{1,0:T(8,128)(2,1)S(1)}, s16[32,2176]{1,0:T(8,128)(2,1)S(1)}, u32[]{:S(2)}, u32[]{:S(2)}) collective-permute-start(s16[32,2176]{1,0:T(8,128)(2,1)S(1)} %shard_map.72.mine), channel_id=1, source_target_pairs={{0,2},{2,0},{1,3},{3,1},{4,6},{6,4},{5,7},{7,5},{8,10},{10,8},{9,1... | collective-permute-start | bytes 417800 | tf_op jit(solution)/shard_map/ppermute | solution.py:538
  72.6 4.6 %collective-permute-start.22 = (f32[32,128]{1,0:T(8,128)S(1)}, f32[32,128]{1,0:T(8,128)S(1)}, u32[]{:S(2)}, u32[]{:S(2)}) collective-permute-start(f32[32,128]{1,0:T(8,128)S(1)} %add.22.after.refs_0_), channel_id=1, source_target_pairs={{0,8},{4,12},{8,0},{12,4},{1,9},{5,13},{9,1},{13,5},{2,10},{6,14},... | collective-permute-start | bytes 49160 | tf_op jit(solution)/shard_map/ppermute | solution.py:538
  77.9 1.8 %collective-permute-start.23 = (f32[32,2048]{1,0:T(8,128)S(1)}, f32[32,2048]{1,0:T(8,128)S(1)}, u32[]{:S(2)}, u32[]{:S(2)}) collective-permute-start(f32[32,2048]{1,0:T(8,128)S(1)} %shard_map.73.after.own), channel_id=1, source_target_pairs={{0,1},{1,0},{2,3},{3,2},{4,5},{5,4},{6,7},{7,6},{8,9},{9,8},{10,11... | collective-permute-start | bytes 786440 | tf_op jit(solution)/shard_map/ppermute | solution.py:526
  81.0 5.7 %collective-permute-start.24 = (f32[32,128]{1,0:T(8,128)S(1)}, f32[32,128]{1,0:T(8,128)S(1)}, u32[]{:S(2)}, u32[]{:S(2)}) collective-permute-start(f32[32,128]{1,0:T(8,128)S(1)} %get-tuple-element.54.refs_0_), channel_id=1, source_target_pairs={{0,4},{4,8},{8,12},{12,0},{1,5},{5,9},{9,13},{13,1},{2,6},{6,10},{... | collective-permute-start | bytes 49160 | tf_op jit(solution)/shard_map/ppermute | solution.py:526
  81.8 4.9 %collective-permute-start.25 = (f32[32,128]{1,0:T(8,128)S(1)}, f32[32,128]{1,0:T(8,128)S(1)}, u32[]{:S(2)}, u32[]{:S(2)}) collective-permute-start(f32[32,128]{1,0:T(8,128)S(1)} %get-tuple-element.54.refs_0_), channel_id=1, source_target_pairs={{0,8},{4,12},{8,0},{12,4},{1,9},{5,13},{9,1},{13,5},{2,10},{6,14},... | collective-permute-start | bytes 49160 | tf_op jit(solution)/shard_map/ppermute | solution.py:526
  83.6 3.7 %collective-permute-start.26 = (f32[32,128]{1,0:T(8,128)S(1)}, f32[32,128]{1,0:T(8,128)S(1)}, u32[]{:S(2)}, u32[]{:S(2)}) collective-permute-start(f32[32,128]{1,0:T(8,128)S(1)} %get-tuple-element.54.refs_0_), channel_id=1, source_target_pairs={{0,12},{4,0},{8,4},{12,8},{1,13},{5,1},{9,5},{13,9},{2,14},{6,2},{... | collective-permute-start | bytes 49160 | tf_op jit(solution)/shard_map/ppermute | solution.py:526

commit v15 on v14

--- a/solution.py
+++ b/solution.py
@@ -22,7 +22,7 @@
 NT = (((1,), (1,)), ((), ()))
 
 
-def call(body, outs, args, smem_in=(), smem_out=(), any_in=(), scratch=(), vmem=48):
+def call(body, outs, args, smem_in=(), smem_out=(), any_in=(), scratch=()):
     single = not isinstance(outs, (list, tuple))
     shapes = [outs] if single else list(outs)
     result = pl.pallas_call(
@@ -33,7 +33,7 @@
         ],
         out_specs=[SMEM if i in smem_out else VMEM for i in range(len(shapes))],
         scratch_shapes=list(scratch),
-        compiler_params=pltpu.CompilerParams(vmem_limit_bytes=vmem * 2**20),
+        compiler_params=pltpu.CompilerParams(vmem_limit_bytes=48 * 2**20),
     )(*args)
     return result[0] if single else result
 
@@ -185,15 +185,16 @@
     return lax.rem(value, jnp.int32(size))
 
 
-def plan_body(dims, me, lists, emb, idx, *refs):
-    sends, arrived = refs[:-1], refs[-1]
+def plan_body(dims, me, *refs):
     row_count, capacity, slots, blocks_here = dims
+    lists, (emb, after, idx) = refs[:row_count], refs[row_count : row_count + 3]
+    sends = refs[row_count + 3 :]
     row = me[0]
     for i in range(slots):
         for line in (0, 1, 2, 4, 5):
             idx[line, i] = 0
 
-    def each(count, step, start):
+    def each(step, start):
         if slots <= 8:
             for s in range(slots):
                 start = step(s, start)
@@ -201,12 +202,11 @@
             lax.fori_loop(0, slots, step, start)
 
     for k in range(row_count):
-        source = remainder(row - k + row_count, row_count)
-        live_count = lists[source, 2, 0]
-
-        def step(s, counts, k=k, source=source, live_count=live_count):
-            near = lists[source, 0, s]
-            far = lists[source, 1, s]
+        live_count = lists[k][2, 0]
+
+        def step(s, counts, k=k, live_count=live_count):
+            near = lists[k][0, s]
+            far = lists[k][1, s]
             owner = quotient(far, blocks_here)
             live = s < live_count
             hit = live & (owner == row)
@@ -228,22 +228,10 @@
             )
             return (counts[0] + hit.astype(jnp.int32), *more)
 
-        each(slots, step, (jnp.int32(0),) * (1 + row_count if k == 0 else 1))
-    copies = []
+        each(step, (jnp.int32(0),) * (1 + row_count if k == 0 else 1))
     for k in range(1, row_count):
         for j in range(capacity):
-            slot = k * capacity + j
-            copies.append(
-                pltpu.make_async_copy(
-                    emb.at[at_block(idx[4, slot]), :],
-                    sends[k - 1].at[j * BLOCK : (j + 1) * BLOCK, :],
-                    arrived.at[slot - capacity],
-                )
-            )
-    for copy in copies:
-        copy.start()
-    for copy in copies:
-        copy.wait()
+            sends[k - 1][j * BLOCK : (j + 1) * BLOCK, :] = emb[at_block(idx[4, k * capacity + j]), :]
 
 
 def squares(block):
@@ -256,7 +244,7 @@
     return left_sq + right_row - 2.0 * inner
 
 
-def self_distance_body(own_blocks, tile_count, me, emb, after, out):
+def self_distance_body(own_blocks, tile_count, me, emb, out):
     for i in range(own_blocks):
         block = emb[at_block(i * tile_count + me[1]), :]
         block_sq = squares(block)
@@ -269,8 +257,9 @@
         out[part, :] = jnp.broadcast_to(squares(emb[part, :]), (BLOCK, BLOCK))
 
 
-def pair_distance_body(row_count, capacity, idx, emb, own_squares, *refs):
-    out = refs[-1]
+def pair_distance_body(order, capacity, idx, emb, own_squares, *refs):
+    far, out = dict(zip(order, refs)), refs[-1]
+    row_count = len(order) + 1
     for k in range(row_count):
         for j in range(capacity):
             slot = k * capacity + j
@@ -280,7 +269,7 @@
                 right = emb[at_block(idx[4, j]), :]
                 right_sq = own_squares[at_block(idx[4, j]), :]
             else:
-                right = refs[k - 1][j * BLOCK : (j + 1) * BLOCK, :]
+                right = far[k][j * BLOCK : (j + 1) * BLOCK, :]
                 right_sq = squares(right)
             part = slice(slot * BLOCK, (slot + 1) * BLOCK)
             out[part, :] = partial_distance(left, right, left_sq, right_sq)
@@ -526,10 +515,6 @@
     return lax.ppermute(value, axes, [(i, (i + shift) % size) for i in range(size)])
 
 
-def exchange(value):
-    return lax.all_to_all(value, "rows", split_axis=0, concat_axis=0, tiled=True)
-
-
 def row_terms(value, row_count):
     return [value] + [shift_by(value, "rows", row_count, k) for k in range(1, row_count)]
 
@@ -569,28 +554,25 @@
     own_list = jnp.concatenate(
         [pair_list[0], jnp.broadcast_to(pair_count[:, None], (1, slots))], axis=0
     )
-    own_list = jnp.pad(own_list, ((0, 5), (0, BLOCK - slots)))
-    lists = exchange(jnp.broadcast_to(own_list[None], (row_count, 8, BLOCK)))
+    lists = row_terms(own_list, row_count)
+    self_part = call(
+        functools.partial(self_distance_body, own_blocks, tile_count),
+        sds((own_blocks * BLOCK, BLOCK), F32),
+        [me, embeddings],
+        smem_in=(0,),
+    )
     planned = call(
         functools.partial(plan_body, (row_count, capacity, slots, blocks_here)),
         [sds((6, slots + 1), jnp.int32)] + [sds((capacity * BLOCK, half_features), BF16) for _ in others],
-        [me, lists, embeddings],
-        smem_in=(0, 1),
-        any_in=(2,),
+        [me, *lists, embeddings, self_part],
+        smem_in=range(1 + row_count),
+        any_in=(row_count + 2,),
         smem_out=(0,),
-        scratch=[pltpu.SemaphoreType.DMA((slots - capacity,))],
-        vmem=53,
     )
     idx, sends = planned[0], planned[1:]
-    far = [shift_by(sends[k - 1], "rows", row_count, -k) for k in others]
-
-    self_part = call(
-        functools.partial(self_distance_body, own_blocks, tile_count),
-        sds((own_blocks * BLOCK, BLOCK), F32),
-        [me, embeddings, idx],
-        smem_in=(0,),
-        any_in=(2,),
-    )
+    order = sorted(others, key=lambda k: abs(k - row_count // 2))
+    far = [shift_by(sends[k - 1], "rows", row_count, -k) for k in order]
+
     self_other = shift_by(self_part, "cols", core_count, 1)
     self_tiles, self_sums = call(
         functools.partial(self_tile_body, own_blocks),
@@ -604,7 +586,7 @@
     coded = tile_count == 2
     own_squares = call(squares_body, sds((rows_here, BLOCK), F32), [embeddings, idx], any_in=(1,))
     pair_part = call(
-        functools.partial(pair_distance_body, row_count, capacity),
+        functools.partial(pair_distance_body, order, capacity),
         sds((slots * BLOCK, BLOCK), F32),
         [idx, embeddings, own_squares, *far],
         smem_in=(0,),

time: 90.9 us -> 86.2 us (0.948)
  waiting for transfers between devices: 34.8 us -> 26.4 us
  starting transfers between devices: 33.8 us -> 38.2 us
  local copies, waits for them, and re-layouts: 1.22 us -> 2.71 us
  Pallas kernels: 18.4 us -> 17.2 us
    ppermute x22 -> x25, starting transfers between devices: 20.4 us -> 30.7 us  [shift_by(): lax.ppermute(value, axes, [(i, (i + shift) % size) for i in range(size)])]
    all_to_all x1 -> x0, starting transfers between devices: 6.32 us -> none  [exchange(): lax.all_to_all(value, 'rows', split_axis=0, concat_axis=0, tiled=True)]
    all_to_all x1 -> x0, waiting for transfers between devices: 5.54 us -> none  [exchange(): lax.all_to_all(value, 'rows', split_axis=0, concat_axis=0, tiled=True)]
    ppermute x22 -> x25, waiting for transfers between devices: 19.3 us -> 16.7 us  [shift_by(): lax.ppermute(value, axes, [(i, (i + shift) % size) for i in range(size)])]
    unnamed x4 -> x6, local copies, waits for them, and re-layouts: 0.01 us -> 1.42 us
    pallas_call x18, Pallas kernels: 18.4 us -> 17.2 us  [call(): pl.pallas_call(body, out_shape=shapes, in_specs=[SMEM if i in smem_in els...]
  transfers between devices with their start and end apart: 28 -> 30, of which waited for: 14 -> 13; matrix products, arithmetic and copies ran while one was open for 1% -> 1% of each run, Pallas kernels for 8% -> 9%
where the time goes in v15:
time: 86.2 us; the launch traced here: 86.1 us
  starting transfers between devices  38.2 us (44%)
  waiting for transfers between devices  26.4 us (31%)
  Pallas kernels  17.2 us (20%)
  local copies, waits for them, and re-layouts  2.71 us (3%)
  between operations  1.48 us (2%)
    ppermute x25, starting transfers between devices, shift_by(): lax.ppermute(value, axes, [(i, (i + shift) % size) for i in range(size)])  30.7 us
    pallas_call x18, Pallas kernels, call(): pl.pallas_call(body, out_shape=shapes, in_specs=[SMEM if i in smem_in els...  17.2 us
    ppermute x25, waiting for transfers between devices, shift_by(): lax.ppermute(value, axes, [(i, (i + shift) % size) for i in range(size)])  16.7 us
    ppermute x5, waiting for transfers between devices, pair_step(): lax.ppermute(value, name, [(i, i ^ flip) for i in range(lax.axis_size(nam...  9.71 us
    ppermute x5, starting transfers between devices, pair_step(): lax.ppermute(value, name, [(i, i ^ flip) for i in range(lax.axis_size(nam...  7.56 us
  transfers between devices with their start and end apart: 30, of which 13 were waited for; matrix products, arithmetic and copies ran while one was open for 1% of the time, Pallas kernels for 9%

profile of v15, /device:TPU:0, one launch (start us, length us, event | category | flops | bytes accessed | tf_op | source)
XLA Modules:
  0.0 86.1 jit_solution(13952974457925532422)
XLA Ops:
  2.0 3.0 %collective-permute-start = (s32[3,8]{1,0:T(4,128)S(1)}, s32[3,8]{1,0:T(4,128)S(1)}, u32[]{:S(2)}, u32[]{:S(2)}) collective-permute-start(s32[3,8]{1,0:T(4,128)S(1)} %concatenate.3.refs_0_), channel_id=1, source_target_pairs={{0,4},{4,8},{8,12},{12,0},{1,5},{5,9},{9,13},{13,1},{2,6},{6,10},{... | collective-permute-start | bytes 296 | tf_op jit(solution)/shard_map/ppermute | solution.py:515
  5.0 2.6 %collective-permute-start.1 = (s32[3,8]{1,0:T(4,128)S(1)}, s32[3,8]{1,0:T(4,128)S(1)}, u32[]{:S(2)}, u32[]{:S(2)}) collective-permute-start(s32[3,8]{1,0:T(4,128)S(1)} %concatenate.3.refs_0_), channel_id=1, source_target_pairs={{0,8},{4,12},{8,0},{12,4},{1,9},{5,13},{9,1},{13,5},{2,10},{6,14},... | collective-permute-start | bytes 296 | tf_op jit(solution)/shard_map/ppermute | solution.py:515
  7.6 1.3 %collective-permute-start.2 = (s32[3,8]{1,0:T(4,128)S(1)}, s32[3,8]{1,0:T(4,128)S(1)}, u32[]{:S(2)}, u32[]{:S(2)}) collective-permute-start(s32[3,8]{1,0:T(4,128)S(1)} %concatenate.3.refs_0_), channel_id=1, source_target_pairs={{0,12},{4,0},{8,4},{12,8},{1,13},{5,1},{9,5},{13,9},{2,14},{6,2},{... | collective-permute-start | bytes 296 | tf_op jit(solution)/shard_map/ppermute | solution.py:515
  9.0 1.4 %copy-done = bf16[2048,384]{1,0:T(8,128)(2,1)S(1)} copy-done((bf16[2048,384]{1,0:T(8,128)(2,1)S(1)}, bf16[2048,384]{1,0:T(8,128)(2,1)}, u32[]{:S(2)}) %copy-start) | copy-done | bytes 1572888
  10.4 1.0 %shard_map.59.refs_5_.mine = f32[1024,128]{1,0:T(8,128)S(1)} custom-call(s32[3]{0:T(128)S(1)} %pad_add_fusion.me, bf16[2048,384]{1,0:T(8,128)(2,1)S(1)} %copy-done), custom_call_target="tpu_custom_call" | custom-call | tf_op jit(solution)/shard_map/pallas_call | solution.py:28
  11.5 1.6 %shard_map.60 = (s32[6,9]{1,0:T(8,128)S(1)}, bf16[256,384]{1,0:T(8,128)(2,1)S(1)}, bf16[256,384]{1,0:T(8,128)(2,1)S(1)}, bf16[256,384]{1,0:T(8,128)(2,1)S(1)}) custom-call(s32[3]{0:T(128)S(1)} %pad_add_fusion.me, s32[3,8]{1,0:T(4,128)S(1)} %concatenate.3.refs_0_, s32[3,8]{1,0:T(4,128)S(1)} %collective-permute-done.refs_1_, ...), custom_call_target="tpu_custom_call" | custom-call | tf_op jit(solution)/shard_map/pallas_call | solution.py:28
  13.8 2.5 %collective-permute-start.4 = (bf16[256,384]{1,0:T(8,128)(2,1)S(1)}, bf16[256,384]{1,0:T(8,128)(2,1)S(1)}, u32[]{:S(2)}, u32[]{:S(2)}) collective-permute-start(bf16[256,384]{1,0:T(8,128)(2,1)S(1)} %get-tuple-element.31), channel_id=1, source_target_pairs={{0,12},{4,0},{8,4},{12,8},{1,13},{5,1},{9,5},{13,9},{2,14},{6,2},{... | collective-permute-start | bytes 589832 | tf_op jit(solution)/shard_map/ppermute | solution.py:515
  17.0 11.6 %collective-permute-done.3.refs_0_ = bf16[256,384]{1,0:T(8,128)(2,1)S(1)} collective-permute-done((bf16[256,384]{1,0:T(8,128)(2,1)S(1)}, bf16[256,384]{1,0:T(8,128)(2,1)S(1)}, u32[]{:S(2)}, u32[]{:S(2)}) %collective-permute-start.3) | collective-permute-done | bytes 196640 | tf_op jit(solution)/shard_map/ppermute | solution.py:515
  28.6 1.1 %shard_map.62.mine = f32[1024,128]{1,0:T(8,128)S(1)} custom-call(s32[6,9]{1,0:T(8,128)S(1)} %get-tuple-element.29.after.idx, bf16[2048,384]{1,0:T(8,128)(2,1)S(1)} %copy-done.1, f32[2048,128]{1,0:T(8,128)S(1)} %shard_map.61.own_squares, bf16[256,384]{1,0:T(8,128)(2,1)S(1)} %collective-permute-done.3.refs_0_, ...), custom_call_target="tpu_custom_call" | custom-call | tf_op jit(solution)/shard_map/pallas_call | solution.py:28
  30.1 1.5 %collective-permute-done.6.other = f32[1024,128]{1,0:T(8,128)S(1)} collective-permute-done((f32[1024,128]{1,0:T(8,128)S(1)}, f32[1024,128]{1,0:T(8,128)S(1)}, u32[]{:S(2)}, u32[]{:S(2)}) %collective-permute-start.6) | collective-permute-done | bytes 524320 | tf_op jit(solution)/shard_map/ppermute | solution.py:515
  32.6 2.6 %collective-permute-start.10 = (f32[64,128]{1,0:T(8,128)S(1)}, f32[64,128]{1,0:T(8,128)S(1)}, u32[]{:S(2)}, u32[]{:S(2)}) collective-permute-start(f32[64,128]{1,0:T(8,128)S(1)} %get-tuple-element.37), channel_id=1, source_target_pairs={{0,12},{4,0},{8,4},{12,8},{1,13},{5,1},{9,5},{13,9},{2,14},{6,2},{... | collective-permute-start | bytes 98312 | tf_op jit(solution)/shard_map/ppermute | solution.py:515
  35.2 2.1 %collective-permute-start.8 = (f32[64,128]{1,0:T(8,128)S(1)}, f32[64,128]{1,0:T(8,128)S(1)}, u32[]{:S(2)}, u32[]{:S(2)}) collective-permute-start(f32[64,128]{1,0:T(8,128)S(1)} %get-tuple-element.37), channel_id=1, source_target_pairs={{0,4},{4,8},{8,12},{12,0},{1,5},{5,9},{9,13},{13,1},{2,6},{6,10},{... | collective-permute-start | bytes 98312 | tf_op jit(solution)/shard_map/ppermute | solution.py:515
  37.2 1.8 %collective-permute-start.9 = (f32[64,128]{1,0:T(8,128)S(1)}, f32[64,128]{1,0:T(8,128)S(1)}, u32[]{:S(2)}, u32[]{:S(2)}) collective-permute-start(f32[64,128]{1,0:T(8,128)S(1)} %get-tuple-element.37), channel_id=1, source_target_pairs={{0,8},{4,12},{8,0},{12,4},{1,9},{5,13},{9,1},{13,5},{2,10},{6,14},... | collective-permute-start | bytes 98312 | tf_op jit(solution)/shard_map/ppermute | solution.py:515
  39.6 2.6 %collective-permute-start.13 = (s16[272,128]{1,0:T(8,128)(2,1)S(1)}, s16[272,128]{1,0:T(8,128)(2,1)S(1)}, u32[]{:S(2)}, u32[]{:S(2)}) collective-permute-start(s16[272,128]{1,0:T(8,128)(2,1)S(1)} %get-tuple-element.44), channel_id=1, source_target_pairs={{0,8},{4,12},{8,0},{12,4},{1,9},{5,13},{9,1},{13,5},{2,10},{6,14},... | collective-permute-start | bytes 208904 | tf_op jit(solution)/shard_map/ppermute | solution.py:515
  43.1 1.6 %collective-permute-start.11 = (f32[64,128]{1,0:T(8,128)S(1)}, f32[64,128]{1,0:T(8,128)S(1)}, u32[]{:S(2)}, u32[]{:S(2)}) collective-permute-start(f32[64,128]{1,0:T(8,128)S(1)} %add_add_fusion.mine), channel_id=1, source_target_pairs={{0,2},{2,0},{1,3},{3,1},{4,6},{6,4},{5,7},{7,5},{8,10},{10,8},{9,1... | collective-permute-start | bytes 98312 | tf_op jit(solution)/shard_map/ppermute | solution.py:523
  44.7 2.4 %collective-permute-done.11.other.refs_3_ = f32[64,128]{1,0:T(8,128)S(1)} collective-permute-done((f32[64,128]{1,0:T(8,128)S(1)}, f32[64,128]{1,0:T(8,128)S(1)}, u32[]{:S(2)}, u32[]{:S(2)}) %collective-permute-start.11) | collective-permute-done | bytes 32800 | tf_op jit(solution)/shard_map/ppermute | solution.py:523
  49.6 1.0 %shard_map.68.mine = s16[32,2176]{1,0:T(8,128)(2,1)S(1)} custom-call(s32[3]{0:T(128)S(1)} %pad_add_fusion.me, s32[6,9]{1,0:T(8,128)S(1)} %get-tuple-element.29.after.idx, f32[64,128]{1,0:T(8,128)S(1)} %get-tuple-element.41.inverse, f32[32,2048]{1,0:T(8,128)S(1)} %get-tuple-element.42.started, bf16[8,256,128]{2,1,0:T(8,128)(2,1)S(1)} %get-tuple-element.38.near_tiles, ...), custom_call_target="tpu_custom_call" | custom-call | tf_op jit(solution)/shard_map/pallas_call | solution.py:28
  50.6 1.6 %collective-permute-start.18 = (s16[32,2176]{1,0:T(8,128)(2,1)S(1)}, s16[32,2176]{1,0:T(8,128)(2,1)S(1)}, u32[]{:S(2)}, u32[]{:S(2)}) collective-permute-start(s16[32,2176]{1,0:T(8,128)(2,1)S(1)} %shard_map.68.mine), channel_id=1, source_target_pairs={{0,2},{2,0},{1,3},{3,1},{4,6},{6,4},{5,7},{7,5},{8,10},{10,8},{9,1... | collective-permute-start | bytes 417800 | tf_op jit(solution)/shard_map/ppermute | solution.py:523
  52.2 4.3 %collective-permute-done.18.other = s16[32,2176]{1,0:T(8,128)(2,1)S(1)} collective-permute-done((s16[32,2176]{1,0:T(8,128)(2,1)S(1)}, s16[32,2176]{1,0:T(8,128)(2,1)S(1)}, u32[]{:S(2)}, u32[]{:S(2)}) %collective-permute-start.18) | collective-permute-done | bytes 139296 | tf_op jit(solution)/shard_map/ppermute | solution.py:523
  57.4 1.6 %collective-permute-start.20 = (s16[144,128]{1,0:T(8,128)(2,1)S(1)}, s16[144,128]{1,0:T(8,128)(2,1)S(1)}, u32[]{:S(2)}, u32[]{:S(2)}) collective-permute-start(s16[144,128]{1,0:T(8,128)(2,1)S(1)} %get-tuple-element.50), channel_id=1, source_target_pairs={{0,4},{4,8},{8,12},{12,0},{1,5},{5,9},{9,13},{13,1},{2,6},{6,10},{... | collective-permute-start | bytes 110600 | tf_op jit(solution)/shard_map/ppermute | solution.py:515
  59.0 1.7 %collective-permute-start.21 = (s16[144,128]{1,0:T(8,128)(2,1)S(1)}, s16[144,128]{1,0:T(8,128)(2,1)S(1)}, u32[]{:S(2)}, u32[]{:S(2)}) collective-permute-start(s16[144,128]{1,0:T(8,128)(2,1)S(1)} %get-tuple-element.51), channel_id=1, source_target_pairs={{0,8},{4,12},{8,0},{12,4},{1,9},{5,13},{9,1},{13,5},{2,10},{6,14},... | collective-permute-start | bytes 110600 | tf_op jit(solution)/shard_map/ppermute | solution.py:515
  62.5 1.2 %collective-permute-start.23 = (f32[32,128]{1,0:T(8,128)S(1)}, f32[32,128]{1,0:T(8,128)S(1)}, u32[]{:S(2)}, u32[]{:S(2)}) collective-permute-start(f32[32,128]{1,0:T(8,128)S(1)} %shard_map.70.after), channel_id=1, source_target_pairs={{0,4},{4,0},{8,12},{12,8},{1,5},{5,1},{9,13},{13,9},{2,6},{6,2},{1... | collective-permute-start | bytes 49160 | tf_op jit(solution)/shard_map/ppermute | solution.py:523
  63.7 1.0 %collective-permute-done.21.refs_7_ = s16[144,128]{1,0:T(8,128)(2,1)S(1)} collective-permute-done((s16[144,128]{1,0:T(8,128)(2,1)S(1)}, s16[144,128]{1,0:T(8,128)(2,1)S(1)}, u32[]{:S(2)}, u32[]{:S(2)}) %collective-permute-start.21) | collective-permute-done | bytes 36896 | tf_op jit(solution)/shard_map/ppermute | solution.py:515
  66.4 1.6 %collective-permute-start.24 = (s16[32,2176]{1,0:T(8,128)(2,1)S(1)}, s16[32,2176]{1,0:T(8,128)(2,1)S(1)}, u32[]{:S(2)}, u32[]{:S(2)}) collective-permute-start(s16[32,2176]{1,0:T(8,128)(2,1)S(1)} %shard_map.72.mine), channel_id=1, source_target_pairs={{0,2},{2,0},{1,3},{3,1},{4,6},{6,4},{5,7},{7,5},{8,10},{10,8},{9,1... | collective-permute-start | bytes 417800 | tf_op jit(solution)/shard_map/ppermute | solution.py:523
  68.0 1.7 %collective-permute-start.25 = (f32[32,128]{1,0:T(8,128)S(1)}, f32[32,128]{1,0:T(8,128)S(1)}, u32[]{:S(2)}, u32[]{:S(2)}) collective-permute-start(f32[32,128]{1,0:T(8,128)S(1)} %add.20.after.refs_0_), channel_id=1, source_target_pairs={{0,8},{4,12},{8,0},{12,4},{1,9},{5,13},{9,1},{13,5},{2,10},{6,14},... | collective-permute-start | bytes 49160 | tf_op jit(solution)/shard_map/ppermute | solution.py:523
  69.7 2.9 %collective-permute-done.25.after.refs_1_ = f32[32,128]{1,0:T(8,128)S(1)} collective-permute-done((f32[32,128]{1,0:T(8,128)S(1)}, f32[32,128]{1,0:T(8,128)S(1)}, u32[]{:S(2)}, u32[]{:S(2)}) %collective-permute-start.25) | collective-permute-done | bytes 16416 | tf_op jit(solution)/shard_map/ppermute | solution.py:523
  73.3 1.7 %shard_map.74.factor = f32[64,64]{1,0:T(8,128)S(1)} custom-call(f32[32,2048]{1,0:T(8,128)S(1)} %shard_map.73.after.own, f32[32,128]{1,0:T(8,128)S(1)} %add.20.after.refs_0_, f32[32,128]{1,0:T(8,128)S(1)} %collective-permute-done.25.after.refs_1_), custom_call_target="tpu_custom_call" | custom-call | tf_op jit(solution)/shard_map/pallas_call | solution.py:28
  75.1 1.4 %shard_map.75 = (bf16[128,2048]{1,0:T(8,128)(2,1)S(1)}, f32[32,128]{1,0:T(8,128)S(1)}) custom-call(s32[3]{0:T(128)S(1)} %pad_add_fusion.me, f32[64,64]{1,0:T(8,128)S(1)} %shard_map.74.factor, f32[32,2048]{1,0:T(8,128)S(1)} %shard_map.73.after.own, f32[32,2048]{1,0:T(8,128)S(1)} %collective-permute-done.26.other), custom_call_target="tpu_custom_call" | custom-call | tf_op jit(solution)/shard_map/pallas_call | solution.py:28
  76.5 1.1 %collective-permute-start.27 = (f32[32,128]{1,0:T(8,128)S(1)}, f32[32,128]{1,0:T(8,128)S(1)}, u32[]{:S(2)}, u32[]{:S(2)}) collective-permute-start(f32[32,128]{1,0:T(8,128)S(1)} %get-tuple-element.54.refs_0_), channel_id=1, source_target_pairs={{0,4},{4,8},{8,12},{12,0},{1,5},{5,9},{9,13},{13,1},{2,6},{6,10},{... | collective-permute-start | bytes 49160 | tf_op jit(solution)/shard_map/ppermute | solution.py:515
  77.6 1.5 %collective-permute-start.28 = (f32[32,128]{1,0:T(8,128)S(1)}, f32[32,128]{1,0:T(8,128)S(1)}, u32[]{:S(2)}, u32[]{:S(2)}) collective-permute-start(f32[32,128]{1,0:T(8,128)S(1)} %get-tuple-element.54.refs_0_), channel_id=1, source_target_pairs={{0,8},{4,12},{8,0},{12,4},{1,9},{5,13},{9,1},{13,5},{2,10},{6,14},... | collective-permute-start | bytes 49160 | tf_op jit(solution)/shard_map/ppermute | solution.py:515
  79.1 2.0 %collective-permute-start.29 = (f32[32,128]{1,0:T(8,128)S(1)}, f32[32,128]{1,0:T(8,128)S(1)}, u32[]{:S(2)}, u32[]{:S(2)}) collective-permute-start(f32[32,128]{1,0:T(8,128)S(1)} %get-tuple-element.54.refs_0_), channel_id=1, source_target_pairs={{0,12},{4,0},{8,4},{12,8},{1,13},{5,1},{9,5},{13,9},{2,14},{6,2},{... | collective-permute-start | bytes 49160 | tf_op jit(solution)/shard_map/ppermute | solution.py:515
  82.9 3.2 %shard_map.76 = f32[32,2048]{1,0:T(8,128)} custom-call(s32[3]{0:T(128)S(1)} %pad_add_fusion.me, bf16[128,2048]{1,0:T(8,128)(2,1)S(1)} %get-tuple-element.53.mapped, f32[32,128]{1,0:T(8,128)S(1)} %get-tuple-element.54.refs_0_, f32[32,128]{1,0:T(8,128)S(1)} %collective-permute-done.27.refs_1_, f32[32,128]{1,0:T(8,128)S(1)} %collective-permute-done.28.refs_2_, ...), custom_call_target="tpu_custom_call" | custom-call | tf_op jit(solution)/shard_map/pallas_call | solution.py:28
  (57 shorter events, 14.4 us)
Async XLA Ops:
  2.0 9.5 %collective-permute-start = (s32[3,8]{1,0:T(4,128)S(1)}, s32[3,8]{1,0:T(4,128)S(1)}, u32[]{:S(2)}, u32[]{:S(2)}) collective-permute-start(s32[3,8]{1,0:T(4,128)S(1)} %concatenate.3.refs_0_), channel_id=1, source_target_pairs={{0,4},{4,8},{8,12},{12,0},{1,5},{5,9},{9,13},{13,1},{2,6},{6,10},{... | collective-permute-start | bytes 296 | tf_op jit(solution)/shard_map/ppermute | solution.py:515
  5.0 6.5 %collective-permute-start.1 = (s32[3,8]{1,0:T(4,128)S(1)}, s32[3,8]{1,0:T(4,128)S(1)}, u32[]{:S(2)}, u32[]{:S(2)}) collective-permute-start(s32[3,8]{1,0:T(4,128)S(1)} %concatenate.3.refs_0_), channel_id=1, source_target_pairs={{0,8},{4,12},{8,0},{12,4},{1,9},{5,13},{9,1},{13,5},{2,10},{6,14},... | collective-permute-start | bytes 296 | tf_op jit(solution)/shard_map/ppermute | solution.py:515
  7.6 3.9 %collective-permute-start.2 = (s32[3,8]{1,0:T(4,128)S(1)}, s32[3,8]{1,0:T(4,128)S(1)}, u32[]{:S(2)}, u32[]{:S(2)}) collective-permute-start(s32[3,8]{1,0:T(4,128)S(1)} %concatenate.3.refs_0_), channel_id=1, source_target_pairs={{0,12},{4,0},{8,4},{12,8},{1,13},{5,1},{9,5},{13,9},{2,14},{6,2},{... | collective-permute-start | bytes 296 | tf_op jit(solution)/shard_map/ppermute | solution.py:515
  11.4 5.2 %copy-start.1 = (bf16[2048,384]{1,0:T(8,128)(2,1)S(1)}, bf16[2048,384]{1,0:T(8,128)(2,1)}, u32[]{:S(2)}) copy-start(bf16[2048,384]{1,0:T(8,128)(2,1)} %emb.5) | copy-start | bytes 4718596
  13.1 15.4 %collective-permute-start.3 = (bf16[256,384]{1,0:T(8,128)(2,1)S(1)}, bf16[256,384]{1,0:T(8,128)(2,1)S(1)}, u32[]{:S(2)}, u32[]{:S(2)}) collective-permute-start(bf16[256,384]{1,0:T(8,128)(2,1)S(1)} %get-tuple-element.30), channel_id=1, source_target_pairs={{0,8},{4,12},{8,0},{12,4},{1,9},{5,13},{9,1},{13,5},{2,10},{6,14},... | collective-permute-start | bytes 589832 | tf_op jit(solution)/shard_map/ppermute | solution.py:515
  13.8 14.8 %collective-permute-start.4 = (bf16[256,384]{1,0:T(8,128)(2,1)S(1)}, bf16[256,384]{1,0:T(8,128)(2,1)S(1)}, u32[]{:S(2)}, u32[]{:S(2)}) collective-permute-start(bf16[256,384]{1,0:T(8,128)(2,1)S(1)} %get-tuple-element.31), channel_id=1, source_target_pairs={{0,12},{4,0},{8,4},{12,8},{1,13},{5,1},{9,5},{13,9},{2,14},{6,2},{... | collective-permute-start | bytes 589832 | tf_op jit(solution)/shard_map/ppermute | solution.py:515
  16.2 12.3 %collective-permute-start.5 = (bf16[256,384]{1,0:T(8,128)(2,1)S(1)}, bf16[256,384]{1,0:T(8,128)(2,1)S(1)}, u32[]{:S(2)}, u32[]{:S(2)}) collective-permute-start(bf16[256,384]{1,0:T(8,128)(2,1)S(1)} %get-tuple-element.32), channel_id=1, source_target_pairs={{0,4},{4,8},{8,12},{12,0},{1,5},{5,9},{9,13},{13,1},{2,6},{6,10},{... | collective-permute-start | bytes 589832 | tf_op jit(solution)/shard_map/ppermute | solution.py:515
  16.6 13.3 %collective-permute-start.7 = (f32[1024,128]{1,0:T(8,128)S(1)}, f32[1024,128]{1,0:T(8,128)S(1)}, u32[]{:S(2)}, u32[]{:S(2)}) collective-permute-start(f32[1024,128]{1,0:T(8,128)S(1)} %shard_map.59.refs_5_.mine), channel_id=1, source_target_pairs={{0,1},{1,0},{2,3},{3,2},{4,5},{5,4},{6,7},{7,6},{8,9},{9,8},{10,11... | collective-permute-start | bytes 1572872 | tf_op jit(solution)/shard_map/ppermute | solution.py:515
  16.9 12.8 %copy-start.2 = (f32[2048,32]{0,1:T(8,128)S(1)}, f32[2048,32]{0,1:T(8,128)}, u32[]{:S(2)}) copy-start(f32[2048,32]{0,1:T(8,128)} %param.5) | copy-start | bytes 786436
  29.7 2.0 %collective-permute-start.6 = (f32[1024,128]{1,0:T(8,128)S(1)}, f32[1024,128]{1,0:T(8,128)S(1)}, u32[]{:S(2)}, u32[]{:S(2)}) collective-permute-start(f32[1024,128]{1,0:T(8,128)S(1)} %shard_map.62.mine), channel_id=1, source_target_pairs={{0,1},{1,0},{2,3},{3,2},{4,5},{5,4},{6,7},{7,6},{8,9},{9,8},{10,11... | collective-permute-start | bytes 1572872 | tf_op jit(solution)/shard_map/ppermute | solution.py:515
  32.6 9.6 %collective-permute-start.10 = (f32[64,128]{1,0:T(8,128)S(1)}, f32[64,128]{1,0:T(8,128)S(1)}, u32[]{:S(2)}, u32[]{:S(2)}) collective-permute-start(f32[64,128]{1,0:T(8,128)S(1)} %get-tuple-element.37), channel_id=1, source_target_pairs={{0,12},{4,0},{8,4},{12,8},{1,13},{5,1},{9,5},{13,9},{2,14},{6,2},{... | collective-permute-start | bytes 98312 | tf_op jit(solution)/shard_map/ppermute | solution.py:515
  35.2 7.9 %collective-permute-start.8 = (f32[64,128]{1,0:T(8,128)S(1)}, f32[64,128]{1,0:T(8,128)S(1)}, u32[]{:S(2)}, u32[]{:S(2)}) collective-permute-start(f32[64,128]{1,0:T(8,128)S(1)} %get-tuple-element.37), channel_id=1, source_target_pairs={{0,4},{4,8},{8,12},{12,0},{1,5},{5,9},{9,13},{13,1},{2,6},{6,10},{... | collective-permute-start | bytes 98312 | tf_op jit(solution)/shard_map/ppermute | solution.py:515
  37.2 5.9 %collective-permute-start.9 = (f32[64,128]{1,0:T(8,128)S(1)}, f32[64,128]{1,0:T(8,128)S(1)}, u32[]{:S(2)}, u32[]{:S(2)}) collective-permute-start(f32[64,128]{1,0:T(8,128)S(1)} %get-tuple-element.37), channel_id=1, source_target_pairs={{0,8},{4,12},{8,0},{12,4},{1,9},{5,13},{9,1},{13,5},{2,10},{6,14},... | collective-permute-start | bytes 98312 | tf_op jit(solution)/shard_map/ppermute | solution.py:515
  39.0 8.1 %collective-permute-start.12 = (s16[272,128]{1,0:T(8,128)(2,1)S(1)}, s16[272,128]{1,0:T(8,128)(2,1)S(1)}, u32[]{:S(2)}, u32[]{:S(2)}) collective-permute-start(s16[272,128]{1,0:T(8,128)(2,1)S(1)} %get-tuple-element.43), channel_id=1, source_target_pairs={{0,4},{4,8},{8,12},{12,0},{1,5},{5,9},{9,13},{13,1},{2,6},{6,10},{... | collective-permute-start | bytes 208904 | tf_op jit(solution)/shard_map/ppermute | solution.py:515
  39.6 8.1 %collective-permute-start.13 = (s16[272,128]{1,0:T(8,128)(2,1)S(1)}, s16[272,128]{1,0:T(8,128)(2,1)S(1)}, u32[]{:S(2)}, u32[]{:S(2)}) collective-permute-start(s16[272,128]{1,0:T(8,128)(2,1)S(1)} %get-tuple-element.44), channel_id=1, source_target_pairs={{0,8},{4,12},{8,0},{12,4},{1,9},{5,13},{9,1},{13,5},{2,10},{6,14},... | collective-permute-start | bytes 208904 | tf_op jit(solution)/shard_map/ppermute | solution.py:515
  42.1 5.6 %collective-permute-start.14 = (s16[272,128]{1,0:T(8,128)(2,1)S(1)}, s16[272,128]{1,0:T(8,128)(2,1)S(1)}, u32[]{:S(2)}, u32[]{:S(2)}) collective-permute-start(s16[272,128]{1,0:T(8,128)(2,1)S(1)} %get-tuple-element.45), channel_id=1, source_target_pairs={{0,12},{4,0},{8,4},{12,8},{1,13},{5,1},{9,5},{13,9},{2,14},{6,2},{... | collective-permute-start | bytes 208904 | tf_op jit(solution)/shard_map/ppermute | solution.py:515
  43.1 4.0 %collective-permute-start.11 = (f32[64,128]{1,0:T(8,128)S(1)}, f32[64,128]{1,0:T(8,128)S(1)}, u32[]{:S(2)}, u32[]{:S(2)}) collective-permute-start(f32[64,128]{1,0:T(8,128)S(1)} %add_add_fusion.mine), channel_id=1, source_target_pairs={{0,2},{2,0},{1,3},{3,1},{4,6},{6,4},{5,7},{7,5},{8,10},{10,8},{9,1... | collective-permute-start | bytes 98312 | tf_op jit(solution)/shard_map/ppermute | solution.py:523
  47.8 1.5 %collective-permute-start.15 = (bf16[1,256,128]{2,1,0:T(8,128)(2,1)S(1)}, bf16[1,256,128]{2,1,0:T(8,128)(2,1)S(1)}, u32[]{:S(2)}, u32[]{:S(2)}) collective-permute-start(bf16[1,256,128]{2,1,0:T(8,128)(2,1)S(1)} %get-tuple-element.46.refs_0_), channel_id=1, source_target_pairs={{0,1},{1,0},{2,3},{3,2},{4,5},{5,4},{6,7},{7,6},{8,9},{9,8},{10,11... | collective-permute-start | bytes 196616 | tf_op jit(solution)/shard_map/ppermute | solution.py:515
  47.9 1.5 %collective-permute-start.16 = (bf16[1,256,128]{2,1,0:T(8,128)(2,1)S(1)}, bf16[1,256,128]{2,1,0:T(8,128)(2,1)S(1)}, u32[]{:S(2)}, u32[]{:S(2)}) collective-permute-start(bf16[1,256,128]{2,1,0:T(8,128)(2,1)S(1)} %get-tuple-element.47.refs_1_), channel_id=1, source_target_pairs={{0,1},{1,0},{2,3},{3,2},{4,5},{5,4},{6,7},{7,6},{8,9},{9,8},{10,11... | collective-permute-start | bytes 196616 | tf_op jit(solution)/shard_map/ppermute | solution.py:515
  48.3 1.3 %collective-permute-start.17 = (bf16[1,256,128]{2,1,0:T(8,128)(2,1)S(1)}, bf16[1,256,128]{2,1,0:T(8,128)(2,1)S(1)}, u32[]{:S(2)}, u32[]{:S(2)}) collective-permute-start(bf16[1,256,128]{2,1,0:T(8,128)(2,1)S(1)} %get-tuple-element.48.refs_2_), channel_id=1, source_target_pairs={{0,1},{1,0},{2,3},{3,2},{4,5},{5,4},{6,7},{7,6},{8,9},{9,8},{10,11... | collective-permute-start | bytes 196616 | tf_op jit(solution)/shard_map/ppermute | solution.py:515
  50.6 5.8 %collective-permute-start.18 = (s16[32,2176]{1,0:T(8,128)(2,1)S(1)}, s16[32,2176]{1,0:T(8,128)(2,1)S(1)}, u32[]{:S(2)}, u32[]{:S(2)}) collective-permute-start(s16[32,2176]{1,0:T(8,128)(2,1)S(1)} %shard_map.68.mine), channel_id=1, source_target_pairs={{0,2},{2,0},{1,3},{3,1},{4,6},{6,4},{5,7},{7,5},{8,10},{10,8},{9,1... | collective-permute-start | bytes 417800 | tf_op jit(solution)/shard_map/ppermute | solution.py:523
  57.3 4.3 %collective-permute-start.19 = (f32[32,2048]{1,0:T(8,128)S(1)}, f32[32,2048]{1,0:T(8,128)S(1)}, u32[]{:S(2)}, u32[]{:S(2)}) collective-permute-start(f32[32,2048]{1,0:T(8,128)S(1)} %get-tuple-element.49.own), channel_id=1, source_target_pairs={{0,1},{1,0},{2,3},{3,2},{4,5},{5,4},{6,7},{7,6},{8,9},{9,8},{10,11... | collective-permute-start | bytes 786440 | tf_op jit(solution)/shard_map/ppermute | solution.py:515
  57.4 6.3 %collective-permute-start.20 = (s16[144,128]{1,0:T(8,128)(2,1)S(1)}, s16[144,128]{1,0:T(8,128)(2,1)S(1)}, u32[]{:S(2)}, u32[]{:S(2)}) collective-permute-start(s16[144,128]{1,0:T(8,128)(2,1)S(1)} %get-tuple-element.50), channel_id=1, source_target_pairs={{0,4},{4,8},{8,12},{12,0},{1,5},{5,9},{9,13},{13,1},{2,6},{6,10},{... | collective-permute-start | bytes 110600 | tf_op jit(solution)/shard_map/ppermute | solution.py:515
  59.0 5.7 %collective-permute-start.21 = (s16[144,128]{1,0:T(8,128)(2,1)S(1)}, s16[144,128]{1,0:T(8,128)(2,1)S(1)}, u32[]{:S(2)}, u32[]{:S(2)}) collective-permute-start(s16[144,128]{1,0:T(8,128)(2,1)S(1)} %get-tuple-element.51), channel_id=1, source_target_pairs={{0,8},{4,12},{8,0},{12,4},{1,9},{5,13},{9,1},{13,5},{2,10},{6,14},... | collective-permute-start | bytes 110600 | tf_op jit(solution)/shard_map/ppermute | solution.py:515
  60.7 4.5 %collective-permute-start.22 = (s16[144,128]{1,0:T(8,128)(2,1)S(1)}, s16[144,128]{1,0:T(8,128)(2,1)S(1)}, u32[]{:S(2)}, u32[]{:S(2)}) collective-permute-start(s16[144,128]{1,0:T(8,128)(2,1)S(1)} %get-tuple-element.52), channel_id=1, source_target_pairs={{0,12},{4,0},{8,4},{12,8},{1,13},{5,1},{9,5},{13,9},{2,14},{6,2},{... | collective-permute-start | bytes 110600 | tf_op jit(solution)/shard_map/ppermute | solution.py:515
  62.5 3.8 %collective-permute-start.23 = (f32[32,128]{1,0:T(8,128)S(1)}, f32[32,128]{1,0:T(8,128)S(1)}, u32[]{:S(2)}, u32[]{:S(2)}) collective-permute-start(f32[32,128]{1,0:T(8,128)S(1)} %shard_map.70.after), channel_id=1, source_target_pairs={{0,4},{4,0},{8,12},{12,8},{1,5},{5,1},{9,13},{13,9},{2,6},{6,2},{1... | collective-permute-start | bytes 49160 | tf_op jit(solution)/shard_map/ppermute | solution.py:523
  66.4 6.2 %collective-permute-start.24 = (s16[32,2176]{1,0:T(8,128)(2,1)S(1)}, s16[32,2176]{1,0:T(8,128)(2,1)S(1)}, u32[]{:S(2)}, u32[]{:S(2)}) collective-permute-start(s16[32,2176]{1,0:T(8,128)(2,1)S(1)} %shard_map.72.mine), channel_id=1, source_target_pairs={{0,2},{2,0},{1,3},{3,1},{4,6},{6,4},{5,7},{7,5},{8,10},{10,8},{9,1... | collective-permute-start | bytes 417800 | tf_op jit(solution)/shard_map/ppermute | solution.py:523
  68.0 4.6 %collective-permute-start.25 = (f32[32,128]{1,0:T(8,128)S(1)}, f32[32,128]{1,0:T(8,128)S(1)}, u32[]{:S(2)}, u32[]{:S(2)}) collective-permute-start(f32[32,128]{1,0:T(8,128)S(1)} %add.20.after.refs_0_), channel_id=1, source_target_pairs={{0,8},{4,12},{8,0},{12,4},{1,9},{5,13},{9,1},{13,5},{2,10},{6,14},... | collective-permute-start | bytes 49160 | tf_op jit(solution)/shard_map/ppermute | solution.py:523
  73.3 1.8 %collective-permute-start.26 = (f32[32,2048]{1,0:T(8,128)S(1)}, f32[32,2048]{1,0:T(8,128)S(1)}, u32[]{:S(2)}, u32[]{:S(2)}) collective-permute-start(f32[32,2048]{1,0:T(8,128)S(1)} %shard_map.73.after.own), channel_id=1, source_target_pairs={{0,1},{1,0},{2,3},{3,2},{4,5},{5,4},{6,7},{7,6},{8,9},{9,8},{10,11... | collective-permute-start | bytes 786440 | tf_op jit(solution)/shard_map/ppermute | solution.py:515
  76.5 5.6 %collective-permute-start.27 = (f32[32,128]{1,0:T(8,128)S(1)}, f32[32,128]{1,0:T(8,128)S(1)}, u32[]{:S(2)}, u32[]{:S(2)}) collective-permute-start(f32[32,128]{1,0:T(8,128)S(1)} %get-tuple-element.54.refs_0_), channel_id=1, source_target_pairs={{0,4},{4,8},{8,12},{12,0},{1,5},{5,9},{9,13},{13,1},{2,6},{6,10},{... | collective-permute-start | bytes 49160 | tf_op jit(solution)/shard_map/ppermute | solution.py:515
  77.6 4.7 %collective-permute-start.28 = (f32[32,128]{1,0:T(8,128)S(1)}, f32[32,128]{1,0:T(8,128)S(1)}, u32[]{:S(2)}, u32[]{:S(2)}) collective-permute-start(f32[32,128]{1,0:T(8,128)S(1)} %get-tuple-element.54.refs_0_), channel_id=1, source_target_pairs={{0,8},{4,12},{8,0},{12,4},{1,9},{5,13},{9,1},{13,5},{2,10},{6,14},... | collective-permute-start | bytes 49160 | tf_op jit(solution)/shard_map/ppermute | solution.py:515
  79.1 3.7 %collective-permute-start.29 = (f32[32,128]{1,0:T(8,128)S(1)}, f32[32,128]{1,0:T(8,128)S(1)}, u32[]{:S(2)}, u32[]{:S(2)}) collective-permute-start(f32[32,128]{1,0:T(8,128)S(1)} %get-tuple-element.54.refs_0_), channel_id=1, source_target_pairs={{0,12},{4,0},{8,4},{12,8},{1,13},{5,1},{9,5},{13,9},{2,14},{6,2},{... | collective-permute-start | bytes 49160 | tf_op jit(solution)/shard_map/ppermute | solution.py:515
  (1 other events, 1.4 us)

commit v16 on v15

--- a/solution.py
+++ b/solution.py
@@ -22,7 +22,20 @@
 NT = (((1,), (1,)), ((), ()))
 
 
-def call(body, outs, args, smem_in=(), smem_out=(), any_in=(), scratch=()):
+ME = None
+
+
+def with_position(body):
+    def inner(*refs):
+        body([lax.axis_index(name) for name in ("rows", "tiles", "cols")], *refs)
+
+    return inner
+
+
+def call(body, outs, args, smem_in=(), smem_out=(), any_in=(), scratch=(), any_out=()):
+    if args[0] is ME:
+        body, args = with_position(body), args[1:]
+        smem_in, any_in = [[i - 1 for i in places] for places in (smem_in, any_in)]
     single = not isinstance(outs, (list, tuple))
     shapes = [outs] if single else list(outs)
     result = pl.pallas_call(
@@ -31,7 +44,9 @@
         in_specs=[
             SMEM if i in smem_in else ANY if i in any_in else VMEM for i in range(len(args))
         ],
-        out_specs=[SMEM if i in smem_out else VMEM for i in range(len(shapes))],
+        out_specs=[
+            SMEM if i in smem_out else ANY if i in any_out else VMEM for i in range(len(shapes))
+        ],
         scratch_shapes=list(scratch),
         compiler_params=pltpu.CompilerParams(vmem_limit_bytes=48 * 2**20),
     )(*args)
@@ -185,9 +200,10 @@
     return lax.rem(value, jnp.int32(size))
 
 
-def plan_body(dims, me, *refs):
+def plan_body(dims, list_order, me, *refs):
     row_count, capacity, slots, blocks_here = dims
     lists, (emb, after, idx) = refs[:row_count], refs[row_count : row_count + 3]
+    lists = dict(zip(list_order, lists))
     sends = refs[row_count + 3 :]
     row = me[0]
     for i in range(slots):
@@ -504,11 +520,19 @@
 
 
 def final_body(me, mapped, *refs):
-    out = refs[-1]
-    factor = lower_inverse(unfolded(refs[:-1]))
-    own_cols = out.shape[0]
+    terms, (out, value, sent) = refs[:-3], refs[-3:]
+    factor = lower_inverse(unfolded(terms))
+    own_cols = value.shape[0]
     part = jnp.where(me[2] == 0, factor[:own_cols], factor[own_cols:])
-    out[...] = times(part, mapped[...])
+    copies = []
+    chunk = value.shape[1] // sent.shape[0]
+    for i in range(sent.shape[0]):
+        at = slice(i * chunk, (i + 1) * chunk)
+        value[:, at] = times(part, mapped[:, at])
+        copies.append(pltpu.make_async_copy(value.at[:, at], out.at[:, at], sent.at[i]))
+        copies[-1].start()
+    for copy in copies:
+        copy.wait()
 
 
 def shift_by(value, axes, size, shift):
@@ -540,7 +564,6 @@
     row_index = lax.axis_index("rows")
     tile_index = lax.axis_index("tiles")
     col_index = lax.axis_index("cols")
-    me = jnp.stack([row_index, tile_index, col_index]).astype(jnp.int32)
     rows_here, half_features = embeddings.shape
     blocks_here = rows_here // BLOCK
     slots = pair_list.shape[2]
@@ -555,16 +578,17 @@
         [pair_list[0], jnp.broadcast_to(pair_count[:, None], (1, slots))], axis=0
     )
     lists = row_terms(own_list, row_count)
+    list_order = [0, *sorted(others, key=lambda k: k * (row_count - k))]
     self_part = call(
         functools.partial(self_distance_body, own_blocks, tile_count),
         sds((own_blocks * BLOCK, BLOCK), F32),
-        [me, embeddings],
+        [ME, embeddings],
         smem_in=(0,),
     )
     planned = call(
-        functools.partial(plan_body, (row_count, capacity, slots, blocks_here)),
+        functools.partial(plan_body, (row_count, capacity, slots, blocks_here), list_order),
         [sds((6, slots + 1), jnp.int32)] + [sds((capacity * BLOCK, half_features), BF16) for _ in others],
-        [me, *lists, embeddings, self_part],
+        [ME, *[lists[k] for k in list_order], embeddings, self_part],
         smem_in=range(1 + row_count),
         any_in=(row_count + 2,),
         smem_out=(0,),
@@ -600,7 +624,7 @@
         functools.partial(pair_tile_body, dims),
         [sds((slots, 2 * BLOCK, BLOCK), BF16), sds((capacity, 2 * BLOCK, BLOCK), BF16), table]
         + [sds((per_core * BLOCK + picked + CODE_ROWS, BLOCK), jnp.int16) for _ in others],
-        [me, idx, pair_part, pair_other, self_sums, *start_codes],
+        [ME, idx, pair_part, pair_other, self_sums, *start_codes],
         smem_in=(0, 1),
     )
     near_tiles, home_tiles, degrees, sends = tiles[0], tiles[1], tiles[2], tiles[3:]
@@ -623,13 +647,13 @@
     started, degree, inverse = call(
         functools.partial(first_own_body, dims),
         [block_shape, table, table],
-        [me, idx, *degree_terms, values, near_tiles, home_tiles, self_tiles],
+        [ME, idx, *degree_terms, values, near_tiles, home_tiles, self_tiles],
         smem_in=(0, 1),
     )
     part = call(
         functools.partial(first_far_body, dims, coded),
         sum_shape,
-        [me, idx, inverse, started, near_tiles, *sent, *shared, *messages],
+        [ME, idx, inverse, started, near_tiles, *sent, *shared, *messages],
         smem_in=(0, 1),
         scratch=[pltpu.VMEM((own_cols, rows_here), F32)],
     )
@@ -637,7 +661,7 @@
     first = call(
         functools.partial(mapped_body, dims, coded),
         [block_shape] + [sds((picked + CODE_ROWS, BLOCK), jnp.int16) for _ in others],
-        [me, idx, inverse, mine, other],
+        [ME, idx, inverse, mine, other],
         smem_in=(0, 1),
         scratch=code_scratch,
     )
@@ -645,11 +669,11 @@
     received = [shift_by(sends[k - 1], "rows", row_count, k) for k in others]
 
     mapped_other = shift_by(mapped, "cols", core_count, 1)
-    first_gram = call(gram_body, folded_square, [me, mapped, mapped_other], smem_in=(0,))
+    first_gram = call(gram_body, folded_square, [ME, mapped, mapped_other], smem_in=(0,))
     part = call(
         functools.partial(second_apply_body, dims),
         block_shape,
-        [me, idx, inverse, first_gram, mapped, home_tiles, self_tiles, near_tiles, *sent, *shared, *received],
+        [ME, idx, inverse, first_gram, mapped, home_tiles, self_tiles, near_tiles, *sent, *shared, *received],
         smem_in=(0, 1),
         any_in=(3,),
     )
@@ -662,7 +686,7 @@
     second = call(
         functools.partial(last_mapped_body, blocks_here, coded),
         block_shape,
-        [me, inverse, mine, other, gram_terms[1]],
+        [ME, inverse, mine, other, gram_terms[1]],
         smem_in=(0,),
         any_in=(4,),
     )
@@ -671,11 +695,15 @@
     full, second_gram = call(
         second_gram_body,
         [sds((4 * own_cols, rows_here), BF16), folded_square],
-        [me, factor, second, second_other],
+        [ME, factor, second, second_other],
         smem_in=(0,),
     )
     vectors = call(
-        final_body, block_shape, [me, full, *row_terms(second_gram, row_count)], smem_in=(0,)
+        final_body,
+        block_shape,
+        [ME, full, *row_terms(second_gram, row_count)],
+        any_out=(0,),
+        scratch=[pltpu.VMEM((own_cols, rows_here), F32), pltpu.SemaphoreType.DMA((4,))],
     )
     own_degree = lax.dynamic_slice_in_dim(degree, row_index * blocks_here, blocks_here, 0)
     return (vectors.T, own_degree.reshape(rows_here))

time: 86.2 us -> 84.5 us (0.980)
  waiting for transfers between devices: 26.4 us -> 29.7 us
  Pallas kernels: 17.2 us -> 14.4 us
  starting transfers between devices: 38.2 us -> 36 us
    ppermute x25, waiting for transfers between devices: 16.7 us -> 19.6 us  [shift_by(): lax.ppermute(value, axes, [(i, (i + shift) % size) for i in range(size)])]
    pallas_call x18, Pallas kernels: 17.2 us -> 14.4 us  [call(): pl.pallas_call(body, out_shape=shapes, in_specs=[SMEM if i in smem_in els...]
    ppermute x25, starting transfers between devices: 30.7 us -> 29.2 us  [shift_by(): lax.ppermute(value, axes, [(i, (i + shift) % size) for i in range(size)])]
  transfers between devices with their start and end apart: 30 -> 30, of which waited for: 13 -> 13; matrix products, arithmetic and copies ran while one was open for 1% -> 1% of each run, Pallas kernels for 9% -> 7%
where the time goes in v16:
time: 84.5 us; the launch traced here: 84.3 us
  starting transfers between devices  36 us (43%)
  waiting for transfers between devices  29.7 us (35%)
  Pallas kernels  14.4 us (17%)
  local copies, waits for them, and re-layouts  2.7 us (3%)
  between operations  1.48 us (2%)
    ppermute x25, starting transfers between devices, shift_by(): lax.ppermute(value, axes, [(i, (i + shift) % size) for i in range(size)])  29.2 us
    ppermute x25, waiting for transfers between devices, shift_by(): lax.ppermute(value, axes, [(i, (i + shift) % size) for i in range(size)])  19.6 us
    pallas_call x18, Pallas kernels, call(): pl.pallas_call(body, out_shape=shapes, in_specs=[SMEM if i in smem_in els...  14.4 us
    ppermute x5, waiting for transfers between devices, pair_step(): lax.ppermute(value, name, [(i, i ^ flip) for i in range(lax.axis_size(nam...  10.1 us
    ppermute x5, starting transfers between devices, pair_step(): lax.ppermute(value, name, [(i, i ^ flip) for i in range(lax.axis_size(nam...  6.8 us
  transfers between devices with their start and end apart: 30, of which 13 were waited for; matrix products, arithmetic and copies ran while one was open for 1% of the time, Pallas kernels for 7%

profile of v16, /device:TPU:0, one launch (start us, length us, event | category | flops | bytes accessed | tf_op | source)
XLA Modules:
  0.0 84.3 jit_solution(11291067347324247341)
XLA Ops:
  2.0 3.0 %collective-permute-start = (s32[3,8]{1,0:T(4,128)S(1)}, s32[3,8]{1,0:T(4,128)S(1)}, u32[]{:S(2)}, u32[]{:S(2)}) collective-permute-start(s32[3,8]{1,0:T(4,128)S(1)} %concatenate.3.refs_0_), channel_id=1, source_target_pairs={{0,4},{4,8},{8,12},{12,0},{1,5},{5,9},{9,13},{13,1},{2,6},{6,10},{... | collective-permute-start | bytes 296 | tf_op jit(solution)/shard_map/ppermute | solution.py:539
  5.0 2.0 %collective-permute-start.1 = (s32[3,8]{1,0:T(4,128)S(1)}, s32[3,8]{1,0:T(4,128)S(1)}, u32[]{:S(2)}, u32[]{:S(2)}) collective-permute-start(s32[3,8]{1,0:T(4,128)S(1)} %concatenate.3.refs_0_), channel_id=1, source_target_pairs={{0,12},{4,0},{8,4},{12,8},{1,13},{5,1},{9,5},{13,9},{2,14},{6,2},{... | collective-permute-start | bytes 296 | tf_op jit(solution)/shard_map/ppermute | solution.py:539
  8.0 1.4 %copy-done = bf16[2048,384]{1,0:T(8,128)(2,1)S(1)} copy-done((bf16[2048,384]{1,0:T(8,128)(2,1)S(1)}, bf16[2048,384]{1,0:T(8,128)(2,1)}, u32[]{:S(2)}) %copy-start) | copy-done | bytes 1572888
  9.9 1.6 %collective-permute-done.2.refs_3_ = s32[3,8]{1,0:T(4,128)S(1)} collective-permute-done((s32[3,8]{1,0:T(4,128)S(1)}, s32[3,8]{1,0:T(4,128)S(1)}, u32[]{:S(2)}, u32[]{:S(2)}) %collective-permute-start.2) | collective-permute-done | bytes 128 | tf_op jit(solution)/shard_map/ppermute | solution.py:539
  11.5 1.6 %shard_map.60 = (s32[6,9]{1,0:T(8,128)S(1)}, bf16[256,384]{1,0:T(8,128)(2,1)S(1)}, bf16[256,384]{1,0:T(8,128)(2,1)S(1)}, bf16[256,384]{1,0:T(8,128)(2,1)S(1)}) custom-call(s32[3,8]{1,0:T(4,128)S(1)} %concatenate.3.refs_0_, s32[3,8]{1,0:T(4,128)S(1)} %collective-permute-done.refs_1_, s32[3,8]{1,0:T(4,128)S(1)} %collective-permute-done.1.refs_2_, ...), custom_call_target="tpu_custom_call" | custom-call | tf_op jit(solution)/shard_map/pallas_call | solution.py:41
  13.1 1.1 %collective-permute-start.3 = (bf16[256,384]{1,0:T(8,128)(2,1)S(1)}, bf16[256,384]{1,0:T(8,128)(2,1)S(1)}, u32[]{:S(2)}, u32[]{:S(2)}) collective-permute-start(bf16[256,384]{1,0:T(8,128)(2,1)S(1)} %get-tuple-element.30), channel_id=1, source_target_pairs={{0,8},{4,12},{8,0},{12,4},{1,9},{5,13},{9,1},{13,5},{2,10},{6,14},... | collective-permute-start | bytes 589832 | tf_op jit(solution)/shard_map/ppermute | solution.py:539
  14.2 1.4 %collective-permute-start.4 = (bf16[256,384]{1,0:T(8,128)(2,1)S(1)}, bf16[256,384]{1,0:T(8,128)(2,1)S(1)}, u32[]{:S(2)}, u32[]{:S(2)}) collective-permute-start(bf16[256,384]{1,0:T(8,128)(2,1)S(1)} %get-tuple-element.31), channel_id=1, source_target_pairs={{0,12},{4,0},{8,4},{12,8},{1,13},{5,1},{9,5},{13,9},{2,14},{6,2},{... | collective-permute-start | bytes 589832 | tf_op jit(solution)/shard_map/ppermute | solution.py:539
  16.6 11.4 %collective-permute-done.3.refs_0_ = bf16[256,384]{1,0:T(8,128)(2,1)S(1)} collective-permute-done((bf16[256,384]{1,0:T(8,128)(2,1)S(1)}, bf16[256,384]{1,0:T(8,128)(2,1)S(1)}, u32[]{:S(2)}, u32[]{:S(2)}) %collective-permute-start.3) | collective-permute-done | bytes 196640 | tf_op jit(solution)/shard_map/ppermute | solution.py:539
  28.0 1.1 %shard_map.62.refs_1_ = f32[1024,128]{1,0:T(8,128)S(1)} custom-call(s32[6,9]{1,0:T(8,128)S(1)} %get-tuple-element.29.after.idx.refs_0_, bf16[2048,384]{1,0:T(8,128)(2,1)S(1)} %copy-done, f32[2048,128]{1,0:T(8,128)S(1)} %shard_map.61.own_squares, bf16[256,384]{1,0:T(8,128)(2,1)S(1)} %collective-permute-done.3.refs_0_, ...), custom_call_target="tpu_custom_call" | custom-call | tf_op jit(solution)/shard_map/pallas_call | solution.py:41
  29.6 1.5 %collective-permute-done.6.refs_2_ = f32[1024,128]{1,0:T(8,128)S(1)} collective-permute-done((f32[1024,128]{1,0:T(8,128)S(1)}, f32[1024,128]{1,0:T(8,128)S(1)}, u32[]{:S(2)}, u32[]{:S(2)}) %collective-permute-start.6) | collective-permute-done | bytes 524320 | tf_op jit(solution)/shard_map/ppermute | solution.py:539
  32.0 2.2 %collective-permute-start.10 = (f32[64,128]{1,0:T(8,128)S(1)}, f32[64,128]{1,0:T(8,128)S(1)}, u32[]{:S(2)}, u32[]{:S(2)}) collective-permute-start(f32[64,128]{1,0:T(8,128)S(1)} %get-tuple-element.37), channel_id=1, source_target_pairs={{0,12},{4,0},{8,4},{12,8},{1,13},{5,1},{9,5},{13,9},{2,14},{6,2},{... | collective-permute-start | bytes 98312 | tf_op jit(solution)/shard_map/ppermute | solution.py:539
  34.3 2.4 %collective-permute-start.8 = (f32[64,128]{1,0:T(8,128)S(1)}, f32[64,128]{1,0:T(8,128)S(1)}, u32[]{:S(2)}, u32[]{:S(2)}) collective-permute-start(f32[64,128]{1,0:T(8,128)S(1)} %get-tuple-element.37), channel_id=1, source_target_pairs={{0,4},{4,8},{8,12},{12,0},{1,5},{5,9},{9,13},{13,1},{2,6},{6,10},{... | collective-permute-start | bytes 98312 | tf_op jit(solution)/shard_map/ppermute | solution.py:539
  36.7 2.2 %collective-permute-start.9 = (f32[64,128]{1,0:T(8,128)S(1)}, f32[64,128]{1,0:T(8,128)S(1)}, u32[]{:S(2)}, u32[]{:S(2)}) collective-permute-start(f32[64,128]{1,0:T(8,128)S(1)} %get-tuple-element.37), channel_id=1, source_target_pairs={{0,8},{4,12},{8,0},{12,4},{1,9},{5,13},{9,1},{13,5},{2,10},{6,14},... | collective-permute-start | bytes 98312 | tf_op jit(solution)/shard_map/ppermute | solution.py:539
  38.9 2.7 %collective-permute-start.13 = (s16[272,128]{1,0:T(8,128)(2,1)S(1)}, s16[272,128]{1,0:T(8,128)(2,1)S(1)}, u32[]{:S(2)}, u32[]{:S(2)}) collective-permute-start(s16[272,128]{1,0:T(8,128)(2,1)S(1)} %get-tuple-element.44), channel_id=1, source_target_pairs={{0,8},{4,12},{8,0},{12,4},{1,9},{5,13},{9,1},{13,5},{2,10},{6,14},... | collective-permute-start | bytes 208904 | tf_op jit(solution)/shard_map/ppermute | solution.py:539
  41.6 1.1 %collective-permute-start.14 = (s16[272,128]{1,0:T(8,128)(2,1)S(1)}, s16[272,128]{1,0:T(8,128)(2,1)S(1)}, u32[]{:S(2)}, u32[]{:S(2)}) collective-permute-start(s16[272,128]{1,0:T(8,128)(2,1)S(1)} %get-tuple-element.45), channel_id=1, source_target_pairs={{0,12},{4,0},{8,4},{12,8},{1,13},{5,1},{9,5},{13,9},{2,14},{6,2},{... | collective-permute-start | bytes 208904 | tf_op jit(solution)/shard_map/ppermute | solution.py:539
  42.7 1.6 %collective-permute-start.11 = (f32[64,128]{1,0:T(8,128)S(1)}, f32[64,128]{1,0:T(8,128)S(1)}, u32[]{:S(2)}, u32[]{:S(2)}) collective-permute-start(f32[64,128]{1,0:T(8,128)S(1)} %add_add_fusion.refs_1_), channel_id=1, source_target_pairs={{0,2},{2,0},{1,3},{3,1},{4,6},{6,4},{5,7},{7,5},{8,10},{10,8},{9,1... | collective-permute-start | bytes 98312 | tf_op jit(solution)/shard_map/ppermute | solution.py:547
  44.3 2.4 %collective-permute-done.11.refs_2_.refs_3_ = f32[64,128]{1,0:T(8,128)S(1)} collective-permute-done((f32[64,128]{1,0:T(8,128)S(1)}, f32[64,128]{1,0:T(8,128)S(1)}, u32[]{:S(2)}, u32[]{:S(2)}) %collective-permute-start.11) | collective-permute-done | bytes 32800 | tf_op jit(solution)/shard_map/ppermute | solution.py:547
  49.3 1.0 %shard_map.68.refs_2_ = s16[32,2176]{1,0:T(8,128)(2,1)S(1)} custom-call(s32[6,9]{1,0:T(8,128)S(1)} %get-tuple-element.29.after.idx.refs_0_, f32[64,128]{1,0:T(8,128)S(1)} %get-tuple-element.41.refs_1_.refs_0_, f32[32,2048]{1,0:T(8,128)S(1)} %get-tuple-element.42.refs_2_, bf16[8,256,128]{2,1,0:T(8,128)(2,1)S(1)} %get-tuple-element.38.refs_4_.refs_3_.refs_6_, ...), custom_call_target="tpu_custom_call" | custom-call | tf_op jit(solution)/shard_map/pallas_call | solution.py:41
  50.3 1.6 %collective-permute-start.18 = (s16[32,2176]{1,0:T(8,128)(2,1)S(1)}, s16[32,2176]{1,0:T(8,128)(2,1)S(1)}, u32[]{:S(2)}, u32[]{:S(2)}) collective-permute-start(s16[32,2176]{1,0:T(8,128)(2,1)S(1)} %shard_map.68.refs_2_), channel_id=1, source_target_pairs={{0,2},{2,0},{1,3},{3,1},{4,6},{6,4},{5,7},{7,5},{8,10},{10,8},{9,1... | collective-permute-start | bytes 417800 | tf_op jit(solution)/shard_map/ppermute | solution.py:547
  51.8 4.3 %collective-permute-done.18.refs_3_ = s16[32,2176]{1,0:T(8,128)(2,1)S(1)} collective-permute-done((s16[32,2176]{1,0:T(8,128)(2,1)S(1)}, s16[32,2176]{1,0:T(8,128)(2,1)S(1)}, u32[]{:S(2)}, u32[]{:S(2)}) %collective-permute-start.18) | collective-permute-done | bytes 139296 | tf_op jit(solution)/shard_map/ppermute | solution.py:547
  57.0 1.4 %collective-permute-start.20 = (s16[144,128]{1,0:T(8,128)(2,1)S(1)}, s16[144,128]{1,0:T(8,128)(2,1)S(1)}, u32[]{:S(2)}, u32[]{:S(2)}) collective-permute-start(s16[144,128]{1,0:T(8,128)(2,1)S(1)} %get-tuple-element.50), channel_id=1, source_target_pairs={{0,4},{4,8},{8,12},{12,0},{1,5},{5,9},{9,13},{13,1},{2,6},{6,10},{... | collective-permute-start | bytes 110600 | tf_op jit(solution)/shard_map/ppermute | solution.py:539
  58.4 1.7 %collective-permute-start.21 = (s16[144,128]{1,0:T(8,128)(2,1)S(1)}, s16[144,128]{1,0:T(8,128)(2,1)S(1)}, u32[]{:S(2)}, u32[]{:S(2)}) collective-permute-start(s16[144,128]{1,0:T(8,128)(2,1)S(1)} %get-tuple-element.51), channel_id=1, source_target_pairs={{0,8},{4,12},{8,0},{12,4},{1,9},{5,13},{9,1},{13,5},{2,10},{6,14},... | collective-permute-start | bytes 110600 | tf_op jit(solution)/shard_map/ppermute | solution.py:539
  60.2 1.2 %collective-permute-start.22 = (s16[144,128]{1,0:T(8,128)(2,1)S(1)}, s16[144,128]{1,0:T(8,128)(2,1)S(1)}, u32[]{:S(2)}, u32[]{:S(2)}) collective-permute-start(s16[144,128]{1,0:T(8,128)(2,1)S(1)} %get-tuple-element.52), channel_id=1, source_target_pairs={{0,12},{4,0},{8,4},{12,8},{1,13},{5,1},{9,5},{13,9},{2,14},{6,2},{... | collective-permute-start | bytes 110600 | tf_op jit(solution)/shard_map/ppermute | solution.py:539
  63.2 1.2 %collective-permute-done.21.refs_14_ = s16[144,128]{1,0:T(8,128)(2,1)S(1)} collective-permute-done((s16[144,128]{1,0:T(8,128)(2,1)S(1)}, s16[144,128]{1,0:T(8,128)(2,1)S(1)}, u32[]{:S(2)}, u32[]{:S(2)}) %collective-permute-start.21) | collective-permute-done | bytes 36896 | tf_op jit(solution)/shard_map/ppermute | solution.py:539
  66.0 1.6 %collective-permute-start.24 = (s16[32,2176]{1,0:T(8,128)(2,1)S(1)}, s16[32,2176]{1,0:T(8,128)(2,1)S(1)}, u32[]{:S(2)}, u32[]{:S(2)}) collective-permute-start(s16[32,2176]{1,0:T(8,128)(2,1)S(1)} %shard_map.72.refs_1_), channel_id=1, source_target_pairs={{0,2},{2,0},{1,3},{3,1},{4,6},{6,4},{5,7},{7,5},{8,10},{10,8},{9,1... | collective-permute-start | bytes 417800 | tf_op jit(solution)/shard_map/ppermute | solution.py:547
  67.6 1.3 %collective-permute-start.25 = (f32[32,128]{1,0:T(8,128)S(1)}, f32[32,128]{1,0:T(8,128)S(1)}, u32[]{:S(2)}, u32[]{:S(2)}) collective-permute-start(f32[32,128]{1,0:T(8,128)S(1)} %add.20.after.refs_0_), channel_id=1, source_target_pairs={{0,8},{4,12},{8,0},{12,4},{1,9},{5,13},{9,1},{13,5},{2,10},{6,14},... | collective-permute-start | bytes 49160 | tf_op jit(solution)/shard_map/ppermute | solution.py:547
  68.8 3.4 %collective-permute-done.25.refs_3_.refs_1_ = f32[32,128]{1,0:T(8,128)S(1)} collective-permute-done((f32[32,128]{1,0:T(8,128)S(1)}, f32[32,128]{1,0:T(8,128)S(1)}, u32[]{:S(2)}, u32[]{:S(2)}) %collective-permute-start.25) | collective-permute-done | bytes 16416 | tf_op jit(solution)/shard_map/ppermute | solution.py:547
  72.4 1.7 %shard_map.74.refs_0_ = f32[64,64]{1,0:T(8,128)S(1)} custom-call(f32[32,2048]{1,0:T(8,128)S(1)} %shard_map.73.after.refs_1_, f32[32,128]{1,0:T(8,128)S(1)} %add.20.after.refs_0_, f32[32,128]{1,0:T(8,128)S(1)} %collective-permute-done.25.refs_3_.refs_1_), custom_call_target="tpu_custom_call" | custom-call | tf_op jit(solution)/shard_map/pallas_call | solution.py:41
  75.8 2.2 %collective-permute-start.28 = (f32[32,128]{1,0:T(8,128)S(1)}, f32[32,128]{1,0:T(8,128)S(1)}, u32[]{:S(2)}, u32[]{:S(2)}) collective-permute-start(f32[32,128]{1,0:T(8,128)S(1)} %get-tuple-element.54.refs_1_), channel_id=1, source_target_pairs={{0,8},{4,12},{8,0},{12,4},{1,9},{5,13},{9,1},{13,5},{2,10},{6,14},... | collective-permute-start | bytes 49160 | tf_op jit(solution)/shard_map/ppermute | solution.py:539
  78.0 1.2 %collective-permute-start.29 = (f32[32,128]{1,0:T(8,128)S(1)}, f32[32,128]{1,0:T(8,128)S(1)}, u32[]{:S(2)}, u32[]{:S(2)}) collective-permute-start(f32[32,128]{1,0:T(8,128)S(1)} %get-tuple-element.54.refs_1_), channel_id=1, source_target_pairs={{0,12},{4,0},{8,4},{12,8},{1,13},{5,1},{9,5},{13,9},{2,14},{6,2},{... | collective-permute-start | bytes 49160 | tf_op jit(solution)/shard_map/ppermute | solution.py:539
  80.6 1.1 %collective-permute-done.29.refs_4_ = f32[32,128]{1,0:T(8,128)S(1)} collective-permute-done((f32[32,128]{1,0:T(8,128)S(1)}, f32[32,128]{1,0:T(8,128)S(1)}, u32[]{:S(2)}, u32[]{:S(2)}) %collective-permute-start.29) | collective-permute-done | bytes 16416 | tf_op jit(solution)/shard_map/ppermute | solution.py:539
  81.7 2.6 %shard_map.76 = f32[32,2048]{1,0:T(8,128)} custom-call(bf16[128,2048]{1,0:T(8,128)(2,1)S(1)} %get-tuple-element.53.refs_0_, f32[32,128]{1,0:T(8,128)S(1)} %get-tuple-element.54.refs_1_, f32[32,128]{1,0:T(8,128)S(1)} %collective-permute-done.27.refs_2_, f32[32,128]{1,0:T(8,128)S(1)} %collective-permute-done.28.refs_3_, ...), custom_call_target="tpu_custom_call" | custom-call | tf_op jit(solution)/shard_map/pallas_call | solution.py:41
  (54 shorter events, 14.6 us)
Async XLA Ops:
  2.0 7.9 %collective-permute-start = (s32[3,8]{1,0:T(4,128)S(1)}, s32[3,8]{1,0:T(4,128)S(1)}, u32[]{:S(2)}, u32[]{:S(2)}) collective-permute-start(s32[3,8]{1,0:T(4,128)S(1)} %concatenate.3.refs_0_), channel_id=1, source_target_pairs={{0,4},{4,8},{8,12},{12,0},{1,5},{5,9},{9,13},{13,1},{2,6},{6,10},{... | collective-permute-start | bytes 296 | tf_op jit(solution)/shard_map/ppermute | solution.py:539
  5.0 4.9 %collective-permute-start.1 = (s32[3,8]{1,0:T(4,128)S(1)}, s32[3,8]{1,0:T(4,128)S(1)}, u32[]{:S(2)}, u32[]{:S(2)}) collective-permute-start(s32[3,8]{1,0:T(4,128)S(1)} %concatenate.3.refs_0_), channel_id=1, source_target_pairs={{0,12},{4,0},{8,4},{12,8},{1,13},{5,1},{9,5},{13,9},{2,14},{6,2},{... | collective-permute-start | bytes 296 | tf_op jit(solution)/shard_map/ppermute | solution.py:539
  7.0 4.5 %collective-permute-start.2 = (s32[3,8]{1,0:T(4,128)S(1)}, s32[3,8]{1,0:T(4,128)S(1)}, u32[]{:S(2)}, u32[]{:S(2)}) collective-permute-start(s32[3,8]{1,0:T(4,128)S(1)} %concatenate.3.refs_0_), channel_id=1, source_target_pairs={{0,8},{4,12},{8,0},{12,4},{1,9},{5,13},{9,1},{13,5},{2,10},{6,14},... | collective-permute-start | bytes 296 | tf_op jit(solution)/shard_map/ppermute | solution.py:539
  8.0 1.4 %copy-start = (bf16[2048,384]{1,0:T(8,128)(2,1)S(1)}, bf16[2048,384]{1,0:T(8,128)(2,1)}, u32[]{:S(2)}) copy-start(bf16[2048,384]{1,0:T(8,128)(2,1)} %emb.3) | copy-start | bytes 4718596
  13.1 14.9 %collective-permute-start.3 = (bf16[256,384]{1,0:T(8,128)(2,1)S(1)}, bf16[256,384]{1,0:T(8,128)(2,1)S(1)}, u32[]{:S(2)}, u32[]{:S(2)}) collective-permute-start(bf16[256,384]{1,0:T(8,128)(2,1)S(1)} %get-tuple-element.30), channel_id=1, source_target_pairs={{0,8},{4,12},{8,0},{12,4},{1,9},{5,13},{9,1},{13,5},{2,10},{6,14},... | collective-permute-start | bytes 589832 | tf_op jit(solution)/shard_map/ppermute | solution.py:539
  14.2 13.8 %collective-permute-start.4 = (bf16[256,384]{1,0:T(8,128)(2,1)S(1)}, bf16[256,384]{1,0:T(8,128)(2,1)S(1)}, u32[]{:S(2)}, u32[]{:S(2)}) collective-permute-start(bf16[256,384]{1,0:T(8,128)(2,1)S(1)} %get-tuple-element.31), channel_id=1, source_target_pairs={{0,12},{4,0},{8,4},{12,8},{1,13},{5,1},{9,5},{13,9},{2,14},{6,2},{... | collective-permute-start | bytes 589832 | tf_op jit(solution)/shard_map/ppermute | solution.py:539
  15.6 12.5 %collective-permute-start.5 = (bf16[256,384]{1,0:T(8,128)(2,1)S(1)}, bf16[256,384]{1,0:T(8,128)(2,1)S(1)}, u32[]{:S(2)}, u32[]{:S(2)}) collective-permute-start(bf16[256,384]{1,0:T(8,128)(2,1)S(1)} %get-tuple-element.32), channel_id=1, source_target_pairs={{0,4},{4,8},{8,12},{12,0},{1,5},{5,9},{9,13},{13,1},{2,6},{6,10},{... | collective-permute-start | bytes 589832 | tf_op jit(solution)/shard_map/ppermute | solution.py:539
  16.2 13.1 %collective-permute-start.7 = (f32[1024,128]{1,0:T(8,128)S(1)}, f32[1024,128]{1,0:T(8,128)S(1)}, u32[]{:S(2)}, u32[]{:S(2)}) collective-permute-start(f32[1024,128]{1,0:T(8,128)S(1)} %shard_map.59.refs_5_.mine), channel_id=1, source_target_pairs={{0,1},{1,0},{2,3},{3,2},{4,5},{5,4},{6,7},{7,6},{8,9},{9,8},{10,11... | collective-permute-start | bytes 1572872 | tf_op jit(solution)/shard_map/ppermute | solution.py:539
  16.6 12.6 %copy-start.1 = (f32[2048,32]{0,1:T(8,128)S(1)}, f32[2048,32]{0,1:T(8,128)}, u32[]{:S(2)}) copy-start(f32[2048,32]{0,1:T(8,128)} %param.5) | copy-start | bytes 786436
  29.1 2.0 %collective-permute-start.6 = (f32[1024,128]{1,0:T(8,128)S(1)}, f32[1024,128]{1,0:T(8,128)S(1)}, u32[]{:S(2)}, u32[]{:S(2)}) collective-permute-start(f32[1024,128]{1,0:T(8,128)S(1)} %shard_map.62.refs_1_), channel_id=1, source_target_pairs={{0,1},{1,0},{2,3},{3,2},{4,5},{5,4},{6,7},{7,6},{8,9},{9,8},{10,11... | collective-permute-start | bytes 1572872 | tf_op jit(solution)/shard_map/ppermute | solution.py:539
  32.0 9.5 %collective-permute-start.10 = (f32[64,128]{1,0:T(8,128)S(1)}, f32[64,128]{1,0:T(8,128)S(1)}, u32[]{:S(2)}, u32[]{:S(2)}) collective-permute-start(f32[64,128]{1,0:T(8,128)S(1)} %get-tuple-element.37), channel_id=1, source_target_pairs={{0,12},{4,0},{8,4},{12,8},{1,13},{5,1},{9,5},{13,9},{2,14},{6,2},{... | collective-permute-start | bytes 98312 | tf_op jit(solution)/shard_map/ppermute | solution.py:539
  34.3 8.4 %collective-permute-start.8 = (f32[64,128]{1,0:T(8,128)S(1)}, f32[64,128]{1,0:T(8,128)S(1)}, u32[]{:S(2)}, u32[]{:S(2)}) collective-permute-start(f32[64,128]{1,0:T(8,128)S(1)} %get-tuple-element.37), channel_id=1, source_target_pairs={{0,4},{4,8},{8,12},{12,0},{1,5},{5,9},{9,13},{13,1},{2,6},{6,10},{... | collective-permute-start | bytes 98312 | tf_op jit(solution)/shard_map/ppermute | solution.py:539
  36.7 6.0 %collective-permute-start.9 = (f32[64,128]{1,0:T(8,128)S(1)}, f32[64,128]{1,0:T(8,128)S(1)}, u32[]{:S(2)}, u32[]{:S(2)}) collective-permute-start(f32[64,128]{1,0:T(8,128)S(1)} %get-tuple-element.37), channel_id=1, source_target_pairs={{0,8},{4,12},{8,0},{12,4},{1,9},{5,13},{9,1},{13,5},{2,10},{6,14},... | collective-permute-start | bytes 98312 | tf_op jit(solution)/shard_map/ppermute | solution.py:539
  38.9 7.8 %collective-permute-start.12 = (s16[272,128]{1,0:T(8,128)(2,1)S(1)}, s16[272,128]{1,0:T(8,128)(2,1)S(1)}, u32[]{:S(2)}, u32[]{:S(2)}) collective-permute-start(s16[272,128]{1,0:T(8,128)(2,1)S(1)} %get-tuple-element.43), channel_id=1, source_target_pairs={{0,4},{4,8},{8,12},{12,0},{1,5},{5,9},{9,13},{13,1},{2,6},{6,10},{... | collective-permute-start | bytes 208904 | tf_op jit(solution)/shard_map/ppermute | solution.py:539
  38.9 8.5 %collective-permute-start.13 = (s16[272,128]{1,0:T(8,128)(2,1)S(1)}, s16[272,128]{1,0:T(8,128)(2,1)S(1)}, u32[]{:S(2)}, u32[]{:S(2)}) collective-permute-start(s16[272,128]{1,0:T(8,128)(2,1)S(1)} %get-tuple-element.44), channel_id=1, source_target_pairs={{0,8},{4,12},{8,0},{12,4},{1,9},{5,13},{9,1},{13,5},{2,10},{6,14},... | collective-permute-start | bytes 208904 | tf_op jit(solution)/shard_map/ppermute | solution.py:539
  41.6 5.8 %collective-permute-start.14 = (s16[272,128]{1,0:T(8,128)(2,1)S(1)}, s16[272,128]{1,0:T(8,128)(2,1)S(1)}, u32[]{:S(2)}, u32[]{:S(2)}) collective-permute-start(s16[272,128]{1,0:T(8,128)(2,1)S(1)} %get-tuple-element.45), channel_id=1, source_target_pairs={{0,12},{4,0},{8,4},{12,8},{1,13},{5,1},{9,5},{13,9},{2,14},{6,2},{... | collective-permute-start | bytes 208904 | tf_op jit(solution)/shard_map/ppermute | solution.py:539
  42.7 4.0 %collective-permute-start.11 = (f32[64,128]{1,0:T(8,128)S(1)}, f32[64,128]{1,0:T(8,128)S(1)}, u32[]{:S(2)}, u32[]{:S(2)}) collective-permute-start(f32[64,128]{1,0:T(8,128)S(1)} %add_add_fusion.refs_1_), channel_id=1, source_target_pairs={{0,2},{2,0},{1,3},{3,1},{4,6},{6,4},{5,7},{7,5},{8,10},{10,8},{9,1... | collective-permute-start | bytes 98312 | tf_op jit(solution)/shard_map/ppermute | solution.py:547
  47.4 1.5 %collective-permute-start.15 = (bf16[1,256,128]{2,1,0:T(8,128)(2,1)S(1)}, bf16[1,256,128]{2,1,0:T(8,128)(2,1)S(1)}, u32[]{:S(2)}, u32[]{:S(2)}) collective-permute-start(bf16[1,256,128]{2,1,0:T(8,128)(2,1)S(1)} %get-tuple-element.46.refs_4_.refs_7_), channel_id=1, source_target_pairs={{0,1},{1,0},{2,3},{3,2},{4,5},{5,4},{6,7},{7,6},{8,9},{9,8},{10,11... | collective-permute-start | bytes 196616 | tf_op jit(solution)/shard_map/ppermute | solution.py:539
  47.5 1.5 %collective-permute-start.16 = (bf16[1,256,128]{2,1,0:T(8,128)(2,1)S(1)}, bf16[1,256,128]{2,1,0:T(8,128)(2,1)S(1)}, u32[]{:S(2)}, u32[]{:S(2)}) collective-permute-start(bf16[1,256,128]{2,1,0:T(8,128)(2,1)S(1)} %get-tuple-element.47.refs_5_.refs_8_), channel_id=1, source_target_pairs={{0,1},{1,0},{2,3},{3,2},{4,5},{5,4},{6,7},{7,6},{8,9},{9,8},{10,11... | collective-permute-start | bytes 196616 | tf_op jit(solution)/shard_map/ppermute | solution.py:539
  48.0 1.3 %collective-permute-start.17 = (bf16[1,256,128]{2,1,0:T(8,128)(2,1)S(1)}, bf16[1,256,128]{2,1,0:T(8,128)(2,1)S(1)}, u32[]{:S(2)}, u32[]{:S(2)}) collective-permute-start(bf16[1,256,128]{2,1,0:T(8,128)(2,1)S(1)} %get-tuple-element.48.refs_6_.refs_9_), channel_id=1, source_target_pairs={{0,1},{1,0},{2,3},{3,2},{4,5},{5,4},{6,7},{7,6},{8,9},{9,8},{10,11... | collective-permute-start | bytes 196616 | tf_op jit(solution)/shard_map/ppermute | solution.py:539
  50.3 5.8 %collective-permute-start.18 = (s16[32,2176]{1,0:T(8,128)(2,1)S(1)}, s16[32,2176]{1,0:T(8,128)(2,1)S(1)}, u32[]{:S(2)}, u32[]{:S(2)}) collective-permute-start(s16[32,2176]{1,0:T(8,128)(2,1)S(1)} %shard_map.68.refs_2_), channel_id=1, source_target_pairs={{0,2},{2,0},{1,3},{3,1},{4,6},{6,4},{5,7},{7,5},{8,10},{10,8},{9,1... | collective-permute-start | bytes 417800 | tf_op jit(solution)/shard_map/ppermute | solution.py:547
  56.9 4.4 %collective-permute-start.19 = (f32[32,2048]{1,0:T(8,128)S(1)}, f32[32,2048]{1,0:T(8,128)S(1)}, u32[]{:S(2)}, u32[]{:S(2)}) collective-permute-start(f32[32,2048]{1,0:T(8,128)S(1)} %get-tuple-element.49.refs_0_.refs_3_), channel_id=1, source_target_pairs={{0,1},{1,0},{2,3},{3,2},{4,5},{5,4},{6,7},{7,6},{8,9},{9,8},{10,11... | collective-permute-start | bytes 786440 | tf_op jit(solution)/shard_map/ppermute | solution.py:539
  57.0 6.2 %collective-permute-start.20 = (s16[144,128]{1,0:T(8,128)(2,1)S(1)}, s16[144,128]{1,0:T(8,128)(2,1)S(1)}, u32[]{:S(2)}, u32[]{:S(2)}) collective-permute-start(s16[144,128]{1,0:T(8,128)(2,1)S(1)} %get-tuple-element.50), channel_id=1, source_target_pairs={{0,4},{4,8},{8,12},{12,0},{1,5},{5,9},{9,13},{13,1},{2,6},{6,10},{... | collective-permute-start | bytes 110600 | tf_op jit(solution)/shard_map/ppermute | solution.py:539
  58.4 5.9 %collective-permute-start.21 = (s16[144,128]{1,0:T(8,128)(2,1)S(1)}, s16[144,128]{1,0:T(8,128)(2,1)S(1)}, u32[]{:S(2)}, u32[]{:S(2)}) collective-permute-start(s16[144,128]{1,0:T(8,128)(2,1)S(1)} %get-tuple-element.51), channel_id=1, source_target_pairs={{0,8},{4,12},{8,0},{12,4},{1,9},{5,13},{9,1},{13,5},{2,10},{6,14},... | collective-permute-start | bytes 110600 | tf_op jit(solution)/shard_map/ppermute | solution.py:539
  60.2 4.7 %collective-permute-start.22 = (s16[144,128]{1,0:T(8,128)(2,1)S(1)}, s16[144,128]{1,0:T(8,128)(2,1)S(1)}, u32[]{:S(2)}, u32[]{:S(2)}) collective-permute-start(s16[144,128]{1,0:T(8,128)(2,1)S(1)} %get-tuple-element.52), channel_id=1, source_target_pairs={{0,12},{4,0},{8,4},{12,8},{1,13},{5,1},{9,5},{13,9},{2,14},{6,2},{... | collective-permute-start | bytes 110600 | tf_op jit(solution)/shard_map/ppermute | solution.py:539
  61.8 4.0 %collective-permute-start.23 = (f32[32,128]{1,0:T(8,128)S(1)}, f32[32,128]{1,0:T(8,128)S(1)}, u32[]{:S(2)}, u32[]{:S(2)}) collective-permute-start(f32[32,128]{1,0:T(8,128)S(1)} %shard_map.70.refs_2_), channel_id=1, source_target_pairs={{0,4},{4,0},{8,12},{12,8},{1,5},{5,1},{9,13},{13,9},{2,6},{6,2},{1... | collective-permute-start | bytes 49160 | tf_op jit(solution)/shard_map/ppermute | solution.py:547
  66.0 6.2 %collective-permute-start.24 = (s16[32,2176]{1,0:T(8,128)(2,1)S(1)}, s16[32,2176]{1,0:T(8,128)(2,1)S(1)}, u32[]{:S(2)}, u32[]{:S(2)}) collective-permute-start(s16[32,2176]{1,0:T(8,128)(2,1)S(1)} %shard_map.72.refs_1_), channel_id=1, source_target_pairs={{0,2},{2,0},{1,3},{3,1},{4,6},{6,4},{5,7},{7,5},{8,10},{10,8},{9,1... | collective-permute-start | bytes 417800 | tf_op jit(solution)/shard_map/ppermute | solution.py:547
  67.6 4.6 %collective-permute-start.25 = (f32[32,128]{1,0:T(8,128)S(1)}, f32[32,128]{1,0:T(8,128)S(1)}, u32[]{:S(2)}, u32[]{:S(2)}) collective-permute-start(f32[32,128]{1,0:T(8,128)S(1)} %add.20.after.refs_0_), channel_id=1, source_target_pairs={{0,8},{4,12},{8,0},{12,4},{1,9},{5,13},{9,1},{13,5},{2,10},{6,14},... | collective-permute-start | bytes 49160 | tf_op jit(solution)/shard_map/ppermute | solution.py:547
  72.3 1.8 %collective-permute-start.26 = (f32[32,2048]{1,0:T(8,128)S(1)}, f32[32,2048]{1,0:T(8,128)S(1)}, u32[]{:S(2)}, u32[]{:S(2)}) collective-permute-start(f32[32,2048]{1,0:T(8,128)S(1)} %shard_map.73.after.refs_1_), channel_id=1, source_target_pairs={{0,1},{1,0},{2,3},{3,2},{4,5},{5,4},{6,7},{7,6},{8,9},{9,8},{10,11... | collective-permute-start | bytes 786440 | tf_op jit(solution)/shard_map/ppermute | solution.py:539
  75.0 5.6 %collective-permute-start.27 = (f32[32,128]{1,0:T(8,128)S(1)}, f32[32,128]{1,0:T(8,128)S(1)}, u32[]{:S(2)}, u32[]{:S(2)}) collective-permute-start(f32[32,128]{1,0:T(8,128)S(1)} %get-tuple-element.54.refs_1_), channel_id=1, source_target_pairs={{0,4},{4,8},{8,12},{12,0},{1,5},{5,9},{9,13},{13,1},{2,6},{6,10},{... | collective-permute-start | bytes 49160 | tf_op jit(solution)/shard_map/ppermute | solution.py:539
  75.8 4.8 %collective-permute-start.28 = (f32[32,128]{1,0:T(8,128)S(1)}, f32[32,128]{1,0:T(8,128)S(1)}, u32[]{:S(2)}, u32[]{:S(2)}) collective-permute-start(f32[32,128]{1,0:T(8,128)S(1)} %get-tuple-element.54.refs_1_), channel_id=1, source_target_pairs={{0,8},{4,12},{8,0},{12,4},{1,9},{5,13},{9,1},{13,5},{2,10},{6,14},... | collective-permute-start | bytes 49160 | tf_op jit(solution)/shard_map/ppermute | solution.py:539
  78.0 3.7 %collective-permute-start.29 = (f32[32,128]{1,0:T(8,128)S(1)}, f32[32,128]{1,0:T(8,128)S(1)}, u32[]{:S(2)}, u32[]{:S(2)}) collective-permute-start(f32[32,128]{1,0:T(8,128)S(1)} %get-tuple-element.54.refs_1_), channel_id=1, source_target_pairs={{0,12},{4,0},{8,4},{12,8},{1,13},{5,1},{9,5},{13,9},{2,14},{6,2},{... | collective-permute-start | bytes 49160 | tf_op jit(solution)/shard_map/ppermute | solution.py:539

commit v17 on v16

--- a/solution.py
+++ b/solution.py
@@ -14,7 +14,6 @@
 CODE_ROWS = 16
 
 VMEM = pl.BlockSpec(memory_space=pltpu.VMEM)
-SMEM = pl.BlockSpec(memory_space=pltpu.SMEM)
 ANY = pl.BlockSpec(memory_space=pl.ANY)
 F32 = jnp.float32
 BF16 = jnp.bfloat16
@@ -27,26 +26,52 @@
 
 def with_position(body):
     def inner(*refs):
-        body([lax.axis_index(name) for name in ("rows", "tiles", "cols")], *refs)
+        return body([lax.axis_index(name) for name in ("rows", "tiles", "cols")], *refs)
 
     return inner
 
 
-def call(body, outs, args, smem_in=(), smem_out=(), any_in=(), scratch=(), any_out=()):
+class Late:
+    def __init__(self, source, table, arrived):
+        self.table = table
+        self.copy = pltpu.make_async_copy(source, table, arrived)
+        self.copy.start()
+
+    def ready(self):
+        self.copy.wait()
+        return self.table
+
+
+def with_late(body, places, count):
+    def inner(*refs):
+        refs, tables, arrived = refs[:-1 - count], refs[-1 - count : -1], refs[-1]
+        refs = list(refs)
+        for i, place in enumerate(places):
+            refs[place] = Late(refs[place], tables[i], arrived.at[i])
+        body(*refs)
+
+    return inner
+
+
+def call(body, outs, args, late=(), any_in=(), scratch=(), any_out=()):
     if args[0] is ME:
         body, args = with_position(body), args[1:]
-        smem_in, any_in = [[i - 1 for i in places] for places in (smem_in, any_in)]
+        late, any_in = [[i - 1 for i in places] for places in (late, any_in)]
+    if late:
+        scratch = [
+            *scratch,
+            *[pltpu.SMEM(args[i].shape, args[i].dtype) for i in late],
+            pltpu.SemaphoreType.DMA((len(late),)),
+        ]
+        any_in = [*any_in, *late]
+        body = with_late(body, late, len(late))
     single = not isinstance(outs, (list, tuple))
     shapes = [outs] if single else list(outs)
     result = pl.pallas_call(
         body,
         out_shape=shapes,
-        in_specs=[
-            SMEM if i in smem_in else ANY if i in any_in else VMEM for i in range(len(args))
-        ],
-        out_specs=[
-            SMEM if i in smem_out else ANY if i in any_out else VMEM for i in range(len(shapes))
-        ],
+        in_specs=[ANY if i in any_in else VMEM for i in range(len(args))],
+        out_specs=[ANY if i in any_out else VMEM for i in range(len(shapes))],
         scratch_shapes=list(scratch),
         compiler_params=pltpu.CompilerParams(vmem_limit_bytes=48 * 2**20),
     )(*args)
@@ -202,13 +227,13 @@
 
 def plan_body(dims, list_order, me, *refs):
     row_count, capacity, slots, blocks_here = dims
-    lists, (emb, after, idx) = refs[:row_count], refs[row_count : row_count + 3]
-    lists = dict(zip(list_order, lists))
-    sends = refs[row_count + 3 :]
+    lists, (emb, after, idx_out) = refs[:row_count], refs[row_count : row_count + 3]
+    sends, (idx, left) = refs[row_count + 3 : -2], refs[-2:]
     row = me[0]
     for i in range(slots):
         for line in (0, 1, 2, 4, 5):
             idx[line, i] = 0
+    lists = dict(zip(list_order, [one.ready() for one in lists]))
 
     def each(step, start):
         if slots <= 8:
@@ -245,18 +270,24 @@
             return (counts[0] + hit.astype(jnp.int32), *more)
 
         each(step, (jnp.int32(0),) * (1 + row_count if k == 0 else 1))
+    leave = pltpu.make_async_copy(idx, idx_out, left)
+    leave.start()
     for k in range(1, row_count):
         for j in range(capacity):
             sends[k - 1][j * BLOCK : (j + 1) * BLOCK, :] = emb[at_block(idx[4, k * capacity + j]), :]
+    leave.wait()
 
 
 def squares(block):
     return jnp.sum(jnp.square(block.astype(F32)), axis=1, keepdims=True)
 
 
-def partial_distance(left, right, left_sq, right_sq):
+def as_row(column):
+    return jnp.sum(jnp.where(eye_mask(BLOCK), column, 0.0), axis=0, keepdims=True)
+
+
+def partial_distance(left, right, left_sq, right_row):
     inner = lax.dot_general(left, right, NT, preferred_element_type=F32)
-    right_row = jnp.sum(jnp.where(eye_mask(BLOCK), right_sq, 0.0), axis=0, keepdims=True)
     return left_sq + right_row - 2.0 * inner
 
 
@@ -264,7 +295,9 @@
     for i in range(own_blocks):
         block = emb[at_block(i * tile_count + me[1]), :]
         block_sq = squares(block)
-        out[i * BLOCK : (i + 1) * BLOCK, :] = partial_distance(block, block, block_sq, block_sq)
+        out[i * BLOCK : (i + 1) * BLOCK, :] = partial_distance(
+            block, block, block_sq, as_row(block_sq)
+        )
 
 
 def squares_body(emb, after, out):
@@ -275,20 +308,24 @@
 
 def pair_distance_body(order, capacity, idx, emb, own_squares, *refs):
     far, out = dict(zip(order, refs)), refs[-1]
-    row_count = len(order) + 1
-    for k in range(row_count):
+    rows = {}
+    for k in order:
+        for j in range(capacity):
+            rows[k, j] = as_row(squares(far[k][j * BLOCK : (j + 1) * BLOCK, :]))
+    idx = idx.ready()
+    for k in range(len(order) + 1):
         for j in range(capacity):
             slot = k * capacity + j
             left = emb[at_block(idx[0, slot]), :]
             left_sq = own_squares[at_block(idx[0, slot]), :]
             if k == 0:
                 right = emb[at_block(idx[4, j]), :]
-                right_sq = own_squares[at_block(idx[4, j]), :]
+                right_row = as_row(own_squares[at_block(idx[4, j]), :])
             else:
                 right = far[k][j * BLOCK : (j + 1) * BLOCK, :]
-                right_sq = squares(right)
+                right_row = rows[k, j]
             part = slice(slot * BLOCK, (slot + 1) * BLOCK)
-            out[part, :] = partial_distance(left, right, left_sq, right_sq)
+            out[part, :] = partial_distance(left, right, left_sq, right_row)
 
 
 def self_tile_body(own_blocks, mine, other, packed, sums):
@@ -311,12 +348,13 @@
         place = pl.ds(block, 1)
         table[place, :] = table[place, :] + line
 
+    all_tiles = jnp.exp(-kernel_gamma * (mine[...] + other[...] - 2.0))
+    idx = idx.ready()
     for k in range(row_count):
         tiles = []
         for j in range(capacity):
             slot = k * capacity + j
-            part = slice(slot * BLOCK, (slot + 1) * BLOCK)
-            tile = jnp.exp(-kernel_gamma * (mine[part, :] + other[part, :] - 2.0))
+            tile = all_tiles[slot * BLOCK : (slot + 1) * BLOCK]
             tile = jnp.where(idx[2, slot] > 0, tile, 0.0)
             turned = tile.T
             near_tiles[slot] = pack(turned)
@@ -387,9 +425,11 @@
     for i in range(blocks_here // tile_count):
         block = i * tile_count + tile_index
         add_product(out, block, self_tiles[i], scaled(block))
+    idx = idx.ready()
     for j in range(capacity):
         add_product(out, idx[0, j], near_tiles[j], scaled(idx[4, j]))
         add_product(out, idx[4, j], home_tiles[j], scaled(idx[0, j]))
+    return idx
 
 
 def apply_far(dims, me, idx, inverse, received, base, near_tiles, sent, shared, out):
@@ -433,7 +473,7 @@
     sent, shared, messages = refs[:others], refs[others : 2 * others], refs[2 * others : 3 * others]
     out, total = refs[3 * others :]
     total[...] = started[...]
-    apply_far(dims, me, idx, inverse, messages, per_core * BLOCK, near_tiles, sent, shared, total)
+    apply_far(dims, me, idx.ready(), inverse, messages, per_core * BLOCK, near_tiles, sent, shared, total)
     put_sum(coded, total, out)
 
 
@@ -441,7 +481,7 @@
     others = dims[0] - 1
     sent, shared, received = refs[:others], refs[others : 2 * others], refs[2 * others : 3 * others]
     out = refs[-1]
-    apply_own(dims, me, idx, inverse, own, near_tiles, home_tiles, self_tiles, out)
+    idx = apply_own(dims, me, idx, inverse, own, near_tiles, home_tiles, self_tiles, out)
     apply_far(dims, me, idx, inverse, received, 0, near_tiles, sent, shared, out)
 
 
@@ -484,6 +524,7 @@
     sends, (codes, powers, parts) = refs[:-3], refs[-3:]
     take_sum(coded, me, blocks_here, inverse, mine, other, out)
     encode_blocks(out, codes, powers, parts)
+    idx = idx.ready()
     for k in range(1, row_count):
         pick_columns(idx, k, row_count, capacity, codes, powers, parts, sends[k - 1], 0, ([], []))
 
@@ -583,15 +624,15 @@
         functools.partial(self_distance_body, own_blocks, tile_count),
         sds((own_blocks * BLOCK, BLOCK), F32),
         [ME, embeddings],
-        smem_in=(0,),
     )
     planned = call(
         functools.partial(plan_body, (row_count, capacity, slots, blocks_here), list_order),
         [sds((6, slots + 1), jnp.int32)] + [sds((capacity * BLOCK, half_features), BF16) for _ in others],
         [ME, *[lists[k] for k in list_order], embeddings, self_part],
-        smem_in=range(1 + row_count),
+        late=range(1, 1 + row_count),
         any_in=(row_count + 2,),
-        smem_out=(0,),
+        any_out=(0,),
+        scratch=[pltpu.SMEM((6, slots + 1), jnp.int32), pltpu.SemaphoreType.DMA],
     )
     idx, sends = planned[0], planned[1:]
     order = sorted(others, key=lambda k: abs(k - row_count // 2))
@@ -613,7 +654,7 @@
         functools.partial(pair_distance_body, order, capacity),
         sds((slots * BLOCK, BLOCK), F32),
         [idx, embeddings, own_squares, *far],
-        smem_in=(0,),
+        late=(0,),
     )
     pair_other = shift_by(pair_part, "cols", core_count, 1)
 
@@ -625,7 +666,7 @@
         [sds((slots, 2 * BLOCK, BLOCK), BF16), sds((capacity, 2 * BLOCK, BLOCK), BF16), table]
         + [sds((per_core * BLOCK + picked + CODE_ROWS, BLOCK), jnp.int16) for _ in others],
         [ME, idx, pair_part, pair_other, self_sums, *start_codes],
-        smem_in=(0, 1),
+        late=(1,),
     )
     near_tiles, home_tiles, degrees, sends = tiles[0], tiles[1], tiles[2], tiles[3:]
     degrees = functools.reduce(jnp.add, row_terms(degrees, row_count))
@@ -648,13 +689,13 @@
         functools.partial(first_own_body, dims),
         [block_shape, table, table],
         [ME, idx, *degree_terms, values, near_tiles, home_tiles, self_tiles],
-        smem_in=(0, 1),
+        late=(1,),
     )
     part = call(
         functools.partial(first_far_body, dims, coded),
         sum_shape,
         [ME, idx, inverse, started, near_tiles, *sent, *shared, *messages],
-        smem_in=(0, 1),
+        late=(1,),
         scratch=[pltpu.VMEM((own_cols, rows_here), F32)],
     )
     mine, other = pair_sum(part, ("tiles",))
@@ -662,19 +703,19 @@
         functools.partial(mapped_body, dims, coded),
         [block_shape] + [sds((picked + CODE_ROWS, BLOCK), jnp.int16) for _ in others],
         [ME, idx, inverse, mine, other],
-        smem_in=(0, 1),
+        late=(1,),
         scratch=code_scratch,
     )
     mapped, sends = first[0], first[1:]
     received = [shift_by(sends[k - 1], "rows", row_count, k) for k in others]
 
     mapped_other = shift_by(mapped, "cols", core_count, 1)
-    first_gram = call(gram_body, folded_square, [ME, mapped, mapped_other], smem_in=(0,))
+    first_gram = call(gram_body, folded_square, [ME, mapped, mapped_other])
     part = call(
         functools.partial(second_apply_body, dims),
         block_shape,
         [ME, idx, inverse, first_gram, mapped, home_tiles, self_tiles, near_tiles, *sent, *shared, *received],
-        smem_in=(0, 1),
+        late=(1,),
         any_in=(3,),
     )
     steps = (row_count - 1).bit_length()
@@ -687,7 +728,6 @@
         functools.partial(last_mapped_body, blocks_here, coded),
         block_shape,
         [ME, inverse, mine, other, gram_terms[1]],
-        smem_in=(0,),
         any_in=(4,),
     )
     second_other = shift_by(second, "cols", core_count, 1)
@@ -696,7 +736,6 @@
         second_gram_body,
         [sds((4 * own_cols, rows_here), BF16), folded_square],
         [ME, factor, second, second_other],
-        smem_in=(0,),
     )
     vectors = call(
         final_body,

time: 84.5 us -> 84.2 us (level)
  no operation moved by 1% of the time
where the time goes in v17:
time: 84.2 us; the launch traced here: 84 us
  starting transfers between devices  36 us (43%)
  waiting for transfers between devices  29.7 us (35%)
  Pallas kernels  14 us (17%)
  local copies, waits for them, and re-layouts  2.7 us (3%)
  between operations  1.5 us (2%)
    ppermute x25, starting transfers between devices, shift_by(): lax.ppermute(value, axes, [(i, (i + shift) % size) for i in range(size)])  29.2 us
    ppermute x25, waiting for transfers between devices, shift_by(): lax.ppermute(value, axes, [(i, (i + shift) % size) for i in range(size)])  19.7 us
    pallas_call x18, Pallas kernels, call(): pl.pallas_call(body, out_shape=shapes, in_specs=[ANY if i in any_in else...  14 us
    ppermute x5, waiting for transfers between devices, pair_step(): lax.ppermute(value, name, [(i, i ^ flip) for i in range(lax.axis_size(nam...  10 us
    ppermute x5, starting transfers between devices, pair_step(): lax.ppermute(value, name, [(i, i ^ flip) for i in range(lax.axis_size(nam...  6.79 us
  transfers between devices with their start and end apart: 30, of which 13 were waited for; matrix products, arithmetic and copies ran while one was open for 1% of the time, Pallas kernels for 7%

profile of v17, /device:TPU:0, one launch (start us, length us, event | category | flops | bytes accessed | tf_op | source)
XLA Modules:
  0.0 84.0 jit_solution(1321478606382572958)
XLA Ops:
  2.0 3.0 %collective-permute-start = (s32[3,8]{1,0:T(4,128)S(1)}, s32[3,8]{1,0:T(4,128)S(1)}, u32[]{:S(2)}, u32[]{:S(2)}) collective-permute-start(s32[3,8]{1,0:T(4,128)S(1)} %concatenate.3.refs_0_), channel_id=1, source_target_pairs={{0,4},{4,8},{8,12},{12,0},{1,5},{5,9},{9,13},{13,1},{2,6},{6,10},{... | collective-permute-start | bytes 296 | tf_op jit(solution)/shard_map/ppermute | solution.py:580
  5.0 2.0 %collective-permute-start.1 = (s32[3,8]{1,0:T(4,128)S(1)}, s32[3,8]{1,0:T(4,128)S(1)}, u32[]{:S(2)}, u32[]{:S(2)}) collective-permute-start(s32[3,8]{1,0:T(4,128)S(1)} %concatenate.3.refs_0_), channel_id=1, source_target_pairs={{0,12},{4,0},{8,4},{12,8},{1,13},{5,1},{9,5},{13,9},{2,14},{6,2},{... | collective-permute-start | bytes 296 | tf_op jit(solution)/shard_map/ppermute | solution.py:580
  7.0 1.0 %collective-permute-start.2 = (s32[3,8]{1,0:T(4,128)S(1)}, s32[3,8]{1,0:T(4,128)S(1)}, u32[]{:S(2)}, u32[]{:S(2)}) collective-permute-start(s32[3,8]{1,0:T(4,128)S(1)} %concatenate.3.refs_0_), channel_id=1, source_target_pairs={{0,8},{4,12},{8,0},{12,4},{1,9},{5,13},{9,1},{13,5},{2,10},{6,14},... | collective-permute-start | bytes 296 | tf_op jit(solution)/shard_map/ppermute | solution.py:580
  8.0 1.4 %copy-done = bf16[2048,384]{1,0:T(8,128)(2,1)S(1)} copy-done((bf16[2048,384]{1,0:T(8,128)(2,1)S(1)}, bf16[2048,384]{1,0:T(8,128)(2,1)}, u32[]{:S(2)}) %copy-start) | copy-done | bytes 1572888
  9.9 1.6 %collective-permute-done.2.refs_3_ = s32[3,8]{1,0:T(4,128)S(1)} collective-permute-done((s32[3,8]{1,0:T(4,128)S(1)}, s32[3,8]{1,0:T(4,128)S(1)}, u32[]{:S(2)}, u32[]{:S(2)}) %collective-permute-start.2) | collective-permute-done | bytes 128 | tf_op jit(solution)/shard_map/ppermute | solution.py:580
  11.5 1.6 %shard_map.60 = (s32[6,9]{1,0:T(8,128)S(1)}, bf16[256,384]{1,0:T(8,128)(2,1)S(1)}, bf16[256,384]{1,0:T(8,128)(2,1)S(1)}, bf16[256,384]{1,0:T(8,128)(2,1)S(1)}) custom-call(s32[3,8]{1,0:T(4,128)S(1)} %concatenate.3.refs_0_, s32[3,8]{1,0:T(4,128)S(1)} %collective-permute-done.refs_1_, s32[3,8]{1,0:T(4,128)S(1)} %collective-permute-done.1.refs_2_, ...), custom_call_target="tpu_custom_call" | custom-call | tf_op jit(solution)/shard_map/pallas_call | solution.py:70
  13.1 1.1 %collective-permute-start.3 = (bf16[256,384]{1,0:T(8,128)(2,1)S(1)}, bf16[256,384]{1,0:T(8,128)(2,1)S(1)}, u32[]{:S(2)}, u32[]{:S(2)}) collective-permute-start(bf16[256,384]{1,0:T(8,128)(2,1)S(1)} %get-tuple-element.30), channel_id=1, source_target_pairs={{0,8},{4,12},{8,0},{12,4},{1,9},{5,13},{9,1},{13,5},{2,10},{6,14},... | collective-permute-start | bytes 589832 | tf_op jit(solution)/shard_map/ppermute | solution.py:580
  14.2 1.4 %collective-permute-start.4 = (bf16[256,384]{1,0:T(8,128)(2,1)S(1)}, bf16[256,384]{1,0:T(8,128)(2,1)S(1)}, u32[]{:S(2)}, u32[]{:S(2)}) collective-permute-start(bf16[256,384]{1,0:T(8,128)(2,1)S(1)} %get-tuple-element.31), channel_id=1, source_target_pairs={{0,12},{4,0},{8,4},{12,8},{1,13},{5,1},{9,5},{13,9},{2,14},{6,2},{... | collective-permute-start | bytes 589832 | tf_op jit(solution)/shard_map/ppermute | solution.py:580
  16.5 11.4 %collective-permute-done.3.refs_3_ = bf16[256,384]{1,0:T(8,128)(2,1)S(1)} collective-permute-done((bf16[256,384]{1,0:T(8,128)(2,1)S(1)}, bf16[256,384]{1,0:T(8,128)(2,1)S(1)}, u32[]{:S(2)}, u32[]{:S(2)}) %collective-permute-start.3) | collective-permute-done | bytes 196640 | tf_op jit(solution)/shard_map/ppermute | solution.py:580
  28.0 1.1 %shard_map.62.refs_1_ = f32[1024,128]{1,0:T(8,128)S(1)} custom-call(s32[6,9]{1,0:T(8,128)S(1)} %get-tuple-element.29.after.refs_0_, bf16[2048,384]{1,0:T(8,128)(2,1)S(1)} %copy-done, f32[2048,128]{1,0:T(8,128)S(1)} %shard_map.61.refs_2_, bf16[256,384]{1,0:T(8,128)(2,1)S(1)} %collective-permute-done.3.refs_3_, ...), custom_call_target="tpu_custom_call" | custom-call | tf_op jit(solution)/shard_map/pallas_call | solution.py:70
  29.5 1.5 %collective-permute-done.6.refs_2_ = f32[1024,128]{1,0:T(8,128)S(1)} collective-permute-done((f32[1024,128]{1,0:T(8,128)S(1)}, f32[1024,128]{1,0:T(8,128)S(1)}, u32[]{:S(2)}, u32[]{:S(2)}) %collective-permute-start.6) | collective-permute-done | bytes 524320 | tf_op jit(solution)/shard_map/ppermute | solution.py:580
  31.9 2.2 %collective-permute-start.10 = (f32[64,128]{1,0:T(8,128)S(1)}, f32[64,128]{1,0:T(8,128)S(1)}, u32[]{:S(2)}, u32[]{:S(2)}) collective-permute-start(f32[64,128]{1,0:T(8,128)S(1)} %get-tuple-element.37), channel_id=1, source_target_pairs={{0,12},{4,0},{8,4},{12,8},{1,13},{5,1},{9,5},{13,9},{2,14},{6,2},{... | collective-permute-start | bytes 98312 | tf_op jit(solution)/shard_map/ppermute | solution.py:580
  34.1 2.4 %collective-permute-start.8 = (f32[64,128]{1,0:T(8,128)S(1)}, f32[64,128]{1,0:T(8,128)S(1)}, u32[]{:S(2)}, u32[]{:S(2)}) collective-permute-start(f32[64,128]{1,0:T(8,128)S(1)} %get-tuple-element.37), channel_id=1, source_target_pairs={{0,4},{4,8},{8,12},{12,0},{1,5},{5,9},{9,13},{13,1},{2,6},{6,10},{... | collective-permute-start | bytes 98312 | tf_op jit(solution)/shard_map/ppermute | solution.py:580
  36.6 2.2 %collective-permute-start.9 = (f32[64,128]{1,0:T(8,128)S(1)}, f32[64,128]{1,0:T(8,128)S(1)}, u32[]{:S(2)}, u32[]{:S(2)}) collective-permute-start(f32[64,128]{1,0:T(8,128)S(1)} %get-tuple-element.37), channel_id=1, source_target_pairs={{0,8},{4,12},{8,0},{12,4},{1,9},{5,13},{9,1},{13,5},{2,10},{6,14},... | collective-permute-start | bytes 98312 | tf_op jit(solution)/shard_map/ppermute | solution.py:580
  38.8 2.7 %collective-permute-start.13 = (s16[272,128]{1,0:T(8,128)(2,1)S(1)}, s16[272,128]{1,0:T(8,128)(2,1)S(1)}, u32[]{:S(2)}, u32[]{:S(2)}) collective-permute-start(s16[272,128]{1,0:T(8,128)(2,1)S(1)} %get-tuple-element.44), channel_id=1, source_target_pairs={{0,8},{4,12},{8,0},{12,4},{1,9},{5,13},{9,1},{13,5},{2,10},{6,14},... | collective-permute-start | bytes 208904 | tf_op jit(solution)/shard_map/ppermute | solution.py:580
  41.5 1.1 %collective-permute-start.14 = (s16[272,128]{1,0:T(8,128)(2,1)S(1)}, s16[272,128]{1,0:T(8,128)(2,1)S(1)}, u32[]{:S(2)}, u32[]{:S(2)}) collective-permute-start(s16[272,128]{1,0:T(8,128)(2,1)S(1)} %get-tuple-element.45), channel_id=1, source_target_pairs={{0,12},{4,0},{8,4},{12,8},{1,13},{5,1},{9,5},{13,9},{2,14},{6,2},{... | collective-permute-start | bytes 208904 | tf_op jit(solution)/shard_map/ppermute | solution.py:580
  42.6 1.6 %collective-permute-start.11 = (f32[64,128]{1,0:T(8,128)S(1)}, f32[64,128]{1,0:T(8,128)S(1)}, u32[]{:S(2)}, u32[]{:S(2)}) collective-permute-start(f32[64,128]{1,0:T(8,128)S(1)} %add_add_fusion.refs_1_), channel_id=1, source_target_pairs={{0,2},{2,0},{1,3},{3,1},{4,6},{6,4},{5,7},{7,5},{8,10},{10,8},{9,1... | collective-permute-start | bytes 98312 | tf_op jit(solution)/shard_map/ppermute | solution.py:588
  44.2 2.4 %collective-permute-done.11.refs_2_.refs_3_ = f32[64,128]{1,0:T(8,128)S(1)} collective-permute-done((f32[64,128]{1,0:T(8,128)S(1)}, f32[64,128]{1,0:T(8,128)S(1)}, u32[]{:S(2)}, u32[]{:S(2)}) %collective-permute-start.11) | collective-permute-done | bytes 32800 | tf_op jit(solution)/shard_map/ppermute | solution.py:588
  50.1 1.6 %collective-permute-start.18 = (s16[32,2176]{1,0:T(8,128)(2,1)S(1)}, s16[32,2176]{1,0:T(8,128)(2,1)S(1)}, u32[]{:S(2)}, u32[]{:S(2)}) collective-permute-start(s16[32,2176]{1,0:T(8,128)(2,1)S(1)} %shard_map.68.refs_2_), channel_id=1, source_target_pairs={{0,2},{2,0},{1,3},{3,1},{4,6},{6,4},{5,7},{7,5},{8,10},{10,8},{9,1... | collective-permute-start | bytes 417800 | tf_op jit(solution)/shard_map/ppermute | solution.py:588
  51.7 4.3 %collective-permute-done.18.refs_3_ = s16[32,2176]{1,0:T(8,128)(2,1)S(1)} collective-permute-done((s16[32,2176]{1,0:T(8,128)(2,1)S(1)}, s16[32,2176]{1,0:T(8,128)(2,1)S(1)}, u32[]{:S(2)}, u32[]{:S(2)}) %collective-permute-start.18) | collective-permute-done | bytes 139296 | tf_op jit(solution)/shard_map/ppermute | solution.py:588
  56.7 1.4 %collective-permute-start.20 = (s16[144,128]{1,0:T(8,128)(2,1)S(1)}, s16[144,128]{1,0:T(8,128)(2,1)S(1)}, u32[]{:S(2)}, u32[]{:S(2)}) collective-permute-start(s16[144,128]{1,0:T(8,128)(2,1)S(1)} %get-tuple-element.50), channel_id=1, source_target_pairs={{0,4},{4,8},{8,12},{12,0},{1,5},{5,9},{9,13},{13,1},{2,6},{6,10},{... | collective-permute-start | bytes 110600 | tf_op jit(solution)/shard_map/ppermute | solution.py:580
  58.1 1.8 %collective-permute-start.21 = (s16[144,128]{1,0:T(8,128)(2,1)S(1)}, s16[144,128]{1,0:T(8,128)(2,1)S(1)}, u32[]{:S(2)}, u32[]{:S(2)}) collective-permute-start(s16[144,128]{1,0:T(8,128)(2,1)S(1)} %get-tuple-element.51), channel_id=1, source_target_pairs={{0,8},{4,12},{8,0},{12,4},{1,9},{5,13},{9,1},{13,5},{2,10},{6,14},... | collective-permute-start | bytes 110600 | tf_op jit(solution)/shard_map/ppermute | solution.py:580
  59.8 1.2 %collective-permute-start.22 = (s16[144,128]{1,0:T(8,128)(2,1)S(1)}, s16[144,128]{1,0:T(8,128)(2,1)S(1)}, u32[]{:S(2)}, u32[]{:S(2)}) collective-permute-start(s16[144,128]{1,0:T(8,128)(2,1)S(1)} %get-tuple-element.52), channel_id=1, source_target_pairs={{0,12},{4,0},{8,4},{12,8},{1,13},{5,1},{9,5},{13,9},{2,14},{6,2},{... | collective-permute-start | bytes 110600 | tf_op jit(solution)/shard_map/ppermute | solution.py:580
  62.9 1.1 %collective-permute-done.21.refs_14_ = s16[144,128]{1,0:T(8,128)(2,1)S(1)} collective-permute-done((s16[144,128]{1,0:T(8,128)(2,1)S(1)}, s16[144,128]{1,0:T(8,128)(2,1)S(1)}, u32[]{:S(2)}, u32[]{:S(2)}) %collective-permute-start.21) | collective-permute-done | bytes 36896 | tf_op jit(solution)/shard_map/ppermute | solution.py:580
  65.7 1.5 %collective-permute-start.24 = (s16[32,2176]{1,0:T(8,128)(2,1)S(1)}, s16[32,2176]{1,0:T(8,128)(2,1)S(1)}, u32[]{:S(2)}, u32[]{:S(2)}) collective-permute-start(s16[32,2176]{1,0:T(8,128)(2,1)S(1)} %shard_map.72.refs_1_), channel_id=1, source_target_pairs={{0,2},{2,0},{1,3},{3,1},{4,6},{6,4},{5,7},{7,5},{8,10},{10,8},{9,1... | collective-permute-start | bytes 417800 | tf_op jit(solution)/shard_map/ppermute | solution.py:588
  67.2 1.3 %collective-permute-start.25 = (f32[32,128]{1,0:T(8,128)S(1)}, f32[32,128]{1,0:T(8,128)S(1)}, u32[]{:S(2)}, u32[]{:S(2)}) collective-permute-start(f32[32,128]{1,0:T(8,128)S(1)} %add.20.after.refs_0_), channel_id=1, source_target_pairs={{0,8},{4,12},{8,0},{12,4},{1,9},{5,13},{9,1},{13,5},{2,10},{6,14},... | collective-permute-start | bytes 49160 | tf_op jit(solution)/shard_map/ppermute | solution.py:588
  68.5 3.4 %collective-permute-done.25.refs_3_.refs_1_ = f32[32,128]{1,0:T(8,128)S(1)} collective-permute-done((f32[32,128]{1,0:T(8,128)S(1)}, f32[32,128]{1,0:T(8,128)S(1)}, u32[]{:S(2)}, u32[]{:S(2)}) %collective-permute-start.25) | collective-permute-done | bytes 16416 | tf_op jit(solution)/shard_map/ppermute | solution.py:588
  72.0 1.7 %shard_map.74.refs_0_ = f32[64,64]{1,0:T(8,128)S(1)} custom-call(f32[32,2048]{1,0:T(8,128)S(1)} %shard_map.73.after.refs_1_, f32[32,128]{1,0:T(8,128)S(1)} %add.20.after.refs_0_, f32[32,128]{1,0:T(8,128)S(1)} %collective-permute-done.25.refs_3_.refs_1_), custom_call_target="tpu_custom_call" | custom-call | tf_op jit(solution)/shard_map/pallas_call | solution.py:70
  75.4 2.2 %collective-permute-start.28 = (f32[32,128]{1,0:T(8,128)S(1)}, f32[32,128]{1,0:T(8,128)S(1)}, u32[]{:S(2)}, u32[]{:S(2)}) collective-permute-start(f32[32,128]{1,0:T(8,128)S(1)} %get-tuple-element.54.refs_1_), channel_id=1, source_target_pairs={{0,8},{4,12},{8,0},{12,4},{1,9},{5,13},{9,1},{13,5},{2,10},{6,14},... | collective-permute-start | bytes 49160 | tf_op jit(solution)/shard_map/ppermute | solution.py:580
  77.6 1.2 %collective-permute-start.29 = (f32[32,128]{1,0:T(8,128)S(1)}, f32[32,128]{1,0:T(8,128)S(1)}, u32[]{:S(2)}, u32[]{:S(2)}) collective-permute-start(f32[32,128]{1,0:T(8,128)S(1)} %get-tuple-element.54.refs_1_), channel_id=1, source_target_pairs={{0,12},{4,0},{8,4},{12,8},{1,13},{5,1},{9,5},{13,9},{2,14},{6,2},{... | collective-permute-start | bytes 49160 | tf_op jit(solution)/shard_map/ppermute | solution.py:580
  80.2 1.1 %collective-permute-done.29.refs_4_ = f32[32,128]{1,0:T(8,128)S(1)} collective-permute-done((f32[32,128]{1,0:T(8,128)S(1)}, f32[32,128]{1,0:T(8,128)S(1)}, u32[]{:S(2)}, u32[]{:S(2)}) %collective-permute-start.29) | collective-permute-done | bytes 16416 | tf_op jit(solution)/shard_map/ppermute | solution.py:580
  81.3 2.6 %shard_map.76 = f32[32,2048]{1,0:T(8,128)} custom-call(bf16[128,2048]{1,0:T(8,128)(2,1)S(1)} %get-tuple-element.53.refs_0_, f32[32,128]{1,0:T(8,128)S(1)} %get-tuple-element.54.refs_1_, f32[32,128]{1,0:T(8,128)S(1)} %collective-permute-done.27.refs_2_, f32[32,128]{1,0:T(8,128)S(1)} %collective-permute-done.28.refs_3_, ...), custom_call_target="tpu_custom_call" | custom-call | tf_op jit(solution)/shard_map/pallas_call | solution.py:70
  (54 shorter events, 14.4 us)
Async XLA Ops:
  2.0 7.9 %collective-permute-start = (s32[3,8]{1,0:T(4,128)S(1)}, s32[3,8]{1,0:T(4,128)S(1)}, u32[]{:S(2)}, u32[]{:S(2)}) collective-permute-start(s32[3,8]{1,0:T(4,128)S(1)} %concatenate.3.refs_0_), channel_id=1, source_target_pairs={{0,4},{4,8},{8,12},{12,0},{1,5},{5,9},{9,13},{13,1},{2,6},{6,10},{... | collective-permute-start | bytes 296 | tf_op jit(solution)/shard_map/ppermute | solution.py:580
  5.0 4.9 %collective-permute-start.1 = (s32[3,8]{1,0:T(4,128)S(1)}, s32[3,8]{1,0:T(4,128)S(1)}, u32[]{:S(2)}, u32[]{:S(2)}) collective-permute-start(s32[3,8]{1,0:T(4,128)S(1)} %concatenate.3.refs_0_), channel_id=1, source_target_pairs={{0,12},{4,0},{8,4},{12,8},{1,13},{5,1},{9,5},{13,9},{2,14},{6,2},{... | collective-permute-start | bytes 296 | tf_op jit(solution)/shard_map/ppermute | solution.py:580
  7.0 4.5 %collective-permute-start.2 = (s32[3,8]{1,0:T(4,128)S(1)}, s32[3,8]{1,0:T(4,128)S(1)}, u32[]{:S(2)}, u32[]{:S(2)}) collective-permute-start(s32[3,8]{1,0:T(4,128)S(1)} %concatenate.3.refs_0_), channel_id=1, source_target_pairs={{0,8},{4,12},{8,0},{12,4},{1,9},{5,13},{9,1},{13,5},{2,10},{6,14},... | collective-permute-start | bytes 296 | tf_op jit(solution)/shard_map/ppermute | solution.py:580
  8.0 1.4 %copy-start = (bf16[2048,384]{1,0:T(8,128)(2,1)S(1)}, bf16[2048,384]{1,0:T(8,128)(2,1)}, u32[]{:S(2)}) copy-start(bf16[2048,384]{1,0:T(8,128)(2,1)} %refs_1_.1) | copy-start | bytes 4718596
  13.1 14.9 %collective-permute-start.3 = (bf16[256,384]{1,0:T(8,128)(2,1)S(1)}, bf16[256,384]{1,0:T(8,128)(2,1)S(1)}, u32[]{:S(2)}, u32[]{:S(2)}) collective-permute-start(bf16[256,384]{1,0:T(8,128)(2,1)S(1)} %get-tuple-element.30), channel_id=1, source_target_pairs={{0,8},{4,12},{8,0},{12,4},{1,9},{5,13},{9,1},{13,5},{2,10},{6,14},... | collective-permute-start | bytes 589832 | tf_op jit(solution)/shard_map/ppermute | solution.py:580
  14.2 13.8 %collective-permute-start.4 = (bf16[256,384]{1,0:T(8,128)(2,1)S(1)}, bf16[256,384]{1,0:T(8,128)(2,1)S(1)}, u32[]{:S(2)}, u32[]{:S(2)}) collective-permute-start(bf16[256,384]{1,0:T(8,128)(2,1)S(1)} %get-tuple-element.31), channel_id=1, source_target_pairs={{0,12},{4,0},{8,4},{12,8},{1,13},{5,1},{9,5},{13,9},{2,14},{6,2},{... | collective-permute-start | bytes 589832 | tf_op jit(solution)/shard_map/ppermute | solution.py:580
  15.5 12.5 %collective-permute-start.5 = (bf16[256,384]{1,0:T(8,128)(2,1)S(1)}, bf16[256,384]{1,0:T(8,128)(2,1)S(1)}, u32[]{:S(2)}, u32[]{:S(2)}) collective-permute-start(bf16[256,384]{1,0:T(8,128)(2,1)S(1)} %get-tuple-element.32), channel_id=1, source_target_pairs={{0,4},{4,8},{8,12},{12,0},{1,5},{5,9},{9,13},{13,1},{2,6},{6,10},{... | collective-permute-start | bytes 589832 | tf_op jit(solution)/shard_map/ppermute | solution.py:580
  16.2 13.1 %collective-permute-start.7 = (f32[1024,128]{1,0:T(8,128)S(1)}, f32[1024,128]{1,0:T(8,128)S(1)}, u32[]{:S(2)}, u32[]{:S(2)}) collective-permute-start(f32[1024,128]{1,0:T(8,128)S(1)} %shard_map.59.refs_5_.mine), channel_id=1, source_target_pairs={{0,1},{1,0},{2,3},{3,2},{4,5},{5,4},{6,7},{7,6},{8,9},{9,8},{10,11... | collective-permute-start | bytes 1572872 | tf_op jit(solution)/shard_map/ppermute | solution.py:580
  16.5 12.6 %copy-start.1 = (f32[2048,32]{0,1:T(8,128)S(1)}, f32[2048,32]{0,1:T(8,128)}, u32[]{:S(2)}) copy-start(f32[2048,32]{0,1:T(8,128)} %param.5) | copy-start | bytes 786436
  29.1 2.0 %collective-permute-start.6 = (f32[1024,128]{1,0:T(8,128)S(1)}, f32[1024,128]{1,0:T(8,128)S(1)}, u32[]{:S(2)}, u32[]{:S(2)}) collective-permute-start(f32[1024,128]{1,0:T(8,128)S(1)} %shard_map.62.refs_1_), channel_id=1, source_target_pairs={{0,1},{1,0},{2,3},{3,2},{4,5},{5,4},{6,7},{7,6},{8,9},{9,8},{10,11... | collective-permute-start | bytes 1572872 | tf_op jit(solution)/shard_map/ppermute | solution.py:580
  31.9 9.5 %collective-permute-start.10 = (f32[64,128]{1,0:T(8,128)S(1)}, f32[64,128]{1,0:T(8,128)S(1)}, u32[]{:S(2)}, u32[]{:S(2)}) collective-permute-start(f32[64,128]{1,0:T(8,128)S(1)} %get-tuple-element.37), channel_id=1, source_target_pairs={{0,12},{4,0},{8,4},{12,8},{1,13},{5,1},{9,5},{13,9},{2,14},{6,2},{... | collective-permute-start | bytes 98312 | tf_op jit(solution)/shard_map/ppermute | solution.py:580
  34.1 8.4 %collective-permute-start.8 = (f32[64,128]{1,0:T(8,128)S(1)}, f32[64,128]{1,0:T(8,128)S(1)}, u32[]{:S(2)}, u32[]{:S(2)}) collective-permute-start(f32[64,128]{1,0:T(8,128)S(1)} %get-tuple-element.37), channel_id=1, source_target_pairs={{0,4},{4,8},{8,12},{12,0},{1,5},{5,9},{9,13},{13,1},{2,6},{6,10},{... | collective-permute-start | bytes 98312 | tf_op jit(solution)/shard_map/ppermute | solution.py:580
  36.6 6.0 %collective-permute-start.9 = (f32[64,128]{1,0:T(8,128)S(1)}, f32[64,128]{1,0:T(8,128)S(1)}, u32[]{:S(2)}, u32[]{:S(2)}) collective-permute-start(f32[64,128]{1,0:T(8,128)S(1)} %get-tuple-element.37), channel_id=1, source_target_pairs={{0,8},{4,12},{8,0},{12,4},{1,9},{5,13},{9,1},{13,5},{2,10},{6,14},... | collective-permute-start | bytes 98312 | tf_op jit(solution)/shard_map/ppermute | solution.py:580
  38.7 7.8 %collective-permute-start.12 = (s16[272,128]{1,0:T(8,128)(2,1)S(1)}, s16[272,128]{1,0:T(8,128)(2,1)S(1)}, u32[]{:S(2)}, u32[]{:S(2)}) collective-permute-start(s16[272,128]{1,0:T(8,128)(2,1)S(1)} %get-tuple-element.43), channel_id=1, source_target_pairs={{0,4},{4,8},{8,12},{12,0},{1,5},{5,9},{9,13},{13,1},{2,6},{6,10},{... | collective-permute-start | bytes 208904 | tf_op jit(solution)/shard_map/ppermute | solution.py:580
  38.8 8.5 %collective-permute-start.13 = (s16[272,128]{1,0:T(8,128)(2,1)S(1)}, s16[272,128]{1,0:T(8,128)(2,1)S(1)}, u32[]{:S(2)}, u32[]{:S(2)}) collective-permute-start(s16[272,128]{1,0:T(8,128)(2,1)S(1)} %get-tuple-element.44), channel_id=1, source_target_pairs={{0,8},{4,12},{8,0},{12,4},{1,9},{5,13},{9,1},{13,5},{2,10},{6,14},... | collective-permute-start | bytes 208904 | tf_op jit(solution)/shard_map/ppermute | solution.py:580
  41.5 5.8 %collective-permute-start.14 = (s16[272,128]{1,0:T(8,128)(2,1)S(1)}, s16[272,128]{1,0:T(8,128)(2,1)S(1)}, u32[]{:S(2)}, u32[]{:S(2)}) collective-permute-start(s16[272,128]{1,0:T(8,128)(2,1)S(1)} %get-tuple-element.45), channel_id=1, source_target_pairs={{0,12},{4,0},{8,4},{12,8},{1,13},{5,1},{9,5},{13,9},{2,14},{6,2},{... | collective-permute-start | bytes 208904 | tf_op jit(solution)/shard_map/ppermute | solution.py:580
  42.6 4.0 %collective-permute-start.11 = (f32[64,128]{1,0:T(8,128)S(1)}, f32[64,128]{1,0:T(8,128)S(1)}, u32[]{:S(2)}, u32[]{:S(2)}) collective-permute-start(f32[64,128]{1,0:T(8,128)S(1)} %add_add_fusion.refs_1_), channel_id=1, source_target_pairs={{0,2},{2,0},{1,3},{3,1},{4,6},{6,4},{5,7},{7,5},{8,10},{10,8},{9,1... | collective-permute-start | bytes 98312 | tf_op jit(solution)/shard_map/ppermute | solution.py:588
  47.3 1.5 %collective-permute-start.15 = (bf16[1,256,128]{2,1,0:T(8,128)(2,1)S(1)}, bf16[1,256,128]{2,1,0:T(8,128)(2,1)S(1)}, u32[]{:S(2)}, u32[]{:S(2)}) collective-permute-start(bf16[1,256,128]{2,1,0:T(8,128)(2,1)S(1)} %get-tuple-element.46.refs_4_.refs_7_), channel_id=1, source_target_pairs={{0,1},{1,0},{2,3},{3,2},{4,5},{5,4},{6,7},{7,6},{8,9},{9,8},{10,11... | collective-permute-start | bytes 196616 | tf_op jit(solution)/shard_map/ppermute | solution.py:580
  47.4 1.4 %collective-permute-start.16 = (bf16[1,256,128]{2,1,0:T(8,128)(2,1)S(1)}, bf16[1,256,128]{2,1,0:T(8,128)(2,1)S(1)}, u32[]{:S(2)}, u32[]{:S(2)}) collective-permute-start(bf16[1,256,128]{2,1,0:T(8,128)(2,1)S(1)} %get-tuple-element.47.refs_5_.refs_8_), channel_id=1, source_target_pairs={{0,1},{1,0},{2,3},{3,2},{4,5},{5,4},{6,7},{7,6},{8,9},{9,8},{10,11... | collective-permute-start | bytes 196616 | tf_op jit(solution)/shard_map/ppermute | solution.py:580
  47.9 1.3 %collective-permute-start.17 = (bf16[1,256,128]{2,1,0:T(8,128)(2,1)S(1)}, bf16[1,256,128]{2,1,0:T(8,128)(2,1)S(1)}, u32[]{:S(2)}, u32[]{:S(2)}) collective-permute-start(bf16[1,256,128]{2,1,0:T(8,128)(2,1)S(1)} %get-tuple-element.48.refs_6_.refs_9_), channel_id=1, source_target_pairs={{0,1},{1,0},{2,3},{3,2},{4,5},{5,4},{6,7},{7,6},{8,9},{9,8},{10,11... | collective-permute-start | bytes 196616 | tf_op jit(solution)/shard_map/ppermute | solution.py:580
  50.1 5.8 %collective-permute-start.18 = (s16[32,2176]{1,0:T(8,128)(2,1)S(1)}, s16[32,2176]{1,0:T(8,128)(2,1)S(1)}, u32[]{:S(2)}, u32[]{:S(2)}) collective-permute-start(s16[32,2176]{1,0:T(8,128)(2,1)S(1)} %shard_map.68.refs_2_), channel_id=1, source_target_pairs={{0,2},{2,0},{1,3},{3,1},{4,6},{6,4},{5,7},{7,5},{8,10},{10,8},{9,1... | collective-permute-start | bytes 417800 | tf_op jit(solution)/shard_map/ppermute | solution.py:588
  56.6 4.4 %collective-permute-start.19 = (f32[32,2048]{1,0:T(8,128)S(1)}, f32[32,2048]{1,0:T(8,128)S(1)}, u32[]{:S(2)}, u32[]{:S(2)}) collective-permute-start(f32[32,2048]{1,0:T(8,128)S(1)} %get-tuple-element.49.refs_0_.refs_3_), channel_id=1, source_target_pairs={{0,1},{1,0},{2,3},{3,2},{4,5},{5,4},{6,7},{7,6},{8,9},{9,8},{10,11... | collective-permute-start | bytes 786440 | tf_op jit(solution)/shard_map/ppermute | solution.py:580
  56.7 6.2 %collective-permute-start.20 = (s16[144,128]{1,0:T(8,128)(2,1)S(1)}, s16[144,128]{1,0:T(8,128)(2,1)S(1)}, u32[]{:S(2)}, u32[]{:S(2)}) collective-permute-start(s16[144,128]{1,0:T(8,128)(2,1)S(1)} %get-tuple-element.50), channel_id=1, source_target_pairs={{0,4},{4,8},{8,12},{12,0},{1,5},{5,9},{9,13},{13,1},{2,6},{6,10},{... | collective-permute-start | bytes 110600 | tf_op jit(solution)/shard_map/ppermute | solution.py:580
  58.1 5.9 %collective-permute-start.21 = (s16[144,128]{1,0:T(8,128)(2,1)S(1)}, s16[144,128]{1,0:T(8,128)(2,1)S(1)}, u32[]{:S(2)}, u32[]{:S(2)}) collective-permute-start(s16[144,128]{1,0:T(8,128)(2,1)S(1)} %get-tuple-element.51), channel_id=1, source_target_pairs={{0,8},{4,12},{8,0},{12,4},{1,9},{5,13},{9,1},{13,5},{2,10},{6,14},... | collective-permute-start | bytes 110600 | tf_op jit(solution)/shard_map/ppermute | solution.py:580
  59.8 4.7 %collective-permute-start.22 = (s16[144,128]{1,0:T(8,128)(2,1)S(1)}, s16[144,128]{1,0:T(8,128)(2,1)S(1)}, u32[]{:S(2)}, u32[]{:S(2)}) collective-permute-start(s16[144,128]{1,0:T(8,128)(2,1)S(1)} %get-tuple-element.52), channel_id=1, source_target_pairs={{0,12},{4,0},{8,4},{12,8},{1,13},{5,1},{9,5},{13,9},{2,14},{6,2},{... | collective-permute-start | bytes 110600 | tf_op jit(solution)/shard_map/ppermute | solution.py:580
  61.5 4.0 %collective-permute-start.23 = (f32[32,128]{1,0:T(8,128)S(1)}, f32[32,128]{1,0:T(8,128)S(1)}, u32[]{:S(2)}, u32[]{:S(2)}) collective-permute-start(f32[32,128]{1,0:T(8,128)S(1)} %shard_map.70.refs_2_), channel_id=1, source_target_pairs={{0,4},{4,0},{8,12},{12,8},{1,5},{5,1},{9,13},{13,9},{2,6},{6,2},{1... | collective-permute-start | bytes 49160 | tf_op jit(solution)/shard_map/ppermute | solution.py:588
  65.7 6.2 %collective-permute-start.24 = (s16[32,2176]{1,0:T(8,128)(2,1)S(1)}, s16[32,2176]{1,0:T(8,128)(2,1)S(1)}, u32[]{:S(2)}, u32[]{:S(2)}) collective-permute-start(s16[32,2176]{1,0:T(8,128)(2,1)S(1)} %shard_map.72.refs_1_), channel_id=1, source_target_pairs={{0,2},{2,0},{1,3},{3,1},{4,6},{6,4},{5,7},{7,5},{8,10},{10,8},{9,1... | collective-permute-start | bytes 417800 | tf_op jit(solution)/shard_map/ppermute | solution.py:588
  67.2 4.6 %collective-permute-start.25 = (f32[32,128]{1,0:T(8,128)S(1)}, f32[32,128]{1,0:T(8,128)S(1)}, u32[]{:S(2)}, u32[]{:S(2)}) collective-permute-start(f32[32,128]{1,0:T(8,128)S(1)} %add.20.after.refs_0_), channel_id=1, source_target_pairs={{0,8},{4,12},{8,0},{12,4},{1,9},{5,13},{9,1},{13,5},{2,10},{6,14},... | collective-permute-start | bytes 49160 | tf_op jit(solution)/shard_map/ppermute | solution.py:588
  72.0 1.8 %collective-permute-start.26 = (f32[32,2048]{1,0:T(8,128)S(1)}, f32[32,2048]{1,0:T(8,128)S(1)}, u32[]{:S(2)}, u32[]{:S(2)}) collective-permute-start(f32[32,2048]{1,0:T(8,128)S(1)} %shard_map.73.after.refs_1_), channel_id=1, source_target_pairs={{0,1},{1,0},{2,3},{3,2},{4,5},{5,4},{6,7},{7,6},{8,9},{9,8},{10,11... | collective-permute-start | bytes 786440 | tf_op jit(solution)/shard_map/ppermute | solution.py:580
  74.6 5.6 %collective-permute-start.27 = (f32[32,128]{1,0:T(8,128)S(1)}, f32[32,128]{1,0:T(8,128)S(1)}, u32[]{:S(2)}, u32[]{:S(2)}) collective-permute-start(f32[32,128]{1,0:T(8,128)S(1)} %get-tuple-element.54.refs_1_), channel_id=1, source_target_pairs={{0,4},{4,8},{8,12},{12,0},{1,5},{5,9},{9,13},{13,1},{2,6},{6,10},{... | collective-permute-start | bytes 49160 | tf_op jit(solution)/shard_map/ppermute | solution.py:580
  75.4 4.8 %collective-permute-start.28 = (f32[32,128]{1,0:T(8,128)S(1)}, f32[32,128]{1,0:T(8,128)S(1)}, u32[]{:S(2)}, u32[]{:S(2)}) collective-permute-start(f32[32,128]{1,0:T(8,128)S(1)} %get-tuple-element.54.refs_1_), channel_id=1, source_target_pairs={{0,8},{4,12},{8,0},{12,4},{1,9},{5,13},{9,1},{13,5},{2,10},{6,14},... | collective-permute-start | bytes 49160 | tf_op jit(solution)/shard_map/ppermute | solution.py:580
  77.6 3.7 %collective-permute-start.29 = (f32[32,128]{1,0:T(8,128)S(1)}, f32[32,128]{1,0:T(8,128)S(1)}, u32[]{:S(2)}, u32[]{:S(2)}) collective-permute-start(f32[32,128]{1,0:T(8,128)S(1)} %get-tuple-element.54.refs_1_), channel_id=1, source_target_pairs={{0,12},{4,0},{8,4},{12,8},{1,13},{5,1},{9,5},{13,9},{2,14},{6,2},{... | collective-permute-start | bytes 49160 | tf_op jit(solution)/shard_map/ppermute | solution.py:580

commit v18 on v17

--- a/solution.py
+++ b/solution.py
@@ -436,12 +436,14 @@
     row_count, capacity, per_core, blocks_here, tile_count = dims
     core = me[2]
     count = out.shape[0]
-    lines = [scale_rows(message[message.shape[0] - CODE_ROWS :, :]) for message in received]
+    order = way_order(row_count)
+    received, sent, shared = [dict(zip(order, refs)) for refs in (received, sent, shared)]
+    lines = {k: scale_rows(received[k][received[k].shape[0] - CODE_ROWS :, :]) for k in order}
     first_line = base // BLOCK
 
     def arrived(k, place, block):
-        steps = received[k - 1][pl.ds(pl.multiple_of(base + place * count, CODE_ROWS), count), :]
-        rows = lines[k - 1][first_line : first_line + 2 * capacity, :]
+        steps = received[k][pl.ds(pl.multiple_of(base + place * count, CODE_ROWS), count), :]
+        rows = lines[k][first_line : first_line + 2 * capacity, :]
         return decode(steps, row_at(rows, place) * inverse[pl.ds(block, 1), :])
 
     for k in range(1, row_count):
@@ -452,10 +454,10 @@
             inner = j % per_core
             if j < per_core:
                 place = core * per_core + inner
-                packed = sent[k - 1][inner]
+                packed = sent[k][inner]
             else:
                 place = (1 - core) * per_core + inner
-                packed = shared[k - 1][inner]
+                packed = shared[k][inner]
             slot = k * capacity + place
             add_product(out, idx[4, slot], packed, arrived(k, place, idx[5, slot]))
 
@@ -580,8 +582,12 @@
     return lax.ppermute(value, axes, [(i, (i + shift) % size) for i in range(size)])
 
 
+def way_order(row_count):
+    return sorted(range(1, row_count), key=lambda k: abs(k - row_count // 2))
+
+
 def row_terms(value, row_count):
-    return [value] + [shift_by(value, "rows", row_count, k) for k in range(1, row_count)]
+    return [value] + [shift_by(value, "rows", row_count, k) for k in way_order(row_count)]
 
 
 def pair_step(value, name, flip):
@@ -614,12 +620,13 @@
     own_cols = start.shape[1]
     block_count = row_count * blocks_here
     others = range(1, row_count)
+    order = way_order(row_count)
 
     own_list = jnp.concatenate(
         [pair_list[0], jnp.broadcast_to(pair_count[:, None], (1, slots))], axis=0
     )
-    lists = row_terms(own_list, row_count)
     list_order = [0, *sorted(others, key=lambda k: k * (row_count - k))]
+    lists = [shift_by(own_list, "rows", row_count, k) if k else own_list for k in list_order]
     self_part = call(
         functools.partial(self_distance_body, own_blocks, tile_count),
         sds((own_blocks * BLOCK, BLOCK), F32),
@@ -628,14 +635,13 @@
     planned = call(
         functools.partial(plan_body, (row_count, capacity, slots, blocks_here), list_order),
         [sds((6, slots + 1), jnp.int32)] + [sds((capacity * BLOCK, half_features), BF16) for _ in others],
-        [ME, *[lists[k] for k in list_order], embeddings, self_part],
+        [ME, *lists, embeddings, self_part],
         late=range(1, 1 + row_count),
         any_in=(row_count + 2,),
         any_out=(0,),
         scratch=[pltpu.SMEM((6, slots + 1), jnp.int32), pltpu.SemaphoreType.DMA],
     )
     idx, sends = planned[0], planned[1:]
-    order = sorted(others, key=lambda k: abs(k - row_count // 2))
     far = [shift_by(sends[k - 1], "rows", row_count, -k) for k in order]
 
     self_other = shift_by(self_part, "cols", core_count, 1)
@@ -669,9 +675,11 @@
         late=(1,),
     )
     near_tiles, home_tiles, degrees, sends = tiles[0], tiles[1], tiles[2], tiles[3:]
-    degrees = functools.reduce(jnp.add, row_terms(degrees, row_count))
+    degrees = functools.reduce(
+        jnp.add, [degrees] + [shift_by(degrees, "rows", row_count, k) for k in reversed(order)]
+    )
     degree_terms = pair_sum(degrees, ("tiles",))
-    messages = [shift_by(sends[k - 1], "rows", row_count, k) for k in others]
+    messages = [shift_by(sends[k - 1], "rows", row_count, k) for k in order]
     sent = call(
         functools.partial(split_body, row_count, per_core),
         [sds((per_core, 2 * BLOCK, BLOCK), BF16) for _ in others],
@@ -707,7 +715,7 @@
         scratch=code_scratch,
     )
     mapped, sends = first[0], first[1:]
-    received = [shift_by(sends[k - 1], "rows", row_count, k) for k in others]
+    received = [shift_by(sends[k - 1], "rows", row_count, k) for k in order]
 
     mapped_other = shift_by(mapped, "cols", core_count, 1)
     first_gram = call(gram_body, folded_square, [ME, mapped, mapped_other])

time: 84.2 us -> 85.9 us (1.020)
  waiting for transfers between devices: 29.7 us -> 31.9 us
    ppermute x5, waiting for transfers between devices: 10 us -> 11.8 us  [pair_step(): lax.ppermute(value, name, [(i, i ^ flip) for i in range(lax.axis_size(nam...]
    ppermute x5, starting transfers between devices: 6.79 us -> 5.36 us  [pair_step(): lax.ppermute(value, name, [(i, i ^ flip) for i in range(lax.axis_size(nam...]
    ppermute x25, starting transfers between devices: 29.2 us -> 30.2 us  [shift_by(): lax.ppermute(value, axes, [(i, (i + shift) % size) for i in range(size)])]
  transfers between devices with their start and end apart: 30 -> 30, of which waited for: 13 -> 14; matrix products, arithmetic and copies ran while one was open for 1% -> 1% of each run, Pallas kernels for 7% -> 7%
where the time goes in v18:
time: 85.9 us; the launch traced here: 85.7 us
  starting transfers between devices  35.6 us (41%)
  waiting for transfers between devices  31.9 us (37%)
  Pallas kernels  14.1 us (16%)
  local copies, waits for them, and re-layouts  2.7 us (3%)
  between operations  1.5 us (2%)
    ppermute x25, starting transfers between devices, shift_by(): lax.ppermute(value, axes, [(i, (i + shift) % size) for i in range(size)])  30.2 us
    ppermute x25, waiting for transfers between devices, shift_by(): lax.ppermute(value, axes, [(i, (i + shift) % size) for i in range(size)])  20.1 us
    pallas_call x18, Pallas kernels, call(): pl.pallas_call(body, out_shape=shapes, in_specs=[ANY if i in any_in else...  14.1 us
    ppermute x5, waiting for transfers between devices, pair_step(): lax.ppermute(value, name, [(i, i ^ flip) for i in range(lax.axis_size(nam...  11.8 us
    ppermute x5, starting transfers between devices, pair_step(): lax.ppermute(value, name, [(i, i ^ flip) for i in range(lax.axis_size(nam...  5.36 us
  transfers between devices with their start and end apart: 30, of which 14 were waited for; matrix products, arithmetic and copies ran while one was open for 1% of the time, Pallas kernels for 7%

profile of v18, /device:TPU:0, one launch (start us, length us, event | category | flops | bytes accessed | tf_op | source)
XLA Modules:
  0.0 85.7 jit_solution(4094599154685493187)
XLA Ops:
  2.0 3.0 %collective-permute-start = (s32[3,8]{1,0:T(4,128)S(1)}, s32[3,8]{1,0:T(4,128)S(1)}, u32[]{:S(2)}, u32[]{:S(2)}) collective-permute-start(s32[3,8]{1,0:T(4,128)S(1)} %concatenate.3.refs_0_), channel_id=1, source_target_pairs={{0,4},{4,8},{8,12},{12,0},{1,5},{5,9},{9,13},{13,1},{2,6},{6,10},{... | collective-permute-start | bytes 296 | tf_op jit(solution)/shard_map/ppermute | solution.py:582
  5.0 2.0 %collective-permute-start.1 = (s32[3,8]{1,0:T(4,128)S(1)}, s32[3,8]{1,0:T(4,128)S(1)}, u32[]{:S(2)}, u32[]{:S(2)}) collective-permute-start(s32[3,8]{1,0:T(4,128)S(1)} %concatenate.3.refs_0_), channel_id=1, source_target_pairs={{0,12},{4,0},{8,4},{12,8},{1,13},{5,1},{9,5},{13,9},{2,14},{6,2},{... | collective-permute-start | bytes 296 | tf_op jit(solution)/shard_map/ppermute | solution.py:582
  7.0 1.0 %collective-permute-start.2 = (s32[3,8]{1,0:T(4,128)S(1)}, s32[3,8]{1,0:T(4,128)S(1)}, u32[]{:S(2)}, u32[]{:S(2)}) collective-permute-start(s32[3,8]{1,0:T(4,128)S(1)} %concatenate.3.refs_0_), channel_id=1, source_target_pairs={{0,8},{4,12},{8,0},{12,4},{1,9},{5,13},{9,1},{13,5},{2,10},{6,14},... | collective-permute-start | bytes 296 | tf_op jit(solution)/shard_map/ppermute | solution.py:582
  8.0 1.4 %copy-done = bf16[2048,384]{1,0:T(8,128)(2,1)S(1)} copy-done((bf16[2048,384]{1,0:T(8,128)(2,1)S(1)}, bf16[2048,384]{1,0:T(8,128)(2,1)}, u32[]{:S(2)}) %copy-start) | copy-done | bytes 1572888
  9.9 1.6 %collective-permute-done.2.refs_3_ = s32[3,8]{1,0:T(4,128)S(1)} collective-permute-done((s32[3,8]{1,0:T(4,128)S(1)}, s32[3,8]{1,0:T(4,128)S(1)}, u32[]{:S(2)}, u32[]{:S(2)}) %collective-permute-start.2) | collective-permute-done | bytes 128 | tf_op jit(solution)/shard_map/ppermute | solution.py:582
  11.5 1.6 %shard_map.60 = (s32[6,9]{1,0:T(8,128)S(1)}, bf16[256,384]{1,0:T(8,128)(2,1)S(1)}, bf16[256,384]{1,0:T(8,128)(2,1)S(1)}, bf16[256,384]{1,0:T(8,128)(2,1)S(1)}) custom-call(s32[3,8]{1,0:T(4,128)S(1)} %concatenate.3.refs_0_, s32[3,8]{1,0:T(4,128)S(1)} %collective-permute-done.refs_1_, s32[3,8]{1,0:T(4,128)S(1)} %collective-permute-done.1.refs_2_, ...), custom_call_target="tpu_custom_call" | custom-call | tf_op jit(solution)/shard_map/pallas_call | solution.py:70
  13.1 1.1 %collective-permute-start.3 = (bf16[256,384]{1,0:T(8,128)(2,1)S(1)}, bf16[256,384]{1,0:T(8,128)(2,1)S(1)}, u32[]{:S(2)}, u32[]{:S(2)}) collective-permute-start(bf16[256,384]{1,0:T(8,128)(2,1)S(1)} %get-tuple-element.30), channel_id=1, source_target_pairs={{0,8},{4,12},{8,0},{12,4},{1,9},{5,13},{9,1},{13,5},{2,10},{6,14},... | collective-permute-start | bytes 589832 | tf_op jit(solution)/shard_map/ppermute | solution.py:582
  14.2 1.4 %collective-permute-start.4 = (bf16[256,384]{1,0:T(8,128)(2,1)S(1)}, bf16[256,384]{1,0:T(8,128)(2,1)S(1)}, u32[]{:S(2)}, u32[]{:S(2)}) collective-permute-start(bf16[256,384]{1,0:T(8,128)(2,1)S(1)} %get-tuple-element.31), channel_id=1, source_target_pairs={{0,12},{4,0},{8,4},{12,8},{1,13},{5,1},{9,5},{13,9},{2,14},{6,2},{... | collective-permute-start | bytes 589832 | tf_op jit(solution)/shard_map/ppermute | solution.py:582
  16.5 11.4 %collective-permute-done.3.refs_3_ = bf16[256,384]{1,0:T(8,128)(2,1)S(1)} collective-permute-done((bf16[256,384]{1,0:T(8,128)(2,1)S(1)}, bf16[256,384]{1,0:T(8,128)(2,1)S(1)}, u32[]{:S(2)}, u32[]{:S(2)}) %collective-permute-start.3) | collective-permute-done | bytes 196640 | tf_op jit(solution)/shard_map/ppermute | solution.py:582
  28.0 1.1 %shard_map.62.refs_1_ = f32[1024,128]{1,0:T(8,128)S(1)} custom-call(s32[6,9]{1,0:T(8,128)S(1)} %get-tuple-element.29.after.refs_0_, bf16[2048,384]{1,0:T(8,128)(2,1)S(1)} %copy-done, f32[2048,128]{1,0:T(8,128)S(1)} %shard_map.61.refs_2_, bf16[256,384]{1,0:T(8,128)(2,1)S(1)} %collective-permute-done.3.refs_3_, ...), custom_call_target="tpu_custom_call" | custom-call | tf_op jit(solution)/shard_map/pallas_call | solution.py:70
  29.5 1.5 %collective-permute-done.6.refs_2_ = f32[1024,128]{1,0:T(8,128)S(1)} collective-permute-done((f32[1024,128]{1,0:T(8,128)S(1)}, f32[1024,128]{1,0:T(8,128)S(1)}, u32[]{:S(2)}, u32[]{:S(2)}) %collective-permute-start.6) | collective-permute-done | bytes 524320 | tf_op jit(solution)/shard_map/ppermute | solution.py:582
  31.9 4.8 %collective-permute-start.10 = (f32[64,128]{1,0:T(8,128)S(1)}, f32[64,128]{1,0:T(8,128)S(1)}, u32[]{:S(2)}, u32[]{:S(2)}) collective-permute-start(f32[64,128]{1,0:T(8,128)S(1)} %get-tuple-element.37), channel_id=1, source_target_pairs={{0,8},{4,12},{8,0},{12,4},{1,9},{5,13},{9,1},{13,5},{2,10},{6,14},... | collective-permute-start | bytes 98312 | tf_op jit(solution)/shard_map/ppermute | solution.py:582
  36.7 2.1 %collective-permute-start.8 = (f32[64,128]{1,0:T(8,128)S(1)}, f32[64,128]{1,0:T(8,128)S(1)}, u32[]{:S(2)}, u32[]{:S(2)}) collective-permute-start(f32[64,128]{1,0:T(8,128)S(1)} %get-tuple-element.37), channel_id=1, source_target_pairs={{0,12},{4,0},{8,4},{12,8},{1,13},{5,1},{9,5},{13,9},{2,14},{6,2},{... | collective-permute-start | bytes 98312 | tf_op jit(solution)/shard_map/ppermute | solution.py:582
  39.4 3.8 %collective-permute-start.13 = (s16[272,128]{1,0:T(8,128)(2,1)S(1)}, s16[272,128]{1,0:T(8,128)(2,1)S(1)}, u32[]{:S(2)}, u32[]{:S(2)}) collective-permute-start(s16[272,128]{1,0:T(8,128)(2,1)S(1)} %get-tuple-element.44), channel_id=1, source_target_pairs={{0,4},{4,8},{8,12},{12,0},{1,5},{5,9},{9,13},{13,1},{2,6},{6,10},{... | collective-permute-start | bytes 208904 | tf_op jit(solution)/shard_map/ppermute | solution.py:582
  43.3 1.9 %collective-permute-done.9 = f32[64,128]{1,0:T(8,128)S(1)} collective-permute-done((f32[64,128]{1,0:T(8,128)S(1)}, f32[64,128]{1,0:T(8,128)S(1)}, u32[]{:S(2)}, u32[]{:S(2)}) %collective-permute-start.9) | collective-permute-done | bytes 32800 | tf_op jit(solution)/shard_map/ppermute | solution.py:582
  45.1 1.6 %collective-permute-start.11 = (f32[64,128]{1,0:T(8,128)S(1)}, f32[64,128]{1,0:T(8,128)S(1)}, u32[]{:S(2)}, u32[]{:S(2)}) collective-permute-start(f32[64,128]{1,0:T(8,128)S(1)} %add_add_fusion.refs_1_), channel_id=1, source_target_pairs={{0,2},{2,0},{1,3},{3,1},{4,6},{6,4},{5,7},{7,5},{8,10},{10,8},{9,1... | collective-permute-start | bytes 98312 | tf_op jit(solution)/shard_map/ppermute | solution.py:594
  46.7 2.4 %collective-permute-done.11.refs_2_.refs_3_ = f32[64,128]{1,0:T(8,128)S(1)} collective-permute-done((f32[64,128]{1,0:T(8,128)S(1)}, f32[64,128]{1,0:T(8,128)S(1)}, u32[]{:S(2)}, u32[]{:S(2)}) %collective-permute-start.11) | collective-permute-done | bytes 32800 | tf_op jit(solution)/shard_map/ppermute | solution.py:594
  51.0 1.0 %shard_map.68.refs_2_ = s16[32,2176]{1,0:T(8,128)(2,1)S(1)} custom-call(s32[6,9]{1,0:T(8,128)S(1)} %get-tuple-element.29.after.refs_0_, f32[64,128]{1,0:T(8,128)S(1)} %get-tuple-element.41.refs_1_.refs_0_, f32[32,2048]{1,0:T(8,128)S(1)} %get-tuple-element.42.refs_2_, bf16[8,256,128]{2,1,0:T(8,128)(2,1)S(1)} %get-tuple-element.38.refs_4_.refs_3_.refs_6_, ...), custom_call_target="tpu_custom_call" | custom-call | tf_op jit(solution)/shard_map/pallas_call | solution.py:70
  52.0 1.6 %collective-permute-start.18 = (s16[32,2176]{1,0:T(8,128)(2,1)S(1)}, s16[32,2176]{1,0:T(8,128)(2,1)S(1)}, u32[]{:S(2)}, u32[]{:S(2)}) collective-permute-start(s16[32,2176]{1,0:T(8,128)(2,1)S(1)} %shard_map.68.refs_2_), channel_id=1, source_target_pairs={{0,2},{2,0},{1,3},{3,1},{4,6},{6,4},{5,7},{7,5},{8,10},{10,8},{9,1... | collective-permute-start | bytes 417800 | tf_op jit(solution)/shard_map/ppermute | solution.py:594
  53.6 4.2 %collective-permute-done.18.refs_3_ = s16[32,2176]{1,0:T(8,128)(2,1)S(1)} collective-permute-done((s16[32,2176]{1,0:T(8,128)(2,1)S(1)}, s16[32,2176]{1,0:T(8,128)(2,1)S(1)}, u32[]{:S(2)}, u32[]{:S(2)}) %collective-permute-start.18) | collective-permute-done | bytes 139296 | tf_op jit(solution)/shard_map/ppermute | solution.py:594
  59.1 1.2 %collective-permute-start.21 = (s16[144,128]{1,0:T(8,128)(2,1)S(1)}, s16[144,128]{1,0:T(8,128)(2,1)S(1)}, u32[]{:S(2)}, u32[]{:S(2)}) collective-permute-start(s16[144,128]{1,0:T(8,128)(2,1)S(1)} %get-tuple-element.51), channel_id=1, source_target_pairs={{0,4},{4,8},{8,12},{12,0},{1,5},{5,9},{9,13},{13,1},{2,6},{6,10},{... | collective-permute-start | bytes 110600 | tf_op jit(solution)/shard_map/ppermute | solution.py:582
  60.3 2.6 %collective-permute-start.22 = (s16[144,128]{1,0:T(8,128)(2,1)S(1)}, s16[144,128]{1,0:T(8,128)(2,1)S(1)}, u32[]{:S(2)}, u32[]{:S(2)}) collective-permute-start(s16[144,128]{1,0:T(8,128)(2,1)S(1)} %get-tuple-element.52), channel_id=1, source_target_pairs={{0,12},{4,0},{8,4},{12,8},{1,13},{5,1},{9,5},{13,9},{2,14},{6,2},{... | collective-permute-start | bytes 110600 | tf_op jit(solution)/shard_map/ppermute | solution.py:582
  63.4 0.9 %collective-permute-done.20.refs_13_ = s16[144,128]{1,0:T(8,128)(2,1)S(1)} collective-permute-done((s16[144,128]{1,0:T(8,128)(2,1)S(1)}, s16[144,128]{1,0:T(8,128)(2,1)S(1)}, u32[]{:S(2)}, u32[]{:S(2)}) %collective-permute-start.20) | collective-permute-done | bytes 36896 | tf_op jit(solution)/shard_map/ppermute | solution.py:582
  65.0 1.0 %shard_map.71.total = f32[32,2048]{1,0:T(8,128)S(1)} custom-call(s32[6,9]{1,0:T(8,128)S(1)} %get-tuple-element.29.after.refs_0_, f32[64,128]{1,0:T(8,128)S(1)} %get-tuple-element.41.refs_1_.refs_0_, f32[32,128]{1,0:T(8,128)S(1)} %shard_map.70.refs_2_, f32[32,2048]{1,0:T(8,128)S(1)} %get-tuple-element.49.refs_0_.refs_3_, ...), custom_call_target="tpu_custom_call" | custom-call | tf_op jit(solution)/shard_map/pallas_call | solution.py:70
  66.0 1.1 %collective-permute-done.23 = f32[32,128]{1,0:T(8,128)S(1)} collective-permute-done((f32[32,128]{1,0:T(8,128)S(1)}, f32[32,128]{1,0:T(8,128)S(1)}, u32[]{:S(2)}, u32[]{:S(2)}) %collective-permute-start.23) | collective-permute-done | bytes 16416 | tf_op jit(solution)/shard_map/ppermute | solution.py:594
  67.3 1.6 %collective-permute-start.24 = (s16[32,2176]{1,0:T(8,128)(2,1)S(1)}, s16[32,2176]{1,0:T(8,128)(2,1)S(1)}, u32[]{:S(2)}, u32[]{:S(2)}) collective-permute-start(s16[32,2176]{1,0:T(8,128)(2,1)S(1)} %shard_map.72.refs_1_), channel_id=1, source_target_pairs={{0,2},{2,0},{1,3},{3,1},{4,6},{6,4},{5,7},{7,5},{8,10},{10,8},{9,1... | collective-permute-start | bytes 417800 | tf_op jit(solution)/shard_map/ppermute | solution.py:594
  69.5 4.0 %collective-permute-done.25.refs_3_.refs_1_ = f32[32,128]{1,0:T(8,128)S(1)} collective-permute-done((f32[32,128]{1,0:T(8,128)S(1)}, f32[32,128]{1,0:T(8,128)S(1)}, u32[]{:S(2)}, u32[]{:S(2)}) %collective-permute-start.25) | collective-permute-done | bytes 16416 | tf_op jit(solution)/shard_map/ppermute | solution.py:594
  73.6 1.7 %shard_map.74.refs_0_ = f32[64,64]{1,0:T(8,128)S(1)} custom-call(f32[32,2048]{1,0:T(8,128)S(1)} %shard_map.73.after.refs_1_, f32[32,128]{1,0:T(8,128)S(1)} %add.20.after.refs_0_, f32[32,128]{1,0:T(8,128)S(1)} %collective-permute-done.25.refs_3_.refs_1_), custom_call_target="tpu_custom_call" | custom-call | tf_op jit(solution)/shard_map/pallas_call | solution.py:70
  76.9 2.4 %collective-permute-start.28 = (f32[32,128]{1,0:T(8,128)S(1)}, f32[32,128]{1,0:T(8,128)S(1)}, u32[]{:S(2)}, u32[]{:S(2)}) collective-permute-start(f32[32,128]{1,0:T(8,128)S(1)} %get-tuple-element.54.refs_1_), channel_id=1, source_target_pairs={{0,4},{4,8},{8,12},{12,0},{1,5},{5,9},{9,13},{13,1},{2,6},{6,10},{... | collective-permute-start | bytes 49160 | tf_op jit(solution)/shard_map/ppermute | solution.py:582
  79.3 1.4 %collective-permute-start.29 = (f32[32,128]{1,0:T(8,128)S(1)}, f32[32,128]{1,0:T(8,128)S(1)}, u32[]{:S(2)}, u32[]{:S(2)}) collective-permute-start(f32[32,128]{1,0:T(8,128)S(1)} %get-tuple-element.54.refs_1_), channel_id=1, source_target_pairs={{0,12},{4,0},{8,4},{12,8},{1,13},{5,1},{9,5},{13,9},{2,14},{6,2},{... | collective-permute-start | bytes 49160 | tf_op jit(solution)/shard_map/ppermute | solution.py:582
  81.3 1.1 %collective-permute-done.28.refs_3_ = f32[32,128]{1,0:T(8,128)S(1)} collective-permute-done((f32[32,128]{1,0:T(8,128)S(1)}, f32[32,128]{1,0:T(8,128)S(1)}, u32[]{:S(2)}, u32[]{:S(2)}) %collective-permute-start.28) | collective-permute-done | bytes 16416 | tf_op jit(solution)/shard_map/ppermute | solution.py:582
  83.1 2.6 %shard_map.76 = f32[32,2048]{1,0:T(8,128)} custom-call(bf16[128,2048]{1,0:T(8,128)(2,1)S(1)} %get-tuple-element.53.refs_0_, f32[32,128]{1,0:T(8,128)S(1)} %get-tuple-element.54.refs_1_, f32[32,128]{1,0:T(8,128)S(1)} %collective-permute-done.27.refs_2_, f32[32,128]{1,0:T(8,128)S(1)} %collective-permute-done.28.refs_3_, ...), custom_call_target="tpu_custom_call" | custom-call | tf_op jit(solution)/shard_map/pallas_call | solution.py:70
  (54 shorter events, 12.1 us)
Async XLA Ops:
  2.0 7.9 %collective-permute-start = (s32[3,8]{1,0:T(4,128)S(1)}, s32[3,8]{1,0:T(4,128)S(1)}, u32[]{:S(2)}, u32[]{:S(2)}) collective-permute-start(s32[3,8]{1,0:T(4,128)S(1)} %concatenate.3.refs_0_), channel_id=1, source_target_pairs={{0,4},{4,8},{8,12},{12,0},{1,5},{5,9},{9,13},{13,1},{2,6},{6,10},{... | collective-permute-start | bytes 296 | tf_op jit(solution)/shard_map/ppermute | solution.py:582
  5.0 4.9 %collective-permute-start.1 = (s32[3,8]{1,0:T(4,128)S(1)}, s32[3,8]{1,0:T(4,128)S(1)}, u32[]{:S(2)}, u32[]{:S(2)}) collective-permute-start(s32[3,8]{1,0:T(4,128)S(1)} %concatenate.3.refs_0_), channel_id=1, source_target_pairs={{0,12},{4,0},{8,4},{12,8},{1,13},{5,1},{9,5},{13,9},{2,14},{6,2},{... | collective-permute-start | bytes 296 | tf_op jit(solution)/shard_map/ppermute | solution.py:582
  7.0 4.5 %collective-permute-start.2 = (s32[3,8]{1,0:T(4,128)S(1)}, s32[3,8]{1,0:T(4,128)S(1)}, u32[]{:S(2)}, u32[]{:S(2)}) collective-permute-start(s32[3,8]{1,0:T(4,128)S(1)} %concatenate.3.refs_0_), channel_id=1, source_target_pairs={{0,8},{4,12},{8,0},{12,4},{1,9},{5,13},{9,1},{13,5},{2,10},{6,14},... | collective-permute-start | bytes 296 | tf_op jit(solution)/shard_map/ppermute | solution.py:582
  8.0 1.4 %copy-start = (bf16[2048,384]{1,0:T(8,128)(2,1)S(1)}, bf16[2048,384]{1,0:T(8,128)(2,1)}, u32[]{:S(2)}) copy-start(bf16[2048,384]{1,0:T(8,128)(2,1)} %refs_1_.1) | copy-start | bytes 4718596
  13.1 14.9 %collective-permute-start.3 = (bf16[256,384]{1,0:T(8,128)(2,1)S(1)}, bf16[256,384]{1,0:T(8,128)(2,1)S(1)}, u32[]{:S(2)}, u32[]{:S(2)}) collective-permute-start(bf16[256,384]{1,0:T(8,128)(2,1)S(1)} %get-tuple-element.30), channel_id=1, source_target_pairs={{0,8},{4,12},{8,0},{12,4},{1,9},{5,13},{9,1},{13,5},{2,10},{6,14},... | collective-permute-start | bytes 589832 | tf_op jit(solution)/shard_map/ppermute | solution.py:582
  14.2 13.8 %collective-permute-start.4 = (bf16[256,384]{1,0:T(8,128)(2,1)S(1)}, bf16[256,384]{1,0:T(8,128)(2,1)S(1)}, u32[]{:S(2)}, u32[]{:S(2)}) collective-permute-start(bf16[256,384]{1,0:T(8,128)(2,1)S(1)} %get-tuple-element.31), channel_id=1, source_target_pairs={{0,12},{4,0},{8,4},{12,8},{1,13},{5,1},{9,5},{13,9},{2,14},{6,2},{... | collective-permute-start | bytes 589832 | tf_op jit(solution)/shard_map/ppermute | solution.py:582
  15.5 12.5 %collective-permute-start.5 = (bf16[256,384]{1,0:T(8,128)(2,1)S(1)}, bf16[256,384]{1,0:T(8,128)(2,1)S(1)}, u32[]{:S(2)}, u32[]{:S(2)}) collective-permute-start(bf16[256,384]{1,0:T(8,128)(2,1)S(1)} %get-tuple-element.32), channel_id=1, source_target_pairs={{0,4},{4,8},{8,12},{12,0},{1,5},{5,9},{9,13},{13,1},{2,6},{6,10},{... | collective-permute-start | bytes 589832 | tf_op jit(solution)/shard_map/ppermute | solution.py:582
  16.2 13.1 %collective-permute-start.7 = (f32[1024,128]{1,0:T(8,128)S(1)}, f32[1024,128]{1,0:T(8,128)S(1)}, u32[]{:S(2)}, u32[]{:S(2)}) collective-permute-start(f32[1024,128]{1,0:T(8,128)S(1)} %shard_map.59.refs_5_.mine), channel_id=1, source_target_pairs={{0,1},{1,0},{2,3},{3,2},{4,5},{5,4},{6,7},{7,6},{8,9},{9,8},{10,11... | collective-permute-start | bytes 1572872 | tf_op jit(solution)/shard_map/ppermute | solution.py:582
  16.5 12.6 %copy-start.1 = (f32[2048,32]{0,1:T(8,128)S(1)}, f32[2048,32]{0,1:T(8,128)}, u32[]{:S(2)}) copy-start(f32[2048,32]{0,1:T(8,128)} %param.5) | copy-start | bytes 786436
  29.1 2.0 %collective-permute-start.6 = (f32[1024,128]{1,0:T(8,128)S(1)}, f32[1024,128]{1,0:T(8,128)S(1)}, u32[]{:S(2)}, u32[]{:S(2)}) collective-permute-start(f32[1024,128]{1,0:T(8,128)S(1)} %shard_map.62.refs_1_), channel_id=1, source_target_pairs={{0,1},{1,0},{2,3},{3,2},{4,5},{5,4},{6,7},{7,6},{8,9},{9,8},{10,11... | collective-permute-start | bytes 1572872 | tf_op jit(solution)/shard_map/ppermute | solution.py:582
  31.9 11.3 %collective-permute-start.10 = (f32[64,128]{1,0:T(8,128)S(1)}, f32[64,128]{1,0:T(8,128)S(1)}, u32[]{:S(2)}, u32[]{:S(2)}) collective-permute-start(f32[64,128]{1,0:T(8,128)S(1)} %get-tuple-element.37), channel_id=1, source_target_pairs={{0,8},{4,12},{8,0},{12,4},{1,9},{5,13},{9,1},{13,5},{2,10},{6,14},... | collective-permute-start | bytes 98312 | tf_op jit(solution)/shard_map/ppermute | solution.py:582
  36.7 6.5 %collective-permute-start.8 = (f32[64,128]{1,0:T(8,128)S(1)}, f32[64,128]{1,0:T(8,128)S(1)}, u32[]{:S(2)}, u32[]{:S(2)}) collective-permute-start(f32[64,128]{1,0:T(8,128)S(1)} %get-tuple-element.37), channel_id=1, source_target_pairs={{0,12},{4,0},{8,4},{12,8},{1,13},{5,1},{9,5},{13,9},{2,14},{6,2},{... | collective-permute-start | bytes 98312 | tf_op jit(solution)/shard_map/ppermute | solution.py:582
  38.9 6.3 %collective-permute-start.9 = (f32[64,128]{1,0:T(8,128)S(1)}, f32[64,128]{1,0:T(8,128)S(1)}, u32[]{:S(2)}, u32[]{:S(2)}) collective-permute-start(f32[64,128]{1,0:T(8,128)S(1)} %get-tuple-element.37), channel_id=1, source_target_pairs={{0,4},{4,8},{8,12},{12,0},{1,5},{5,9},{9,13},{13,1},{2,6},{6,10},{... | collective-permute-start | bytes 98312 | tf_op jit(solution)/shard_map/ppermute | solution.py:582
  38.9 10.3 %collective-permute-start.12 = (s16[272,128]{1,0:T(8,128)(2,1)S(1)}, s16[272,128]{1,0:T(8,128)(2,1)S(1)}, u32[]{:S(2)}, u32[]{:S(2)}) collective-permute-start(s16[272,128]{1,0:T(8,128)(2,1)S(1)} %get-tuple-element.43), channel_id=1, source_target_pairs={{0,8},{4,12},{8,0},{12,4},{1,9},{5,13},{9,1},{13,5},{2,10},{6,14},... | collective-permute-start | bytes 208904 | tf_op jit(solution)/shard_map/ppermute | solution.py:582
  39.4 9.7 %collective-permute-start.13 = (s16[272,128]{1,0:T(8,128)(2,1)S(1)}, s16[272,128]{1,0:T(8,128)(2,1)S(1)}, u32[]{:S(2)}, u32[]{:S(2)}) collective-permute-start(s16[272,128]{1,0:T(8,128)(2,1)S(1)} %get-tuple-element.44), channel_id=1, source_target_pairs={{0,4},{4,8},{8,12},{12,0},{1,5},{5,9},{9,13},{13,1},{2,6},{6,10},{... | collective-permute-start | bytes 208904 | tf_op jit(solution)/shard_map/ppermute | solution.py:582
  43.3 5.9 %collective-permute-start.14 = (s16[272,128]{1,0:T(8,128)(2,1)S(1)}, s16[272,128]{1,0:T(8,128)(2,1)S(1)}, u32[]{:S(2)}, u32[]{:S(2)}) collective-permute-start(s16[272,128]{1,0:T(8,128)(2,1)S(1)} %get-tuple-element.45), channel_id=1, source_target_pairs={{0,12},{4,0},{8,4},{12,8},{1,13},{5,1},{9,5},{13,9},{2,14},{6,2},{... | collective-permute-start | bytes 208904 | tf_op jit(solution)/shard_map/ppermute | solution.py:582
  45.1 4.0 %collective-permute-start.11 = (f32[64,128]{1,0:T(8,128)S(1)}, f32[64,128]{1,0:T(8,128)S(1)}, u32[]{:S(2)}, u32[]{:S(2)}) collective-permute-start(f32[64,128]{1,0:T(8,128)S(1)} %add_add_fusion.refs_1_), channel_id=1, source_target_pairs={{0,2},{2,0},{1,3},{3,1},{4,6},{6,4},{5,7},{7,5},{8,10},{10,8},{9,1... | collective-permute-start | bytes 98312 | tf_op jit(solution)/shard_map/ppermute | solution.py:594
  49.2 1.5 %collective-permute-start.15 = (bf16[1,256,128]{2,1,0:T(8,128)(2,1)S(1)}, bf16[1,256,128]{2,1,0:T(8,128)(2,1)S(1)}, u32[]{:S(2)}, u32[]{:S(2)}) collective-permute-start(bf16[1,256,128]{2,1,0:T(8,128)(2,1)S(1)} %get-tuple-element.46.refs_4_.refs_7_), channel_id=1, source_target_pairs={{0,1},{1,0},{2,3},{3,2},{4,5},{5,4},{6,7},{7,6},{8,9},{9,8},{10,11... | collective-permute-start | bytes 196616 | tf_op jit(solution)/shard_map/ppermute | solution.py:582
  49.3 1.4 %collective-permute-start.16 = (bf16[1,256,128]{2,1,0:T(8,128)(2,1)S(1)}, bf16[1,256,128]{2,1,0:T(8,128)(2,1)S(1)}, u32[]{:S(2)}, u32[]{:S(2)}) collective-permute-start(bf16[1,256,128]{2,1,0:T(8,128)(2,1)S(1)} %get-tuple-element.47.refs_5_.refs_8_), channel_id=1, source_target_pairs={{0,1},{1,0},{2,3},{3,2},{4,5},{5,4},{6,7},{7,6},{8,9},{9,8},{10,11... | collective-permute-start | bytes 196616 | tf_op jit(solution)/shard_map/ppermute | solution.py:582
  49.8 1.3 %collective-permute-start.17 = (bf16[1,256,128]{2,1,0:T(8,128)(2,1)S(1)}, bf16[1,256,128]{2,1,0:T(8,128)(2,1)S(1)}, u32[]{:S(2)}, u32[]{:S(2)}) collective-permute-start(bf16[1,256,128]{2,1,0:T(8,128)(2,1)S(1)} %get-tuple-element.48.refs_6_.refs_9_), channel_id=1, source_target_pairs={{0,1},{1,0},{2,3},{3,2},{4,5},{5,4},{6,7},{7,6},{8,9},{9,8},{10,11... | collective-permute-start | bytes 196616 | tf_op jit(solution)/shard_map/ppermute | solution.py:582
  52.0 5.8 %collective-permute-start.18 = (s16[32,2176]{1,0:T(8,128)(2,1)S(1)}, s16[32,2176]{1,0:T(8,128)(2,1)S(1)}, u32[]{:S(2)}, u32[]{:S(2)}) collective-permute-start(s16[32,2176]{1,0:T(8,128)(2,1)S(1)} %shard_map.68.refs_2_), channel_id=1, source_target_pairs={{0,2},{2,0},{1,3},{3,1},{4,6},{6,4},{5,7},{7,5},{8,10},{10,8},{9,1... | collective-permute-start | bytes 417800 | tf_op jit(solution)/shard_map/ppermute | solution.py:594
  58.5 4.4 %collective-permute-start.19 = (f32[32,2048]{1,0:T(8,128)S(1)}, f32[32,2048]{1,0:T(8,128)S(1)}, u32[]{:S(2)}, u32[]{:S(2)}) collective-permute-start(f32[32,2048]{1,0:T(8,128)S(1)} %get-tuple-element.49.refs_0_.refs_3_), channel_id=1, source_target_pairs={{0,1},{1,0},{2,3},{3,2},{4,5},{5,4},{6,7},{7,6},{8,9},{9,8},{10,11... | collective-permute-start | bytes 786440 | tf_op jit(solution)/shard_map/ppermute | solution.py:582
  58.6 5.7 %collective-permute-start.20 = (s16[144,128]{1,0:T(8,128)(2,1)S(1)}, s16[144,128]{1,0:T(8,128)(2,1)S(1)}, u32[]{:S(2)}, u32[]{:S(2)}) collective-permute-start(s16[144,128]{1,0:T(8,128)(2,1)S(1)} %get-tuple-element.50), channel_id=1, source_target_pairs={{0,8},{4,12},{8,0},{12,4},{1,9},{5,13},{9,1},{13,5},{2,10},{6,14},... | collective-permute-start | bytes 110600 | tf_op jit(solution)/shard_map/ppermute | solution.py:582
  59.1 5.8 %collective-permute-start.21 = (s16[144,128]{1,0:T(8,128)(2,1)S(1)}, s16[144,128]{1,0:T(8,128)(2,1)S(1)}, u32[]{:S(2)}, u32[]{:S(2)}) collective-permute-start(s16[144,128]{1,0:T(8,128)(2,1)S(1)} %get-tuple-element.51), channel_id=1, source_target_pairs={{0,4},{4,8},{8,12},{12,0},{1,5},{5,9},{9,13},{13,1},{2,6},{6,10},{... | collective-permute-start | bytes 110600 | tf_op jit(solution)/shard_map/ppermute | solution.py:582
  60.3 4.7 %collective-permute-start.22 = (s16[144,128]{1,0:T(8,128)(2,1)S(1)}, s16[144,128]{1,0:T(8,128)(2,1)S(1)}, u32[]{:S(2)}, u32[]{:S(2)}) collective-permute-start(s16[144,128]{1,0:T(8,128)(2,1)S(1)} %get-tuple-element.52), channel_id=1, source_target_pairs={{0,12},{4,0},{8,4},{12,8},{1,13},{5,1},{9,5},{13,9},{2,14},{6,2},{... | collective-permute-start | bytes 110600 | tf_op jit(solution)/shard_map/ppermute | solution.py:582
  63.4 3.8 %collective-permute-start.23 = (f32[32,128]{1,0:T(8,128)S(1)}, f32[32,128]{1,0:T(8,128)S(1)}, u32[]{:S(2)}, u32[]{:S(2)}) collective-permute-start(f32[32,128]{1,0:T(8,128)S(1)} %shard_map.70.refs_2_), channel_id=1, source_target_pairs={{0,4},{4,0},{8,12},{12,8},{1,5},{5,1},{9,13},{13,9},{2,6},{6,2},{1... | collective-permute-start | bytes 49160 | tf_op jit(solution)/shard_map/ppermute | solution.py:594
  67.3 6.2 %collective-permute-start.24 = (s16[32,2176]{1,0:T(8,128)(2,1)S(1)}, s16[32,2176]{1,0:T(8,128)(2,1)S(1)}, u32[]{:S(2)}, u32[]{:S(2)}) collective-permute-start(s16[32,2176]{1,0:T(8,128)(2,1)S(1)} %shard_map.72.refs_1_), channel_id=1, source_target_pairs={{0,2},{2,0},{1,3},{3,1},{4,6},{6,4},{5,7},{7,5},{8,10},{10,8},{9,1... | collective-permute-start | bytes 417800 | tf_op jit(solution)/shard_map/ppermute | solution.py:594
  68.8 4.6 %collective-permute-start.25 = (f32[32,128]{1,0:T(8,128)S(1)}, f32[32,128]{1,0:T(8,128)S(1)}, u32[]{:S(2)}, u32[]{:S(2)}) collective-permute-start(f32[32,128]{1,0:T(8,128)S(1)} %add.20.after.refs_0_), channel_id=1, source_target_pairs={{0,8},{4,12},{8,0},{12,4},{1,9},{5,13},{9,1},{13,5},{2,10},{6,14},... | collective-permute-start | bytes 49160 | tf_op jit(solution)/shard_map/ppermute | solution.py:594
  73.6 1.8 %collective-permute-start.26 = (f32[32,2048]{1,0:T(8,128)S(1)}, f32[32,2048]{1,0:T(8,128)S(1)}, u32[]{:S(2)}, u32[]{:S(2)}) collective-permute-start(f32[32,2048]{1,0:T(8,128)S(1)} %shard_map.73.after.refs_1_), channel_id=1, source_target_pairs={{0,1},{1,0},{2,3},{3,2},{4,5},{5,4},{6,7},{7,6},{8,9},{9,8},{10,11... | collective-permute-start | bytes 786440 | tf_op jit(solution)/shard_map/ppermute | solution.py:582
  76.2 5.1 %collective-permute-start.27 = (f32[32,128]{1,0:T(8,128)S(1)}, f32[32,128]{1,0:T(8,128)S(1)}, u32[]{:S(2)}, u32[]{:S(2)}) collective-permute-start(f32[32,128]{1,0:T(8,128)S(1)} %get-tuple-element.54.refs_1_), channel_id=1, source_target_pairs={{0,8},{4,12},{8,0},{12,4},{1,9},{5,13},{9,1},{13,5},{2,10},{6,14},... | collective-permute-start | bytes 49160 | tf_op jit(solution)/shard_map/ppermute | solution.py:582
  76.9 5.5 %collective-permute-start.28 = (f32[32,128]{1,0:T(8,128)S(1)}, f32[32,128]{1,0:T(8,128)S(1)}, u32[]{:S(2)}, u32[]{:S(2)}) collective-permute-start(f32[32,128]{1,0:T(8,128)S(1)} %get-tuple-element.54.refs_1_), channel_id=1, source_target_pairs={{0,4},{4,8},{8,12},{12,0},{1,5},{5,9},{9,13},{13,1},{2,6},{6,10},{... | collective-permute-start | bytes 49160 | tf_op jit(solution)/shard_map/ppermute | solution.py:582
  79.3 3.7 %collective-permute-start.29 = (f32[32,128]{1,0:T(8,128)S(1)}, f32[32,128]{1,0:T(8,128)S(1)}, u32[]{:S(2)}, u32[]{:S(2)}) collective-permute-start(f32[32,128]{1,0:T(8,128)S(1)} %get-tuple-element.54.refs_1_), channel_id=1, source_target_pairs={{0,12},{4,0},{8,4},{12,8},{1,13},{5,1},{9,5},{13,9},{2,14},{6,2},{... | collective-permute-start | bytes 49160 | tf_op jit(solution)/shard_map/ppermute | solution.py:582

commit v19 on v17

--- a/solution.py
+++ b/solution.py
@@ -174,34 +174,41 @@
     return both[m:] + both[:m]
 
 
-def lower_inverse(matrix, step=8):
+def lower_inverse(matrix):
     n = matrix.shape[0]
+    step = 8
     state = jnp.concatenate([matrix, eye_mask(n).astype(F32)], axis=1)
+    tiles = [state[i : i + step] for i in range(0, n, step)]
+    shape = tiles[0].shape
+    rows = lax.broadcasted_iota(jnp.int32, shape, 0)
     done = []
     for j in range(0, n, step):
-        top = j // 8 * 8
-        if top > n - state.shape[0]:
-            done.append(state[:8])
-            state = state[8:]
-        base = j - top
-        rows = lax.broadcasted_iota(jnp.int32, state.shape, 0)
-        columns = [jnp.broadcast_to(state[:, j + i : j + i + 1], state.shape) for i in range(step)]
-        lines = [state[base + i : base + i + 1, :] for i in range(step)]
-        pivot = [[columns[k][base + i : base + i + 1, :] for k in range(step)] for i in range(step)]
+        columns = [
+            [jnp.broadcast_to(tile[:, j + i : j + i + 1], shape) for tile in tiles] for i in range(step)
+        ]
+        lines = [jnp.broadcast_to(tiles[0][i : i + 1, :], shape) for i in range(step)]
+        pivot = {
+            (i, k): jnp.broadcast_to(columns[k][0][i : i + 1, :], shape)
+            for i in range(step)
+            for k in range(i, step)
+        }
         for i in range(step):
             if i % 2 == 0:
-                first, cross, second = pivot[i][i], pivot[i][i + 1], pivot[i + 1][i + 1]
+                first, cross, second = pivot[i, i], pivot[i, i + 1], pivot[i + 1, i + 1]
                 reciprocals = (1.0 / first, first / (first * second - cross * cross))
             reciprocal = reciprocals[i % 2]
             scaled = lines[i] * reciprocal
-            ratio = [pivot[i][k] * reciprocal for k in range(step)]
+            ratio = {k: pivot[i, k] * reciprocal for k in range(i + 1, step)}
             for k in range(i + 1, step):
-                lines[k] = lines[k] - pivot[k][i] * scaled
-                columns[k] = columns[k] - columns[i] * ratio[k]
-                for m in range(i + 1, step):
-                    pivot[k][m] = pivot[k][m] - pivot[k][i] * ratio[m]
-            state = state - jnp.where(rows > base + i, columns[i], 0.0) * scaled
-    state = jnp.concatenate([*done, state], axis=0)
+                lines[k] = lines[k] - pivot[i, k] * scaled
+                columns[k] = [one - other * ratio[k] for one, other in zip(columns[k], columns[i])]
+                for m in range(k, step):
+                    pivot[k, m] = pivot[k, m] - pivot[i, k] * ratio[m]
+            left = [jnp.where(rows > i, columns[i][0], 0.0), *columns[i][1:]]
+            tiles = [tile - one * scaled for tile, one in zip(tiles, left)]
+        done.append(tiles[0])
+        tiles = tiles[1:]
+    state = jnp.concatenate(done, axis=0)
     pivots = jnp.sum(jnp.where(eye_mask(n), state[:, :n], 0.0), axis=1, keepdims=True)
     return state[:, n:] / jnp.sqrt(pivots)
 

time: 84.2 us -> 84.8 us (level)
  transfers between devices with their start and end apart: 30 -> 30, of which waited for: 13 -> 13; matrix products, arithmetic and copies ran while one was open for 1% -> 1% of each run, Pallas kernels for 7% -> 8%
where the time goes in v19:
time: 84.8 us; the launch traced here: 84.6 us
  starting transfers between devices  36 us (42%)
  waiting for transfers between devices  29.7 us (35%)
  Pallas kernels  14.6 us (17%)
  local copies, waits for them, and re-layouts  2.7 us (3%)
  between operations  1.5 us (2%)
    ppermute x25, starting transfers between devices, shift_by(): lax.ppermute(value, axes, [(i, (i + shift) % size) for i in range(size)])  29.2 us
    ppermute x25, waiting for transfers between devices, shift_by(): lax.ppermute(value, axes, [(i, (i + shift) % size) for i in range(size)])  19.6 us
    pallas_call x18, Pallas kernels, call(): pl.pallas_call(body, out_shape=shapes, in_specs=[ANY if i in any_in else...  14.6 us
    ppermute x5, waiting for transfers between devices, pair_step(): lax.ppermute(value, name, [(i, i ^ flip) for i in range(lax.axis_size(nam...  10 us
    ppermute x5, starting transfers between devices, pair_step(): lax.ppermute(value, name, [(i, i ^ flip) for i in range(lax.axis_size(nam...  6.78 us
  transfers between devices with their start and end apart: 30, of which 13 were waited for; matrix products, arithmetic and copies ran while one was open for 1% of the time, Pallas kernels for 8%

profile of v19, /device:TPU:0, one launch (start us, length us, event | category | flops | bytes accessed | tf_op | source)
XLA Modules:
  0.0 84.6 jit_solution(14349648175837211822)
XLA Ops:
  2.0 3.0 %collective-permute-start = (s32[3,8]{1,0:T(4,128)S(1)}, s32[3,8]{1,0:T(4,128)S(1)}, u32[]{:S(2)}, u32[]{:S(2)}) collective-permute-start(s32[3,8]{1,0:T(4,128)S(1)} %concatenate.3.refs_0_), channel_id=1, source_target_pairs={{0,4},{4,8},{8,12},{12,0},{1,5},{5,9},{9,13},{13,1},{2,6},{6,10},{... | collective-permute-start | bytes 296 | tf_op jit(solution)/shard_map/ppermute | solution.py:587
  5.0 2.0 %collective-permute-start.1 = (s32[3,8]{1,0:T(4,128)S(1)}, s32[3,8]{1,0:T(4,128)S(1)}, u32[]{:S(2)}, u32[]{:S(2)}) collective-permute-start(s32[3,8]{1,0:T(4,128)S(1)} %concatenate.3.refs_0_), channel_id=1, source_target_pairs={{0,12},{4,0},{8,4},{12,8},{1,13},{5,1},{9,5},{13,9},{2,14},{6,2},{... | collective-permute-start | bytes 296 | tf_op jit(solution)/shard_map/ppermute | solution.py:587
  7.0 1.0 %collective-permute-start.2 = (s32[3,8]{1,0:T(4,128)S(1)}, s32[3,8]{1,0:T(4,128)S(1)}, u32[]{:S(2)}, u32[]{:S(2)}) collective-permute-start(s32[3,8]{1,0:T(4,128)S(1)} %concatenate.3.refs_0_), channel_id=1, source_target_pairs={{0,8},{4,12},{8,0},{12,4},{1,9},{5,13},{9,1},{13,5},{2,10},{6,14},... | collective-permute-start | bytes 296 | tf_op jit(solution)/shard_map/ppermute | solution.py:587
  8.0 1.4 %copy-done = bf16[2048,384]{1,0:T(8,128)(2,1)S(1)} copy-done((bf16[2048,384]{1,0:T(8,128)(2,1)S(1)}, bf16[2048,384]{1,0:T(8,128)(2,1)}, u32[]{:S(2)}) %copy-start) | copy-done | bytes 1572888
  9.9 1.6 %collective-permute-done.2.refs_3_ = s32[3,8]{1,0:T(4,128)S(1)} collective-permute-done((s32[3,8]{1,0:T(4,128)S(1)}, s32[3,8]{1,0:T(4,128)S(1)}, u32[]{:S(2)}, u32[]{:S(2)}) %collective-permute-start.2) | collective-permute-done | bytes 128 | tf_op jit(solution)/shard_map/ppermute | solution.py:587
  11.5 1.6 %shard_map.60 = (s32[6,9]{1,0:T(8,128)S(1)}, bf16[256,384]{1,0:T(8,128)(2,1)S(1)}, bf16[256,384]{1,0:T(8,128)(2,1)S(1)}, bf16[256,384]{1,0:T(8,128)(2,1)S(1)}) custom-call(s32[3,8]{1,0:T(4,128)S(1)} %concatenate.3.refs_0_, s32[3,8]{1,0:T(4,128)S(1)} %collective-permute-done.refs_1_, s32[3,8]{1,0:T(4,128)S(1)} %collective-permute-done.1.refs_2_, ...), custom_call_target="tpu_custom_call" | custom-call | tf_op jit(solution)/shard_map/pallas_call | solution.py:70
  13.1 1.1 %collective-permute-start.3 = (bf16[256,384]{1,0:T(8,128)(2,1)S(1)}, bf16[256,384]{1,0:T(8,128)(2,1)S(1)}, u32[]{:S(2)}, u32[]{:S(2)}) collective-permute-start(bf16[256,384]{1,0:T(8,128)(2,1)S(1)} %get-tuple-element.30), channel_id=1, source_target_pairs={{0,8},{4,12},{8,0},{12,4},{1,9},{5,13},{9,1},{13,5},{2,10},{6,14},... | collective-permute-start | bytes 589832 | tf_op jit(solution)/shard_map/ppermute | solution.py:587
  14.2 1.4 %collective-permute-start.4 = (bf16[256,384]{1,0:T(8,128)(2,1)S(1)}, bf16[256,384]{1,0:T(8,128)(2,1)S(1)}, u32[]{:S(2)}, u32[]{:S(2)}) collective-permute-start(bf16[256,384]{1,0:T(8,128)(2,1)S(1)} %get-tuple-element.31), channel_id=1, source_target_pairs={{0,12},{4,0},{8,4},{12,8},{1,13},{5,1},{9,5},{13,9},{2,14},{6,2},{... | collective-permute-start | bytes 589832 | tf_op jit(solution)/shard_map/ppermute | solution.py:587
  16.5 11.4 %collective-permute-done.3.refs_3_ = bf16[256,384]{1,0:T(8,128)(2,1)S(1)} collective-permute-done((bf16[256,384]{1,0:T(8,128)(2,1)S(1)}, bf16[256,384]{1,0:T(8,128)(2,1)S(1)}, u32[]{:S(2)}, u32[]{:S(2)}) %collective-permute-start.3) | collective-permute-done | bytes 196640 | tf_op jit(solution)/shard_map/ppermute | solution.py:587
  28.0 1.1 %shard_map.62.refs_1_ = f32[1024,128]{1,0:T(8,128)S(1)} custom-call(s32[6,9]{1,0:T(8,128)S(1)} %get-tuple-element.29.after.refs_0_, bf16[2048,384]{1,0:T(8,128)(2,1)S(1)} %copy-done, f32[2048,128]{1,0:T(8,128)S(1)} %shard_map.61.refs_2_, bf16[256,384]{1,0:T(8,128)(2,1)S(1)} %collective-permute-done.3.refs_3_, ...), custom_call_target="tpu_custom_call" | custom-call | tf_op jit(solution)/shard_map/pallas_call | solution.py:70
  29.5 1.5 %collective-permute-done.6.refs_2_ = f32[1024,128]{1,0:T(8,128)S(1)} collective-permute-done((f32[1024,128]{1,0:T(8,128)S(1)}, f32[1024,128]{1,0:T(8,128)S(1)}, u32[]{:S(2)}, u32[]{:S(2)}) %collective-permute-start.6) | collective-permute-done | bytes 524320 | tf_op jit(solution)/shard_map/ppermute | solution.py:587
  31.9 2.2 %collective-permute-start.10 = (f32[64,128]{1,0:T(8,128)S(1)}, f32[64,128]{1,0:T(8,128)S(1)}, u32[]{:S(2)}, u32[]{:S(2)}) collective-permute-start(f32[64,128]{1,0:T(8,128)S(1)} %get-tuple-element.37), channel_id=1, source_target_pairs={{0,12},{4,0},{8,4},{12,8},{1,13},{5,1},{9,5},{13,9},{2,14},{6,2},{... | collective-permute-start | bytes 98312 | tf_op jit(solution)/shard_map/ppermute | solution.py:587
  34.1 2.4 %collective-permute-start.8 = (f32[64,128]{1,0:T(8,128)S(1)}, f32[64,128]{1,0:T(8,128)S(1)}, u32[]{:S(2)}, u32[]{:S(2)}) collective-permute-start(f32[64,128]{1,0:T(8,128)S(1)} %get-tuple-element.37), channel_id=1, source_target_pairs={{0,4},{4,8},{8,12},{12,0},{1,5},{5,9},{9,13},{13,1},{2,6},{6,10},{... | collective-permute-start | bytes 98312 | tf_op jit(solution)/shard_map/ppermute | solution.py:587
  36.6 2.2 %collective-permute-start.9 = (f32[64,128]{1,0:T(8,128)S(1)}, f32[64,128]{1,0:T(8,128)S(1)}, u32[]{:S(2)}, u32[]{:S(2)}) collective-permute-start(f32[64,128]{1,0:T(8,128)S(1)} %get-tuple-element.37), channel_id=1, source_target_pairs={{0,8},{4,12},{8,0},{12,4},{1,9},{5,13},{9,1},{13,5},{2,10},{6,14},... | collective-permute-start | bytes 98312 | tf_op jit(solution)/shard_map/ppermute | solution.py:587
  38.8 2.7 %collective-permute-start.13 = (s16[272,128]{1,0:T(8,128)(2,1)S(1)}, s16[272,128]{1,0:T(8,128)(2,1)S(1)}, u32[]{:S(2)}, u32[]{:S(2)}) collective-permute-start(s16[272,128]{1,0:T(8,128)(2,1)S(1)} %get-tuple-element.44), channel_id=1, source_target_pairs={{0,8},{4,12},{8,0},{12,4},{1,9},{5,13},{9,1},{13,5},{2,10},{6,14},... | collective-permute-start | bytes 208904 | tf_op jit(solution)/shard_map/ppermute | solution.py:587
  41.5 1.1 %collective-permute-start.14 = (s16[272,128]{1,0:T(8,128)(2,1)S(1)}, s16[272,128]{1,0:T(8,128)(2,1)S(1)}, u32[]{:S(2)}, u32[]{:S(2)}) collective-permute-start(s16[272,128]{1,0:T(8,128)(2,1)S(1)} %get-tuple-element.45), channel_id=1, source_target_pairs={{0,12},{4,0},{8,4},{12,8},{1,13},{5,1},{9,5},{13,9},{2,14},{6,2},{... | collective-permute-start | bytes 208904 | tf_op jit(solution)/shard_map/ppermute | solution.py:587
  42.6 1.6 %collective-permute-start.11 = (f32[64,128]{1,0:T(8,128)S(1)}, f32[64,128]{1,0:T(8,128)S(1)}, u32[]{:S(2)}, u32[]{:S(2)}) collective-permute-start(f32[64,128]{1,0:T(8,128)S(1)} %add_add_fusion.refs_1_), channel_id=1, source_target_pairs={{0,2},{2,0},{1,3},{3,1},{4,6},{6,4},{5,7},{7,5},{8,10},{10,8},{9,1... | collective-permute-start | bytes 98312 | tf_op jit(solution)/shard_map/ppermute | solution.py:595
  44.2 2.4 %collective-permute-done.11.refs_2_.refs_3_ = f32[64,128]{1,0:T(8,128)S(1)} collective-permute-done((f32[64,128]{1,0:T(8,128)S(1)}, f32[64,128]{1,0:T(8,128)S(1)}, u32[]{:S(2)}, u32[]{:S(2)}) %collective-permute-start.11) | collective-permute-done | bytes 32800 | tf_op jit(solution)/shard_map/ppermute | solution.py:595
  50.2 1.5 %collective-permute-start.18 = (s16[32,2176]{1,0:T(8,128)(2,1)S(1)}, s16[32,2176]{1,0:T(8,128)(2,1)S(1)}, u32[]{:S(2)}, u32[]{:S(2)}) collective-permute-start(s16[32,2176]{1,0:T(8,128)(2,1)S(1)} %shard_map.68.refs_2_), channel_id=1, source_target_pairs={{0,2},{2,0},{1,3},{3,1},{4,6},{6,4},{5,7},{7,5},{8,10},{10,8},{9,1... | collective-permute-start | bytes 417800 | tf_op jit(solution)/shard_map/ppermute | solution.py:595
  51.7 4.3 %collective-permute-done.18.refs_3_ = s16[32,2176]{1,0:T(8,128)(2,1)S(1)} collective-permute-done((s16[32,2176]{1,0:T(8,128)(2,1)S(1)}, s16[32,2176]{1,0:T(8,128)(2,1)S(1)}, u32[]{:S(2)}, u32[]{:S(2)}) %collective-permute-start.18) | collective-permute-done | bytes 139296 | tf_op jit(solution)/shard_map/ppermute | solution.py:595
  56.7 1.4 %collective-permute-start.20 = (s16[144,128]{1,0:T(8,128)(2,1)S(1)}, s16[144,128]{1,0:T(8,128)(2,1)S(1)}, u32[]{:S(2)}, u32[]{:S(2)}) collective-permute-start(s16[144,128]{1,0:T(8,128)(2,1)S(1)} %get-tuple-element.50), channel_id=1, source_target_pairs={{0,4},{4,8},{8,12},{12,0},{1,5},{5,9},{9,13},{13,1},{2,6},{6,10},{... | collective-permute-start | bytes 110600 | tf_op jit(solution)/shard_map/ppermute | solution.py:587
  58.1 1.7 %collective-permute-start.21 = (s16[144,128]{1,0:T(8,128)(2,1)S(1)}, s16[144,128]{1,0:T(8,128)(2,1)S(1)}, u32[]{:S(2)}, u32[]{:S(2)}) collective-permute-start(s16[144,128]{1,0:T(8,128)(2,1)S(1)} %get-tuple-element.51), channel_id=1, source_target_pairs={{0,8},{4,12},{8,0},{12,4},{1,9},{5,13},{9,1},{13,5},{2,10},{6,14},... | collective-permute-start | bytes 110600 | tf_op jit(solution)/shard_map/ppermute | solution.py:587
  59.8 1.2 %collective-permute-start.22 = (s16[144,128]{1,0:T(8,128)(2,1)S(1)}, s16[144,128]{1,0:T(8,128)(2,1)S(1)}, u32[]{:S(2)}, u32[]{:S(2)}) collective-permute-start(s16[144,128]{1,0:T(8,128)(2,1)S(1)} %get-tuple-element.52), channel_id=1, source_target_pairs={{0,12},{4,0},{8,4},{12,8},{1,13},{5,1},{9,5},{13,9},{2,14},{6,2},{... | collective-permute-start | bytes 110600 | tf_op jit(solution)/shard_map/ppermute | solution.py:587
  62.9 1.2 %collective-permute-done.21.refs_14_ = s16[144,128]{1,0:T(8,128)(2,1)S(1)} collective-permute-done((s16[144,128]{1,0:T(8,128)(2,1)S(1)}, s16[144,128]{1,0:T(8,128)(2,1)S(1)}, u32[]{:S(2)}, u32[]{:S(2)}) %collective-permute-start.21) | collective-permute-done | bytes 36896 | tf_op jit(solution)/shard_map/ppermute | solution.py:587
  65.7 1.5 %collective-permute-start.24 = (s16[32,2176]{1,0:T(8,128)(2,1)S(1)}, s16[32,2176]{1,0:T(8,128)(2,1)S(1)}, u32[]{:S(2)}, u32[]{:S(2)}) collective-permute-start(s16[32,2176]{1,0:T(8,128)(2,1)S(1)} %shard_map.72.refs_1_), channel_id=1, source_target_pairs={{0,2},{2,0},{1,3},{3,1},{4,6},{6,4},{5,7},{7,5},{8,10},{10,8},{9,1... | collective-permute-start | bytes 417800 | tf_op jit(solution)/shard_map/ppermute | solution.py:595
  67.2 1.3 %collective-permute-start.25 = (f32[32,128]{1,0:T(8,128)S(1)}, f32[32,128]{1,0:T(8,128)S(1)}, u32[]{:S(2)}, u32[]{:S(2)}) collective-permute-start(f32[32,128]{1,0:T(8,128)S(1)} %add.20.after.refs_0_), channel_id=1, source_target_pairs={{0,8},{4,12},{8,0},{12,4},{1,9},{5,13},{9,1},{13,5},{2,10},{6,14},... | collective-permute-start | bytes 49160 | tf_op jit(solution)/shard_map/ppermute | solution.py:595
  68.5 3.4 %collective-permute-done.25.refs_3_.refs_1_ = f32[32,128]{1,0:T(8,128)S(1)} collective-permute-done((f32[32,128]{1,0:T(8,128)S(1)}, f32[32,128]{1,0:T(8,128)S(1)}, u32[]{:S(2)}, u32[]{:S(2)}) %collective-permute-start.25) | collective-permute-done | bytes 16416 | tf_op jit(solution)/shard_map/ppermute | solution.py:595
  72.0 2.0 %shard_map.74.refs_0_ = f32[64,64]{1,0:T(8,128)S(1)} custom-call(f32[32,2048]{1,0:T(8,128)S(1)} %shard_map.73.after.refs_1_, f32[32,128]{1,0:T(8,128)S(1)} %add.20.after.refs_0_, f32[32,128]{1,0:T(8,128)S(1)} %collective-permute-done.25.refs_3_.refs_1_), custom_call_target="tpu_custom_call" | custom-call | tf_op jit(solution)/shard_map/pallas_call | solution.py:70
  75.7 2.2 %collective-permute-start.28 = (f32[32,128]{1,0:T(8,128)S(1)}, f32[32,128]{1,0:T(8,128)S(1)}, u32[]{:S(2)}, u32[]{:S(2)}) collective-permute-start(f32[32,128]{1,0:T(8,128)S(1)} %get-tuple-element.54.refs_1_), channel_id=1, source_target_pairs={{0,8},{4,12},{8,0},{12,4},{1,9},{5,13},{9,1},{13,5},{2,10},{6,14},... | collective-permute-start | bytes 49160 | tf_op jit(solution)/shard_map/ppermute | solution.py:587
  77.9 1.2 %collective-permute-start.29 = (f32[32,128]{1,0:T(8,128)S(1)}, f32[32,128]{1,0:T(8,128)S(1)}, u32[]{:S(2)}, u32[]{:S(2)}) collective-permute-start(f32[32,128]{1,0:T(8,128)S(1)} %get-tuple-element.54.refs_1_), channel_id=1, source_target_pairs={{0,12},{4,0},{8,4},{12,8},{1,13},{5,1},{9,5},{13,9},{2,14},{6,2},{... | collective-permute-start | bytes 49160 | tf_op jit(solution)/shard_map/ppermute | solution.py:587
  80.5 1.1 %collective-permute-done.29.refs_4_ = f32[32,128]{1,0:T(8,128)S(1)} collective-permute-done((f32[32,128]{1,0:T(8,128)S(1)}, f32[32,128]{1,0:T(8,128)S(1)}, u32[]{:S(2)}, u32[]{:S(2)}) %collective-permute-start.29) | collective-permute-done | bytes 16416 | tf_op jit(solution)/shard_map/ppermute | solution.py:587
  81.7 2.9 %shard_map.76 = f32[32,2048]{1,0:T(8,128)} custom-call(bf16[128,2048]{1,0:T(8,128)(2,1)S(1)} %get-tuple-element.53.refs_0_, f32[32,128]{1,0:T(8,128)S(1)} %get-tuple-element.54.refs_1_, f32[32,128]{1,0:T(8,128)S(1)} %collective-permute-done.27.refs_2_, f32[32,128]{1,0:T(8,128)S(1)} %collective-permute-done.28.refs_3_, ...), custom_call_target="tpu_custom_call" | custom-call | tf_op jit(solution)/shard_map/pallas_call | solution.py:70
  (54 shorter events, 14.4 us)
Async XLA Ops:
  2.0 7.9 %collective-permute-start = (s32[3,8]{1,0:T(4,128)S(1)}, s32[3,8]{1,0:T(4,128)S(1)}, u32[]{:S(2)}, u32[]{:S(2)}) collective-permute-start(s32[3,8]{1,0:T(4,128)S(1)} %concatenate.3.refs_0_), channel_id=1, source_target_pairs={{0,4},{4,8},{8,12},{12,0},{1,5},{5,9},{9,13},{13,1},{2,6},{6,10},{... | collective-permute-start | bytes 296 | tf_op jit(solution)/shard_map/ppermute | solution.py:587
  5.0 4.9 %collective-permute-start.1 = (s32[3,8]{1,0:T(4,128)S(1)}, s32[3,8]{1,0:T(4,128)S(1)}, u32[]{:S(2)}, u32[]{:S(2)}) collective-permute-start(s32[3,8]{1,0:T(4,128)S(1)} %concatenate.3.refs_0_), channel_id=1, source_target_pairs={{0,12},{4,0},{8,4},{12,8},{1,13},{5,1},{9,5},{13,9},{2,14},{6,2},{... | collective-permute-start | bytes 296 | tf_op jit(solution)/shard_map/ppermute | solution.py:587
  7.0 4.5 %collective-permute-start.2 = (s32[3,8]{1,0:T(4,128)S(1)}, s32[3,8]{1,0:T(4,128)S(1)}, u32[]{:S(2)}, u32[]{:S(2)}) collective-permute-start(s32[3,8]{1,0:T(4,128)S(1)} %concatenate.3.refs_0_), channel_id=1, source_target_pairs={{0,8},{4,12},{8,0},{12,4},{1,9},{5,13},{9,1},{13,5},{2,10},{6,14},... | collective-permute-start | bytes 296 | tf_op jit(solution)/shard_map/ppermute | solution.py:587
  8.0 1.4 %copy-start = (bf16[2048,384]{1,0:T(8,128)(2,1)S(1)}, bf16[2048,384]{1,0:T(8,128)(2,1)}, u32[]{:S(2)}) copy-start(bf16[2048,384]{1,0:T(8,128)(2,1)} %refs_1_.1) | copy-start | bytes 4718596
  13.1 14.9 %collective-permute-start.3 = (bf16[256,384]{1,0:T(8,128)(2,1)S(1)}, bf16[256,384]{1,0:T(8,128)(2,1)S(1)}, u32[]{:S(2)}, u32[]{:S(2)}) collective-permute-start(bf16[256,384]{1,0:T(8,128)(2,1)S(1)} %get-tuple-element.30), channel_id=1, source_target_pairs={{0,8},{4,12},{8,0},{12,4},{1,9},{5,13},{9,1},{13,5},{2,10},{6,14},... | collective-permute-start | bytes 589832 | tf_op jit(solution)/shard_map/ppermute | solution.py:587
  14.2 13.8 %collective-permute-start.4 = (bf16[256,384]{1,0:T(8,128)(2,1)S(1)}, bf16[256,384]{1,0:T(8,128)(2,1)S(1)}, u32[]{:S(2)}, u32[]{:S(2)}) collective-permute-start(bf16[256,384]{1,0:T(8,128)(2,1)S(1)} %get-tuple-element.31), channel_id=1, source_target_pairs={{0,12},{4,0},{8,4},{12,8},{1,13},{5,1},{9,5},{13,9},{2,14},{6,2},{... | collective-permute-start | bytes 589832 | tf_op jit(solution)/shard_map/ppermute | solution.py:587
  15.5 12.5 %collective-permute-start.5 = (bf16[256,384]{1,0:T(8,128)(2,1)S(1)}, bf16[256,384]{1,0:T(8,128)(2,1)S(1)}, u32[]{:S(2)}, u32[]{:S(2)}) collective-permute-start(bf16[256,384]{1,0:T(8,128)(2,1)S(1)} %get-tuple-element.32), channel_id=1, source_target_pairs={{0,4},{4,8},{8,12},{12,0},{1,5},{5,9},{9,13},{13,1},{2,6},{6,10},{... | collective-permute-start | bytes 589832 | tf_op jit(solution)/shard_map/ppermute | solution.py:587
  16.2 13.1 %collective-permute-start.7 = (f32[1024,128]{1,0:T(8,128)S(1)}, f32[1024,128]{1,0:T(8,128)S(1)}, u32[]{:S(2)}, u32[]{:S(2)}) collective-permute-start(f32[1024,128]{1,0:T(8,128)S(1)} %shard_map.59.refs_5_.mine), channel_id=1, source_target_pairs={{0,1},{1,0},{2,3},{3,2},{4,5},{5,4},{6,7},{7,6},{8,9},{9,8},{10,11... | collective-permute-start | bytes 1572872 | tf_op jit(solution)/shard_map/ppermute | solution.py:587
  16.5 12.6 %copy-start.1 = (f32[2048,32]{0,1:T(8,128)S(1)}, f32[2048,32]{0,1:T(8,128)}, u32[]{:S(2)}) copy-start(f32[2048,32]{0,1:T(8,128)} %param.5) | copy-start | bytes 786436
  29.1 2.0 %collective-permute-start.6 = (f32[1024,128]{1,0:T(8,128)S(1)}, f32[1024,128]{1,0:T(8,128)S(1)}, u32[]{:S(2)}, u32[]{:S(2)}) collective-permute-start(f32[1024,128]{1,0:T(8,128)S(1)} %shard_map.62.refs_1_), channel_id=1, source_target_pairs={{0,1},{1,0},{2,3},{3,2},{4,5},{5,4},{6,7},{7,6},{8,9},{9,8},{10,11... | collective-permute-start | bytes 1572872 | tf_op jit(solution)/shard_map/ppermute | solution.py:587
  31.9 9.5 %collective-permute-start.10 = (f32[64,128]{1,0:T(8,128)S(1)}, f32[64,128]{1,0:T(8,128)S(1)}, u32[]{:S(2)}, u32[]{:S(2)}) collective-permute-start(f32[64,128]{1,0:T(8,128)S(1)} %get-tuple-element.37), channel_id=1, source_target_pairs={{0,12},{4,0},{8,4},{12,8},{1,13},{5,1},{9,5},{13,9},{2,14},{6,2},{... | collective-permute-start | bytes 98312 | tf_op jit(solution)/shard_map/ppermute | solution.py:587
  34.1 8.4 %collective-permute-start.8 = (f32[64,128]{1,0:T(8,128)S(1)}, f32[64,128]{1,0:T(8,128)S(1)}, u32[]{:S(2)}, u32[]{:S(2)}) collective-permute-start(f32[64,128]{1,0:T(8,128)S(1)} %get-tuple-element.37), channel_id=1, source_target_pairs={{0,4},{4,8},{8,12},{12,0},{1,5},{5,9},{9,13},{13,1},{2,6},{6,10},{... | collective-permute-start | bytes 98312 | tf_op jit(solution)/shard_map/ppermute | solution.py:587
  36.6 6.0 %collective-permute-start.9 = (f32[64,128]{1,0:T(8,128)S(1)}, f32[64,128]{1,0:T(8,128)S(1)}, u32[]{:S(2)}, u32[]{:S(2)}) collective-permute-start(f32[64,128]{1,0:T(8,128)S(1)} %get-tuple-element.37), channel_id=1, source_target_pairs={{0,8},{4,12},{8,0},{12,4},{1,9},{5,13},{9,1},{13,5},{2,10},{6,14},... | collective-permute-start | bytes 98312 | tf_op jit(solution)/shard_map/ppermute | solution.py:587
  38.8 7.8 %collective-permute-start.12 = (s16[272,128]{1,0:T(8,128)(2,1)S(1)}, s16[272,128]{1,0:T(8,128)(2,1)S(1)}, u32[]{:S(2)}, u32[]{:S(2)}) collective-permute-start(s16[272,128]{1,0:T(8,128)(2,1)S(1)} %get-tuple-element.43), channel_id=1, source_target_pairs={{0,4},{4,8},{8,12},{12,0},{1,5},{5,9},{9,13},{13,1},{2,6},{6,10},{... | collective-permute-start | bytes 208904 | tf_op jit(solution)/shard_map/ppermute | solution.py:587
  38.8 8.5 %collective-permute-start.13 = (s16[272,128]{1,0:T(8,128)(2,1)S(1)}, s16[272,128]{1,0:T(8,128)(2,1)S(1)}, u32[]{:S(2)}, u32[]{:S(2)}) collective-permute-start(s16[272,128]{1,0:T(8,128)(2,1)S(1)} %get-tuple-element.44), channel_id=1, source_target_pairs={{0,8},{4,12},{8,0},{12,4},{1,9},{5,13},{9,1},{13,5},{2,10},{6,14},... | collective-permute-start | bytes 208904 | tf_op jit(solution)/shard_map/ppermute | solution.py:587
  41.5 5.8 %collective-permute-start.14 = (s16[272,128]{1,0:T(8,128)(2,1)S(1)}, s16[272,128]{1,0:T(8,128)(2,1)S(1)}, u32[]{:S(2)}, u32[]{:S(2)}) collective-permute-start(s16[272,128]{1,0:T(8,128)(2,1)S(1)} %get-tuple-element.45), channel_id=1, source_target_pairs={{0,12},{4,0},{8,4},{12,8},{1,13},{5,1},{9,5},{13,9},{2,14},{6,2},{... | collective-permute-start | bytes 208904 | tf_op jit(solution)/shard_map/ppermute | solution.py:587
  42.6 4.0 %collective-permute-start.11 = (f32[64,128]{1,0:T(8,128)S(1)}, f32[64,128]{1,0:T(8,128)S(1)}, u32[]{:S(2)}, u32[]{:S(2)}) collective-permute-start(f32[64,128]{1,0:T(8,128)S(1)} %add_add_fusion.refs_1_), channel_id=1, source_target_pairs={{0,2},{2,0},{1,3},{3,1},{4,6},{6,4},{5,7},{7,5},{8,10},{10,8},{9,1... | collective-permute-start | bytes 98312 | tf_op jit(solution)/shard_map/ppermute | solution.py:595
  47.3 1.5 %collective-permute-start.15 = (bf16[1,256,128]{2,1,0:T(8,128)(2,1)S(1)}, bf16[1,256,128]{2,1,0:T(8,128)(2,1)S(1)}, u32[]{:S(2)}, u32[]{:S(2)}) collective-permute-start(bf16[1,256,128]{2,1,0:T(8,128)(2,1)S(1)} %get-tuple-element.46.refs_4_.refs_7_), channel_id=1, source_target_pairs={{0,1},{1,0},{2,3},{3,2},{4,5},{5,4},{6,7},{7,6},{8,9},{9,8},{10,11... | collective-permute-start | bytes 196616 | tf_op jit(solution)/shard_map/ppermute | solution.py:587
  47.4 1.4 %collective-permute-start.16 = (bf16[1,256,128]{2,1,0:T(8,128)(2,1)S(1)}, bf16[1,256,128]{2,1,0:T(8,128)(2,1)S(1)}, u32[]{:S(2)}, u32[]{:S(2)}) collective-permute-start(bf16[1,256,128]{2,1,0:T(8,128)(2,1)S(1)} %get-tuple-element.47.refs_5_.refs_8_), channel_id=1, source_target_pairs={{0,1},{1,0},{2,3},{3,2},{4,5},{5,4},{6,7},{7,6},{8,9},{9,8},{10,11... | collective-permute-start | bytes 196616 | tf_op jit(solution)/shard_map/ppermute | solution.py:587
  47.9 1.3 %collective-permute-start.17 = (bf16[1,256,128]{2,1,0:T(8,128)(2,1)S(1)}, bf16[1,256,128]{2,1,0:T(8,128)(2,1)S(1)}, u32[]{:S(2)}, u32[]{:S(2)}) collective-permute-start(bf16[1,256,128]{2,1,0:T(8,128)(2,1)S(1)} %get-tuple-element.48.refs_6_.refs_9_), channel_id=1, source_target_pairs={{0,1},{1,0},{2,3},{3,2},{4,5},{5,4},{6,7},{7,6},{8,9},{9,8},{10,11... | collective-permute-start | bytes 196616 | tf_op jit(solution)/shard_map/ppermute | solution.py:587
  50.2 5.8 %collective-permute-start.18 = (s16[32,2176]{1,0:T(8,128)(2,1)S(1)}, s16[32,2176]{1,0:T(8,128)(2,1)S(1)}, u32[]{:S(2)}, u32[]{:S(2)}) collective-permute-start(s16[32,2176]{1,0:T(8,128)(2,1)S(1)} %shard_map.68.refs_2_), channel_id=1, source_target_pairs={{0,2},{2,0},{1,3},{3,1},{4,6},{6,4},{5,7},{7,5},{8,10},{10,8},{9,1... | collective-permute-start | bytes 417800 | tf_op jit(solution)/shard_map/ppermute | solution.py:595
  56.6 4.4 %collective-permute-start.19 = (f32[32,2048]{1,0:T(8,128)S(1)}, f32[32,2048]{1,0:T(8,128)S(1)}, u32[]{:S(2)}, u32[]{:S(2)}) collective-permute-start(f32[32,2048]{1,0:T(8,128)S(1)} %get-tuple-element.49.refs_0_.refs_3_), channel_id=1, source_target_pairs={{0,1},{1,0},{2,3},{3,2},{4,5},{5,4},{6,7},{7,6},{8,9},{9,8},{10,11... | collective-permute-start | bytes 786440 | tf_op jit(solution)/shard_map/ppermute | solution.py:587
  56.7 6.2 %collective-permute-start.20 = (s16[144,128]{1,0:T(8,128)(2,1)S(1)}, s16[144,128]{1,0:T(8,128)(2,1)S(1)}, u32[]{:S(2)}, u32[]{:S(2)}) collective-permute-start(s16[144,128]{1,0:T(8,128)(2,1)S(1)} %get-tuple-element.50), channel_id=1, source_target_pairs={{0,4},{4,8},{8,12},{12,0},{1,5},{5,9},{9,13},{13,1},{2,6},{6,10},{... | collective-permute-start | bytes 110600 | tf_op jit(solution)/shard_map/ppermute | solution.py:587
  58.1 5.9 %collective-permute-start.21 = (s16[144,128]{1,0:T(8,128)(2,1)S(1)}, s16[144,128]{1,0:T(8,128)(2,1)S(1)}, u32[]{:S(2)}, u32[]{:S(2)}) collective-permute-start(s16[144,128]{1,0:T(8,128)(2,1)S(1)} %get-tuple-element.51), channel_id=1, source_target_pairs={{0,8},{4,12},{8,0},{12,4},{1,9},{5,13},{9,1},{13,5},{2,10},{6,14},... | collective-permute-start | bytes 110600 | tf_op jit(solution)/shard_map/ppermute | solution.py:587
  59.8 4.7 %collective-permute-start.22 = (s16[144,128]{1,0:T(8,128)(2,1)S(1)}, s16[144,128]{1,0:T(8,128)(2,1)S(1)}, u32[]{:S(2)}, u32[]{:S(2)}) collective-permute-start(s16[144,128]{1,0:T(8,128)(2,1)S(1)} %get-tuple-element.52), channel_id=1, source_target_pairs={{0,12},{4,0},{8,4},{12,8},{1,13},{5,1},{9,5},{13,9},{2,14},{6,2},{... | collective-permute-start | bytes 110600 | tf_op jit(solution)/shard_map/ppermute | solution.py:587
  61.5 4.0 %collective-permute-start.23 = (f32[32,128]{1,0:T(8,128)S(1)}, f32[32,128]{1,0:T(8,128)S(1)}, u32[]{:S(2)}, u32[]{:S(2)}) collective-permute-start(f32[32,128]{1,0:T(8,128)S(1)} %shard_map.70.refs_2_), channel_id=1, source_target_pairs={{0,4},{4,0},{8,12},{12,8},{1,5},{5,1},{9,13},{13,9},{2,6},{6,2},{1... | collective-permute-start | bytes 49160 | tf_op jit(solution)/shard_map/ppermute | solution.py:595
  65.7 6.2 %collective-permute-start.24 = (s16[32,2176]{1,0:T(8,128)(2,1)S(1)}, s16[32,2176]{1,0:T(8,128)(2,1)S(1)}, u32[]{:S(2)}, u32[]{:S(2)}) collective-permute-start(s16[32,2176]{1,0:T(8,128)(2,1)S(1)} %shard_map.72.refs_1_), channel_id=1, source_target_pairs={{0,2},{2,0},{1,3},{3,1},{4,6},{6,4},{5,7},{7,5},{8,10},{10,8},{9,1... | collective-permute-start | bytes 417800 | tf_op jit(solution)/shard_map/ppermute | solution.py:595
  67.2 4.6 %collective-permute-start.25 = (f32[32,128]{1,0:T(8,128)S(1)}, f32[32,128]{1,0:T(8,128)S(1)}, u32[]{:S(2)}, u32[]{:S(2)}) collective-permute-start(f32[32,128]{1,0:T(8,128)S(1)} %add.20.after.refs_0_), channel_id=1, source_target_pairs={{0,8},{4,12},{8,0},{12,4},{1,9},{5,13},{9,1},{13,5},{2,10},{6,14},... | collective-permute-start | bytes 49160 | tf_op jit(solution)/shard_map/ppermute | solution.py:595
  72.0 2.1 %collective-permute-start.26 = (f32[32,2048]{1,0:T(8,128)S(1)}, f32[32,2048]{1,0:T(8,128)S(1)}, u32[]{:S(2)}, u32[]{:S(2)}) collective-permute-start(f32[32,2048]{1,0:T(8,128)S(1)} %shard_map.73.after.refs_1_), channel_id=1, source_target_pairs={{0,1},{1,0},{2,3},{3,2},{4,5},{5,4},{6,7},{7,6},{8,9},{9,8},{10,11... | collective-permute-start | bytes 786440 | tf_op jit(solution)/shard_map/ppermute | solution.py:587
  74.9 5.6 %collective-permute-start.27 = (f32[32,128]{1,0:T(8,128)S(1)}, f32[32,128]{1,0:T(8,128)S(1)}, u32[]{:S(2)}, u32[]{:S(2)}) collective-permute-start(f32[32,128]{1,0:T(8,128)S(1)} %get-tuple-element.54.refs_1_), channel_id=1, source_target_pairs={{0,4},{4,8},{8,12},{12,0},{1,5},{5,9},{9,13},{13,1},{2,6},{6,10},{... | collective-permute-start | bytes 49160 | tf_op jit(solution)/shard_map/ppermute | solution.py:587
  75.7 4.8 %collective-permute-start.28 = (f32[32,128]{1,0:T(8,128)S(1)}, f32[32,128]{1,0:T(8,128)S(1)}, u32[]{:S(2)}, u32[]{:S(2)}) collective-permute-start(f32[32,128]{1,0:T(8,128)S(1)} %get-tuple-element.54.refs_1_), channel_id=1, source_target_pairs={{0,8},{4,12},{8,0},{12,4},{1,9},{5,13},{9,1},{13,5},{2,10},{6,14},... | collective-permute-start | bytes 49160 | tf_op jit(solution)/shard_map/ppermute | solution.py:587
  77.9 3.7 %collective-permute-start.29 = (f32[32,128]{1,0:T(8,128)S(1)}, f32[32,128]{1,0:T(8,128)S(1)}, u32[]{:S(2)}, u32[]{:S(2)}) collective-permute-start(f32[32,128]{1,0:T(8,128)S(1)} %get-tuple-element.54.refs_1_), channel_id=1, source_target_pairs={{0,12},{4,0},{8,4},{12,8},{1,13},{5,1},{9,5},{13,9},{2,14},{6,2},{... | collective-permute-start | bytes 49160 | tf_op jit(solution)/shard_map/ppermute | solution.py:587

commit v20 on v17

--- a/solution.py
+++ b/solution.py
@@ -225,7 +225,7 @@
     return lax.rem(value, jnp.int32(size))
 
 
-def plan_body(dims, list_order, me, *refs):
+def plan_body(dims, list_order, me, live_count, *refs):
     row_count, capacity, slots, blocks_here = dims
     lists, (emb, after, idx_out) = refs[:row_count], refs[row_count : row_count + 3]
     sends, (idx, left) = refs[row_count + 3 : -2], refs[-2:]
@@ -234,6 +234,7 @@
         for line in (0, 1, 2, 4, 5):
             idx[line, i] = 0
     lists = dict(zip(list_order, [one.ready() for one in lists]))
+    live_count = live_count.ready()[0]
 
     def each(step, start):
         if slots <= 8:
@@ -243,14 +244,17 @@
             lax.fori_loop(0, slots, step, start)
 
     for k in range(row_count):
-        live_count = lists[k][2, 0]
-
-        def step(s, counts, k=k, live_count=live_count):
+
+        def step(s, counts, k=k):
             near = lists[k][0, s]
             far = lists[k][1, s]
             owner = quotient(far, blocks_here)
-            live = s < live_count
-            hit = live & (owner == row)
+            hit = owner == row
+            if k > 0:
+                hit = hit & (counts[0] < capacity)
+            else:
+                live = s < live_count
+                hit = hit & live
             slot = jnp.where(hit, k * capacity + counts[0], slots)
             idx[4, slot] = far - row * blocks_here
             idx[5, slot] = near
@@ -615,11 +619,8 @@
     block_count = row_count * blocks_here
     others = range(1, row_count)
 
-    own_list = jnp.concatenate(
-        [pair_list[0], jnp.broadcast_to(pair_count[:, None], (1, slots))], axis=0
-    )
-    lists = row_terms(own_list, row_count)
     list_order = [0, *sorted(others, key=lambda k: k * (row_count - k))]
+    lists = [shift_by(pair_list[0], "rows", row_count, k) if k else pair_list[0] for k in list_order]
     self_part = call(
         functools.partial(self_distance_body, own_blocks, tile_count),
         sds((own_blocks * BLOCK, BLOCK), F32),
@@ -628,9 +629,9 @@
     planned = call(
         functools.partial(plan_body, (row_count, capacity, slots, blocks_here), list_order),
         [sds((6, slots + 1), jnp.int32)] + [sds((capacity * BLOCK, half_features), BF16) for _ in others],
-        [ME, *[lists[k] for k in list_order], embeddings, self_part],
-        late=range(1, 1 + row_count),
-        any_in=(row_count + 2,),
+        [ME, pair_count, *lists, embeddings, self_part],
+        late=range(1, 2 + row_count),
+        any_in=(row_count + 3,),
         any_out=(0,),
         scratch=[pltpu.SMEM((6, slots + 1), jnp.int32), pltpu.SemaphoreType.DMA],
     )

time: 84.2 us -> 83.1 us (0.987)
  transfers between devices with their start and end apart: 30 -> 30, of which waited for: 13 -> 13; matrix products, arithmetic and copies ran while one was open for 1% -> 1% of each run, Pallas kernels for 7% -> 8%
where the time goes in v20:
time: 83.1 us; the launch traced here: 82.9 us
  starting transfers between devices  35.7 us (43%)
  waiting for transfers between devices  29.7 us (36%)
  Pallas kernels  14 us (17%)
  local copies, waits for them, and re-layouts  2.02 us (2%)
  between operations  1.51 us (2%)
    ppermute x25, starting transfers between devices, shift_by(): lax.ppermute(value, axes, [(i, (i + shift) % size) for i in range(size)])  28.9 us
    ppermute x25, waiting for transfers between devices, shift_by(): lax.ppermute(value, axes, [(i, (i + shift) % size) for i in range(size)])  19.6 us
    pallas_call x18, Pallas kernels, call(): pl.pallas_call(body, out_shape=shapes, in_specs=[ANY if i in any_in else...  14 us
    ppermute x5, waiting for transfers between devices, pair_step(): lax.ppermute(value, name, [(i, i ^ flip) for i in range(lax.axis_size(nam...  10.1 us
    ppermute x5, starting transfers between devices, pair_step(): lax.ppermute(value, name, [(i, i ^ flip) for i in range(lax.axis_size(nam...  6.75 us
  transfers between devices with their start and end apart: 30, of which 13 were waited for; matrix products, arithmetic and copies ran while one was open for 1% of the time, Pallas kernels for 8%

profile of v20, /device:TPU:0, one launch (start us, length us, event | category | flops | bytes accessed | tf_op | source)
XLA Modules:
  0.0 82.9 jit_solution(5989461846848375962)
XLA Ops:
  0.6 3.1 %collective-permute-start = (s32[2,8]{1,0:T(2,128)}, s32[2,8]{1,0:T(2,128)S(1)}, u32[]{:S(2)}, u32[]{:S(2)}) collective-permute-start(s32[2,8]{1,0:T(2,128)} %bitcast.7), channel_id=1, source_target_pairs={{0,4},{4,8},{8,12},{12,0},{1,5},{5,9},{9,13},{13,1},{2,6},{6,10},{... | collective-permute-start | bytes 200 | tf_op jit(solution)/shard_map/ppermute | solution.py:584
  3.7 2.1 %collective-permute-start.1 = (s32[2,8]{1,0:T(2,128)}, s32[2,8]{1,0:T(2,128)S(1)}, u32[]{:S(2)}, u32[]{:S(2)}) collective-permute-start(s32[2,8]{1,0:T(2,128)} %bitcast.8), channel_id=1, source_target_pairs={{0,12},{4,0},{8,4},{12,8},{1,13},{5,1},{9,5},{13,9},{2,14},{6,2},{... | collective-permute-start | bytes 200 | tf_op jit(solution)/shard_map/ppermute | solution.py:584
  6.8 1.4 %copy-done = bf16[2048,384]{1,0:T(8,128)(2,1)S(1)} copy-done((bf16[2048,384]{1,0:T(8,128)(2,1)S(1)}, bf16[2048,384]{1,0:T(8,128)(2,1)}, u32[]{:S(2)}) %copy-start) | copy-done | bytes 1572888
  9.3 1.2 %collective-permute-done.2.refs_4_ = s32[2,8]{1,0:T(2,128)S(1)} collective-permute-done((s32[2,8]{1,0:T(2,128)}, s32[2,8]{1,0:T(2,128)S(1)}, u32[]{:S(2)}, u32[]{:S(2)}) %collective-permute-start.2) | collective-permute-done | bytes 96 | tf_op jit(solution)/shard_map/ppermute | solution.py:584
  10.5 1.6 %shard_map.60 = (s32[6,9]{1,0:T(8,128)S(1)}, bf16[256,384]{1,0:T(8,128)(2,1)S(1)}, bf16[256,384]{1,0:T(8,128)(2,1)S(1)}, bf16[256,384]{1,0:T(8,128)(2,1)S(1)}) custom-call(s32[1]{0:T(128)S(6)} %copy.6.refs_0_, s32[2,8]{1,0:T(2,128)S(1)} %bitcast.10, s32[2,8]{1,0:T(2,128)S(1)} %collective-permute-done.refs_2_, s32[2,8]{1,0:T(2,128)S(1)} %collective-permute-done.1.refs_3_, ...), custom_call_target="tpu_custom_call" | custom-call | tf_op jit(solution)/shard_map/pallas_call | solution.py:70
  12.1 1.0 %collective-permute-start.3 = (bf16[256,384]{1,0:T(8,128)(2,1)S(1)}, bf16[256,384]{1,0:T(8,128)(2,1)S(1)}, u32[]{:S(2)}, u32[]{:S(2)}) collective-permute-start(bf16[256,384]{1,0:T(8,128)(2,1)S(1)} %get-tuple-element.30), channel_id=1, source_target_pairs={{0,8},{4,12},{8,0},{12,4},{1,9},{5,13},{9,1},{13,5},{2,10},{6,14},... | collective-permute-start | bytes 589832 | tf_op jit(solution)/shard_map/ppermute | solution.py:584
  13.1 1.8 %collective-permute-start.4 = (bf16[256,384]{1,0:T(8,128)(2,1)S(1)}, bf16[256,384]{1,0:T(8,128)(2,1)S(1)}, u32[]{:S(2)}, u32[]{:S(2)}) collective-permute-start(bf16[256,384]{1,0:T(8,128)(2,1)S(1)} %get-tuple-element.31), channel_id=1, source_target_pairs={{0,12},{4,0},{8,4},{12,8},{1,13},{5,1},{9,5},{13,9},{2,14},{6,2},{... | collective-permute-start | bytes 589832 | tf_op jit(solution)/shard_map/ppermute | solution.py:584
  15.5 11.8 %collective-permute-done.3.refs_3_ = bf16[256,384]{1,0:T(8,128)(2,1)S(1)} collective-permute-done((bf16[256,384]{1,0:T(8,128)(2,1)S(1)}, bf16[256,384]{1,0:T(8,128)(2,1)S(1)}, u32[]{:S(2)}, u32[]{:S(2)}) %collective-permute-start.3) | collective-permute-done | bytes 196640 | tf_op jit(solution)/shard_map/ppermute | solution.py:584
  27.3 1.1 %shard_map.62.refs_1_ = f32[1024,128]{1,0:T(8,128)S(1)} custom-call(s32[6,9]{1,0:T(8,128)S(1)} %get-tuple-element.29.after.refs_0_, bf16[2048,384]{1,0:T(8,128)(2,1)S(1)} %copy-done, f32[2048,128]{1,0:T(8,128)S(1)} %shard_map.61.refs_2_, bf16[256,384]{1,0:T(8,128)(2,1)S(1)} %collective-permute-done.3.refs_3_, ...), custom_call_target="tpu_custom_call" | custom-call | tf_op jit(solution)/shard_map/pallas_call | solution.py:70
  28.8 1.5 %collective-permute-done.6.refs_2_ = f32[1024,128]{1,0:T(8,128)S(1)} collective-permute-done((f32[1024,128]{1,0:T(8,128)S(1)}, f32[1024,128]{1,0:T(8,128)S(1)}, u32[]{:S(2)}, u32[]{:S(2)}) %collective-permute-start.6) | collective-permute-done | bytes 524320 | tf_op jit(solution)/shard_map/ppermute | solution.py:584
  31.2 2.2 %collective-permute-start.10 = (f32[64,128]{1,0:T(8,128)S(1)}, f32[64,128]{1,0:T(8,128)S(1)}, u32[]{:S(2)}, u32[]{:S(2)}) collective-permute-start(f32[64,128]{1,0:T(8,128)S(1)} %get-tuple-element.37), channel_id=1, source_target_pairs={{0,12},{4,0},{8,4},{12,8},{1,13},{5,1},{9,5},{13,9},{2,14},{6,2},{... | collective-permute-start | bytes 98312 | tf_op jit(solution)/shard_map/ppermute | solution.py:584
  33.4 2.0 %collective-permute-start.8 = (f32[64,128]{1,0:T(8,128)S(1)}, f32[64,128]{1,0:T(8,128)S(1)}, u32[]{:S(2)}, u32[]{:S(2)}) collective-permute-start(f32[64,128]{1,0:T(8,128)S(1)} %get-tuple-element.37), channel_id=1, source_target_pairs={{0,4},{4,8},{8,12},{12,0},{1,5},{5,9},{9,13},{13,1},{2,6},{6,10},{... | collective-permute-start | bytes 98312 | tf_op jit(solution)/shard_map/ppermute | solution.py:584
  35.5 2.2 %collective-permute-start.9 = (f32[64,128]{1,0:T(8,128)S(1)}, f32[64,128]{1,0:T(8,128)S(1)}, u32[]{:S(2)}, u32[]{:S(2)}) collective-permute-start(f32[64,128]{1,0:T(8,128)S(1)} %get-tuple-element.37), channel_id=1, source_target_pairs={{0,8},{4,12},{8,0},{12,4},{1,9},{5,13},{9,1},{13,5},{2,10},{6,14},... | collective-permute-start | bytes 98312 | tf_op jit(solution)/shard_map/ppermute | solution.py:584
  37.8 2.5 %collective-permute-start.13 = (s16[272,128]{1,0:T(8,128)(2,1)S(1)}, s16[272,128]{1,0:T(8,128)(2,1)S(1)}, u32[]{:S(2)}, u32[]{:S(2)}) collective-permute-start(s16[272,128]{1,0:T(8,128)(2,1)S(1)} %get-tuple-element.44), channel_id=1, source_target_pairs={{0,8},{4,12},{8,0},{12,4},{1,9},{5,13},{9,1},{13,5},{2,10},{6,14},... | collective-permute-start | bytes 208904 | tf_op jit(solution)/shard_map/ppermute | solution.py:584
  40.4 1.2 %collective-permute-start.14 = (s16[272,128]{1,0:T(8,128)(2,1)S(1)}, s16[272,128]{1,0:T(8,128)(2,1)S(1)}, u32[]{:S(2)}, u32[]{:S(2)}) collective-permute-start(s16[272,128]{1,0:T(8,128)(2,1)S(1)} %get-tuple-element.45), channel_id=1, source_target_pairs={{0,12},{4,0},{8,4},{12,8},{1,13},{5,1},{9,5},{13,9},{2,14},{6,2},{... | collective-permute-start | bytes 208904 | tf_op jit(solution)/shard_map/ppermute | solution.py:584
  41.6 1.6 %collective-permute-start.11 = (f32[64,128]{1,0:T(8,128)S(1)}, f32[64,128]{1,0:T(8,128)S(1)}, u32[]{:S(2)}, u32[]{:S(2)}) collective-permute-start(f32[64,128]{1,0:T(8,128)S(1)} %add_add_fusion.refs_1_), channel_id=1, source_target_pairs={{0,2},{2,0},{1,3},{3,1},{4,6},{6,4},{5,7},{7,5},{8,10},{10,8},{9,1... | collective-permute-start | bytes 98312 | tf_op jit(solution)/shard_map/ppermute | solution.py:592
  43.1 2.4 %collective-permute-done.11.refs_2_.refs_3_ = f32[64,128]{1,0:T(8,128)S(1)} collective-permute-done((f32[64,128]{1,0:T(8,128)S(1)}, f32[64,128]{1,0:T(8,128)S(1)}, u32[]{:S(2)}, u32[]{:S(2)}) %collective-permute-start.11) | collective-permute-done | bytes 32800 | tf_op jit(solution)/shard_map/ppermute | solution.py:592
  48.1 1.0 %shard_map.68.refs_2_ = s16[32,2176]{1,0:T(8,128)(2,1)S(1)} custom-call(s32[6,9]{1,0:T(8,128)S(1)} %get-tuple-element.29.after.refs_0_, f32[64,128]{1,0:T(8,128)S(1)} %get-tuple-element.41.refs_1_.refs_0_, f32[32,2048]{1,0:T(8,128)S(1)} %get-tuple-element.42.refs_2_, bf16[8,256,128]{2,1,0:T(8,128)(2,1)S(1)} %get-tuple-element.38.refs_4_.refs_3_.refs_6_, ...), custom_call_target="tpu_custom_call" | custom-call | tf_op jit(solution)/shard_map/pallas_call | solution.py:70
  49.1 1.5 %collective-permute-start.18 = (s16[32,2176]{1,0:T(8,128)(2,1)S(1)}, s16[32,2176]{1,0:T(8,128)(2,1)S(1)}, u32[]{:S(2)}, u32[]{:S(2)}) collective-permute-start(s16[32,2176]{1,0:T(8,128)(2,1)S(1)} %shard_map.68.refs_2_), channel_id=1, source_target_pairs={{0,2},{2,0},{1,3},{3,1},{4,6},{6,4},{5,7},{7,5},{8,10},{10,8},{9,1... | collective-permute-start | bytes 417800 | tf_op jit(solution)/shard_map/ppermute | solution.py:592
  50.6 4.3 %collective-permute-done.18.refs_3_ = s16[32,2176]{1,0:T(8,128)(2,1)S(1)} collective-permute-done((s16[32,2176]{1,0:T(8,128)(2,1)S(1)}, s16[32,2176]{1,0:T(8,128)(2,1)S(1)}, u32[]{:S(2)}, u32[]{:S(2)}) %collective-permute-start.18) | collective-permute-done | bytes 139296 | tf_op jit(solution)/shard_map/ppermute | solution.py:592
  55.6 1.4 %collective-permute-start.20 = (s16[144,128]{1,0:T(8,128)(2,1)S(1)}, s16[144,128]{1,0:T(8,128)(2,1)S(1)}, u32[]{:S(2)}, u32[]{:S(2)}) collective-permute-start(s16[144,128]{1,0:T(8,128)(2,1)S(1)} %get-tuple-element.50), channel_id=1, source_target_pairs={{0,4},{4,8},{8,12},{12,0},{1,5},{5,9},{9,13},{13,1},{2,6},{6,10},{... | collective-permute-start | bytes 110600 | tf_op jit(solution)/shard_map/ppermute | solution.py:584
  57.0 1.8 %collective-permute-start.21 = (s16[144,128]{1,0:T(8,128)(2,1)S(1)}, s16[144,128]{1,0:T(8,128)(2,1)S(1)}, u32[]{:S(2)}, u32[]{:S(2)}) collective-permute-start(s16[144,128]{1,0:T(8,128)(2,1)S(1)} %get-tuple-element.51), channel_id=1, source_target_pairs={{0,8},{4,12},{8,0},{12,4},{1,9},{5,13},{9,1},{13,5},{2,10},{6,14},... | collective-permute-start | bytes 110600 | tf_op jit(solution)/shard_map/ppermute | solution.py:584
  58.8 1.2 %collective-permute-start.22 = (s16[144,128]{1,0:T(8,128)(2,1)S(1)}, s16[144,128]{1,0:T(8,128)(2,1)S(1)}, u32[]{:S(2)}, u32[]{:S(2)}) collective-permute-start(s16[144,128]{1,0:T(8,128)(2,1)S(1)} %get-tuple-element.52), channel_id=1, source_target_pairs={{0,12},{4,0},{8,4},{12,8},{1,13},{5,1},{9,5},{13,9},{2,14},{6,2},{... | collective-permute-start | bytes 110600 | tf_op jit(solution)/shard_map/ppermute | solution.py:584
  61.8 1.2 %collective-permute-done.21.refs_14_ = s16[144,128]{1,0:T(8,128)(2,1)S(1)} collective-permute-done((s16[144,128]{1,0:T(8,128)(2,1)S(1)}, s16[144,128]{1,0:T(8,128)(2,1)S(1)}, u32[]{:S(2)}, u32[]{:S(2)}) %collective-permute-start.21) | collective-permute-done | bytes 36896 | tf_op jit(solution)/shard_map/ppermute | solution.py:584
  64.6 1.5 %collective-permute-start.24 = (s16[32,2176]{1,0:T(8,128)(2,1)S(1)}, s16[32,2176]{1,0:T(8,128)(2,1)S(1)}, u32[]{:S(2)}, u32[]{:S(2)}) collective-permute-start(s16[32,2176]{1,0:T(8,128)(2,1)S(1)} %shard_map.72.refs_1_), channel_id=1, source_target_pairs={{0,2},{2,0},{1,3},{3,1},{4,6},{6,4},{5,7},{7,5},{8,10},{10,8},{9,1... | collective-permute-start | bytes 417800 | tf_op jit(solution)/shard_map/ppermute | solution.py:592
  66.2 1.3 %collective-permute-start.25 = (f32[32,128]{1,0:T(8,128)S(1)}, f32[32,128]{1,0:T(8,128)S(1)}, u32[]{:S(2)}, u32[]{:S(2)}) collective-permute-start(f32[32,128]{1,0:T(8,128)S(1)} %add.18.after.refs_0_), channel_id=1, source_target_pairs={{0,8},{4,12},{8,0},{12,4},{1,9},{5,13},{9,1},{13,5},{2,10},{6,14},... | collective-permute-start | bytes 49160 | tf_op jit(solution)/shard_map/ppermute | solution.py:592
  67.4 3.4 %collective-permute-done.25.refs_3_.refs_1_ = f32[32,128]{1,0:T(8,128)S(1)} collective-permute-done((f32[32,128]{1,0:T(8,128)S(1)}, f32[32,128]{1,0:T(8,128)S(1)}, u32[]{:S(2)}, u32[]{:S(2)}) %collective-permute-start.25) | collective-permute-done | bytes 16416 | tf_op jit(solution)/shard_map/ppermute | solution.py:592
  71.0 1.7 %shard_map.74.refs_0_ = f32[64,64]{1,0:T(8,128)S(1)} custom-call(f32[32,2048]{1,0:T(8,128)S(1)} %shard_map.73.after.refs_1_, f32[32,128]{1,0:T(8,128)S(1)} %add.18.after.refs_0_, f32[32,128]{1,0:T(8,128)S(1)} %collective-permute-done.25.refs_3_.refs_1_), custom_call_target="tpu_custom_call" | custom-call | tf_op jit(solution)/shard_map/pallas_call | solution.py:70
  74.3 2.2 %collective-permute-start.28 = (f32[32,128]{1,0:T(8,128)S(1)}, f32[32,128]{1,0:T(8,128)S(1)}, u32[]{:S(2)}, u32[]{:S(2)}) collective-permute-start(f32[32,128]{1,0:T(8,128)S(1)} %get-tuple-element.54.refs_1_), channel_id=1, source_target_pairs={{0,8},{4,12},{8,0},{12,4},{1,9},{5,13},{9,1},{13,5},{2,10},{6,14},... | collective-permute-start | bytes 49160 | tf_op jit(solution)/shard_map/ppermute | solution.py:584
  76.6 1.2 %collective-permute-start.29 = (f32[32,128]{1,0:T(8,128)S(1)}, f32[32,128]{1,0:T(8,128)S(1)}, u32[]{:S(2)}, u32[]{:S(2)}) collective-permute-start(f32[32,128]{1,0:T(8,128)S(1)} %get-tuple-element.54.refs_1_), channel_id=1, source_target_pairs={{0,12},{4,0},{8,4},{12,8},{1,13},{5,1},{9,5},{13,9},{2,14},{6,2},{... | collective-permute-start | bytes 49160 | tf_op jit(solution)/shard_map/ppermute | solution.py:584
  79.2 1.1 %collective-permute-done.29.refs_4_ = f32[32,128]{1,0:T(8,128)S(1)} collective-permute-done((f32[32,128]{1,0:T(8,128)S(1)}, f32[32,128]{1,0:T(8,128)S(1)}, u32[]{:S(2)}, u32[]{:S(2)}) %collective-permute-start.29) | collective-permute-done | bytes 16416 | tf_op jit(solution)/shard_map/ppermute | solution.py:584
  80.3 2.6 %shard_map.76 = f32[32,2048]{1,0:T(8,128)} custom-call(bf16[128,2048]{1,0:T(8,128)(2,1)S(1)} %get-tuple-element.53.refs_0_, f32[32,128]{1,0:T(8,128)S(1)} %get-tuple-element.54.refs_1_, f32[32,128]{1,0:T(8,128)S(1)} %collective-permute-done.27.refs_2_, f32[32,128]{1,0:T(8,128)S(1)} %collective-permute-done.28.refs_3_, ...), custom_call_target="tpu_custom_call" | custom-call | tf_op jit(solution)/shard_map/pallas_call | solution.py:70
  (55 shorter events, 13.2 us)
Async XLA Ops:
  0.6 9.9 %copy-start.2 = (s32[1,2,8]{2,1,0:T(2,128)S(1)}, s32[1,2,8]{2,1,0:T(2,128)}, u32[]{:S(2)}) copy-start(s32[1,2,8]{2,1,0:T(2,128)} %param.6) | copy-start | bytes 196
  0.6 8.6 %collective-permute-start = (s32[2,8]{1,0:T(2,128)}, s32[2,8]{1,0:T(2,128)S(1)}, u32[]{:S(2)}, u32[]{:S(2)}) collective-permute-start(s32[2,8]{1,0:T(2,128)} %bitcast.7), channel_id=1, source_target_pairs={{0,4},{4,8},{8,12},{12,0},{1,5},{5,9},{9,13},{13,1},{2,6},{6,10},{... | collective-permute-start | bytes 200 | tf_op jit(solution)/shard_map/ppermute | solution.py:584
  3.7 5.6 %collective-permute-start.1 = (s32[2,8]{1,0:T(2,128)}, s32[2,8]{1,0:T(2,128)S(1)}, u32[]{:S(2)}, u32[]{:S(2)}) collective-permute-start(s32[2,8]{1,0:T(2,128)} %bitcast.8), channel_id=1, source_target_pairs={{0,12},{4,0},{8,4},{12,8},{1,13},{5,1},{9,5},{13,9},{2,14},{6,2},{... | collective-permute-start | bytes 200 | tf_op jit(solution)/shard_map/ppermute | solution.py:584
  5.8 4.7 %collective-permute-start.2 = (s32[2,8]{1,0:T(2,128)}, s32[2,8]{1,0:T(2,128)S(1)}, u32[]{:S(2)}, u32[]{:S(2)}) collective-permute-start(s32[2,8]{1,0:T(2,128)} %bitcast.9), channel_id=1, source_target_pairs={{0,8},{4,12},{8,0},{12,4},{1,9},{5,13},{9,1},{13,5},{2,10},{6,14},... | collective-permute-start | bytes 200 | tf_op jit(solution)/shard_map/ppermute | solution.py:584
  12.1 15.2 %collective-permute-start.3 = (bf16[256,384]{1,0:T(8,128)(2,1)S(1)}, bf16[256,384]{1,0:T(8,128)(2,1)S(1)}, u32[]{:S(2)}, u32[]{:S(2)}) collective-permute-start(bf16[256,384]{1,0:T(8,128)(2,1)S(1)} %get-tuple-element.30), channel_id=1, source_target_pairs={{0,8},{4,12},{8,0},{12,4},{1,9},{5,13},{9,1},{13,5},{2,10},{6,14},... | collective-permute-start | bytes 589832 | tf_op jit(solution)/shard_map/ppermute | solution.py:584
  13.1 14.2 %collective-permute-start.4 = (bf16[256,384]{1,0:T(8,128)(2,1)S(1)}, bf16[256,384]{1,0:T(8,128)(2,1)S(1)}, u32[]{:S(2)}, u32[]{:S(2)}) collective-permute-start(bf16[256,384]{1,0:T(8,128)(2,1)S(1)} %get-tuple-element.31), channel_id=1, source_target_pairs={{0,12},{4,0},{8,4},{12,8},{1,13},{5,1},{9,5},{13,9},{2,14},{6,2},{... | collective-permute-start | bytes 589832 | tf_op jit(solution)/shard_map/ppermute | solution.py:584
  14.9 12.4 %collective-permute-start.5 = (bf16[256,384]{1,0:T(8,128)(2,1)S(1)}, bf16[256,384]{1,0:T(8,128)(2,1)S(1)}, u32[]{:S(2)}, u32[]{:S(2)}) collective-permute-start(bf16[256,384]{1,0:T(8,128)(2,1)S(1)} %get-tuple-element.32), channel_id=1, source_target_pairs={{0,4},{4,8},{8,12},{12,0},{1,5},{5,9},{9,13},{13,1},{2,6},{6,10},{... | collective-permute-start | bytes 589832 | tf_op jit(solution)/shard_map/ppermute | solution.py:584
  15.1 13.5 %collective-permute-start.7 = (f32[1024,128]{1,0:T(8,128)S(1)}, f32[1024,128]{1,0:T(8,128)S(1)}, u32[]{:S(2)}, u32[]{:S(2)}) collective-permute-start(f32[1024,128]{1,0:T(8,128)S(1)} %shard_map.59.refs_6_.mine), channel_id=1, source_target_pairs={{0,1},{1,0},{2,3},{3,2},{4,5},{5,4},{6,7},{7,6},{8,9},{9,8},{10,11... | collective-permute-start | bytes 1572872 | tf_op jit(solution)/shard_map/ppermute | solution.py:584
  15.4 13.0 %copy-start.1 = (f32[2048,32]{0,1:T(8,128)S(1)}, f32[2048,32]{0,1:T(8,128)}, u32[]{:S(2)}) copy-start(f32[2048,32]{0,1:T(8,128)} %param.5) | copy-start | bytes 786436
  28.4 2.0 %collective-permute-start.6 = (f32[1024,128]{1,0:T(8,128)S(1)}, f32[1024,128]{1,0:T(8,128)S(1)}, u32[]{:S(2)}, u32[]{:S(2)}) collective-permute-start(f32[1024,128]{1,0:T(8,128)S(1)} %shard_map.62.refs_1_), channel_id=1, source_target_pairs={{0,1},{1,0},{2,3},{3,2},{4,5},{5,4},{6,7},{7,6},{8,9},{9,8},{10,11... | collective-permute-start | bytes 1572872 | tf_op jit(solution)/shard_map/ppermute | solution.py:584
  31.2 9.2 %collective-permute-start.10 = (f32[64,128]{1,0:T(8,128)S(1)}, f32[64,128]{1,0:T(8,128)S(1)}, u32[]{:S(2)}, u32[]{:S(2)}) collective-permute-start(f32[64,128]{1,0:T(8,128)S(1)} %get-tuple-element.37), channel_id=1, source_target_pairs={{0,12},{4,0},{8,4},{12,8},{1,13},{5,1},{9,5},{13,9},{2,14},{6,2},{... | collective-permute-start | bytes 98312 | tf_op jit(solution)/shard_map/ppermute | solution.py:584
  33.4 8.1 %collective-permute-start.8 = (f32[64,128]{1,0:T(8,128)S(1)}, f32[64,128]{1,0:T(8,128)S(1)}, u32[]{:S(2)}, u32[]{:S(2)}) collective-permute-start(f32[64,128]{1,0:T(8,128)S(1)} %get-tuple-element.37), channel_id=1, source_target_pairs={{0,4},{4,8},{8,12},{12,0},{1,5},{5,9},{9,13},{13,1},{2,6},{6,10},{... | collective-permute-start | bytes 98312 | tf_op jit(solution)/shard_map/ppermute | solution.py:584
  35.5 6.1 %collective-permute-start.9 = (f32[64,128]{1,0:T(8,128)S(1)}, f32[64,128]{1,0:T(8,128)S(1)}, u32[]{:S(2)}, u32[]{:S(2)}) collective-permute-start(f32[64,128]{1,0:T(8,128)S(1)} %get-tuple-element.37), channel_id=1, source_target_pairs={{0,8},{4,12},{8,0},{12,4},{1,9},{5,13},{9,1},{13,5},{2,10},{6,14},... | collective-permute-start | bytes 98312 | tf_op jit(solution)/shard_map/ppermute | solution.py:584
  37.7 7.8 %collective-permute-start.12 = (s16[272,128]{1,0:T(8,128)(2,1)S(1)}, s16[272,128]{1,0:T(8,128)(2,1)S(1)}, u32[]{:S(2)}, u32[]{:S(2)}) collective-permute-start(s16[272,128]{1,0:T(8,128)(2,1)S(1)} %get-tuple-element.43), channel_id=1, source_target_pairs={{0,4},{4,8},{8,12},{12,0},{1,5},{5,9},{9,13},{13,1},{2,6},{6,10},{... | collective-permute-start | bytes 208904 | tf_op jit(solution)/shard_map/ppermute | solution.py:584
  37.8 8.3 %collective-permute-start.13 = (s16[272,128]{1,0:T(8,128)(2,1)S(1)}, s16[272,128]{1,0:T(8,128)(2,1)S(1)}, u32[]{:S(2)}, u32[]{:S(2)}) collective-permute-start(s16[272,128]{1,0:T(8,128)(2,1)S(1)} %get-tuple-element.44), channel_id=1, source_target_pairs={{0,8},{4,12},{8,0},{12,4},{1,9},{5,13},{9,1},{13,5},{2,10},{6,14},... | collective-permute-start | bytes 208904 | tf_op jit(solution)/shard_map/ppermute | solution.py:584
  40.4 5.8 %collective-permute-start.14 = (s16[272,128]{1,0:T(8,128)(2,1)S(1)}, s16[272,128]{1,0:T(8,128)(2,1)S(1)}, u32[]{:S(2)}, u32[]{:S(2)}) collective-permute-start(s16[272,128]{1,0:T(8,128)(2,1)S(1)} %get-tuple-element.45), channel_id=1, source_target_pairs={{0,12},{4,0},{8,4},{12,8},{1,13},{5,1},{9,5},{13,9},{2,14},{6,2},{... | collective-permute-start | bytes 208904 | tf_op jit(solution)/shard_map/ppermute | solution.py:584
  41.6 4.0 %collective-permute-start.11 = (f32[64,128]{1,0:T(8,128)S(1)}, f32[64,128]{1,0:T(8,128)S(1)}, u32[]{:S(2)}, u32[]{:S(2)}) collective-permute-start(f32[64,128]{1,0:T(8,128)S(1)} %add_add_fusion.refs_1_), channel_id=1, source_target_pairs={{0,2},{2,0},{1,3},{3,1},{4,6},{6,4},{5,7},{7,5},{8,10},{10,8},{9,1... | collective-permute-start | bytes 98312 | tf_op jit(solution)/shard_map/ppermute | solution.py:592
  46.2 1.5 %collective-permute-start.15 = (bf16[1,256,128]{2,1,0:T(8,128)(2,1)S(1)}, bf16[1,256,128]{2,1,0:T(8,128)(2,1)S(1)}, u32[]{:S(2)}, u32[]{:S(2)}) collective-permute-start(bf16[1,256,128]{2,1,0:T(8,128)(2,1)S(1)} %get-tuple-element.46.refs_4_.refs_7_), channel_id=1, source_target_pairs={{0,1},{1,0},{2,3},{3,2},{4,5},{5,4},{6,7},{7,6},{8,9},{9,8},{10,11... | collective-permute-start | bytes 196616 | tf_op jit(solution)/shard_map/ppermute | solution.py:584
  46.3 1.4 %collective-permute-start.16 = (bf16[1,256,128]{2,1,0:T(8,128)(2,1)S(1)}, bf16[1,256,128]{2,1,0:T(8,128)(2,1)S(1)}, u32[]{:S(2)}, u32[]{:S(2)}) collective-permute-start(bf16[1,256,128]{2,1,0:T(8,128)(2,1)S(1)} %get-tuple-element.47.refs_5_.refs_8_), channel_id=1, source_target_pairs={{0,1},{1,0},{2,3},{3,2},{4,5},{5,4},{6,7},{7,6},{8,9},{9,8},{10,11... | collective-permute-start | bytes 196616 | tf_op jit(solution)/shard_map/ppermute | solution.py:584
  46.8 1.3 %collective-permute-start.17 = (bf16[1,256,128]{2,1,0:T(8,128)(2,1)S(1)}, bf16[1,256,128]{2,1,0:T(8,128)(2,1)S(1)}, u32[]{:S(2)}, u32[]{:S(2)}) collective-permute-start(bf16[1,256,128]{2,1,0:T(8,128)(2,1)S(1)} %get-tuple-element.48.refs_6_.refs_9_), channel_id=1, source_target_pairs={{0,1},{1,0},{2,3},{3,2},{4,5},{5,4},{6,7},{7,6},{8,9},{9,8},{10,11... | collective-permute-start | bytes 196616 | tf_op jit(solution)/shard_map/ppermute | solution.py:584
  49.1 5.8 %collective-permute-start.18 = (s16[32,2176]{1,0:T(8,128)(2,1)S(1)}, s16[32,2176]{1,0:T(8,128)(2,1)S(1)}, u32[]{:S(2)}, u32[]{:S(2)}) collective-permute-start(s16[32,2176]{1,0:T(8,128)(2,1)S(1)} %shard_map.68.refs_2_), channel_id=1, source_target_pairs={{0,2},{2,0},{1,3},{3,1},{4,6},{6,4},{5,7},{7,5},{8,10},{10,8},{9,1... | collective-permute-start | bytes 417800 | tf_op jit(solution)/shard_map/ppermute | solution.py:592
  55.5 4.5 %collective-permute-start.19 = (f32[32,2048]{1,0:T(8,128)S(1)}, f32[32,2048]{1,0:T(8,128)S(1)}, u32[]{:S(2)}, u32[]{:S(2)}) collective-permute-start(f32[32,2048]{1,0:T(8,128)S(1)} %get-tuple-element.49.refs_0_.refs_3_), channel_id=1, source_target_pairs={{0,1},{1,0},{2,3},{3,2},{4,5},{5,4},{6,7},{7,6},{8,9},{9,8},{10,11... | collective-permute-start | bytes 786440 | tf_op jit(solution)/shard_map/ppermute | solution.py:584
  55.6 6.2 %collective-permute-start.20 = (s16[144,128]{1,0:T(8,128)(2,1)S(1)}, s16[144,128]{1,0:T(8,128)(2,1)S(1)}, u32[]{:S(2)}, u32[]{:S(2)}) collective-permute-start(s16[144,128]{1,0:T(8,128)(2,1)S(1)} %get-tuple-element.50), channel_id=1, source_target_pairs={{0,4},{4,8},{8,12},{12,0},{1,5},{5,9},{9,13},{13,1},{2,6},{6,10},{... | collective-permute-start | bytes 110600 | tf_op jit(solution)/shard_map/ppermute | solution.py:584
  57.0 5.9 %collective-permute-start.21 = (s16[144,128]{1,0:T(8,128)(2,1)S(1)}, s16[144,128]{1,0:T(8,128)(2,1)S(1)}, u32[]{:S(2)}, u32[]{:S(2)}) collective-permute-start(s16[144,128]{1,0:T(8,128)(2,1)S(1)} %get-tuple-element.51), channel_id=1, source_target_pairs={{0,8},{4,12},{8,0},{12,4},{1,9},{5,13},{9,1},{13,5},{2,10},{6,14},... | collective-permute-start | bytes 110600 | tf_op jit(solution)/shard_map/ppermute | solution.py:584
  58.8 4.7 %collective-permute-start.22 = (s16[144,128]{1,0:T(8,128)(2,1)S(1)}, s16[144,128]{1,0:T(8,128)(2,1)S(1)}, u32[]{:S(2)}, u32[]{:S(2)}) collective-permute-start(s16[144,128]{1,0:T(8,128)(2,1)S(1)} %get-tuple-element.52), channel_id=1, source_target_pairs={{0,12},{4,0},{8,4},{12,8},{1,13},{5,1},{9,5},{13,9},{2,14},{6,2},{... | collective-permute-start | bytes 110600 | tf_op jit(solution)/shard_map/ppermute | solution.py:584
  60.4 4.0 %collective-permute-start.23 = (f32[32,128]{1,0:T(8,128)S(1)}, f32[32,128]{1,0:T(8,128)S(1)}, u32[]{:S(2)}, u32[]{:S(2)}) collective-permute-start(f32[32,128]{1,0:T(8,128)S(1)} %shard_map.70.refs_2_), channel_id=1, source_target_pairs={{0,4},{4,0},{8,12},{12,8},{1,5},{5,1},{9,13},{13,9},{2,6},{6,2},{1... | collective-permute-start | bytes 49160 | tf_op jit(solution)/shard_map/ppermute | solution.py:592
  64.6 6.2 %collective-permute-start.24 = (s16[32,2176]{1,0:T(8,128)(2,1)S(1)}, s16[32,2176]{1,0:T(8,128)(2,1)S(1)}, u32[]{:S(2)}, u32[]{:S(2)}) collective-permute-start(s16[32,2176]{1,0:T(8,128)(2,1)S(1)} %shard_map.72.refs_1_), channel_id=1, source_target_pairs={{0,2},{2,0},{1,3},{3,1},{4,6},{6,4},{5,7},{7,5},{8,10},{10,8},{9,1... | collective-permute-start | bytes 417800 | tf_op jit(solution)/shard_map/ppermute | solution.py:592
  66.2 4.6 %collective-permute-start.25 = (f32[32,128]{1,0:T(8,128)S(1)}, f32[32,128]{1,0:T(8,128)S(1)}, u32[]{:S(2)}, u32[]{:S(2)}) collective-permute-start(f32[32,128]{1,0:T(8,128)S(1)} %add.18.after.refs_0_), channel_id=1, source_target_pairs={{0,8},{4,12},{8,0},{12,4},{1,9},{5,13},{9,1},{13,5},{2,10},{6,14},... | collective-permute-start | bytes 49160 | tf_op jit(solution)/shard_map/ppermute | solution.py:592
  70.9 1.8 %collective-permute-start.26 = (f32[32,2048]{1,0:T(8,128)S(1)}, f32[32,2048]{1,0:T(8,128)S(1)}, u32[]{:S(2)}, u32[]{:S(2)}) collective-permute-start(f32[32,2048]{1,0:T(8,128)S(1)} %shard_map.73.after.refs_1_), channel_id=1, source_target_pairs={{0,1},{1,0},{2,3},{3,2},{4,5},{5,4},{6,7},{7,6},{8,9},{9,8},{10,11... | collective-permute-start | bytes 786440 | tf_op jit(solution)/shard_map/ppermute | solution.py:584
  73.5 5.6 %collective-permute-start.27 = (f32[32,128]{1,0:T(8,128)S(1)}, f32[32,128]{1,0:T(8,128)S(1)}, u32[]{:S(2)}, u32[]{:S(2)}) collective-permute-start(f32[32,128]{1,0:T(8,128)S(1)} %get-tuple-element.54.refs_1_), channel_id=1, source_target_pairs={{0,4},{4,8},{8,12},{12,0},{1,5},{5,9},{9,13},{13,1},{2,6},{6,10},{... | collective-permute-start | bytes 49160 | tf_op jit(solution)/shard_map/ppermute | solution.py:584
  74.3 4.8 %collective-permute-start.28 = (f32[32,128]{1,0:T(8,128)S(1)}, f32[32,128]{1,0:T(8,128)S(1)}, u32[]{:S(2)}, u32[]{:S(2)}) collective-permute-start(f32[32,128]{1,0:T(8,128)S(1)} %get-tuple-element.54.refs_1_), channel_id=1, source_target_pairs={{0,8},{4,12},{8,0},{12,4},{1,9},{5,13},{9,1},{13,5},{2,10},{6,14},... | collective-permute-start | bytes 49160 | tf_op jit(solution)/shard_map/ppermute | solution.py:584
  76.6 3.7 %collective-permute-start.29 = (f32[32,128]{1,0:T(8,128)S(1)}, f32[32,128]{1,0:T(8,128)S(1)}, u32[]{:S(2)}, u32[]{:S(2)}) collective-permute-start(f32[32,128]{1,0:T(8,128)S(1)} %get-tuple-element.54.refs_1_), channel_id=1, source_target_pairs={{0,12},{4,0},{8,4},{12,8},{1,13},{5,1},{9,5},{13,9},{2,14},{6,2},{... | collective-permute-start | bytes 49160 | tf_op jit(solution)/shard_map/ppermute | solution.py:584
  (1 other events, 1.4 us)

commit v21 on v17

--- a/solution.py
+++ b/solution.py
@@ -231,8 +231,9 @@
     sends, (idx, left) = refs[row_count + 3 : -2], refs[-2:]
     row = me[0]
     for i in range(slots):
-        for line in (0, 1, 2, 4, 5):
+        for line in (0, 1, 4, 5):
             idx[line, i] = 0
+        idx[3, i] = slots
     lists = dict(zip(list_order, [one.ready() for one in lists]))
 
     def each(step, start):
@@ -243,33 +244,31 @@
             lax.fori_loop(0, slots, step, start)
 
     for k in range(row_count):
-        live_count = lists[k][2, 0]
-
-        def step(s, counts, k=k, live_count=live_count):
+
+        def step(s, counts, k=k):
             near = lists[k][0, s]
             far = lists[k][1, s]
             owner = quotient(far, blocks_here)
-            live = s < live_count
-            hit = live & (owner == row)
-            slot = jnp.where(hit, k * capacity + counts[0], slots)
+            if k > 0:
+                hit = (owner == row) & (counts[0] < capacity)
+                slot = jnp.where(hit, k * capacity + counts[0], slots)
+                idx[4, slot] = far - row * blocks_here
+                idx[5, slot] = near
+                return (counts[0] + hit.astype(jnp.int32),)
+            shift = remainder(owner - row + row_count, row_count)
+            rank = counts[0]
+            for d in range(1, row_count):
+                rank = jnp.where(shift == d, counts[d], rank)
+            slot = jnp.where(rank < capacity, shift * capacity + rank, slots)
+            idx[0, slot] = near - row * blocks_here
+            idx[1, slot] = far
+            idx[3, slot] = s
+            slot = jnp.where(shift == 0, slot, slots)
             idx[4, slot] = far - row * blocks_here
             idx[5, slot] = near
-            if k > 0:
-                return (counts[0] + hit.astype(jnp.int32),)
-            shift = remainder(owner - row + row_count, row_count)
-            rank = counts[1]
-            for d in range(1, row_count):
-                rank = jnp.where(shift == d, counts[1 + d], rank)
-            slot = jnp.where(live, shift * capacity + rank, slots)
-            idx[0, slot] = near - row * blocks_here
-            idx[1, slot] = far
-            idx[2, slot] = 1
-            more = tuple(
-                counts[1 + d] + (live & (shift == d)).astype(jnp.int32) for d in range(row_count)
-            )
-            return (counts[0] + hit.astype(jnp.int32), *more)
-
-        each(step, (jnp.int32(0),) * (1 + row_count if k == 0 else 1))
+            return tuple(counts[d] + (shift == d).astype(jnp.int32) for d in range(row_count))
+
+        each(step, (jnp.int32(0),) * (row_count if k == 0 else 1))
     leave = pltpu.make_async_copy(idx, idx_out, left)
     leave.start()
     for k in range(1, row_count):
@@ -337,7 +336,7 @@
         sums[i : i + 1, :] = jnp.sum(tile, axis=0, keepdims=True)
 
 
-def pair_tile_body(dims, me, idx, mine, other, self_sums, codes, powers, parts, near_tiles, home_tiles, table, *sends):
+def pair_tile_body(dims, me, idx, live_count, mine, other, self_sums, codes, powers, parts, near_tiles, home_tiles, table, *sends):
     row_count, capacity, per_core, blocks_here, tile_count = dims
     row, tile_index, core = me[0], me[1], me[2]
     table[...] = jnp.zeros(table.shape, F32)
@@ -350,12 +349,13 @@
 
     all_tiles = jnp.exp(-kernel_gamma * (mine[...] + other[...] - 2.0))
     idx = idx.ready()
+    live_count = live_count.ready()[0]
     for k in range(row_count):
         tiles = []
         for j in range(capacity):
             slot = k * capacity + j
             tile = all_tiles[slot * BLOCK : (slot + 1) * BLOCK]
-            tile = jnp.where(idx[2, slot] > 0, tile, 0.0)
+            tile = jnp.where(idx[3, slot] < live_count, tile, 0.0)
             turned = tile.T
             near_tiles[slot] = pack(turned)
             add(row * blocks_here + idx[0, slot], jnp.sum(turned, axis=0, keepdims=True))
@@ -615,11 +615,8 @@
     block_count = row_count * blocks_here
     others = range(1, row_count)
 
-    own_list = jnp.concatenate(
-        [pair_list[0], jnp.broadcast_to(pair_count[:, None], (1, slots))], axis=0
-    )
-    lists = row_terms(own_list, row_count)
     list_order = [0, *sorted(others, key=lambda k: k * (row_count - k))]
+    lists = [shift_by(pair_list[0], "rows", row_count, k) if k else pair_list[0] for k in list_order]
     self_part = call(
         functools.partial(self_distance_body, own_blocks, tile_count),
         sds((own_blocks * BLOCK, BLOCK), F32),
@@ -628,7 +625,7 @@
     planned = call(
         functools.partial(plan_body, (row_count, capacity, slots, blocks_here), list_order),
         [sds((6, slots + 1), jnp.int32)] + [sds((capacity * BLOCK, half_features), BF16) for _ in others],
-        [ME, *[lists[k] for k in list_order], embeddings, self_part],
+        [ME, *lists, embeddings, self_part],
         late=range(1, 1 + row_count),
         any_in=(row_count + 2,),
         any_out=(0,),
@@ -665,8 +662,8 @@
         functools.partial(pair_tile_body, dims),
         [sds((slots, 2 * BLOCK, BLOCK), BF16), sds((capacity, 2 * BLOCK, BLOCK), BF16), table]
         + [sds((per_core * BLOCK + picked + CODE_ROWS, BLOCK), jnp.int16) for _ in others],
-        [ME, idx, pair_part, pair_other, self_sums, *start_codes],
-        late=(1,),
+        [ME, idx, pair_count, pair_part, pair_other, self_sums, *start_codes],
+        late=(1, 2),
     )
     near_tiles, home_tiles, degrees, sends = tiles[0], tiles[1], tiles[2], tiles[3:]
     degrees = functools.reduce(jnp.add, row_terms(degrees, row_count))

time: 84.2 us -> 82.9 us (0.985)
  transfers between devices with their start and end apart: 30 -> 30, of which waited for: 13 -> 13; matrix products, arithmetic and copies ran while one was open for 1% -> 1% of each run, Pallas kernels for 7% -> 8%
where the time goes in v21:
time: 82.9 us; the launch traced here: 82.8 us
  starting transfers between devices  36 us (43%)
  waiting for transfers between devices  29.2 us (35%)
  Pallas kernels  14 us (17%)
  local copies, waits for them, and re-layouts  2.02 us (2%)
  between operations  1.52 us (2%)
    ppermute x25, starting transfers between devices, shift_by(): lax.ppermute(value, axes, [(i, (i + shift) % size) for i in range(size)])  29.3 us
    ppermute x25, waiting for transfers between devices, shift_by(): lax.ppermute(value, axes, [(i, (i + shift) % size) for i in range(size)])  19.2 us
    pallas_call x18, Pallas kernels, call(): pl.pallas_call(body, out_shape=shapes, in_specs=[ANY if i in any_in else...  14 us
    ppermute x5, waiting for transfers between devices, pair_step(): lax.ppermute(value, name, [(i, i ^ flip) for i in range(lax.axis_size(nam...  10 us
    ppermute x5, starting transfers between devices, pair_step(): lax.ppermute(value, name, [(i, i ^ flip) for i in range(lax.axis_size(nam...  6.64 us
  transfers between devices with their start and end apart: 30, of which 13 were waited for; matrix products, arithmetic and copies ran while one was open for 1% of the time, Pallas kernels for 8%

profile of v21, /device:TPU:0, one launch (start us, length us, event | category | flops | bytes accessed | tf_op | source)
XLA Modules:
  0.0 82.8 jit_solution(7117996774111326306)
XLA Ops:
  0.6 3.1 %collective-permute-start = (s32[2,8]{1,0:T(2,128)}, s32[2,8]{1,0:T(2,128)S(1)}, u32[]{:S(2)}, u32[]{:S(2)}) collective-permute-start(s32[2,8]{1,0:T(2,128)} %bitcast.7), channel_id=1, source_target_pairs={{0,4},{4,8},{8,12},{12,0},{1,5},{5,9},{9,13},{13,1},{2,6},{6,10},{... | collective-permute-start | bytes 200 | tf_op jit(solution)/shard_map/ppermute | solution.py:580
  3.7 2.1 %collective-permute-start.1 = (s32[2,8]{1,0:T(2,128)}, s32[2,8]{1,0:T(2,128)S(1)}, u32[]{:S(2)}, u32[]{:S(2)}) collective-permute-start(s32[2,8]{1,0:T(2,128)} %bitcast.8), channel_id=1, source_target_pairs={{0,12},{4,0},{8,4},{12,8},{1,13},{5,1},{9,5},{13,9},{2,14},{6,2},{... | collective-permute-start | bytes 200 | tf_op jit(solution)/shard_map/ppermute | solution.py:580
  6.8 1.4 %copy-done = bf16[2048,384]{1,0:T(8,128)(2,1)S(1)} copy-done((bf16[2048,384]{1,0:T(8,128)(2,1)S(1)}, bf16[2048,384]{1,0:T(8,128)(2,1)}, u32[]{:S(2)}) %copy-start) | copy-done | bytes 1572888
  8.7 1.8 %collective-permute-done.2.refs_3_ = s32[2,8]{1,0:T(2,128)S(1)} collective-permute-done((s32[2,8]{1,0:T(2,128)}, s32[2,8]{1,0:T(2,128)S(1)}, u32[]{:S(2)}, u32[]{:S(2)}) %collective-permute-start.2) | collective-permute-done | bytes 96 | tf_op jit(solution)/shard_map/ppermute | solution.py:580
  10.5 1.5 %shard_map.60 = (s32[6,9]{1,0:T(8,128)S(1)}, bf16[256,384]{1,0:T(8,128)(2,1)S(1)}, bf16[256,384]{1,0:T(8,128)(2,1)S(1)}, bf16[256,384]{1,0:T(8,128)(2,1)S(1)}) custom-call(s32[2,8]{1,0:T(2,128)S(1)} %bitcast.10, s32[2,8]{1,0:T(2,128)S(1)} %collective-permute-done.refs_1_, s32[2,8]{1,0:T(2,128)S(1)} %collective-permute-done.1.refs_2_, ...), custom_call_target="tpu_custom_call" | custom-call | tf_op jit(solution)/shard_map/pallas_call | solution.py:70
  12.0 1.0 %collective-permute-start.3 = (bf16[256,384]{1,0:T(8,128)(2,1)S(1)}, bf16[256,384]{1,0:T(8,128)(2,1)S(1)}, u32[]{:S(2)}, u32[]{:S(2)}) collective-permute-start(bf16[256,384]{1,0:T(8,128)(2,1)S(1)} %get-tuple-element.30), channel_id=1, source_target_pairs={{0,8},{4,12},{8,0},{12,4},{1,9},{5,13},{9,1},{13,5},{2,10},{6,14},... | collective-permute-start | bytes 589832 | tf_op jit(solution)/shard_map/ppermute | solution.py:580
  13.0 1.3 %collective-permute-start.4 = (bf16[256,384]{1,0:T(8,128)(2,1)S(1)}, bf16[256,384]{1,0:T(8,128)(2,1)S(1)}, u32[]{:S(2)}, u32[]{:S(2)}) collective-permute-start(bf16[256,384]{1,0:T(8,128)(2,1)S(1)} %get-tuple-element.31), channel_id=1, source_target_pairs={{0,12},{4,0},{8,4},{12,8},{1,13},{5,1},{9,5},{13,9},{2,14},{6,2},{... | collective-permute-start | bytes 589832 | tf_op jit(solution)/shard_map/ppermute | solution.py:580
  15.4 11.5 %collective-permute-done.3.refs_3_ = bf16[256,384]{1,0:T(8,128)(2,1)S(1)} collective-permute-done((bf16[256,384]{1,0:T(8,128)(2,1)S(1)}, bf16[256,384]{1,0:T(8,128)(2,1)S(1)}, u32[]{:S(2)}, u32[]{:S(2)}) %collective-permute-start.3) | collective-permute-done | bytes 196640 | tf_op jit(solution)/shard_map/ppermute | solution.py:580
  26.9 1.1 %shard_map.62.refs_2_ = f32[1024,128]{1,0:T(8,128)S(1)} custom-call(s32[6,9]{1,0:T(8,128)S(1)} %get-tuple-element.29.after.refs_0_, bf16[2048,384]{1,0:T(8,128)(2,1)S(1)} %copy-done, f32[2048,128]{1,0:T(8,128)S(1)} %shard_map.61.refs_2_, bf16[256,384]{1,0:T(8,128)(2,1)S(1)} %collective-permute-done.3.refs_3_, ...), custom_call_target="tpu_custom_call" | custom-call | tf_op jit(solution)/shard_map/pallas_call | solution.py:70
  30.9 2.3 %collective-permute-start.10 = (f32[64,128]{1,0:T(8,128)S(1)}, f32[64,128]{1,0:T(8,128)S(1)}, u32[]{:S(2)}, u32[]{:S(2)}) collective-permute-start(f32[64,128]{1,0:T(8,128)S(1)} %get-tuple-element.37), channel_id=1, source_target_pairs={{0,12},{4,0},{8,4},{12,8},{1,13},{5,1},{9,5},{13,9},{2,14},{6,2},{... | collective-permute-start | bytes 98312 | tf_op jit(solution)/shard_map/ppermute | solution.py:580
  33.2 2.1 %collective-permute-start.8 = (f32[64,128]{1,0:T(8,128)S(1)}, f32[64,128]{1,0:T(8,128)S(1)}, u32[]{:S(2)}, u32[]{:S(2)}) collective-permute-start(f32[64,128]{1,0:T(8,128)S(1)} %get-tuple-element.37), channel_id=1, source_target_pairs={{0,4},{4,8},{8,12},{12,0},{1,5},{5,9},{9,13},{13,1},{2,6},{6,10},{... | collective-permute-start | bytes 98312 | tf_op jit(solution)/shard_map/ppermute | solution.py:580
  35.3 2.3 %collective-permute-start.9 = (f32[64,128]{1,0:T(8,128)S(1)}, f32[64,128]{1,0:T(8,128)S(1)}, u32[]{:S(2)}, u32[]{:S(2)}) collective-permute-start(f32[64,128]{1,0:T(8,128)S(1)} %get-tuple-element.37), channel_id=1, source_target_pairs={{0,8},{4,12},{8,0},{12,4},{1,9},{5,13},{9,1},{13,5},{2,10},{6,14},... | collective-permute-start | bytes 98312 | tf_op jit(solution)/shard_map/ppermute | solution.py:580
  37.7 2.6 %collective-permute-start.13 = (s16[272,128]{1,0:T(8,128)(2,1)S(1)}, s16[272,128]{1,0:T(8,128)(2,1)S(1)}, u32[]{:S(2)}, u32[]{:S(2)}) collective-permute-start(s16[272,128]{1,0:T(8,128)(2,1)S(1)} %get-tuple-element.44), channel_id=1, source_target_pairs={{0,8},{4,12},{8,0},{12,4},{1,9},{5,13},{9,1},{13,5},{2,10},{6,14},... | collective-permute-start | bytes 208904 | tf_op jit(solution)/shard_map/ppermute | solution.py:580
  40.2 1.3 %collective-permute-start.14 = (s16[272,128]{1,0:T(8,128)(2,1)S(1)}, s16[272,128]{1,0:T(8,128)(2,1)S(1)}, u32[]{:S(2)}, u32[]{:S(2)}) collective-permute-start(s16[272,128]{1,0:T(8,128)(2,1)S(1)} %get-tuple-element.45), channel_id=1, source_target_pairs={{0,12},{4,0},{8,4},{12,8},{1,13},{5,1},{9,5},{13,9},{2,14},{6,2},{... | collective-permute-start | bytes 208904 | tf_op jit(solution)/shard_map/ppermute | solution.py:580
  41.5 1.6 %collective-permute-start.11 = (f32[64,128]{1,0:T(8,128)S(1)}, f32[64,128]{1,0:T(8,128)S(1)}, u32[]{:S(2)}, u32[]{:S(2)}) collective-permute-start(f32[64,128]{1,0:T(8,128)S(1)} %add_add_fusion.refs_1_), channel_id=1, source_target_pairs={{0,2},{2,0},{1,3},{3,1},{4,6},{6,4},{5,7},{7,5},{8,10},{10,8},{9,1... | collective-permute-start | bytes 98312 | tf_op jit(solution)/shard_map/ppermute | solution.py:588
  43.1 2.4 %collective-permute-done.11.refs_2_.refs_3_ = f32[64,128]{1,0:T(8,128)S(1)} collective-permute-done((f32[64,128]{1,0:T(8,128)S(1)}, f32[64,128]{1,0:T(8,128)S(1)}, u32[]{:S(2)}, u32[]{:S(2)}) %collective-permute-start.11) | collective-permute-done | bytes 32800 | tf_op jit(solution)/shard_map/ppermute | solution.py:588
  47.9 1.0 %shard_map.68.refs_2_ = s16[32,2176]{1,0:T(8,128)(2,1)S(1)} custom-call(s32[6,9]{1,0:T(8,128)S(1)} %get-tuple-element.29.after.refs_0_, f32[64,128]{1,0:T(8,128)S(1)} %get-tuple-element.41.refs_1_.refs_0_, f32[32,2048]{1,0:T(8,128)S(1)} %get-tuple-element.42.refs_2_, bf16[8,256,128]{2,1,0:T(8,128)(2,1)S(1)} %get-tuple-element.38.refs_4_.refs_3_.refs_6_, ...), custom_call_target="tpu_custom_call" | custom-call | tf_op jit(solution)/shard_map/pallas_call | solution.py:70
  48.9 1.6 %collective-permute-start.18 = (s16[32,2176]{1,0:T(8,128)(2,1)S(1)}, s16[32,2176]{1,0:T(8,128)(2,1)S(1)}, u32[]{:S(2)}, u32[]{:S(2)}) collective-permute-start(s16[32,2176]{1,0:T(8,128)(2,1)S(1)} %shard_map.68.refs_2_), channel_id=1, source_target_pairs={{0,2},{2,0},{1,3},{3,1},{4,6},{6,4},{5,7},{7,5},{8,10},{10,8},{9,1... | collective-permute-start | bytes 417800 | tf_op jit(solution)/shard_map/ppermute | solution.py:588
  50.5 4.2 %collective-permute-done.18.refs_3_ = s16[32,2176]{1,0:T(8,128)(2,1)S(1)} collective-permute-done((s16[32,2176]{1,0:T(8,128)(2,1)S(1)}, s16[32,2176]{1,0:T(8,128)(2,1)S(1)}, u32[]{:S(2)}, u32[]{:S(2)}) %collective-permute-start.18) | collective-permute-done | bytes 139296 | tf_op jit(solution)/shard_map/ppermute | solution.py:588
  55.5 1.4 %collective-permute-start.20 = (s16[144,128]{1,0:T(8,128)(2,1)S(1)}, s16[144,128]{1,0:T(8,128)(2,1)S(1)}, u32[]{:S(2)}, u32[]{:S(2)}) collective-permute-start(s16[144,128]{1,0:T(8,128)(2,1)S(1)} %get-tuple-element.50), channel_id=1, source_target_pairs={{0,4},{4,8},{8,12},{12,0},{1,5},{5,9},{9,13},{13,1},{2,6},{6,10},{... | collective-permute-start | bytes 110600 | tf_op jit(solution)/shard_map/ppermute | solution.py:580
  56.9 1.8 %collective-permute-start.21 = (s16[144,128]{1,0:T(8,128)(2,1)S(1)}, s16[144,128]{1,0:T(8,128)(2,1)S(1)}, u32[]{:S(2)}, u32[]{:S(2)}) collective-permute-start(s16[144,128]{1,0:T(8,128)(2,1)S(1)} %get-tuple-element.51), channel_id=1, source_target_pairs={{0,8},{4,12},{8,0},{12,4},{1,9},{5,13},{9,1},{13,5},{2,10},{6,14},... | collective-permute-start | bytes 110600 | tf_op jit(solution)/shard_map/ppermute | solution.py:580
  58.6 1.3 %collective-permute-start.22 = (s16[144,128]{1,0:T(8,128)(2,1)S(1)}, s16[144,128]{1,0:T(8,128)(2,1)S(1)}, u32[]{:S(2)}, u32[]{:S(2)}) collective-permute-start(s16[144,128]{1,0:T(8,128)(2,1)S(1)} %get-tuple-element.52), channel_id=1, source_target_pairs={{0,12},{4,0},{8,4},{12,8},{1,13},{5,1},{9,5},{13,9},{2,14},{6,2},{... | collective-permute-start | bytes 110600 | tf_op jit(solution)/shard_map/ppermute | solution.py:580
  61.6 1.1 %collective-permute-done.21.refs_14_ = s16[144,128]{1,0:T(8,128)(2,1)S(1)} collective-permute-done((s16[144,128]{1,0:T(8,128)(2,1)S(1)}, s16[144,128]{1,0:T(8,128)(2,1)S(1)}, u32[]{:S(2)}, u32[]{:S(2)}) %collective-permute-start.21) | collective-permute-done | bytes 36896 | tf_op jit(solution)/shard_map/ppermute | solution.py:580
  63.3 1.0 %shard_map.71.total = f32[32,2048]{1,0:T(8,128)S(1)} custom-call(s32[6,9]{1,0:T(8,128)S(1)} %get-tuple-element.29.after.refs_0_, f32[64,128]{1,0:T(8,128)S(1)} %get-tuple-element.41.refs_1_.refs_0_, f32[32,128]{1,0:T(8,128)S(1)} %shard_map.70.refs_2_, f32[32,2048]{1,0:T(8,128)S(1)} %get-tuple-element.49.refs_0_.refs_3_, ...), custom_call_target="tpu_custom_call" | custom-call | tf_op jit(solution)/shard_map/pallas_call | solution.py:70
  64.5 1.6 %collective-permute-start.24 = (s16[32,2176]{1,0:T(8,128)(2,1)S(1)}, s16[32,2176]{1,0:T(8,128)(2,1)S(1)}, u32[]{:S(2)}, u32[]{:S(2)}) collective-permute-start(s16[32,2176]{1,0:T(8,128)(2,1)S(1)} %shard_map.72.refs_1_), channel_id=1, source_target_pairs={{0,2},{2,0},{1,3},{3,1},{4,6},{6,4},{5,7},{7,5},{8,10},{10,8},{9,1... | collective-permute-start | bytes 417800 | tf_op jit(solution)/shard_map/ppermute | solution.py:588
  66.0 1.3 %collective-permute-start.25 = (f32[32,128]{1,0:T(8,128)S(1)}, f32[32,128]{1,0:T(8,128)S(1)}, u32[]{:S(2)}, u32[]{:S(2)}) collective-permute-start(f32[32,128]{1,0:T(8,128)S(1)} %add.18.after.refs_0_), channel_id=1, source_target_pairs={{0,8},{4,12},{8,0},{12,4},{1,9},{5,13},{9,1},{13,5},{2,10},{6,14},... | collective-permute-start | bytes 49160 | tf_op jit(solution)/shard_map/ppermute | solution.py:588
  67.3 3.4 %collective-permute-done.25.refs_3_.refs_1_ = f32[32,128]{1,0:T(8,128)S(1)} collective-permute-done((f32[32,128]{1,0:T(8,128)S(1)}, f32[32,128]{1,0:T(8,128)S(1)}, u32[]{:S(2)}, u32[]{:S(2)}) %collective-permute-start.25) | collective-permute-done | bytes 16416 | tf_op jit(solution)/shard_map/ppermute | solution.py:588
  70.8 1.7 %shard_map.74.refs_0_ = f32[64,64]{1,0:T(8,128)S(1)} custom-call(f32[32,2048]{1,0:T(8,128)S(1)} %shard_map.73.after.refs_1_, f32[32,128]{1,0:T(8,128)S(1)} %add.18.after.refs_0_, f32[32,128]{1,0:T(8,128)S(1)} %collective-permute-done.25.refs_3_.refs_1_), custom_call_target="tpu_custom_call" | custom-call | tf_op jit(solution)/shard_map/pallas_call | solution.py:70
  74.2 2.2 %collective-permute-start.28 = (f32[32,128]{1,0:T(8,128)S(1)}, f32[32,128]{1,0:T(8,128)S(1)}, u32[]{:S(2)}, u32[]{:S(2)}) collective-permute-start(f32[32,128]{1,0:T(8,128)S(1)} %get-tuple-element.54.refs_1_), channel_id=1, source_target_pairs={{0,8},{4,12},{8,0},{12,4},{1,9},{5,13},{9,1},{13,5},{2,10},{6,14},... | collective-permute-start | bytes 49160 | tf_op jit(solution)/shard_map/ppermute | solution.py:580
  76.4 1.2 %collective-permute-start.29 = (f32[32,128]{1,0:T(8,128)S(1)}, f32[32,128]{1,0:T(8,128)S(1)}, u32[]{:S(2)}, u32[]{:S(2)}) collective-permute-start(f32[32,128]{1,0:T(8,128)S(1)} %get-tuple-element.54.refs_1_), channel_id=1, source_target_pairs={{0,12},{4,0},{8,4},{12,8},{1,13},{5,1},{9,5},{13,9},{2,14},{6,2},{... | collective-permute-start | bytes 49160 | tf_op jit(solution)/shard_map/ppermute | solution.py:580
  79.0 1.2 %collective-permute-done.29.refs_4_ = f32[32,128]{1,0:T(8,128)S(1)} collective-permute-done((f32[32,128]{1,0:T(8,128)S(1)}, f32[32,128]{1,0:T(8,128)S(1)}, u32[]{:S(2)}, u32[]{:S(2)}) %collective-permute-start.29) | collective-permute-done | bytes 16416 | tf_op jit(solution)/shard_map/ppermute | solution.py:580
  80.2 2.6 %shard_map.76 = f32[32,2048]{1,0:T(8,128)} custom-call(bf16[128,2048]{1,0:T(8,128)(2,1)S(1)} %get-tuple-element.53.refs_0_, f32[32,128]{1,0:T(8,128)S(1)} %get-tuple-element.54.refs_1_, f32[32,128]{1,0:T(8,128)S(1)} %collective-permute-done.27.refs_2_, f32[32,128]{1,0:T(8,128)S(1)} %collective-permute-done.28.refs_3_, ...), custom_call_target="tpu_custom_call" | custom-call | tf_op jit(solution)/shard_map/pallas_call | solution.py:70
  (55 shorter events, 13.3 us)
Async XLA Ops:
  0.6 9.9 %copy-start.2 = (s32[1,2,8]{2,1,0:T(2,128)S(1)}, s32[1,2,8]{2,1,0:T(2,128)}, u32[]{:S(2)}) copy-start(s32[1,2,8]{2,1,0:T(2,128)} %param.6) | copy-start | bytes 196
  0.6 8.0 %collective-permute-start = (s32[2,8]{1,0:T(2,128)}, s32[2,8]{1,0:T(2,128)S(1)}, u32[]{:S(2)}, u32[]{:S(2)}) collective-permute-start(s32[2,8]{1,0:T(2,128)} %bitcast.7), channel_id=1, source_target_pairs={{0,4},{4,8},{8,12},{12,0},{1,5},{5,9},{9,13},{13,1},{2,6},{6,10},{... | collective-permute-start | bytes 200 | tf_op jit(solution)/shard_map/ppermute | solution.py:580
  3.7 4.9 %collective-permute-start.1 = (s32[2,8]{1,0:T(2,128)}, s32[2,8]{1,0:T(2,128)S(1)}, u32[]{:S(2)}, u32[]{:S(2)}) collective-permute-start(s32[2,8]{1,0:T(2,128)} %bitcast.8), channel_id=1, source_target_pairs={{0,12},{4,0},{8,4},{12,8},{1,13},{5,1},{9,5},{13,9},{2,14},{6,2},{... | collective-permute-start | bytes 200 | tf_op jit(solution)/shard_map/ppermute | solution.py:580
  5.8 4.7 %collective-permute-start.2 = (s32[2,8]{1,0:T(2,128)}, s32[2,8]{1,0:T(2,128)S(1)}, u32[]{:S(2)}, u32[]{:S(2)}) collective-permute-start(s32[2,8]{1,0:T(2,128)} %bitcast.9), channel_id=1, source_target_pairs={{0,8},{4,12},{8,0},{12,4},{1,9},{5,13},{9,1},{13,5},{2,10},{6,14},... | collective-permute-start | bytes 200 | tf_op jit(solution)/shard_map/ppermute | solution.py:580
  12.0 14.9 %collective-permute-start.3 = (bf16[256,384]{1,0:T(8,128)(2,1)S(1)}, bf16[256,384]{1,0:T(8,128)(2,1)S(1)}, u32[]{:S(2)}, u32[]{:S(2)}) collective-permute-start(bf16[256,384]{1,0:T(8,128)(2,1)S(1)} %get-tuple-element.30), channel_id=1, source_target_pairs={{0,8},{4,12},{8,0},{12,4},{1,9},{5,13},{9,1},{13,5},{2,10},{6,14},... | collective-permute-start | bytes 589832 | tf_op jit(solution)/shard_map/ppermute | solution.py:580
  13.0 13.9 %collective-permute-start.4 = (bf16[256,384]{1,0:T(8,128)(2,1)S(1)}, bf16[256,384]{1,0:T(8,128)(2,1)S(1)}, u32[]{:S(2)}, u32[]{:S(2)}) collective-permute-start(bf16[256,384]{1,0:T(8,128)(2,1)S(1)} %get-tuple-element.31), channel_id=1, source_target_pairs={{0,12},{4,0},{8,4},{12,8},{1,13},{5,1},{9,5},{13,9},{2,14},{6,2},{... | collective-permute-start | bytes 589832 | tf_op jit(solution)/shard_map/ppermute | solution.py:580
  14.4 12.5 %collective-permute-start.5 = (bf16[256,384]{1,0:T(8,128)(2,1)S(1)}, bf16[256,384]{1,0:T(8,128)(2,1)S(1)}, u32[]{:S(2)}, u32[]{:S(2)}) collective-permute-start(bf16[256,384]{1,0:T(8,128)(2,1)S(1)} %get-tuple-element.32), channel_id=1, source_target_pairs={{0,4},{4,8},{8,12},{12,0},{1,5},{5,9},{9,13},{13,1},{2,6},{6,10},{... | collective-permute-start | bytes 589832 | tf_op jit(solution)/shard_map/ppermute | solution.py:580
  15.1 13.8 %collective-permute-start.7 = (f32[1024,128]{1,0:T(8,128)S(1)}, f32[1024,128]{1,0:T(8,128)S(1)}, u32[]{:S(2)}, u32[]{:S(2)}) collective-permute-start(f32[1024,128]{1,0:T(8,128)S(1)} %shard_map.59.refs_5_.mine), channel_id=1, source_target_pairs={{0,1},{1,0},{2,3},{3,2},{4,5},{5,4},{6,7},{7,6},{8,9},{9,8},{10,11... | collective-permute-start | bytes 1572872 | tf_op jit(solution)/shard_map/ppermute | solution.py:580
  15.4 12.7 %copy-start.1 = (f32[2048,32]{0,1:T(8,128)S(1)}, f32[2048,32]{0,1:T(8,128)}, u32[]{:S(2)}) copy-start(f32[2048,32]{0,1:T(8,128)} %param.5) | copy-start | bytes 786436
  28.0 2.0 %collective-permute-start.6 = (f32[1024,128]{1,0:T(8,128)S(1)}, f32[1024,128]{1,0:T(8,128)S(1)}, u32[]{:S(2)}, u32[]{:S(2)}) collective-permute-start(f32[1024,128]{1,0:T(8,128)S(1)} %shard_map.62.refs_2_), channel_id=1, source_target_pairs={{0,1},{1,0},{2,3},{3,2},{4,5},{5,4},{6,7},{7,6},{8,9},{9,8},{10,11... | collective-permute-start | bytes 1572872 | tf_op jit(solution)/shard_map/ppermute | solution.py:580
  30.9 9.3 %collective-permute-start.10 = (f32[64,128]{1,0:T(8,128)S(1)}, f32[64,128]{1,0:T(8,128)S(1)}, u32[]{:S(2)}, u32[]{:S(2)}) collective-permute-start(f32[64,128]{1,0:T(8,128)S(1)} %get-tuple-element.37), channel_id=1, source_target_pairs={{0,12},{4,0},{8,4},{12,8},{1,13},{5,1},{9,5},{13,9},{2,14},{6,2},{... | collective-permute-start | bytes 98312 | tf_op jit(solution)/shard_map/ppermute | solution.py:580
  33.2 8.3 %collective-permute-start.8 = (f32[64,128]{1,0:T(8,128)S(1)}, f32[64,128]{1,0:T(8,128)S(1)}, u32[]{:S(2)}, u32[]{:S(2)}) collective-permute-start(f32[64,128]{1,0:T(8,128)S(1)} %get-tuple-element.37), channel_id=1, source_target_pairs={{0,4},{4,8},{8,12},{12,0},{1,5},{5,9},{9,13},{13,1},{2,6},{6,10},{... | collective-permute-start | bytes 98312 | tf_op jit(solution)/shard_map/ppermute | solution.py:580
  35.3 6.2 %collective-permute-start.9 = (f32[64,128]{1,0:T(8,128)S(1)}, f32[64,128]{1,0:T(8,128)S(1)}, u32[]{:S(2)}, u32[]{:S(2)}) collective-permute-start(f32[64,128]{1,0:T(8,128)S(1)} %get-tuple-element.37), channel_id=1, source_target_pairs={{0,8},{4,12},{8,0},{12,4},{1,9},{5,13},{9,1},{13,5},{2,10},{6,14},... | collective-permute-start | bytes 98312 | tf_op jit(solution)/shard_map/ppermute | solution.py:580
  37.7 7.8 %collective-permute-start.12 = (s16[272,128]{1,0:T(8,128)(2,1)S(1)}, s16[272,128]{1,0:T(8,128)(2,1)S(1)}, u32[]{:S(2)}, u32[]{:S(2)}) collective-permute-start(s16[272,128]{1,0:T(8,128)(2,1)S(1)} %get-tuple-element.43), channel_id=1, source_target_pairs={{0,4},{4,8},{8,12},{12,0},{1,5},{5,9},{9,13},{13,1},{2,6},{6,10},{... | collective-permute-start | bytes 208904 | tf_op jit(solution)/shard_map/ppermute | solution.py:580
  37.7 8.4 %collective-permute-start.13 = (s16[272,128]{1,0:T(8,128)(2,1)S(1)}, s16[272,128]{1,0:T(8,128)(2,1)S(1)}, u32[]{:S(2)}, u32[]{:S(2)}) collective-permute-start(s16[272,128]{1,0:T(8,128)(2,1)S(1)} %get-tuple-element.44), channel_id=1, source_target_pairs={{0,8},{4,12},{8,0},{12,4},{1,9},{5,13},{9,1},{13,5},{2,10},{6,14},... | collective-permute-start | bytes 208904 | tf_op jit(solution)/shard_map/ppermute | solution.py:580
  40.2 5.8 %collective-permute-start.14 = (s16[272,128]{1,0:T(8,128)(2,1)S(1)}, s16[272,128]{1,0:T(8,128)(2,1)S(1)}, u32[]{:S(2)}, u32[]{:S(2)}) collective-permute-start(s16[272,128]{1,0:T(8,128)(2,1)S(1)} %get-tuple-element.45), channel_id=1, source_target_pairs={{0,12},{4,0},{8,4},{12,8},{1,13},{5,1},{9,5},{13,9},{2,14},{6,2},{... | collective-permute-start | bytes 208904 | tf_op jit(solution)/shard_map/ppermute | solution.py:580
  41.5 4.0 %collective-permute-start.11 = (f32[64,128]{1,0:T(8,128)S(1)}, f32[64,128]{1,0:T(8,128)S(1)}, u32[]{:S(2)}, u32[]{:S(2)}) collective-permute-start(f32[64,128]{1,0:T(8,128)S(1)} %add_add_fusion.refs_1_), channel_id=1, source_target_pairs={{0,2},{2,0},{1,3},{3,1},{4,6},{6,4},{5,7},{7,5},{8,10},{10,8},{9,1... | collective-permute-start | bytes 98312 | tf_op jit(solution)/shard_map/ppermute | solution.py:588
  46.1 1.5 %collective-permute-start.15 = (bf16[1,256,128]{2,1,0:T(8,128)(2,1)S(1)}, bf16[1,256,128]{2,1,0:T(8,128)(2,1)S(1)}, u32[]{:S(2)}, u32[]{:S(2)}) collective-permute-start(bf16[1,256,128]{2,1,0:T(8,128)(2,1)S(1)} %get-tuple-element.46.refs_4_.refs_7_), channel_id=1, source_target_pairs={{0,1},{1,0},{2,3},{3,2},{4,5},{5,4},{6,7},{7,6},{8,9},{9,8},{10,11... | collective-permute-start | bytes 196616 | tf_op jit(solution)/shard_map/ppermute | solution.py:580
  46.2 1.4 %collective-permute-start.16 = (bf16[1,256,128]{2,1,0:T(8,128)(2,1)S(1)}, bf16[1,256,128]{2,1,0:T(8,128)(2,1)S(1)}, u32[]{:S(2)}, u32[]{:S(2)}) collective-permute-start(bf16[1,256,128]{2,1,0:T(8,128)(2,1)S(1)} %get-tuple-element.47.refs_5_.refs_8_), channel_id=1, source_target_pairs={{0,1},{1,0},{2,3},{3,2},{4,5},{5,4},{6,7},{7,6},{8,9},{9,8},{10,11... | collective-permute-start | bytes 196616 | tf_op jit(solution)/shard_map/ppermute | solution.py:580
  46.6 1.3 %collective-permute-start.17 = (bf16[1,256,128]{2,1,0:T(8,128)(2,1)S(1)}, bf16[1,256,128]{2,1,0:T(8,128)(2,1)S(1)}, u32[]{:S(2)}, u32[]{:S(2)}) collective-permute-start(bf16[1,256,128]{2,1,0:T(8,128)(2,1)S(1)} %get-tuple-element.48.refs_6_.refs_9_), channel_id=1, source_target_pairs={{0,1},{1,0},{2,3},{3,2},{4,5},{5,4},{6,7},{7,6},{8,9},{9,8},{10,11... | collective-permute-start | bytes 196616 | tf_op jit(solution)/shard_map/ppermute | solution.py:580
  48.9 5.8 %collective-permute-start.18 = (s16[32,2176]{1,0:T(8,128)(2,1)S(1)}, s16[32,2176]{1,0:T(8,128)(2,1)S(1)}, u32[]{:S(2)}, u32[]{:S(2)}) collective-permute-start(s16[32,2176]{1,0:T(8,128)(2,1)S(1)} %shard_map.68.refs_2_), channel_id=1, source_target_pairs={{0,2},{2,0},{1,3},{3,1},{4,6},{6,4},{5,7},{7,5},{8,10},{10,8},{9,1... | collective-permute-start | bytes 417800 | tf_op jit(solution)/shard_map/ppermute | solution.py:588
  55.4 4.6 %collective-permute-start.19 = (f32[32,2048]{1,0:T(8,128)S(1)}, f32[32,2048]{1,0:T(8,128)S(1)}, u32[]{:S(2)}, u32[]{:S(2)}) collective-permute-start(f32[32,2048]{1,0:T(8,128)S(1)} %get-tuple-element.49.refs_0_.refs_3_), channel_id=1, source_target_pairs={{0,1},{1,0},{2,3},{3,2},{4,5},{5,4},{6,7},{7,6},{8,9},{9,8},{10,11... | collective-permute-start | bytes 786440 | tf_op jit(solution)/shard_map/ppermute | solution.py:580
  55.5 6.2 %collective-permute-start.20 = (s16[144,128]{1,0:T(8,128)(2,1)S(1)}, s16[144,128]{1,0:T(8,128)(2,1)S(1)}, u32[]{:S(2)}, u32[]{:S(2)}) collective-permute-start(s16[144,128]{1,0:T(8,128)(2,1)S(1)} %get-tuple-element.50), channel_id=1, source_target_pairs={{0,4},{4,8},{8,12},{12,0},{1,5},{5,9},{9,13},{13,1},{2,6},{6,10},{... | collective-permute-start | bytes 110600 | tf_op jit(solution)/shard_map/ppermute | solution.py:580
  56.9 5.9 %collective-permute-start.21 = (s16[144,128]{1,0:T(8,128)(2,1)S(1)}, s16[144,128]{1,0:T(8,128)(2,1)S(1)}, u32[]{:S(2)}, u32[]{:S(2)}) collective-permute-start(s16[144,128]{1,0:T(8,128)(2,1)S(1)} %get-tuple-element.51), channel_id=1, source_target_pairs={{0,8},{4,12},{8,0},{12,4},{1,9},{5,13},{9,1},{13,5},{2,10},{6,14},... | collective-permute-start | bytes 110600 | tf_op jit(solution)/shard_map/ppermute | solution.py:580
  58.6 4.7 %collective-permute-start.22 = (s16[144,128]{1,0:T(8,128)(2,1)S(1)}, s16[144,128]{1,0:T(8,128)(2,1)S(1)}, u32[]{:S(2)}, u32[]{:S(2)}) collective-permute-start(s16[144,128]{1,0:T(8,128)(2,1)S(1)} %get-tuple-element.52), channel_id=1, source_target_pairs={{0,12},{4,0},{8,4},{12,8},{1,13},{5,1},{9,5},{13,9},{2,14},{6,2},{... | collective-permute-start | bytes 110600 | tf_op jit(solution)/shard_map/ppermute | solution.py:580
  60.4 3.9 %collective-permute-start.23 = (f32[32,128]{1,0:T(8,128)S(1)}, f32[32,128]{1,0:T(8,128)S(1)}, u32[]{:S(2)}, u32[]{:S(2)}) collective-permute-start(f32[32,128]{1,0:T(8,128)S(1)} %shard_map.70.refs_2_), channel_id=1, source_target_pairs={{0,4},{4,0},{8,12},{12,8},{1,5},{5,1},{9,13},{13,9},{2,6},{6,2},{1... | collective-permute-start | bytes 49160 | tf_op jit(solution)/shard_map/ppermute | solution.py:588
  64.5 6.2 %collective-permute-start.24 = (s16[32,2176]{1,0:T(8,128)(2,1)S(1)}, s16[32,2176]{1,0:T(8,128)(2,1)S(1)}, u32[]{:S(2)}, u32[]{:S(2)}) collective-permute-start(s16[32,2176]{1,0:T(8,128)(2,1)S(1)} %shard_map.72.refs_1_), channel_id=1, source_target_pairs={{0,2},{2,0},{1,3},{3,1},{4,6},{6,4},{5,7},{7,5},{8,10},{10,8},{9,1... | collective-permute-start | bytes 417800 | tf_op jit(solution)/shard_map/ppermute | solution.py:588
  66.0 4.6 %collective-permute-start.25 = (f32[32,128]{1,0:T(8,128)S(1)}, f32[32,128]{1,0:T(8,128)S(1)}, u32[]{:S(2)}, u32[]{:S(2)}) collective-permute-start(f32[32,128]{1,0:T(8,128)S(1)} %add.18.after.refs_0_), channel_id=1, source_target_pairs={{0,8},{4,12},{8,0},{12,4},{1,9},{5,13},{9,1},{13,5},{2,10},{6,14},... | collective-permute-start | bytes 49160 | tf_op jit(solution)/shard_map/ppermute | solution.py:588
  70.7 1.8 %collective-permute-start.26 = (f32[32,2048]{1,0:T(8,128)S(1)}, f32[32,2048]{1,0:T(8,128)S(1)}, u32[]{:S(2)}, u32[]{:S(2)}) collective-permute-start(f32[32,2048]{1,0:T(8,128)S(1)} %shard_map.73.after.refs_1_), channel_id=1, source_target_pairs={{0,1},{1,0},{2,3},{3,2},{4,5},{5,4},{6,7},{7,6},{8,9},{9,8},{10,11... | collective-permute-start | bytes 786440 | tf_op jit(solution)/shard_map/ppermute | solution.py:580
  73.4 5.6 %collective-permute-start.27 = (f32[32,128]{1,0:T(8,128)S(1)}, f32[32,128]{1,0:T(8,128)S(1)}, u32[]{:S(2)}, u32[]{:S(2)}) collective-permute-start(f32[32,128]{1,0:T(8,128)S(1)} %get-tuple-element.54.refs_1_), channel_id=1, source_target_pairs={{0,4},{4,8},{8,12},{12,0},{1,5},{5,9},{9,13},{13,1},{2,6},{6,10},{... | collective-permute-start | bytes 49160 | tf_op jit(solution)/shard_map/ppermute | solution.py:580
  74.2 4.8 %collective-permute-start.28 = (f32[32,128]{1,0:T(8,128)S(1)}, f32[32,128]{1,0:T(8,128)S(1)}, u32[]{:S(2)}, u32[]{:S(2)}) collective-permute-start(f32[32,128]{1,0:T(8,128)S(1)} %get-tuple-element.54.refs_1_), channel_id=1, source_target_pairs={{0,8},{4,12},{8,0},{12,4},{1,9},{5,13},{9,1},{13,5},{2,10},{6,14},... | collective-permute-start | bytes 49160 | tf_op jit(solution)/shard_map/ppermute | solution.py:580
  76.4 3.7 %collective-permute-start.29 = (f32[32,128]{1,0:T(8,128)S(1)}, f32[32,128]{1,0:T(8,128)S(1)}, u32[]{:S(2)}, u32[]{:S(2)}) collective-permute-start(f32[32,128]{1,0:T(8,128)S(1)} %get-tuple-element.54.refs_1_), channel_id=1, source_target_pairs={{0,12},{4,0},{8,4},{12,8},{1,13},{5,1},{9,5},{13,9},{2,14},{6,2},{... | collective-permute-start | bytes 49160 | tf_op jit(solution)/shard_map/ppermute | solution.py:580
  (1 other events, 1.4 us)

commit v22 on v21

--- a/solution.py
+++ b/solution.py
@@ -299,32 +299,34 @@
         )
 
 
-def squares_body(emb, after, out):
+def squares_body(capacity, idx, emb, out, home):
     for b in range(out.shape[0] // BLOCK):
         part = slice(b * BLOCK, (b + 1) * BLOCK)
         out[part, :] = jnp.broadcast_to(squares(emb[part, :]), (BLOCK, BLOCK))
-
-
-def pair_distance_body(order, capacity, idx, emb, own_squares, *refs):
+    idx = idx.ready()
+    for j in range(capacity):
+        left, right = at_block(idx[0, j]), at_block(idx[4, j])
+        home[j * BLOCK : (j + 1) * BLOCK, :] = partial_distance(
+            emb[left, :], emb[right, :], out[left, :], as_row(out[right, :])
+        )
+
+
+def pair_distance_body(order, capacity, idx, emb, own_squares, home, *refs):
     far, out = dict(zip(order, refs)), refs[-1]
     rows = {}
     for k in order:
         for j in range(capacity):
             rows[k, j] = as_row(squares(far[k][j * BLOCK : (j + 1) * BLOCK, :]))
     idx = idx.ready()
-    for k in range(len(order) + 1):
+    out[: capacity * BLOCK, :] = home[...]
+    for k in range(1, len(order) + 1):
         for j in range(capacity):
             slot = k * capacity + j
             left = emb[at_block(idx[0, slot]), :]
             left_sq = own_squares[at_block(idx[0, slot]), :]
-            if k == 0:
-                right = emb[at_block(idx[4, j]), :]
-                right_row = as_row(own_squares[at_block(idx[4, j]), :])
-            else:
-                right = far[k][j * BLOCK : (j + 1) * BLOCK, :]
-                right_row = rows[k, j]
+            right = far[k][j * BLOCK : (j + 1) * BLOCK, :]
             part = slice(slot * BLOCK, (slot + 1) * BLOCK)
-            out[part, :] = partial_distance(left, right, left_sq, right_row)
+            out[part, :] = partial_distance(left, right, left_sq, rows[k, j])
 
 
 def self_tile_body(own_blocks, mine, other, packed, sums):
@@ -615,7 +617,7 @@
     block_count = row_count * blocks_here
     others = range(1, row_count)
 
-    list_order = [0, *sorted(others, key=lambda k: k * (row_count - k))]
+    list_order = [0, *sorted(others, key=lambda k: abs(k - row_count // 2))]
     lists = [shift_by(pair_list[0], "rows", row_count, k) if k else pair_list[0] for k in list_order]
     self_part = call(
         functools.partial(self_distance_body, own_blocks, tile_count),
@@ -646,11 +648,16 @@
     start_codes = call(start_body, [sds(*shape) for shape in code_shapes], [values])
     code_scratch = [pltpu.VMEM(*shape) for shape in code_shapes]
     coded = tile_count == 2
-    own_squares = call(squares_body, sds((rows_here, BLOCK), F32), [embeddings, idx], any_in=(1,))
+    own_squares, home = call(
+        functools.partial(squares_body, capacity),
+        [sds((rows_here, BLOCK), F32), sds((capacity * BLOCK, BLOCK), F32)],
+        [idx, embeddings],
+        late=(0,),
+    )
     pair_part = call(
         functools.partial(pair_distance_body, order, capacity),
         sds((slots * BLOCK, BLOCK), F32),
-        [idx, embeddings, own_squares, *far],
+        [idx, embeddings, own_squares, home, *far],
         late=(0,),
     )
     pair_other = shift_by(pair_part, "cols", core_count, 1)

time: 82.9 us -> 83.1 us (level)
  waiting for transfers between devices: 29.2 us -> 25.9 us
  starting transfers between devices: 36 us -> 39.1 us
    ppermute x25, waiting for transfers between devices: 19.2 us -> 15.8 us  [shift_by(): lax.ppermute(value, axes, [(i, (i + shift) % size) for i in range(size)])]
    ppermute x25, starting transfers between devices: 29.3 us -> 32 us  [shift_by(): lax.ppermute(value, axes, [(i, (i + shift) % size) for i in range(size)])]
where the time goes in v22:
time: 83.1 us; the launch traced here: 82.9 us
  starting transfers between devices  39.1 us (47%)
  waiting for transfers between devices  25.9 us (31%)
  Pallas kernels  14.4 us (17%)
  local copies, waits for them, and re-layouts  2.01 us (2%)
  between operations  1.53 us (2%)
    ppermute x25, starting transfers between devices, shift_by(): lax.ppermute(value, axes, [(i, (i + shift) % size) for i in range(size)])  32 us
    ppermute x25, waiting for transfers between devices, shift_by(): lax.ppermute(value, axes, [(i, (i + shift) % size) for i in range(size)])  15.8 us
    pallas_call x18, Pallas kernels, call(): pl.pallas_call(body, out_shape=shapes, in_specs=[ANY if i in any_in else...  14.4 us
    ppermute x5, waiting for transfers between devices, pair_step(): lax.ppermute(value, name, [(i, i ^ flip) for i in range(lax.axis_size(nam...  10.1 us
    ppermute x5, starting transfers between devices, pair_step(): lax.ppermute(value, name, [(i, i ^ flip) for i in range(lax.axis_size(nam...  7.13 us
  transfers between devices with their start and end apart: 30, of which 13 were waited for; matrix products, arithmetic and copies ran while one was open for 1% of the time, Pallas kernels for 8%

profile of v22, /device:TPU:0, one launch (start us, length us, event | category | flops | bytes accessed | tf_op | source)
XLA Modules:
  0.0 82.9 jit_solution(8136065471755032466)
XLA Ops:
  0.6 4.1 %collective-permute-start = (s32[2,8]{1,0:T(2,128)}, s32[2,8]{1,0:T(2,128)S(1)}, u32[]{:S(2)}, u32[]{:S(2)}) collective-permute-start(s32[2,8]{1,0:T(2,128)} %bitcast.7), channel_id=1, source_target_pairs={{0,8},{4,12},{8,0},{12,4},{1,9},{5,13},{9,1},{13,5},{2,10},{6,14},... | collective-permute-start | bytes 200 | tf_op jit(solution)/shard_map/ppermute | solution.py:582
  4.7 1.6 %collective-permute-start.1 = (s32[2,8]{1,0:T(2,128)}, s32[2,8]{1,0:T(2,128)S(1)}, u32[]{:S(2)}, u32[]{:S(2)}) collective-permute-start(s32[2,8]{1,0:T(2,128)} %bitcast.8), channel_id=1, source_target_pairs={{0,4},{4,8},{8,12},{12,0},{1,5},{5,9},{9,13},{13,1},{2,6},{6,10},{... | collective-permute-start | bytes 200 | tf_op jit(solution)/shard_map/ppermute | solution.py:582
  6.3 2.2 %collective-permute-start.2 = (s32[2,8]{1,0:T(2,128)}, s32[2,8]{1,0:T(2,128)S(1)}, u32[]{:S(2)}, u32[]{:S(2)}) collective-permute-start(s32[2,8]{1,0:T(2,128)} %bitcast.9), channel_id=1, source_target_pairs={{0,12},{4,0},{8,4},{12,8},{1,13},{5,1},{9,5},{13,9},{2,14},{6,2},{... | collective-permute-start | bytes 200 | tf_op jit(solution)/shard_map/ppermute | solution.py:582
  8.6 1.4 %copy-done = bf16[2048,384]{1,0:T(8,128)(2,1)S(1)} copy-done((bf16[2048,384]{1,0:T(8,128)(2,1)S(1)}, bf16[2048,384]{1,0:T(8,128)(2,1)}, u32[]{:S(2)}) %copy-start) | copy-done | bytes 1572888
  10.5 1.5 %shard_map.60 = (s32[6,9]{1,0:T(8,128)S(1)}, bf16[256,384]{1,0:T(8,128)(2,1)S(1)}, bf16[256,384]{1,0:T(8,128)(2,1)S(1)}, bf16[256,384]{1,0:T(8,128)(2,1)S(1)}) custom-call(s32[2,8]{1,0:T(2,128)S(1)} %bitcast.10, s32[2,8]{1,0:T(2,128)S(1)} %collective-permute-done.refs_1_, s32[2,8]{1,0:T(2,128)S(1)} %collective-permute-done.1.refs_2_, ...), custom_call_target="tpu_custom_call" | custom-call | tf_op jit(solution)/shard_map/pallas_call | solution.py:70
  12.5 3.3 %collective-permute-start.4 = (bf16[256,384]{1,0:T(8,128)(2,1)S(1)}, bf16[256,384]{1,0:T(8,128)(2,1)S(1)}, u32[]{:S(2)}, u32[]{:S(2)}) collective-permute-start(bf16[256,384]{1,0:T(8,128)(2,1)S(1)} %get-tuple-element.35), channel_id=1, source_target_pairs={{0,12},{4,0},{8,4},{12,8},{1,13},{5,1},{9,5},{13,9},{2,14},{6,2},{... | collective-permute-start | bytes 589832 | tf_op jit(solution)/shard_map/ppermute | solution.py:582
  17.1 8.2 %collective-permute-done.3.refs_4_ = bf16[256,384]{1,0:T(8,128)(2,1)S(1)} collective-permute-done((bf16[256,384]{1,0:T(8,128)(2,1)S(1)}, bf16[256,384]{1,0:T(8,128)(2,1)S(1)}, u32[]{:S(2)}, u32[]{:S(2)}) %collective-permute-start.3) | collective-permute-done | bytes 196640 | tf_op jit(solution)/shard_map/ppermute | solution.py:582
  25.4 2.1 %collective-permute-done.5.refs_6_ = bf16[256,384]{1,0:T(8,128)(2,1)S(1)} collective-permute-done((bf16[256,384]{1,0:T(8,128)(2,1)S(1)}, bf16[256,384]{1,0:T(8,128)(2,1)S(1)}, u32[]{:S(2)}, u32[]{:S(2)}) %collective-permute-start.5) | collective-permute-done | bytes 196640 | tf_op jit(solution)/shard_map/ppermute | solution.py:582
  27.5 1.0 %shard_map.62.refs_2_ = f32[1024,128]{1,0:T(8,128)S(1)} custom-call(s32[6,9]{1,0:T(8,128)S(1)} %get-tuple-element.31.refs_0_, bf16[2048,384]{1,0:T(8,128)(2,1)S(1)} %copy-done, f32[2048,128]{1,0:T(8,128)S(1)} %get-tuple-element.32.refs_2_, f32[256,128]{1,0:T(8,128)S(1)} %get-tuple-element.33.refs_3_, bf16[256,384]{1,0:T(8,128)(2,1)S(1)} %collective-permute-done.3.refs_4_, ...), custom_call_target="tpu_custom_call" | custom-call | tf_op jit(solution)/shard_map/pallas_call | solution.py:70
  31.4 2.8 %collective-permute-start.10 = (f32[64,128]{1,0:T(8,128)S(1)}, f32[64,128]{1,0:T(8,128)S(1)}, u32[]{:S(2)}, u32[]{:S(2)}) collective-permute-start(f32[64,128]{1,0:T(8,128)S(1)} %get-tuple-element.41), channel_id=1, source_target_pairs={{0,12},{4,0},{8,4},{12,8},{1,13},{5,1},{9,5},{13,9},{2,14},{6,2},{... | collective-permute-start | bytes 98312 | tf_op jit(solution)/shard_map/ppermute | solution.py:582
  34.2 1.8 %collective-permute-start.8 = (f32[64,128]{1,0:T(8,128)S(1)}, f32[64,128]{1,0:T(8,128)S(1)}, u32[]{:S(2)}, u32[]{:S(2)}) collective-permute-start(f32[64,128]{1,0:T(8,128)S(1)} %get-tuple-element.41), channel_id=1, source_target_pairs={{0,4},{4,8},{8,12},{12,0},{1,5},{5,9},{9,13},{13,1},{2,6},{6,10},{... | collective-permute-start | bytes 98312 | tf_op jit(solution)/shard_map/ppermute | solution.py:582
  36.0 1.7 %collective-permute-start.9 = (f32[64,128]{1,0:T(8,128)S(1)}, f32[64,128]{1,0:T(8,128)S(1)}, u32[]{:S(2)}, u32[]{:S(2)}) collective-permute-start(f32[64,128]{1,0:T(8,128)S(1)} %get-tuple-element.41), channel_id=1, source_target_pairs={{0,8},{4,12},{8,0},{12,4},{1,9},{5,13},{9,1},{13,5},{2,10},{6,14},... | collective-permute-start | bytes 98312 | tf_op jit(solution)/shard_map/ppermute | solution.py:582
  38.6 2.3 %collective-permute-start.13 = (s16[272,128]{1,0:T(8,128)(2,1)S(1)}, s16[272,128]{1,0:T(8,128)(2,1)S(1)}, u32[]{:S(2)}, u32[]{:S(2)}) collective-permute-start(s16[272,128]{1,0:T(8,128)(2,1)S(1)} %get-tuple-element.48), channel_id=1, source_target_pairs={{0,8},{4,12},{8,0},{12,4},{1,9},{5,13},{9,1},{13,5},{2,10},{6,14},... | collective-permute-start | bytes 208904 | tf_op jit(solution)/shard_map/ppermute | solution.py:582
  40.9 1.0 %collective-permute-start.14 = (s16[272,128]{1,0:T(8,128)(2,1)S(1)}, s16[272,128]{1,0:T(8,128)(2,1)S(1)}, u32[]{:S(2)}, u32[]{:S(2)}) collective-permute-start(s16[272,128]{1,0:T(8,128)(2,1)S(1)} %get-tuple-element.49), channel_id=1, source_target_pairs={{0,12},{4,0},{8,4},{12,8},{1,13},{5,1},{9,5},{13,9},{2,14},{6,2},{... | collective-permute-start | bytes 208904 | tf_op jit(solution)/shard_map/ppermute | solution.py:582
  41.9 1.6 %collective-permute-start.11 = (f32[64,128]{1,0:T(8,128)S(1)}, f32[64,128]{1,0:T(8,128)S(1)}, u32[]{:S(2)}, u32[]{:S(2)}) collective-permute-start(f32[64,128]{1,0:T(8,128)S(1)} %add_add_fusion.refs_1_), channel_id=1, source_target_pairs={{0,2},{2,0},{1,3},{3,1},{4,6},{6,4},{5,7},{7,5},{8,10},{10,8},{9,1... | collective-permute-start | bytes 98312 | tf_op jit(solution)/shard_map/ppermute | solution.py:590
  43.4 2.4 %collective-permute-done.11.refs_2_.refs_3_ = f32[64,128]{1,0:T(8,128)S(1)} collective-permute-done((f32[64,128]{1,0:T(8,128)S(1)}, f32[64,128]{1,0:T(8,128)S(1)}, u32[]{:S(2)}, u32[]{:S(2)}) %collective-permute-start.11) | collective-permute-done | bytes 32800 | tf_op jit(solution)/shard_map/ppermute | solution.py:590
  48.2 1.0 %shard_map.68.refs_2_ = s16[32,2176]{1,0:T(8,128)(2,1)S(1)} custom-call(s32[6,9]{1,0:T(8,128)S(1)} %get-tuple-element.31.refs_0_, f32[64,128]{1,0:T(8,128)S(1)} %get-tuple-element.45.refs_1_.refs_0_, f32[32,2048]{1,0:T(8,128)S(1)} %get-tuple-element.46.refs_2_, bf16[8,256,128]{2,1,0:T(8,128)(2,1)S(1)} %get-tuple-element.42.refs_4_.refs_3_.refs_6_, ...), custom_call_target="tpu_custom_call" | custom-call | tf_op jit(solution)/shard_map/pallas_call | solution.py:70
  49.2 1.5 %collective-permute-start.18 = (s16[32,2176]{1,0:T(8,128)(2,1)S(1)}, s16[32,2176]{1,0:T(8,128)(2,1)S(1)}, u32[]{:S(2)}, u32[]{:S(2)}) collective-permute-start(s16[32,2176]{1,0:T(8,128)(2,1)S(1)} %shard_map.68.refs_2_), channel_id=1, source_target_pairs={{0,2},{2,0},{1,3},{3,1},{4,6},{6,4},{5,7},{7,5},{8,10},{10,8},{9,1... | collective-permute-start | bytes 417800 | tf_op jit(solution)/shard_map/ppermute | solution.py:590
  50.7 4.3 %collective-permute-done.18.refs_3_ = s16[32,2176]{1,0:T(8,128)(2,1)S(1)} collective-permute-done((s16[32,2176]{1,0:T(8,128)(2,1)S(1)}, s16[32,2176]{1,0:T(8,128)(2,1)S(1)}, u32[]{:S(2)}, u32[]{:S(2)}) %collective-permute-start.18) | collective-permute-done | bytes 139296 | tf_op jit(solution)/shard_map/ppermute | solution.py:590
  55.7 1.8 %collective-permute-start.20 = (s16[144,128]{1,0:T(8,128)(2,1)S(1)}, s16[144,128]{1,0:T(8,128)(2,1)S(1)}, u32[]{:S(2)}, u32[]{:S(2)}) collective-permute-start(s16[144,128]{1,0:T(8,128)(2,1)S(1)} %get-tuple-element.54), channel_id=1, source_target_pairs={{0,4},{4,8},{8,12},{12,0},{1,5},{5,9},{9,13},{13,1},{2,6},{6,10},{... | collective-permute-start | bytes 110600 | tf_op jit(solution)/shard_map/ppermute | solution.py:582
  57.5 1.6 %collective-permute-start.21 = (s16[144,128]{1,0:T(8,128)(2,1)S(1)}, s16[144,128]{1,0:T(8,128)(2,1)S(1)}, u32[]{:S(2)}, u32[]{:S(2)}) collective-permute-start(s16[144,128]{1,0:T(8,128)(2,1)S(1)} %get-tuple-element.55), channel_id=1, source_target_pairs={{0,8},{4,12},{8,0},{12,4},{1,9},{5,13},{9,1},{13,5},{2,10},{6,14},... | collective-permute-start | bytes 110600 | tf_op jit(solution)/shard_map/ppermute | solution.py:582
  60.4 1.2 %collective-permute-start.23 = (f32[32,128]{1,0:T(8,128)S(1)}, f32[32,128]{1,0:T(8,128)S(1)}, u32[]{:S(2)}, u32[]{:S(2)}) collective-permute-start(f32[32,128]{1,0:T(8,128)S(1)} %shard_map.70.refs_2_), channel_id=1, source_target_pairs={{0,4},{4,0},{8,12},{12,8},{1,5},{5,1},{9,13},{13,9},{2,6},{6,2},{1... | collective-permute-start | bytes 49160 | tf_op jit(solution)/shard_map/ppermute | solution.py:590
  61.9 1.2 %collective-permute-done.21.refs_14_ = s16[144,128]{1,0:T(8,128)(2,1)S(1)} collective-permute-done((s16[144,128]{1,0:T(8,128)(2,1)S(1)}, s16[144,128]{1,0:T(8,128)(2,1)S(1)}, u32[]{:S(2)}, u32[]{:S(2)}) %collective-permute-start.21) | collective-permute-done | bytes 36896 | tf_op jit(solution)/shard_map/ppermute | solution.py:582
  63.5 1.0 %shard_map.71.total = f32[32,2048]{1,0:T(8,128)S(1)} custom-call(s32[6,9]{1,0:T(8,128)S(1)} %get-tuple-element.31.refs_0_, f32[64,128]{1,0:T(8,128)S(1)} %get-tuple-element.45.refs_1_.refs_0_, f32[32,128]{1,0:T(8,128)S(1)} %shard_map.70.refs_2_, f32[32,2048]{1,0:T(8,128)S(1)} %get-tuple-element.53.refs_0_.refs_3_, ...), custom_call_target="tpu_custom_call" | custom-call | tf_op jit(solution)/shard_map/pallas_call | solution.py:70
  64.7 1.6 %collective-permute-start.24 = (s16[32,2176]{1,0:T(8,128)(2,1)S(1)}, s16[32,2176]{1,0:T(8,128)(2,1)S(1)}, u32[]{:S(2)}, u32[]{:S(2)}) collective-permute-start(s16[32,2176]{1,0:T(8,128)(2,1)S(1)} %shard_map.72.refs_1_), channel_id=1, source_target_pairs={{0,2},{2,0},{1,3},{3,1},{4,6},{6,4},{5,7},{7,5},{8,10},{10,8},{9,1... | collective-permute-start | bytes 417800 | tf_op jit(solution)/shard_map/ppermute | solution.py:590
  66.3 1.3 %collective-permute-start.25 = (f32[32,128]{1,0:T(8,128)S(1)}, f32[32,128]{1,0:T(8,128)S(1)}, u32[]{:S(2)}, u32[]{:S(2)}) collective-permute-start(f32[32,128]{1,0:T(8,128)S(1)} %add.18.after.refs_0_), channel_id=1, source_target_pairs={{0,8},{4,12},{8,0},{12,4},{1,9},{5,13},{9,1},{13,5},{2,10},{6,14},... | collective-permute-start | bytes 49160 | tf_op jit(solution)/shard_map/ppermute | solution.py:590
  67.5 3.4 %collective-permute-done.25.refs_3_.refs_1_ = f32[32,128]{1,0:T(8,128)S(1)} collective-permute-done((f32[32,128]{1,0:T(8,128)S(1)}, f32[32,128]{1,0:T(8,128)S(1)}, u32[]{:S(2)}, u32[]{:S(2)}) %collective-permute-start.25) | collective-permute-done | bytes 16416 | tf_op jit(solution)/shard_map/ppermute | solution.py:590
  71.1 1.7 %shard_map.74.refs_0_ = f32[64,64]{1,0:T(8,128)S(1)} custom-call(f32[32,2048]{1,0:T(8,128)S(1)} %shard_map.73.after.refs_1_, f32[32,128]{1,0:T(8,128)S(1)} %add.18.after.refs_0_, f32[32,128]{1,0:T(8,128)S(1)} %collective-permute-done.25.refs_3_.refs_1_), custom_call_target="tpu_custom_call" | custom-call | tf_op jit(solution)/shard_map/pallas_call | solution.py:70
  74.4 2.1 %collective-permute-start.28 = (f32[32,128]{1,0:T(8,128)S(1)}, f32[32,128]{1,0:T(8,128)S(1)}, u32[]{:S(2)}, u32[]{:S(2)}) collective-permute-start(f32[32,128]{1,0:T(8,128)S(1)} %get-tuple-element.58.refs_1_), channel_id=1, source_target_pairs={{0,8},{4,12},{8,0},{12,4},{1,9},{5,13},{9,1},{13,5},{2,10},{6,14},... | collective-permute-start | bytes 49160 | tf_op jit(solution)/shard_map/ppermute | solution.py:582
  76.6 1.3 %collective-permute-start.29 = (f32[32,128]{1,0:T(8,128)S(1)}, f32[32,128]{1,0:T(8,128)S(1)}, u32[]{:S(2)}, u32[]{:S(2)}) collective-permute-start(f32[32,128]{1,0:T(8,128)S(1)} %get-tuple-element.58.refs_1_), channel_id=1, source_target_pairs={{0,12},{4,0},{8,4},{12,8},{1,13},{5,1},{9,5},{13,9},{2,14},{6,2},{... | collective-permute-start | bytes 49160 | tf_op jit(solution)/shard_map/ppermute | solution.py:582
  79.3 1.0 %collective-permute-done.29.refs_4_ = f32[32,128]{1,0:T(8,128)S(1)} collective-permute-done((f32[32,128]{1,0:T(8,128)S(1)}, f32[32,128]{1,0:T(8,128)S(1)}, u32[]{:S(2)}, u32[]{:S(2)}) %collective-permute-start.29) | collective-permute-done | bytes 16416 | tf_op jit(solution)/shard_map/ppermute | solution.py:582
  80.3 2.6 %shard_map.76 = f32[32,2048]{1,0:T(8,128)} custom-call(bf16[128,2048]{1,0:T(8,128)(2,1)S(1)} %get-tuple-element.57.refs_0_, f32[32,128]{1,0:T(8,128)S(1)} %get-tuple-element.58.refs_1_, f32[32,128]{1,0:T(8,128)S(1)} %collective-permute-done.27.refs_2_, f32[32,128]{1,0:T(8,128)S(1)} %collective-permute-done.28.refs_3_, ...), custom_call_target="tpu_custom_call" | custom-call | tf_op jit(solution)/shard_map/pallas_call | solution.py:70
  (55 shorter events, 13.9 us)
Async XLA Ops:
  0.6 9.8 %copy-start.2 = (s32[1,2,8]{2,1,0:T(2,128)S(1)}, s32[1,2,8]{2,1,0:T(2,128)}, u32[]{:S(2)}) copy-start(s32[1,2,8]{2,1,0:T(2,128)} %param.6) | copy-start | bytes 196
  0.6 9.8 %collective-permute-start = (s32[2,8]{1,0:T(2,128)}, s32[2,8]{1,0:T(2,128)S(1)}, u32[]{:S(2)}, u32[]{:S(2)}) collective-permute-start(s32[2,8]{1,0:T(2,128)} %bitcast.7), channel_id=1, source_target_pairs={{0,8},{4,12},{8,0},{12,4},{1,9},{5,13},{9,1},{13,5},{2,10},{6,14},... | collective-permute-start | bytes 200 | tf_op jit(solution)/shard_map/ppermute | solution.py:582
  4.7 5.7 %collective-permute-start.1 = (s32[2,8]{1,0:T(2,128)}, s32[2,8]{1,0:T(2,128)S(1)}, u32[]{:S(2)}, u32[]{:S(2)}) collective-permute-start(s32[2,8]{1,0:T(2,128)} %bitcast.8), channel_id=1, source_target_pairs={{0,4},{4,8},{8,12},{12,0},{1,5},{5,9},{9,13},{13,1},{2,6},{6,10},{... | collective-permute-start | bytes 200 | tf_op jit(solution)/shard_map/ppermute | solution.py:582
  6.3 4.1 %collective-permute-start.2 = (s32[2,8]{1,0:T(2,128)}, s32[2,8]{1,0:T(2,128)S(1)}, u32[]{:S(2)}, u32[]{:S(2)}) collective-permute-start(s32[2,8]{1,0:T(2,128)} %bitcast.9), channel_id=1, source_target_pairs={{0,12},{4,0},{8,4},{12,8},{1,13},{5,1},{9,5},{13,9},{2,14},{6,2},{... | collective-permute-start | bytes 200 | tf_op jit(solution)/shard_map/ppermute | solution.py:582
  8.6 1.4 %copy-start = (bf16[2048,384]{1,0:T(8,128)(2,1)S(1)}, bf16[2048,384]{1,0:T(8,128)(2,1)}, u32[]{:S(2)}) copy-start(bf16[2048,384]{1,0:T(8,128)(2,1)} %refs_1_.4) | copy-start | bytes 4718596
  12.0 13.3 %collective-permute-start.3 = (bf16[256,384]{1,0:T(8,128)(2,1)S(1)}, bf16[256,384]{1,0:T(8,128)(2,1)S(1)}, u32[]{:S(2)}, u32[]{:S(2)}) collective-permute-start(bf16[256,384]{1,0:T(8,128)(2,1)S(1)} %get-tuple-element.34), channel_id=1, source_target_pairs={{0,8},{4,12},{8,0},{12,4},{1,9},{5,13},{9,1},{13,5},{2,10},{6,14},... | collective-permute-start | bytes 589832 | tf_op jit(solution)/shard_map/ppermute | solution.py:582
  12.5 12.8 %collective-permute-start.4 = (bf16[256,384]{1,0:T(8,128)(2,1)S(1)}, bf16[256,384]{1,0:T(8,128)(2,1)S(1)}, u32[]{:S(2)}, u32[]{:S(2)}) collective-permute-start(bf16[256,384]{1,0:T(8,128)(2,1)S(1)} %get-tuple-element.35), channel_id=1, source_target_pairs={{0,12},{4,0},{8,4},{12,8},{1,13},{5,1},{9,5},{13,9},{2,14},{6,2},{... | collective-permute-start | bytes 589832 | tf_op jit(solution)/shard_map/ppermute | solution.py:582
  15.8 11.7 %collective-permute-start.5 = (bf16[256,384]{1,0:T(8,128)(2,1)S(1)}, bf16[256,384]{1,0:T(8,128)(2,1)S(1)}, u32[]{:S(2)}, u32[]{:S(2)}) collective-permute-start(bf16[256,384]{1,0:T(8,128)(2,1)S(1)} %get-tuple-element.36), channel_id=1, source_target_pairs={{0,4},{4,8},{8,12},{12,0},{1,5},{5,9},{9,13},{13,1},{2,6},{6,10},{... | collective-permute-start | bytes 589832 | tf_op jit(solution)/shard_map/ppermute | solution.py:582
  16.3 13.1 %collective-permute-start.7 = (f32[1024,128]{1,0:T(8,128)S(1)}, f32[1024,128]{1,0:T(8,128)S(1)}, u32[]{:S(2)}, u32[]{:S(2)}) collective-permute-start(f32[1024,128]{1,0:T(8,128)S(1)} %shard_map.59.refs_5_.mine), channel_id=1, source_target_pairs={{0,1},{1,0},{2,3},{3,2},{4,5},{5,4},{6,7},{7,6},{8,9},{9,8},{10,11... | collective-permute-start | bytes 1572872 | tf_op jit(solution)/shard_map/ppermute | solution.py:582
  28.5 2.0 %collective-permute-start.6 = (f32[1024,128]{1,0:T(8,128)S(1)}, f32[1024,128]{1,0:T(8,128)S(1)}, u32[]{:S(2)}, u32[]{:S(2)}) collective-permute-start(f32[1024,128]{1,0:T(8,128)S(1)} %shard_map.62.refs_2_), channel_id=1, source_target_pairs={{0,1},{1,0},{2,3},{3,2},{4,5},{5,4},{6,7},{7,6},{8,9},{9,8},{10,11... | collective-permute-start | bytes 1572872 | tf_op jit(solution)/shard_map/ppermute | solution.py:582
  31.4 9.5 %collective-permute-start.10 = (f32[64,128]{1,0:T(8,128)S(1)}, f32[64,128]{1,0:T(8,128)S(1)}, u32[]{:S(2)}, u32[]{:S(2)}) collective-permute-start(f32[64,128]{1,0:T(8,128)S(1)} %get-tuple-element.41), channel_id=1, source_target_pairs={{0,12},{4,0},{8,4},{12,8},{1,13},{5,1},{9,5},{13,9},{2,14},{6,2},{... | collective-permute-start | bytes 98312 | tf_op jit(solution)/shard_map/ppermute | solution.py:582
  34.2 7.7 %collective-permute-start.8 = (f32[64,128]{1,0:T(8,128)S(1)}, f32[64,128]{1,0:T(8,128)S(1)}, u32[]{:S(2)}, u32[]{:S(2)}) collective-permute-start(f32[64,128]{1,0:T(8,128)S(1)} %get-tuple-element.41), channel_id=1, source_target_pairs={{0,4},{4,8},{8,12},{12,0},{1,5},{5,9},{9,13},{13,1},{2,6},{6,10},{... | collective-permute-start | bytes 98312 | tf_op jit(solution)/shard_map/ppermute | solution.py:582
  36.0 5.9 %collective-permute-start.9 = (f32[64,128]{1,0:T(8,128)S(1)}, f32[64,128]{1,0:T(8,128)S(1)}, u32[]{:S(2)}, u32[]{:S(2)}) collective-permute-start(f32[64,128]{1,0:T(8,128)S(1)} %get-tuple-element.41), channel_id=1, source_target_pairs={{0,8},{4,12},{8,0},{12,4},{1,9},{5,13},{9,1},{13,5},{2,10},{6,14},... | collective-permute-start | bytes 98312 | tf_op jit(solution)/shard_map/ppermute | solution.py:582
  37.7 8.2 %collective-permute-start.12 = (s16[272,128]{1,0:T(8,128)(2,1)S(1)}, s16[272,128]{1,0:T(8,128)(2,1)S(1)}, u32[]{:S(2)}, u32[]{:S(2)}) collective-permute-start(s16[272,128]{1,0:T(8,128)(2,1)S(1)} %get-tuple-element.47), channel_id=1, source_target_pairs={{0,4},{4,8},{8,12},{12,0},{1,5},{5,9},{9,13},{13,1},{2,6},{6,10},{... | collective-permute-start | bytes 208904 | tf_op jit(solution)/shard_map/ppermute | solution.py:582
  38.6 7.7 %collective-permute-start.13 = (s16[272,128]{1,0:T(8,128)(2,1)S(1)}, s16[272,128]{1,0:T(8,128)(2,1)S(1)}, u32[]{:S(2)}, u32[]{:S(2)}) collective-permute-start(s16[272,128]{1,0:T(8,128)(2,1)S(1)} %get-tuple-element.48), channel_id=1, source_target_pairs={{0,8},{4,12},{8,0},{12,4},{1,9},{5,13},{9,1},{13,5},{2,10},{6,14},... | collective-permute-start | bytes 208904 | tf_op jit(solution)/shard_map/ppermute | solution.py:582
  40.9 5.4 %collective-permute-start.14 = (s16[272,128]{1,0:T(8,128)(2,1)S(1)}, s16[272,128]{1,0:T(8,128)(2,1)S(1)}, u32[]{:S(2)}, u32[]{:S(2)}) collective-permute-start(s16[272,128]{1,0:T(8,128)(2,1)S(1)} %get-tuple-element.49), channel_id=1, source_target_pairs={{0,12},{4,0},{8,4},{12,8},{1,13},{5,1},{9,5},{13,9},{2,14},{6,2},{... | collective-permute-start | bytes 208904 | tf_op jit(solution)/shard_map/ppermute | solution.py:582
  41.9 4.0 %collective-permute-start.11 = (f32[64,128]{1,0:T(8,128)S(1)}, f32[64,128]{1,0:T(8,128)S(1)}, u32[]{:S(2)}, u32[]{:S(2)}) collective-permute-start(f32[64,128]{1,0:T(8,128)S(1)} %add_add_fusion.refs_1_), channel_id=1, source_target_pairs={{0,2},{2,0},{1,3},{3,1},{4,6},{6,4},{5,7},{7,5},{8,10},{10,8},{9,1... | collective-permute-start | bytes 98312 | tf_op jit(solution)/shard_map/ppermute | solution.py:590
  46.3 1.5 %collective-permute-start.15 = (bf16[1,256,128]{2,1,0:T(8,128)(2,1)S(1)}, bf16[1,256,128]{2,1,0:T(8,128)(2,1)S(1)}, u32[]{:S(2)}, u32[]{:S(2)}) collective-permute-start(bf16[1,256,128]{2,1,0:T(8,128)(2,1)S(1)} %get-tuple-element.50.refs_4_.refs_7_), channel_id=1, source_target_pairs={{0,1},{1,0},{2,3},{3,2},{4,5},{5,4},{6,7},{7,6},{8,9},{9,8},{10,11... | collective-permute-start | bytes 196616 | tf_op jit(solution)/shard_map/ppermute | solution.py:582
  46.4 1.4 %collective-permute-start.16 = (bf16[1,256,128]{2,1,0:T(8,128)(2,1)S(1)}, bf16[1,256,128]{2,1,0:T(8,128)(2,1)S(1)}, u32[]{:S(2)}, u32[]{:S(2)}) collective-permute-start(bf16[1,256,128]{2,1,0:T(8,128)(2,1)S(1)} %get-tuple-element.51.refs_5_.refs_8_), channel_id=1, source_target_pairs={{0,1},{1,0},{2,3},{3,2},{4,5},{5,4},{6,7},{7,6},{8,9},{9,8},{10,11... | collective-permute-start | bytes 196616 | tf_op jit(solution)/shard_map/ppermute | solution.py:582
  46.9 1.3 %collective-permute-start.17 = (bf16[1,256,128]{2,1,0:T(8,128)(2,1)S(1)}, bf16[1,256,128]{2,1,0:T(8,128)(2,1)S(1)}, u32[]{:S(2)}, u32[]{:S(2)}) collective-permute-start(bf16[1,256,128]{2,1,0:T(8,128)(2,1)S(1)} %get-tuple-element.52.refs_6_.refs_9_), channel_id=1, source_target_pairs={{0,1},{1,0},{2,3},{3,2},{4,5},{5,4},{6,7},{7,6},{8,9},{9,8},{10,11... | collective-permute-start | bytes 196616 | tf_op jit(solution)/shard_map/ppermute | solution.py:582
  49.2 5.8 %collective-permute-start.18 = (s16[32,2176]{1,0:T(8,128)(2,1)S(1)}, s16[32,2176]{1,0:T(8,128)(2,1)S(1)}, u32[]{:S(2)}, u32[]{:S(2)}) collective-permute-start(s16[32,2176]{1,0:T(8,128)(2,1)S(1)} %shard_map.68.refs_2_), channel_id=1, source_target_pairs={{0,2},{2,0},{1,3},{3,1},{4,6},{6,4},{5,7},{7,5},{8,10},{10,8},{9,1... | collective-permute-start | bytes 417800 | tf_op jit(solution)/shard_map/ppermute | solution.py:590
  55.6 4.3 %collective-permute-start.19 = (f32[32,2048]{1,0:T(8,128)S(1)}, f32[32,2048]{1,0:T(8,128)S(1)}, u32[]{:S(2)}, u32[]{:S(2)}) collective-permute-start(f32[32,2048]{1,0:T(8,128)S(1)} %get-tuple-element.53.refs_0_.refs_3_), channel_id=1, source_target_pairs={{0,1},{1,0},{2,3},{3,2},{4,5},{5,4},{6,7},{7,6},{8,9},{9,8},{10,11... | collective-permute-start | bytes 786440 | tf_op jit(solution)/shard_map/ppermute | solution.py:582
  55.7 6.2 %collective-permute-start.20 = (s16[144,128]{1,0:T(8,128)(2,1)S(1)}, s16[144,128]{1,0:T(8,128)(2,1)S(1)}, u32[]{:S(2)}, u32[]{:S(2)}) collective-permute-start(s16[144,128]{1,0:T(8,128)(2,1)S(1)} %get-tuple-element.54), channel_id=1, source_target_pairs={{0,4},{4,8},{8,12},{12,0},{1,5},{5,9},{9,13},{13,1},{2,6},{6,10},{... | collective-permute-start | bytes 110600 | tf_op jit(solution)/shard_map/ppermute | solution.py:582
  57.5 5.5 %collective-permute-start.21 = (s16[144,128]{1,0:T(8,128)(2,1)S(1)}, s16[144,128]{1,0:T(8,128)(2,1)S(1)}, u32[]{:S(2)}, u32[]{:S(2)}) collective-permute-start(s16[144,128]{1,0:T(8,128)(2,1)S(1)} %get-tuple-element.55), channel_id=1, source_target_pairs={{0,8},{4,12},{8,0},{12,4},{1,9},{5,13},{9,1},{13,5},{2,10},{6,14},... | collective-permute-start | bytes 110600 | tf_op jit(solution)/shard_map/ppermute | solution.py:582
  59.1 4.4 %collective-permute-start.22 = (s16[144,128]{1,0:T(8,128)(2,1)S(1)}, s16[144,128]{1,0:T(8,128)(2,1)S(1)}, u32[]{:S(2)}, u32[]{:S(2)}) collective-permute-start(s16[144,128]{1,0:T(8,128)(2,1)S(1)} %get-tuple-element.56), channel_id=1, source_target_pairs={{0,12},{4,0},{8,4},{12,8},{1,13},{5,1},{9,5},{13,9},{2,14},{6,2},{... | collective-permute-start | bytes 110600 | tf_op jit(solution)/shard_map/ppermute | solution.py:582
  60.4 4.1 %collective-permute-start.23 = (f32[32,128]{1,0:T(8,128)S(1)}, f32[32,128]{1,0:T(8,128)S(1)}, u32[]{:S(2)}, u32[]{:S(2)}) collective-permute-start(f32[32,128]{1,0:T(8,128)S(1)} %shard_map.70.refs_2_), channel_id=1, source_target_pairs={{0,4},{4,0},{8,12},{12,8},{1,5},{5,1},{9,13},{13,9},{2,6},{6,2},{1... | collective-permute-start | bytes 49160 | tf_op jit(solution)/shard_map/ppermute | solution.py:590
  64.7 6.2 %collective-permute-start.24 = (s16[32,2176]{1,0:T(8,128)(2,1)S(1)}, s16[32,2176]{1,0:T(8,128)(2,1)S(1)}, u32[]{:S(2)}, u32[]{:S(2)}) collective-permute-start(s16[32,2176]{1,0:T(8,128)(2,1)S(1)} %shard_map.72.refs_1_), channel_id=1, source_target_pairs={{0,2},{2,0},{1,3},{3,1},{4,6},{6,4},{5,7},{7,5},{8,10},{10,8},{9,1... | collective-permute-start | bytes 417800 | tf_op jit(solution)/shard_map/ppermute | solution.py:590
  66.3 4.6 %collective-permute-start.25 = (f32[32,128]{1,0:T(8,128)S(1)}, f32[32,128]{1,0:T(8,128)S(1)}, u32[]{:S(2)}, u32[]{:S(2)}) collective-permute-start(f32[32,128]{1,0:T(8,128)S(1)} %add.18.after.refs_0_), channel_id=1, source_target_pairs={{0,8},{4,12},{8,0},{12,4},{1,9},{5,13},{9,1},{13,5},{2,10},{6,14},... | collective-permute-start | bytes 49160 | tf_op jit(solution)/shard_map/ppermute | solution.py:590
  71.0 1.8 %collective-permute-start.26 = (f32[32,2048]{1,0:T(8,128)S(1)}, f32[32,2048]{1,0:T(8,128)S(1)}, u32[]{:S(2)}, u32[]{:S(2)}) collective-permute-start(f32[32,2048]{1,0:T(8,128)S(1)} %shard_map.73.after.refs_1_), channel_id=1, source_target_pairs={{0,1},{1,0},{2,3},{3,2},{4,5},{5,4},{6,7},{7,6},{8,9},{9,8},{10,11... | collective-permute-start | bytes 786440 | tf_op jit(solution)/shard_map/ppermute | solution.py:582
  73.6 5.6 %collective-permute-start.27 = (f32[32,128]{1,0:T(8,128)S(1)}, f32[32,128]{1,0:T(8,128)S(1)}, u32[]{:S(2)}, u32[]{:S(2)}) collective-permute-start(f32[32,128]{1,0:T(8,128)S(1)} %get-tuple-element.58.refs_1_), channel_id=1, source_target_pairs={{0,4},{4,8},{8,12},{12,0},{1,5},{5,9},{9,13},{13,1},{2,6},{6,10},{... | collective-permute-start | bytes 49160 | tf_op jit(solution)/shard_map/ppermute | solution.py:582
  74.4 4.8 %collective-permute-start.28 = (f32[32,128]{1,0:T(8,128)S(1)}, f32[32,128]{1,0:T(8,128)S(1)}, u32[]{:S(2)}, u32[]{:S(2)}) collective-permute-start(f32[32,128]{1,0:T(8,128)S(1)} %get-tuple-element.58.refs_1_), channel_id=1, source_target_pairs={{0,8},{4,12},{8,0},{12,4},{1,9},{5,13},{9,1},{13,5},{2,10},{6,14},... | collective-permute-start | bytes 49160 | tf_op jit(solution)/shard_map/ppermute | solution.py:582
  76.6 3.7 %collective-permute-start.29 = (f32[32,128]{1,0:T(8,128)S(1)}, f32[32,128]{1,0:T(8,128)S(1)}, u32[]{:S(2)}, u32[]{:S(2)}) collective-permute-start(f32[32,128]{1,0:T(8,128)S(1)} %get-tuple-element.58.refs_1_), channel_id=1, source_target_pairs={{0,12},{4,0},{8,4},{12,8},{1,13},{5,1},{9,5},{13,9},{2,14},{6,2},{... | collective-permute-start | bytes 49160 | tf_op jit(solution)/shard_map/ppermute | solution.py:582
  (1 other events, 1.1 us)

commit v23 on v22

--- a/solution.py
+++ b/solution.py
@@ -617,7 +617,7 @@
     block_count = row_count * blocks_here
     others = range(1, row_count)
 
-    list_order = [0, *sorted(others, key=lambda k: abs(k - row_count // 2))]
+    list_order = [0, *sorted(others, key=lambda k: k * (row_count - k))]
     lists = [shift_by(pair_list[0], "rows", row_count, k) if k else pair_list[0] for k in list_order]
     self_part = call(
         functools.partial(self_distance_body, own_blocks, tile_count),

time: 83.1 us -> 82.8 us (level)
  starting transfers between devices: 39.1 us -> 36 us
  waiting for transfers between devices: 25.9 us -> 28.8 us
    ppermute x25, waiting for transfers between devices: 15.8 us -> 18.7 us  [shift_by(): lax.ppermute(value, axes, [(i, (i + shift) % size) for i in range(size)])]
    ppermute x25, starting transfers between devices: 32 us -> 29.3 us  [shift_by(): lax.ppermute(value, axes, [(i, (i + shift) % size) for i in range(size)])]
where the time goes in v23:
time: 82.8 us; the launch traced here: 82.7 us
  starting transfers between devices  36 us (43%)
  waiting for transfers between devices  28.8 us (35%)
  Pallas kernels  14.4 us (17%)
  local copies, waits for them, and re-layouts  2.01 us (2%)
  between operations  1.52 us (2%)
    ppermute x25, starting transfers between devices, shift_by(): lax.ppermute(value, axes, [(i, (i + shift) % size) for i in range(size)])  29.3 us
    ppermute x25, waiting for transfers between devices, shift_by(): lax.ppermute(value, axes, [(i, (i + shift) % size) for i in range(size)])  18.7 us
    pallas_call x18, Pallas kernels, call(): pl.pallas_call(body, out_shape=shapes, in_specs=[ANY if i in any_in else...  14.4 us
    ppermute x5, waiting for transfers between devices, pair_step(): lax.ppermute(value, name, [(i, i ^ flip) for i in range(lax.axis_size(nam...  10.1 us
    ppermute x5, starting transfers between devices, pair_step(): lax.ppermute(value, name, [(i, i ^ flip) for i in range(lax.axis_size(nam...  6.64 us
  transfers between devices with their start and end apart: 30, of which 13 were waited for; matrix products, arithmetic and copies ran while one was open for 1% of the time, Pallas kernels for 8%

profile of v23, /device:TPU:0, one launch (start us, length us, event | category | flops | bytes accessed | tf_op | source)
XLA Modules:
  0.0 82.7 jit_solution(3748828920282362755)
XLA Ops:
  0.6 3.1 %collective-permute-start = (s32[2,8]{1,0:T(2,128)}, s32[2,8]{1,0:T(2,128)S(1)}, u32[]{:S(2)}, u32[]{:S(2)}) collective-permute-start(s32[2,8]{1,0:T(2,128)} %bitcast.7), channel_id=1, source_target_pairs={{0,4},{4,8},{8,12},{12,0},{1,5},{5,9},{9,13},{13,1},{2,6},{6,10},{... | collective-permute-start | bytes 200 | tf_op jit(solution)/shard_map/ppermute | solution.py:582
  3.7 2.1 %collective-permute-start.1 = (s32[2,8]{1,0:T(2,128)}, s32[2,8]{1,0:T(2,128)S(1)}, u32[]{:S(2)}, u32[]{:S(2)}) collective-permute-start(s32[2,8]{1,0:T(2,128)} %bitcast.8), channel_id=1, source_target_pairs={{0,12},{4,0},{8,4},{12,8},{1,13},{5,1},{9,5},{13,9},{2,14},{6,2},{... | collective-permute-start | bytes 200 | tf_op jit(solution)/shard_map/ppermute | solution.py:582
  6.8 1.4 %copy-done = bf16[2048,384]{1,0:T(8,128)(2,1)S(1)} copy-done((bf16[2048,384]{1,0:T(8,128)(2,1)S(1)}, bf16[2048,384]{1,0:T(8,128)(2,1)}, u32[]{:S(2)}) %copy-start) | copy-done | bytes 1572888
  8.7 1.8 %collective-permute-done.2.refs_3_ = s32[2,8]{1,0:T(2,128)S(1)} collective-permute-done((s32[2,8]{1,0:T(2,128)}, s32[2,8]{1,0:T(2,128)S(1)}, u32[]{:S(2)}, u32[]{:S(2)}) %collective-permute-start.2) | collective-permute-done | bytes 96 | tf_op jit(solution)/shard_map/ppermute | solution.py:582
  10.5 1.5 %shard_map.60 = (s32[6,9]{1,0:T(8,128)S(1)}, bf16[256,384]{1,0:T(8,128)(2,1)S(1)}, bf16[256,384]{1,0:T(8,128)(2,1)S(1)}, bf16[256,384]{1,0:T(8,128)(2,1)S(1)}) custom-call(s32[2,8]{1,0:T(2,128)S(1)} %bitcast.10, s32[2,8]{1,0:T(2,128)S(1)} %collective-permute-done.refs_1_, s32[2,8]{1,0:T(2,128)S(1)} %collective-permute-done.1.refs_2_, ...), custom_call_target="tpu_custom_call" | custom-call | tf_op jit(solution)/shard_map/pallas_call | solution.py:70
  12.0 1.0 %collective-permute-start.3 = (bf16[256,384]{1,0:T(8,128)(2,1)S(1)}, bf16[256,384]{1,0:T(8,128)(2,1)S(1)}, u32[]{:S(2)}, u32[]{:S(2)}) collective-permute-start(bf16[256,384]{1,0:T(8,128)(2,1)S(1)} %get-tuple-element.34), channel_id=1, source_target_pairs={{0,8},{4,12},{8,0},{12,4},{1,9},{5,13},{9,1},{13,5},{2,10},{6,14},... | collective-permute-start | bytes 589832 | tf_op jit(solution)/shard_map/ppermute | solution.py:582
  13.0 1.3 %collective-permute-start.4 = (bf16[256,384]{1,0:T(8,128)(2,1)S(1)}, bf16[256,384]{1,0:T(8,128)(2,1)S(1)}, u32[]{:S(2)}, u32[]{:S(2)}) collective-permute-start(bf16[256,384]{1,0:T(8,128)(2,1)S(1)} %get-tuple-element.35), channel_id=1, source_target_pairs={{0,12},{4,0},{8,4},{12,8},{1,13},{5,1},{9,5},{13,9},{2,14},{6,2},{... | collective-permute-start | bytes 589832 | tf_op jit(solution)/shard_map/ppermute | solution.py:582
  15.9 11.0 %collective-permute-done.3.refs_4_ = bf16[256,384]{1,0:T(8,128)(2,1)S(1)} collective-permute-done((bf16[256,384]{1,0:T(8,128)(2,1)S(1)}, bf16[256,384]{1,0:T(8,128)(2,1)S(1)}, u32[]{:S(2)}, u32[]{:S(2)}) %collective-permute-start.3) | collective-permute-done | bytes 196640 | tf_op jit(solution)/shard_map/ppermute | solution.py:582
  26.9 1.0 %shard_map.62.refs_2_ = f32[1024,128]{1,0:T(8,128)S(1)} custom-call(s32[6,9]{1,0:T(8,128)S(1)} %get-tuple-element.31.refs_0_, bf16[2048,384]{1,0:T(8,128)(2,1)S(1)} %copy-done, f32[2048,128]{1,0:T(8,128)S(1)} %get-tuple-element.32.refs_2_, f32[256,128]{1,0:T(8,128)S(1)} %get-tuple-element.33.refs_3_, bf16[256,384]{1,0:T(8,128)(2,1)S(1)} %collective-permute-done.3.refs_4_, ...), custom_call_target="tpu_custom_call" | custom-call | tf_op jit(solution)/shard_map/pallas_call | solution.py:70
  30.8 2.3 %collective-permute-start.10 = (f32[64,128]{1,0:T(8,128)S(1)}, f32[64,128]{1,0:T(8,128)S(1)}, u32[]{:S(2)}, u32[]{:S(2)}) collective-permute-start(f32[64,128]{1,0:T(8,128)S(1)} %get-tuple-element.41), channel_id=1, source_target_pairs={{0,12},{4,0},{8,4},{12,8},{1,13},{5,1},{9,5},{13,9},{2,14},{6,2},{... | collective-permute-start | bytes 98312 | tf_op jit(solution)/shard_map/ppermute | solution.py:582
  33.1 2.1 %collective-permute-start.8 = (f32[64,128]{1,0:T(8,128)S(1)}, f32[64,128]{1,0:T(8,128)S(1)}, u32[]{:S(2)}, u32[]{:S(2)}) collective-permute-start(f32[64,128]{1,0:T(8,128)S(1)} %get-tuple-element.41), channel_id=1, source_target_pairs={{0,4},{4,8},{8,12},{12,0},{1,5},{5,9},{9,13},{13,1},{2,6},{6,10},{... | collective-permute-start | bytes 98312 | tf_op jit(solution)/shard_map/ppermute | solution.py:582
  35.2 2.3 %collective-permute-start.9 = (f32[64,128]{1,0:T(8,128)S(1)}, f32[64,128]{1,0:T(8,128)S(1)}, u32[]{:S(2)}, u32[]{:S(2)}) collective-permute-start(f32[64,128]{1,0:T(8,128)S(1)} %get-tuple-element.41), channel_id=1, source_target_pairs={{0,8},{4,12},{8,0},{12,4},{1,9},{5,13},{9,1},{13,5},{2,10},{6,14},... | collective-permute-start | bytes 98312 | tf_op jit(solution)/shard_map/ppermute | solution.py:582
  37.6 2.5 %collective-permute-start.13 = (s16[272,128]{1,0:T(8,128)(2,1)S(1)}, s16[272,128]{1,0:T(8,128)(2,1)S(1)}, u32[]{:S(2)}, u32[]{:S(2)}) collective-permute-start(s16[272,128]{1,0:T(8,128)(2,1)S(1)} %get-tuple-element.48), channel_id=1, source_target_pairs={{0,8},{4,12},{8,0},{12,4},{1,9},{5,13},{9,1},{13,5},{2,10},{6,14},... | collective-permute-start | bytes 208904 | tf_op jit(solution)/shard_map/ppermute | solution.py:582
  40.1 1.3 %collective-permute-start.14 = (s16[272,128]{1,0:T(8,128)(2,1)S(1)}, s16[272,128]{1,0:T(8,128)(2,1)S(1)}, u32[]{:S(2)}, u32[]{:S(2)}) collective-permute-start(s16[272,128]{1,0:T(8,128)(2,1)S(1)} %get-tuple-element.49), channel_id=1, source_target_pairs={{0,12},{4,0},{8,4},{12,8},{1,13},{5,1},{9,5},{13,9},{2,14},{6,2},{... | collective-permute-start | bytes 208904 | tf_op jit(solution)/shard_map/ppermute | solution.py:582
  41.4 1.6 %collective-permute-start.11 = (f32[64,128]{1,0:T(8,128)S(1)}, f32[64,128]{1,0:T(8,128)S(1)}, u32[]{:S(2)}, u32[]{:S(2)}) collective-permute-start(f32[64,128]{1,0:T(8,128)S(1)} %add_add_fusion.refs_1_), channel_id=1, source_target_pairs={{0,2},{2,0},{1,3},{3,1},{4,6},{6,4},{5,7},{7,5},{8,10},{10,8},{9,1... | collective-permute-start | bytes 98312 | tf_op jit(solution)/shard_map/ppermute | solution.py:590
  43.0 2.4 %collective-permute-done.11.refs_2_.refs_3_ = f32[64,128]{1,0:T(8,128)S(1)} collective-permute-done((f32[64,128]{1,0:T(8,128)S(1)}, f32[64,128]{1,0:T(8,128)S(1)}, u32[]{:S(2)}, u32[]{:S(2)}) %collective-permute-start.11) | collective-permute-done | bytes 32800 | tf_op jit(solution)/shard_map/ppermute | solution.py:590
  47.8 1.0 %shard_map.68.refs_2_ = s16[32,2176]{1,0:T(8,128)(2,1)S(1)} custom-call(s32[6,9]{1,0:T(8,128)S(1)} %get-tuple-element.31.refs_0_, f32[64,128]{1,0:T(8,128)S(1)} %get-tuple-element.45.refs_1_.refs_0_, f32[32,2048]{1,0:T(8,128)S(1)} %get-tuple-element.46.refs_2_, bf16[8,256,128]{2,1,0:T(8,128)(2,1)S(1)} %get-tuple-element.42.refs_4_.refs_3_.refs_6_, ...), custom_call_target="tpu_custom_call" | custom-call | tf_op jit(solution)/shard_map/pallas_call | solution.py:70
  48.8 1.6 %collective-permute-start.18 = (s16[32,2176]{1,0:T(8,128)(2,1)S(1)}, s16[32,2176]{1,0:T(8,128)(2,1)S(1)}, u32[]{:S(2)}, u32[]{:S(2)}) collective-permute-start(s16[32,2176]{1,0:T(8,128)(2,1)S(1)} %shard_map.68.refs_2_), channel_id=1, source_target_pairs={{0,2},{2,0},{1,3},{3,1},{4,6},{6,4},{5,7},{7,5},{8,10},{10,8},{9,1... | collective-permute-start | bytes 417800 | tf_op jit(solution)/shard_map/ppermute | solution.py:590
  50.4 4.2 %collective-permute-done.18.refs_3_ = s16[32,2176]{1,0:T(8,128)(2,1)S(1)} collective-permute-done((s16[32,2176]{1,0:T(8,128)(2,1)S(1)}, s16[32,2176]{1,0:T(8,128)(2,1)S(1)}, u32[]{:S(2)}, u32[]{:S(2)}) %collective-permute-start.18) | collective-permute-done | bytes 139296 | tf_op jit(solution)/shard_map/ppermute | solution.py:590
  55.3 1.4 %collective-permute-start.20 = (s16[144,128]{1,0:T(8,128)(2,1)S(1)}, s16[144,128]{1,0:T(8,128)(2,1)S(1)}, u32[]{:S(2)}, u32[]{:S(2)}) collective-permute-start(s16[144,128]{1,0:T(8,128)(2,1)S(1)} %get-tuple-element.54), channel_id=1, source_target_pairs={{0,4},{4,8},{8,12},{12,0},{1,5},{5,9},{9,13},{13,1},{2,6},{6,10},{... | collective-permute-start | bytes 110600 | tf_op jit(solution)/shard_map/ppermute | solution.py:582
  56.8 1.7 %collective-permute-start.21 = (s16[144,128]{1,0:T(8,128)(2,1)S(1)}, s16[144,128]{1,0:T(8,128)(2,1)S(1)}, u32[]{:S(2)}, u32[]{:S(2)}) collective-permute-start(s16[144,128]{1,0:T(8,128)(2,1)S(1)} %get-tuple-element.55), channel_id=1, source_target_pairs={{0,8},{4,12},{8,0},{12,4},{1,9},{5,13},{9,1},{13,5},{2,10},{6,14},... | collective-permute-start | bytes 110600 | tf_op jit(solution)/shard_map/ppermute | solution.py:582
  58.5 1.4 %collective-permute-start.22 = (s16[144,128]{1,0:T(8,128)(2,1)S(1)}, s16[144,128]{1,0:T(8,128)(2,1)S(1)}, u32[]{:S(2)}, u32[]{:S(2)}) collective-permute-start(s16[144,128]{1,0:T(8,128)(2,1)S(1)} %get-tuple-element.56), channel_id=1, source_target_pairs={{0,12},{4,0},{8,4},{12,8},{1,13},{5,1},{9,5},{13,9},{2,14},{6,2},{... | collective-permute-start | bytes 110600 | tf_op jit(solution)/shard_map/ppermute | solution.py:582
  61.5 1.2 %collective-permute-done.21.refs_14_ = s16[144,128]{1,0:T(8,128)(2,1)S(1)} collective-permute-done((s16[144,128]{1,0:T(8,128)(2,1)S(1)}, s16[144,128]{1,0:T(8,128)(2,1)S(1)}, u32[]{:S(2)}, u32[]{:S(2)}) %collective-permute-start.21) | collective-permute-done | bytes 36896 | tf_op jit(solution)/shard_map/ppermute | solution.py:582
  63.2 1.0 %shard_map.71.total = f32[32,2048]{1,0:T(8,128)S(1)} custom-call(s32[6,9]{1,0:T(8,128)S(1)} %get-tuple-element.31.refs_0_, f32[64,128]{1,0:T(8,128)S(1)} %get-tuple-element.45.refs_1_.refs_0_, f32[32,128]{1,0:T(8,128)S(1)} %shard_map.70.refs_2_, f32[32,2048]{1,0:T(8,128)S(1)} %get-tuple-element.53.refs_0_.refs_3_, ...), custom_call_target="tpu_custom_call" | custom-call | tf_op jit(solution)/shard_map/pallas_call | solution.py:70
  64.3 1.6 %collective-permute-start.24 = (s16[32,2176]{1,0:T(8,128)(2,1)S(1)}, s16[32,2176]{1,0:T(8,128)(2,1)S(1)}, u32[]{:S(2)}, u32[]{:S(2)}) collective-permute-start(s16[32,2176]{1,0:T(8,128)(2,1)S(1)} %shard_map.72.refs_1_), channel_id=1, source_target_pairs={{0,2},{2,0},{1,3},{3,1},{4,6},{6,4},{5,7},{7,5},{8,10},{10,8},{9,1... | collective-permute-start | bytes 417800 | tf_op jit(solution)/shard_map/ppermute | solution.py:590
  65.9 1.3 %collective-permute-start.25 = (f32[32,128]{1,0:T(8,128)S(1)}, f32[32,128]{1,0:T(8,128)S(1)}, u32[]{:S(2)}, u32[]{:S(2)}) collective-permute-start(f32[32,128]{1,0:T(8,128)S(1)} %add.18.after.refs_0_), channel_id=1, source_target_pairs={{0,8},{4,12},{8,0},{12,4},{1,9},{5,13},{9,1},{13,5},{2,10},{6,14},... | collective-permute-start | bytes 49160 | tf_op jit(solution)/shard_map/ppermute | solution.py:590
  67.2 3.4 %collective-permute-done.25.refs_3_.refs_1_ = f32[32,128]{1,0:T(8,128)S(1)} collective-permute-done((f32[32,128]{1,0:T(8,128)S(1)}, f32[32,128]{1,0:T(8,128)S(1)}, u32[]{:S(2)}, u32[]{:S(2)}) %collective-permute-start.25) | collective-permute-done | bytes 16416 | tf_op jit(solution)/shard_map/ppermute | solution.py:590
  70.7 1.7 %shard_map.74.refs_0_ = f32[64,64]{1,0:T(8,128)S(1)} custom-call(f32[32,2048]{1,0:T(8,128)S(1)} %shard_map.73.after.refs_1_, f32[32,128]{1,0:T(8,128)S(1)} %add.18.after.refs_0_, f32[32,128]{1,0:T(8,128)S(1)} %collective-permute-done.25.refs_3_.refs_1_), custom_call_target="tpu_custom_call" | custom-call | tf_op jit(solution)/shard_map/pallas_call | solution.py:70
  74.1 2.2 %collective-permute-start.28 = (f32[32,128]{1,0:T(8,128)S(1)}, f32[32,128]{1,0:T(8,128)S(1)}, u32[]{:S(2)}, u32[]{:S(2)}) collective-permute-start(f32[32,128]{1,0:T(8,128)S(1)} %get-tuple-element.58.refs_1_), channel_id=1, source_target_pairs={{0,8},{4,12},{8,0},{12,4},{1,9},{5,13},{9,1},{13,5},{2,10},{6,14},... | collective-permute-start | bytes 49160 | tf_op jit(solution)/shard_map/ppermute | solution.py:582
  76.3 1.2 %collective-permute-start.29 = (f32[32,128]{1,0:T(8,128)S(1)}, f32[32,128]{1,0:T(8,128)S(1)}, u32[]{:S(2)}, u32[]{:S(2)}) collective-permute-start(f32[32,128]{1,0:T(8,128)S(1)} %get-tuple-element.58.refs_1_), channel_id=1, source_target_pairs={{0,12},{4,0},{8,4},{12,8},{1,13},{5,1},{9,5},{13,9},{2,14},{6,2},{... | collective-permute-start | bytes 49160 | tf_op jit(solution)/shard_map/ppermute | solution.py:582
  78.9 1.2 %collective-permute-done.29.refs_4_ = f32[32,128]{1,0:T(8,128)S(1)} collective-permute-done((f32[32,128]{1,0:T(8,128)S(1)}, f32[32,128]{1,0:T(8,128)S(1)}, u32[]{:S(2)}, u32[]{:S(2)}) %collective-permute-start.29) | collective-permute-done | bytes 16416 | tf_op jit(solution)/shard_map/ppermute | solution.py:582
  80.1 2.6 %shard_map.76 = f32[32,2048]{1,0:T(8,128)} custom-call(bf16[128,2048]{1,0:T(8,128)(2,1)S(1)} %get-tuple-element.57.refs_0_, f32[32,128]{1,0:T(8,128)S(1)} %get-tuple-element.58.refs_1_, f32[32,128]{1,0:T(8,128)S(1)} %collective-permute-done.27.refs_2_, f32[32,128]{1,0:T(8,128)S(1)} %collective-permute-done.28.refs_3_, ...), custom_call_target="tpu_custom_call" | custom-call | tf_op jit(solution)/shard_map/pallas_call | solution.py:70
  (55 shorter events, 13.7 us)
Async XLA Ops:
  0.6 9.9 %copy-start.2 = (s32[1,2,8]{2,1,0:T(2,128)S(1)}, s32[1,2,8]{2,1,0:T(2,128)}, u32[]{:S(2)}) copy-start(s32[1,2,8]{2,1,0:T(2,128)} %param.6) | copy-start | bytes 196
  0.6 8.0 %collective-permute-start = (s32[2,8]{1,0:T(2,128)}, s32[2,8]{1,0:T(2,128)S(1)}, u32[]{:S(2)}, u32[]{:S(2)}) collective-permute-start(s32[2,8]{1,0:T(2,128)} %bitcast.7), channel_id=1, source_target_pairs={{0,4},{4,8},{8,12},{12,0},{1,5},{5,9},{9,13},{13,1},{2,6},{6,10},{... | collective-permute-start | bytes 200 | tf_op jit(solution)/shard_map/ppermute | solution.py:582
  3.7 4.9 %collective-permute-start.1 = (s32[2,8]{1,0:T(2,128)}, s32[2,8]{1,0:T(2,128)S(1)}, u32[]{:S(2)}, u32[]{:S(2)}) collective-permute-start(s32[2,8]{1,0:T(2,128)} %bitcast.8), channel_id=1, source_target_pairs={{0,12},{4,0},{8,4},{12,8},{1,13},{5,1},{9,5},{13,9},{2,14},{6,2},{... | collective-permute-start | bytes 200 | tf_op jit(solution)/shard_map/ppermute | solution.py:582
  5.8 4.7 %collective-permute-start.2 = (s32[2,8]{1,0:T(2,128)}, s32[2,8]{1,0:T(2,128)S(1)}, u32[]{:S(2)}, u32[]{:S(2)}) collective-permute-start(s32[2,8]{1,0:T(2,128)} %bitcast.9), channel_id=1, source_target_pairs={{0,8},{4,12},{8,0},{12,4},{1,9},{5,13},{9,1},{13,5},{2,10},{6,14},... | collective-permute-start | bytes 200 | tf_op jit(solution)/shard_map/ppermute | solution.py:582
  6.8 1.4 %copy-start = (bf16[2048,384]{1,0:T(8,128)(2,1)S(1)}, bf16[2048,384]{1,0:T(8,128)(2,1)}, u32[]{:S(2)}) copy-start(bf16[2048,384]{1,0:T(8,128)(2,1)} %refs_1_.4) | copy-start | bytes 4718596
  12.0 14.9 %collective-permute-start.3 = (bf16[256,384]{1,0:T(8,128)(2,1)S(1)}, bf16[256,384]{1,0:T(8,128)(2,1)S(1)}, u32[]{:S(2)}, u32[]{:S(2)}) collective-permute-start(bf16[256,384]{1,0:T(8,128)(2,1)S(1)} %get-tuple-element.34), channel_id=1, source_target_pairs={{0,8},{4,12},{8,0},{12,4},{1,9},{5,13},{9,1},{13,5},{2,10},{6,14},... | collective-permute-start | bytes 589832 | tf_op jit(solution)/shard_map/ppermute | solution.py:582
  13.0 13.9 %collective-permute-start.4 = (bf16[256,384]{1,0:T(8,128)(2,1)S(1)}, bf16[256,384]{1,0:T(8,128)(2,1)S(1)}, u32[]{:S(2)}, u32[]{:S(2)}) collective-permute-start(bf16[256,384]{1,0:T(8,128)(2,1)S(1)} %get-tuple-element.35), channel_id=1, source_target_pairs={{0,12},{4,0},{8,4},{12,8},{1,13},{5,1},{9,5},{13,9},{2,14},{6,2},{... | collective-permute-start | bytes 589832 | tf_op jit(solution)/shard_map/ppermute | solution.py:582
  14.4 12.5 %collective-permute-start.5 = (bf16[256,384]{1,0:T(8,128)(2,1)S(1)}, bf16[256,384]{1,0:T(8,128)(2,1)S(1)}, u32[]{:S(2)}, u32[]{:S(2)}) collective-permute-start(bf16[256,384]{1,0:T(8,128)(2,1)S(1)} %get-tuple-element.36), channel_id=1, source_target_pairs={{0,4},{4,8},{8,12},{12,0},{1,5},{5,9},{9,13},{13,1},{2,6},{6,10},{... | collective-permute-start | bytes 589832 | tf_op jit(solution)/shard_map/ppermute | solution.py:582
  15.1 13.7 %collective-permute-start.7 = (f32[1024,128]{1,0:T(8,128)S(1)}, f32[1024,128]{1,0:T(8,128)S(1)}, u32[]{:S(2)}, u32[]{:S(2)}) collective-permute-start(f32[1024,128]{1,0:T(8,128)S(1)} %shard_map.59.refs_5_.mine), channel_id=1, source_target_pairs={{0,1},{1,0},{2,3},{3,2},{4,5},{5,4},{6,7},{7,6},{8,9},{9,8},{10,11... | collective-permute-start | bytes 1572872 | tf_op jit(solution)/shard_map/ppermute | solution.py:582
  27.9 2.0 %collective-permute-start.6 = (f32[1024,128]{1,0:T(8,128)S(1)}, f32[1024,128]{1,0:T(8,128)S(1)}, u32[]{:S(2)}, u32[]{:S(2)}) collective-permute-start(f32[1024,128]{1,0:T(8,128)S(1)} %shard_map.62.refs_2_), channel_id=1, source_target_pairs={{0,1},{1,0},{2,3},{3,2},{4,5},{5,4},{6,7},{7,6},{8,9},{9,8},{10,11... | collective-permute-start | bytes 1572872 | tf_op jit(solution)/shard_map/ppermute | solution.py:582
  30.8 9.3 %collective-permute-start.10 = (f32[64,128]{1,0:T(8,128)S(1)}, f32[64,128]{1,0:T(8,128)S(1)}, u32[]{:S(2)}, u32[]{:S(2)}) collective-permute-start(f32[64,128]{1,0:T(8,128)S(1)} %get-tuple-element.41), channel_id=1, source_target_pairs={{0,12},{4,0},{8,4},{12,8},{1,13},{5,1},{9,5},{13,9},{2,14},{6,2},{... | collective-permute-start | bytes 98312 | tf_op jit(solution)/shard_map/ppermute | solution.py:582
  33.1 8.3 %collective-permute-start.8 = (f32[64,128]{1,0:T(8,128)S(1)}, f32[64,128]{1,0:T(8,128)S(1)}, u32[]{:S(2)}, u32[]{:S(2)}) collective-permute-start(f32[64,128]{1,0:T(8,128)S(1)} %get-tuple-element.41), channel_id=1, source_target_pairs={{0,4},{4,8},{8,12},{12,0},{1,5},{5,9},{9,13},{13,1},{2,6},{6,10},{... | collective-permute-start | bytes 98312 | tf_op jit(solution)/shard_map/ppermute | solution.py:582
  35.2 6.2 %collective-permute-start.9 = (f32[64,128]{1,0:T(8,128)S(1)}, f32[64,128]{1,0:T(8,128)S(1)}, u32[]{:S(2)}, u32[]{:S(2)}) collective-permute-start(f32[64,128]{1,0:T(8,128)S(1)} %get-tuple-element.41), channel_id=1, source_target_pairs={{0,8},{4,12},{8,0},{12,4},{1,9},{5,13},{9,1},{13,5},{2,10},{6,14},... | collective-permute-start | bytes 98312 | tf_op jit(solution)/shard_map/ppermute | solution.py:582
  37.6 7.8 %collective-permute-start.12 = (s16[272,128]{1,0:T(8,128)(2,1)S(1)}, s16[272,128]{1,0:T(8,128)(2,1)S(1)}, u32[]{:S(2)}, u32[]{:S(2)}) collective-permute-start(s16[272,128]{1,0:T(8,128)(2,1)S(1)} %get-tuple-element.47), channel_id=1, source_target_pairs={{0,4},{4,8},{8,12},{12,0},{1,5},{5,9},{9,13},{13,1},{2,6},{6,10},{... | collective-permute-start | bytes 208904 | tf_op jit(solution)/shard_map/ppermute | solution.py:582
  37.6 8.3 %collective-permute-start.13 = (s16[272,128]{1,0:T(8,128)(2,1)S(1)}, s16[272,128]{1,0:T(8,128)(2,1)S(1)}, u32[]{:S(2)}, u32[]{:S(2)}) collective-permute-start(s16[272,128]{1,0:T(8,128)(2,1)S(1)} %get-tuple-element.48), channel_id=1, source_target_pairs={{0,8},{4,12},{8,0},{12,4},{1,9},{5,13},{9,1},{13,5},{2,10},{6,14},... | collective-permute-start | bytes 208904 | tf_op jit(solution)/shard_map/ppermute | solution.py:582
  40.1 5.8 %collective-permute-start.14 = (s16[272,128]{1,0:T(8,128)(2,1)S(1)}, s16[272,128]{1,0:T(8,128)(2,1)S(1)}, u32[]{:S(2)}, u32[]{:S(2)}) collective-permute-start(s16[272,128]{1,0:T(8,128)(2,1)S(1)} %get-tuple-element.49), channel_id=1, source_target_pairs={{0,12},{4,0},{8,4},{12,8},{1,13},{5,1},{9,5},{13,9},{2,14},{6,2},{... | collective-permute-start | bytes 208904 | tf_op jit(solution)/shard_map/ppermute | solution.py:582
  41.4 4.0 %collective-permute-start.11 = (f32[64,128]{1,0:T(8,128)S(1)}, f32[64,128]{1,0:T(8,128)S(1)}, u32[]{:S(2)}, u32[]{:S(2)}) collective-permute-start(f32[64,128]{1,0:T(8,128)S(1)} %add_add_fusion.refs_1_), channel_id=1, source_target_pairs={{0,2},{2,0},{1,3},{3,1},{4,6},{6,4},{5,7},{7,5},{8,10},{10,8},{9,1... | collective-permute-start | bytes 98312 | tf_op jit(solution)/shard_map/ppermute | solution.py:590
  46.0 1.5 %collective-permute-start.15 = (bf16[1,256,128]{2,1,0:T(8,128)(2,1)S(1)}, bf16[1,256,128]{2,1,0:T(8,128)(2,1)S(1)}, u32[]{:S(2)}, u32[]{:S(2)}) collective-permute-start(bf16[1,256,128]{2,1,0:T(8,128)(2,1)S(1)} %get-tuple-element.50.refs_4_.refs_7_), channel_id=1, source_target_pairs={{0,1},{1,0},{2,3},{3,2},{4,5},{5,4},{6,7},{7,6},{8,9},{9,8},{10,11... | collective-permute-start | bytes 196616 | tf_op jit(solution)/shard_map/ppermute | solution.py:582
  46.0 1.4 %collective-permute-start.16 = (bf16[1,256,128]{2,1,0:T(8,128)(2,1)S(1)}, bf16[1,256,128]{2,1,0:T(8,128)(2,1)S(1)}, u32[]{:S(2)}, u32[]{:S(2)}) collective-permute-start(bf16[1,256,128]{2,1,0:T(8,128)(2,1)S(1)} %get-tuple-element.51.refs_5_.refs_8_), channel_id=1, source_target_pairs={{0,1},{1,0},{2,3},{3,2},{4,5},{5,4},{6,7},{7,6},{8,9},{9,8},{10,11... | collective-permute-start | bytes 196616 | tf_op jit(solution)/shard_map/ppermute | solution.py:582
  46.5 1.3 %collective-permute-start.17 = (bf16[1,256,128]{2,1,0:T(8,128)(2,1)S(1)}, bf16[1,256,128]{2,1,0:T(8,128)(2,1)S(1)}, u32[]{:S(2)}, u32[]{:S(2)}) collective-permute-start(bf16[1,256,128]{2,1,0:T(8,128)(2,1)S(1)} %get-tuple-element.52.refs_6_.refs_9_), channel_id=1, source_target_pairs={{0,1},{1,0},{2,3},{3,2},{4,5},{5,4},{6,7},{7,6},{8,9},{9,8},{10,11... | collective-permute-start | bytes 196616 | tf_op jit(solution)/shard_map/ppermute | solution.py:582
  48.8 5.8 %collective-permute-start.18 = (s16[32,2176]{1,0:T(8,128)(2,1)S(1)}, s16[32,2176]{1,0:T(8,128)(2,1)S(1)}, u32[]{:S(2)}, u32[]{:S(2)}) collective-permute-start(s16[32,2176]{1,0:T(8,128)(2,1)S(1)} %shard_map.68.refs_2_), channel_id=1, source_target_pairs={{0,2},{2,0},{1,3},{3,1},{4,6},{6,4},{5,7},{7,5},{8,10},{10,8},{9,1... | collective-permute-start | bytes 417800 | tf_op jit(solution)/shard_map/ppermute | solution.py:590
  55.3 4.6 %collective-permute-start.19 = (f32[32,2048]{1,0:T(8,128)S(1)}, f32[32,2048]{1,0:T(8,128)S(1)}, u32[]{:S(2)}, u32[]{:S(2)}) collective-permute-start(f32[32,2048]{1,0:T(8,128)S(1)} %get-tuple-element.53.refs_0_.refs_3_), channel_id=1, source_target_pairs={{0,1},{1,0},{2,3},{3,2},{4,5},{5,4},{6,7},{7,6},{8,9},{9,8},{10,11... | collective-permute-start | bytes 786440 | tf_op jit(solution)/shard_map/ppermute | solution.py:582
  55.3 6.2 %collective-permute-start.20 = (s16[144,128]{1,0:T(8,128)(2,1)S(1)}, s16[144,128]{1,0:T(8,128)(2,1)S(1)}, u32[]{:S(2)}, u32[]{:S(2)}) collective-permute-start(s16[144,128]{1,0:T(8,128)(2,1)S(1)} %get-tuple-element.54), channel_id=1, source_target_pairs={{0,4},{4,8},{8,12},{12,0},{1,5},{5,9},{9,13},{13,1},{2,6},{6,10},{... | collective-permute-start | bytes 110600 | tf_op jit(solution)/shard_map/ppermute | solution.py:582
  56.8 5.9 %collective-permute-start.21 = (s16[144,128]{1,0:T(8,128)(2,1)S(1)}, s16[144,128]{1,0:T(8,128)(2,1)S(1)}, u32[]{:S(2)}, u32[]{:S(2)}) collective-permute-start(s16[144,128]{1,0:T(8,128)(2,1)S(1)} %get-tuple-element.55), channel_id=1, source_target_pairs={{0,8},{4,12},{8,0},{12,4},{1,9},{5,13},{9,1},{13,5},{2,10},{6,14},... | collective-permute-start | bytes 110600 | tf_op jit(solution)/shard_map/ppermute | solution.py:582
  58.5 4.7 %collective-permute-start.22 = (s16[144,128]{1,0:T(8,128)(2,1)S(1)}, s16[144,128]{1,0:T(8,128)(2,1)S(1)}, u32[]{:S(2)}, u32[]{:S(2)}) collective-permute-start(s16[144,128]{1,0:T(8,128)(2,1)S(1)} %get-tuple-element.56), channel_id=1, source_target_pairs={{0,12},{4,0},{8,4},{12,8},{1,13},{5,1},{9,5},{13,9},{2,14},{6,2},{... | collective-permute-start | bytes 110600 | tf_op jit(solution)/shard_map/ppermute | solution.py:582
  60.3 3.9 %collective-permute-start.23 = (f32[32,128]{1,0:T(8,128)S(1)}, f32[32,128]{1,0:T(8,128)S(1)}, u32[]{:S(2)}, u32[]{:S(2)}) collective-permute-start(f32[32,128]{1,0:T(8,128)S(1)} %shard_map.70.refs_2_), channel_id=1, source_target_pairs={{0,4},{4,0},{8,12},{12,8},{1,5},{5,1},{9,13},{13,9},{2,6},{6,2},{1... | collective-permute-start | bytes 49160 | tf_op jit(solution)/shard_map/ppermute | solution.py:590
  64.3 6.2 %collective-permute-start.24 = (s16[32,2176]{1,0:T(8,128)(2,1)S(1)}, s16[32,2176]{1,0:T(8,128)(2,1)S(1)}, u32[]{:S(2)}, u32[]{:S(2)}) collective-permute-start(s16[32,2176]{1,0:T(8,128)(2,1)S(1)} %shard_map.72.refs_1_), channel_id=1, source_target_pairs={{0,2},{2,0},{1,3},{3,1},{4,6},{6,4},{5,7},{7,5},{8,10},{10,8},{9,1... | collective-permute-start | bytes 417800 | tf_op jit(solution)/shard_map/ppermute | solution.py:590
  65.9 4.6 %collective-permute-start.25 = (f32[32,128]{1,0:T(8,128)S(1)}, f32[32,128]{1,0:T(8,128)S(1)}, u32[]{:S(2)}, u32[]{:S(2)}) collective-permute-start(f32[32,128]{1,0:T(8,128)S(1)} %add.18.after.refs_0_), channel_id=1, source_target_pairs={{0,8},{4,12},{8,0},{12,4},{1,9},{5,13},{9,1},{13,5},{2,10},{6,14},... | collective-permute-start | bytes 49160 | tf_op jit(solution)/shard_map/ppermute | solution.py:590
  70.6 1.8 %collective-permute-start.26 = (f32[32,2048]{1,0:T(8,128)S(1)}, f32[32,2048]{1,0:T(8,128)S(1)}, u32[]{:S(2)}, u32[]{:S(2)}) collective-permute-start(f32[32,2048]{1,0:T(8,128)S(1)} %shard_map.73.after.refs_1_), channel_id=1, source_target_pairs={{0,1},{1,0},{2,3},{3,2},{4,5},{5,4},{6,7},{7,6},{8,9},{9,8},{10,11... | collective-permute-start | bytes 786440 | tf_op jit(solution)/shard_map/ppermute | solution.py:582
  73.3 5.6 %collective-permute-start.27 = (f32[32,128]{1,0:T(8,128)S(1)}, f32[32,128]{1,0:T(8,128)S(1)}, u32[]{:S(2)}, u32[]{:S(2)}) collective-permute-start(f32[32,128]{1,0:T(8,128)S(1)} %get-tuple-element.58.refs_1_), channel_id=1, source_target_pairs={{0,4},{4,8},{8,12},{12,0},{1,5},{5,9},{9,13},{13,1},{2,6},{6,10},{... | collective-permute-start | bytes 49160 | tf_op jit(solution)/shard_map/ppermute | solution.py:582
  74.1 4.8 %collective-permute-start.28 = (f32[32,128]{1,0:T(8,128)S(1)}, f32[32,128]{1,0:T(8,128)S(1)}, u32[]{:S(2)}, u32[]{:S(2)}) collective-permute-start(f32[32,128]{1,0:T(8,128)S(1)} %get-tuple-element.58.refs_1_), channel_id=1, source_target_pairs={{0,8},{4,12},{8,0},{12,4},{1,9},{5,13},{9,1},{13,5},{2,10},{6,14},... | collective-permute-start | bytes 49160 | tf_op jit(solution)/shard_map/ppermute | solution.py:582
  76.3 3.7 %collective-permute-start.29 = (f32[32,128]{1,0:T(8,128)S(1)}, f32[32,128]{1,0:T(8,128)S(1)}, u32[]{:S(2)}, u32[]{:S(2)}) collective-permute-start(f32[32,128]{1,0:T(8,128)S(1)} %get-tuple-element.58.refs_1_), channel_id=1, source_target_pairs={{0,12},{4,0},{8,4},{12,8},{1,13},{5,1},{9,5},{13,9},{2,14},{6,2},{... | collective-permute-start | bytes 49160 | tf_op jit(solution)/shard_map/ppermute | solution.py:582
  (1 other events, 1.1 us)

commit v24 on v23

--- a/solution.py
+++ b/solution.py
@@ -196,10 +196,10 @@
             scaled = lines[i] * reciprocal
             ratio = [pivot[i][k] * reciprocal for k in range(step)]
             for k in range(i + 1, step):
-                lines[k] = lines[k] - pivot[k][i] * scaled
+                lines[k] = lines[k] - pivot[i][k] * scaled
                 columns[k] = columns[k] - columns[i] * ratio[k]
-                for m in range(i + 1, step):
-                    pivot[k][m] = pivot[k][m] - pivot[k][i] * ratio[m]
+                for m in range(k, step):
+                    pivot[k][m] = pivot[k][m] - pivot[i][k] * ratio[m]
             state = state - jnp.where(rows > base + i, columns[i], 0.0) * scaled
     state = jnp.concatenate([*done, state], axis=0)
     pivots = jnp.sum(jnp.where(eye_mask(n), state[:, :n], 0.0), axis=1, keepdims=True)

time: 82.8 us -> 82.7 us (level)
  no operation moved by 1% of the time
where the time goes in v24:
time: 82.7 us; the launch traced here: 82.5 us
  starting transfers between devices  36 us (44%)
  waiting for transfers between devices  28.8 us (35%)
  Pallas kernels  14.2 us (17%)
  local copies, waits for them, and re-layouts  2.01 us (2%)
  between operations  1.52 us (2%)
    ppermute x25, starting transfers between devices, shift_by(): lax.ppermute(value, axes, [(i, (i + shift) % size) for i in range(size)])  29.3 us
    ppermute x25, waiting for transfers between devices, shift_by(): lax.ppermute(value, axes, [(i, (i + shift) % size) for i in range(size)])  18.7 us
    pallas_call x18, Pallas kernels, call(): pl.pallas_call(body, out_shape=shapes, in_specs=[ANY if i in any_in else...  14.2 us
    ppermute x5, waiting for transfers between devices, pair_step(): lax.ppermute(value, name, [(i, i ^ flip) for i in range(lax.axis_size(nam...  10.1 us
    ppermute x5, starting transfers between devices, pair_step(): lax.ppermute(value, name, [(i, i ^ flip) for i in range(lax.axis_size(nam...  6.65 us
  transfers between devices with their start and end apart: 30, of which 13 were waited for; matrix products, arithmetic and copies ran while one was open for 1% of the time, Pallas kernels for 8%

profile of v24, /device:TPU:0, one launch (start us, length us, event | category | flops | bytes accessed | tf_op | source)
XLA Modules:
  0.0 82.5 jit_solution(4343087424485090690)
XLA Ops:
  0.6 3.1 %collective-permute-start = (s32[2,8]{1,0:T(2,128)}, s32[2,8]{1,0:T(2,128)S(1)}, u32[]{:S(2)}, u32[]{:S(2)}) collective-permute-start(s32[2,8]{1,0:T(2,128)} %bitcast.7), channel_id=1, source_target_pairs={{0,4},{4,8},{8,12},{12,0},{1,5},{5,9},{9,13},{13,1},{2,6},{6,10},{... | collective-permute-start | bytes 200 | tf_op jit(solution)/shard_map/ppermute | solution.py:582
  3.7 2.1 %collective-permute-start.1 = (s32[2,8]{1,0:T(2,128)}, s32[2,8]{1,0:T(2,128)S(1)}, u32[]{:S(2)}, u32[]{:S(2)}) collective-permute-start(s32[2,8]{1,0:T(2,128)} %bitcast.8), channel_id=1, source_target_pairs={{0,12},{4,0},{8,4},{12,8},{1,13},{5,1},{9,5},{13,9},{2,14},{6,2},{... | collective-permute-start | bytes 200 | tf_op jit(solution)/shard_map/ppermute | solution.py:582
  6.8 1.4 %copy-done = bf16[2048,384]{1,0:T(8,128)(2,1)S(1)} copy-done((bf16[2048,384]{1,0:T(8,128)(2,1)S(1)}, bf16[2048,384]{1,0:T(8,128)(2,1)}, u32[]{:S(2)}) %copy-start) | copy-done | bytes 1572888
  8.7 1.8 %collective-permute-done.2.refs_3_ = s32[2,8]{1,0:T(2,128)S(1)} collective-permute-done((s32[2,8]{1,0:T(2,128)}, s32[2,8]{1,0:T(2,128)S(1)}, u32[]{:S(2)}, u32[]{:S(2)}) %collective-permute-start.2) | collective-permute-done | bytes 96 | tf_op jit(solution)/shard_map/ppermute | solution.py:582
  10.5 1.5 %shard_map.60 = (s32[6,9]{1,0:T(8,128)S(1)}, bf16[256,384]{1,0:T(8,128)(2,1)S(1)}, bf16[256,384]{1,0:T(8,128)(2,1)S(1)}, bf16[256,384]{1,0:T(8,128)(2,1)S(1)}) custom-call(s32[2,8]{1,0:T(2,128)S(1)} %bitcast.10, s32[2,8]{1,0:T(2,128)S(1)} %collective-permute-done.refs_1_, s32[2,8]{1,0:T(2,128)S(1)} %collective-permute-done.1.refs_2_, ...), custom_call_target="tpu_custom_call" | custom-call | tf_op jit(solution)/shard_map/pallas_call | solution.py:70
  12.0 1.0 %collective-permute-start.3 = (bf16[256,384]{1,0:T(8,128)(2,1)S(1)}, bf16[256,384]{1,0:T(8,128)(2,1)S(1)}, u32[]{:S(2)}, u32[]{:S(2)}) collective-permute-start(bf16[256,384]{1,0:T(8,128)(2,1)S(1)} %get-tuple-element.34), channel_id=1, source_target_pairs={{0,8},{4,12},{8,0},{12,4},{1,9},{5,13},{9,1},{13,5},{2,10},{6,14},... | collective-permute-start | bytes 589832 | tf_op jit(solution)/shard_map/ppermute | solution.py:582
  13.0 1.3 %collective-permute-start.4 = (bf16[256,384]{1,0:T(8,128)(2,1)S(1)}, bf16[256,384]{1,0:T(8,128)(2,1)S(1)}, u32[]{:S(2)}, u32[]{:S(2)}) collective-permute-start(bf16[256,384]{1,0:T(8,128)(2,1)S(1)} %get-tuple-element.35), channel_id=1, source_target_pairs={{0,12},{4,0},{8,4},{12,8},{1,13},{5,1},{9,5},{13,9},{2,14},{6,2},{... | collective-permute-start | bytes 589832 | tf_op jit(solution)/shard_map/ppermute | solution.py:582
  15.9 11.0 %collective-permute-done.3.refs_4_ = bf16[256,384]{1,0:T(8,128)(2,1)S(1)} collective-permute-done((bf16[256,384]{1,0:T(8,128)(2,1)S(1)}, bf16[256,384]{1,0:T(8,128)(2,1)S(1)}, u32[]{:S(2)}, u32[]{:S(2)}) %collective-permute-start.3) | collective-permute-done | bytes 196640 | tf_op jit(solution)/shard_map/ppermute | solution.py:582
  26.9 1.0 %shard_map.62.refs_2_ = f32[1024,128]{1,0:T(8,128)S(1)} custom-call(s32[6,9]{1,0:T(8,128)S(1)} %get-tuple-element.31.refs_0_, bf16[2048,384]{1,0:T(8,128)(2,1)S(1)} %copy-done, f32[2048,128]{1,0:T(8,128)S(1)} %get-tuple-element.32.refs_2_, f32[256,128]{1,0:T(8,128)S(1)} %get-tuple-element.33.refs_3_, bf16[256,384]{1,0:T(8,128)(2,1)S(1)} %collective-permute-done.3.refs_4_, ...), custom_call_target="tpu_custom_call" | custom-call | tf_op jit(solution)/shard_map/pallas_call | solution.py:70
  30.8 2.3 %collective-permute-start.10 = (f32[64,128]{1,0:T(8,128)S(1)}, f32[64,128]{1,0:T(8,128)S(1)}, u32[]{:S(2)}, u32[]{:S(2)}) collective-permute-start(f32[64,128]{1,0:T(8,128)S(1)} %get-tuple-element.41), channel_id=1, source_target_pairs={{0,12},{4,0},{8,4},{12,8},{1,13},{5,1},{9,5},{13,9},{2,14},{6,2},{... | collective-permute-start | bytes 98312 | tf_op jit(solution)/shard_map/ppermute | solution.py:582
  33.1 2.1 %collective-permute-start.8 = (f32[64,128]{1,0:T(8,128)S(1)}, f32[64,128]{1,0:T(8,128)S(1)}, u32[]{:S(2)}, u32[]{:S(2)}) collective-permute-start(f32[64,128]{1,0:T(8,128)S(1)} %get-tuple-element.41), channel_id=1, source_target_pairs={{0,4},{4,8},{8,12},{12,0},{1,5},{5,9},{9,13},{13,1},{2,6},{6,10},{... | collective-permute-start | bytes 98312 | tf_op jit(solution)/shard_map/ppermute | solution.py:582
  35.2 2.3 %collective-permute-start.9 = (f32[64,128]{1,0:T(8,128)S(1)}, f32[64,128]{1,0:T(8,128)S(1)}, u32[]{:S(2)}, u32[]{:S(2)}) collective-permute-start(f32[64,128]{1,0:T(8,128)S(1)} %get-tuple-element.41), channel_id=1, source_target_pairs={{0,8},{4,12},{8,0},{12,4},{1,9},{5,13},{9,1},{13,5},{2,10},{6,14},... | collective-permute-start | bytes 98312 | tf_op jit(solution)/shard_map/ppermute | solution.py:582
  37.6 2.5 %collective-permute-start.13 = (s16[272,128]{1,0:T(8,128)(2,1)S(1)}, s16[272,128]{1,0:T(8,128)(2,1)S(1)}, u32[]{:S(2)}, u32[]{:S(2)}) collective-permute-start(s16[272,128]{1,0:T(8,128)(2,1)S(1)} %get-tuple-element.48), channel_id=1, source_target_pairs={{0,8},{4,12},{8,0},{12,4},{1,9},{5,13},{9,1},{13,5},{2,10},{6,14},... | collective-permute-start | bytes 208904 | tf_op jit(solution)/shard_map/ppermute | solution.py:582
  40.1 1.3 %collective-permute-start.14 = (s16[272,128]{1,0:T(8,128)(2,1)S(1)}, s16[272,128]{1,0:T(8,128)(2,1)S(1)}, u32[]{:S(2)}, u32[]{:S(2)}) collective-permute-start(s16[272,128]{1,0:T(8,128)(2,1)S(1)} %get-tuple-element.49), channel_id=1, source_target_pairs={{0,12},{4,0},{8,4},{12,8},{1,13},{5,1},{9,5},{13,9},{2,14},{6,2},{... | collective-permute-start | bytes 208904 | tf_op jit(solution)/shard_map/ppermute | solution.py:582
  41.4 1.6 %collective-permute-start.11 = (f32[64,128]{1,0:T(8,128)S(1)}, f32[64,128]{1,0:T(8,128)S(1)}, u32[]{:S(2)}, u32[]{:S(2)}) collective-permute-start(f32[64,128]{1,0:T(8,128)S(1)} %add_add_fusion.refs_1_), channel_id=1, source_target_pairs={{0,2},{2,0},{1,3},{3,1},{4,6},{6,4},{5,7},{7,5},{8,10},{10,8},{9,1... | collective-permute-start | bytes 98312 | tf_op jit(solution)/shard_map/ppermute | solution.py:590
  43.0 2.4 %collective-permute-done.11.refs_2_.refs_3_ = f32[64,128]{1,0:T(8,128)S(1)} collective-permute-done((f32[64,128]{1,0:T(8,128)S(1)}, f32[64,128]{1,0:T(8,128)S(1)}, u32[]{:S(2)}, u32[]{:S(2)}) %collective-permute-start.11) | collective-permute-done | bytes 32800 | tf_op jit(solution)/shard_map/ppermute | solution.py:590
  47.8 1.0 %shard_map.68.refs_2_ = s16[32,2176]{1,0:T(8,128)(2,1)S(1)} custom-call(s32[6,9]{1,0:T(8,128)S(1)} %get-tuple-element.31.refs_0_, f32[64,128]{1,0:T(8,128)S(1)} %get-tuple-element.45.refs_1_.refs_0_, f32[32,2048]{1,0:T(8,128)S(1)} %get-tuple-element.46.refs_2_, bf16[8,256,128]{2,1,0:T(8,128)(2,1)S(1)} %get-tuple-element.42.refs_4_.refs_3_.refs_6_, ...), custom_call_target="tpu_custom_call" | custom-call | tf_op jit(solution)/shard_map/pallas_call | solution.py:70
  48.8 1.6 %collective-permute-start.18 = (s16[32,2176]{1,0:T(8,128)(2,1)S(1)}, s16[32,2176]{1,0:T(8,128)(2,1)S(1)}, u32[]{:S(2)}, u32[]{:S(2)}) collective-permute-start(s16[32,2176]{1,0:T(8,128)(2,1)S(1)} %shard_map.68.refs_2_), channel_id=1, source_target_pairs={{0,2},{2,0},{1,3},{3,1},{4,6},{6,4},{5,7},{7,5},{8,10},{10,8},{9,1... | collective-permute-start | bytes 417800 | tf_op jit(solution)/shard_map/ppermute | solution.py:590
  50.4 4.2 %collective-permute-done.18.refs_3_ = s16[32,2176]{1,0:T(8,128)(2,1)S(1)} collective-permute-done((s16[32,2176]{1,0:T(8,128)(2,1)S(1)}, s16[32,2176]{1,0:T(8,128)(2,1)S(1)}, u32[]{:S(2)}, u32[]{:S(2)}) %collective-permute-start.18) | collective-permute-done | bytes 139296 | tf_op jit(solution)/shard_map/ppermute | solution.py:590
  55.4 1.4 %collective-permute-start.20 = (s16[144,128]{1,0:T(8,128)(2,1)S(1)}, s16[144,128]{1,0:T(8,128)(2,1)S(1)}, u32[]{:S(2)}, u32[]{:S(2)}) collective-permute-start(s16[144,128]{1,0:T(8,128)(2,1)S(1)} %get-tuple-element.54), channel_id=1, source_target_pairs={{0,4},{4,8},{8,12},{12,0},{1,5},{5,9},{9,13},{13,1},{2,6},{6,10},{... | collective-permute-start | bytes 110600 | tf_op jit(solution)/shard_map/ppermute | solution.py:582
  56.8 1.8 %collective-permute-start.21 = (s16[144,128]{1,0:T(8,128)(2,1)S(1)}, s16[144,128]{1,0:T(8,128)(2,1)S(1)}, u32[]{:S(2)}, u32[]{:S(2)}) collective-permute-start(s16[144,128]{1,0:T(8,128)(2,1)S(1)} %get-tuple-element.55), channel_id=1, source_target_pairs={{0,8},{4,12},{8,0},{12,4},{1,9},{5,13},{9,1},{13,5},{2,10},{6,14},... | collective-permute-start | bytes 110600 | tf_op jit(solution)/shard_map/ppermute | solution.py:582
  58.5 1.3 %collective-permute-start.22 = (s16[144,128]{1,0:T(8,128)(2,1)S(1)}, s16[144,128]{1,0:T(8,128)(2,1)S(1)}, u32[]{:S(2)}, u32[]{:S(2)}) collective-permute-start(s16[144,128]{1,0:T(8,128)(2,1)S(1)} %get-tuple-element.56), channel_id=1, source_target_pairs={{0,12},{4,0},{8,4},{12,8},{1,13},{5,1},{9,5},{13,9},{2,14},{6,2},{... | collective-permute-start | bytes 110600 | tf_op jit(solution)/shard_map/ppermute | solution.py:582
  61.5 1.1 %collective-permute-done.21.refs_14_ = s16[144,128]{1,0:T(8,128)(2,1)S(1)} collective-permute-done((s16[144,128]{1,0:T(8,128)(2,1)S(1)}, s16[144,128]{1,0:T(8,128)(2,1)S(1)}, u32[]{:S(2)}, u32[]{:S(2)}) %collective-permute-start.21) | collective-permute-done | bytes 36896 | tf_op jit(solution)/shard_map/ppermute | solution.py:582
  63.2 1.0 %shard_map.71.total = f32[32,2048]{1,0:T(8,128)S(1)} custom-call(s32[6,9]{1,0:T(8,128)S(1)} %get-tuple-element.31.refs_0_, f32[64,128]{1,0:T(8,128)S(1)} %get-tuple-element.45.refs_1_.refs_0_, f32[32,128]{1,0:T(8,128)S(1)} %shard_map.70.refs_2_, f32[32,2048]{1,0:T(8,128)S(1)} %get-tuple-element.53.refs_0_.refs_3_, ...), custom_call_target="tpu_custom_call" | custom-call | tf_op jit(solution)/shard_map/pallas_call | solution.py:70
  64.3 1.6 %collective-permute-start.24 = (s16[32,2176]{1,0:T(8,128)(2,1)S(1)}, s16[32,2176]{1,0:T(8,128)(2,1)S(1)}, u32[]{:S(2)}, u32[]{:S(2)}) collective-permute-start(s16[32,2176]{1,0:T(8,128)(2,1)S(1)} %shard_map.72.refs_1_), channel_id=1, source_target_pairs={{0,2},{2,0},{1,3},{3,1},{4,6},{6,4},{5,7},{7,5},{8,10},{10,8},{9,1... | collective-permute-start | bytes 417800 | tf_op jit(solution)/shard_map/ppermute | solution.py:590
  65.9 1.3 %collective-permute-start.25 = (f32[32,128]{1,0:T(8,128)S(1)}, f32[32,128]{1,0:T(8,128)S(1)}, u32[]{:S(2)}, u32[]{:S(2)}) collective-permute-start(f32[32,128]{1,0:T(8,128)S(1)} %add.18.after.refs_0_), channel_id=1, source_target_pairs={{0,8},{4,12},{8,0},{12,4},{1,9},{5,13},{9,1},{13,5},{2,10},{6,14},... | collective-permute-start | bytes 49160 | tf_op jit(solution)/shard_map/ppermute | solution.py:590
  67.2 3.4 %collective-permute-done.25.refs_3_.refs_1_ = f32[32,128]{1,0:T(8,128)S(1)} collective-permute-done((f32[32,128]{1,0:T(8,128)S(1)}, f32[32,128]{1,0:T(8,128)S(1)}, u32[]{:S(2)}, u32[]{:S(2)}) %collective-permute-start.25) | collective-permute-done | bytes 16416 | tf_op jit(solution)/shard_map/ppermute | solution.py:590
  70.7 1.7 %shard_map.74.refs_0_ = f32[64,64]{1,0:T(8,128)S(1)} custom-call(f32[32,2048]{1,0:T(8,128)S(1)} %shard_map.73.after.refs_1_, f32[32,128]{1,0:T(8,128)S(1)} %add.18.after.refs_0_, f32[32,128]{1,0:T(8,128)S(1)} %collective-permute-done.25.refs_3_.refs_1_), custom_call_target="tpu_custom_call" | custom-call | tf_op jit(solution)/shard_map/pallas_call | solution.py:70
  74.0 2.2 %collective-permute-start.28 = (f32[32,128]{1,0:T(8,128)S(1)}, f32[32,128]{1,0:T(8,128)S(1)}, u32[]{:S(2)}, u32[]{:S(2)}) collective-permute-start(f32[32,128]{1,0:T(8,128)S(1)} %get-tuple-element.58.refs_1_), channel_id=1, source_target_pairs={{0,8},{4,12},{8,0},{12,4},{1,9},{5,13},{9,1},{13,5},{2,10},{6,14},... | collective-permute-start | bytes 49160 | tf_op jit(solution)/shard_map/ppermute | solution.py:582
  76.2 1.2 %collective-permute-start.29 = (f32[32,128]{1,0:T(8,128)S(1)}, f32[32,128]{1,0:T(8,128)S(1)}, u32[]{:S(2)}, u32[]{:S(2)}) collective-permute-start(f32[32,128]{1,0:T(8,128)S(1)} %get-tuple-element.58.refs_1_), channel_id=1, source_target_pairs={{0,12},{4,0},{8,4},{12,8},{1,13},{5,1},{9,5},{13,9},{2,14},{6,2},{... | collective-permute-start | bytes 49160 | tf_op jit(solution)/shard_map/ppermute | solution.py:582
  78.8 1.2 %collective-permute-done.29.refs_4_ = f32[32,128]{1,0:T(8,128)S(1)} collective-permute-done((f32[32,128]{1,0:T(8,128)S(1)}, f32[32,128]{1,0:T(8,128)S(1)}, u32[]{:S(2)}, u32[]{:S(2)}) %collective-permute-start.29) | collective-permute-done | bytes 16416 | tf_op jit(solution)/shard_map/ppermute | solution.py:582
  80.0 2.5 %shard_map.76 = f32[32,2048]{1,0:T(8,128)} custom-call(bf16[128,2048]{1,0:T(8,128)(2,1)S(1)} %get-tuple-element.57.refs_0_, f32[32,128]{1,0:T(8,128)S(1)} %get-tuple-element.58.refs_1_, f32[32,128]{1,0:T(8,128)S(1)} %collective-permute-done.27.refs_2_, f32[32,128]{1,0:T(8,128)S(1)} %collective-permute-done.28.refs_3_, ...), custom_call_target="tpu_custom_call" | custom-call | tf_op jit(solution)/shard_map/pallas_call | solution.py:70
  (55 shorter events, 13.7 us)
Async XLA Ops:
  0.6 9.9 %copy-start.2 = (s32[1,2,8]{2,1,0:T(2,128)S(1)}, s32[1,2,8]{2,1,0:T(2,128)}, u32[]{:S(2)}) copy-start(s32[1,2,8]{2,1,0:T(2,128)} %param.6) | copy-start | bytes 196
  0.6 8.0 %collective-permute-start = (s32[2,8]{1,0:T(2,128)}, s32[2,8]{1,0:T(2,128)S(1)}, u32[]{:S(2)}, u32[]{:S(2)}) collective-permute-start(s32[2,8]{1,0:T(2,128)} %bitcast.7), channel_id=1, source_target_pairs={{0,4},{4,8},{8,12},{12,0},{1,5},{5,9},{9,13},{13,1},{2,6},{6,10},{... | collective-permute-start | bytes 200 | tf_op jit(solution)/shard_map/ppermute | solution.py:582
  3.7 4.9 %collective-permute-start.1 = (s32[2,8]{1,0:T(2,128)}, s32[2,8]{1,0:T(2,128)S(1)}, u32[]{:S(2)}, u32[]{:S(2)}) collective-permute-start(s32[2,8]{1,0:T(2,128)} %bitcast.8), channel_id=1, source_target_pairs={{0,12},{4,0},{8,4},{12,8},{1,13},{5,1},{9,5},{13,9},{2,14},{6,2},{... | collective-permute-start | bytes 200 | tf_op jit(solution)/shard_map/ppermute | solution.py:582
  5.8 4.7 %collective-permute-start.2 = (s32[2,8]{1,0:T(2,128)}, s32[2,8]{1,0:T(2,128)S(1)}, u32[]{:S(2)}, u32[]{:S(2)}) collective-permute-start(s32[2,8]{1,0:T(2,128)} %bitcast.9), channel_id=1, source_target_pairs={{0,8},{4,12},{8,0},{12,4},{1,9},{5,13},{9,1},{13,5},{2,10},{6,14},... | collective-permute-start | bytes 200 | tf_op jit(solution)/shard_map/ppermute | solution.py:582
  6.8 1.4 %copy-start = (bf16[2048,384]{1,0:T(8,128)(2,1)S(1)}, bf16[2048,384]{1,0:T(8,128)(2,1)}, u32[]{:S(2)}) copy-start(bf16[2048,384]{1,0:T(8,128)(2,1)} %refs_1_.4) | copy-start | bytes 4718596
  12.0 14.9 %collective-permute-start.3 = (bf16[256,384]{1,0:T(8,128)(2,1)S(1)}, bf16[256,384]{1,0:T(8,128)(2,1)S(1)}, u32[]{:S(2)}, u32[]{:S(2)}) collective-permute-start(bf16[256,384]{1,0:T(8,128)(2,1)S(1)} %get-tuple-element.34), channel_id=1, source_target_pairs={{0,8},{4,12},{8,0},{12,4},{1,9},{5,13},{9,1},{13,5},{2,10},{6,14},... | collective-permute-start | bytes 589832 | tf_op jit(solution)/shard_map/ppermute | solution.py:582
  13.0 13.9 %collective-permute-start.4 = (bf16[256,384]{1,0:T(8,128)(2,1)S(1)}, bf16[256,384]{1,0:T(8,128)(2,1)S(1)}, u32[]{:S(2)}, u32[]{:S(2)}) collective-permute-start(bf16[256,384]{1,0:T(8,128)(2,1)S(1)} %get-tuple-element.35), channel_id=1, source_target_pairs={{0,12},{4,0},{8,4},{12,8},{1,13},{5,1},{9,5},{13,9},{2,14},{6,2},{... | collective-permute-start | bytes 589832 | tf_op jit(solution)/shard_map/ppermute | solution.py:582
  14.4 12.5 %collective-permute-start.5 = (bf16[256,384]{1,0:T(8,128)(2,1)S(1)}, bf16[256,384]{1,0:T(8,128)(2,1)S(1)}, u32[]{:S(2)}, u32[]{:S(2)}) collective-permute-start(bf16[256,384]{1,0:T(8,128)(2,1)S(1)} %get-tuple-element.36), channel_id=1, source_target_pairs={{0,4},{4,8},{8,12},{12,0},{1,5},{5,9},{9,13},{13,1},{2,6},{6,10},{... | collective-permute-start | bytes 589832 | tf_op jit(solution)/shard_map/ppermute | solution.py:582
  15.1 13.7 %collective-permute-start.7 = (f32[1024,128]{1,0:T(8,128)S(1)}, f32[1024,128]{1,0:T(8,128)S(1)}, u32[]{:S(2)}, u32[]{:S(2)}) collective-permute-start(f32[1024,128]{1,0:T(8,128)S(1)} %shard_map.59.refs_5_.mine), channel_id=1, source_target_pairs={{0,1},{1,0},{2,3},{3,2},{4,5},{5,4},{6,7},{7,6},{8,9},{9,8},{10,11... | collective-permute-start | bytes 1572872 | tf_op jit(solution)/shard_map/ppermute | solution.py:582
  27.9 2.0 %collective-permute-start.6 = (f32[1024,128]{1,0:T(8,128)S(1)}, f32[1024,128]{1,0:T(8,128)S(1)}, u32[]{:S(2)}, u32[]{:S(2)}) collective-permute-start(f32[1024,128]{1,0:T(8,128)S(1)} %shard_map.62.refs_2_), channel_id=1, source_target_pairs={{0,1},{1,0},{2,3},{3,2},{4,5},{5,4},{6,7},{7,6},{8,9},{9,8},{10,11... | collective-permute-start | bytes 1572872 | tf_op jit(solution)/shard_map/ppermute | solution.py:582
  30.8 9.3 %collective-permute-start.10 = (f32[64,128]{1,0:T(8,128)S(1)}, f32[64,128]{1,0:T(8,128)S(1)}, u32[]{:S(2)}, u32[]{:S(2)}) collective-permute-start(f32[64,128]{1,0:T(8,128)S(1)} %get-tuple-element.41), channel_id=1, source_target_pairs={{0,12},{4,0},{8,4},{12,8},{1,13},{5,1},{9,5},{13,9},{2,14},{6,2},{... | collective-permute-start | bytes 98312 | tf_op jit(solution)/shard_map/ppermute | solution.py:582
  33.1 8.3 %collective-permute-start.8 = (f32[64,128]{1,0:T(8,128)S(1)}, f32[64,128]{1,0:T(8,128)S(1)}, u32[]{:S(2)}, u32[]{:S(2)}) collective-permute-start(f32[64,128]{1,0:T(8,128)S(1)} %get-tuple-element.41), channel_id=1, source_target_pairs={{0,4},{4,8},{8,12},{12,0},{1,5},{5,9},{9,13},{13,1},{2,6},{6,10},{... | collective-permute-start | bytes 98312 | tf_op jit(solution)/shard_map/ppermute | solution.py:582
  35.2 6.2 %collective-permute-start.9 = (f32[64,128]{1,0:T(8,128)S(1)}, f32[64,128]{1,0:T(8,128)S(1)}, u32[]{:S(2)}, u32[]{:S(2)}) collective-permute-start(f32[64,128]{1,0:T(8,128)S(1)} %get-tuple-element.41), channel_id=1, source_target_pairs={{0,8},{4,12},{8,0},{12,4},{1,9},{5,13},{9,1},{13,5},{2,10},{6,14},... | collective-permute-start | bytes 98312 | tf_op jit(solution)/shard_map/ppermute | solution.py:582
  37.6 7.8 %collective-permute-start.12 = (s16[272,128]{1,0:T(8,128)(2,1)S(1)}, s16[272,128]{1,0:T(8,128)(2,1)S(1)}, u32[]{:S(2)}, u32[]{:S(2)}) collective-permute-start(s16[272,128]{1,0:T(8,128)(2,1)S(1)} %get-tuple-element.47), channel_id=1, source_target_pairs={{0,4},{4,8},{8,12},{12,0},{1,5},{5,9},{9,13},{13,1},{2,6},{6,10},{... | collective-permute-start | bytes 208904 | tf_op jit(solution)/shard_map/ppermute | solution.py:582
  37.6 8.3 %collective-permute-start.13 = (s16[272,128]{1,0:T(8,128)(2,1)S(1)}, s16[272,128]{1,0:T(8,128)(2,1)S(1)}, u32[]{:S(2)}, u32[]{:S(2)}) collective-permute-start(s16[272,128]{1,0:T(8,128)(2,1)S(1)} %get-tuple-element.48), channel_id=1, source_target_pairs={{0,8},{4,12},{8,0},{12,4},{1,9},{5,13},{9,1},{13,5},{2,10},{6,14},... | collective-permute-start | bytes 208904 | tf_op jit(solution)/shard_map/ppermute | solution.py:582
  40.1 5.8 %collective-permute-start.14 = (s16[272,128]{1,0:T(8,128)(2,1)S(1)}, s16[272,128]{1,0:T(8,128)(2,1)S(1)}, u32[]{:S(2)}, u32[]{:S(2)}) collective-permute-start(s16[272,128]{1,0:T(8,128)(2,1)S(1)} %get-tuple-element.49), channel_id=1, source_target_pairs={{0,12},{4,0},{8,4},{12,8},{1,13},{5,1},{9,5},{13,9},{2,14},{6,2},{... | collective-permute-start | bytes 208904 | tf_op jit(solution)/shard_map/ppermute | solution.py:582
  41.4 4.0 %collective-permute-start.11 = (f32[64,128]{1,0:T(8,128)S(1)}, f32[64,128]{1,0:T(8,128)S(1)}, u32[]{:S(2)}, u32[]{:S(2)}) collective-permute-start(f32[64,128]{1,0:T(8,128)S(1)} %add_add_fusion.refs_1_), channel_id=1, source_target_pairs={{0,2},{2,0},{1,3},{3,1},{4,6},{6,4},{5,7},{7,5},{8,10},{10,8},{9,1... | collective-permute-start | bytes 98312 | tf_op jit(solution)/shard_map/ppermute | solution.py:590
  46.0 1.5 %collective-permute-start.15 = (bf16[1,256,128]{2,1,0:T(8,128)(2,1)S(1)}, bf16[1,256,128]{2,1,0:T(8,128)(2,1)S(1)}, u32[]{:S(2)}, u32[]{:S(2)}) collective-permute-start(bf16[1,256,128]{2,1,0:T(8,128)(2,1)S(1)} %get-tuple-element.50.refs_4_.refs_7_), channel_id=1, source_target_pairs={{0,1},{1,0},{2,3},{3,2},{4,5},{5,4},{6,7},{7,6},{8,9},{9,8},{10,11... | collective-permute-start | bytes 196616 | tf_op jit(solution)/shard_map/ppermute | solution.py:582
  46.0 1.4 %collective-permute-start.16 = (bf16[1,256,128]{2,1,0:T(8,128)(2,1)S(1)}, bf16[1,256,128]{2,1,0:T(8,128)(2,1)S(1)}, u32[]{:S(2)}, u32[]{:S(2)}) collective-permute-start(bf16[1,256,128]{2,1,0:T(8,128)(2,1)S(1)} %get-tuple-element.51.refs_5_.refs_8_), channel_id=1, source_target_pairs={{0,1},{1,0},{2,3},{3,2},{4,5},{5,4},{6,7},{7,6},{8,9},{9,8},{10,11... | collective-permute-start | bytes 196616 | tf_op jit(solution)/shard_map/ppermute | solution.py:582
  46.5 1.3 %collective-permute-start.17 = (bf16[1,256,128]{2,1,0:T(8,128)(2,1)S(1)}, bf16[1,256,128]{2,1,0:T(8,128)(2,1)S(1)}, u32[]{:S(2)}, u32[]{:S(2)}) collective-permute-start(bf16[1,256,128]{2,1,0:T(8,128)(2,1)S(1)} %get-tuple-element.52.refs_6_.refs_9_), channel_id=1, source_target_pairs={{0,1},{1,0},{2,3},{3,2},{4,5},{5,4},{6,7},{7,6},{8,9},{9,8},{10,11... | collective-permute-start | bytes 196616 | tf_op jit(solution)/shard_map/ppermute | solution.py:582
  48.8 5.8 %collective-permute-start.18 = (s16[32,2176]{1,0:T(8,128)(2,1)S(1)}, s16[32,2176]{1,0:T(8,128)(2,1)S(1)}, u32[]{:S(2)}, u32[]{:S(2)}) collective-permute-start(s16[32,2176]{1,0:T(8,128)(2,1)S(1)} %shard_map.68.refs_2_), channel_id=1, source_target_pairs={{0,2},{2,0},{1,3},{3,1},{4,6},{6,4},{5,7},{7,5},{8,10},{10,8},{9,1... | collective-permute-start | bytes 417800 | tf_op jit(solution)/shard_map/ppermute | solution.py:590
  55.3 4.6 %collective-permute-start.19 = (f32[32,2048]{1,0:T(8,128)S(1)}, f32[32,2048]{1,0:T(8,128)S(1)}, u32[]{:S(2)}, u32[]{:S(2)}) collective-permute-start(f32[32,2048]{1,0:T(8,128)S(1)} %get-tuple-element.53.refs_0_.refs_3_), channel_id=1, source_target_pairs={{0,1},{1,0},{2,3},{3,2},{4,5},{5,4},{6,7},{7,6},{8,9},{9,8},{10,11... | collective-permute-start | bytes 786440 | tf_op jit(solution)/shard_map/ppermute | solution.py:582
  55.4 6.2 %collective-permute-start.20 = (s16[144,128]{1,0:T(8,128)(2,1)S(1)}, s16[144,128]{1,0:T(8,128)(2,1)S(1)}, u32[]{:S(2)}, u32[]{:S(2)}) collective-permute-start(s16[144,128]{1,0:T(8,128)(2,1)S(1)} %get-tuple-element.54), channel_id=1, source_target_pairs={{0,4},{4,8},{8,12},{12,0},{1,5},{5,9},{9,13},{13,1},{2,6},{6,10},{... | collective-permute-start | bytes 110600 | tf_op jit(solution)/shard_map/ppermute | solution.py:582
  56.8 5.9 %collective-permute-start.21 = (s16[144,128]{1,0:T(8,128)(2,1)S(1)}, s16[144,128]{1,0:T(8,128)(2,1)S(1)}, u32[]{:S(2)}, u32[]{:S(2)}) collective-permute-start(s16[144,128]{1,0:T(8,128)(2,1)S(1)} %get-tuple-element.55), channel_id=1, source_target_pairs={{0,8},{4,12},{8,0},{12,4},{1,9},{5,13},{9,1},{13,5},{2,10},{6,14},... | collective-permute-start | bytes 110600 | tf_op jit(solution)/shard_map/ppermute | solution.py:582
  58.5 4.7 %collective-permute-start.22 = (s16[144,128]{1,0:T(8,128)(2,1)S(1)}, s16[144,128]{1,0:T(8,128)(2,1)S(1)}, u32[]{:S(2)}, u32[]{:S(2)}) collective-permute-start(s16[144,128]{1,0:T(8,128)(2,1)S(1)} %get-tuple-element.56), channel_id=1, source_target_pairs={{0,12},{4,0},{8,4},{12,8},{1,13},{5,1},{9,5},{13,9},{2,14},{6,2},{... | collective-permute-start | bytes 110600 | tf_op jit(solution)/shard_map/ppermute | solution.py:582
  60.3 3.9 %collective-permute-start.23 = (f32[32,128]{1,0:T(8,128)S(1)}, f32[32,128]{1,0:T(8,128)S(1)}, u32[]{:S(2)}, u32[]{:S(2)}) collective-permute-start(f32[32,128]{1,0:T(8,128)S(1)} %shard_map.70.refs_2_), channel_id=1, source_target_pairs={{0,4},{4,0},{8,12},{12,8},{1,5},{5,1},{9,13},{13,9},{2,6},{6,2},{1... | collective-permute-start | bytes 49160 | tf_op jit(solution)/shard_map/ppermute | solution.py:590
  64.3 6.2 %collective-permute-start.24 = (s16[32,2176]{1,0:T(8,128)(2,1)S(1)}, s16[32,2176]{1,0:T(8,128)(2,1)S(1)}, u32[]{:S(2)}, u32[]{:S(2)}) collective-permute-start(s16[32,2176]{1,0:T(8,128)(2,1)S(1)} %shard_map.72.refs_1_), channel_id=1, source_target_pairs={{0,2},{2,0},{1,3},{3,1},{4,6},{6,4},{5,7},{7,5},{8,10},{10,8},{9,1... | collective-permute-start | bytes 417800 | tf_op jit(solution)/shard_map/ppermute | solution.py:590
  65.9 4.6 %collective-permute-start.25 = (f32[32,128]{1,0:T(8,128)S(1)}, f32[32,128]{1,0:T(8,128)S(1)}, u32[]{:S(2)}, u32[]{:S(2)}) collective-permute-start(f32[32,128]{1,0:T(8,128)S(1)} %add.18.after.refs_0_), channel_id=1, source_target_pairs={{0,8},{4,12},{8,0},{12,4},{1,9},{5,13},{9,1},{13,5},{2,10},{6,14},... | collective-permute-start | bytes 49160 | tf_op jit(solution)/shard_map/ppermute | solution.py:590
  70.6 1.7 %collective-permute-start.26 = (f32[32,2048]{1,0:T(8,128)S(1)}, f32[32,2048]{1,0:T(8,128)S(1)}, u32[]{:S(2)}, u32[]{:S(2)}) collective-permute-start(f32[32,2048]{1,0:T(8,128)S(1)} %shard_map.73.after.refs_1_), channel_id=1, source_target_pairs={{0,1},{1,0},{2,3},{3,2},{4,5},{5,4},{6,7},{7,6},{8,9},{9,8},{10,11... | collective-permute-start | bytes 786440 | tf_op jit(solution)/shard_map/ppermute | solution.py:582
  73.2 5.6 %collective-permute-start.27 = (f32[32,128]{1,0:T(8,128)S(1)}, f32[32,128]{1,0:T(8,128)S(1)}, u32[]{:S(2)}, u32[]{:S(2)}) collective-permute-start(f32[32,128]{1,0:T(8,128)S(1)} %get-tuple-element.58.refs_1_), channel_id=1, source_target_pairs={{0,4},{4,8},{8,12},{12,0},{1,5},{5,9},{9,13},{13,1},{2,6},{6,10},{... | collective-permute-start | bytes 49160 | tf_op jit(solution)/shard_map/ppermute | solution.py:582
  74.0 4.8 %collective-permute-start.28 = (f32[32,128]{1,0:T(8,128)S(1)}, f32[32,128]{1,0:T(8,128)S(1)}, u32[]{:S(2)}, u32[]{:S(2)}) collective-permute-start(f32[32,128]{1,0:T(8,128)S(1)} %get-tuple-element.58.refs_1_), channel_id=1, source_target_pairs={{0,8},{4,12},{8,0},{12,4},{1,9},{5,13},{9,1},{13,5},{2,10},{6,14},... | collective-permute-start | bytes 49160 | tf_op jit(solution)/shard_map/ppermute | solution.py:582
  76.2 3.7 %collective-permute-start.29 = (f32[32,128]{1,0:T(8,128)S(1)}, f32[32,128]{1,0:T(8,128)S(1)}, u32[]{:S(2)}, u32[]{:S(2)}) collective-permute-start(f32[32,128]{1,0:T(8,128)S(1)} %get-tuple-element.58.refs_1_), channel_id=1, source_target_pairs={{0,12},{4,0},{8,4},{12,8},{1,13},{5,1},{9,5},{13,9},{2,14},{6,2},{... | collective-permute-start | bytes 49160 | tf_op jit(solution)/shard_map/ppermute | solution.py:582
  (1 other events, 1.1 us)

commit v25 on v24

--- a/solution.py
+++ b/solution.py
@@ -673,7 +673,9 @@
         late=(1, 2),
     )
     near_tiles, home_tiles, degrees, sends = tiles[0], tiles[1], tiles[2], tiles[3:]
-    degrees = functools.reduce(jnp.add, row_terms(degrees, row_count))
+    degrees = functools.reduce(
+        jnp.add, [degrees] + [shift_by(degrees, "rows", row_count, k) for k in reversed(others)]
+    )
     degree_terms = pair_sum(degrees, ("tiles",))
     messages = [shift_by(sends[k - 1], "rows", row_count, k) for k in others]
     sent = call(

time: 82.7 us -> 82.7 us (level)
  no operation moved by 1% of the time
where the time goes in v25:
time: 82.7 us; the launch traced here: 82.5 us
  starting transfers between devices  36 us (44%)
  waiting for transfers between devices  28.7 us (35%)
  Pallas kernels  14.2 us (17%)
  local copies, waits for them, and re-layouts  2.01 us (2%)
  between operations  1.52 us (2%)
    ppermute x25, starting transfers between devices, shift_by(): lax.ppermute(value, axes, [(i, (i + shift) % size) for i in range(size)])  29.3 us
    ppermute x25, waiting for transfers between devices, shift_by(): lax.ppermute(value, axes, [(i, (i + shift) % size) for i in range(size)])  18.7 us
    pallas_call x18, Pallas kernels, call(): pl.pallas_call(body, out_shape=shapes, in_specs=[ANY if i in any_in else...  14.2 us
    ppermute x5, waiting for transfers between devices, pair_step(): lax.ppermute(value, name, [(i, i ^ flip) for i in range(lax.axis_size(nam...  9.99 us
    ppermute x5, starting transfers between devices, pair_step(): lax.ppermute(value, name, [(i, i ^ flip) for i in range(lax.axis_size(nam...  6.67 us
  transfers between devices with their start and end apart: 30, of which 13 were waited for; matrix products, arithmetic and copies ran while one was open for 1% of the time, Pallas kernels for 8%

profile of v25, /device:TPU:0, one launch (start us, length us, event | category | flops | bytes accessed | tf_op | source)
XLA Modules:
  0.0 82.5 jit_solution(13065638244925444752)
XLA Ops:
  0.6 3.1 %collective-permute-start = (s32[2,8]{1,0:T(2,128)}, s32[2,8]{1,0:T(2,128)S(1)}, u32[]{:S(2)}, u32[]{:S(2)}) collective-permute-start(s32[2,8]{1,0:T(2,128)} %bitcast.7), channel_id=1, source_target_pairs={{0,4},{4,8},{8,12},{12,0},{1,5},{5,9},{9,13},{13,1},{2,6},{6,10},{... | collective-permute-start | bytes 200 | tf_op jit(solution)/shard_map/ppermute | solution.py:582
  3.7 2.1 %collective-permute-start.1 = (s32[2,8]{1,0:T(2,128)}, s32[2,8]{1,0:T(2,128)S(1)}, u32[]{:S(2)}, u32[]{:S(2)}) collective-permute-start(s32[2,8]{1,0:T(2,128)} %bitcast.8), channel_id=1, source_target_pairs={{0,12},{4,0},{8,4},{12,8},{1,13},{5,1},{9,5},{13,9},{2,14},{6,2},{... | collective-permute-start | bytes 200 | tf_op jit(solution)/shard_map/ppermute | solution.py:582
  5.8 0.9 %collective-permute-start.2 = (s32[2,8]{1,0:T(2,128)}, s32[2,8]{1,0:T(2,128)S(1)}, u32[]{:S(2)}, u32[]{:S(2)}) collective-permute-start(s32[2,8]{1,0:T(2,128)} %bitcast.9), channel_id=1, source_target_pairs={{0,8},{4,12},{8,0},{12,4},{1,9},{5,13},{9,1},{13,5},{2,10},{6,14},... | collective-permute-start | bytes 200 | tf_op jit(solution)/shard_map/ppermute | solution.py:582
  6.8 1.4 %copy-done = bf16[2048,384]{1,0:T(8,128)(2,1)S(1)} copy-done((bf16[2048,384]{1,0:T(8,128)(2,1)S(1)}, bf16[2048,384]{1,0:T(8,128)(2,1)}, u32[]{:S(2)}) %copy-start) | copy-done | bytes 1572888
  8.7 1.8 %collective-permute-done.2.refs_3_ = s32[2,8]{1,0:T(2,128)S(1)} collective-permute-done((s32[2,8]{1,0:T(2,128)}, s32[2,8]{1,0:T(2,128)S(1)}, u32[]{:S(2)}, u32[]{:S(2)}) %collective-permute-start.2) | collective-permute-done | bytes 96 | tf_op jit(solution)/shard_map/ppermute | solution.py:582
  10.5 1.5 %shard_map.60 = (s32[6,9]{1,0:T(8,128)S(1)}, bf16[256,384]{1,0:T(8,128)(2,1)S(1)}, bf16[256,384]{1,0:T(8,128)(2,1)S(1)}, bf16[256,384]{1,0:T(8,128)(2,1)S(1)}) custom-call(s32[2,8]{1,0:T(2,128)S(1)} %bitcast.10, s32[2,8]{1,0:T(2,128)S(1)} %collective-permute-done.refs_1_, s32[2,8]{1,0:T(2,128)S(1)} %collective-permute-done.1.refs_2_, ...), custom_call_target="tpu_custom_call" | custom-call | tf_op jit(solution)/shard_map/pallas_call | solution.py:70
  12.0 1.0 %collective-permute-start.3 = (bf16[256,384]{1,0:T(8,128)(2,1)S(1)}, bf16[256,384]{1,0:T(8,128)(2,1)S(1)}, u32[]{:S(2)}, u32[]{:S(2)}) collective-permute-start(bf16[256,384]{1,0:T(8,128)(2,1)S(1)} %get-tuple-element.34), channel_id=1, source_target_pairs={{0,8},{4,12},{8,0},{12,4},{1,9},{5,13},{9,1},{13,5},{2,10},{6,14},... | collective-permute-start | bytes 589832 | tf_op jit(solution)/shard_map/ppermute | solution.py:582
  13.0 1.3 %collective-permute-start.4 = (bf16[256,384]{1,0:T(8,128)(2,1)S(1)}, bf16[256,384]{1,0:T(8,128)(2,1)S(1)}, u32[]{:S(2)}, u32[]{:S(2)}) collective-permute-start(bf16[256,384]{1,0:T(8,128)(2,1)S(1)} %get-tuple-element.35), channel_id=1, source_target_pairs={{0,12},{4,0},{8,4},{12,8},{1,13},{5,1},{9,5},{13,9},{2,14},{6,2},{... | collective-permute-start | bytes 589832 | tf_op jit(solution)/shard_map/ppermute | solution.py:582
  15.9 11.0 %collective-permute-done.3.refs_4_ = bf16[256,384]{1,0:T(8,128)(2,1)S(1)} collective-permute-done((bf16[256,384]{1,0:T(8,128)(2,1)S(1)}, bf16[256,384]{1,0:T(8,128)(2,1)S(1)}, u32[]{:S(2)}, u32[]{:S(2)}) %collective-permute-start.3) | collective-permute-done | bytes 196640 | tf_op jit(solution)/shard_map/ppermute | solution.py:582
  26.9 1.0 %shard_map.62.refs_2_ = f32[1024,128]{1,0:T(8,128)S(1)} custom-call(s32[6,9]{1,0:T(8,128)S(1)} %get-tuple-element.31.refs_0_, bf16[2048,384]{1,0:T(8,128)(2,1)S(1)} %copy-done, f32[2048,128]{1,0:T(8,128)S(1)} %get-tuple-element.32.refs_2_, f32[256,128]{1,0:T(8,128)S(1)} %get-tuple-element.33.refs_3_, bf16[256,384]{1,0:T(8,128)(2,1)S(1)} %collective-permute-done.3.refs_4_, ...), custom_call_target="tpu_custom_call" | custom-call | tf_op jit(solution)/shard_map/pallas_call | solution.py:70
  30.8 4.4 %collective-permute-start.10 = (f32[64,128]{1,0:T(8,128)S(1)}, f32[64,128]{1,0:T(8,128)S(1)}, u32[]{:S(2)}, u32[]{:S(2)}) collective-permute-start(f32[64,128]{1,0:T(8,128)S(1)} %get-tuple-element.41), channel_id=1, source_target_pairs={{0,4},{4,8},{8,12},{12,0},{1,5},{5,9},{9,13},{13,1},{2,6},{6,10},{... | collective-permute-start | bytes 98312 | tf_op jit(solution)/shard_map/ppermute | solution.py:582
  35.2 2.4 %collective-permute-start.9 = (f32[64,128]{1,0:T(8,128)S(1)}, f32[64,128]{1,0:T(8,128)S(1)}, u32[]{:S(2)}, u32[]{:S(2)}) collective-permute-start(f32[64,128]{1,0:T(8,128)S(1)} %get-tuple-element.41), channel_id=1, source_target_pairs={{0,8},{4,12},{8,0},{12,4},{1,9},{5,13},{9,1},{13,5},{2,10},{6,14},... | collective-permute-start | bytes 98312 | tf_op jit(solution)/shard_map/ppermute | solution.py:582
  37.6 2.5 %collective-permute-start.13 = (s16[272,128]{1,0:T(8,128)(2,1)S(1)}, s16[272,128]{1,0:T(8,128)(2,1)S(1)}, u32[]{:S(2)}, u32[]{:S(2)}) collective-permute-start(s16[272,128]{1,0:T(8,128)(2,1)S(1)} %get-tuple-element.48), channel_id=1, source_target_pairs={{0,8},{4,12},{8,0},{12,4},{1,9},{5,13},{9,1},{13,5},{2,10},{6,14},... | collective-permute-start | bytes 208904 | tf_op jit(solution)/shard_map/ppermute | solution.py:582
  40.1 1.3 %collective-permute-start.14 = (s16[272,128]{1,0:T(8,128)(2,1)S(1)}, s16[272,128]{1,0:T(8,128)(2,1)S(1)}, u32[]{:S(2)}, u32[]{:S(2)}) collective-permute-start(s16[272,128]{1,0:T(8,128)(2,1)S(1)} %get-tuple-element.49), channel_id=1, source_target_pairs={{0,12},{4,0},{8,4},{12,8},{1,13},{5,1},{9,5},{13,9},{2,14},{6,2},{... | collective-permute-start | bytes 208904 | tf_op jit(solution)/shard_map/ppermute | solution.py:582
  41.4 1.6 %collective-permute-start.11 = (f32[64,128]{1,0:T(8,128)S(1)}, f32[64,128]{1,0:T(8,128)S(1)}, u32[]{:S(2)}, u32[]{:S(2)}) collective-permute-start(f32[64,128]{1,0:T(8,128)S(1)} %add_add_fusion.refs_1_), channel_id=1, source_target_pairs={{0,2},{2,0},{1,3},{3,1},{4,6},{6,4},{5,7},{7,5},{8,10},{10,8},{9,1... | collective-permute-start | bytes 98312 | tf_op jit(solution)/shard_map/ppermute | solution.py:590
  43.0 2.4 %collective-permute-done.11.refs_2_.refs_3_ = f32[64,128]{1,0:T(8,128)S(1)} collective-permute-done((f32[64,128]{1,0:T(8,128)S(1)}, f32[64,128]{1,0:T(8,128)S(1)}, u32[]{:S(2)}, u32[]{:S(2)}) %collective-permute-start.11) | collective-permute-done | bytes 32800 | tf_op jit(solution)/shard_map/ppermute | solution.py:590
  47.9 1.0 %shard_map.68.refs_2_ = s16[32,2176]{1,0:T(8,128)(2,1)S(1)} custom-call(s32[6,9]{1,0:T(8,128)S(1)} %get-tuple-element.31.refs_0_, f32[64,128]{1,0:T(8,128)S(1)} %get-tuple-element.45.refs_1_.refs_0_, f32[32,2048]{1,0:T(8,128)S(1)} %get-tuple-element.46.refs_2_, bf16[8,256,128]{2,1,0:T(8,128)(2,1)S(1)} %get-tuple-element.42.refs_4_.refs_3_.refs_6_, ...), custom_call_target="tpu_custom_call" | custom-call | tf_op jit(solution)/shard_map/pallas_call | solution.py:70
  48.9 1.6 %collective-permute-start.18 = (s16[32,2176]{1,0:T(8,128)(2,1)S(1)}, s16[32,2176]{1,0:T(8,128)(2,1)S(1)}, u32[]{:S(2)}, u32[]{:S(2)}) collective-permute-start(s16[32,2176]{1,0:T(8,128)(2,1)S(1)} %shard_map.68.refs_2_), channel_id=1, source_target_pairs={{0,2},{2,0},{1,3},{3,1},{4,6},{6,4},{5,7},{7,5},{8,10},{10,8},{9,1... | collective-permute-start | bytes 417800 | tf_op jit(solution)/shard_map/ppermute | solution.py:590
  50.4 4.3 %collective-permute-done.18.refs_3_ = s16[32,2176]{1,0:T(8,128)(2,1)S(1)} collective-permute-done((s16[32,2176]{1,0:T(8,128)(2,1)S(1)}, s16[32,2176]{1,0:T(8,128)(2,1)S(1)}, u32[]{:S(2)}, u32[]{:S(2)}) %collective-permute-start.18) | collective-permute-done | bytes 139296 | tf_op jit(solution)/shard_map/ppermute | solution.py:590
  55.4 1.4 %collective-permute-start.20 = (s16[144,128]{1,0:T(8,128)(2,1)S(1)}, s16[144,128]{1,0:T(8,128)(2,1)S(1)}, u32[]{:S(2)}, u32[]{:S(2)}) collective-permute-start(s16[144,128]{1,0:T(8,128)(2,1)S(1)} %get-tuple-element.54), channel_id=1, source_target_pairs={{0,4},{4,8},{8,12},{12,0},{1,5},{5,9},{9,13},{13,1},{2,6},{6,10},{... | collective-permute-start | bytes 110600 | tf_op jit(solution)/shard_map/ppermute | solution.py:582
  56.8 1.7 %collective-permute-start.21 = (s16[144,128]{1,0:T(8,128)(2,1)S(1)}, s16[144,128]{1,0:T(8,128)(2,1)S(1)}, u32[]{:S(2)}, u32[]{:S(2)}) collective-permute-start(s16[144,128]{1,0:T(8,128)(2,1)S(1)} %get-tuple-element.55), channel_id=1, source_target_pairs={{0,8},{4,12},{8,0},{12,4},{1,9},{5,13},{9,1},{13,5},{2,10},{6,14},... | collective-permute-start | bytes 110600 | tf_op jit(solution)/shard_map/ppermute | solution.py:582
  58.5 1.4 %collective-permute-start.22 = (s16[144,128]{1,0:T(8,128)(2,1)S(1)}, s16[144,128]{1,0:T(8,128)(2,1)S(1)}, u32[]{:S(2)}, u32[]{:S(2)}) collective-permute-start(s16[144,128]{1,0:T(8,128)(2,1)S(1)} %get-tuple-element.56), channel_id=1, source_target_pairs={{0,12},{4,0},{8,4},{12,8},{1,13},{5,1},{9,5},{13,9},{2,14},{6,2},{... | collective-permute-start | bytes 110600 | tf_op jit(solution)/shard_map/ppermute | solution.py:582
  61.6 1.2 %collective-permute-done.21.refs_14_ = s16[144,128]{1,0:T(8,128)(2,1)S(1)} collective-permute-done((s16[144,128]{1,0:T(8,128)(2,1)S(1)}, s16[144,128]{1,0:T(8,128)(2,1)S(1)}, u32[]{:S(2)}, u32[]{:S(2)}) %collective-permute-start.21) | collective-permute-done | bytes 36896 | tf_op jit(solution)/shard_map/ppermute | solution.py:582
  63.2 1.0 %shard_map.71.total = f32[32,2048]{1,0:T(8,128)S(1)} custom-call(s32[6,9]{1,0:T(8,128)S(1)} %get-tuple-element.31.refs_0_, f32[64,128]{1,0:T(8,128)S(1)} %get-tuple-element.45.refs_1_.refs_0_, f32[32,128]{1,0:T(8,128)S(1)} %shard_map.70.refs_2_, f32[32,2048]{1,0:T(8,128)S(1)} %get-tuple-element.53.refs_0_.refs_3_, ...), custom_call_target="tpu_custom_call" | custom-call | tf_op jit(solution)/shard_map/pallas_call | solution.py:70
  64.3 1.6 %collective-permute-start.24 = (s16[32,2176]{1,0:T(8,128)(2,1)S(1)}, s16[32,2176]{1,0:T(8,128)(2,1)S(1)}, u32[]{:S(2)}, u32[]{:S(2)}) collective-permute-start(s16[32,2176]{1,0:T(8,128)(2,1)S(1)} %shard_map.72.refs_1_), channel_id=1, source_target_pairs={{0,2},{2,0},{1,3},{3,1},{4,6},{6,4},{5,7},{7,5},{8,10},{10,8},{9,1... | collective-permute-start | bytes 417800 | tf_op jit(solution)/shard_map/ppermute | solution.py:590
  65.9 1.3 %collective-permute-start.25 = (f32[32,128]{1,0:T(8,128)S(1)}, f32[32,128]{1,0:T(8,128)S(1)}, u32[]{:S(2)}, u32[]{:S(2)}) collective-permute-start(f32[32,128]{1,0:T(8,128)S(1)} %add.18.after.refs_0_), channel_id=1, source_target_pairs={{0,8},{4,12},{8,0},{12,4},{1,9},{5,13},{9,1},{13,5},{2,10},{6,14},... | collective-permute-start | bytes 49160 | tf_op jit(solution)/shard_map/ppermute | solution.py:590
  67.2 3.3 %collective-permute-done.25.refs_3_.refs_1_ = f32[32,128]{1,0:T(8,128)S(1)} collective-permute-done((f32[32,128]{1,0:T(8,128)S(1)}, f32[32,128]{1,0:T(8,128)S(1)}, u32[]{:S(2)}, u32[]{:S(2)}) %collective-permute-start.25) | collective-permute-done | bytes 16416 | tf_op jit(solution)/shard_map/ppermute | solution.py:590
  70.7 1.7 %shard_map.74.refs_0_ = f32[64,64]{1,0:T(8,128)S(1)} custom-call(f32[32,2048]{1,0:T(8,128)S(1)} %shard_map.73.after.refs_1_, f32[32,128]{1,0:T(8,128)S(1)} %add.18.after.refs_0_, f32[32,128]{1,0:T(8,128)S(1)} %collective-permute-done.25.refs_3_.refs_1_), custom_call_target="tpu_custom_call" | custom-call | tf_op jit(solution)/shard_map/pallas_call | solution.py:70
  74.0 2.2 %collective-permute-start.28 = (f32[32,128]{1,0:T(8,128)S(1)}, f32[32,128]{1,0:T(8,128)S(1)}, u32[]{:S(2)}, u32[]{:S(2)}) collective-permute-start(f32[32,128]{1,0:T(8,128)S(1)} %get-tuple-element.58.refs_1_), channel_id=1, source_target_pairs={{0,8},{4,12},{8,0},{12,4},{1,9},{5,13},{9,1},{13,5},{2,10},{6,14},... | collective-permute-start | bytes 49160 | tf_op jit(solution)/shard_map/ppermute | solution.py:582
  76.2 1.2 %collective-permute-start.29 = (f32[32,128]{1,0:T(8,128)S(1)}, f32[32,128]{1,0:T(8,128)S(1)}, u32[]{:S(2)}, u32[]{:S(2)}) collective-permute-start(f32[32,128]{1,0:T(8,128)S(1)} %get-tuple-element.58.refs_1_), channel_id=1, source_target_pairs={{0,12},{4,0},{8,4},{12,8},{1,13},{5,1},{9,5},{13,9},{2,14},{6,2},{... | collective-permute-start | bytes 49160 | tf_op jit(solution)/shard_map/ppermute | solution.py:582
  78.9 1.1 %collective-permute-done.29.refs_4_ = f32[32,128]{1,0:T(8,128)S(1)} collective-permute-done((f32[32,128]{1,0:T(8,128)S(1)}, f32[32,128]{1,0:T(8,128)S(1)}, u32[]{:S(2)}, u32[]{:S(2)}) %collective-permute-start.29) | collective-permute-done | bytes 16416 | tf_op jit(solution)/shard_map/ppermute | solution.py:582
  80.0 2.5 %shard_map.76 = f32[32,2048]{1,0:T(8,128)} custom-call(bf16[128,2048]{1,0:T(8,128)(2,1)S(1)} %get-tuple-element.57.refs_0_, f32[32,128]{1,0:T(8,128)S(1)} %get-tuple-element.58.refs_1_, f32[32,128]{1,0:T(8,128)S(1)} %collective-permute-done.27.refs_2_, f32[32,128]{1,0:T(8,128)S(1)} %collective-permute-done.28.refs_3_, ...), custom_call_target="tpu_custom_call" | custom-call | tf_op jit(solution)/shard_map/pallas_call | solution.py:70
  (55 shorter events, 13.0 us)
Async XLA Ops:
  0.6 9.9 %copy-start.2 = (s32[1,2,8]{2,1,0:T(2,128)S(1)}, s32[1,2,8]{2,1,0:T(2,128)}, u32[]{:S(2)}) copy-start(s32[1,2,8]{2,1,0:T(2,128)} %param.6) | copy-start | bytes 196
  0.6 8.0 %collective-permute-start = (s32[2,8]{1,0:T(2,128)}, s32[2,8]{1,0:T(2,128)S(1)}, u32[]{:S(2)}, u32[]{:S(2)}) collective-permute-start(s32[2,8]{1,0:T(2,128)} %bitcast.7), channel_id=1, source_target_pairs={{0,4},{4,8},{8,12},{12,0},{1,5},{5,9},{9,13},{13,1},{2,6},{6,10},{... | collective-permute-start | bytes 200 | tf_op jit(solution)/shard_map/ppermute | solution.py:582
  3.7 4.9 %collective-permute-start.1 = (s32[2,8]{1,0:T(2,128)}, s32[2,8]{1,0:T(2,128)S(1)}, u32[]{:S(2)}, u32[]{:S(2)}) collective-permute-start(s32[2,8]{1,0:T(2,128)} %bitcast.8), channel_id=1, source_target_pairs={{0,12},{4,0},{8,4},{12,8},{1,13},{5,1},{9,5},{13,9},{2,14},{6,2},{... | collective-permute-start | bytes 200 | tf_op jit(solution)/shard_map/ppermute | solution.py:582
  5.8 4.7 %collective-permute-start.2 = (s32[2,8]{1,0:T(2,128)}, s32[2,8]{1,0:T(2,128)S(1)}, u32[]{:S(2)}, u32[]{:S(2)}) collective-permute-start(s32[2,8]{1,0:T(2,128)} %bitcast.9), channel_id=1, source_target_pairs={{0,8},{4,12},{8,0},{12,4},{1,9},{5,13},{9,1},{13,5},{2,10},{6,14},... | collective-permute-start | bytes 200 | tf_op jit(solution)/shard_map/ppermute | solution.py:582
  6.8 1.4 %copy-start = (bf16[2048,384]{1,0:T(8,128)(2,1)S(1)}, bf16[2048,384]{1,0:T(8,128)(2,1)}, u32[]{:S(2)}) copy-start(bf16[2048,384]{1,0:T(8,128)(2,1)} %refs_1_.4) | copy-start | bytes 4718596
  12.0 14.9 %collective-permute-start.3 = (bf16[256,384]{1,0:T(8,128)(2,1)S(1)}, bf16[256,384]{1,0:T(8,128)(2,1)S(1)}, u32[]{:S(2)}, u32[]{:S(2)}) collective-permute-start(bf16[256,384]{1,0:T(8,128)(2,1)S(1)} %get-tuple-element.34), channel_id=1, source_target_pairs={{0,8},{4,12},{8,0},{12,4},{1,9},{5,13},{9,1},{13,5},{2,10},{6,14},... | collective-permute-start | bytes 589832 | tf_op jit(solution)/shard_map/ppermute | solution.py:582
  13.0 13.9 %collective-permute-start.4 = (bf16[256,384]{1,0:T(8,128)(2,1)S(1)}, bf16[256,384]{1,0:T(8,128)(2,1)S(1)}, u32[]{:S(2)}, u32[]{:S(2)}) collective-permute-start(bf16[256,384]{1,0:T(8,128)(2,1)S(1)} %get-tuple-element.35), channel_id=1, source_target_pairs={{0,12},{4,0},{8,4},{12,8},{1,13},{5,1},{9,5},{13,9},{2,14},{6,2},{... | collective-permute-start | bytes 589832 | tf_op jit(solution)/shard_map/ppermute | solution.py:582
  14.4 12.5 %collective-permute-start.5 = (bf16[256,384]{1,0:T(8,128)(2,1)S(1)}, bf16[256,384]{1,0:T(8,128)(2,1)S(1)}, u32[]{:S(2)}, u32[]{:S(2)}) collective-permute-start(bf16[256,384]{1,0:T(8,128)(2,1)S(1)} %get-tuple-element.36), channel_id=1, source_target_pairs={{0,4},{4,8},{8,12},{12,0},{1,5},{5,9},{9,13},{13,1},{2,6},{6,10},{... | collective-permute-start | bytes 589832 | tf_op jit(solution)/shard_map/ppermute | solution.py:582
  15.1 13.7 %collective-permute-start.7 = (f32[1024,128]{1,0:T(8,128)S(1)}, f32[1024,128]{1,0:T(8,128)S(1)}, u32[]{:S(2)}, u32[]{:S(2)}) collective-permute-start(f32[1024,128]{1,0:T(8,128)S(1)} %shard_map.59.refs_5_.mine), channel_id=1, source_target_pairs={{0,1},{1,0},{2,3},{3,2},{4,5},{5,4},{6,7},{7,6},{8,9},{9,8},{10,11... | collective-permute-start | bytes 1572872 | tf_op jit(solution)/shard_map/ppermute | solution.py:582
  27.9 2.0 %collective-permute-start.6 = (f32[1024,128]{1,0:T(8,128)S(1)}, f32[1024,128]{1,0:T(8,128)S(1)}, u32[]{:S(2)}, u32[]{:S(2)}) collective-permute-start(f32[1024,128]{1,0:T(8,128)S(1)} %shard_map.62.refs_2_), channel_id=1, source_target_pairs={{0,1},{1,0},{2,3},{3,2},{4,5},{5,4},{6,7},{7,6},{8,9},{9,8},{10,11... | collective-permute-start | bytes 1572872 | tf_op jit(solution)/shard_map/ppermute | solution.py:582
  30.8 9.3 %collective-permute-start.10 = (f32[64,128]{1,0:T(8,128)S(1)}, f32[64,128]{1,0:T(8,128)S(1)}, u32[]{:S(2)}, u32[]{:S(2)}) collective-permute-start(f32[64,128]{1,0:T(8,128)S(1)} %get-tuple-element.41), channel_id=1, source_target_pairs={{0,4},{4,8},{8,12},{12,0},{1,5},{5,9},{9,13},{13,1},{2,6},{6,10},{... | collective-permute-start | bytes 98312 | tf_op jit(solution)/shard_map/ppermute | solution.py:582
  35.2 6.2 %collective-permute-start.8 = (f32[64,128]{1,0:T(8,128)S(1)}, f32[64,128]{1,0:T(8,128)S(1)}, u32[]{:S(2)}, u32[]{:S(2)}) collective-permute-start(f32[64,128]{1,0:T(8,128)S(1)} %get-tuple-element.41), channel_id=1, source_target_pairs={{0,12},{4,0},{8,4},{12,8},{1,13},{5,1},{9,5},{13,9},{2,14},{6,2},{... | collective-permute-start | bytes 98312 | tf_op jit(solution)/shard_map/ppermute | solution.py:582
  35.2 6.2 %collective-permute-start.9 = (f32[64,128]{1,0:T(8,128)S(1)}, f32[64,128]{1,0:T(8,128)S(1)}, u32[]{:S(2)}, u32[]{:S(2)}) collective-permute-start(f32[64,128]{1,0:T(8,128)S(1)} %get-tuple-element.41), channel_id=1, source_target_pairs={{0,8},{4,12},{8,0},{12,4},{1,9},{5,13},{9,1},{13,5},{2,10},{6,14},... | collective-permute-start | bytes 98312 | tf_op jit(solution)/shard_map/ppermute | solution.py:582
  37.6 7.8 %collective-permute-start.12 = (s16[272,128]{1,0:T(8,128)(2,1)S(1)}, s16[272,128]{1,0:T(8,128)(2,1)S(1)}, u32[]{:S(2)}, u32[]{:S(2)}) collective-permute-start(s16[272,128]{1,0:T(8,128)(2,1)S(1)} %get-tuple-element.47), channel_id=1, source_target_pairs={{0,4},{4,8},{8,12},{12,0},{1,5},{5,9},{9,13},{13,1},{2,6},{6,10},{... | collective-permute-start | bytes 208904 | tf_op jit(solution)/shard_map/ppermute | solution.py:582
  37.6 8.3 %collective-permute-start.13 = (s16[272,128]{1,0:T(8,128)(2,1)S(1)}, s16[272,128]{1,0:T(8,128)(2,1)S(1)}, u32[]{:S(2)}, u32[]{:S(2)}) collective-permute-start(s16[272,128]{1,0:T(8,128)(2,1)S(1)} %get-tuple-element.48), channel_id=1, source_target_pairs={{0,8},{4,12},{8,0},{12,4},{1,9},{5,13},{9,1},{13,5},{2,10},{6,14},... | collective-permute-start | bytes 208904 | tf_op jit(solution)/shard_map/ppermute | solution.py:582
  40.1 5.9 %collective-permute-start.14 = (s16[272,128]{1,0:T(8,128)(2,1)S(1)}, s16[272,128]{1,0:T(8,128)(2,1)S(1)}, u32[]{:S(2)}, u32[]{:S(2)}) collective-permute-start(s16[272,128]{1,0:T(8,128)(2,1)S(1)} %get-tuple-element.49), channel_id=1, source_target_pairs={{0,12},{4,0},{8,4},{12,8},{1,13},{5,1},{9,5},{13,9},{2,14},{6,2},{... | collective-permute-start | bytes 208904 | tf_op jit(solution)/shard_map/ppermute | solution.py:582
  41.4 4.0 %collective-permute-start.11 = (f32[64,128]{1,0:T(8,128)S(1)}, f32[64,128]{1,0:T(8,128)S(1)}, u32[]{:S(2)}, u32[]{:S(2)}) collective-permute-start(f32[64,128]{1,0:T(8,128)S(1)} %add_add_fusion.refs_1_), channel_id=1, source_target_pairs={{0,2},{2,0},{1,3},{3,1},{4,6},{6,4},{5,7},{7,5},{8,10},{10,8},{9,1... | collective-permute-start | bytes 98312 | tf_op jit(solution)/shard_map/ppermute | solution.py:590
  46.0 1.5 %collective-permute-start.15 = (bf16[1,256,128]{2,1,0:T(8,128)(2,1)S(1)}, bf16[1,256,128]{2,1,0:T(8,128)(2,1)S(1)}, u32[]{:S(2)}, u32[]{:S(2)}) collective-permute-start(bf16[1,256,128]{2,1,0:T(8,128)(2,1)S(1)} %get-tuple-element.50.refs_4_.refs_7_), channel_id=1, source_target_pairs={{0,1},{1,0},{2,3},{3,2},{4,5},{5,4},{6,7},{7,6},{8,9},{9,8},{10,11... | collective-permute-start | bytes 196616 | tf_op jit(solution)/shard_map/ppermute | solution.py:582
  46.1 1.4 %collective-permute-start.16 = (bf16[1,256,128]{2,1,0:T(8,128)(2,1)S(1)}, bf16[1,256,128]{2,1,0:T(8,128)(2,1)S(1)}, u32[]{:S(2)}, u32[]{:S(2)}) collective-permute-start(bf16[1,256,128]{2,1,0:T(8,128)(2,1)S(1)} %get-tuple-element.51.refs_5_.refs_8_), channel_id=1, source_target_pairs={{0,1},{1,0},{2,3},{3,2},{4,5},{5,4},{6,7},{7,6},{8,9},{9,8},{10,11... | collective-permute-start | bytes 196616 | tf_op jit(solution)/shard_map/ppermute | solution.py:582
  46.6 1.3 %collective-permute-start.17 = (bf16[1,256,128]{2,1,0:T(8,128)(2,1)S(1)}, bf16[1,256,128]{2,1,0:T(8,128)(2,1)S(1)}, u32[]{:S(2)}, u32[]{:S(2)}) collective-permute-start(bf16[1,256,128]{2,1,0:T(8,128)(2,1)S(1)} %get-tuple-element.52.refs_6_.refs_9_), channel_id=1, source_target_pairs={{0,1},{1,0},{2,3},{3,2},{4,5},{5,4},{6,7},{7,6},{8,9},{9,8},{10,11... | collective-permute-start | bytes 196616 | tf_op jit(solution)/shard_map/ppermute | solution.py:582
  48.9 5.8 %collective-permute-start.18 = (s16[32,2176]{1,0:T(8,128)(2,1)S(1)}, s16[32,2176]{1,0:T(8,128)(2,1)S(1)}, u32[]{:S(2)}, u32[]{:S(2)}) collective-permute-start(s16[32,2176]{1,0:T(8,128)(2,1)S(1)} %shard_map.68.refs_2_), channel_id=1, source_target_pairs={{0,2},{2,0},{1,3},{3,1},{4,6},{6,4},{5,7},{7,5},{8,10},{10,8},{9,1... | collective-permute-start | bytes 417800 | tf_op jit(solution)/shard_map/ppermute | solution.py:590
  55.3 4.5 %collective-permute-start.19 = (f32[32,2048]{1,0:T(8,128)S(1)}, f32[32,2048]{1,0:T(8,128)S(1)}, u32[]{:S(2)}, u32[]{:S(2)}) collective-permute-start(f32[32,2048]{1,0:T(8,128)S(1)} %get-tuple-element.53.refs_0_.refs_3_), channel_id=1, source_target_pairs={{0,1},{1,0},{2,3},{3,2},{4,5},{5,4},{6,7},{7,6},{8,9},{9,8},{10,11... | collective-permute-start | bytes 786440 | tf_op jit(solution)/shard_map/ppermute | solution.py:582
  55.4 6.2 %collective-permute-start.20 = (s16[144,128]{1,0:T(8,128)(2,1)S(1)}, s16[144,128]{1,0:T(8,128)(2,1)S(1)}, u32[]{:S(2)}, u32[]{:S(2)}) collective-permute-start(s16[144,128]{1,0:T(8,128)(2,1)S(1)} %get-tuple-element.54), channel_id=1, source_target_pairs={{0,4},{4,8},{8,12},{12,0},{1,5},{5,9},{9,13},{13,1},{2,6},{6,10},{... | collective-permute-start | bytes 110600 | tf_op jit(solution)/shard_map/ppermute | solution.py:582
  56.8 6.0 %collective-permute-start.21 = (s16[144,128]{1,0:T(8,128)(2,1)S(1)}, s16[144,128]{1,0:T(8,128)(2,1)S(1)}, u32[]{:S(2)}, u32[]{:S(2)}) collective-permute-start(s16[144,128]{1,0:T(8,128)(2,1)S(1)} %get-tuple-element.55), channel_id=1, source_target_pairs={{0,8},{4,12},{8,0},{12,4},{1,9},{5,13},{9,1},{13,5},{2,10},{6,14},... | collective-permute-start | bytes 110600 | tf_op jit(solution)/shard_map/ppermute | solution.py:582
  58.5 4.7 %collective-permute-start.22 = (s16[144,128]{1,0:T(8,128)(2,1)S(1)}, s16[144,128]{1,0:T(8,128)(2,1)S(1)}, u32[]{:S(2)}, u32[]{:S(2)}) collective-permute-start(s16[144,128]{1,0:T(8,128)(2,1)S(1)} %get-tuple-element.56), channel_id=1, source_target_pairs={{0,12},{4,0},{8,4},{12,8},{1,13},{5,1},{9,5},{13,9},{2,14},{6,2},{... | collective-permute-start | bytes 110600 | tf_op jit(solution)/shard_map/ppermute | solution.py:582
  60.3 3.9 %collective-permute-start.23 = (f32[32,128]{1,0:T(8,128)S(1)}, f32[32,128]{1,0:T(8,128)S(1)}, u32[]{:S(2)}, u32[]{:S(2)}) collective-permute-start(f32[32,128]{1,0:T(8,128)S(1)} %shard_map.70.refs_2_), channel_id=1, source_target_pairs={{0,4},{4,0},{8,12},{12,8},{1,5},{5,1},{9,13},{13,9},{2,6},{6,2},{1... | collective-permute-start | bytes 49160 | tf_op jit(solution)/shard_map/ppermute | solution.py:590
  64.3 6.2 %collective-permute-start.24 = (s16[32,2176]{1,0:T(8,128)(2,1)S(1)}, s16[32,2176]{1,0:T(8,128)(2,1)S(1)}, u32[]{:S(2)}, u32[]{:S(2)}) collective-permute-start(s16[32,2176]{1,0:T(8,128)(2,1)S(1)} %shard_map.72.refs_1_), channel_id=1, source_target_pairs={{0,2},{2,0},{1,3},{3,1},{4,6},{6,4},{5,7},{7,5},{8,10},{10,8},{9,1... | collective-permute-start | bytes 417800 | tf_op jit(solution)/shard_map/ppermute | solution.py:590
  65.9 4.6 %collective-permute-start.25 = (f32[32,128]{1,0:T(8,128)S(1)}, f32[32,128]{1,0:T(8,128)S(1)}, u32[]{:S(2)}, u32[]{:S(2)}) collective-permute-start(f32[32,128]{1,0:T(8,128)S(1)} %add.18.after.refs_0_), channel_id=1, source_target_pairs={{0,8},{4,12},{8,0},{12,4},{1,9},{5,13},{9,1},{13,5},{2,10},{6,14},... | collective-permute-start | bytes 49160 | tf_op jit(solution)/shard_map/ppermute | solution.py:590
  70.6 1.7 %collective-permute-start.26 = (f32[32,2048]{1,0:T(8,128)S(1)}, f32[32,2048]{1,0:T(8,128)S(1)}, u32[]{:S(2)}, u32[]{:S(2)}) collective-permute-start(f32[32,2048]{1,0:T(8,128)S(1)} %shard_map.73.after.refs_1_), channel_id=1, source_target_pairs={{0,1},{1,0},{2,3},{3,2},{4,5},{5,4},{6,7},{7,6},{8,9},{9,8},{10,11... | collective-permute-start | bytes 786440 | tf_op jit(solution)/shard_map/ppermute | solution.py:582
  73.2 5.6 %collective-permute-start.27 = (f32[32,128]{1,0:T(8,128)S(1)}, f32[32,128]{1,0:T(8,128)S(1)}, u32[]{:S(2)}, u32[]{:S(2)}) collective-permute-start(f32[32,128]{1,0:T(8,128)S(1)} %get-tuple-element.58.refs_1_), channel_id=1, source_target_pairs={{0,4},{4,8},{8,12},{12,0},{1,5},{5,9},{9,13},{13,1},{2,6},{6,10},{... | collective-permute-start | bytes 49160 | tf_op jit(solution)/shard_map/ppermute | solution.py:582
  74.0 4.8 %collective-permute-start.28 = (f32[32,128]{1,0:T(8,128)S(1)}, f32[32,128]{1,0:T(8,128)S(1)}, u32[]{:S(2)}, u32[]{:S(2)}) collective-permute-start(f32[32,128]{1,0:T(8,128)S(1)} %get-tuple-element.58.refs_1_), channel_id=1, source_target_pairs={{0,8},{4,12},{8,0},{12,4},{1,9},{5,13},{9,1},{13,5},{2,10},{6,14},... | collective-permute-start | bytes 49160 | tf_op jit(solution)/shard_map/ppermute | solution.py:582
  76.2 3.7 %collective-permute-start.29 = (f32[32,128]{1,0:T(8,128)S(1)}, f32[32,128]{1,0:T(8,128)S(1)}, u32[]{:S(2)}, u32[]{:S(2)}) collective-permute-start(f32[32,128]{1,0:T(8,128)S(1)} %get-tuple-element.58.refs_1_), channel_id=1, source_target_pairs={{0,12},{4,0},{8,4},{12,8},{1,13},{5,1},{9,5},{13,9},{2,14},{6,2},{... | collective-permute-start | bytes 49160 | tf_op jit(solution)/shard_map/ppermute | solution.py:582
  (1 other events, 1.1 us)
